TPU v7x, 256 devices: a whole 4x4x8 slice. The times are simulated.
256 devices in a mesh: row: 16 (over y, x_hi, core), res: 16 (over z, x_lo).
Axes of the slice: x: 4 (x_hi: 2, x_lo: 2; x = x_hi * 2 + x_lo), y: 4, z: 8, core: 2. Of those that a mesh axis runs over, the one named last changes fastest.
Arguments:
- sequence_stack: bfloat16 [128, 1024, 768], P('row', 'res'), may hold values from -6 to 6
- asking_projector: bfloat16 [768, 768], replicated, may hold values from -0.5 to 0.5
- lookup_projector: bfloat16 [768, 768], replicated, may hold values from -0.5 to 0.5
- content_projector: bfloat16 [768, 768], replicated, may hold values from -0.21875 to 0.21875
- final_projector: bfloat16 [768, 768], replicated, may hold values from -0.21875 to 0.21875
Outputs:
- attended: bfloat16 [128, 1024, 768], P('row', 'res')
All inputs are finite; a program needn't handle non-finite values.
Results may differ from a plain program's by a relative error of at most 0.012.
The roundings to bfloat16 on the way count: a program that leaves them out, or rounds other values in their place, can miss the bound.
Values may be sent and summed in bfloat16 or wider, within the bound.
No kernel may reach another device: no remote copies, remote signals or barrier semaphores. Data moves between devices by JAX's collectives and lax.ppermute only.
A program may use at most 128 MiB of HBM per device.

v0:
```python
import math

import jax
import jax.numpy as jnp
from jax import lax
from jax.sharding import PartitionSpec as P

H = 12
DH = 64


def standardize_block(values_in):
    widened = values_in.astype(jnp.float32)
    average = jnp.mean(widened, axis=-1, keepdims=True)
    centred = widened - average
    variance = jnp.mean(centred * centred, axis=-1, keepdims=True)
    return (centred * lax.rsqrt(variance + 1e-05)).astype(jnp.bfloat16)


def project(standardized_activity, weight_matrix):
    return jnp.dot(standardized_activity, weight_matrix, preferred_element_type=jnp.float32).astype(
        jnp.bfloat16
    )


def softmax_rows(logits):
    shifted = logits - jnp.max(logits, axis=-1, keepdims=True)
    powered = jnp.exp(shifted)
    return powered / jnp.sum(powered, axis=-1, keepdims=True)


def local(sequence_stack, asking_projector, lookup_projector, content_projector, final_projector):
    sequence_number, position_window, embedding_dimension = sequence_stack.shape
    standardized_activity = standardize_block(sequence_stack).reshape(
        sequence_number * position_window, embedding_dimension
    )
    queries = project(standardized_activity, asking_projector).reshape(
        sequence_number, position_window, H, DH
    )
    keys = project(standardized_activity, lookup_projector).reshape(
        sequence_number, position_window, embedding_dimension
    )
    values = project(standardized_activity, content_projector).reshape(
        sequence_number, position_window, embedding_dimension
    )
    factor = 1.0 / math.sqrt(DH * sequence_number * lax.axis_size("row"))
    portion = lax.all_gather(keys, "res", axis=1, tiled=True)
    count = portion.shape[1]
    products = jnp.einsum(
        "rihd,rjhd->hij",
        queries,
        portion.reshape(sequence_number, count, H, DH),
        preferred_element_type=jnp.float32,
    )
    summed = lax.psum(products, "row")
    probs = softmax_rows(summed * factor).astype(jnp.bfloat16)
    portion = lax.all_gather(values, "res", axis=1, tiled=True)
    count = portion.shape[1]
    mixed_sum = jnp.einsum(
        "hij,rjhd->rihd",
        probs,
        portion.reshape(sequence_number, count, H, DH),
        preferred_element_type=jnp.float32,
    )
    mixed = mixed_sum.astype(jnp.bfloat16).reshape(
        sequence_number * position_window, embedding_dimension
    )
    return project(mixed, final_projector).reshape(
        sequence_number, position_window, embedding_dimension
    )


def solution(mesh):
    return jax.shard_map(
        local,
        mesh=mesh,
        in_specs=(P("row", "res", None), P(), P(), P(), P()),
        out_specs=P("row", "res", None),
        check_vma=False,
    )
```

profile of v0, /device:TPU:1, one launch (start us, length us, event | category | flops | bytes accessed | tf_op | source)
XLA Modules:
  0.0 737.1 jit_solution(9362770076145694760)
XLA Ops:
  6.5 0.0 copy-start
  6.5 0.0 copy-start.2
  6.5 0.0 all-gather.5.cloned.1.call-start
  6.5 1.4 convert_reduce_fusion
  8.0 1.5 fusion.16
  9.5 0.0 copy-done.2
  9.5 0.3 fusion.17
  9.8 0.0 copy-done
  9.8 0.8 convolution_convert_fusion.1
  10.6 1.3 copy.17
  11.9 0.0 all-gather.5.cloned.1.call-update
  11.9 0.0 all-gather.3.cloned.1.call-start
  12.0 2.0 convolution_convert_fusion.3
  14.0 1.4 copy.14
  15.4 0.0 all-gather.3.cloned.1.call-update
  15.4 0.2 all-reduce.2.cloned.1.call-start
  15.6 2.0 convolution_convert_fusion.2
  17.7 1.3 reshape.48
  19.0 263.6 %all-gather.5.cloned.1.call-done = bf16[8,1024,768]{2,0,1:T(8,128)(2,1)} async-done(((bf16[8,64,768]{2,0,1:T(8,128)(2,1)}), bf16[8,1024,768]{2,0,1:T(8,128)(2,1)}) %all-gather.5.cloned.1.call-update) | async-done | bytes 12582928 | tf_op jit(solution)/shard_map/all_gather | solution.py:47
  282.6 16.5 %copy.18 = bf16[8,1024,768]{1,2,0:T(8,128)(2,1)} copy(bf16[8,1024,768]{2,0,1:T(8,128)(2,1)} %all-gather.5.cloned.1.call-done) | data formatting | bytes 25165824 | tf_op jit(solution)/shard_map/all_gather | solution.py:47
  299.1 8.6 %fusion.8 = f32[12,64,1024]{2,1,0:T(8,128)} fusion(bf16[8,1024,12,64]{1,3,2,0:T(8,128)(2,1)} %bitcast.31, bf16[8,64,12,64]{3,2,1,0:T(8,128)(2,1)S(1)} %reshape.48), kind=kOutput, calls=%fused_computation.11 | convolution fusion | flops 805306368 | bytes 16515072 | tf_op jit(solution)/shard_map/rihd,rjhd->hij/dot_general | solution.py:49
  307.7 0.0 all-reduce.2.cloned.1.call-update
  307.7 245.9 %all-gather.3.cloned.1.call-done = bf16[8,1024,768]{2,0,1:T(8,128)(2,1)} async-done(((bf16[8,64,768]{2,0,1:T(8,128)(2,1)}), bf16[8,1024,768]{2,0,1:T(8,128)(2,1)}) %all-gather.3.cloned.1.call-update) | async-done | bytes 12582928 | tf_op jit(solution)/shard_map/all_gather | solution.py:57
  553.6 16.5 %copy.15 = bf16[8,1024,768]{1,2,0:T(8,128)(2,1)} copy(bf16[8,1024,768]{2,0,1:T(8,128)(2,1)} %all-gather.3.cloned.1.call-done) | data formatting | bytes 25165824 | tf_op jit(solution)/shard_map/all_gather | solution.py:57
  570.2 143.4 %all-reduce.2.cloned.1.call-done = f32[12,64,1024]{2,1,0:T(8,128)} async-done(((f32[12,64,1024]{2,1,0:T(8,128)}), f32[12,64,1024]{2,1,0:T(8,128)}) %all-reduce.2.cloned.1.call-update) | async-done | bytes 3145744 | tf_op jit(solution)/shard_map/psum | solution.py:55
  713.6 3.7 fusion.27
  717.3 8.1 %fusion.21 = bf16[8,64,12,64]{1,3,0,2:T(8,128)(2,1)S(1)} fusion(f32[12,64,1024]{2,1,0:T(8,128)S(1)} %get-tuple-element.6, f32[12,64]{1,0:T(8,128)S(1)} %get-tuple-element.5, bf16[8,1024,12,64]{1,3,2,0:T(8,128)(2,1)} %bitcast.30), kind=kOutput, calls=%fused_computation.20 | convolution fusion | flops 807272448 | bytes 16518144 | tf_op jit(solution)/shard_map/hij,rjhd->rihd/dot_general | solution.py:59
  725.4 1.2 copy.22
  726.6 0.0 copy-start.1
  726.6 1.0 reshape.44
  727.6 3.0 convolution_convert_fusion
  730.6 0.0 copy-done.1
  (2 shorter events, 0.0 us)
Async XLA Ops:
  6.5 3.2 copy-start
  6.5 3.0 copy-start.2
  6.5 276.0 %all-gather.5.cloned.1.call-start = ((), (), s32[]{:S(2)}) async-start(), calls=%async_computation.1 | async-start | bytes 13369344 | tf_op jit(solution)/shard_map/all_gather | solution.py:47
  11.9 541.7 %all-gather.3.cloned.1.call-start = ((), (), s32[]{:S(2)}) async-start(), calls=%async_computation | async-start | bytes 13369344 | tf_op jit(solution)/shard_map/all_gather | solution.py:57
  15.4 698.2 %all-reduce.2.cloned.1.call-start = ((), (), s32[]{:S(2)}) async-start(), calls=%async_computation.2 | async-start | bytes 6291456 | tf_op jit(solution)/shard_map/psum | solution.py:55
  726.6 4.0 copy-start.1
Sparse Core Ops, SparseCore 0:
  12.0 270.4 all-gather.4
  284.4 269.2 all-gather.2
  556.3 157.2 all-reduce.1
where the time goes:
time: 739 us; the launch traced here: 737 us
  waiting for transfers between devices  653 us (88%)
  local copies, waits for them, and re-layouts  39.2 us (5%)
  matrix products  24.5 us (3%)
  between operations  13.2 us (2%)
    all_gather x1, waiting for transfers between devices, local(): portion = lax.all_gather(keys, 'res', axis=1, tiled=True)  264 us
    all_gather x1, waiting for transfers between devices, local(): portion = lax.all_gather(values, 'res', axis=1, tiled=True)  246 us
    psum x1, waiting for transfers between devices, local(): summed = lax.psum(products, 'row')  143 us
    all_gather x1, local copies, waits for them, and re-layouts, local(): portion = lax.all_gather(values, 'res', axis=1, tiled=True)  16.5 us
    all_gather x1, local copies, waits for them, and re-layouts, local(): portion = lax.all_gather(keys, 'res', axis=1, tiled=True)  16.5 us
  transfers between devices with their start and end apart: 3, of which 3 were waited for; matrix products, arithmetic and copies ran while one was open for 7% of the time, Pallas kernels for 0%

commit v1 on v0

v1 whole, which is shorter than its diff:
```python
import functools
import math

import jax
import jax.numpy as jnp
from jax import lax
from jax.experimental import pallas as pl
from jax.experimental.pallas import tpu as pltpu
from jax.sharding import Mesh, PartitionSpec as P

H = 12
DH = 64
EMBED = 768
ROWS = 8
RES = 64
Z = 8
CHUNK = EMBED // Z
FULL = DH
HALF = CHUNK - DH
PEERS = 8
SUB = RES // 2
QUERIES = Z * SUB
KEYS = 2 * Z * RES

f32 = jnp.float32
bf16 = jnp.bfloat16
PARAMS = pltpu.CompilerParams(vmem_limit_bytes=48 * 1024 * 1024)
VMEM = pl.BlockSpec(memory_space=pltpu.VMEM)
SMEM = pl.BlockSpec(memory_space=pltpu.SMEM)


def chunk_pieces(z):
    base = z * CHUNK
    if z % 2 == 0:
        return (base, FULL), (base + FULL, HALF)
    return (base + HALF, FULL), (base, HALF)


def dot(a, b, ca, cb):
    return lax.dot_general(a, b, (((ca,), (cb,)), ((), ())), preferred_element_type=f32)


def embed_kernel(x_ref, wq_ref, wk_ref, wv_ref, q_ref, k_ref, v_ref, n_ref):
    x = x_ref[...].astype(f32)
    centred = x - jnp.mean(x, axis=-1, keepdims=True)
    var = jnp.mean(centred * centred, axis=-1, keepdims=True)
    n_ref[...] = (centred * lax.rsqrt(var + 1e-05)).astype(bf16)
    n = n_ref[...].reshape(ROWS * RES, EMBED)
    for w_ref, o_ref in ((wk_ref, k_ref), (wv_ref, v_ref)):
        t = dot(w_ref[...], n, 0, 1).astype(bf16)
        for z in range(Z):
            (a, na), (b, nb) = chunk_pieces(z)
            o_ref[z, 0:FULL, :] = t[a : a + na]
            o_ref[z, FULL:CHUNK, :] = t[b : b + nb]
    for c in range(2):
        n = n_ref[:, c * SUB : (c + 1) * SUB, :].reshape(ROWS * SUB, EMBED)
        t = dot(wq_ref[...], n, 0, 1).astype(bf16)
        for z in range(Z):
            (a, na), (b, nb) = chunk_pieces(z)
            q_ref[2 * z + c, 0:FULL, :] = t[a : a + na]
            q_ref[2 * z + c, FULL:CHUNK, :] = t[b : b + nb]


def embed(x, wq, wk, wv):
    return pl.pallas_call(
        embed_kernel,
        out_shape=(
            jax.ShapeDtypeStruct((2 * Z, CHUNK, ROWS * SUB), bf16),
            jax.ShapeDtypeStruct((Z, CHUNK, ROWS * RES), bf16),
            jax.ShapeDtypeStruct((Z, CHUNK, ROWS * RES), bf16),
        ),
        in_specs=[VMEM] * 4,
        out_specs=(VMEM,) * 3,
        scratch_shapes=[pltpu.VMEM((ROWS, RES, EMBED), bf16)],
        compiler_params=PARAMS,
    )(x, wq, wk, wv)


def widen(refs, r):
    return jnp.concatenate(
        [ref[z][:, r * RES : (r + 1) * RES] for ref in refs for z in range(Z)], axis=1
    )


def score_kernel(me_ref, q_ref, k00, k01, k10, k11, *rest):
    outs, (qf, qh, kf, kh) = rest[:PEERS], rest[PEERS:]
    me, core = me_ref[0], me_ref[1]
    for cr, ks in ((0, (k00, k01)), (1, (k10, k11))):
        c = jnp.bitwise_xor(core, cr)
        blocks = [q_ref[2 * jnp.bitwise_xor(me, s) + c] for s in range(PEERS)]
        for r in range(ROWS):
            n = cr * ROWS + r
            t = jnp.concatenate([b[:, r * SUB : (r + 1) * SUB] for b in blocks], axis=1)
            qf[n * FULL : (n + 1) * FULL, :] = t[:FULL]
            qh[n * HALF : (n + 1) * HALF, :] = t[FULL:]
            t = widen(ks, r)
            kf[n * FULL : (n + 1) * FULL, :] = t[:FULL]
            kh[n * HALF : (n + 1) * HALF, :] = t[FULL:]
    for i, (a, b) in enumerate(((qf, kf), (qh, kh))):
        s = dot(a[...], b[...], 0, 0)
        for p in range(PEERS):
            outs[p][i] = s[p * SUB : (p + 1) * SUB]


def score(me, q, ks):
    rows = 2 * ROWS
    return pl.pallas_call(
        score_kernel,
        out_shape=(jax.ShapeDtypeStruct((2, SUB, KEYS), f32),) * PEERS,
        in_specs=[SMEM] + [VMEM] * 5,
        out_specs=(VMEM,) * PEERS,
        scratch_shapes=[
            pltpu.VMEM((rows * FULL, QUERIES), bf16),
            pltpu.VMEM((rows * HALF, QUERIES), bf16),
            pltpu.VMEM((rows * FULL, KEYS), bf16),
            pltpu.VMEM((rows * HALF, KEYS), bf16),
        ],
        compiler_params=PARAMS,
    )(me, q, *ks)


def total_kernel(*refs):
    ins, (full, half) = refs[:PEERS], refs[PEERS:]
    for i, out in enumerate((full, half)):
        t = ins[0][i]
        for ref in ins[1:]:
            t = t + ref[i]
        out[...] = t


def total(parts):
    return pl.pallas_call(
        total_kernel,
        out_shape=(jax.ShapeDtypeStruct((SUB, KEYS), f32),) * 2,
        in_specs=[VMEM] * PEERS,
        out_specs=(VMEM,) * 2,
        compiler_params=PARAMS,
    )(*parts)


def softmax_kernel(factor, full, half, other, out):
    for i, logits in enumerate((full[...], half[...] + other[...])):
        logits = logits * factor
        powered = jnp.exp(logits - jnp.max(logits, axis=-1, keepdims=True))
        out[i] = (powered / jnp.sum(powered, axis=-1, keepdims=True)).astype(bf16)


def softmax(factor, full, half, other):
    return pl.pallas_call(
        functools.partial(softmax_kernel, factor),
        out_shape=jax.ShapeDtypeStruct((2, SUB, KEYS), bf16),
        in_specs=[VMEM] * 3,
        out_specs=VMEM,
        compiler_params=PARAMS,
    )(full, half, other)


def mix_kernel(me_ref, v00, v01, v10, v11, *rest):
    ps, o_ref, (vf, vh) = rest[:PEERS], rest[PEERS], rest[PEERS + 1 :]
    me, core = me_ref[0], me_ref[1]
    pf = jnp.concatenate([p[0] for p in ps], axis=0)
    ph = jnp.concatenate([p[1] for p in ps], axis=0)
    for cr, vs in ((0, (v00, v01)), (1, (v10, v11))):
        c = jnp.bitwise_xor(core, cr)
        for r in range(ROWS):
            t = widen(vs, r)
            vf[r * FULL : (r + 1) * FULL, :] = t[:FULL]
            vh[r * HALF : (r + 1) * HALF, :] = t[FULL:]
        for v, p, first, n in ((vf, pf, 0, FULL), (vh, ph, FULL, HALF)):
            mixed = dot(v[...], p, 1, 1).astype(bf16)
            for s in range(PEERS):
                o_ref[2 * jnp.bitwise_xor(me, s) + c, first : first + n, :] = jnp.concatenate(
                    [mixed[r * n : (r + 1) * n, s * SUB : (s + 1) * SUB] for r in range(ROWS)], axis=1
                )


def mix(me, vs, ps):
    return pl.pallas_call(
        mix_kernel,
        out_shape=jax.ShapeDtypeStruct((2 * Z, CHUNK, ROWS * SUB), bf16),
        in_specs=[SMEM] + [VMEM] * (4 + PEERS),
        out_specs=VMEM,
        scratch_shapes=[
            pltpu.VMEM((ROWS * FULL, KEYS), bf16),
            pltpu.VMEM((ROWS * HALF, KEYS), bf16),
        ],
        compiler_params=PARAMS,
    )(me, *vs, *ps)


def final_kernel(m_ref, w_ref, o_ref, t_ref):
    for c in range(2):
        for z in range(Z):
            (a, na), (b, nb) = chunk_pieces(z)
            t_ref[a : a + na, :] = m_ref[2 * z + c, 0:FULL, :]
            t_ref[b : b + nb, :] = m_ref[2 * z + c, FULL:CHUNK, :]
        attended = dot(t_ref[...], w_ref[...], 0, 0).astype(bf16)
        o_ref[:, c * SUB : (c + 1) * SUB, :] = attended.reshape(ROWS, SUB, EMBED)


def final(m, w):
    return pl.pallas_call(
        final_kernel,
        out_shape=jax.ShapeDtypeStruct((ROWS, RES, EMBED), bf16),
        in_specs=[VMEM] * 2,
        out_specs=VMEM,
        scratch_shapes=[pltpu.VMEM((EMBED, ROWS * SUB), bf16)],
        compiler_params=PARAMS,
    )(m, w)


def flip(x, axes, n, s):
    return lax.ppermute(x, axes, [(i, i ^ s) for i in range(n)])


def gather4(own):
    far = flip(own, "xl", 2, 1)
    return own, far, flip(own, "c", 2, 1), flip(far, "c", 2, 1)


def local(x, wq, wk, wv, wf):
    me = jnp.stack([lax.axis_index(("y", "xh")), lax.axis_index("c")]).astype(jnp.int32)
    q, k, v = embed(x, wq, wk, wv)
    ks = gather4(lax.all_to_all(k, "z", 0, 0, tiled=True))
    q = lax.all_to_all(q, ("z", "c"), 0, 0, tiled=True)
    parts = score(me, q, ks)
    parts = [parts[0]] + [flip(parts[s], ("y", "xh"), PEERS, s) for s in range(1, PEERS)]
    vs = gather4(lax.all_to_all(v, "z", 0, 0, tiled=True))
    full, half = total(parts)
    rows = ROWS * 2 * PEERS
    probs = softmax(1.0 / math.sqrt(DH * rows), full, half, flip(half, "z", Z, 1))
    ps = [probs] + [flip(probs, ("y", "xh"), PEERS, s) for s in range(1, PEERS)]
    mixed = lax.all_to_all(mix(me, vs, ps), ("z", "c"), 0, 0, tiled=True)
    return final(mixed, wf)


def solution(mesh):
    fine = Mesh(mesh.devices.reshape(4, 2, 2, 8, 2), ("y", "xh", "c", "z", "xl"))
    spec = P(("y", "xh", "c"), ("z", "xl"), None)
    return jax.shard_map(
        local,
        mesh=fine,
        in_specs=(spec, P(), P(), P(), P()),
        out_specs=spec,
        check_vma=False,
    )
```

time: 739 us -> 194 us (0.26)
  waiting for transfers between devices: 653 us -> 81.8 us
  blocking collectives: 0 us -> 58.1 us
  starting transfers between devices: 0.27 us -> 36.4 us
  local copies, waits for them, and re-layouts: 39.2 us -> 3.68 us
  matrix products: 24.5 us -> 0 us
  Pallas kernels: 0 us -> 13.2 us
  between operations: 13.2 us -> 0.09 us
    all_gather x2 -> x0, waiting for transfers between devices: 510 us -> none  [the longest x1 264 us: local(): portion = lax.all_gather(keys, 'res', axis=1, tiled=True)]
    psum x1 -> x0, waiting for transfers between devices: 143 us -> none  [local(): summed = lax.psum(products, 'row')]
    all_to_all x0 -> x2, blocking collectives: none -> 58.1 us  [the longest x1 30.4 us: local(): ks = gather4(lax.all_to_all(k, 'z', 0, 0, tiled=True))]
    ppermute x0 -> x21, waiting for transfers between devices: none -> 41.1 us  [flip(): return lax.ppermute(x, axes, [(i, i ^ s) for i in range(n)])]
    all_to_all x0 -> x2, waiting for transfers between devices: none -> 40.7 us  [the longest x1 20.9 us: local(): q = lax.all_to_all(q, ('z', 'c'), 0, 0, tiled=True)]
    all_gather x2 -> x0, local copies, waits for them, and re-layouts: 33.1 us -> none  [the longest x1 16.5 us: local(): portion = lax.all_gather(values, 'res', axis=1, tiled=True)]
    ppermute x0 -> x21, starting transfers between devices: none -> 26.6 us  [flip(): return lax.ppermute(x, axes, [(i, i ^ s) for i in range(n)])]
    dot_general x6 -> x0, matrix products: 24.5 us -> none  [the longest x1 8.6 us: local(): jnp.einsum('rihd,rjhd->hij', queries, portion.reshape(sequence_number, co...]
  transfers between devices with their start and end apart: 3 -> 23, of which waited for: 3 -> 11; matrix products, arithmetic and copies ran while one was open for 7% -> 0% of each run, Pallas kernels for 0% -> 2%
where the time goes in v1:
time: 194 us; the launch traced here: 193 us
  waiting for transfers between devices  81.8 us (42%)
  blocking collectives  58.1 us (30%)
  starting transfers between devices  36.4 us (19%)
  Pallas kernels  13.2 us (7%)
  local copies, waits for them, and re-layouts  3.68 us (2%)
    ppermute x21, waiting for transfers between devices, flip(): return lax.ppermute(x, axes, [(i, i ^ s) for i in range(n)])  41.1 us
    all_to_all x1, blocking collectives, local(): ks = gather4(lax.all_to_all(k, 'z', 0, 0, tiled=True))  30.4 us
    all_to_all x1, blocking collectives, local(): mixed = lax.all_to_all(mix(me, vs, ps), ('z', 'c'), 0, 0, tiled=True)  27.7 us
    ppermute x21, starting transfers between devices, flip(): return lax.ppermute(x, axes, [(i, i ^ s) for i in range(n)])  26.6 us
    all_to_all x1, waiting for transfers between devices, local(): q = lax.all_to_all(q, ('z', 'c'), 0, 0, tiled=True)  20.9 us
    all_to_all x1, waiting for transfers between devices, local(): vs = gather4(lax.all_to_all(v, 'z', 0, 0, tiled=True))  19.8 us
    all_to_all x1, starting transfers between devices, local(): q = lax.all_to_all(q, ('z', 'c'), 0, 0, tiled=True)  6.28 us
    pallas_call x1, Pallas kernels, embed(): pl.pallas_call(embed_kernel, out_shape=(jax.ShapeDtypeStruct((2 * Z, CHUN...  4.63 us
  transfers between devices with their start and end apart: 23, of which 11 were waited for; matrix products, arithmetic and copies ran while one was open for 0% of the time, Pallas kernels for 2%

profile of v1, /device:TPU:1, one launch (start us, length us, event | category | flops | bytes accessed | tf_op | source)
XLA Modules:
  0.0 193.3 jit_solution(2456293373243064580)
XLA Ops:
  0.0 1.3 copy-done
  1.3 1.3 copy-done.1
  2.5 1.1 copy-done.3
  3.7 4.6 %shard_map.55 = (bf16[16,96,256]{2,1,0:T(8,128)(2,1)}, bf16[8,96,512]{2,1,0:T(8,128)(2,1)S(1)}, bf16[8,96,512]{2,1,0:T(8,128)(2,1)}) custom-call(bf16[8,64,768]{2,1,0:T(8,128)(2,1)S(1)} %copy-done.3, bf16[768,768]{1,0:T(8,128)(2,1)S(1)} %copy-done, bf16[768,768]{1,0:T(8,128)(2,1)S(1)} %copy-done.1, bf16[768,768]{1,0:T(8,128)(2,1)} %wv_ref.1), custom_call_target="tpu_custom_call" | custom-call | tf_op jit(solution)/shard_map/pallas_call | solution.py:65
  8.3 30.4 %all_to_all.20.k00 = bf16[8,96,512]{2,1,0:T(8,128)(2,1)S(1)} all-to-all(bf16[8,96,512]{2,1,0:T(8,128)(2,1)S(1)} %get-tuple-element.20), channel_id=1, replica_groups=mesh['y'=4,'xh'=2,'c'=2,'z'=8,'xl'=2] {'z'}, dimensions={0} | all-to-all | bytes 1572864 | tf_op jit(solution)/shard_map/all_to_all | solution.py:224
  38.7 3.5 %all-to-all-start = ((bf16[8,96,512]{2,1,0:T(8,128)(2,1)}), bf16[8,96,512]{2,1,0:T(8,128)(2,1)S(1)}, u32[]{:S(2)}, u32[]{:S(2)}) async-start(bf16[8,96,512]{2,1,0:T(8,128)(2,1)} %get-tuple-element.18), calls=%async_computation | async-start | bytes 1572864 | tf_op jit(solution)/shard_map/all_to_all | solution.py:228
  42.2 1.3 collective-permute-start.3
  43.6 19.8 %all-to-all-done.v00 = bf16[8,96,512]{2,1,0:T(8,128)(2,1)S(1)} async-done(((bf16[8,96,512]{2,1,0:T(8,128)(2,1)}), bf16[8,96,512]{2,1,0:T(8,128)(2,1)S(1)}, u32[]{:S(2)}, u32[]{:S(2)}) %all-to-all-start) | async-done | bytes 786464 | tf_op jit(solution)/shard_map/all_to_all | solution.py:228
  63.4 6.3 %all-to-all-start.1 = ((bf16[16,96,256]{2,1,0:T(8,128)(2,1)}), bf16[16,96,256]{2,1,0:T(8,128)(2,1)S(1)}, u32[]{:S(2)}, u32[]{:S(2)}) async-start(bf16[16,96,256]{2,1,0:T(8,128)(2,1)} %get-tuple-element.19), calls=%async_computation.1 | async-start | bytes 1572864 | tf_op jit(solution)/shard_map/all_to_all | solution.py:225
  70.2 1.3 collective-permute-start
  71.5 20.9 %all-to-all-done.1.q_ref = bf16[16,96,256]{2,1,0:T(8,128)(2,1)S(1)} async-done(((bf16[16,96,256]{2,1,0:T(8,128)(2,1)}), bf16[16,96,256]{2,1,0:T(8,128)(2,1)S(1)}, u32[]{:S(2)}, u32[]{:S(2)}) %all-to-all-start.1) | async-done | bytes 786464 | tf_op jit(solution)/shard_map/all_to_all | solution.py:225
  92.4 3.8 %shard_map.56 = (f32[2,32,1024]{2,1,0:T(8,128)S(1)}, f32[2,32,1024]{2,1,0:T(8,128)S(1)}, f32[2,32,1024]{2,1,0:T(8,128)S(1)}, f32[2,32,1024]{2,1,0:T(8,128)S(1)},...) custom-call(s32[2]{0:T(128)S(1)} %pad_add_fusion.me_ref, ...), custom_call_target="tpu_custom_call" | custom-call | tf_op jit(solution)/shard_map/pallas_call | solution.py:107
  96.2 2.9 %collective-permute-start.6 = (f32[2,32,1024]{2,1,0:T(8,128)S(1)}, f32[2,32,1024]{2,1,0:T(8,128)S(1)}, u32[]{:S(2)}, u32[]{:S(2)}) collective-permute-start(f32[2,32,1024]{2,1,0:T(8,128)S(1)} %get-tuple-element.22), channel_id=1, source_target_pairs={{0,32},{32,0},{64,96},{96,64},{128,160},{160,128},{192,224},{224,1... | collective-permute-start | bytes 786440 | tf_op jit(solution)/shard_map/ppermute | solution.py:213
  99.1 1.3 collective-permute-start.7
  100.4 2.9 %collective-permute-start.9 = (f32[2,32,1024]{2,1,0:T(8,128)S(1)}, f32[2,32,1024]{2,1,0:T(8,128)S(1)}, u32[]{:S(2)}, u32[]{:S(2)}) collective-permute-start(f32[2,32,1024]{2,1,0:T(8,128)S(1)} %get-tuple-element.25), channel_id=1, source_target_pairs={{0,128},{32,160},{64,192},{96,224},{128,0},{160,32},{192,64},{224,... | collective-permute-start | bytes 786440 | tf_op jit(solution)/shard_map/ppermute | solution.py:213
  103.4 2.3 %collective-permute-done.6.refs_1_ = f32[2,32,1024]{2,1,0:T(8,128)S(1)} collective-permute-done((f32[2,32,1024]{2,1,0:T(8,128)S(1)}, f32[2,32,1024]{2,1,0:T(8,128)S(1)}, u32[]{:S(2)}, u32[]{:S(2)}) %collective-permute-start.6) | collective-permute-done | bytes 262176 | tf_op jit(solution)/shard_map/ppermute | solution.py:213
  105.7 7.0 %collective-permute-done.7.refs_2_ = f32[2,32,1024]{2,1,0:T(8,128)S(1)} collective-permute-done((f32[2,32,1024]{2,1,0:T(8,128)S(1)}, f32[2,32,1024]{2,1,0:T(8,128)S(1)}, u32[]{:S(2)}, u32[]{:S(2)}) %collective-permute-start.7) | collective-permute-done | bytes 262176 | tf_op jit(solution)/shard_map/ppermute | solution.py:213
  112.7 3.0 %collective-permute-start.11 = (f32[2,32,1024]{2,1,0:T(8,128)S(1)}, f32[2,32,1024]{2,1,0:T(8,128)S(1)}, u32[]{:S(2)}, u32[]{:S(2)}) collective-permute-start(f32[2,32,1024]{2,1,0:T(8,128)S(1)} %get-tuple-element.27), channel_id=1, source_target_pairs={{0,192},{32,224},{64,128},{96,160},{128,64},{160,96},{192,0},{224,... | collective-permute-start | bytes 786440 | tf_op jit(solution)/shard_map/ppermute | solution.py:213
  115.8 9.6 %collective-permute-done.9.refs_4_ = f32[2,32,1024]{2,1,0:T(8,128)S(1)} collective-permute-done((f32[2,32,1024]{2,1,0:T(8,128)S(1)}, f32[2,32,1024]{2,1,0:T(8,128)S(1)}, u32[]{:S(2)}, u32[]{:S(2)}) %collective-permute-start.9) | collective-permute-done | bytes 262176 | tf_op jit(solution)/shard_map/ppermute | solution.py:213
  125.9 7.5 %collective-permute-done.11.refs_6_ = f32[2,32,1024]{2,1,0:T(8,128)S(1)} collective-permute-done((f32[2,32,1024]{2,1,0:T(8,128)S(1)}, f32[2,32,1024]{2,1,0:T(8,128)S(1)}, u32[]{:S(2)}, u32[]{:S(2)}) %collective-permute-start.11) | collective-permute-done | bytes 262176 | tf_op jit(solution)/shard_map/ppermute | solution.py:213
  133.4 3.8 %collective-permute-done.12.refs_7_ = f32[2,32,1024]{2,1,0:T(8,128)S(1)} collective-permute-done((f32[2,32,1024]{2,1,0:T(8,128)S(1)}, f32[2,32,1024]{2,1,0:T(8,128)S(1)}, u32[]{:S(2)}, u32[]{:S(2)}) %collective-permute-start.12) | collective-permute-done | bytes 262176 | tf_op jit(solution)/shard_map/ppermute | solution.py:213
  137.6 4.7 %collective-permute-done.13.other = f32[32,1024]{1,0:T(8,128)S(1)} collective-permute-done((f32[32,1024]{1,0:T(8,128)S(1)}, f32[32,1024]{1,0:T(8,128)S(1)}, u32[]{:S(2)}, u32[]{:S(2)}) %collective-permute-start.13) | collective-permute-done | bytes 131104 | tf_op jit(solution)/shard_map/ppermute | solution.py:213
  142.6 2.6 %collective-permute-start.19 = (bf16[2,32,1024]{2,1,0:T(8,128)(2,1)S(1)}, bf16[2,32,1024]{2,1,0:T(8,128)(2,1)S(1)}, u32[]{:S(2)}, u32[]{:S(2)}) collective-permute-start(bf16[2,32,1024]{2,1,0:T(8,128)(2,1)S(1)} %shard_map.58.rest_0_), channel_id=1, source_target_pairs={{0,192},{32,224},{64,128},{96,160},{128,64},{160,96},{192,0},{224,... | collective-permute-start | bytes 393224 | tf_op jit(solution)/shard_map/ppermute | solution.py:213
  145.2 1.0 collective-permute-start.18
  146.3 4.4 %collective-permute-start.17 = (bf16[2,32,1024]{2,1,0:T(8,128)(2,1)S(1)}, bf16[2,32,1024]{2,1,0:T(8,128)(2,1)S(1)}, u32[]{:S(2)}, u32[]{:S(2)}) collective-permute-start(bf16[2,32,1024]{2,1,0:T(8,128)(2,1)S(1)} %shard_map.58.rest_0_), channel_id=1, source_target_pairs={{0,128},{32,160},{64,192},{96,224},{128,0},{160,32},{192,64},{224,... | collective-permute-start | bytes 393224 | tf_op jit(solution)/shard_map/ppermute | solution.py:213
  150.7 1.4 collective-permute-start.15
  152.1 3.4 %collective-permute-done.19.rest_6_ = bf16[2,32,1024]{2,1,0:T(8,128)(2,1)S(1)} collective-permute-done((bf16[2,32,1024]{2,1,0:T(8,128)(2,1)S(1)}, bf16[2,32,1024]{2,1,0:T(8,128)(2,1)S(1)}, u32[]{:S(2)}, u32[]{:S(2)}) %collective-permute-start.19) | collective-permute-done | bytes 131104 | tf_op jit(solution)/shard_map/ppermute | solution.py:213
  155.5 2.9 %collective-permute-start.14 = (bf16[2,32,1024]{2,1,0:T(8,128)(2,1)S(1)}, bf16[2,32,1024]{2,1,0:T(8,128)(2,1)S(1)}, u32[]{:S(2)}, u32[]{:S(2)}) collective-permute-start(bf16[2,32,1024]{2,1,0:T(8,128)(2,1)S(1)} %shard_map.58.rest_0_), channel_id=1, source_target_pairs={{0,32},{32,0},{64,96},{96,64},{128,160},{160,128},{192,224},{224,1... | collective-permute-start | bytes 393224 | tf_op jit(solution)/shard_map/ppermute | solution.py:213
  158.4 2.1 %collective-permute-done.17.rest_4_ = bf16[2,32,1024]{2,1,0:T(8,128)(2,1)S(1)} collective-permute-done((bf16[2,32,1024]{2,1,0:T(8,128)(2,1)S(1)}, bf16[2,32,1024]{2,1,0:T(8,128)(2,1)S(1)}, u32[]{:S(2)}, u32[]{:S(2)}) %collective-permute-start.17) | collective-permute-done | bytes 131104 | tf_op jit(solution)/shard_map/ppermute | solution.py:213
  161.1 2.8 %shard_map.59 = bf16[16,96,256]{2,1,0:T(8,128)(2,1)S(1)} custom-call(s32[2]{0:T(128)S(1)} %pad_add_fusion.me_ref, bf16[8,96,512]{2,1,0:T(8,128)(2,1)S(1)} %all-to-all-done.v00, bf16[8,96,512]{2,1,0:T(8,128)(2,1)S(1)} %collective-permute-done.v01, bf16[8,96,512]{2,1,0:T(8,128)(2,1)S(1)} %collective-permute-done.1.v10, ...), custom_call_target="tpu_custom_call" | custom-call | tf_op jit(solution)/shard_map/pallas_call | solution.py:178
  163.9 27.7 %all_to_all.21.m_ref = bf16[16,96,256]{2,1,0:T(8,128)(2,1)S(1)} all-to-all(bf16[16,96,256]{2,1,0:T(8,128)(2,1)S(1)} %shard_map.59), channel_id=1, replica_groups=mesh['y'=4,'xh'=2,'c'=2,'z'=8,'xl'=2] {'z','c'}, dimensions={0} | all-to-all | bytes 1572864 | tf_op jit(solution)/shard_map/all_to_all | solution.py:233
  191.6 1.7 shard_map.60
  (31 shorter events, 2.5 us)
Async XLA Ops:
  0.0 1.3 copy-start
  1.3 1.3 copy-start.1
  2.5 1.1 copy-start.3
  38.7 24.7 %all-to-all-start = ((bf16[8,96,512]{2,1,0:T(8,128)(2,1)}), bf16[8,96,512]{2,1,0:T(8,128)(2,1)S(1)}, u32[]{:S(2)}, u32[]{:S(2)}) async-start(bf16[8,96,512]{2,1,0:T(8,128)(2,1)} %get-tuple-element.18), calls=%async_computation | async-start | bytes 1572864 | tf_op jit(solution)/shard_map/all_to_all | solution.py:228
  42.2 27.7 %collective-permute-start.3 = (bf16[8,96,512]{2,1,0:T(8,128)(2,1)S(1)}, bf16[8,96,512]{2,1,0:T(8,128)(2,1)}, u32[]{:S(2)}, u32[]{:S(2)}) collective-permute-start(bf16[8,96,512]{2,1,0:T(8,128)(2,1)S(1)} %all_to_all.20.k00), channel_id=1, source_target_pairs={{0,1},{1,0},{2,3},{3,2},{4,5},{5,4},{6,7},{7,6},{8,9},{9,8},{10,11... | collective-permute-start | bytes 2359304 | tf_op jit(solution)/shard_map/ppermute | solution.py:213
  63.4 29.0 %all-to-all-start.1 = ((bf16[16,96,256]{2,1,0:T(8,128)(2,1)}), bf16[16,96,256]{2,1,0:T(8,128)(2,1)S(1)}, u32[]{:S(2)}, u32[]{:S(2)}) async-start(bf16[16,96,256]{2,1,0:T(8,128)(2,1)} %get-tuple-element.19), calls=%async_computation.1 | async-start | bytes 1572864 | tf_op jit(solution)/shard_map/all_to_all | solution.py:225
  69.7 22.7 %collective-permute-start.4 = (bf16[8,96,512]{2,1,0:T(8,128)(2,1)S(1)}, bf16[8,96,512]{2,1,0:T(8,128)(2,1)}, u32[]{:S(2)}, u32[]{:S(2)}) collective-permute-start(bf16[8,96,512]{2,1,0:T(8,128)(2,1)S(1)} %all_to_all.20.k00), channel_id=1, source_target_pairs={{0,16},{16,0},{1,17},{17,1},{2,18},{18,2},{3,19},{19,3},{4,20},{20... | collective-permute-start | bytes 2359304 | tf_op jit(solution)/shard_map/ppermute | solution.py:213
  70.0 22.4 %collective-permute-start.5 = (bf16[8,96,512]{2,1,0:T(8,128)(2,1)}, bf16[8,96,512]{2,1,0:T(8,128)(2,1)}, u32[]{:S(2)}, u32[]{:S(2)}) collective-permute-start(bf16[8,96,512]{2,1,0:T(8,128)(2,1)} %collective-permute-done.3.k01), channel_id=1, source_target_pairs={{0,16},{16,0},{1,17},{17,1},{2,18},{18,2},{3,19},{19,3},{4,20},{20... | collective-permute-start | bytes 2359304 | tf_op jit(solution)/shard_map/ppermute | solution.py:213
  70.2 33.2 %collective-permute-start = (bf16[8,96,512]{2,1,0:T(8,128)(2,1)S(1)}, bf16[8,96,512]{2,1,0:T(8,128)(2,1)S(1)}, u32[]{:S(2)}, u32[]{:S(2)}) collective-permute-start(bf16[8,96,512]{2,1,0:T(8,128)(2,1)S(1)} %all-to-all-done.v00), channel_id=1, source_target_pairs={{0,1},{1,0},{2,3},{3,2},{4,5},{5,4},{6,7},{7,6},{8,9},{9,8},{10,11... | collective-permute-start | bytes 2359304 | tf_op jit(solution)/shard_map/ppermute | solution.py:213
  96.2 9.5 %collective-permute-start.6 = (f32[2,32,1024]{2,1,0:T(8,128)S(1)}, f32[2,32,1024]{2,1,0:T(8,128)S(1)}, u32[]{:S(2)}, u32[]{:S(2)}) collective-permute-start(f32[2,32,1024]{2,1,0:T(8,128)S(1)} %get-tuple-element.22), channel_id=1, source_target_pairs={{0,32},{32,0},{64,96},{96,64},{128,160},{160,128},{192,224},{224,1... | collective-permute-start | bytes 786440 | tf_op jit(solution)/shard_map/ppermute | solution.py:213
  99.1 13.7 %collective-permute-start.7 = (f32[2,32,1024]{2,1,0:T(8,128)S(1)}, f32[2,32,1024]{2,1,0:T(8,128)S(1)}, u32[]{:S(2)}, u32[]{:S(2)}) collective-permute-start(f32[2,32,1024]{2,1,0:T(8,128)S(1)} %get-tuple-element.23), channel_id=1, source_target_pairs={{0,64},{32,96},{64,0},{96,32},{128,192},{160,224},{192,128},{224,1... | collective-permute-start | bytes 786440 | tf_op jit(solution)/shard_map/ppermute | solution.py:213
  100.4 12.4 %collective-permute-start.8 = (f32[2,32,1024]{2,1,0:T(8,128)S(1)}, f32[2,32,1024]{2,1,0:T(8,128)S(1)}, u32[]{:S(2)}, u32[]{:S(2)}) collective-permute-start(f32[2,32,1024]{2,1,0:T(8,128)S(1)} %get-tuple-element.24), channel_id=1, source_target_pairs={{0,96},{32,64},{64,32},{96,0},{128,224},{160,192},{192,160},{224,1... | collective-permute-start | bytes 786440 | tf_op jit(solution)/shard_map/ppermute | solution.py:213
  100.4 24.9 %collective-permute-start.9 = (f32[2,32,1024]{2,1,0:T(8,128)S(1)}, f32[2,32,1024]{2,1,0:T(8,128)S(1)}, u32[]{:S(2)}, u32[]{:S(2)}) collective-permute-start(f32[2,32,1024]{2,1,0:T(8,128)S(1)} %get-tuple-element.25), channel_id=1, source_target_pairs={{0,128},{32,160},{64,192},{96,224},{128,0},{160,32},{192,64},{224,... | collective-permute-start | bytes 786440 | tf_op jit(solution)/shard_map/ppermute | solution.py:213
  103.4 42.9 %collective-permute-start.1 = (bf16[8,96,512]{2,1,0:T(8,128)(2,1)S(1)}, bf16[8,96,512]{2,1,0:T(8,128)(2,1)S(1)}, u32[]{:S(2)}, u32[]{:S(2)}) collective-permute-start(bf16[8,96,512]{2,1,0:T(8,128)(2,1)S(1)} %all-to-all-done.v00), channel_id=1, source_target_pairs={{0,16},{16,0},{1,17},{17,1},{2,18},{18,2},{3,19},{19,3},{4,20},{20... | collective-permute-start | bytes 2359304 | tf_op jit(solution)/shard_map/ppermute | solution.py:213
  105.7 45.0 %collective-permute-start.2 = (bf16[8,96,512]{2,1,0:T(8,128)(2,1)S(1)}, bf16[8,96,512]{2,1,0:T(8,128)(2,1)S(1)}, u32[]{:S(2)}, u32[]{:S(2)}) collective-permute-start(bf16[8,96,512]{2,1,0:T(8,128)(2,1)S(1)} %collective-permute-done.v01), channel_id=1, source_target_pairs={{0,16},{16,0},{1,17},{17,1},{2,18},{18,2},{3,19},{19,3},{4,20},{20... | collective-permute-start | bytes 2359304 | tf_op jit(solution)/shard_map/ppermute | solution.py:213
  112.7 13.1 %collective-permute-start.10 = (f32[2,32,1024]{2,1,0:T(8,128)S(1)}, f32[2,32,1024]{2,1,0:T(8,128)S(1)}, u32[]{:S(2)}, u32[]{:S(2)}) collective-permute-start(f32[2,32,1024]{2,1,0:T(8,128)S(1)} %get-tuple-element.26), channel_id=1, source_target_pairs={{0,160},{32,128},{64,224},{96,192},{128,32},{160,0},{192,96},{224,... | collective-permute-start | bytes 786440 | tf_op jit(solution)/shard_map/ppermute | solution.py:213
  112.7 20.7 %collective-permute-start.11 = (f32[2,32,1024]{2,1,0:T(8,128)S(1)}, f32[2,32,1024]{2,1,0:T(8,128)S(1)}, u32[]{:S(2)}, u32[]{:S(2)}) collective-permute-start(f32[2,32,1024]{2,1,0:T(8,128)S(1)} %get-tuple-element.27), channel_id=1, source_target_pairs={{0,192},{32,224},{64,128},{96,160},{128,64},{160,96},{192,0},{224,... | collective-permute-start | bytes 786440 | tf_op jit(solution)/shard_map/ppermute | solution.py:213
  125.4 11.9 %collective-permute-start.12 = (f32[2,32,1024]{2,1,0:T(8,128)S(1)}, f32[2,32,1024]{2,1,0:T(8,128)S(1)}, u32[]{:S(2)}, u32[]{:S(2)}) collective-permute-start(f32[2,32,1024]{2,1,0:T(8,128)S(1)} %get-tuple-element.28), channel_id=1, source_target_pairs={{0,224},{32,192},{64,160},{96,128},{128,96},{160,64},{192,32},{224... | collective-permute-start | bytes 786440 | tf_op jit(solution)/shard_map/ppermute | solution.py:213
  137.4 5.0 %collective-permute-start.13 = (f32[32,1024]{1,0:T(8,128)S(1)}, f32[32,1024]{1,0:T(8,128)S(1)}, u32[]{:S(2)}, u32[]{:S(2)}) collective-permute-start(f32[32,1024]{1,0:T(8,128)S(1)} %get-tuple-element.30.half), channel_id=1, source_target_pairs={{0,2},{2,0},{4,6},{6,4},{8,10},{10,8},{12,14},{14,12},{1,3},{3,1},... | collective-permute-start | bytes 393224 | tf_op jit(solution)/shard_map/ppermute | solution.py:213
  142.5 8.2 %collective-permute-start.20 = (bf16[2,32,1024]{2,1,0:T(8,128)(2,1)S(1)}, bf16[2,32,1024]{2,1,0:T(8,128)(2,1)S(1)}, u32[]{:S(2)}, u32[]{:S(2)}) collective-permute-start(bf16[2,32,1024]{2,1,0:T(8,128)(2,1)S(1)} %shard_map.58.rest_0_), channel_id=1, source_target_pairs={{0,224},{32,192},{64,160},{96,128},{128,96},{160,64},{192,32},{224... | collective-permute-start | bytes 393224 | tf_op jit(solution)/shard_map/ppermute | solution.py:213
  142.6 12.9 %collective-permute-start.19 = (bf16[2,32,1024]{2,1,0:T(8,128)(2,1)S(1)}, bf16[2,32,1024]{2,1,0:T(8,128)(2,1)S(1)}, u32[]{:S(2)}, u32[]{:S(2)}) collective-permute-start(bf16[2,32,1024]{2,1,0:T(8,128)(2,1)S(1)} %shard_map.58.rest_0_), channel_id=1, source_target_pairs={{0,192},{32,224},{64,128},{96,160},{128,64},{160,96},{192,0},{224,... | collective-permute-start | bytes 393224 | tf_op jit(solution)/shard_map/ppermute | solution.py:213
  145.2 13.2 %collective-permute-start.18 = (bf16[2,32,1024]{2,1,0:T(8,128)(2,1)S(1)}, bf16[2,32,1024]{2,1,0:T(8,128)(2,1)S(1)}, u32[]{:S(2)}, u32[]{:S(2)}) collective-permute-start(bf16[2,32,1024]{2,1,0:T(8,128)(2,1)S(1)} %shard_map.58.rest_0_), channel_id=1, source_target_pairs={{0,160},{32,128},{64,224},{96,192},{128,32},{160,0},{192,96},{224,... | collective-permute-start | bytes 393224 | tf_op jit(solution)/shard_map/ppermute | solution.py:213
  146.3 14.2 %collective-permute-start.17 = (bf16[2,32,1024]{2,1,0:T(8,128)(2,1)S(1)}, bf16[2,32,1024]{2,1,0:T(8,128)(2,1)S(1)}, u32[]{:S(2)}, u32[]{:S(2)}) collective-permute-start(bf16[2,32,1024]{2,1,0:T(8,128)(2,1)S(1)} %shard_map.58.rest_0_), channel_id=1, source_target_pairs={{0,128},{32,160},{64,192},{96,224},{128,0},{160,32},{192,64},{224,... | collective-permute-start | bytes 393224 | tf_op jit(solution)/shard_map/ppermute | solution.py:213
  150.7 9.8 %collective-permute-start.16 = (bf16[2,32,1024]{2,1,0:T(8,128)(2,1)S(1)}, bf16[2,32,1024]{2,1,0:T(8,128)(2,1)S(1)}, u32[]{:S(2)}, u32[]{:S(2)}) collective-permute-start(bf16[2,32,1024]{2,1,0:T(8,128)(2,1)S(1)} %shard_map.58.rest_0_), channel_id=1, source_target_pairs={{0,96},{32,64},{64,32},{96,0},{128,224},{160,192},{192,160},{224,1... | collective-permute-start | bytes 393224 | tf_op jit(solution)/shard_map/ppermute | solution.py:213
  150.7 9.8 %collective-permute-start.15 = (bf16[2,32,1024]{2,1,0:T(8,128)(2,1)S(1)}, bf16[2,32,1024]{2,1,0:T(8,128)(2,1)S(1)}, u32[]{:S(2)}, u32[]{:S(2)}) collective-permute-start(bf16[2,32,1024]{2,1,0:T(8,128)(2,1)S(1)} %shard_map.58.rest_0_), channel_id=1, source_target_pairs={{0,64},{32,96},{64,0},{96,32},{128,192},{160,224},{192,128},{224,1... | collective-permute-start | bytes 393224 | tf_op jit(solution)/shard_map/ppermute | solution.py:213
  155.5 5.6 %collective-permute-start.14 = (bf16[2,32,1024]{2,1,0:T(8,128)(2,1)S(1)}, bf16[2,32,1024]{2,1,0:T(8,128)(2,1)S(1)}, u32[]{:S(2)}, u32[]{:S(2)}) collective-permute-start(bf16[2,32,1024]{2,1,0:T(8,128)(2,1)S(1)} %shard_map.58.rest_0_), channel_id=1, source_target_pairs={{0,32},{32,0},{64,96},{96,64},{128,160},{160,128},{192,224},{224,1... | collective-permute-start | bytes 393224 | tf_op jit(solution)/shard_map/ppermute | solution.py:213
  163.9 27.7 %copy-start.2 = (bf16[768,768]{1,0:T(8,128)(2,1)S(1)}, bf16[768,768]{1,0:T(8,128)(2,1)}, u32[]{:S(2)}) copy-start(bf16[768,768]{1,0:T(8,128)(2,1)} %w_ref.1) | copy-start | bytes 3538948

commit v2 on v1

v2 whole, which is shorter than its diff:
```python
import functools
import math

import jax
import jax.numpy as jnp
from jax import lax
from jax.experimental import pallas as pl
from jax.experimental.pallas import tpu as pltpu
from jax.sharding import Mesh, PartitionSpec as P

H = 12
DH = 64
EMBED = 768
ROWS = 8
RES = 64
Z = 8
CHUNK = EMBED // Z
FULL = DH
HALF = CHUNK - DH
PEERS = 8
SUB = RES // 2
QUERIES = Z * SUB
KEYS = 2 * Z * RES

f32 = jnp.float32
bf16 = jnp.bfloat16
PARAMS = pltpu.CompilerParams(vmem_limit_bytes=48 * 1024 * 1024)
PROJECTION = pl.CostEstimate(
    flops=2 * ROWS * RES * EMBED * EMBED, bytes_accessed=2 * EMBED * (EMBED + 2 * ROWS * RES), transcendentals=0
)
VMEM = pl.BlockSpec(memory_space=pltpu.VMEM)
SMEM = pl.BlockSpec(memory_space=pltpu.SMEM)


def chunk_pieces(z):
    base = z * CHUNK
    if z % 2 == 0:
        return (base, FULL), (base + FULL, HALF)
    return (base + HALF, FULL), (base, HALF)


def dot(a, b, ca, cb):
    return lax.dot_general(a, b, (((ca,), (cb,)), ((), ())), preferred_element_type=f32)


def chunk_rows(z):
    odd = lax.rem(z, 2)
    base = z * CHUNK
    return pl.multiple_of(base + odd * HALF, HALF), pl.multiple_of(base + (1 - odd) * FULL, HALF)


def send_pieces(z, t_ref, outs):
    for s, out in enumerate(outs):
        full, half = chunk_rows(lax.rem(z + s, Z))
        out[0:FULL, :] = t_ref[pl.ds(full, FULL), :]
        out[FULL:CHUNK, :] = t_ref[pl.ds(half, HALF), :]


def key_kernel(me_ref, x_ref, w_ref, n_ref, *rest):
    outs, t_ref = rest[:Z], rest[Z]
    x = x_ref[...].astype(f32)
    centred = x - jnp.mean(x, axis=-1, keepdims=True)
    var = jnp.mean(centred * centred, axis=-1, keepdims=True)
    n_ref[...] = (centred * lax.rsqrt(var + 1e-05)).astype(bf16)
    t_ref[...] = dot(w_ref[...], n_ref[...].reshape(ROWS * RES, EMBED), 0, 1).astype(bf16)
    send_pieces(me_ref[2], t_ref, outs)


def key_chunks(me, x, w):
    n, *k = pl.pallas_call(
        key_kernel,
        out_shape=(jax.ShapeDtypeStruct((ROWS, RES, EMBED), bf16),)
        + (jax.ShapeDtypeStruct((CHUNK, ROWS * RES), bf16),) * Z,
        in_specs=[SMEM, VMEM, VMEM],
        out_specs=(VMEM,) * (Z + 1),
        scratch_shapes=[pltpu.VMEM((EMBED, ROWS * RES), bf16)],
        compiler_params=PARAMS,
    )(me, x, w)
    return n, k


def query_kernel(n_ref, w_ref, q_ref):
    for c in range(2):
        n = n_ref[:, c * SUB : (c + 1) * SUB, :].reshape(ROWS * SUB, EMBED)
        t = dot(w_ref[...], n, 0, 1).astype(bf16)
        for z in range(Z):
            (a, na), (b, nb) = chunk_pieces(z)
            q_ref[2 * z + c, 0:FULL, :] = t[a : a + na]
            q_ref[2 * z + c, FULL:CHUNK, :] = t[b : b + nb]


def query_chunks(n, w):
    return pl.pallas_call(
        query_kernel,
        out_shape=jax.ShapeDtypeStruct((2 * Z, CHUNK, ROWS * SUB), bf16),
        in_specs=[VMEM] * 2,
        out_specs=VMEM,
        compiler_params=PARAMS,
        cost_estimate=PROJECTION,
    )(n, w)


def value_kernel(me_ref, n_ref, w_ref, *rest):
    outs, t_ref = rest[:Z], rest[Z]
    t_ref[...] = dot(w_ref[...], n_ref[...].reshape(ROWS * RES, EMBED), 0, 1).astype(bf16)
    send_pieces(me_ref[2], t_ref, outs)


def value_chunks(me, n, w):
    return pl.pallas_call(
        value_kernel,
        out_shape=(jax.ShapeDtypeStruct((CHUNK, ROWS * RES), bf16),) * Z,
        in_specs=[SMEM, VMEM, VMEM],
        out_specs=(VMEM,) * Z,
        scratch_shapes=[pltpu.VMEM((EMBED, ROWS * RES), bf16)],
        compiler_params=PARAMS,
        cost_estimate=PROJECTION,
    )(me, n, w)


def arrived(z, refs):
    return [ref[lax.rem(z - source + Z, Z)] for ref in refs for source in range(Z)]


def widen(blocks, r):
    return jnp.concatenate([b[:, r * RES : (r + 1) * RES] for b in blocks], axis=1)


def score_kernel(me_ref, q_ref, k00, k01, k10, k11, out, qf, qh, kf, kh):
    core, z = me_ref[1], me_ref[2]
    for cr, ks in ((0, (k00, k01)), (1, (k10, k11))):
        c = jnp.bitwise_xor(core, cr)
        queries = [q_ref[2 * p + c] for p in range(PEERS)]
        keys = arrived(z, ks)
        for r in range(ROWS):
            n = cr * ROWS + r
            t = jnp.concatenate([b[:, r * SUB : (r + 1) * SUB] for b in queries], axis=1)
            qf[n * FULL : (n + 1) * FULL, :] = t[:FULL]
            qh[n * HALF : (n + 1) * HALF, :] = t[FULL:]
            t = widen(keys, r)
            kf[n * FULL : (n + 1) * FULL, :] = t[:FULL]
            kh[n * HALF : (n + 1) * HALF, :] = t[FULL:]
    for i, (a, b) in enumerate(((qf, kf), (qh, kh))):
        s = dot(a[...], b[...], 0, 0)
        for p in range(PEERS):
            out[p, i] = s[p * SUB : (p + 1) * SUB]


def score(me, q, ks):
    rows = 2 * ROWS
    return pl.pallas_call(
        score_kernel,
        out_shape=jax.ShapeDtypeStruct((PEERS, 2, SUB, KEYS), f32),
        in_specs=[SMEM] + [VMEM] * 5,
        out_specs=VMEM,
        scratch_shapes=[
            pltpu.VMEM((rows * FULL, QUERIES), bf16),
            pltpu.VMEM((rows * HALF, QUERIES), bf16),
            pltpu.VMEM((rows * FULL, KEYS), bf16),
            pltpu.VMEM((rows * HALF, KEYS), bf16),
        ],
        compiler_params=PARAMS,
    )(me, q, *ks)


def total_kernel(parts, full, half):
    for i, out in enumerate((full, half)):
        t = parts[0, i]
        for p in range(1, PEERS):
            t = t + parts[p, i]
        out[...] = t


def total(parts):
    return pl.pallas_call(
        total_kernel,
        out_shape=(jax.ShapeDtypeStruct((SUB, KEYS), f32),) * 2,
        in_specs=[VMEM],
        out_specs=(VMEM,) * 2,
        compiler_params=PARAMS,
    )(parts)


def softmax_kernel(factor, full, half, other, out):
    for i, logits in enumerate((full[...], half[...] + other[...])):
        logits = logits * factor
        powered = jnp.exp(logits - jnp.max(logits, axis=-1, keepdims=True))
        probs = (powered / jnp.sum(powered, axis=-1, keepdims=True)).astype(bf16)
        for p in range(PEERS):
            out[p, i] = probs


def softmax(factor, full, half, other):
    return pl.pallas_call(
        functools.partial(softmax_kernel, factor),
        out_shape=jax.ShapeDtypeStruct((PEERS, 2, SUB, KEYS), bf16),
        in_specs=[VMEM] * 3,
        out_specs=VMEM,
        compiler_params=PARAMS,
    )(full, half, other)


def mix_kernel(me_ref, v00, v01, v10, v11, p_ref, o_ref, vf, vh):
    core, z = me_ref[1], me_ref[2]
    pf, ph = (p_ref[:, i].reshape(QUERIES, KEYS) for i in range(2))
    for cr, vs in ((0, (v00, v01)), (1, (v10, v11))):
        c = jnp.bitwise_xor(core, cr)
        values = arrived(z, vs)
        for r in range(ROWS):
            t = widen(values, r)
            vf[r * FULL : (r + 1) * FULL, :] = t[:FULL]
            vh[r * HALF : (r + 1) * HALF, :] = t[FULL:]
        for v, p, first, n in ((vf, pf, 0, FULL), (vh, ph, FULL, HALF)):
            mixed = dot(v[...], p, 1, 1).astype(bf16)
            for s in range(PEERS):
                o_ref[2 * s + c, first : first + n, :] = jnp.concatenate(
                    [mixed[r * n : (r + 1) * n, s * SUB : (s + 1) * SUB] for r in range(ROWS)], axis=1
                )


def mix(me, vs, probs):
    return pl.pallas_call(
        mix_kernel,
        out_shape=jax.ShapeDtypeStruct((2 * Z, CHUNK, ROWS * SUB), bf16),
        in_specs=[SMEM] + [VMEM] * 5,
        out_specs=VMEM,
        scratch_shapes=[
            pltpu.VMEM((ROWS * FULL, KEYS), bf16),
            pltpu.VMEM((ROWS * HALF, KEYS), bf16),
        ],
        compiler_params=PARAMS,
    )(me, *vs, probs)


def final_kernel(m_ref, w_ref, o_ref, t_ref):
    for c in range(2):
        for z in range(Z):
            (a, na), (b, nb) = chunk_pieces(z)
            t_ref[a : a + na, :] = m_ref[2 * z + c, 0:FULL, :]
            t_ref[b : b + nb, :] = m_ref[2 * z + c, FULL:CHUNK, :]
        attended = dot(t_ref[...], w_ref[...], 0, 0).astype(bf16)
        o_ref[:, c * SUB : (c + 1) * SUB, :] = attended.reshape(ROWS, SUB, EMBED)


def final(m, w):
    return pl.pallas_call(
        final_kernel,
        out_shape=jax.ShapeDtypeStruct((ROWS, RES, EMBED), bf16),
        in_specs=[VMEM] * 2,
        out_specs=VMEM,
        scratch_shapes=[pltpu.VMEM((EMBED, ROWS * SUB), bf16)],
        compiler_params=PARAMS,
    )(m, w)


def flip(x, axes, n, s):
    return lax.ppermute(x, axes, [(i, i ^ s) for i in range(n)])


def gather4(own):
    far = flip(own, "xl", 2, 1)
    return own, far, flip(own, "c", 2, 1), flip(far, "c", 2, 1)


def spread(pieces):
    got = {0: pieces[0]}
    for s in (1, 7, 2, 6, 3, 5, 4):
        got[s] = lax.ppermute(pieces[s], "z", [(i, (i + s) % Z) for i in range(Z)])
    return jnp.stack([got[s] for s in range(Z)])


def local(x, wq, wk, wv, wf):
    me = jnp.stack([lax.axis_index(("y", "xh")), lax.axis_index("c"), lax.axis_index("z")])
    me = me.astype(jnp.int32)
    n, k = key_chunks(me, x, wk)
    q = query_chunks(n, wq)
    v = value_chunks(me, n, wv)
    ks = gather4(spread(k))
    q = lax.all_to_all(q, ("z", "c"), 0, 0, tiled=True)
    v, scores = lax.optimization_barrier((v, score(me, q, ks)))
    parts = lax.all_to_all(scores, ("y", "xh"), 0, 0, tiled=True)
    vs = gather4(spread(v))
    full, half = total(parts)
    rows = ROWS * 2 * PEERS
    probs = softmax(1.0 / math.sqrt(DH * rows), full, half, flip(half, "z", Z, 1))
    probs = lax.all_to_all(probs, ("y", "xh"), 0, 0, tiled=True)
    mixed = lax.all_to_all(mix(me, vs, probs), ("z", "c"), 0, 0, tiled=True)
    return final(mixed, wf)


def solution(mesh):
    fine = Mesh(mesh.devices.reshape(4, 2, 2, 8, 2), ("y", "xh", "c", "z", "xl"))
    spec = P(("y", "xh", "c"), ("z", "xl"), None)
    return jax.shard_map(
        local,
        mesh=fine,
        in_specs=(spec, P(), P(), P(), P()),
        out_specs=spec,
        check_vma=False,
    )
```

time: 194 us -> 172 us (0.89)
  blocking collectives: 58.1 us -> 30.3 us
  waiting for transfers between devices: 81.8 us -> 61.9 us
  starting transfers between devices: 36.4 us -> 53.7 us
  local copies, waits for them, and re-layouts: 3.68 us -> 8.24 us
  Pallas kernels: 13.2 us -> 16.7 us
    ppermute x0 -> x14, starting transfers between devices: none -> 29.4 us  [spread(): got[s] = lax.ppermute(pieces[s], 'z', [(i, (i + s) % Z) for i in range(Z)])]
    all_to_all x2 -> x1, blocking collectives: 58.1 us -> 30.3 us  [local(): mixed = lax.all_to_all(mix(me, vs, probs), ('z', 'c'), 0, 0, tiled=True)]
    ppermute x0 -> x14, waiting for transfers between devices: none -> 25.6 us  [spread(): got[s] = lax.ppermute(pieces[s], 'z', [(i, (i + s) % Z) for i in range(Z)])]
    ppermute x21 -> x7, waiting for transfers between devices: 41.1 us -> 20.5 us  [flip(): return lax.ppermute(x, axes, [(i, i ^ s) for i in range(n)])]
    ppermute x21 -> x7, starting transfers between devices: 26.6 us -> 8.67 us  [flip(): return lax.ppermute(x, axes, [(i, i ^ s) for i in range(n)])]
    all_to_all x1, waiting for transfers between devices: 20.9 us -> 5.56 us  [local(): q = lax.all_to_all(q, ('z', 'c'), 0, 0, tiled=True)]
    all_to_all x1 -> x2, waiting for transfers between devices: 19.8 us -> 10.3 us  [the longest x1 8.01 us: local(): probs = lax.all_to_all(probs, ('y', 'xh'), 0, 0, tiled=True)]
    all_to_all x1 -> x2, starting transfers between devices: 3.55 us -> 10 us  [the longest x1 6.48 us: local(): parts = lax.all_to_all(scores, ('y', 'xh'), 0, 0, tiled=True)]
  transfers between devices with their start and end apart: 23 -> 24, of which waited for: 11 -> 16; matrix products, arithmetic and copies ran while one was open for 0% -> 0% of each run, Pallas kernels for 2% -> 3%
where the time goes in v2:
time: 172 us; the launch traced here: 171 us
  waiting for transfers between devices  61.9 us (36%)
  starting transfers between devices  53.7 us (31%)
  blocking collectives  30.3 us (18%)
  Pallas kernels  16.7 us (10%)
  local copies, waits for them, and re-layouts  8.24 us (5%)
    all_to_all x1, blocking collectives, local(): mixed = lax.all_to_all(mix(me, vs, probs), ('z', 'c'), 0, 0, tiled=True)  30.3 us
    ppermute x14, starting transfers between devices, spread(): got[s] = lax.ppermute(pieces[s], 'z', [(i, (i + s) % Z) for i in range(Z)])  29.4 us
    ppermute x14, waiting for transfers between devices, spread(): got[s] = lax.ppermute(pieces[s], 'z', [(i, (i + s) % Z) for i in range(Z)])  25.6 us
    ppermute x7, waiting for transfers between devices, flip(): return lax.ppermute(x, axes, [(i, i ^ s) for i in range(n)])  20.5 us
    ppermute x7, starting transfers between devices, flip(): return lax.ppermute(x, axes, [(i, i ^ s) for i in range(n)])  8.67 us
    unnamed x40, local copies, waits for them, and re-layouts  8.23 us
    all_to_all x1, waiting for transfers between devices, local(): probs = lax.all_to_all(probs, ('y', 'xh'), 0, 0, tiled=True)  8.01 us
    all_to_all x1, starting transfers between devices, local(): parts = lax.all_to_all(scores, ('y', 'xh'), 0, 0, tiled=True)  6.48 us
  transfers between devices with their start and end apart: 24, of which 16 were waited for; matrix products, arithmetic and copies ran while one was open for 0% of the time, Pallas kernels for 3%

profile of v2, /device:TPU:1, one launch (start us, length us, event | category | flops | bytes accessed | tf_op | source)
XLA Modules:
  0.0 171.1 jit_solution(17568505725258723461)
XLA Ops:
  2.5 1.8 %shard_map.55 = (bf16[8,64,768]{2,1,0:T(8,128)(2,1)S(1)}, bf16[96,512]{1,0:T(8,128)(2,1)S(1)}, bf16[96,512]{1,0:T(8,128)(2,1)S(1)}, bf16[96,512]{1,0:T(8,128)(2,...) custom-call(s32[3]{0:T(128)S(1)} %pad_add_fusion.me_ref, ...), custom_call_target="tpu_custom_call" | custom-call | tf_op jit(solution)/shard_map/pallas_call | solution.py:70
  4.3 2.5 %collective-permute-start = (bf16[96,512]{1,0:T(8,128)(2,1)S(1)}, bf16[96,512]{1,0:T(8,128)(2,1)S(1)}, u32[]{:S(2)}, u32[]{:S(2)}) collective-permute-start(bf16[96,512]{1,0:T(8,128)(2,1)S(1)} %get-tuple-element.43), channel_id=1, source_target_pairs={{0,2},{2,4},{4,6},{6,8},{8,10},{10,12},{12,14},{14,0},{1,3},{3,5},... | collective-permute-start | bytes 294920 | tf_op jit(solution)/shard_map/ppermute | solution.py:268
  6.9 3.0 %collective-permute-start.1 = (bf16[96,512]{1,0:T(8,128)(2,1)S(1)}, bf16[96,512]{1,0:T(8,128)(2,1)S(1)}, u32[]{:S(2)}, u32[]{:S(2)}) collective-permute-start(bf16[96,512]{1,0:T(8,128)(2,1)S(1)} %get-tuple-element.44), channel_id=1, source_target_pairs={{0,4},{2,6},{4,8},{6,10},{8,12},{10,14},{12,0},{14,2},{1,5},{3,7},... | collective-permute-start | bytes 294920 | tf_op jit(solution)/shard_map/ppermute | solution.py:268
  9.9 3.8 %collective-permute-start.2 = (bf16[96,512]{1,0:T(8,128)(2,1)S(1)}, bf16[96,512]{1,0:T(8,128)(2,1)S(1)}, u32[]{:S(2)}, u32[]{:S(2)}) collective-permute-start(bf16[96,512]{1,0:T(8,128)(2,1)S(1)} %get-tuple-element.45), channel_id=1, source_target_pairs={{0,6},{2,8},{4,10},{6,12},{8,14},{10,0},{12,2},{14,4},{1,7},{3,9},... | collective-permute-start | bytes 294920 | tf_op jit(solution)/shard_map/ppermute | solution.py:268
  14.1 4.5 %collective-permute-start.4 = (bf16[96,512]{1,0:T(8,128)(2,1)S(1)}, bf16[96,512]{1,0:T(8,128)(2,1)S(1)}, u32[]{:S(2)}, u32[]{:S(2)}) collective-permute-start(bf16[96,512]{1,0:T(8,128)(2,1)S(1)} %get-tuple-element.47), channel_id=1, source_target_pairs={{0,10},{2,12},{4,14},{6,0},{8,2},{10,4},{12,6},{14,8},{1,11},{3,13... | collective-permute-start | bytes 294920 | tf_op jit(solution)/shard_map/ppermute | solution.py:268
  18.6 2.5 %collective-permute-start.5 = (bf16[96,512]{1,0:T(8,128)(2,1)S(1)}, bf16[96,512]{1,0:T(8,128)(2,1)S(1)}, u32[]{:S(2)}, u32[]{:S(2)}) collective-permute-start(bf16[96,512]{1,0:T(8,128)(2,1)S(1)} %get-tuple-element.48), channel_id=1, source_target_pairs={{0,12},{2,14},{4,0},{6,2},{8,4},{10,6},{12,8},{14,10},{1,13},{3,15... | collective-permute-start | bytes 294920 | tf_op jit(solution)/shard_map/ppermute | solution.py:268
  21.9 1.8 %collective-permute-done.2 = bf16[96,512]{1,0:T(8,128)(2,1)S(1)} collective-permute-done((bf16[96,512]{1,0:T(8,128)(2,1)S(1)}, bf16[96,512]{1,0:T(8,128)(2,1)S(1)}, u32[]{:S(2)}, u32[]{:S(2)}) %collective-permute-start.2) | collective-permute-done | bytes 98336 | tf_op jit(solution)/shard_map/ppermute | solution.py:268
  23.7 2.2 %collective-permute-done.3 = bf16[96,512]{1,0:T(8,128)(2,1)S(1)} collective-permute-done((bf16[96,512]{1,0:T(8,128)(2,1)S(1)}, bf16[96,512]{1,0:T(8,128)(2,1)S(1)}, u32[]{:S(2)}, u32[]{:S(2)}) %collective-permute-start.3) | collective-permute-done | bytes 98336 | tf_op jit(solution)/shard_map/ppermute | solution.py:268
  26.9 6.6 %collective-permute-done.5 = bf16[96,512]{1,0:T(8,128)(2,1)S(1)} collective-permute-done((bf16[96,512]{1,0:T(8,128)(2,1)S(1)}, bf16[96,512]{1,0:T(8,128)(2,1)S(1)}, u32[]{:S(2)}, u32[]{:S(2)}) %collective-permute-start.5) | collective-permute-done | bytes 98336 | tf_op jit(solution)/shard_map/ppermute | solution.py:268
  35.6 1.7 %shard_map.57 = bf16[16,96,256]{2,1,0:T(8,128)(2,1)} custom-call(bf16[8,64,768]{2,1,0:T(8,128)(2,1)S(1)} %get-tuple-element.33.n_ref, bf16[768,768]{1,0:T(8,128)(2,1)S(1)} %copy-done.1), custom_call_target="tpu_custom_call" | custom-call | flops 603979776 | bytes 2752512 | tf_op jit(solution)/shard_map/pallas_call | solution.py:93
  37.3 5.6 %all-to-all-start = ((bf16[16,96,256]{2,1,0:T(8,128)(2,1)}), bf16[16,96,256]{2,1,0:T(8,128)(2,1)S(1)}, u32[]{:S(2)}, u32[]{:S(2)}) async-start(bf16[16,96,256]{2,1,0:T(8,128)(2,1)} %shard_map.57), calls=%async_computation | async-start | bytes 1572864 | tf_op jit(solution)/shard_map/all_to_all | solution.py:279
  43.1 9.6 %collective-permute-done.7.k01 = bf16[8,96,512]{2,1,0:T(8,128)(2,1)S(1)} collective-permute-done((bf16[8,96,512]{2,1,0:T(8,128)(2,1)S(1)}, bf16[8,96,512]{2,1,0:T(8,128)(2,1)S(1)}, u32[]{:S(2)}, u32[]{:S(2)}) %collective-permute-start.7) | collective-permute-done | bytes 786464 | tf_op jit(solution)/shard_map/ppermute | solution.py:257
  56.7 2.1 %shard_map.56 = (bf16[96,512]{1,0:T(8,128)(2,1)S(1)}, bf16[96,512]{1,0:T(8,128)(2,1)}, bf16[96,512]{1,0:T(8,128)(2,1)}, bf16[96,512]{1,0:T(8,128)(2,1)S(1)}, bf1...) custom-call(s32[3]{0:T(128)S(1)} %pad_add_fusion.me_ref, ...), custom_call_target="tpu_custom_call" | custom-call | flops 603979776 | bytes 2752512 | tf_op jit(solution)/shard_map/pallas_call | solution.py:110
  60.1 5.6 %all-to-all-done.q_ref = bf16[16,96,256]{2,1,0:T(8,128)(2,1)S(1)} async-done(((bf16[16,96,256]{2,1,0:T(8,128)(2,1)}), bf16[16,96,256]{2,1,0:T(8,128)(2,1)S(1)}, u32[]{:S(2)}, u32[]{:S(2)}) %all-to-all-start) | async-done | bytes 786464 | tf_op jit(solution)/shard_map/all_to_all | solution.py:279
  65.6 4.7 %shard_map.58 = f32[8,2,32,1024]{3,2,1,0:T(8,128)} custom-call(s32[3]{0:T(128)S(1)} %pad_add_fusion.me_ref, bf16[16,96,256]{2,1,0:T(8,128)(2,1)S(1)} %all-to-all-done.q_ref, bf16[8,96,512]{2,1,0:T(8,128)(2,1)S(1)} %bitcast_dynamic-update-slice_fusion.8.k00, bf16[8,96,512]{2,1,0:T(8,128)(2,1)S(1)} %collective-permute-done.7.k01, ...), custom_call_target="tpu_custom_call" | custom-call | tf_op jit(solution)/shard_map/pallas_call | solution.py:151
  70.3 6.5 %all-to-all-start.1 = ((f32[8,2,32,1024]{3,2,1,0:T(8,128)}), f32[8,2,32,1024]{3,2,1,0:T(8,128)S(1)}, u32[]{:S(2)}, u32[]{:S(2)}) async-start(f32[8,2,32,1024]{3,2,1,0:T(8,128)} %shard_map.58), calls=%async_computation.1 | async-start | bytes 4194304 | tf_op jit(solution)/shard_map/all_to_all | solution.py:281
  79.5 3.1 %collective-permute-start.13 = (bf16[96,512]{1,0:T(8,128)(2,1)S(1)}, bf16[96,512]{1,0:T(8,128)(2,1)S(1)}, u32[]{:S(2)}, u32[]{:S(2)}) collective-permute-start(bf16[96,512]{1,0:T(8,128)(2,1)S(1)} %copy-done.10), channel_id=1, source_target_pairs={{0,8},{2,10},{4,12},{6,14},{8,0},{10,2},{12,4},{14,6},{1,9},{3,11}... | collective-permute-start | bytes 294920 | tf_op jit(solution)/shard_map/ppermute | solution.py:268
  85.3 1.6 collective-permute-start.15
  87.0 3.3 %collective-permute-start.16 = (bf16[96,512]{1,0:T(8,128)(2,1)S(1)}, bf16[96,512]{1,0:T(8,128)(2,1)S(1)}, u32[]{:S(2)}, u32[]{:S(2)}) collective-permute-start(bf16[96,512]{1,0:T(8,128)(2,1)S(1)} %get-tuple-element.57), channel_id=1, source_target_pairs={{0,14},{2,0},{4,2},{6,4},{8,6},{10,8},{12,10},{14,12},{1,15},{3,1}... | collective-permute-start | bytes 294920 | tf_op jit(solution)/shard_map/ppermute | solution.py:268
  90.3 4.2 %collective-permute-done.12 = bf16[96,512]{1,0:T(8,128)(2,1)S(1)} collective-permute-done((bf16[96,512]{1,0:T(8,128)(2,1)S(1)}, bf16[96,512]{1,0:T(8,128)(2,1)S(1)}, u32[]{:S(2)}, u32[]{:S(2)}) %collective-permute-start.12) | collective-permute-done | bytes 98336 | tf_op jit(solution)/shard_map/ppermute | solution.py:268
  94.5 5.8 %collective-permute-done.15 = bf16[96,512]{1,0:T(8,128)(2,1)S(1)} collective-permute-done((bf16[96,512]{1,0:T(8,128)(2,1)S(1)}, bf16[96,512]{1,0:T(8,128)(2,1)S(1)}, u32[]{:S(2)}, u32[]{:S(2)}) %collective-permute-start.15) | collective-permute-done | bytes 98336 | tf_op jit(solution)/shard_map/ppermute | solution.py:268
  102.1 2.3 %all-to-all-done.1.parts = f32[8,2,32,1024]{3,2,1,0:T(8,128)S(1)} async-done(((f32[8,2,32,1024]{3,2,1,0:T(8,128)}), f32[8,2,32,1024]{3,2,1,0:T(8,128)S(1)}, u32[]{:S(2)}, u32[]{:S(2)}) %all-to-all-start.1) | async-done | bytes 2097184 | tf_op jit(solution)/shard_map/all_to_all | solution.py:281
  104.6 5.6 %collective-permute-done.20.other = f32[32,1024]{1,0:T(8,128)S(1)} collective-permute-done((f32[32,1024]{1,0:T(8,128)S(1)}, f32[32,1024]{1,0:T(8,128)S(1)}, u32[]{:S(2)}, u32[]{:S(2)}) %collective-permute-start.20) | collective-permute-done | bytes 131104 | tf_op jit(solution)/shard_map/ppermute | solution.py:257
  111.5 3.6 %all-to-all-start.2 = ((bf16[8,2,32,1024]{3,2,1,0:T(8,128)(2,1)}), bf16[8,2,32,1024]{3,2,1,0:T(8,128)(2,1)S(1)}, u32[]{:S(2)}, u32[]{:S(2)}) async-start(bf16[8,2,32,1024]{3,2,1,0:T(8,128)(2,1)} %shard_map.60), calls=%async_computation.2 | async-start | bytes 2097152 | tf_op jit(solution)/shard_map/all_to_all | solution.py:286
  115.0 2.2 %collective-permute-start.18 = (bf16[8,96,512]{2,1,0:T(8,128)(2,1)S(1)}, bf16[8,96,512]{2,1,0:T(8,128)(2,1)S(1)}, u32[]{:S(2)}, u32[]{:S(2)}) collective-permute-start(bf16[8,96,512]{2,1,0:T(8,128)(2,1)S(1)} %bitcast_dynamic-update-slice_fusion.v00), channel_id=1, source_target_pairs={{0,16},{16,0},{1,17},{17,1},{2,18},{18,2},{3,19},{19,3},{4,20},{20... | collective-permute-start | bytes 2359304 | tf_op jit(solution)/shard_map/ppermute | solution.py:257
  117.2 3.1 %collective-permute-done.17.v01 = bf16[8,96,512]{2,1,0:T(8,128)(2,1)} collective-permute-done((bf16[8,96,512]{2,1,0:T(8,128)(2,1)S(1)}, bf16[8,96,512]{2,1,0:T(8,128)(2,1)}, u32[]{:S(2)}, u32[]{:S(2)}) %collective-permute-start.17) | collective-permute-done | bytes 786464 | tf_op jit(solution)/shard_map/ppermute | solution.py:257
  120.3 3.3 %collective-permute-start.19 = (bf16[8,96,512]{2,1,0:T(8,128)(2,1)}, bf16[8,96,512]{2,1,0:T(8,128)(2,1)S(1)}, u32[]{:S(2)}, u32[]{:S(2)}) collective-permute-start(bf16[8,96,512]{2,1,0:T(8,128)(2,1)} %collective-permute-done.17.v01), channel_id=1, source_target_pairs={{0,16},{16,0},{1,17},{17,1},{2,18},{18,2},{3,19},{19,3},{4,20},{20... | collective-permute-start | bytes 2359304 | tf_op jit(solution)/shard_map/ppermute | solution.py:257
  123.6 2.1 %collective-permute-done.19.v11 = bf16[8,96,512]{2,1,0:T(8,128)(2,1)S(1)} collective-permute-done((bf16[8,96,512]{2,1,0:T(8,128)(2,1)}, bf16[8,96,512]{2,1,0:T(8,128)(2,1)S(1)}, u32[]{:S(2)}, u32[]{:S(2)}) %collective-permute-start.19) | collective-permute-done | bytes 786464 | tf_op jit(solution)/shard_map/ppermute | solution.py:257
  126.6 8.0 %all-to-all-done.2.p_ref = bf16[8,2,32,1024]{3,2,1,0:T(8,128)(2,1)S(1)} async-done(((bf16[8,2,32,1024]{3,2,1,0:T(8,128)(2,1)}), bf16[8,2,32,1024]{3,2,1,0:T(8,128)(2,1)S(1)}, u32[]{:S(2)}, u32[]{:S(2)}) %all-to-all-start.2) | async-done | bytes 1048608 | tf_op jit(solution)/shard_map/all_to_all | solution.py:286
  135.8 3.4 %shard_map.61 = bf16[16,96,256]{2,1,0:T(8,128)(2,1)S(1)} custom-call(s32[3]{0:T(128)S(1)} %pad_add_fusion.me_ref, bf16[8,96,512]{2,1,0:T(8,128)(2,1)S(1)} %bitcast_dynamic-update-slice_fusion.v00, bf16[8,96,512]{2,1,0:T(8,128)(2,1)} %collective-permute-done.17.v01, bf16[8,96,512]{2,1,0:T(8,128)(2,1)S(1)} %collective-permute-done.18.v10, ...), custom_call_target="tpu_custom_call" | custom-call | tf_op jit(solution)/shard_map/pallas_call | solution.py:222
  139.1 30.3 %all_to_all.20.m_ref = bf16[16,96,256]{2,1,0:T(8,128)(2,1)S(1)} all-to-all(bf16[16,96,256]{2,1,0:T(8,128)(2,1)S(1)} %shard_map.61), channel_id=1, replica_groups=mesh['y'=4,'xh'=2,'c'=2,'z'=8,'xl'=2] {'z','c'}, dimensions={0} | all-to-all | bytes 1572864 | tf_op jit(solution)/shard_map/all_to_all | solution.py:287
  169.4 1.7 shard_map.62
  (68 shorter events, 22.8 us)
Async XLA Ops:
  0.1 1.3 copy-start
  4.3 31.3 %copy-start.6 = (bf16[8,64,768]{2,1,0:T(8,128)(2,1)}, bf16[8,64,768]{2,1,0:T(8,128)(2,1)S(1)}, u32[]{:S(2)}) copy-start(bf16[8,64,768]{2,1,0:T(8,128)(2,1)S(1)} %get-tuple-element.33.n_ref) | copy-start | bytes 2359300
  4.3 31.3 %copy-start.1 = (bf16[768,768]{1,0:T(8,128)(2,1)S(1)}, bf16[768,768]{1,0:T(8,128)(2,1)}, u32[]{:S(2)}) copy-start(bf16[768,768]{1,0:T(8,128)(2,1)} %w_ref.6) | copy-start | bytes 3538948
  4.3 14.2 %collective-permute-start = (bf16[96,512]{1,0:T(8,128)(2,1)S(1)}, bf16[96,512]{1,0:T(8,128)(2,1)S(1)}, u32[]{:S(2)}, u32[]{:S(2)}) collective-permute-start(bf16[96,512]{1,0:T(8,128)(2,1)S(1)} %get-tuple-element.43), channel_id=1, source_target_pairs={{0,2},{2,4},{4,6},{6,8},{8,10},{10,12},{12,14},{14,0},{1,3},{3,5},... | collective-permute-start | bytes 294920 | tf_op jit(solution)/shard_map/ppermute | solution.py:268
  6.9 14.2 %collective-permute-start.1 = (bf16[96,512]{1,0:T(8,128)(2,1)S(1)}, bf16[96,512]{1,0:T(8,128)(2,1)S(1)}, u32[]{:S(2)}, u32[]{:S(2)}) collective-permute-start(bf16[96,512]{1,0:T(8,128)(2,1)S(1)} %get-tuple-element.44), channel_id=1, source_target_pairs={{0,4},{2,6},{4,8},{6,10},{8,12},{10,14},{12,0},{14,2},{1,5},{3,7},... | collective-permute-start | bytes 294920 | tf_op jit(solution)/shard_map/ppermute | solution.py:268
  9.9 13.8 %collective-permute-start.2 = (bf16[96,512]{1,0:T(8,128)(2,1)S(1)}, bf16[96,512]{1,0:T(8,128)(2,1)S(1)}, u32[]{:S(2)}, u32[]{:S(2)}) collective-permute-start(bf16[96,512]{1,0:T(8,128)(2,1)S(1)} %get-tuple-element.45), channel_id=1, source_target_pairs={{0,6},{2,8},{4,10},{6,12},{8,14},{10,0},{12,2},{14,4},{1,7},{3,9},... | collective-permute-start | bytes 294920 | tf_op jit(solution)/shard_map/ppermute | solution.py:268
  13.6 12.3 %collective-permute-start.3 = (bf16[96,512]{1,0:T(8,128)(2,1)S(1)}, bf16[96,512]{1,0:T(8,128)(2,1)S(1)}, u32[]{:S(2)}, u32[]{:S(2)}) collective-permute-start(bf16[96,512]{1,0:T(8,128)(2,1)S(1)} %get-tuple-element.46), channel_id=1, source_target_pairs={{0,8},{2,10},{4,12},{6,14},{8,0},{10,2},{12,4},{14,6},{1,9},{3,11}... | collective-permute-start | bytes 294920 | tf_op jit(solution)/shard_map/ppermute | solution.py:268
  14.1 12.8 %collective-permute-start.4 = (bf16[96,512]{1,0:T(8,128)(2,1)S(1)}, bf16[96,512]{1,0:T(8,128)(2,1)S(1)}, u32[]{:S(2)}, u32[]{:S(2)}) collective-permute-start(bf16[96,512]{1,0:T(8,128)(2,1)S(1)} %get-tuple-element.47), channel_id=1, source_target_pairs={{0,10},{2,12},{4,14},{6,0},{8,2},{10,4},{12,6},{14,8},{1,11},{3,13... | collective-permute-start | bytes 294920 | tf_op jit(solution)/shard_map/ppermute | solution.py:268
  18.6 14.9 %collective-permute-start.5 = (bf16[96,512]{1,0:T(8,128)(2,1)S(1)}, bf16[96,512]{1,0:T(8,128)(2,1)S(1)}, u32[]{:S(2)}, u32[]{:S(2)}) collective-permute-start(bf16[96,512]{1,0:T(8,128)(2,1)S(1)} %get-tuple-element.48), channel_id=1, source_target_pairs={{0,12},{2,14},{4,0},{6,2},{8,4},{10,6},{12,8},{14,10},{1,13},{3,15... | collective-permute-start | bytes 294920 | tf_op jit(solution)/shard_map/ppermute | solution.py:268
  21.0 13.2 %collective-permute-start.6 = (bf16[96,512]{1,0:T(8,128)(2,1)S(1)}, bf16[96,512]{1,0:T(8,128)(2,1)S(1)}, u32[]{:S(2)}, u32[]{:S(2)}) collective-permute-start(bf16[96,512]{1,0:T(8,128)(2,1)S(1)} %get-tuple-element.49), channel_id=1, source_target_pairs={{0,14},{2,0},{4,2},{6,4},{8,6},{10,8},{12,10},{14,12},{1,15},{3,1}... | collective-permute-start | bytes 294920 | tf_op jit(solution)/shard_map/ppermute | solution.py:268
  34.3 18.5 %collective-permute-start.7 = (bf16[8,96,512]{2,1,0:T(8,128)(2,1)S(1)}, bf16[8,96,512]{2,1,0:T(8,128)(2,1)S(1)}, u32[]{:S(2)}, u32[]{:S(2)}) collective-permute-start(bf16[8,96,512]{2,1,0:T(8,128)(2,1)S(1)} %bitcast_dynamic-update-slice_fusion.8.k00), channel_id=1, source_target_pairs={{0,1},{1,0},{2,3},{3,2},{4,5},{5,4},{6,7},{7,6},{8,9},{9,8},{10,11... | collective-permute-start | bytes 2359304 | tf_op jit(solution)/shard_map/ppermute | solution.py:257
  37.3 28.3 %all-to-all-start = ((bf16[16,96,256]{2,1,0:T(8,128)(2,1)}), bf16[16,96,256]{2,1,0:T(8,128)(2,1)S(1)}, u32[]{:S(2)}, u32[]{:S(2)}) async-start(bf16[16,96,256]{2,1,0:T(8,128)(2,1)} %shard_map.57), calls=%async_computation | async-start | bytes 1572864 | tf_op jit(solution)/shard_map/all_to_all | solution.py:279
  43.0 17.1 %collective-permute-start.8 = (bf16[8,96,512]{2,1,0:T(8,128)(2,1)S(1)}, bf16[8,96,512]{2,1,0:T(8,128)(2,1)S(1)}, u32[]{:S(2)}, u32[]{:S(2)}) collective-permute-start(bf16[8,96,512]{2,1,0:T(8,128)(2,1)S(1)} %bitcast_dynamic-update-slice_fusion.8.k00), channel_id=1, source_target_pairs={{0,16},{16,0},{1,17},{17,1},{2,18},{18,2},{3,19},{19,3},{4,20},{20... | collective-permute-start | bytes 2359304 | tf_op jit(solution)/shard_map/ppermute | solution.py:257
  52.7 12.9 %collective-permute-start.9 = (bf16[8,96,512]{2,1,0:T(8,128)(2,1)S(1)}, bf16[8,96,512]{2,1,0:T(8,128)(2,1)}, u32[]{:S(2)}, u32[]{:S(2)}) collective-permute-start(bf16[8,96,512]{2,1,0:T(8,128)(2,1)S(1)} %collective-permute-done.7.k01), channel_id=1, source_target_pairs={{0,16},{16,0},{1,17},{17,1},{2,18},{18,2},{3,19},{19,3},{4,20},{20... | collective-permute-start | bytes 2359304 | tf_op jit(solution)/shard_map/ppermute | solution.py:257
  55.4 1.3 copy-start.8
  70.3 7.9 %copy-start.12 = (bf16[96,512]{1,0:T(8,128)(2,1)S(1)}, bf16[96,512]{1,0:T(8,128)(2,1)}, u32[]{:S(2)}) copy-start(bf16[96,512]{1,0:T(8,128)(2,1)} %copy-done.11) | copy-start | bytes 294916
  70.3 9.1 %copy-start.10 = (bf16[96,512]{1,0:T(8,128)(2,1)S(1)}, bf16[96,512]{1,0:T(8,128)(2,1)}, u32[]{:S(2)}) copy-start(bf16[96,512]{1,0:T(8,128)(2,1)} %copy-done.9) | copy-start | bytes 294916
  70.3 34.1 %all-to-all-start.1 = ((f32[8,2,32,1024]{3,2,1,0:T(8,128)}), f32[8,2,32,1024]{3,2,1,0:T(8,128)S(1)}, u32[]{:S(2)}, u32[]{:S(2)}) async-start(f32[8,2,32,1024]{3,2,1,0:T(8,128)} %shard_map.58), calls=%async_computation.1 | async-start | bytes 4194304 | tf_op jit(solution)/shard_map/all_to_all | solution.py:281
  76.8 8.5 %collective-permute-start.10 = (bf16[96,512]{1,0:T(8,128)(2,1)}, bf16[96,512]{1,0:T(8,128)(2,1)S(1)}, u32[]{:S(2)}, u32[]{:S(2)}) collective-permute-start(bf16[96,512]{1,0:T(8,128)(2,1)} %get-tuple-element.51), channel_id=1, source_target_pairs={{0,2},{2,4},{4,6},{6,8},{8,10},{10,12},{12,14},{14,0},{1,3},{3,5},... | collective-permute-start | bytes 294920 | tf_op jit(solution)/shard_map/ppermute | solution.py:268
  76.8 10.1 %collective-permute-start.11 = (bf16[96,512]{1,0:T(8,128)(2,1)}, bf16[96,512]{1,0:T(8,128)(2,1)S(1)}, u32[]{:S(2)}, u32[]{:S(2)}) collective-permute-start(bf16[96,512]{1,0:T(8,128)(2,1)} %get-tuple-element.52), channel_id=1, source_target_pairs={{0,4},{2,6},{4,8},{6,10},{8,12},{10,14},{12,0},{14,2},{1,5},{3,7},... | collective-permute-start | bytes 294920 | tf_op jit(solution)/shard_map/ppermute | solution.py:268
  78.2 16.3 %collective-permute-start.12 = (bf16[96,512]{1,0:T(8,128)(2,1)S(1)}, bf16[96,512]{1,0:T(8,128)(2,1)S(1)}, u32[]{:S(2)}, u32[]{:S(2)}) collective-permute-start(bf16[96,512]{1,0:T(8,128)(2,1)S(1)} %copy-done.12), channel_id=1, source_target_pairs={{0,6},{2,8},{4,10},{6,12},{8,14},{10,0},{12,2},{14,4},{1,7},{3,9},... | collective-permute-start | bytes 294920 | tf_op jit(solution)/shard_map/ppermute | solution.py:268
  79.5 15.0 %collective-permute-start.13 = (bf16[96,512]{1,0:T(8,128)(2,1)S(1)}, bf16[96,512]{1,0:T(8,128)(2,1)S(1)}, u32[]{:S(2)}, u32[]{:S(2)}) collective-permute-start(bf16[96,512]{1,0:T(8,128)(2,1)S(1)} %copy-done.10), channel_id=1, source_target_pairs={{0,8},{2,10},{4,12},{6,14},{8,0},{10,2},{12,4},{14,6},{1,9},{3,11}... | collective-permute-start | bytes 294920 | tf_op jit(solution)/shard_map/ppermute | solution.py:268
  82.6 11.9 %collective-permute-start.14 = (bf16[96,512]{1,0:T(8,128)(2,1)S(1)}, bf16[96,512]{1,0:T(8,128)(2,1)S(1)}, u32[]{:S(2)}, u32[]{:S(2)}) collective-permute-start(bf16[96,512]{1,0:T(8,128)(2,1)S(1)} %get-tuple-element.55), channel_id=1, source_target_pairs={{0,10},{2,12},{4,14},{6,0},{8,2},{10,4},{12,6},{14,8},{1,11},{3,13... | collective-permute-start | bytes 294920 | tf_op jit(solution)/shard_map/ppermute | solution.py:268
  85.3 15.1 %collective-permute-start.15 = (bf16[96,512]{1,0:T(8,128)(2,1)S(1)}, bf16[96,512]{1,0:T(8,128)(2,1)S(1)}, u32[]{:S(2)}, u32[]{:S(2)}) collective-permute-start(bf16[96,512]{1,0:T(8,128)(2,1)S(1)} %get-tuple-element.56), channel_id=1, source_target_pairs={{0,12},{2,14},{4,0},{6,2},{8,4},{10,6},{12,8},{14,10},{1,13},{3,15... | collective-permute-start | bytes 294920 | tf_op jit(solution)/shard_map/ppermute | solution.py:268
  87.0 15.1 %collective-permute-start.16 = (bf16[96,512]{1,0:T(8,128)(2,1)S(1)}, bf16[96,512]{1,0:T(8,128)(2,1)S(1)}, u32[]{:S(2)}, u32[]{:S(2)}) collective-permute-start(bf16[96,512]{1,0:T(8,128)(2,1)S(1)} %get-tuple-element.57), channel_id=1, source_target_pairs={{0,14},{2,0},{4,2},{6,4},{8,6},{10,8},{12,10},{14,12},{1,15},{3,1}... | collective-permute-start | bytes 294920 | tf_op jit(solution)/shard_map/ppermute | solution.py:268
  102.0 18.3 %collective-permute-start.17 = (bf16[8,96,512]{2,1,0:T(8,128)(2,1)S(1)}, bf16[8,96,512]{2,1,0:T(8,128)(2,1)}, u32[]{:S(2)}, u32[]{:S(2)}) collective-permute-start(bf16[8,96,512]{2,1,0:T(8,128)(2,1)S(1)} %bitcast_dynamic-update-slice_fusion.v00), channel_id=1, source_target_pairs={{0,1},{1,0},{2,3},{3,2},{4,5},{5,4},{6,7},{7,6},{8,9},{9,8},{10,11... | collective-permute-start | bytes 2359304 | tf_op jit(solution)/shard_map/ppermute | solution.py:257
  104.5 5.7 %collective-permute-start.20 = (f32[32,1024]{1,0:T(8,128)S(1)}, f32[32,1024]{1,0:T(8,128)S(1)}, u32[]{:S(2)}, u32[]{:S(2)}) collective-permute-start(f32[32,1024]{1,0:T(8,128)S(1)} %get-tuple-element.60.half), channel_id=1, source_target_pairs={{0,2},{2,0},{4,6},{6,4},{8,10},{10,8},{12,14},{14,12},{1,3},{3,1},... | collective-permute-start | bytes 393224 | tf_op jit(solution)/shard_map/ppermute | solution.py:257
  111.5 23.1 %all-to-all-start.2 = ((bf16[8,2,32,1024]{3,2,1,0:T(8,128)(2,1)}), bf16[8,2,32,1024]{3,2,1,0:T(8,128)(2,1)S(1)}, u32[]{:S(2)}, u32[]{:S(2)}) async-start(bf16[8,2,32,1024]{3,2,1,0:T(8,128)(2,1)} %shard_map.60), calls=%async_computation.2 | async-start | bytes 2097152 | tf_op jit(solution)/shard_map/all_to_all | solution.py:286
  115.0 8.6 %collective-permute-start.18 = (bf16[8,96,512]{2,1,0:T(8,128)(2,1)S(1)}, bf16[8,96,512]{2,1,0:T(8,128)(2,1)S(1)}, u32[]{:S(2)}, u32[]{:S(2)}) collective-permute-start(bf16[8,96,512]{2,1,0:T(8,128)(2,1)S(1)} %bitcast_dynamic-update-slice_fusion.v00), channel_id=1, source_target_pairs={{0,16},{16,0},{1,17},{17,1},{2,18},{18,2},{3,19},{19,3},{4,20},{20... | collective-permute-start | bytes 2359304 | tf_op jit(solution)/shard_map/ppermute | solution.py:257
  120.3 5.4 %collective-permute-start.19 = (bf16[8,96,512]{2,1,0:T(8,128)(2,1)}, bf16[8,96,512]{2,1,0:T(8,128)(2,1)S(1)}, u32[]{:S(2)}, u32[]{:S(2)}) collective-permute-start(bf16[8,96,512]{2,1,0:T(8,128)(2,1)} %collective-permute-done.17.v01), channel_id=1, source_target_pairs={{0,16},{16,0},{1,17},{17,1},{2,18},{18,2},{3,19},{19,3},{4,20},{20... | collective-permute-start | bytes 2359304 | tf_op jit(solution)/shard_map/ppermute | solution.py:257
  134.6 1.1 copy-start.4
  139.1 30.3 %copy-start.2 = (bf16[768,768]{1,0:T(8,128)(2,1)S(1)}, bf16[768,768]{1,0:T(8,128)(2,1)}, u32[]{:S(2)}) copy-start(bf16[768,768]{1,0:T(8,128)(2,1)} %w_ref.7) | copy-start | bytes 3538948
  (5 other events, 4.4 us)

commit v3 on v2

--- a/solution.py
+++ b/solution.py
@@ -19,15 +19,18 @@
 HALF = CHUNK - DH
 PEERS = 8
 SUB = RES // 2
+KSTEP = 2 * FULL + FULL
 QUERIES = Z * SUB
 KEYS = 2 * Z * RES
 
 f32 = jnp.float32
 bf16 = jnp.bfloat16
-PARAMS = pltpu.CompilerParams(vmem_limit_bytes=48 * 1024 * 1024)
+PARAMS = pltpu.CompilerParams(vmem_limit_bytes=8 * 1024 * 1024)
 PROJECTION = pl.CostEstimate(
     flops=2 * ROWS * RES * EMBED * EMBED, bytes_accessed=2 * EMBED * (EMBED + 2 * ROWS * RES), transcendentals=0
 )
+LAYOUT = pl.CostEstimate(flops=0, bytes_accessed=16 * ROWS * RES * EMBED, transcendentals=0)
+KEY_SHAPES = ((2 * ROWS * FULL, KEYS // 2), (2 * ROWS * FULL, KEYS // 4))
 VMEM = pl.BlockSpec(memory_space=pltpu.VMEM)
 SMEM = pl.BlockSpec(memory_space=pltpu.SMEM)
 
@@ -63,14 +66,19 @@
     var = jnp.mean(centred * centred, axis=-1, keepdims=True)
     n_ref[...] = (centred * lax.rsqrt(var + 1e-05)).astype(bf16)
     t_ref[...] = dot(w_ref[...], n_ref[...].reshape(ROWS * RES, EMBED), 0, 1).astype(bf16)
-    send_pieces(me_ref[2], t_ref, outs)
+    for s, out in enumerate(outs):
+        z = lax.rem(me_ref[2] + s, Z)
+        out[0:FULL, :] = t_ref[pl.ds(chunk_rows(z)[0], FULL), :]
+        if s % 2 == 0:
+            shared = pl.multiple_of(lax.div(z, 2) * (2 * CHUNK) + FULL, FULL)
+            out[FULL:, :] = t_ref[pl.ds(shared, FULL), :]
 
 
 def key_chunks(me, x, w):
     n, *k = pl.pallas_call(
         key_kernel,
         out_shape=(jax.ShapeDtypeStruct((ROWS, RES, EMBED), bf16),)
-        + (jax.ShapeDtypeStruct((CHUNK, ROWS * RES), bf16),) * Z,
+        + tuple(jax.ShapeDtypeStruct((FULL * (2 - s % 2), ROWS * RES), bf16) for s in range(Z)),
         in_specs=[SMEM, VMEM, VMEM],
         out_specs=(VMEM,) * (Z + 1),
         scratch_shapes=[pltpu.VMEM((EMBED, ROWS * RES), bf16)],
@@ -84,15 +92,16 @@
         n = n_ref[:, c * SUB : (c + 1) * SUB, :].reshape(ROWS * SUB, EMBED)
         t = dot(w_ref[...], n, 0, 1).astype(bf16)
         for z in range(Z):
-            (a, na), (b, nb) = chunk_pieces(z)
+            (a, na), _ = chunk_pieces(z)
+            b = (z // 2) * 2 * CHUNK + FULL
             q_ref[2 * z + c, 0:FULL, :] = t[a : a + na]
-            q_ref[2 * z + c, FULL:CHUNK, :] = t[b : b + nb]
+            q_ref[2 * z + c, FULL:, :] = t[b : b + FULL]
 
 
 def query_chunks(n, w):
     return pl.pallas_call(
         query_kernel,
-        out_shape=jax.ShapeDtypeStruct((2 * Z, CHUNK, ROWS * SUB), bf16),
+        out_shape=jax.ShapeDtypeStruct((2 * Z, 2 * FULL, ROWS * SUB), bf16),
         in_specs=[VMEM] * 2,
         out_specs=VMEM,
         compiler_params=PARAMS,
@@ -118,63 +127,84 @@
     )(me, n, w)
 
 
-def arrived(z, refs):
-    return [ref[lax.rem(z - source + Z, Z)] for ref in refs for source in range(Z)]
-
-
 def widen(blocks, r):
     return jnp.concatenate([b[:, r * RES : (r + 1) * RES] for b in blocks], axis=1)
 
 
-def score_kernel(me_ref, q_ref, k00, k01, k10, k11, out, qf, qh, kf, kh):
-    core, z = me_ref[1], me_ref[2]
-    for cr, ks in ((0, (k00, k01)), (1, (k10, k11))):
+def lay_keys(z, own, other, kf, kh):
+    def piece(ref, source, extra):
+        s = lax.rem(z - source + Z, Z)
+        first = lax.div(s, 2) * KSTEP + lax.rem(s, 2) * (2 * FULL) + extra
+        return ref[pl.ds(pl.multiple_of(first, FULL), FULL), :]
+
+    odd = lax.rem(z, 2)
+    for cr, ref in enumerate((own, other)):
+        whole = [piece(ref, source, 0) for source in range(Z)]
+        shared = [piece(ref, 2 * source + odd, FULL) for source in range(Z // 2)]
+        for r in range(ROWS):
+            rows = slice((cr * ROWS + r) * FULL, (cr * ROWS + r + 1) * FULL)
+            kf[rows, :] = widen(whole, r)
+            kh[rows, :] = widen(shared, r)
+
+
+def keys_kernel(me_ref, own, other, kf, kh):
+    lay_keys(me_ref[2], own, other, kf, kh)
+
+
+def keys_laid(me, own, other):
+    return pl.pallas_call(
+        keys_kernel,
+        out_shape=tuple(jax.ShapeDtypeStruct(s, bf16) for s in KEY_SHAPES),
+        in_specs=[SMEM, VMEM, VMEM],
+        out_specs=(VMEM,) * 2,
+        compiler_params=PARAMS,
+        cost_estimate=LAYOUT,
+    )(me, own, other)
+
+
+def score_kernel(me_ref, q_ref, kf0, kh0, own, other, out, qf, qh, kf1, kh1):
+    core = me_ref[1]
+    lay_keys(me_ref[2], own, other, kf1, kh1)
+    for cr in range(2):
         c = jnp.bitwise_xor(core, cr)
         queries = [q_ref[2 * p + c] for p in range(PEERS)]
-        keys = arrived(z, ks)
         for r in range(ROWS):
-            n = cr * ROWS + r
+            rows = slice((cr * ROWS + r) * FULL, (cr * ROWS + r + 1) * FULL)
             t = jnp.concatenate([b[:, r * SUB : (r + 1) * SUB] for b in queries], axis=1)
-            qf[n * FULL : (n + 1) * FULL, :] = t[:FULL]
-            qh[n * HALF : (n + 1) * HALF, :] = t[FULL:]
-            t = widen(keys, r)
-            kf[n * FULL : (n + 1) * FULL, :] = t[:FULL]
-            kh[n * HALF : (n + 1) * HALF, :] = t[FULL:]
-    for i, (a, b) in enumerate(((qf, kf), (qh, kh))):
+            qf[rows, :] = t[:FULL]
+            qh[rows, :] = t[FULL:]
+    first = 0
+    for a, b in ((qf, kf0), (qf, kf1), (qh, kh0), (qh, kh1)):
         s = dot(a[...], b[...], 0, 0)
         for p in range(PEERS):
-            out[p, i] = s[p * SUB : (p + 1) * SUB]
-
-
-def score(me, q, ks):
-    rows = 2 * ROWS
+            out[p, :, first : first + s.shape[1]] = s[p * SUB : (p + 1) * SUB]
+        first += s.shape[1]
+
+
+def score(me, q, laid, own, other):
+    rows = 2 * ROWS * FULL
     return pl.pallas_call(
         score_kernel,
-        out_shape=jax.ShapeDtypeStruct((PEERS, 2, SUB, KEYS), f32),
+        out_shape=jax.ShapeDtypeStruct((PEERS, SUB, KEYS + KEYS // 2), f32),
         in_specs=[SMEM] + [VMEM] * 5,
         out_specs=VMEM,
-        scratch_shapes=[
-            pltpu.VMEM((rows * FULL, QUERIES), bf16),
-            pltpu.VMEM((rows * HALF, QUERIES), bf16),
-            pltpu.VMEM((rows * FULL, KEYS), bf16),
-            pltpu.VMEM((rows * HALF, KEYS), bf16),
-        ],
-        compiler_params=PARAMS,
-    )(me, q, *ks)
+        scratch_shapes=[pltpu.VMEM((rows, QUERIES), bf16)] * 2 + [pltpu.VMEM(s, bf16) for s in KEY_SHAPES],
+        compiler_params=PARAMS,
+    )(me, q, *laid, own, other)
 
 
 def total_kernel(parts, full, half):
-    for i, out in enumerate((full, half)):
-        t = parts[0, i]
-        for p in range(1, PEERS):
-            t = t + parts[p, i]
-        out[...] = t
+    t = parts[0]
+    for p in range(1, PEERS):
+        t = t + parts[p]
+    full[...] = t[:, :KEYS]
+    half[...] = t[:, KEYS:]
 
 
 def total(parts):
     return pl.pallas_call(
         total_kernel,
-        out_shape=(jax.ShapeDtypeStruct((SUB, KEYS), f32),) * 2,
+        out_shape=tuple(jax.ShapeDtypeStruct((SUB, n), f32) for n in (KEYS, KEYS // 2)),
         in_specs=[VMEM],
         out_specs=(VMEM,) * 2,
         compiler_params=PARAMS,
@@ -182,7 +212,7 @@
 
 
 def softmax_kernel(factor, full, half, other, out):
-    for i, logits in enumerate((full[...], half[...] + other[...])):
+    for i, logits in enumerate((full[...], jnp.concatenate([half[...], other[...]], axis=1))):
         logits = logits * factor
         powered = jnp.exp(logits - jnp.max(logits, axis=-1, keepdims=True))
         probs = (powered / jnp.sum(powered, axis=-1, keepdims=True)).astype(bf16)
@@ -200,36 +230,56 @@
     )(full, half, other)
 
 
-def mix_kernel(me_ref, v00, v01, v10, v11, p_ref, o_ref, vf, vh):
-    core, z = me_ref[1], me_ref[2]
-    pf, ph = (p_ref[:, i].reshape(QUERIES, KEYS) for i in range(2))
-    for cr, vs in ((0, (v00, v01)), (1, (v10, v11))):
-        c = jnp.bitwise_xor(core, cr)
-        values = arrived(z, vs)
+def values_kernel(me_ref, v00, v01, v10, v11, vf, vh):
+    z = me_ref[2]
+    odd = lax.rem(z, 2)
+    for cr, refs in enumerate(((v00, v01), (v10, v11))):
+        blocks = [[ref[lax.rem(z - source + Z, Z)] for source in range(Z)] for ref in refs]
+        shared = [
+            ref[lax.rem(z - (2 * source + parity) + Z, Z), FULL:CHUNK, :]
+            for parity in (odd, 1 - odd)
+            for ref in refs
+            for source in range(Z // 2)
+        ]
+        whole = [b[:FULL] for ref in blocks for b in ref]
         for r in range(ROWS):
-            t = widen(values, r)
-            vf[r * FULL : (r + 1) * FULL, :] = t[:FULL]
-            vh[r * HALF : (r + 1) * HALF, :] = t[FULL:]
-        for v, p, first, n in ((vf, pf, 0, FULL), (vh, ph, FULL, HALF)):
-            mixed = dot(v[...], p, 1, 1).astype(bf16)
+            n = cr * ROWS + r
+            vf[n * FULL : (n + 1) * FULL, :] = widen(whole, r)
+            vh[n * HALF : (n + 1) * HALF, :] = widen(shared, r)
+
+
+def values_laid(me, vs):
+    return pl.pallas_call(
+        values_kernel,
+        out_shape=tuple(jax.ShapeDtypeStruct((2 * ROWS * n, KEYS), bf16) for n in (FULL, HALF)),
+        in_specs=[SMEM] + [VMEM] * 4,
+        out_specs=(VMEM,) * 2,
+        compiler_params=PARAMS,
+        cost_estimate=LAYOUT,
+    )(me, *vs)
+
+
+def mix_kernel(me_ref, vf, vh, p_ref, o_ref):
+    core = me_ref[1]
+    for i, (v, first, n) in enumerate(((vf, 0, FULL), (vh, FULL, HALF))):
+        probs = p_ref[:, i].reshape(QUERIES, KEYS)
+        for cr in range(2):
+            c = jnp.bitwise_xor(core, cr)
+            mixed = dot(v[cr * ROWS * n : (cr + 1) * ROWS * n, :], probs, 1, 1).astype(bf16)
             for s in range(PEERS):
                 o_ref[2 * s + c, first : first + n, :] = jnp.concatenate(
                     [mixed[r * n : (r + 1) * n, s * SUB : (s + 1) * SUB] for r in range(ROWS)], axis=1
                 )
 
 
-def mix(me, vs, probs):
+def mix(me, laid, probs):
     return pl.pallas_call(
         mix_kernel,
         out_shape=jax.ShapeDtypeStruct((2 * Z, CHUNK, ROWS * SUB), bf16),
-        in_specs=[SMEM] + [VMEM] * 5,
-        out_specs=VMEM,
-        scratch_shapes=[
-            pltpu.VMEM((ROWS * FULL, KEYS), bf16),
-            pltpu.VMEM((ROWS * HALF, KEYS), bf16),
-        ],
-        compiler_params=PARAMS,
-    )(me, *vs, probs)
+        in_specs=[SMEM] + [VMEM] * 3,
+        out_specs=VMEM,
+        compiler_params=PARAMS,
+    )(me, *laid, probs)
 
 
 def final_kernel(m_ref, w_ref, o_ref, t_ref):
@@ -262,11 +312,14 @@
     return own, far, flip(own, "c", 2, 1), flip(far, "c", 2, 1)
 
 
+ORDER = (1, 7, 2, 6, 3, 5, 4)
+
+
 def spread(pieces):
     got = {0: pieces[0]}
-    for s in (1, 7, 2, 6, 3, 5, 4):
+    for s in ORDER:
         got[s] = lax.ppermute(pieces[s], "z", [(i, (i + s) % Z) for i in range(Z)])
-    return jnp.stack([got[s] for s in range(Z)])
+    return [got[s] for s in range(Z)]
 
 
 def local(x, wq, wk, wv, wf):
@@ -275,16 +328,18 @@
     n, k = key_chunks(me, x, wk)
     q = query_chunks(n, wq)
     v = value_chunks(me, n, wv)
-    ks = gather4(spread(k))
+    k = spread(k)
+    q, k[1] = lax.optimization_barrier((q, k[1]))
     q = lax.all_to_all(q, ("z", "c"), 0, 0, tiled=True)
-    v, scores = lax.optimization_barrier((v, score(me, q, ks)))
+    k00, k01, k10, k11 = gather4(jnp.concatenate(k))
+    v, scores = lax.optimization_barrier((v, score(me, q, keys_laid(me, k00, k10), k01, k11)))
     parts = lax.all_to_all(scores, ("y", "xh"), 0, 0, tiled=True)
-    vs = gather4(spread(v))
+    laid = values_laid(me, gather4(jnp.stack(spread(v))))
     full, half = total(parts)
     rows = ROWS * 2 * PEERS
     probs = softmax(1.0 / math.sqrt(DH * rows), full, half, flip(half, "z", Z, 1))
     probs = lax.all_to_all(probs, ("y", "xh"), 0, 0, tiled=True)
-    mixed = lax.all_to_all(mix(me, vs, probs), ("z", "c"), 0, 0, tiled=True)
+    mixed = lax.all_to_all(mix(me, laid, probs), ("z", "c"), 0, 0, tiled=True)
     return final(mixed, wf)
 
 

time: 172 us -> 192 us (1.12)
  starting transfers between devices: 53.7 us -> 67.9 us
  local copies, waits for them, and re-layouts: 8.24 us -> 14.6 us
    ppermute x14, waiting for transfers between devices: 25.6 us -> 37.5 us  [spread(): got[s] = lax.ppermute(pieces[s], 'z', [(i, (i + s) % Z) for i in range(Z)])]
    ppermute x7, starting transfers between devices: 8.67 us -> 15.5 us  [flip(): return lax.ppermute(x, axes, [(i, i ^ s) for i in range(n)])]
    all_to_all x1, waiting for transfers between devices: 5.56 us -> 0.01 us  [local(): q = lax.all_to_all(q, ('z', 'c'), 0, 0, tiled=True)]
    unnamed x40 -> x72, local copies, waits for them, and re-layouts: 8.23 us -> 13.7 us
    all_to_all x1, waiting for transfers between devices: 8.01 us -> 3.93 us  [local(): probs = lax.all_to_all(probs, ('y', 'xh'), 0, 0, tiled=True)]
    all_to_all x1, starting transfers between devices: 3.56 us -> 7.17 us  [local(): probs = lax.all_to_all(probs, ('y', 'xh'), 0, 0, tiled=True)]
    ppermute x14, starting transfers between devices: 29.4 us -> 32.2 us  [spread(): got[s] = lax.ppermute(pieces[s], 'z', [(i, (i + s) % Z) for i in range(Z)])]
    all_to_all x1, waiting for transfers between devices: 2.3 us -> 0.01 us  [local(): parts = lax.all_to_all(scores, ('y', 'xh'), 0, 0, tiled=True)]
  transfers between devices with their start and end apart: 24 -> 24, of which waited for: 16 -> 11; matrix products, arithmetic and copies ran while one was open for 0% -> 2% of each run, Pallas kernels for 3% -> 4%
where the time goes in v3:
time: 192 us; the launch traced here: 191 us
  starting transfers between devices  67.9 us (35%)
  waiting for transfers between devices  60.7 us (32%)
  blocking collectives  30.9 us (16%)
  Pallas kernels  16.5 us (9%)
  local copies, waits for them, and re-layouts  14.6 us (8%)
    ppermute x14, waiting for transfers between devices, spread(): got[s] = lax.ppermute(pieces[s], 'z', [(i, (i + s) % Z) for i in range(Z)])  37.5 us
    ppermute x14, starting transfers between devices, spread(): got[s] = lax.ppermute(pieces[s], 'z', [(i, (i + s) % Z) for i in range(Z)])  32.2 us
    all_to_all x1, blocking collectives, local(): mixed = lax.all_to_all(mix(me, laid, probs), ('z', 'c'), 0, 0, tiled=True)  30.9 us
    ppermute x7, waiting for transfers between devices, flip(): return lax.ppermute(x, axes, [(i, i ^ s) for i in range(n)])  19.3 us
    ppermute x7, starting transfers between devices, flip(): return lax.ppermute(x, axes, [(i, i ^ s) for i in range(n)])  15.5 us
    unnamed x72, local copies, waits for them, and re-layouts  13.7 us
    all_to_all x1, starting transfers between devices, local(): probs = lax.all_to_all(probs, ('y', 'xh'), 0, 0, tiled=True)  7.17 us
    all_to_all x1, starting transfers between devices, local(): parts = lax.all_to_all(scores, ('y', 'xh'), 0, 0, tiled=True)  6.8 us
  transfers between devices with their start and end apart: 24, of which 11 were waited for; matrix products, arithmetic and copies ran while one was open for 2% of the time, Pallas kernels for 4%

profile of v3, /device:TPU:1, one launch (start us, length us, event | category | flops | bytes accessed | tf_op | source)
XLA Modules:
  0.0 191.1 jit_solution(6535035163698577200)
XLA Ops:
  2.5 1.8 shard_map.55
  4.3 2.5 %collective-permute-start = (bf16[64,512]{1,0:T(8,128)(2,1)S(1)}, bf16[64,512]{1,0:T(8,128)(2,1)}, u32[]{:S(2)}, u32[]{:S(2)}) collective-permute-start(bf16[64,512]{1,0:T(8,128)(2,1)S(1)} %get-tuple-element.48), channel_id=1, source_target_pairs={{0,2},{2,4},{4,6},{6,8},{8,10},{10,12},{12,14},{14,0},{1,3},{3,5},... | collective-permute-start | bytes 196616 | tf_op jit(solution)/shard_map/ppermute | solution.py:321
  6.9 5.6 %collective-permute-start.2 = (bf16[64,512]{1,0:T(8,128)(2,1)S(1)}, bf16[64,512]{1,0:T(8,128)(2,1)}, u32[]{:S(2)}, u32[]{:S(2)}) collective-permute-start(bf16[64,512]{1,0:T(8,128)(2,1)S(1)} %get-tuple-element.53), channel_id=1, source_target_pairs={{0,6},{2,8},{4,10},{6,12},{8,14},{10,0},{12,2},{14,4},{1,7},{3,9},... | collective-permute-start | bytes 196616 | tf_op jit(solution)/shard_map/ppermute | solution.py:321
  12.4 1.7 collective-permute-start.6
  14.4 1.9 shard_map.57
  16.2 4.9 %collective-permute-start.3 = (bf16[128,512]{1,0:T(8,128)(2,1)S(1)}, bf16[128,512]{1,0:T(8,128)(2,1)S(1)}, u32[]{:S(2)}, u32[]{:S(2)}) collective-permute-start(bf16[128,512]{1,0:T(8,128)(2,1)S(1)} %get-tuple-element.54), channel_id=1, source_target_pairs={{0,8},{2,10},{4,12},{6,14},{8,0},{10,2},{12,4},{14,6},{1,9},{3,11}... | collective-permute-start | bytes 393224 | tf_op jit(solution)/shard_map/ppermute | solution.py:321
  21.1 6.3 %all-to-all-start = ((bf16[16,128,256]{2,1,0:T(8,128)(2,1)}), bf16[16,128,256]{2,1,0:T(8,128)(2,1)S(1)}, u32[]{:S(2)}, u32[]{:S(2)}) async-start(bf16[16,128,256]{2,1,0:T(8,128)(2,1)} %shard_map.57), calls=%async_computation | async-start | bytes 2097152 | tf_op jit(solution)/shard_map/all_to_all | solution.py:333
  28.4 3.5 %collective-permute-start.5 = (bf16[128,512]{1,0:T(8,128)(2,1)S(1)}, bf16[128,512]{1,0:T(8,128)(2,1)S(1)}, u32[]{:S(2)}, u32[]{:S(2)}) collective-permute-start(bf16[128,512]{1,0:T(8,128)(2,1)S(1)} %get-tuple-element.56), channel_id=1, source_target_pairs={{0,12},{2,14},{4,0},{6,2},{8,4},{10,6},{12,8},{14,10},{1,13},{3,15... | collective-permute-start | bytes 393224 | tf_op jit(solution)/shard_map/ppermute | solution.py:321
  33.6 24.7 %collective-permute-done.5 = bf16[128,512]{1,0:T(8,128)(2,1)S(1)} collective-permute-done((bf16[128,512]{1,0:T(8,128)(2,1)S(1)}, bf16[128,512]{1,0:T(8,128)(2,1)S(1)}, u32[]{:S(2)}, u32[]{:S(2)}) %collective-permute-start.5) | collective-permute-done | bytes 131104 | tf_op jit(solution)/shard_map/ppermute | solution.py:321
  60.4 1.7 collective-permute-start.7
  62.1 14.8 %collective-permute-done.8.own = bf16[768,512]{1,0:T(8,128)(2,1)S(1)} collective-permute-done((bf16[768,512]{1,0:T(8,128)(2,1)S(1)}, bf16[768,512]{1,0:T(8,128)(2,1)S(1)}, u32[]{:S(2)}, u32[]{:S(2)}) %collective-permute-start.8) | collective-permute-done | bytes 786464 | tf_op jit(solution)/shard_map/ppermute | solution.py:307
  76.9 2.3 %collective-permute-start.9 = (bf16[768,512]{1,0:T(8,128)(2,1)S(1)}, bf16[768,512]{1,0:T(8,128)(2,1)S(1)}, u32[]{:S(2)}, u32[]{:S(2)}) collective-permute-start(bf16[768,512]{1,0:T(8,128)(2,1)S(1)} %collective-permute-done.8.own), channel_id=1, source_target_pairs={{0,16},{16,0},{1,17},{17,1},{2,18},{18,2},{3,19},{19,3},{4,20},{20... | collective-permute-start | bytes 2359304 | tf_op jit(solution)/shard_map/ppermute | solution.py:307
  79.2 1.4 shard_map.56
  85.0 4.0 %shard_map.59 = f32[8,32,1536]{2,1,0:T(8,128)} custom-call(s32[3]{0:T(128)S(1)} %pad_add_fusion.me_ref, bf16[16,128,256]{2,1,0:T(8,128)(2,1)S(1)} %all-to-all-done.q_ref, bf16[1024,512]{1,0:T(8,128)(2,1)S(1)} %get-tuple-element.58.kf0, bf16[1024,256]{1,0:T(8,128)(2,1)S(1)} %get-tuple-element.59.kh0, bf16[768,512]{1,0:T(8,128)(2,1)S(1)} %copy-done.11, ...), custom_call_target="tpu_custom_call" | custom-call | tf_op jit(solution)/shard_map/pallas_call | solution.py:186
  89.1 6.8 %all-to-all-start.1 = ((f32[8,32,1536]{2,1,0:T(8,128)}), f32[8,32,1536]{2,1,0:T(8,128)S(1)}, u32[]{:S(2)}, u32[]{:S(2)}) async-start(f32[8,32,1536]{2,1,0:T(8,128)} %shard_map.59), calls=%async_computation.1 | async-start | bytes 3145728 | tf_op jit(solution)/shard_map/all_to_all | solution.py:336
  96.4 3.6 %collective-permute-start.11 = (bf16[96,512]{1,0:T(8,128)(2,1)S(1)}, bf16[96,512]{1,0:T(8,128)(2,1)S(1)}, u32[]{:S(2)}, u32[]{:S(2)}) collective-permute-start(bf16[96,512]{1,0:T(8,128)(2,1)S(1)} %copy-done.26), channel_id=1, source_target_pairs={{0,4},{2,6},{4,8},{6,10},{8,12},{10,14},{12,0},{14,2},{1,5},{3,7},... | collective-permute-start | bytes 294920 | tf_op jit(solution)/shard_map/ppermute | solution.py:321
  100.3 5.2 %collective-permute-start.13 = (bf16[96,512]{1,0:T(8,128)(2,1)S(1)}, bf16[96,512]{1,0:T(8,128)(2,1)S(1)}, u32[]{:S(2)}, u32[]{:S(2)}) collective-permute-start(bf16[96,512]{1,0:T(8,128)(2,1)S(1)} %copy-done.22), channel_id=1, source_target_pairs={{0,8},{2,10},{4,12},{6,14},{8,0},{10,2},{12,4},{14,6},{1,9},{3,11}... | collective-permute-start | bytes 294920 | tf_op jit(solution)/shard_map/ppermute | solution.py:321
  105.6 2.6 %collective-permute-start.15 = (bf16[96,512]{1,0:T(8,128)(2,1)S(1)}, bf16[96,512]{1,0:T(8,128)(2,1)S(1)}, u32[]{:S(2)}, u32[]{:S(2)}) collective-permute-start(bf16[96,512]{1,0:T(8,128)(2,1)S(1)} %copy-done.18), channel_id=1, source_target_pairs={{0,12},{2,14},{4,0},{6,2},{8,4},{10,6},{12,8},{14,10},{1,13},{3,15... | collective-permute-start | bytes 294920 | tf_op jit(solution)/shard_map/ppermute | solution.py:321
  108.2 1.4 collective-permute-start.16
  109.9 5.4 %collective-permute-done.13 = bf16[96,512]{1,0:T(8,128)(2,1)S(1)} collective-permute-done((bf16[96,512]{1,0:T(8,128)(2,1)S(1)}, bf16[96,512]{1,0:T(8,128)(2,1)S(1)}, u32[]{:S(2)}, u32[]{:S(2)}) %collective-permute-start.13) | collective-permute-done | bytes 98336 | tf_op jit(solution)/shard_map/ppermute | solution.py:321
  115.6 6.0 %collective-permute-done.15 = bf16[96,512]{1,0:T(8,128)(2,1)S(1)} collective-permute-done((bf16[96,512]{1,0:T(8,128)(2,1)S(1)}, bf16[96,512]{1,0:T(8,128)(2,1)S(1)}, u32[]{:S(2)}, u32[]{:S(2)}) %collective-permute-start.15) | collective-permute-done | bytes 98336 | tf_op jit(solution)/shard_map/ppermute | solution.py:321
  123.0 1.6 collective-permute-start.20
  124.6 1.7 collective-permute-done.20.other
  127.5 7.2 %all-to-all-start.2 = ((bf16[8,2,32,1024]{3,2,1,0:T(8,128)(2,1)}), bf16[8,2,32,1024]{3,2,1,0:T(8,128)(2,1)S(1)}, u32[]{:S(2)}, u32[]{:S(2)}) async-start(bf16[8,2,32,1024]{3,2,1,0:T(8,128)(2,1)} %shard_map.62), calls=%async_computation.2 | async-start | bytes 2097152 | tf_op jit(solution)/shard_map/all_to_all | solution.py:341
  134.7 3.5 %collective-permute-start.18 = (bf16[8,96,512]{2,1,0:T(8,128)(2,1)S(1)}, bf16[8,96,512]{2,1,0:T(8,128)(2,1)S(1)}, u32[]{:S(2)}, u32[]{:S(2)}) collective-permute-start(bf16[8,96,512]{2,1,0:T(8,128)(2,1)S(1)} %bitcast_dynamic-update-slice_fusion.v00), channel_id=1, source_target_pairs={{0,16},{16,0},{1,17},{17,1},{2,18},{18,2},{3,19},{19,3},{4,20},{20... | collective-permute-start | bytes 2359304 | tf_op jit(solution)/shard_map/ppermute | solution.py:307
  138.1 1.8 collective-permute-done.17.v01
  139.9 4.9 %collective-permute-start.19 = (bf16[8,96,512]{2,1,0:T(8,128)(2,1)S(1)}, bf16[8,96,512]{2,1,0:T(8,128)(2,1)S(1)}, u32[]{:S(2)}, u32[]{:S(2)}) collective-permute-start(bf16[8,96,512]{2,1,0:T(8,128)(2,1)S(1)} %collective-permute-done.17.v01), channel_id=1, source_target_pairs={{0,16},{16,0},{1,17},{17,1},{2,18},{18,2},{3,19},{19,3},{4,20},{20... | collective-permute-start | bytes 2359304 | tf_op jit(solution)/shard_map/ppermute | solution.py:307
  149.0 1.4 shard_map.60
  151.4 3.9 %all-to-all-done.2.p_ref = bf16[8,2,32,1024]{3,2,1,0:T(8,128)(2,1)S(1)} async-done(((bf16[8,2,32,1024]{3,2,1,0:T(8,128)(2,1)}), bf16[8,2,32,1024]{3,2,1,0:T(8,128)(2,1)S(1)}, u32[]{:S(2)}, u32[]{:S(2)}) %all-to-all-start.2) | async-done | bytes 1048608 | tf_op jit(solution)/shard_map/all_to_all | solution.py:341
  156.6 1.9 shard_map.63
  158.5 30.9 %all_to_all.20.m_ref = bf16[16,96,256]{2,1,0:T(8,128)(2,1)S(1)} all-to-all(bf16[16,96,256]{2,1,0:T(8,128)(2,1)S(1)} %shard_map.63), channel_id=1, replica_groups=mesh['y'=4,'xh'=2,'c'=2,'z'=8,'xl'=2] {'z','c'}, dimensions={0} | all-to-all | bytes 1572864 | tf_op jit(solution)/shard_map/all_to_all | solution.py:342
  189.4 1.7 shard_map.64
  (102 shorter events, 22.1 us)
Async XLA Ops:
  2.5 11.9 %copy-start.1 = (bf16[768,768]{1,0:T(8,128)(2,1)S(1)}, bf16[768,768]{1,0:T(8,128)(2,1)}, u32[]{:S(2)}) copy-start(bf16[768,768]{1,0:T(8,128)(2,1)} %w_ref.6) | copy-start | bytes 3538948
  4.3 11.9 %collective-permute-start = (bf16[64,512]{1,0:T(8,128)(2,1)S(1)}, bf16[64,512]{1,0:T(8,128)(2,1)}, u32[]{:S(2)}, u32[]{:S(2)}) collective-permute-start(bf16[64,512]{1,0:T(8,128)(2,1)S(1)} %get-tuple-element.48), channel_id=1, source_target_pairs={{0,2},{2,4},{4,6},{6,8},{8,10},{10,12},{12,14},{14,0},{1,3},{3,5},... | collective-permute-start | bytes 196616 | tf_op jit(solution)/shard_map/ppermute | solution.py:321
  6.9 25.1 %collective-permute-start.2 = (bf16[64,512]{1,0:T(8,128)(2,1)S(1)}, bf16[64,512]{1,0:T(8,128)(2,1)}, u32[]{:S(2)}, u32[]{:S(2)}) collective-permute-start(bf16[64,512]{1,0:T(8,128)(2,1)S(1)} %get-tuple-element.53), channel_id=1, source_target_pairs={{0,6},{2,8},{4,10},{6,12},{8,14},{10,0},{12,2},{14,4},{1,7},{3,9},... | collective-permute-start | bytes 196616 | tf_op jit(solution)/shard_map/ppermute | solution.py:321
  12.4 20.4 %collective-permute-start.4 = (bf16[64,512]{1,0:T(8,128)(2,1)S(1)}, bf16[64,512]{1,0:T(8,128)(2,1)}, u32[]{:S(2)}, u32[]{:S(2)}) collective-permute-start(bf16[64,512]{1,0:T(8,128)(2,1)S(1)} %get-tuple-element.55), channel_id=1, source_target_pairs={{0,10},{2,12},{4,14},{6,0},{8,2},{10,4},{12,6},{14,8},{1,11},{3,13... | collective-permute-start | bytes 196616 | tf_op jit(solution)/shard_map/ppermute | solution.py:321
  12.4 45.9 %collective-permute-start.6 = (bf16[64,512]{1,0:T(8,128)(2,1)S(1)}, bf16[64,512]{1,0:T(8,128)(2,1)}, u32[]{:S(2)}, u32[]{:S(2)}) collective-permute-start(bf16[64,512]{1,0:T(8,128)(2,1)S(1)} %get-tuple-element.57), channel_id=1, source_target_pairs={{0,14},{2,0},{4,2},{6,4},{8,6},{10,8},{12,10},{14,12},{1,15},{3,1}... | collective-permute-start | bytes 196616 | tf_op jit(solution)/shard_map/ppermute | solution.py:321
  14.1 14.2 %collective-permute-start.1 = (bf16[128,512]{1,0:T(8,128)(2,1)S(1)}, bf16[128,512]{1,0:T(8,128)(2,1)S(1)}, u32[]{:S(2)}, u32[]{:S(2)}) collective-permute-start(bf16[128,512]{1,0:T(8,128)(2,1)S(1)} %get-tuple-element.52), channel_id=1, source_target_pairs={{0,4},{2,6},{4,8},{6,10},{8,12},{10,14},{12,0},{14,2},{1,5},{3,7},... | collective-permute-start | bytes 393224 | tf_op jit(solution)/shard_map/ppermute | solution.py:321
  16.2 16.5 %collective-permute-start.3 = (bf16[128,512]{1,0:T(8,128)(2,1)S(1)}, bf16[128,512]{1,0:T(8,128)(2,1)S(1)}, u32[]{:S(2)}, u32[]{:S(2)}) collective-permute-start(bf16[128,512]{1,0:T(8,128)(2,1)S(1)} %get-tuple-element.54), channel_id=1, source_target_pairs={{0,8},{2,10},{4,12},{6,14},{8,0},{10,2},{12,4},{14,6},{1,9},{3,11}... | collective-permute-start | bytes 393224 | tf_op jit(solution)/shard_map/ppermute | solution.py:321
  21.1 61.6 %all-to-all-start = ((bf16[16,128,256]{2,1,0:T(8,128)(2,1)}), bf16[16,128,256]{2,1,0:T(8,128)(2,1)S(1)}, u32[]{:S(2)}, u32[]{:S(2)}) async-start(bf16[16,128,256]{2,1,0:T(8,128)(2,1)} %shard_map.57), calls=%async_computation | async-start | bytes 2097152 | tf_op jit(solution)/shard_map/all_to_all | solution.py:333
  27.4 51.7 %copy-start.14 = (bf16[768,768]{1,0:T(8,128)(2,1)S(1)}, bf16[768,768]{1,0:T(8,128)(2,1)}, u32[]{:S(2)}) copy-start(bf16[768,768]{1,0:T(8,128)(2,1)} %w_ref.5) | copy-start | bytes 3538948
  28.4 29.9 %collective-permute-start.5 = (bf16[128,512]{1,0:T(8,128)(2,1)S(1)}, bf16[128,512]{1,0:T(8,128)(2,1)S(1)}, u32[]{:S(2)}, u32[]{:S(2)}) collective-permute-start(bf16[128,512]{1,0:T(8,128)(2,1)S(1)} %get-tuple-element.56), channel_id=1, source_target_pairs={{0,12},{2,14},{4,0},{6,2},{8,4},{10,6},{12,8},{14,10},{1,13},{3,15... | collective-permute-start | bytes 393224 | tf_op jit(solution)/shard_map/ppermute | solution.py:321
  59.2 17.7 %collective-permute-start.8 = (bf16[768,512]{1,0:T(8,128)(2,1)S(1)}, bf16[768,512]{1,0:T(8,128)(2,1)S(1)}, u32[]{:S(2)}, u32[]{:S(2)}) collective-permute-start(bf16[768,512]{1,0:T(8,128)(2,1)S(1)} %constant_dynamic-update-slice_fusion.own), channel_id=1, source_target_pairs={{0,1},{1,0},{2,3},{3,2},{4,5},{5,4},{6,7},{7,6},{8,9},{9,8},{10,11... | collective-permute-start | bytes 2359304 | tf_op jit(solution)/shard_map/ppermute | solution.py:307
  60.4 20.2 %collective-permute-start.7 = (bf16[768,512]{1,0:T(8,128)(2,1)S(1)}, bf16[768,512]{1,0:T(8,128)(2,1)S(1)}, u32[]{:S(2)}, u32[]{:S(2)}) collective-permute-start(bf16[768,512]{1,0:T(8,128)(2,1)S(1)} %constant_dynamic-update-slice_fusion.own), channel_id=1, source_target_pairs={{0,16},{16,0},{1,17},{17,1},{2,18},{18,2},{3,19},{19,3},{4,20},{20... | collective-permute-start | bytes 2359304 | tf_op jit(solution)/shard_map/ppermute | solution.py:307
  76.9 5.0 %collective-permute-start.9 = (bf16[768,512]{1,0:T(8,128)(2,1)S(1)}, bf16[768,512]{1,0:T(8,128)(2,1)S(1)}, u32[]{:S(2)}, u32[]{:S(2)}) collective-permute-start(bf16[768,512]{1,0:T(8,128)(2,1)S(1)} %collective-permute-done.8.own), channel_id=1, source_target_pairs={{0,16},{16,0},{1,17},{17,1},{2,18},{18,2},{3,19},{19,3},{4,20},{20... | collective-permute-start | bytes 2359304 | tf_op jit(solution)/shard_map/ppermute | solution.py:307
  89.0 11.3 %copy-start.22 = (bf16[96,512]{1,0:T(8,128)(2,1)S(1)}, bf16[96,512]{1,0:T(8,128)(2,1)}, u32[]{:S(2)}) copy-start(bf16[96,512]{1,0:T(8,128)(2,1)} %copy-done.21) | copy-start | bytes 294916
  89.0 16.6 %copy-start.20 = (bf16[96,512]{1,0:T(8,128)(2,1)S(1)}, bf16[96,512]{1,0:T(8,128)(2,1)}, u32[]{:S(2)}) copy-start(bf16[96,512]{1,0:T(8,128)(2,1)} %copy-done.19) | copy-start | bytes 294916
  89.0 16.6 %copy-start.18 = (bf16[96,512]{1,0:T(8,128)(2,1)S(1)}, bf16[96,512]{1,0:T(8,128)(2,1)}, u32[]{:S(2)}) copy-start(bf16[96,512]{1,0:T(8,128)(2,1)} %copy-done.17) | copy-start | bytes 294916
  89.0 19.2 %copy-start.16 = (bf16[96,512]{1,0:T(8,128)(2,1)S(1)}, bf16[96,512]{1,0:T(8,128)(2,1)}, u32[]{:S(2)}) copy-start(bf16[96,512]{1,0:T(8,128)(2,1)} %copy-done.15) | copy-start | bytes 294916
  89.1 33.9 %all-to-all-start.1 = ((f32[8,32,1536]{2,1,0:T(8,128)}), f32[8,32,1536]{2,1,0:T(8,128)S(1)}, u32[]{:S(2)}, u32[]{:S(2)}) async-start(f32[8,32,1536]{2,1,0:T(8,128)} %shard_map.59), calls=%async_computation.1 | async-start | bytes 3145728 | tf_op jit(solution)/shard_map/all_to_all | solution.py:336
  95.9 9.7 %collective-permute-start.10 = (bf16[96,512]{1,0:T(8,128)(2,1)S(1)}, bf16[96,512]{1,0:T(8,128)(2,1)S(1)}, u32[]{:S(2)}, u32[]{:S(2)}) collective-permute-start(bf16[96,512]{1,0:T(8,128)(2,1)S(1)} %copy-done.28), channel_id=1, source_target_pairs={{0,2},{2,4},{4,6},{6,8},{8,10},{10,12},{12,14},{14,0},{1,3},{3,5},... | collective-permute-start | bytes 294920 | tf_op jit(solution)/shard_map/ppermute | solution.py:321
  96.4 11.8 %collective-permute-start.11 = (bf16[96,512]{1,0:T(8,128)(2,1)S(1)}, bf16[96,512]{1,0:T(8,128)(2,1)S(1)}, u32[]{:S(2)}, u32[]{:S(2)}) collective-permute-start(bf16[96,512]{1,0:T(8,128)(2,1)S(1)} %copy-done.26), channel_id=1, source_target_pairs={{0,4},{2,6},{4,8},{6,10},{8,12},{10,14},{12,0},{14,2},{1,5},{3,7},... | collective-permute-start | bytes 294920 | tf_op jit(solution)/shard_map/ppermute | solution.py:321
  100.0 9.9 %collective-permute-start.12 = (bf16[96,512]{1,0:T(8,128)(2,1)S(1)}, bf16[96,512]{1,0:T(8,128)(2,1)S(1)}, u32[]{:S(2)}, u32[]{:S(2)}) collective-permute-start(bf16[96,512]{1,0:T(8,128)(2,1)S(1)} %copy-done.24), channel_id=1, source_target_pairs={{0,6},{2,8},{4,10},{6,12},{8,14},{10,0},{12,2},{14,4},{1,7},{3,9},... | collective-permute-start | bytes 294920 | tf_op jit(solution)/shard_map/ppermute | solution.py:321
  100.3 15.0 %collective-permute-start.13 = (bf16[96,512]{1,0:T(8,128)(2,1)S(1)}, bf16[96,512]{1,0:T(8,128)(2,1)S(1)}, u32[]{:S(2)}, u32[]{:S(2)}) collective-permute-start(bf16[96,512]{1,0:T(8,128)(2,1)S(1)} %copy-done.22), channel_id=1, source_target_pairs={{0,8},{2,10},{4,12},{6,14},{8,0},{10,2},{12,4},{14,6},{1,9},{3,11}... | collective-permute-start | bytes 294920 | tf_op jit(solution)/shard_map/ppermute | solution.py:321
  105.6 10.0 %collective-permute-start.14 = (bf16[96,512]{1,0:T(8,128)(2,1)S(1)}, bf16[96,512]{1,0:T(8,128)(2,1)S(1)}, u32[]{:S(2)}, u32[]{:S(2)}) collective-permute-start(bf16[96,512]{1,0:T(8,128)(2,1)S(1)} %copy-done.20), channel_id=1, source_target_pairs={{0,10},{2,12},{4,14},{6,0},{8,2},{10,4},{12,6},{14,8},{1,11},{3,13... | collective-permute-start | bytes 294920 | tf_op jit(solution)/shard_map/ppermute | solution.py:321
  105.6 16.0 %collective-permute-start.15 = (bf16[96,512]{1,0:T(8,128)(2,1)S(1)}, bf16[96,512]{1,0:T(8,128)(2,1)S(1)}, u32[]{:S(2)}, u32[]{:S(2)}) collective-permute-start(bf16[96,512]{1,0:T(8,128)(2,1)S(1)} %copy-done.18), channel_id=1, source_target_pairs={{0,12},{2,14},{4,0},{6,2},{8,4},{10,6},{12,8},{14,10},{1,13},{3,15... | collective-permute-start | bytes 294920 | tf_op jit(solution)/shard_map/ppermute | solution.py:321
  108.2 14.3 %collective-permute-start.16 = (bf16[96,512]{1,0:T(8,128)(2,1)S(1)}, bf16[96,512]{1,0:T(8,128)(2,1)S(1)}, u32[]{:S(2)}, u32[]{:S(2)}) collective-permute-start(bf16[96,512]{1,0:T(8,128)(2,1)S(1)} %copy-done.16), channel_id=1, source_target_pairs={{0,14},{2,0},{4,2},{6,4},{8,6},{10,8},{12,10},{14,12},{1,15},{3,1}... | collective-permute-start | bytes 294920 | tf_op jit(solution)/shard_map/ppermute | solution.py:321
  122.5 12.2 %copy-start.5 = (bf16[8,96,512]{2,1,0:T(8,128)(2,1)}, bf16[8,96,512]{2,1,0:T(8,128)(2,1)S(1)}, u32[]{:S(2)}) copy-start(bf16[8,96,512]{2,1,0:T(8,128)(2,1)S(1)} %bitcast_dynamic-update-slice_fusion.v00) | copy-start | bytes 2359300
  122.5 17.4 %collective-permute-start.17 = (bf16[8,96,512]{2,1,0:T(8,128)(2,1)S(1)}, bf16[8,96,512]{2,1,0:T(8,128)(2,1)S(1)}, u32[]{:S(2)}, u32[]{:S(2)}) collective-permute-start(bf16[8,96,512]{2,1,0:T(8,128)(2,1)S(1)} %bitcast_dynamic-update-slice_fusion.v00), channel_id=1, source_target_pairs={{0,1},{1,0},{2,3},{3,2},{4,5},{5,4},{6,7},{7,6},{8,9},{9,8},{10,11... | collective-permute-start | bytes 2359304 | tf_op jit(solution)/shard_map/ppermute | solution.py:307
  123.0 3.2 %collective-permute-start.20 = (f32[32,512]{1,0:T(8,128)S(1)}, f32[32,512]{1,0:T(8,128)S(1)}, u32[]{:S(2)}, u32[]{:S(2)}) collective-permute-start(f32[32,512]{1,0:T(8,128)S(1)} %get-tuple-element.72.half), channel_id=1, source_target_pairs={{0,2},{2,0},{4,6},{6,4},{8,10},{10,8},{12,14},{14,12},{1,3},{3,1},... | collective-permute-start | bytes 196616 | tf_op jit(solution)/shard_map/ppermute | solution.py:307
  127.5 27.8 %all-to-all-start.2 = ((bf16[8,2,32,1024]{3,2,1,0:T(8,128)(2,1)}), bf16[8,2,32,1024]{3,2,1,0:T(8,128)(2,1)S(1)}, u32[]{:S(2)}, u32[]{:S(2)}) async-start(bf16[8,2,32,1024]{3,2,1,0:T(8,128)(2,1)} %shard_map.62), calls=%async_computation.2 | async-start | bytes 2097152 | tf_op jit(solution)/shard_map/all_to_all | solution.py:341
  134.7 11.0 %collective-permute-start.18 = (bf16[8,96,512]{2,1,0:T(8,128)(2,1)S(1)}, bf16[8,96,512]{2,1,0:T(8,128)(2,1)S(1)}, u32[]{:S(2)}, u32[]{:S(2)}) collective-permute-start(bf16[8,96,512]{2,1,0:T(8,128)(2,1)S(1)} %bitcast_dynamic-update-slice_fusion.v00), channel_id=1, source_target_pairs={{0,16},{16,0},{1,17},{17,1},{2,18},{18,2},{3,19},{19,3},{4,20},{20... | collective-permute-start | bytes 2359304 | tf_op jit(solution)/shard_map/ppermute | solution.py:307
  139.9 6.8 %collective-permute-start.19 = (bf16[8,96,512]{2,1,0:T(8,128)(2,1)S(1)}, bf16[8,96,512]{2,1,0:T(8,128)(2,1)S(1)}, u32[]{:S(2)}, u32[]{:S(2)}) collective-permute-start(bf16[8,96,512]{2,1,0:T(8,128)(2,1)S(1)} %collective-permute-done.17.v01), channel_id=1, source_target_pairs={{0,16},{16,0},{1,17},{17,1},{2,18},{18,2},{3,19},{19,3},{4,20},{20... | collective-permute-start | bytes 2359304 | tf_op jit(solution)/shard_map/ppermute | solution.py:307
  158.4 30.9 %copy-start.2 = (bf16[768,768]{1,0:T(8,128)(2,1)S(1)}, bf16[768,768]{1,0:T(8,128)(2,1)}, u32[]{:S(2)}) copy-start(bf16[768,768]{1,0:T(8,128)(2,1)} %w_ref.7) | copy-start | bytes 3538948
  (21 other events, 49.2 us)

commit v4 on v3

v4 whole, which is shorter than its diff:
```python
import functools
import math

import jax
import jax.numpy as jnp
from jax import lax
from jax.experimental import pallas as pl
from jax.experimental.pallas import tpu as pltpu
from jax.sharding import Mesh, PartitionSpec as P

H = 12
DH = 64
EMBED = 768
ROWS = 8
RES = 64
Z = 8
CHUNK = EMBED // Z
FULL = DH
HALF = CHUNK - DH
PEERS = 8
SUB = RES // 2
TOKENS = ROWS * SUB
QUERIES = Z * SUB
KEYS = 2 * Z * RES

f32 = jnp.float32
bf16 = jnp.bfloat16
PARAMS = pltpu.CompilerParams(vmem_limit_bytes=8 * 1024 * 1024)
PROJECTION = pl.CostEstimate(
    flops=2 * ROWS * RES * EMBED * EMBED, bytes_accessed=2 * EMBED * (EMBED + 2 * ROWS * RES), transcendentals=0
)
LAYOUT = pl.CostEstimate(flops=0, bytes_accessed=16 * ROWS * RES * EMBED, transcendentals=0)
KEY_SHAPES = ((2 * ROWS * FULL, KEYS // 2), (2 * ROWS * FULL, KEYS // 4))
VMEM = pl.BlockSpec(memory_space=pltpu.VMEM)
SMEM = pl.BlockSpec(memory_space=pltpu.SMEM)


def chunk_pieces(z):
    base = z * CHUNK
    if z % 2 == 0:
        return (base, FULL), (base + FULL, HALF)
    return (base + HALF, FULL), (base, HALF)


def dot(a, b, ca, cb):
    return lax.dot_general(a, b, (((ca,), (cb,)), ((), ())), preferred_element_type=f32)


def shared_head(z):
    return z // 2 * (2 * CHUNK) + FULL if isinstance(z, int) else lax.div(z, 2) * (2 * CHUNK) + FULL


def chunk_rows(z):
    odd = lax.rem(z, 2)
    base = z * CHUNK
    return pl.multiple_of(base + odd * HALF, HALF), pl.multiple_of(base + (1 - odd) * FULL, HALF)


def key_kernel(me_ref, x_ref, w_ref, n_ref, give_ref, k_ref):
    x = x_ref[...].astype(f32)
    centred = x - jnp.mean(x, axis=-1, keepdims=True)
    var = jnp.mean(centred * centred, axis=-1, keepdims=True)
    normed = (centred * lax.rsqrt(var + 1e-05)).astype(bf16)
    for h in range(2):
        n_ref[h] = normed[:, h * SUB : (h + 1) * SUB, :]
    give_ref[...] = n_ref[1 - me_ref[1]]
    t = dot(w_ref[...], n_ref[...].reshape(ROWS * RES, EMBED), 0, 1).astype(bf16)
    for z in range(Z):
        (a, _), _ = chunk_pieces(z)
        b, lanes = shared_head(z), slice(z % 2 * TOKENS, (z % 2 + 1) * TOKENS)
        k_ref[z, 0:FULL, :] = t[a : a + FULL]
        k_ref[z, FULL:CHUNK, :TOKENS] = t[b : b + HALF, lanes]
        k_ref[z, FULL:CHUNK, TOKENS:] = t[b + HALF : b + FULL, lanes]


def key_chunks(me, x, w):
    return pl.pallas_call(
        key_kernel,
        out_shape=(
            jax.ShapeDtypeStruct((2, ROWS, SUB, EMBED), bf16),
            jax.ShapeDtypeStruct((ROWS, SUB, EMBED), bf16),
            jax.ShapeDtypeStruct((Z, CHUNK, ROWS * RES), bf16),
        ),
        in_specs=[SMEM, VMEM, VMEM],
        out_specs=(VMEM,) * 3,
        compiler_params=PARAMS,
    )(me, x, w)


def query_kernel(me_ref, n_ref, got_ref, w_ref, *rest):
    outs, t_ref = rest[:Z], rest[Z]
    for c, n in enumerate((n_ref[me_ref[1]], got_ref[...])):
        t = dot(w_ref[...], n.reshape(TOKENS, EMBED), 0, 1)
        t_ref[:, c * TOKENS : (c + 1) * TOKENS] = t.astype(bf16)
    for s, out in enumerate(outs):
        z = lax.rem(me_ref[2] + s, Z)
        out[0:FULL, :] = t_ref[pl.ds(chunk_rows(z)[0], FULL), :]
        out[FULL:, :] = t_ref[pl.ds(pl.multiple_of(shared_head(z), FULL), FULL), :]


def query_chunks(me, n, got, w):
    return pl.pallas_call(
        query_kernel,
        out_shape=(jax.ShapeDtypeStruct((2 * FULL, 2 * TOKENS), bf16),) * Z,
        in_specs=[SMEM] + [VMEM] * 3,
        out_specs=(VMEM,) * Z,
        scratch_shapes=[pltpu.VMEM((EMBED, 2 * TOKENS), bf16)],
        compiler_params=PARAMS,
        cost_estimate=PROJECTION,
    )(me, n, got, w)


def value_kernel(me_ref, n_ref, w_ref, *rest):
    outs, t_ref = rest[:Z], rest[Z]
    t_ref[...] = dot(w_ref[...], n_ref[...].reshape(ROWS * RES, EMBED), 0, 1).astype(bf16)
    for s, out in enumerate(outs):
        full, half = chunk_rows(lax.rem(me_ref[2] + s, Z))
        out[0:FULL, :] = t_ref[pl.ds(full, FULL), :]
        out[FULL:CHUNK, :] = t_ref[pl.ds(half, HALF), :]


def value_chunks(me, n, w):
    return pl.pallas_call(
        value_kernel,
        out_shape=(jax.ShapeDtypeStruct((CHUNK, ROWS * RES), bf16),) * Z,
        in_specs=[SMEM, VMEM, VMEM],
        out_specs=(VMEM,) * Z,
        scratch_shapes=[pltpu.VMEM((EMBED, ROWS * RES), bf16)],
        compiler_params=PARAMS,
        cost_estimate=PROJECTION,
    )(me, n, w)


def lay_keys(own, other, kf, kh):
    for cr, ref in enumerate((own, other)):
        for r in range(ROWS):
            n = (cr * ROWS + r) * FULL
            whole = [ref[z, 0:FULL, h * TOKENS + r * SUB : h * TOKENS + (r + 1) * SUB] for z in range(Z) for h in range(2)]
            kf[n : n + FULL, :] = jnp.concatenate(whole, axis=1)
            for d in range(2):
                first = d * TOKENS + r * SUB
                shared = [ref[z, FULL:CHUNK, first : first + SUB] for z in range(Z)]
                kh[n + d * HALF : n + (d + 1) * HALF, :] = jnp.concatenate(shared, axis=1)


def keys_laid(own, other):
    return pl.pallas_call(
        lay_keys,
        out_shape=tuple(jax.ShapeDtypeStruct(s, bf16) for s in KEY_SHAPES),
        in_specs=[VMEM, VMEM],
        out_specs=(VMEM,) * 2,
        compiler_params=PARAMS,
        cost_estimate=LAYOUT,
    )(own, other)


def score_kernel(me_ref, kf0, kh0, own, other, *rest):
    qs, out, (qf, qh, kf1, kh1) = rest[:Z], rest[Z], rest[Z + 1 :]
    lay_keys(own, other, kf1, kh1)
    for n in range(2 * ROWS):
        t = jnp.concatenate([q[:, n * SUB : (n + 1) * SUB] for q in qs], axis=1)
        qf[n * FULL : (n + 1) * FULL, :] = t[:FULL]
        qh[n * FULL : (n + 1) * FULL, :] = t[FULL:]
    first = 0
    for a, b in ((qf, kf0), (qf, kf1), (qh, kh0), (qh, kh1)):
        t = dot(a[...], b[...], 0, 0)
        for s in range(Z):
            source = lax.rem(me_ref[2] - s + Z, Z)
            out[source, :, first : first + t.shape[1]] = t[s * SUB : (s + 1) * SUB]
        first += t.shape[1]


def score(me, qs, laid, own, other):
    rows = 2 * ROWS * FULL
    return pl.pallas_call(
        score_kernel,
        out_shape=jax.ShapeDtypeStruct((PEERS, SUB, KEYS + KEYS // 2), f32),
        in_specs=[SMEM] + [VMEM] * (4 + Z),
        out_specs=VMEM,
        scratch_shapes=[pltpu.VMEM((rows, QUERIES), bf16)] * 2 + [pltpu.VMEM(s, bf16) for s in KEY_SHAPES],
        compiler_params=PARAMS,
    )(me, *laid, own, other, *qs)


def total_kernel(parts, full, half):
    t = parts[0]
    for p in range(1, PEERS):
        t = t + parts[p]
    full[...] = t[:, :KEYS]
    half[...] = t[:, KEYS:]


def total(parts):
    return pl.pallas_call(
        total_kernel,
        out_shape=tuple(jax.ShapeDtypeStruct((SUB, n), f32) for n in (KEYS, KEYS // 2)),
        in_specs=[VMEM],
        out_specs=(VMEM,) * 2,
        compiler_params=PARAMS,
    )(parts)


def softmax_kernel(factor, full, half, other, out):
    for i, logits in enumerate((full[...], jnp.concatenate([half[...], other[...]], axis=1))):
        logits = logits * factor
        powered = jnp.exp(logits - jnp.max(logits, axis=-1, keepdims=True))
        probs = (powered / jnp.sum(powered, axis=-1, keepdims=True)).astype(bf16)
        for p in range(PEERS):
            out[p, i] = probs


def softmax(factor, full, half, other):
    return pl.pallas_call(
        functools.partial(softmax_kernel, factor),
        out_shape=jax.ShapeDtypeStruct((PEERS, 2, SUB, KEYS), bf16),
        in_specs=[VMEM] * 3,
        out_specs=VMEM,
        compiler_params=PARAMS,
    )(full, half, other)


def values_kernel(me_ref, v00, v01, v10, v11, vf, vh):
    z = me_ref[2]
    odd = lax.rem(z, 2)
    where = [lax.rem(z - source + Z, Z) for source in range(Z)]
    for cr, refs in enumerate(((v00, v01), (v10, v11))):
        halves = [
            ref[i, FULL:CHUNK, pl.ds(pl.multiple_of(h * TOKENS, TOKENS), TOKENS)]
            for h in (odd, 1 - odd)
            for ref in refs
            for i in where
        ]
        whole = [ref[i, 0:FULL, h * TOKENS : (h + 1) * TOKENS] for ref in refs for i in where for h in range(2)]
        for r in range(ROWS):
            n = cr * ROWS + r
            lanes = slice(r * SUB, (r + 1) * SUB)
            vf[n * FULL : (n + 1) * FULL, :] = jnp.concatenate([b[:, lanes] for b in whole], axis=1)
            vh[n * HALF : (n + 1) * HALF, :] = jnp.concatenate([b[:, lanes] for b in halves], axis=1)


def values_laid(me, vs):
    return pl.pallas_call(
        values_kernel,
        out_shape=tuple(jax.ShapeDtypeStruct((2 * ROWS * n, KEYS), bf16) for n in (FULL, HALF)),
        in_specs=[SMEM] + [VMEM] * 4,
        out_specs=(VMEM,) * 2,
        compiler_params=PARAMS,
        cost_estimate=LAYOUT,
    )(me, *vs)


def mix_kernel(me_ref, vf, vh, p_ref, o_ref):
    core = me_ref[1]
    for i, (v, first, n) in enumerate(((vf, 0, FULL), (vh, FULL, HALF))):
        probs = p_ref[:, i].reshape(QUERIES, KEYS)
        for cr in range(2):
            c = jnp.bitwise_xor(core, cr)
            mixed = dot(v[cr * ROWS * n : (cr + 1) * ROWS * n, :], probs, 1, 1).astype(bf16)
            for s in range(PEERS):
                o_ref[2 * s + c, first : first + n, :] = jnp.concatenate(
                    [mixed[r * n : (r + 1) * n, s * SUB : (s + 1) * SUB] for r in range(ROWS)], axis=1
                )


def mix(me, laid, probs):
    return pl.pallas_call(
        mix_kernel,
        out_shape=jax.ShapeDtypeStruct((2 * Z, CHUNK, ROWS * SUB), bf16),
        in_specs=[SMEM] + [VMEM] * 3,
        out_specs=VMEM,
        compiler_params=PARAMS,
    )(me, *laid, probs)


def final_kernel(m_ref, w_ref, o_ref, t_ref):
    for c in range(2):
        for z in range(Z):
            (a, na), (b, nb) = chunk_pieces(z)
            t_ref[a : a + na, :] = m_ref[2 * z + c, 0:FULL, :]
            t_ref[b : b + nb, :] = m_ref[2 * z + c, FULL:CHUNK, :]
        attended = dot(t_ref[...], w_ref[...], 0, 0).astype(bf16)
        o_ref[:, c * SUB : (c + 1) * SUB, :] = attended.reshape(ROWS, SUB, EMBED)


def final(m, w):
    return pl.pallas_call(
        final_kernel,
        out_shape=jax.ShapeDtypeStruct((ROWS, RES, EMBED), bf16),
        in_specs=[VMEM] * 2,
        out_specs=VMEM,
        scratch_shapes=[pltpu.VMEM((EMBED, ROWS * SUB), bf16)],
        compiler_params=PARAMS,
    )(m, w)


def flip(x, axes, n, s):
    return lax.ppermute(x, axes, [(i, i ^ s) for i in range(n)])


def gather4(own):
    far = flip(own, "xl", 2, 1)
    return own, far, flip(own, "c", 2, 1), flip(far, "c", 2, 1)


ORDER = (1, 7, 2, 6, 3, 5, 4)
WINDOW = 4


class Stream:
    def __init__(self):
        self.got = []

    def send(self, x, axis, permutation):
        if len(self.got) >= WINDOW:
            x, self.got[-WINDOW] = lax.optimization_barrier((x, self.got[-WINDOW]))
        self.got.append(lax.ppermute(x, axis, permutation))
        return len(self.got) - 1

    def spread(self, pieces):
        return {s: self.send(pieces[s], "z", [(i, (i + s) % Z) for i in range(Z)]) for s in ORDER}

    def arrived(self, own, places):
        return [own] + [self.got[places[s]] for s in range(1, Z)]


def local(x, wq, wk, wv, wf):
    me = jnp.stack([lax.axis_index(("y", "xh")), lax.axis_index("c"), lax.axis_index("z")])
    me = me.astype(jnp.int32)
    n, give, k = key_chunks(me, x, wk)
    k = lax.all_to_all(k, "z", 0, 0, tiled=True)
    q = query_chunks(me, n, flip(give, "c", 2, 1), wq)
    v = value_chunks(me, n, wv)
    stream = Stream()
    q_places = stream.spread(q)
    first = q_places[ORDER[0]]
    k, stream.got[first] = lax.optimization_barrier((k, stream.got[first]))
    far = flip(k, "xl", 2, 1)
    near = stream.send(k, "c", [(0, 1), (1, 0)])
    v_places = stream.spread(v)
    k_near = stream.got[near]
    scores = score(me, stream.arrived(q[0], q_places), keys_laid(k, k_near), far, flip(far, "c", 2, 1))
    parts = lax.all_to_all(scores, ("y", "xh"), 0, 0, tiled=True)
    vs = gather4(jnp.stack(stream.arrived(v[0], v_places)))
    full, half = total(parts)
    rows = ROWS * 2 * PEERS
    probs = softmax(1.0 / math.sqrt(DH * rows), full, half, flip(half, "z", Z, 1))
    probs = lax.all_to_all(probs, ("y", "xh"), 0, 0, tiled=True)
    mixed = lax.all_to_all(mix(me, values_laid(me, vs), probs), ("z", "c"), 0, 0, tiled=True)
    return final(mixed, wf)


def solution(mesh):
    fine = Mesh(mesh.devices.reshape(4, 2, 2, 8, 2), ("y", "xh", "c", "z", "xl"))
    spec = P(("y", "xh", "c"), ("z", "xl"), None)
    return jax.shard_map(
        local,
        mesh=fine,
        in_specs=(spec, P(), P(), P(), P()),
        out_specs=spec,
        check_vma=False,
    )
```

time: 192 us -> 190 us (0.990)
  blocking collectives: 30.9 us -> 38.3 us
  starting transfers between devices: 67.9 us -> 63.1 us
  Pallas kernels: 16.5 us -> 20.5 us
  waiting for transfers between devices: 60.7 us -> 56.7 us
  local copies, waits for them, and re-layouts: 14.6 us -> 11.1 us
    all_to_all x1, waiting for transfers between devices: 0.01 us -> 15.5 us  [local(): parts = lax.all_to_all(scores, ('y', 'xh'), 0, 0, tiled=True)]
    ppermute x7, waiting for transfers between devices: 19.3 us -> 5.12 us  [flip(): return lax.ppermute(x, axes, [(i, i ^ s) for i in range(n)])]
    all_to_all x1, blocking collectives: 30.9 us -> 38.3 us  [local(): lax.all_to_all(mix(me, values_laid(me, vs), probs), ('z', 'c'), 0, 0, til...]
    ppermute x14 -> x15, waiting for transfers between devices: 37.5 us -> 33.3 us  [send(): self.got.append(lax.ppermute(x, axis, permutation))]
    ppermute x14 -> x15, starting transfers between devices: 32.2 us -> 28.4 us  [send(): self.got.append(lax.ppermute(x, axis, permutation))]
    all_to_all x1, starting transfers between devices: 7.17 us -> 3.62 us  [local(): probs = lax.all_to_all(probs, ('y', 'xh'), 0, 0, tiled=True)]
    all_to_all x1, waiting for transfers between devices: 3.93 us -> 0.95 us  [local(): probs = lax.all_to_all(probs, ('y', 'xh'), 0, 0, tiled=True)]
    all_to_all x1, starting transfers between devices: 6.31 us -> 9.14 us  [local(): k = lax.all_to_all(k, 'z', 0, 0, tiled=True)]
  transfers between devices with their start and end apart: 24 -> 25, of which waited for: 11 -> 14; matrix products, arithmetic and copies ran while one was open for 2% -> 0% of each run, Pallas kernels for 4% -> 7%
where the time goes in v4:
time: 190 us
  starting transfers between devices  63.1 us (33%)
  waiting for transfers between devices  56.7 us (30%)
  blocking collectives  38.3 us (20%)
  Pallas kernels  20.5 us (11%)
  local copies, waits for them, and re-layouts  11.1 us (6%)
    all_to_all x1, blocking collectives, local(): lax.all_to_all(mix(me, values_laid(me, vs), probs), ('z', 'c'), 0, 0, til...  38.3 us
    ppermute x15, waiting for transfers between devices, send(): self.got.append(lax.ppermute(x, axis, permutation))  33.3 us
    ppermute x15, starting transfers between devices, send(): self.got.append(lax.ppermute(x, axis, permutation))  28.4 us
    ppermute x7, starting transfers between devices, flip(): return lax.ppermute(x, axes, [(i, i ^ s) for i in range(n)])  15.5 us
    all_to_all x1, waiting for transfers between devices, local(): parts = lax.all_to_all(scores, ('y', 'xh'), 0, 0, tiled=True)  15.5 us
    unnamed x37, local copies, waits for them, and re-layouts  11.1 us
    all_to_all x1, starting transfers between devices, local(): k = lax.all_to_all(k, 'z', 0, 0, tiled=True)  9.14 us
    all_to_all x1, starting transfers between devices, local(): parts = lax.all_to_all(scores, ('y', 'xh'), 0, 0, tiled=True)  6.49 us
  transfers between devices with their start and end apart: 25, of which 14 were waited for; matrix products, arithmetic and copies ran while one was open for 0% of the time, Pallas kernels for 7%

profile of v4, /device:TPU:1, one launch (start us, length us, event | category | flops | bytes accessed | tf_op | source)
XLA Modules:
  0.0 189.9 jit_solution(8168534598120600676)
XLA Ops:
  2.5 2.7 %shard_map.55 = (bf16[2,8,32,768]{3,2,1,0:T(8,128)(2,1)S(1)}, bf16[8,32,768]{2,1,0:T(8,128)(2,1)S(1)}, bf16[8,96,512]{2,1,0:T(8,128)(2,1)}) custom-call(s32[3]{0:T(128)S(1)} %pad_add_fusion.me_ref, bf16[8,64,768]{2,1,0:T(8,128)(2,1)S(1)} %copy-done.7, bf16[768,768]{1,0:T(8,128)(2,1)S(1)} %copy-done.1), custom_call_target="tpu_custom_call" | custom-call | tf_op jit(solution)/shard_map/pallas_call | solution.py:77
  5.2 9.1 %all-to-all-start = ((bf16[8,96,512]{2,1,0:T(8,128)(2,1)}), bf16[8,96,512]{2,1,0:T(8,128)(2,1)S(1)}, u32[]{:S(2)}, u32[]{:S(2)}) async-start(bf16[8,96,512]{2,1,0:T(8,128)(2,1)} %get-tuple-element.81), calls=%async_computation | async-start | bytes 1572864 | tf_op jit(solution)/shard_map/all_to_all | solution.py:330
  15.3 1.3 collective-permute-done.got_ref
  16.7 1.4 shard_map.57
  19.4 1.7 collective-permute-start.1
  21.2 14.8 %collective-permute-done.1.rest_1_ = bf16[128,512]{1,0:T(8,128)(2,1)S(1)} collective-permute-done((bf16[128,512]{1,0:T(8,128)(2,1)S(1)}, bf16[128,512]{1,0:T(8,128)(2,1)S(1)}, u32[]{:S(2)}, u32[]{:S(2)}) %collective-permute-start.1) | collective-permute-done | bytes 131104 | tf_op jit(solution)/shard_map/ppermute | solution.py:316
  36.0 1.8 all-to-all-done.own
  39.5 3.9 %collective-permute-done.9.rest_7_ = bf16[128,512]{1,0:T(8,128)(2,1)S(1)} collective-permute-done((bf16[128,512]{1,0:T(8,128)(2,1)}, bf16[128,512]{1,0:T(8,128)(2,1)S(1)}, u32[]{:S(2)}, u32[]{:S(2)}) %collective-permute-start.9) | collective-permute-done | bytes 131104 | tf_op jit(solution)/shard_map/ppermute | solution.py:316
  43.3 3.4 %collective-permute-start.10 = (bf16[128,512]{1,0:T(8,128)(2,1)S(1)}, bf16[128,512]{1,0:T(8,128)(2,1)S(1)}, u32[]{:S(2)}, u32[]{:S(2)}) collective-permute-start(bf16[128,512]{1,0:T(8,128)(2,1)S(1)} %get-tuple-element.77), channel_id=1, source_target_pairs={{0,10},{2,12},{4,14},{6,0},{8,2},{10,4},{12,6},{14,8},{1,11},{3,13... | collective-permute-start | bytes 393224 | tf_op jit(solution)/shard_map/ppermute | solution.py:316
  46.8 4.6 %collective-permute-start.5 = (bf16[128,512]{1,0:T(8,128)(2,1)S(1)}, bf16[128,512]{1,0:T(8,128)(2,1)S(1)}, u32[]{:S(2)}, u32[]{:S(2)}) collective-permute-start(bf16[128,512]{1,0:T(8,128)(2,1)S(1)} %get-tuple-element.68), channel_id=1, source_target_pairs={{0,8},{2,10},{4,12},{6,14},{8,0},{10,2},{12,4},{14,6},{1,9},{3,11}... | collective-permute-start | bytes 393224 | tf_op jit(solution)/shard_map/ppermute | solution.py:316
  51.4 3.1 %collective-permute-start.13 = (bf16[128,512]{1,0:T(8,128)(2,1)S(1)}, bf16[128,512]{1,0:T(8,128)(2,1)S(1)}, u32[]{:S(2)}, u32[]{:S(2)}) collective-permute-start(bf16[128,512]{1,0:T(8,128)(2,1)S(1)} %get-tuple-element.84), channel_id=1, source_target_pairs={{0,12},{2,14},{4,0},{6,2},{8,4},{10,6},{12,8},{14,10},{1,13},{3,15... | collective-permute-start | bytes 393224 | tf_op jit(solution)/shard_map/ppermute | solution.py:316
  55.8 2.1 %shard_map.56 = (bf16[96,512]{1,0:T(8,128)(2,1)S(1)}, bf16[96,512]{1,0:T(8,128)(2,1)S(1)}, bf16[96,512]{1,0:T(8,128)(2,1)S(1)}, bf16[96,512]{1,0:T(8,128)(2,1)S(...) custom-call(s32[3]{0:T(128)S(1)} %pad_add_fusion.me_ref, ...), custom_call_target="tpu_custom_call" | custom-call | flops 603979776 | bytes 2752512 | tf_op jit(solution)/shard_map/pallas_call | solution.py:123
  58.5 7.6 %collective-permute-done.2.rest_3_ = bf16[128,512]{1,0:T(8,128)(2,1)S(1)} collective-permute-done((bf16[128,512]{1,0:T(8,128)(2,1)S(1)}, bf16[128,512]{1,0:T(8,128)(2,1)S(1)}, u32[]{:S(2)}, u32[]{:S(2)}) %collective-permute-start.2) | collective-permute-done | bytes 131104 | tf_op jit(solution)/shard_map/ppermute | solution.py:316
  66.2 1.7 collective-permute-start.3
  67.9 2.4 %collective-permute-start.14 = (bf16[8,96,512]{2,1,0:T(8,128)(2,1)S(1)}, bf16[8,96,512]{2,1,0:T(8,128)(2,1)S(1)}, u32[]{:S(2)}, u32[]{:S(2)}) collective-permute-start(bf16[8,96,512]{2,1,0:T(8,128)(2,1)S(1)} %all-to-all-done.own), channel_id=1, source_target_pairs={{0,16},{16,0},{1,17},{17,1},{2,18},{18,2},{3,19},{19,3},{4,20},{20... | collective-permute-start | bytes 2359304 | tf_op jit(solution)/shard_map/ppermute | solution.py:316
  70.6 4.0 %collective-permute-start.12 = (bf16[96,512]{1,0:T(8,128)(2,1)}, bf16[96,512]{1,0:T(8,128)(2,1)S(1)}, u32[]{:S(2)}, u32[]{:S(2)}) collective-permute-start(bf16[96,512]{1,0:T(8,128)(2,1)} %get-tuple-element.79), channel_id=1, source_target_pairs={{0,10},{2,12},{4,14},{6,0},{8,2},{10,4},{12,6},{14,8},{1,11},{3,13... | collective-permute-start | bytes 294920 | tf_op jit(solution)/shard_map/ppermute | solution.py:316
  75.0 3.1 %collective-permute-start.7 = (bf16[96,512]{1,0:T(8,128)(2,1)S(1)}, bf16[96,512]{1,0:T(8,128)(2,1)S(1)}, u32[]{:S(2)}, u32[]{:S(2)}) collective-permute-start(bf16[96,512]{1,0:T(8,128)(2,1)S(1)} %get-tuple-element.71), channel_id=1, source_target_pairs={{0,6},{2,8},{4,10},{6,12},{8,14},{10,0},{12,2},{14,4},{1,7},{3,9},... | collective-permute-start | bytes 294920 | tf_op jit(solution)/shard_map/ppermute | solution.py:316
  78.2 3.1 %collective-permute-start.8 = (bf16[96,512]{1,0:T(8,128)(2,1)}, bf16[96,512]{1,0:T(8,128)(2,1)S(1)}, u32[]{:S(2)}, u32[]{:S(2)}) collective-permute-start(bf16[96,512]{1,0:T(8,128)(2,1)} %get-tuple-element.72), channel_id=1, source_target_pairs={{0,8},{2,10},{4,12},{6,14},{8,0},{10,2},{12,4},{14,6},{1,9},{3,11}... | collective-permute-start | bytes 294920 | tf_op jit(solution)/shard_map/ppermute | solution.py:316
  81.3 2.7 %collective-permute-done.7 = bf16[96,512]{1,0:T(8,128)(2,1)S(1)} collective-permute-done((bf16[96,512]{1,0:T(8,128)(2,1)S(1)}, bf16[96,512]{1,0:T(8,128)(2,1)S(1)}, u32[]{:S(2)}, u32[]{:S(2)}) %collective-permute-start.7) | collective-permute-done | bytes 98336 | tf_op jit(solution)/shard_map/ppermute | solution.py:316
  84.0 1.3 shard_map.59
  85.3 5.0 %shard_map.60 = f32[8,32,1536]{2,1,0:T(8,128)} custom-call(s32[3]{0:T(128)S(1)} %pad_add_fusion.me_ref, bf16[1024,512]{1,0:T(8,128)(2,1)S(1)} %get-tuple-element.91.kf0, bf16[1024,256]{1,0:T(8,128)(2,1)S(1)} %get-tuple-element.92.kh0, bf16[8,96,512]{2,1,0:T(8,128)(2,1)S(1)} %collective-permute-done.19.own, ...), custom_call_target="tpu_custom_call" | custom-call | tf_op jit(solution)/shard_map/pallas_call | solution.py:175
  90.3 6.5 %all-to-all-start.1 = ((f32[8,32,1536]{2,1,0:T(8,128)}), f32[8,32,1536]{2,1,0:T(8,128)S(1)}, u32[]{:S(2)}, u32[]{:S(2)}) async-start(f32[8,32,1536]{2,1,0:T(8,128)} %shard_map.60), calls=%async_computation.1 | async-start | bytes 3145728 | tf_op jit(solution)/shard_map/all_to_all | solution.py:342
  97.6 3.7 %collective-permute-done.15 = bf16[96,512]{1,0:T(8,128)(2,1)S(1)} collective-permute-done((bf16[96,512]{1,0:T(8,128)(2,1)S(1)}, bf16[96,512]{1,0:T(8,128)(2,1)S(1)}, u32[]{:S(2)}, u32[]{:S(2)}) %collective-permute-start.15) | collective-permute-done | bytes 98336 | tf_op jit(solution)/shard_map/ppermute | solution.py:316
  101.4 15.5 %all-to-all-done.1.parts = f32[8,32,1536]{2,1,0:T(8,128)S(1)} async-done(((f32[8,32,1536]{2,1,0:T(8,128)}), f32[8,32,1536]{2,1,0:T(8,128)S(1)}, u32[]{:S(2)}, u32[]{:S(2)}) %all-to-all-start.1) | async-done | bytes 1572896 | tf_op jit(solution)/shard_map/all_to_all | solution.py:342
  117.0 9.1 %collective-permute-start.21 = (f32[32,512]{1,0:T(8,128)S(1)}, f32[32,512]{1,0:T(8,128)S(1)}, u32[]{:S(2)}, u32[]{:S(2)}) collective-permute-start(f32[32,512]{1,0:T(8,128)S(1)} %get-tuple-element.102.half), channel_id=1, source_target_pairs={{0,2},{2,0},{4,6},{6,4},{8,10},{10,8},{12,14},{14,12},{1,3},{3,1},... | collective-permute-start | bytes 196616 | tf_op jit(solution)/shard_map/ppermute | solution.py:297
  126.1 2.0 %collective-permute-done.21.other = f32[32,512]{1,0:T(8,128)S(1)} collective-permute-done((f32[32,512]{1,0:T(8,128)S(1)}, f32[32,512]{1,0:T(8,128)S(1)}, u32[]{:S(2)}, u32[]{:S(2)}) %collective-permute-start.21) | collective-permute-done | bytes 65568 | tf_op jit(solution)/shard_map/ppermute | solution.py:297
  129.3 3.6 %all-to-all-start.2 = ((bf16[8,2,32,1024]{3,2,1,0:T(8,128)(2,1)}), bf16[8,2,32,1024]{3,2,1,0:T(8,128)(2,1)S(1)}, u32[]{:S(2)}, u32[]{:S(2)}) async-start(bf16[8,2,32,1024]{3,2,1,0:T(8,128)(2,1)} %shard_map.62), calls=%async_computation.2 | async-start | bytes 2097152 | tf_op jit(solution)/shard_map/all_to_all | solution.py:347
  132.9 3.5 %collective-permute-start.17 = (bf16[8,96,512]{2,1,0:T(8,128)(2,1)S(1)}, bf16[8,96,512]{2,1,0:T(8,128)(2,1)S(1)}, u32[]{:S(2)}, u32[]{:S(2)}) collective-permute-start(bf16[8,96,512]{2,1,0:T(8,128)(2,1)S(1)} %bitcast_dynamic-update-slice_fusion.v00), channel_id=1, source_target_pairs={{0,16},{16,0},{1,17},{17,1},{2,18},{18,2},{3,19},{19,3},{4,20},{20... | collective-permute-start | bytes 2359304 | tf_op jit(solution)/shard_map/ppermute | solution.py:297
  141.8 3.1 %shard_map.58 = (bf16[1024,1024]{1,0:T(8,128)(2,1)S(1)}, bf16[512,1024]{1,0:T(8,128)(2,1)S(1)}) custom-call(s32[3]{0:T(128)S(1)} %pad_add_fusion.me_ref, bf16[8,96,512]{2,1,0:T(8,128)(2,1)S(1)} %copy-done.6, bf16[8,96,512]{2,1,0:T(8,128)(2,1)S(1)} %copy-done.9, bf16[8,96,512]{2,1,0:T(8,128)(2,1)S(1)} %collective-permute-done.17.v10, ...), custom_call_target="tpu_custom_call" | custom-call | bytes 6291456 | tf_op jit(solution)/shard_map/pallas_call | solution.py:242
  148.0 1.9 shard_map.63
  149.9 38.3 %all_to_all.20.m_ref = bf16[16,96,256]{2,1,0:T(8,128)(2,1)S(1)} all-to-all(bf16[16,96,256]{2,1,0:T(8,128)(2,1)S(1)} %shard_map.63), channel_id=1, replica_groups=mesh['y'=4,'xh'=2,'c'=2,'z'=8,'xl'=2] {'z','c'}, dimensions={0} | all-to-all | bytes 1572864 | tf_op jit(solution)/shard_map/all_to_all | solution.py:348
  188.2 1.7 shard_map.64
  (68 shorter events, 19.9 us)
Async XLA Ops:
  0.1 1.3 copy-start.1
  5.2 11.5 %copy-start = (bf16[768,768]{1,0:T(8,128)(2,1)S(1)}, bf16[768,768]{1,0:T(8,128)(2,1)}, u32[]{:S(2)}) copy-start(bf16[768,768]{1,0:T(8,128)(2,1)} %w_ref.6) | copy-start | bytes 3538948
  5.2 32.6 %all-to-all-start = ((bf16[8,96,512]{2,1,0:T(8,128)(2,1)}), bf16[8,96,512]{2,1,0:T(8,128)(2,1)S(1)}, u32[]{:S(2)}, u32[]{:S(2)}) async-start(bf16[8,96,512]{2,1,0:T(8,128)(2,1)} %get-tuple-element.81), calls=%async_computation | async-start | bytes 1572864 | tf_op jit(solution)/shard_map/all_to_all | solution.py:330
  14.3 2.3 %collective-permute-start = (bf16[8,32,768]{2,1,0:T(8,128)(2,1)S(1)}, bf16[8,32,768]{2,1,0:T(8,128)(2,1)S(1)}, u32[]{:S(2)}, u32[]{:S(2)}) collective-permute-start(bf16[8,32,768]{2,1,0:T(8,128)(2,1)S(1)} %get-tuple-element.58), channel_id=1, source_target_pairs={{0,16},{16,0},{1,17},{17,1},{2,18},{18,2},{3,19},{19,3},{4,20},{20... | collective-permute-start | bytes 1179656 | tf_op jit(solution)/shard_map/ppermute | solution.py:297
  19.4 16.6 %collective-permute-start.1 = (bf16[128,512]{1,0:T(8,128)(2,1)S(1)}, bf16[128,512]{1,0:T(8,128)(2,1)S(1)}, u32[]{:S(2)}, u32[]{:S(2)}) collective-permute-start(bf16[128,512]{1,0:T(8,128)(2,1)S(1)} %get-tuple-element.60), channel_id=1, source_target_pairs={{0,2},{2,4},{4,6},{6,8},{8,10},{10,12},{12,14},{14,0},{1,3},{3,5},... | collective-permute-start | bytes 393224 | tf_op jit(solution)/shard_map/ppermute | solution.py:316
  37.8 32.5 %collective-permute-start.19 = (bf16[8,96,512]{2,1,0:T(8,128)(2,1)S(1)}, bf16[8,96,512]{2,1,0:T(8,128)(2,1)S(1)}, u32[]{:S(2)}, u32[]{:S(2)}) collective-permute-start(bf16[8,96,512]{2,1,0:T(8,128)(2,1)S(1)} %all-to-all-done.own), channel_id=1, source_target_pairs={{0,1},{1,0},{2,3},{3,2},{4,5},{5,4},{6,7},{7,6},{8,9},{9,8},{10,11... | collective-permute-start | bytes 2359304 | tf_op jit(solution)/shard_map/ppermute | solution.py:297
  39.0 4.3 %collective-permute-start.9 = (bf16[128,512]{1,0:T(8,128)(2,1)}, bf16[128,512]{1,0:T(8,128)(2,1)S(1)}, u32[]{:S(2)}, u32[]{:S(2)}) collective-permute-start(bf16[128,512]{1,0:T(8,128)(2,1)} %copy-done.12), channel_id=1, source_target_pairs={{0,14},{2,0},{4,2},{6,4},{8,6},{10,8},{12,10},{14,12},{1,15},{3,1}... | collective-permute-start | bytes 393224 | tf_op jit(solution)/shard_map/ppermute | solution.py:316
  39.4 7.4 %collective-permute-start.4 = (bf16[128,512]{1,0:T(8,128)(2,1)}, bf16[128,512]{1,0:T(8,128)(2,1)S(1)}, u32[]{:S(2)}, u32[]{:S(2)}) collective-permute-start(bf16[128,512]{1,0:T(8,128)(2,1)} %copy-done.11), channel_id=1, source_target_pairs={{0,4},{2,6},{4,8},{6,10},{8,12},{10,14},{12,0},{14,2},{1,5},{3,7},... | collective-permute-start | bytes 393224 | tf_op jit(solution)/shard_map/ppermute | solution.py:316
  43.3 15.2 %collective-permute-start.10 = (bf16[128,512]{1,0:T(8,128)(2,1)S(1)}, bf16[128,512]{1,0:T(8,128)(2,1)S(1)}, u32[]{:S(2)}, u32[]{:S(2)}) collective-permute-start(bf16[128,512]{1,0:T(8,128)(2,1)S(1)} %get-tuple-element.77), channel_id=1, source_target_pairs={{0,10},{2,12},{4,14},{6,0},{8,2},{10,4},{12,6},{14,8},{1,11},{3,13... | collective-permute-start | bytes 393224 | tf_op jit(solution)/shard_map/ppermute | solution.py:316
  46.8 11.7 %collective-permute-start.5 = (bf16[128,512]{1,0:T(8,128)(2,1)S(1)}, bf16[128,512]{1,0:T(8,128)(2,1)S(1)}, u32[]{:S(2)}, u32[]{:S(2)}) collective-permute-start(bf16[128,512]{1,0:T(8,128)(2,1)S(1)} %get-tuple-element.68), channel_id=1, source_target_pairs={{0,8},{2,10},{4,12},{6,14},{8,0},{10,2},{12,4},{14,6},{1,9},{3,11}... | collective-permute-start | bytes 393224 | tf_op jit(solution)/shard_map/ppermute | solution.py:316
  51.4 14.8 %collective-permute-start.2 = (bf16[128,512]{1,0:T(8,128)(2,1)S(1)}, bf16[128,512]{1,0:T(8,128)(2,1)S(1)}, u32[]{:S(2)}, u32[]{:S(2)}) collective-permute-start(bf16[128,512]{1,0:T(8,128)(2,1)S(1)} %get-tuple-element.61), channel_id=1, source_target_pairs={{0,6},{2,8},{4,10},{6,12},{8,14},{10,0},{12,2},{14,4},{1,7},{3,9},... | collective-permute-start | bytes 393224 | tf_op jit(solution)/shard_map/ppermute | solution.py:316
  51.4 16.5 %collective-permute-start.13 = (bf16[128,512]{1,0:T(8,128)(2,1)S(1)}, bf16[128,512]{1,0:T(8,128)(2,1)S(1)}, u32[]{:S(2)}, u32[]{:S(2)}) collective-permute-start(bf16[128,512]{1,0:T(8,128)(2,1)S(1)} %get-tuple-element.84), channel_id=1, source_target_pairs={{0,12},{2,14},{4,0},{6,2},{8,4},{10,6},{12,8},{14,10},{1,13},{3,15... | collective-permute-start | bytes 393224 | tf_op jit(solution)/shard_map/ppermute | solution.py:316
  54.5 1.3 copy-start.10
  66.2 4.4 %collective-permute-start.11 = (bf16[96,512]{1,0:T(8,128)(2,1)S(1)}, bf16[96,512]{1,0:T(8,128)(2,1)S(1)}, u32[]{:S(2)}, u32[]{:S(2)}) collective-permute-start(bf16[96,512]{1,0:T(8,128)(2,1)S(1)} %get-tuple-element.78), channel_id=1, source_target_pairs={{0,14},{2,0},{4,2},{6,4},{8,6},{10,8},{12,10},{14,12},{1,15},{3,1}... | collective-permute-start | bytes 294920 | tf_op jit(solution)/shard_map/ppermute | solution.py:316
  66.2 8.4 %collective-permute-start.6 = (bf16[96,512]{1,0:T(8,128)(2,1)S(1)}, bf16[96,512]{1,0:T(8,128)(2,1)S(1)}, u32[]{:S(2)}, u32[]{:S(2)}) collective-permute-start(bf16[96,512]{1,0:T(8,128)(2,1)S(1)} %get-tuple-element.69), channel_id=1, source_target_pairs={{0,4},{2,6},{4,8},{6,10},{8,12},{10,14},{12,0},{14,2},{1,5},{3,7},... | collective-permute-start | bytes 294920 | tf_op jit(solution)/shard_map/ppermute | solution.py:316
  66.2 8.9 %collective-permute-start.3 = (bf16[96,512]{1,0:T(8,128)(2,1)S(1)}, bf16[96,512]{1,0:T(8,128)(2,1)S(1)}, u32[]{:S(2)}, u32[]{:S(2)}) collective-permute-start(bf16[96,512]{1,0:T(8,128)(2,1)S(1)} %get-tuple-element.62), channel_id=1, source_target_pairs={{0,2},{2,4},{4,6},{6,8},{8,10},{10,12},{12,14},{14,0},{1,3},{3,5},... | collective-permute-start | bytes 294920 | tf_op jit(solution)/shard_map/ppermute | solution.py:316
  67.9 16.2 %collective-permute-start.14 = (bf16[8,96,512]{2,1,0:T(8,128)(2,1)S(1)}, bf16[8,96,512]{2,1,0:T(8,128)(2,1)S(1)}, u32[]{:S(2)}, u32[]{:S(2)}) collective-permute-start(bf16[8,96,512]{2,1,0:T(8,128)(2,1)S(1)} %all-to-all-done.own), channel_id=1, source_target_pairs={{0,16},{16,0},{1,17},{17,1},{2,18},{18,2},{3,19},{19,3},{4,20},{20... | collective-permute-start | bytes 2359304 | tf_op jit(solution)/shard_map/ppermute | solution.py:316
  70.3 15.0 %collective-permute-start.20 = (bf16[8,96,512]{2,1,0:T(8,128)(2,1)S(1)}, bf16[8,96,512]{2,1,0:T(8,128)(2,1)S(1)}, u32[]{:S(2)}, u32[]{:S(2)}) collective-permute-start(bf16[8,96,512]{2,1,0:T(8,128)(2,1)S(1)} %collective-permute-done.19.own), channel_id=1, source_target_pairs={{0,16},{16,0},{1,17},{17,1},{2,18},{18,2},{3,19},{19,3},{4,20},{20... | collective-permute-start | bytes 2359304 | tf_op jit(solution)/shard_map/ppermute | solution.py:297
  70.6 27.0 %collective-permute-start.12 = (bf16[96,512]{1,0:T(8,128)(2,1)}, bf16[96,512]{1,0:T(8,128)(2,1)S(1)}, u32[]{:S(2)}, u32[]{:S(2)}) collective-permute-start(bf16[96,512]{1,0:T(8,128)(2,1)} %get-tuple-element.79), channel_id=1, source_target_pairs={{0,10},{2,12},{4,14},{6,0},{8,2},{10,4},{12,6},{14,8},{1,11},{3,13... | collective-permute-start | bytes 294920 | tf_op jit(solution)/shard_map/ppermute | solution.py:316
  75.0 9.0 %collective-permute-start.7 = (bf16[96,512]{1,0:T(8,128)(2,1)S(1)}, bf16[96,512]{1,0:T(8,128)(2,1)S(1)}, u32[]{:S(2)}, u32[]{:S(2)}) collective-permute-start(bf16[96,512]{1,0:T(8,128)(2,1)S(1)} %get-tuple-element.71), channel_id=1, source_target_pairs={{0,6},{2,8},{4,10},{6,12},{8,14},{10,0},{12,2},{14,4},{1,7},{3,9},... | collective-permute-start | bytes 294920 | tf_op jit(solution)/shard_map/ppermute | solution.py:316
  78.2 18.7 %collective-permute-start.8 = (bf16[96,512]{1,0:T(8,128)(2,1)}, bf16[96,512]{1,0:T(8,128)(2,1)S(1)}, u32[]{:S(2)}, u32[]{:S(2)}) collective-permute-start(bf16[96,512]{1,0:T(8,128)(2,1)} %get-tuple-element.72), channel_id=1, source_target_pairs={{0,8},{2,10},{4,12},{6,14},{8,0},{10,2},{12,4},{14,6},{1,9},{3,11}... | collective-permute-start | bytes 294920 | tf_op jit(solution)/shard_map/ppermute | solution.py:316
  90.3 6.5 %copy-start.14 = (bf16[96,512]{1,0:T(8,128)(2,1)S(1)}, bf16[96,512]{1,0:T(8,128)(2,1)}, u32[]{:S(2)}) copy-start(bf16[96,512]{1,0:T(8,128)(2,1)} %copy-done.13) | copy-start | bytes 294916
  90.3 26.6 %all-to-all-start.1 = ((f32[8,32,1536]{2,1,0:T(8,128)}), f32[8,32,1536]{2,1,0:T(8,128)S(1)}, u32[]{:S(2)}, u32[]{:S(2)}) async-start(f32[8,32,1536]{2,1,0:T(8,128)} %shard_map.60), calls=%async_computation.1 | async-start | bytes 3145728 | tf_op jit(solution)/shard_map/all_to_all | solution.py:342
  96.9 4.4 %collective-permute-start.15 = (bf16[96,512]{1,0:T(8,128)(2,1)S(1)}, bf16[96,512]{1,0:T(8,128)(2,1)S(1)}, u32[]{:S(2)}, u32[]{:S(2)}) collective-permute-start(bf16[96,512]{1,0:T(8,128)(2,1)S(1)} %copy-done.14), channel_id=1, source_target_pairs={{0,12},{2,14},{4,0},{6,2},{8,4},{10,6},{12,8},{14,10},{1,13},{3,15... | collective-permute-start | bytes 294920 | tf_op jit(solution)/shard_map/ppermute | solution.py:316
  101.3 31.6 %copy-start.5 = (bf16[8,96,512]{2,1,0:T(8,128)(2,1)}, bf16[8,96,512]{2,1,0:T(8,128)(2,1)S(1)}, u32[]{:S(2)}) copy-start(bf16[8,96,512]{2,1,0:T(8,128)(2,1)S(1)} %bitcast_dynamic-update-slice_fusion.v00) | copy-start | bytes 2359300
  101.3 35.1 %collective-permute-start.16 = (bf16[8,96,512]{2,1,0:T(8,128)(2,1)S(1)}, bf16[8,96,512]{2,1,0:T(8,128)(2,1)S(1)}, u32[]{:S(2)}, u32[]{:S(2)}) collective-permute-start(bf16[8,96,512]{2,1,0:T(8,128)(2,1)S(1)} %bitcast_dynamic-update-slice_fusion.v00), channel_id=1, source_target_pairs={{0,1},{1,0},{2,3},{3,2},{4,5},{5,4},{6,7},{7,6},{8,9},{9,8},{10,11... | collective-permute-start | bytes 2359304 | tf_op jit(solution)/shard_map/ppermute | solution.py:297
  117.0 11.0 %collective-permute-start.21 = (f32[32,512]{1,0:T(8,128)S(1)}, f32[32,512]{1,0:T(8,128)S(1)}, u32[]{:S(2)}, u32[]{:S(2)}) collective-permute-start(f32[32,512]{1,0:T(8,128)S(1)} %get-tuple-element.102.half), channel_id=1, source_target_pairs={{0,2},{2,0},{4,6},{6,4},{8,10},{10,8},{12,14},{14,12},{1,3},{3,1},... | collective-permute-start | bytes 196616 | tf_op jit(solution)/shard_map/ppermute | solution.py:297
  129.3 17.5 %all-to-all-start.2 = ((bf16[8,2,32,1024]{3,2,1,0:T(8,128)(2,1)}), bf16[8,2,32,1024]{3,2,1,0:T(8,128)(2,1)S(1)}, u32[]{:S(2)}, u32[]{:S(2)}) async-start(bf16[8,2,32,1024]{3,2,1,0:T(8,128)(2,1)} %shard_map.62), calls=%async_computation.2 | async-start | bytes 2097152 | tf_op jit(solution)/shard_map/all_to_all | solution.py:347
  132.9 5.4 %collective-permute-start.17 = (bf16[8,96,512]{2,1,0:T(8,128)(2,1)S(1)}, bf16[8,96,512]{2,1,0:T(8,128)(2,1)S(1)}, u32[]{:S(2)}, u32[]{:S(2)}) collective-permute-start(bf16[8,96,512]{2,1,0:T(8,128)(2,1)S(1)} %bitcast_dynamic-update-slice_fusion.v00), channel_id=1, source_target_pairs={{0,16},{16,0},{1,17},{17,1},{2,18},{18,2},{3,19},{19,3},{4,20},{20... | collective-permute-start | bytes 2359304 | tf_op jit(solution)/shard_map/ppermute | solution.py:297
  136.5 3.0 %collective-permute-start.18 = (bf16[8,96,512]{2,1,0:T(8,128)(2,1)S(1)}, bf16[8,96,512]{2,1,0:T(8,128)(2,1)S(1)}, u32[]{:S(2)}, u32[]{:S(2)}) collective-permute-start(bf16[8,96,512]{2,1,0:T(8,128)(2,1)S(1)} %collective-permute-done.16.v01), channel_id=1, source_target_pairs={{0,16},{16,0},{1,17},{17,1},{2,18},{18,2},{3,19},{19,3},{4,20},{20... | collective-permute-start | bytes 2359304 | tf_op jit(solution)/shard_map/ppermute | solution.py:297
  146.8 1.2 copy-start.4
  149.9 38.3 %copy-start.2 = (bf16[768,768]{1,0:T(8,128)(2,1)S(1)}, bf16[768,768]{1,0:T(8,128)(2,1)}, u32[]{:S(2)}) copy-start(bf16[768,768]{1,0:T(8,128)(2,1)} %w_ref.7) | copy-start | bytes 3538948
  (8 other events, 7.3 us)

commit v5 on v4

v5 whole, which is shorter than its diff:
```python
import functools
import math

import jax
import jax.numpy as jnp
from jax import lax
from jax.experimental import pallas as pl
from jax.experimental.pallas import tpu as pltpu
from jax.sharding import Mesh, PartitionSpec as P

H = 12
DH = 64
EMBED = 768
ROWS = 8
RES = 64
Z = 8
CHUNK = EMBED // Z
FULL = DH
HALF = CHUNK - DH
PEERS = 8
SUB = RES // 2
TOKENS = ROWS * SUB
QUERIES = Z * SUB
KEYS = 2 * Z * RES
LOGITS = KEYS + KEYS // 2

f32 = jnp.float32
bf16 = jnp.bfloat16
PARAMS = pltpu.CompilerParams(vmem_limit_bytes=8 * 1024 * 1024)
PROJECTION = pl.CostEstimate(
    flops=2 * ROWS * RES * EMBED * EMBED, bytes_accessed=2 * EMBED * (EMBED + 2 * ROWS * RES), transcendentals=0
)
LAYOUT = pl.CostEstimate(flops=0, bytes_accessed=16 * ROWS * RES * EMBED, transcendentals=0)
KEY_SHAPES = ((2 * ROWS * FULL, KEYS // 2), (2 * ROWS * FULL, KEYS // 4))
WIDE = pltpu.CompilerParams(vmem_limit_bytes=16 * 1024 * 1024)
VMEM = pl.BlockSpec(memory_space=pltpu.VMEM)
SMEM = pl.BlockSpec(memory_space=pltpu.SMEM)
ANY = pl.BlockSpec(memory_space=pl.ANY)
HBM = pl.BlockSpec(memory_space=pltpu.HBM)


def chunk_pieces(z):
    base = z * CHUNK
    if z % 2 == 0:
        return (base, FULL), (base + FULL, HALF)
    return (base + HALF, FULL), (base, HALF)


def dot(a, b, ca, cb):
    return lax.dot_general(a, b, (((ca,), (cb,)), ((), ())), preferred_element_type=f32)


def shared_head(z):
    return z // 2 * (2 * CHUNK) + FULL


def fetches(sources, buffers, sems):
    copies = [pltpu.make_async_copy(a, b, sems.at[i]) for i, (a, b) in enumerate(zip(sources, buffers))]
    for copy in copies:
        copy.start()
    return copies


def key_kernel(x_hbm, w_hbm, n_ref, k_ref, x_ref, w_ref, sems):
    copy_x, copy_w = fetches((x_hbm, w_hbm), (x_ref, w_ref), sems)
    copy_x.wait()
    x = x_ref[...].astype(f32)
    centred = x - jnp.mean(x, axis=-1, keepdims=True)
    var = jnp.mean(centred * centred, axis=-1, keepdims=True)
    normed = (centred * lax.rsqrt(var + 1e-05)).astype(bf16)
    for h in range(2):
        n_ref[h] = normed[:, h * SUB : (h + 1) * SUB, :]
    copy_w.wait()
    t = dot(w_ref[...], n_ref[...].reshape(ROWS * RES, EMBED), 0, 1).astype(bf16)
    for z in range(Z):
        (a, _), _ = chunk_pieces(z)
        b, lanes = shared_head(z), slice(z % 2 * TOKENS, (z % 2 + 1) * TOKENS)
        k_ref[z, 0:FULL, :] = t[a : a + FULL]
        k_ref[z, FULL:CHUNK, :TOKENS] = t[b : b + HALF, lanes]
        k_ref[z, FULL:CHUNK, TOKENS:] = t[b + HALF : b + FULL, lanes]


def key_chunks(x, w):
    return pl.pallas_call(
        key_kernel,
        out_shape=(
            jax.ShapeDtypeStruct((2, ROWS, SUB, EMBED), bf16),
            jax.ShapeDtypeStruct((Z, CHUNK, ROWS * RES), bf16),
        ),
        in_specs=[HBM, HBM],
        out_specs=(VMEM,) * 2,
        scratch_shapes=[
            pltpu.VMEM((ROWS, RES, EMBED), bf16),
            pltpu.VMEM((EMBED, EMBED), bf16),
            pltpu.SemaphoreType.DMA((2,)),
        ],
        compiler_params=PARAMS,
    )(x, w)


def query_kernel(n_ref, w_ref, q_ref):
    for c in range(2):
        t = dot(w_ref[...], n_ref[c].reshape(TOKENS, EMBED), 0, 1).astype(bf16)
        for z in range(Z):
            a, b = chunk_pieces(z)[0][0], shared_head(z)
            q_ref[2 * z + c, 0:FULL, :] = t[a : a + FULL]
            q_ref[2 * z + c, FULL:, :] = t[b : b + FULL]


def query_chunks(n, w):
    return pl.pallas_call(
        query_kernel,
        out_shape=jax.ShapeDtypeStruct((2 * Z, 2 * FULL, TOKENS), bf16),
        in_specs=[VMEM] * 2,
        out_specs=VMEM,
        compiler_params=PARAMS,
        cost_estimate=PROJECTION,
    )(n, w)


def value_kernel(n_ref, w_ref, v_ref):
    t = dot(w_ref[...], n_ref[...].reshape(ROWS * RES, EMBED), 0, 1).astype(bf16)
    for z in range(Z):
        (a, na), (b, nb) = chunk_pieces(z)
        v_ref[z, 0:FULL, :] = t[a : a + na]
        v_ref[z, FULL:CHUNK, :] = t[b : b + nb]


def value_chunks(n, w):
    return pl.pallas_call(
        value_kernel,
        out_shape=jax.ShapeDtypeStruct((Z, CHUNK, ROWS * RES), bf16),
        in_specs=[VMEM, VMEM],
        out_specs=VMEM,
        compiler_params=PARAMS,
        cost_estimate=PROJECTION,
    )(n, w)


def lay_keys(own, other, kf, kh):
    for cr, ref in enumerate((own, other)):
        for r in range(ROWS):
            n = (cr * ROWS + r) * FULL
            whole = [ref[z, 0:FULL, h * TOKENS + r * SUB : h * TOKENS + (r + 1) * SUB] for z in range(Z) for h in range(2)]
            kf[n : n + FULL, :] = jnp.concatenate(whole, axis=1)
            for d in range(2):
                first = d * TOKENS + r * SUB
                shared = [ref[z, FULL:CHUNK, first : first + SUB] for z in range(Z)]
                kh[n + d * HALF : n + (d + 1) * HALF, :] = jnp.concatenate(shared, axis=1)


def keys_kernel(own, other, kf, kh, a, b, sems):
    for copy in fetches((own, other), (a, b), sems):
        copy.wait()
    lay_keys(a, b, kf, kh)


def keys_laid(own, other):
    return pl.pallas_call(
        keys_kernel,
        out_shape=tuple(jax.ShapeDtypeStruct(s, bf16) for s in KEY_SHAPES),
        in_specs=[ANY, ANY],
        out_specs=(VMEM,) * 2,
        scratch_shapes=[pltpu.VMEM(own.shape, bf16)] * 2 + [pltpu.SemaphoreType.DMA((2,))],
        compiler_params=PARAMS,
        cost_estimate=LAYOUT,
    )(own, other)


def score_kernel(me_ref, *refs):
    sources, results, rest = refs[:5], refs[5:9], refs[9:]
    outs, (qf, qh, kf1, kh1), sems = rest[5], rest[6:10], rest[10]
    own, other, q_ref, kf0, kh0 = rest[:5]
    copies = fetches(sources, rest[:5], sems)
    for copy in copies[:2]:
        copy.wait()
    lay_keys(own, other, kf1, kh1)
    for copy in copies[2:]:
        copy.wait()
    peers = [jnp.bitwise_xor(me_ref[0], 2 * s + t) for s in range(4) for t in range(2)]
    for cr in range(2):
        c = jnp.bitwise_xor(me_ref[1], cr)
        queries = [q_ref[2 * p + c] for p in peers]
        for r in range(ROWS):
            n = (cr * ROWS + r) * FULL
            t = jnp.concatenate([b[:, r * SUB : (r + 1) * SUB] for b in queries], axis=1)
            qf[n : n + FULL, :] = t[:FULL]
            qh[n : n + FULL, :] = t[FULL:]
    first = 0
    for a, b in ((qf, kf0), (qf, kf1), (qh, kh0), (qh, kh1)):
        t = dot(a[...], b[...], 0, 0)
        for p in range(PEERS):
            outs[p // 2, p % 2, :, first : first + t.shape[1]] = t[p * SUB : (p + 1) * SUB]
        first += t.shape[1]
    for copy in fetches([outs.at[s] for s in range(4)], results, sems):
        copy.wait()


def score(me, q, laid, own, other):
    rows = 2 * ROWS * FULL
    return pl.pallas_call(
        score_kernel,
        out_shape=(pltpu.HBM((2, SUB, LOGITS), f32),) * 4,
        in_specs=[SMEM] + [ANY] * 5,
        out_specs=(HBM,) * 4,
        scratch_shapes=[pltpu.VMEM(a.shape, bf16) for a in (own, other, q, *laid)]
        + [pltpu.VMEM((4, 2, SUB, LOGITS), f32)]
        + [pltpu.VMEM((rows, QUERIES), bf16)] * 2
        + [pltpu.VMEM(s, bf16) for s in KEY_SHAPES]
        + [pltpu.SemaphoreType.DMA((5,))],
        compiler_params=WIDE,
    )(me, own, other, q, *laid)


def total_kernel(p0, p1, p2, p3, own, shared, give, give_shared):
    t = p0[...] + p1[...] + (p2[...] + p3[...])
    own[...] = t[0]
    shared[...] = t[0, :, KEYS:]
    give[...] = t[1]
    give_shared[...] = t[1, :, KEYS:]


def total(parts):
    return pl.pallas_call(
        total_kernel,
        out_shape=tuple(jax.ShapeDtypeStruct((SUB, n), f32) for n in (LOGITS, KEYS // 2) * 2),
        in_specs=[VMEM] * 4,
        out_specs=(VMEM,) * 4,
        compiler_params=PARAMS,
    )(*parts)


def softmax_kernel(factor, own, got, near, far, out):
    whole = (own[...] + got[...]) * factor
    shared = jnp.concatenate([whole[:, KEYS:], (near[...] + far[...]) * factor], axis=1)
    for i, logits in enumerate((whole[:, :KEYS], shared)):
        powered = jnp.exp(logits - jnp.max(logits, axis=-1, keepdims=True))
        probs = (powered / jnp.sum(powered, axis=-1, keepdims=True)).astype(bf16)
        for p in range(PEERS):
            out[p, i] = probs


def softmax(factor, *parts):
    return pl.pallas_call(
        functools.partial(softmax_kernel, factor),
        out_shape=jax.ShapeDtypeStruct((PEERS, 2, SUB, KEYS), bf16),
        in_specs=[VMEM] * 4,
        out_specs=VMEM,
        compiler_params=PARAMS,
    )(*parts)


def values_kernel(me_ref, *refs):
    (vf, vh), (v00, v01, v10, v11), sems = refs[4:6], refs[6:10], refs[10]
    for copy in fetches(refs[:4], refs[6:10], sems):
        copy.wait()
    odd = lax.rem(me_ref[2], 2)
    for cr, refs in enumerate(((v00, v01), (v10, v11))):
        halves = [
            ref[i, FULL:CHUNK, pl.ds(pl.multiple_of(h * TOKENS, TOKENS), TOKENS)]
            for h in (odd, 1 - odd)
            for ref in refs
            for i in range(Z)
        ]
        whole = [ref[i, 0:FULL, h * TOKENS : (h + 1) * TOKENS] for ref in refs for i in range(Z) for h in range(2)]
        for r in range(ROWS):
            n = cr * ROWS + r
            lanes = slice(r * SUB, (r + 1) * SUB)
            vf[n * FULL : (n + 1) * FULL, :] = jnp.concatenate([b[:, lanes] for b in whole], axis=1)
            vh[n * HALF : (n + 1) * HALF, :] = jnp.concatenate([b[:, lanes] for b in halves], axis=1)


def values_laid(me, vs):
    return pl.pallas_call(
        values_kernel,
        out_shape=tuple(jax.ShapeDtypeStruct((2 * ROWS * n, KEYS), bf16) for n in (FULL, HALF)),
        in_specs=[SMEM] + [ANY] * 4,
        out_specs=(VMEM,) * 2,
        scratch_shapes=[pltpu.VMEM(v.shape, bf16) for v in vs] + [pltpu.SemaphoreType.DMA((4,))],
        compiler_params=WIDE,
        cost_estimate=LAYOUT,
    )(me, *vs)


def mix_kernel(me_ref, p_hbm, vf_hbm, vh_hbm, o_ref, p_ref, vf, vh, sems):
    core = me_ref[1]
    copies = fetches((p_hbm, vf_hbm, vh_hbm), (p_ref, vf, vh), sems)
    copies[0].wait()
    for i, (v, first, n) in enumerate(((vf, 0, FULL), (vh, FULL, HALF))):
        copies[1 + i].wait()
        probs = p_ref[:, i].reshape(QUERIES, KEYS)
        for cr in range(2):
            c = jnp.bitwise_xor(core, cr)
            mixed = dot(v[cr * ROWS * n : (cr + 1) * ROWS * n, :], probs, 1, 1).astype(bf16)
            for s in range(PEERS):
                o_ref[2 * s + c, first : first + n, :] = jnp.concatenate(
                    [mixed[r * n : (r + 1) * n, s * SUB : (s + 1) * SUB] for r in range(ROWS)], axis=1
                )


def mix(me, laid, probs):
    return pl.pallas_call(
        mix_kernel,
        out_shape=jax.ShapeDtypeStruct((2 * Z, CHUNK, ROWS * SUB), bf16),
        in_specs=[SMEM] + [ANY] * 3,
        out_specs=VMEM,
        scratch_shapes=[pltpu.VMEM(a.shape, bf16) for a in (probs, *laid)] + [pltpu.SemaphoreType.DMA((3,))],
        compiler_params=WIDE,
    )(me, probs, *laid)


def final_kernel(m_ref, w_ref, o_ref, t_ref):
    for c in range(2):
        for z in range(Z):
            (a, na), (b, nb) = chunk_pieces(z)
            t_ref[a : a + na, :] = m_ref[2 * z + c, 0:FULL, :]
            t_ref[b : b + nb, :] = m_ref[2 * z + c, FULL:CHUNK, :]
        attended = dot(t_ref[...], w_ref[...], 0, 0).astype(bf16)
        o_ref[:, c * SUB : (c + 1) * SUB, :] = attended.reshape(ROWS, SUB, EMBED)


def final(m, w):
    return pl.pallas_call(
        final_kernel,
        out_shape=jax.ShapeDtypeStruct((ROWS, RES, EMBED), bf16),
        in_specs=[VMEM] * 2,
        out_specs=VMEM,
        scratch_shapes=[pltpu.VMEM((EMBED, ROWS * SUB), bf16)],
        compiler_params=PARAMS,
    )(m, w)


def flip(x, axes, n, s):
    return lax.ppermute(x, axes, [(i, i ^ s) for i in range(n)])


def gather4(own):
    far = flip(own, "xl", 2, 1)
    return own, far, flip(own, "c", 2, 1), flip(far, "c", 2, 1)


def local(x, wq, wk, wv, wf):
    me = jnp.stack([lax.axis_index(("y", "xh")), lax.axis_index("c"), lax.axis_index("z")])
    me = me.astype(jnp.int32)
    n, k = key_chunks(x, wk)
    q = query_chunks(n, wq)
    v = value_chunks(n, wv)
    k = lax.all_to_all(k, "z", 0, 0, tiled=True)
    q, k = lax.optimization_barrier((q, k))
    q = lax.all_to_all(q, ("z", "c"), 0, 0, tiled=True)
    k00, k01, k10, k11 = gather4(k)
    parts = score(me, q, keys_laid(k00, k10), k01, k11)
    v, kept = lax.optimization_barrier((v, parts[0]))
    parts = [kept] + [flip(parts[s], "y", 4, s) for s in range(1, 4)]
    v = lax.all_to_all(v, "z", 0, 0, tiled=True)
    own, shared, give, give_shared = total(parts)
    v, own = lax.optimization_barrier((v, own))
    vs = gather4(v)
    rows = ROWS * 2 * PEERS
    probs = softmax(
        1.0 / math.sqrt(DH * rows),
        own,
        flip(give, "xh", 2, 1),
        flip(shared, "z", Z, 1),
        flip(give_shared, ("xh", "z"), 2 * Z, Z + 1),
    )
    probs = lax.all_to_all(probs, ("y", "xh"), 0, 0, tiled=True)
    mixed = lax.all_to_all(mix(me, values_laid(me, vs), probs), ("z", "c"), 0, 0, tiled=True)
    return final(mixed, wf)


def solution(mesh):
    fine = Mesh(mesh.devices.reshape(4, 2, 2, 8, 2), ("y", "xh", "c", "z", "xl"))
    spec = P(("y", "xh", "c"), ("z", "xl"), None)
    return jax.shard_map(
        local,
        mesh=fine,
        in_specs=(spec, P(), P(), P(), P()),
        out_specs=spec,
        check_vma=False,
    )
```

time: 190 us -> 188 us (0.989)
  waiting for transfers between devices: 56.7 us -> 85 us
  starting transfers between devices: 63.1 us -> 38.4 us
  blocking collectives: 38.3 us -> 29.3 us
    ppermute x7 -> x12, waiting for transfers between devices: 5.12 us -> 58 us  [flip(): return lax.ppermute(x, axes, [(i, i ^ s) for i in range(n)])]
    ppermute x15 -> x0, waiting for transfers between devices: 33.3 us -> none  [send(): self.got.append(lax.ppermute(x, axis, permutation))]
    ppermute x15 -> x0, starting transfers between devices: 28.4 us -> none  [send(): self.got.append(lax.ppermute(x, axis, permutation))]
    all_to_all x1, waiting for transfers between devices: 1.78 us -> 20.5 us  [local(): k = lax.all_to_all(k, 'z', 0, 0, tiled=True)]
    all_to_all x1 -> x2, waiting for transfers between devices: 15.5 us -> 1.59 us  [the longest x1 1.43 us: local(): q = lax.all_to_all(q, ('z', 'c'), 0, 0, tiled=True)]
    all_to_all x1, blocking collectives: 38.3 us -> 29.3 us  [local(): lax.all_to_all(mix(me, values_laid(me, vs), probs), ('z', 'c'), 0, 0, til...]
    all_to_all x1, waiting for transfers between devices: 0.95 us -> 4.91 us  [local(): probs = lax.all_to_all(probs, ('y', 'xh'), 0, 0, tiled=True)]
    all_to_all x1 -> x2, starting transfers between devices: 6.49 us -> 9.29 us  [the longest x1 5.36 us: local(): v = lax.all_to_all(v, 'z', 0, 0, tiled=True)]
  transfers between devices with their start and end apart: 25 -> 16, of which waited for: 14 -> 13; matrix products, arithmetic and copies ran while one was open for 0% -> 0% of each run, Pallas kernels for 7% -> 5%
where the time goes in v5:
time: 188 us; the launch traced here: 187 us
  waiting for transfers between devices  85 us (45%)
  starting transfers between devices  38.4 us (20%)
  blocking collectives  29.3 us (16%)
  Pallas kernels  22.4 us (12%)
  local copies, waits for them, and re-layouts  11.9 us (6%)
    ppermute x12, waiting for transfers between devices, flip(): return lax.ppermute(x, axes, [(i, i ^ s) for i in range(n)])  58 us
    all_to_all x1, blocking collectives, local(): lax.all_to_all(mix(me, values_laid(me, vs), probs), ('z', 'c'), 0, 0, til...  29.3 us
    all_to_all x1, waiting for transfers between devices, local(): k = lax.all_to_all(k, 'z', 0, 0, tiled=True)  20.5 us
    ppermute x12, starting transfers between devices, flip(): return lax.ppermute(x, axes, [(i, i ^ s) for i in range(n)])  14 us
    unnamed x30, local copies, waits for them, and re-layouts  11.9 us
    all_to_all x1, starting transfers between devices, local(): k = lax.all_to_all(k, 'z', 0, 0, tiled=True)  9.03 us
    pallas_call x1, Pallas kernels, score(): pl.pallas_call(score_kernel, out_shape=(pltpu.HBM((2, SUB, LOGITS), f32),...  6.1 us
    all_to_all x1, starting transfers between devices, local(): probs = lax.all_to_all(probs, ('y', 'xh'), 0, 0, tiled=True)  6.08 us
  transfers between devices with their start and end apart: 16, of which 13 were waited for; matrix products, arithmetic and copies ran while one was open for 0% of the time, Pallas kernels for 5%

profile of v5, /device:TPU:1, one launch (start us, length us, event | category | flops | bytes accessed | tf_op | source)
XLA Modules:
  0.0 187.2 jit_solution(16878796301744828051)
XLA Ops:
  0.0 1.3 copy-done.2
  2.4 2.4 %shard_map.55 = (bf16[2,8,32,768]{3,2,1,0:T(8,128)(2,1)S(1)}, bf16[8,96,512]{2,1,0:T(8,128)(2,1)}) custom-call(bf16[8,64,768]{2,1,0:T(8,128)(2,1)S(1)} %copy-done.8, bf16[768,768]{1,0:T(8,128)(2,1)S(1)} %copy-done.2), custom_call_target="tpu_custom_call" | custom-call | tf_op jit(solution)/shard_map/pallas_call | solution.py:84
  4.8 9.0 %all-to-all-start = ((bf16[8,96,512]{2,1,0:T(8,128)(2,1)}), bf16[8,96,512]{2,1,0:T(8,128)(2,1)S(1)}, u32[]{:S(2)}, u32[]{:S(2)}) async-start(bf16[8,96,512]{2,1,0:T(8,128)(2,1)} %get-tuple-element.26), calls=%async_computation | async-start | bytes 1572864 | tf_op jit(solution)/shard_map/all_to_all | solution.py:348
  13.9 1.3 copy-done.3
  15.1 1.8 shard_map.57
  16.9 20.5 %all-to-all-done.own = bf16[8,96,512]{2,1,0:T(8,128)(2,1)S(1)} async-done(((bf16[8,96,512]{2,1,0:T(8,128)(2,1)}), bf16[8,96,512]{2,1,0:T(8,128)(2,1)S(1)}, u32[]{:S(2)}, u32[]{:S(2)}) %all-to-all-start) | async-done | bytes 786464 | tf_op jit(solution)/shard_map/all_to_all | solution.py:348
  37.4 3.9 %all-to-all-start.1 = ((bf16[16,128,256]{2,1,0:T(8,128)(2,1)}), bf16[16,128,256]{2,1,0:T(8,128)(2,1)S(1)}, u32[]{:S(2)}, u32[]{:S(2)}) async-start(bf16[16,128,256]{2,1,0:T(8,128)(2,1)} %shard_map.57), calls=%async_computation.1 | async-start | bytes 2097152 | tf_op jit(solution)/shard_map/all_to_all | solution.py:350
  43.2 17.1 %collective-permute-done.refs_0_ = bf16[8,96,512]{2,1,0:T(8,128)(2,1)} collective-permute-done((bf16[8,96,512]{2,1,0:T(8,128)(2,1)S(1)}, bf16[8,96,512]{2,1,0:T(8,128)(2,1)}, u32[]{:S(2)}, u32[]{:S(2)}) %collective-permute-start) | collective-permute-done | bytes 786464 | tf_op jit(solution)/shard_map/ppermute | solution.py:334
  61.4 1.3 copy-done.4
  62.7 1.7 shard_map.56
  66.5 1.4 shard_map.58
  67.9 1.4 all-to-all-done.1.refs_2_
  69.3 6.1 %shard_map.59 = (f32[2,32,1536]{2,1,0:T(8,128)}, f32[2,32,1536]{2,1,0:T(8,128)}, f32[2,32,1536]{2,1,0:T(8,128)}, f32[2,32,1536]{2,1,0:T(8,128)}) custom-call(s32[3]{0:T(128)S(1)} %pad_add_fusion.me_ref, bf16[8,96,512]{2,1,0:T(8,128)(2,1)} %collective-permute-done.refs_0_, bf16[8,96,512]{2,1,0:T(8,128)(2,1)} %collective-permute-done.1.refs_1_, ...), custom_call_target="tpu_custom_call" | custom-call | tf_op jit(solution)/shard_map/pallas_call | solution.py:201
  75.5 5.4 %all-to-all-start.2 = ((bf16[8,96,512]{2,1,0:T(8,128)(2,1)}), bf16[8,96,512]{2,1,0:T(8,128)(2,1)S(1)}, u32[]{:S(2)}, u32[]{:S(2)}) async-start(bf16[8,96,512]{2,1,0:T(8,128)(2,1)} %shard_map.56), calls=%async_computation.2 | async-start | bytes 1572864 | tf_op jit(solution)/shard_map/all_to_all | solution.py:355
  80.9 1.4 collective-permute-start.3
  82.2 2.6 %collective-permute-start.4 = (f32[2,32,1536]{2,1,0:T(8,128)S(1)}, f32[2,32,1536]{2,1,0:T(8,128)S(1)}, u32[]{:S(2)}, u32[]{:S(2)}) collective-permute-start(f32[2,32,1536]{2,1,0:T(8,128)S(1)} %copy-done.13), channel_id=1, source_target_pairs={{0,128},{64,192},{128,0},{192,64},{1,129},{65,193},{129,1},{193,65... | collective-permute-start | bytes 1179656 | tf_op jit(solution)/shard_map/ppermute | solution.py:334
  84.9 6.5 %collective-permute-done.3.p1 = f32[2,32,1536]{2,1,0:T(8,128)S(1)} collective-permute-done((f32[2,32,1536]{2,1,0:T(8,128)S(1)}, f32[2,32,1536]{2,1,0:T(8,128)S(1)}, u32[]{:S(2)}, u32[]{:S(2)}) %collective-permute-start.3) | collective-permute-done | bytes 393248 | tf_op jit(solution)/shard_map/ppermute | solution.py:334
  91.4 10.9 %collective-permute-done.4.p2 = f32[2,32,1536]{2,1,0:T(8,128)S(1)} collective-permute-done((f32[2,32,1536]{2,1,0:T(8,128)S(1)}, f32[2,32,1536]{2,1,0:T(8,128)S(1)}, u32[]{:S(2)}, u32[]{:S(2)}) %collective-permute-start.4) | collective-permute-done | bytes 393248 | tf_op jit(solution)/shard_map/ppermute | solution.py:334
  102.3 2.0 %collective-permute-done.5.p3 = f32[2,32,1536]{2,1,0:T(8,128)S(1)} collective-permute-done((f32[2,32,1536]{2,1,0:T(8,128)S(1)}, f32[2,32,1536]{2,1,0:T(8,128)S(1)}, u32[]{:S(2)}, u32[]{:S(2)}) %collective-permute-start.5) | collective-permute-done | bytes 393248 | tf_op jit(solution)/shard_map/ppermute | solution.py:334
  105.7 2.4 %collective-permute-start.6 = (f32[32,1536]{1,0:T(8,128)S(1)}, f32[32,1536]{1,0:T(8,128)S(1)}, u32[]{:S(2)}, u32[]{:S(2)}) collective-permute-start(f32[32,1536]{1,0:T(8,128)S(1)} %get-tuple-element.39), channel_id=1, source_target_pairs={{0,32},{32,0},{1,33},{33,1},{2,34},{34,2},{3,35},{35,3},{4,36},{36... | collective-permute-start | bytes 589832 | tf_op jit(solution)/shard_map/ppermute | solution.py:334
  109.9 1.7 collective-permute-done.7.near
  111.6 3.4 %collective-permute-done.8.far = f32[32,512]{1,0:T(8,128)S(1)} collective-permute-done((f32[32,512]{1,0:T(8,128)S(1)}, f32[32,512]{1,0:T(8,128)S(1)}, u32[]{:S(2)}, u32[]{:S(2)}) %collective-permute-start.8) | collective-permute-done | bytes 65568 | tf_op jit(solution)/shard_map/ppermute | solution.py:334
  115.0 14.3 %collective-permute-done.6.got = f32[32,1536]{1,0:T(8,128)S(1)} collective-permute-done((f32[32,1536]{1,0:T(8,128)S(1)}, f32[32,1536]{1,0:T(8,128)S(1)}, u32[]{:S(2)}, u32[]{:S(2)}) %collective-permute-start.6) | collective-permute-done | bytes 196640 | tf_op jit(solution)/shard_map/ppermute | solution.py:334
  130.5 6.1 %all-to-all-start.3 = ((bf16[8,2,32,1024]{3,2,1,0:T(8,128)(2,1)}), bf16[8,2,32,1024]{3,2,1,0:T(8,128)(2,1)S(1)}, u32[]{:S(2)}, u32[]{:S(2)}) async-start(bf16[8,2,32,1024]{3,2,1,0:T(8,128)(2,1)} %shard_map.61), calls=%async_computation.3 | async-start | bytes 2097152 | tf_op jit(solution)/shard_map/all_to_all | solution.py:367
  136.6 1.6 collective-permute-start.10
  142.4 3.3 %shard_map.62 = (bf16[1024,1024]{1,0:T(8,128)(2,1)S(1)}, bf16[512,1024]{1,0:T(8,128)(2,1)S(1)}) custom-call(s32[3]{0:T(128)S(1)} %pad_add_fusion.me_ref, bf16[8,96,512]{2,1,0:T(8,128)(2,1)S(1)} %all-to-all-done.2.refs_0_, bf16[8,96,512]{2,1,0:T(8,128)(2,1)S(1)} %copy-done.10, bf16[8,96,512]{2,1,0:T(8,128)(2,1)S(1)} %collective-permute-done.10.refs_2_, ...), custom_call_target="tpu_custom_call" | custom-call | bytes 6291456 | tf_op jit(solution)/shard_map/pallas_call | solution.py:274
  145.7 1.4 copy-done
  147.1 4.9 %all-to-all-done.3.p_hbm = bf16[8,2,32,1024]{3,2,1,0:T(8,128)(2,1)S(1)} async-done(((bf16[8,2,32,1024]{3,2,1,0:T(8,128)(2,1)}), bf16[8,2,32,1024]{3,2,1,0:T(8,128)(2,1)S(1)}, u32[]{:S(2)}, u32[]{:S(2)}) %all-to-all-start.3) | async-done | bytes 1048608 | tf_op jit(solution)/shard_map/all_to_all | solution.py:367
  152.0 1.6 copy-done.1
  153.6 2.7 %shard_map.63 = bf16[16,96,256]{2,1,0:T(8,128)(2,1)S(1)} custom-call(s32[3]{0:T(128)S(1)} %pad_add_fusion.me_ref, bf16[8,2,32,1024]{3,2,1,0:T(8,128)(2,1)S(1)} %all-to-all-done.3.p_hbm, bf16[1024,1024]{1,0:T(8,128)(2,1)S(1)} %copy-done.1, bf16[512,1024]{1,0:T(8,128)(2,1)S(1)} %get-tuple-element.44.vh_hbm), custom_call_target="tpu_custom_call" | custom-call | tf_op jit(solution)/shard_map/pallas_call | solution.py:302
  156.2 29.3 %all_to_all.25.m_ref = bf16[16,96,256]{2,1,0:T(8,128)(2,1)S(1)} all-to-all(bf16[16,96,256]{2,1,0:T(8,128)(2,1)S(1)} %shard_map.63), channel_id=1, replica_groups=mesh['y'=4,'xh'=2,'c'=2,'z'=8,'xl'=2] {'z','c'}, dimensions={0} | all-to-all | bytes 1572864 | tf_op jit(solution)/shard_map/all_to_all | solution.py:368
  185.5 1.7 shard_map.64
  (42 shorter events, 14.8 us)
Async XLA Ops:
  0.0 1.3 copy-start.2
  1.3 1.1 copy-start.8
  4.8 32.6 %all-to-all-start = ((bf16[8,96,512]{2,1,0:T(8,128)(2,1)}), bf16[8,96,512]{2,1,0:T(8,128)(2,1)S(1)}, u32[]{:S(2)}, u32[]{:S(2)}) async-start(bf16[8,96,512]{2,1,0:T(8,128)(2,1)} %get-tuple-element.26), calls=%async_computation | async-start | bytes 1572864 | tf_op jit(solution)/shard_map/all_to_all | solution.py:348
  13.9 1.3 copy-start.3
  37.4 31.9 %all-to-all-start.1 = ((bf16[16,128,256]{2,1,0:T(8,128)(2,1)}), bf16[16,128,256]{2,1,0:T(8,128)(2,1)S(1)}, u32[]{:S(2)}, u32[]{:S(2)}) async-start(bf16[16,128,256]{2,1,0:T(8,128)(2,1)} %shard_map.57), calls=%async_computation.1 | async-start | bytes 2097152 | tf_op jit(solution)/shard_map/all_to_all | solution.py:350
  41.4 18.9 %collective-permute-start = (bf16[8,96,512]{2,1,0:T(8,128)(2,1)S(1)}, bf16[8,96,512]{2,1,0:T(8,128)(2,1)}, u32[]{:S(2)}, u32[]{:S(2)}) collective-permute-start(bf16[8,96,512]{2,1,0:T(8,128)(2,1)S(1)} %all-to-all-done.own), channel_id=1, source_target_pairs={{0,1},{1,0},{2,3},{3,2},{4,5},{5,4},{6,7},{7,6},{8,9},{9,8},{10,11... | collective-permute-start | bytes 2359304 | tf_op jit(solution)/shard_map/ppermute | solution.py:334
  42.6 21.9 %collective-permute-start.2 = (bf16[8,96,512]{2,1,0:T(8,128)(2,1)S(1)}, bf16[8,96,512]{2,1,0:T(8,128)(2,1)S(1)}, u32[]{:S(2)}, u32[]{:S(2)}) collective-permute-start(bf16[8,96,512]{2,1,0:T(8,128)(2,1)S(1)} %all-to-all-done.own), channel_id=1, source_target_pairs={{0,16},{16,0},{1,17},{17,1},{2,18},{18,2},{3,19},{19,3},{4,20},{20... | collective-permute-start | bytes 2359304 | tf_op jit(solution)/shard_map/ppermute | solution.py:334
  60.3 7.6 %collective-permute-start.1 = (bf16[8,96,512]{2,1,0:T(8,128)(2,1)}, bf16[8,96,512]{2,1,0:T(8,128)(2,1)}, u32[]{:S(2)}, u32[]{:S(2)}) collective-permute-start(bf16[8,96,512]{2,1,0:T(8,128)(2,1)} %collective-permute-done.refs_0_), channel_id=1, source_target_pairs={{0,16},{16,0},{1,17},{17,1},{2,18},{18,2},{3,19},{19,3},{4,20},{20... | collective-permute-start | bytes 2359304 | tf_op jit(solution)/shard_map/ppermute | solution.py:334
  61.4 1.3 copy-start.4
  64.5 0.9 copy-start.6
  65.4 1.1 copy-start.7
  75.5 5.4 %copy-start.14 = (f32[2,32,1536]{2,1,0:T(8,128)S(1)}, f32[2,32,1536]{2,1,0:T(8,128)}, u32[]{:S(2)}) copy-start(f32[2,32,1536]{2,1,0:T(8,128)} %get-tuple-element.34) | copy-start | bytes 1179652
  75.5 6.8 %copy-start.13 = (f32[2,32,1536]{2,1,0:T(8,128)S(1)}, f32[2,32,1536]{2,1,0:T(8,128)}, u32[]{:S(2)}) copy-start(f32[2,32,1536]{2,1,0:T(8,128)} %get-tuple-element.35) | copy-start | bytes 1179652
  75.5 9.4 %copy-start.12 = (f32[2,32,1536]{2,1,0:T(8,128)S(1)}, f32[2,32,1536]{2,1,0:T(8,128)}, u32[]{:S(2)}) copy-start(f32[2,32,1536]{2,1,0:T(8,128)} %get-tuple-element.36) | copy-start | bytes 1179652
  75.5 28.8 %copy-start.11 = (f32[2,32,1536]{2,1,0:T(8,128)S(1)}, f32[2,32,1536]{2,1,0:T(8,128)}, u32[]{:S(2)}) copy-start(f32[2,32,1536]{2,1,0:T(8,128)} %get-tuple-element.33.p0) | copy-start | bytes 1179652
  75.5 29.0 %all-to-all-start.2 = ((bf16[8,96,512]{2,1,0:T(8,128)(2,1)}), bf16[8,96,512]{2,1,0:T(8,128)(2,1)S(1)}, u32[]{:S(2)}, u32[]{:S(2)}) async-start(bf16[8,96,512]{2,1,0:T(8,128)(2,1)} %shard_map.56), calls=%async_computation.2 | async-start | bytes 1572864 | tf_op jit(solution)/shard_map/all_to_all | solution.py:355
  80.9 10.5 %collective-permute-start.3 = (f32[2,32,1536]{2,1,0:T(8,128)S(1)}, f32[2,32,1536]{2,1,0:T(8,128)S(1)}, u32[]{:S(2)}, u32[]{:S(2)}) collective-permute-start(f32[2,32,1536]{2,1,0:T(8,128)S(1)} %copy-done.14), channel_id=1, source_target_pairs={{0,64},{64,0},{128,192},{192,128},{1,65},{65,1},{129,193},{193,129... | collective-permute-start | bytes 1179656 | tf_op jit(solution)/shard_map/ppermute | solution.py:334
  82.2 20.0 %collective-permute-start.4 = (f32[2,32,1536]{2,1,0:T(8,128)S(1)}, f32[2,32,1536]{2,1,0:T(8,128)S(1)}, u32[]{:S(2)}, u32[]{:S(2)}) collective-permute-start(f32[2,32,1536]{2,1,0:T(8,128)S(1)} %copy-done.13), channel_id=1, source_target_pairs={{0,128},{64,192},{128,0},{192,64},{1,129},{65,193},{129,1},{193,65... | collective-permute-start | bytes 1179656 | tf_op jit(solution)/shard_map/ppermute | solution.py:334
  84.8 19.4 %collective-permute-start.5 = (f32[2,32,1536]{2,1,0:T(8,128)S(1)}, f32[2,32,1536]{2,1,0:T(8,128)S(1)}, u32[]{:S(2)}, u32[]{:S(2)}) collective-permute-start(f32[2,32,1536]{2,1,0:T(8,128)S(1)} %copy-done.12), channel_id=1, source_target_pairs={{0,192},{64,128},{128,64},{192,0},{1,193},{65,129},{129,65},{193,1... | collective-permute-start | bytes 1179656 | tf_op jit(solution)/shard_map/ppermute | solution.py:334
  104.5 33.7 %collective-permute-start.9 = (bf16[8,96,512]{2,1,0:T(8,128)(2,1)S(1)}, bf16[8,96,512]{2,1,0:T(8,128)(2,1)S(1)}, u32[]{:S(2)}, u32[]{:S(2)}) collective-permute-start(bf16[8,96,512]{2,1,0:T(8,128)(2,1)S(1)} %all-to-all-done.2.refs_0_), channel_id=1, source_target_pairs={{0,1},{1,0},{2,3},{3,2},{4,5},{5,4},{6,7},{7,6},{8,9},{9,8},{10,11... | collective-permute-start | bytes 2359304 | tf_op jit(solution)/shard_map/ppermute | solution.py:334
  105.7 23.6 %collective-permute-start.6 = (f32[32,1536]{1,0:T(8,128)S(1)}, f32[32,1536]{1,0:T(8,128)S(1)}, u32[]{:S(2)}, u32[]{:S(2)}) collective-permute-start(f32[32,1536]{1,0:T(8,128)S(1)} %get-tuple-element.39), channel_id=1, source_target_pairs={{0,32},{32,0},{1,33},{33,1},{2,34},{34,2},{3,35},{35,3},{4,36},{36... | collective-permute-start | bytes 589832 | tf_op jit(solution)/shard_map/ppermute | solution.py:334
  108.1 3.4 %collective-permute-start.7 = (f32[32,512]{1,0:T(8,128)S(1)}, f32[32,512]{1,0:T(8,128)S(1)}, u32[]{:S(2)}, u32[]{:S(2)}) collective-permute-start(f32[32,512]{1,0:T(8,128)S(1)} %get-tuple-element.40), channel_id=1, source_target_pairs={{0,2},{2,0},{4,6},{6,4},{8,10},{10,8},{12,14},{14,12},{1,3},{3,1},... | collective-permute-start | bytes 196616 | tf_op jit(solution)/shard_map/ppermute | solution.py:334
  109.2 5.8 %collective-permute-start.8 = (f32[32,512]{1,0:T(8,128)S(1)}, f32[32,512]{1,0:T(8,128)S(1)}, u32[]{:S(2)}, u32[]{:S(2)}) collective-permute-start(f32[32,512]{1,0:T(8,128)S(1)} %get-tuple-element.41), channel_id=1, source_target_pairs={{0,34},{2,32},{4,38},{6,36},{8,42},{10,40},{12,46},{14,44},{32,2},... | collective-permute-start | bytes 196616 | tf_op jit(solution)/shard_map/ppermute | solution.py:334
  130.5 21.4 %all-to-all-start.3 = ((bf16[8,2,32,1024]{3,2,1,0:T(8,128)(2,1)}), bf16[8,2,32,1024]{3,2,1,0:T(8,128)(2,1)S(1)}, u32[]{:S(2)}, u32[]{:S(2)}) async-start(bf16[8,2,32,1024]{3,2,1,0:T(8,128)(2,1)} %shard_map.61), calls=%async_computation.3 | async-start | bytes 2097152 | tf_op jit(solution)/shard_map/all_to_all | solution.py:367
  136.6 3.5 %collective-permute-start.10 = (bf16[8,96,512]{2,1,0:T(8,128)(2,1)S(1)}, bf16[8,96,512]{2,1,0:T(8,128)(2,1)S(1)}, u32[]{:S(2)}, u32[]{:S(2)}) collective-permute-start(bf16[8,96,512]{2,1,0:T(8,128)(2,1)S(1)} %all-to-all-done.2.refs_0_), channel_id=1, source_target_pairs={{0,16},{16,0},{1,17},{17,1},{2,18},{18,2},{3,19},{19,3},{4,20},{20... | collective-permute-start | bytes 2359304 | tf_op jit(solution)/shard_map/ppermute | solution.py:334
  138.2 3.0 %collective-permute-start.11 = (bf16[8,96,512]{2,1,0:T(8,128)(2,1)S(1)}, bf16[8,96,512]{2,1,0:T(8,128)(2,1)S(1)}, u32[]{:S(2)}, u32[]{:S(2)}) collective-permute-start(bf16[8,96,512]{2,1,0:T(8,128)(2,1)S(1)} %collective-permute-done.9.refs_1_), channel_id=1, source_target_pairs={{0,16},{16,0},{1,17},{17,1},{2,18},{18,2},{3,19},{19,3},{4,20},{20... | collective-permute-start | bytes 2359304 | tf_op jit(solution)/shard_map/ppermute | solution.py:334
  138.3 0.9 copy-start.9
  141.2 1.1 copy-start.10
  145.7 1.4 copy-start
  152.0 1.6 copy-start.1
  156.2 29.3 %copy-start.5 = (bf16[768,768]{1,0:T(8,128)(2,1)S(1)}, bf16[768,768]{1,0:T(8,128)(2,1)}, u32[]{:S(2)}) copy-start(bf16[768,768]{1,0:T(8,128)(2,1)} %w_ref.5) | copy-start | bytes 3538948

commit v6 on v5

--- a/solution.py
+++ b/solution.py
@@ -54,6 +54,12 @@
     return z // 2 * (2 * CHUNK) + FULL
 
 
+def chunk_rows(z):
+    odd = lax.rem(z, 2)
+    base = z * CHUNK
+    return pl.multiple_of(base + odd * HALF, HALF), pl.multiple_of(base + (1 - odd) * FULL, HALF)
+
+
 def fetches(sources, buffers, sems):
     copies = [pltpu.make_async_copy(a, b, sems.at[i]) for i, (a, b) in enumerate(zip(sources, buffers))]
     for copy in copies:
@@ -61,7 +67,12 @@
     return copies
 
 
-def key_kernel(x_hbm, w_hbm, n_ref, k_ref, x_ref, w_ref, sems):
+def in_hbm(*arrays):
+    return [pltpu.with_memory_space_constraint(a, pltpu.HBM) for a in arrays]
+
+
+def key_kernel(me_ref, x_hbm, w_hbm, n_ref, *rest):
+    outs, (x_ref, w_ref, t_ref, sems) = rest[:Z], rest[Z:]
     copy_x, copy_w = fetches((x_hbm, w_hbm), (x_ref, w_ref), sems)
     copy_x.wait()
     x = x_ref[...].astype(f32)
@@ -71,31 +82,33 @@
     for h in range(2):
         n_ref[h] = normed[:, h * SUB : (h + 1) * SUB, :]
     copy_w.wait()
-    t = dot(w_ref[...], n_ref[...].reshape(ROWS * RES, EMBED), 0, 1).astype(bf16)
-    for z in range(Z):
-        (a, _), _ = chunk_pieces(z)
-        b, lanes = shared_head(z), slice(z % 2 * TOKENS, (z % 2 + 1) * TOKENS)
-        k_ref[z, 0:FULL, :] = t[a : a + FULL]
-        k_ref[z, FULL:CHUNK, :TOKENS] = t[b : b + HALF, lanes]
-        k_ref[z, FULL:CHUNK, TOKENS:] = t[b + HALF : b + FULL, lanes]
-
-
-def key_chunks(x, w):
-    return pl.pallas_call(
+    t_ref[...] = dot(w_ref[...], n_ref[...].reshape(ROWS * RES, EMBED), 0, 1).astype(bf16)
+    for s, out in enumerate(outs):
+        z = lax.rem(me_ref[2] + s, Z)
+        first, odd = shared_head(z), lax.rem(z, 2)
+        lanes = pl.ds(pl.multiple_of(odd * TOKENS, TOKENS), TOKENS)
+        out[0:FULL, :] = t_ref[pl.ds(chunk_rows(z)[0], FULL), :]
+        for d in range(2):
+            rows = pl.ds(pl.multiple_of(first + d * HALF, HALF), HALF)
+            out[FULL:CHUNK, d * TOKENS : (d + 1) * TOKENS] = t_ref[rows, lanes]
+
+
+def key_chunks(me, x, w):
+    n, *k = pl.pallas_call(
         key_kernel,
-        out_shape=(
-            jax.ShapeDtypeStruct((2, ROWS, SUB, EMBED), bf16),
-            jax.ShapeDtypeStruct((Z, CHUNK, ROWS * RES), bf16),
-        ),
-        in_specs=[HBM, HBM],
-        out_specs=(VMEM,) * 2,
+        out_shape=(jax.ShapeDtypeStruct((2, ROWS, SUB, EMBED), bf16),)
+        + (jax.ShapeDtypeStruct((CHUNK, ROWS * RES), bf16),) * Z,
+        in_specs=[SMEM, ANY, ANY],
+        out_specs=(VMEM,) * (1 + Z),
         scratch_shapes=[
             pltpu.VMEM((ROWS, RES, EMBED), bf16),
             pltpu.VMEM((EMBED, EMBED), bf16),
+            pltpu.VMEM((EMBED, ROWS * RES), bf16),
             pltpu.SemaphoreType.DMA((2,)),
         ],
         compiler_params=PARAMS,
-    )(x, w)
+    )(me, *in_hbm(x, w))
+    return n, k
 
 
 def query_kernel(n_ref, w_ref, q_ref):
@@ -137,34 +150,35 @@
     )(n, w)
 
 
-def lay_keys(own, other, kf, kh):
+def lay_keys(me, own, other, kf, kh):
+    where = [lax.rem(me - z + Z, Z) for z in range(Z)]
     for cr, ref in enumerate((own, other)):
         for r in range(ROWS):
             n = (cr * ROWS + r) * FULL
-            whole = [ref[z, 0:FULL, h * TOKENS + r * SUB : h * TOKENS + (r + 1) * SUB] for z in range(Z) for h in range(2)]
+            whole = [ref[z, 0:FULL, h * TOKENS + r * SUB : h * TOKENS + (r + 1) * SUB] for z in where for h in range(2)]
             kf[n : n + FULL, :] = jnp.concatenate(whole, axis=1)
             for d in range(2):
                 first = d * TOKENS + r * SUB
-                shared = [ref[z, FULL:CHUNK, first : first + SUB] for z in range(Z)]
+                shared = [ref[z, FULL:CHUNK, first : first + SUB] for z in where]
                 kh[n + d * HALF : n + (d + 1) * HALF, :] = jnp.concatenate(shared, axis=1)
 
 
-def keys_kernel(own, other, kf, kh, a, b, sems):
+def keys_kernel(me_ref, own, other, kf, kh, a, b, sems):
     for copy in fetches((own, other), (a, b), sems):
         copy.wait()
-    lay_keys(a, b, kf, kh)
-
-
-def keys_laid(own, other):
+    lay_keys(me_ref[2], a, b, kf, kh)
+
+
+def keys_laid(me, own, other):
     return pl.pallas_call(
         keys_kernel,
         out_shape=tuple(jax.ShapeDtypeStruct(s, bf16) for s in KEY_SHAPES),
-        in_specs=[ANY, ANY],
+        in_specs=[SMEM, ANY, ANY],
         out_specs=(VMEM,) * 2,
         scratch_shapes=[pltpu.VMEM(own.shape, bf16)] * 2 + [pltpu.SemaphoreType.DMA((2,))],
         compiler_params=PARAMS,
         cost_estimate=LAYOUT,
-    )(own, other)
+    )(me, own, other)
 
 
 def score_kernel(me_ref, *refs):
@@ -174,7 +188,7 @@
     copies = fetches(sources, rest[:5], sems)
     for copy in copies[:2]:
         copy.wait()
-    lay_keys(own, other, kf1, kh1)
+    lay_keys(me_ref[2], own, other, kf1, kh1)
     for copy in copies[2:]:
         copy.wait()
     peers = [jnp.bitwise_xor(me_ref[0], 2 * s + t) for s in range(4) for t in range(2)]
@@ -250,84 +264,86 @@
     )(*parts)
 
 
-def values_kernel(me_ref, *refs):
-    (vf, vh), (v00, v01, v10, v11), sems = refs[4:6], refs[6:10], refs[10]
-    for copy in fetches(refs[:4], refs[6:10], sems):
+def values_kernel(me_ref, own_hbm, far_hbm, vf, vh, own, far, sems):
+    for copy in fetches((own_hbm, far_hbm), (own, far), sems):
         copy.wait()
     odd = lax.rem(me_ref[2], 2)
-    for cr, refs in enumerate(((v00, v01), (v10, v11))):
-        halves = [
-            ref[i, FULL:CHUNK, pl.ds(pl.multiple_of(h * TOKENS, TOKENS), TOKENS)]
-            for h in (odd, 1 - odd)
-            for ref in refs
-            for i in range(Z)
-        ]
-        whole = [ref[i, 0:FULL, h * TOKENS : (h + 1) * TOKENS] for ref in refs for i in range(Z) for h in range(2)]
-        for r in range(ROWS):
-            n = cr * ROWS + r
-            lanes = slice(r * SUB, (r + 1) * SUB)
-            vf[n * FULL : (n + 1) * FULL, :] = jnp.concatenate([b[:, lanes] for b in whole], axis=1)
-            vh[n * HALF : (n + 1) * HALF, :] = jnp.concatenate([b[:, lanes] for b in halves], axis=1)
-
-
-def values_laid(me, vs):
+    halves = [
+        ref[z, FULL:CHUNK, pl.ds(pl.multiple_of(h * TOKENS, TOKENS), TOKENS)]
+        for h in (odd, 1 - odd)
+        for ref in (own, far)
+        for z in range(Z)
+    ]
+    whole = [ref[z, 0:FULL, h * TOKENS : (h + 1) * TOKENS] for ref in (own, far) for z in range(Z) for h in range(2)]
+    for r in range(ROWS):
+        lanes = slice(r * SUB, (r + 1) * SUB)
+        vf[r * FULL : (r + 1) * FULL, :] = jnp.concatenate([b[:, lanes] for b in whole], axis=1)
+        vh[r * HALF : (r + 1) * HALF, :] = jnp.concatenate([b[:, lanes] for b in halves], axis=1)
+
+
+def values_laid(me, own, far):
     return pl.pallas_call(
         values_kernel,
-        out_shape=tuple(jax.ShapeDtypeStruct((2 * ROWS * n, KEYS), bf16) for n in (FULL, HALF)),
-        in_specs=[SMEM] + [ANY] * 4,
+        out_shape=tuple(jax.ShapeDtypeStruct((ROWS * n, KEYS), bf16) for n in (FULL, HALF)),
+        in_specs=[SMEM] + [ANY] * 2,
         out_specs=(VMEM,) * 2,
-        scratch_shapes=[pltpu.VMEM(v.shape, bf16) for v in vs] + [pltpu.SemaphoreType.DMA((4,))],
+        scratch_shapes=[pltpu.VMEM(own.shape, bf16)] * 2 + [pltpu.SemaphoreType.DMA((2,))],
         compiler_params=WIDE,
         cost_estimate=LAYOUT,
-    )(me, *vs)
-
-
-def mix_kernel(me_ref, p_hbm, vf_hbm, vh_hbm, o_ref, p_ref, vf, vh, sems):
-    core = me_ref[1]
-    copies = fetches((p_hbm, vf_hbm, vh_hbm), (p_ref, vf, vh), sems)
-    copies[0].wait()
+    )(me, own, far)
+
+
+def mix_kernel(me_ref, own_hbm, other_hbm, vf_hbm, vh_hbm, *rest):
+    outs, (p_ref, vf, vh, sems) = rest[:Z], rest[Z:]
+    core, z = me_ref[1], me_ref[2]
+    copies = fetches(
+        (own_hbm, other_hbm, vf_hbm, vh_hbm), (p_ref.at[core], p_ref.at[1 - core], vf, vh), sems
+    )
+    for copy in copies:
+        copy.wait()
     for i, (v, first, n) in enumerate(((vf, 0, FULL), (vh, FULL, HALF))):
-        copies[1 + i].wait()
-        probs = p_ref[:, i].reshape(QUERIES, KEYS)
-        for cr in range(2):
-            c = jnp.bitwise_xor(core, cr)
-            mixed = dot(v[cr * ROWS * n : (cr + 1) * ROWS * n, :], probs, 1, 1).astype(bf16)
-            for s in range(PEERS):
-                o_ref[2 * s + c, first : first + n, :] = jnp.concatenate(
+        for h in range(2):
+            probs = jnp.concatenate([p_ref[h, lax.rem(z + s, Z), i] for s in range(Z)], axis=0)
+            mixed = dot(v[...], probs, 1, 1).astype(bf16)
+            for s, out in enumerate(outs):
+                out[first : first + n, h * TOKENS : (h + 1) * TOKENS] = jnp.concatenate(
                     [mixed[r * n : (r + 1) * n, s * SUB : (s + 1) * SUB] for r in range(ROWS)], axis=1
                 )
 
 
-def mix(me, laid, probs):
+def mix(me, laid, own, other):
     return pl.pallas_call(
         mix_kernel,
-        out_shape=jax.ShapeDtypeStruct((2 * Z, CHUNK, ROWS * SUB), bf16),
-        in_specs=[SMEM] + [ANY] * 3,
-        out_specs=VMEM,
-        scratch_shapes=[pltpu.VMEM(a.shape, bf16) for a in (probs, *laid)] + [pltpu.SemaphoreType.DMA((3,))],
+        out_shape=(jax.ShapeDtypeStruct((CHUNK, ROWS * RES), bf16),) * Z,
+        in_specs=[SMEM] + [ANY] * 4,
+        out_specs=(VMEM,) * Z,
+        scratch_shapes=[pltpu.VMEM((2, *own.shape), bf16)]
+        + [pltpu.VMEM(a.shape, bf16) for a in laid]
+        + [pltpu.SemaphoreType.DMA((4,))],
         compiler_params=WIDE,
-    )(me, probs, *laid)
-
-
-def final_kernel(m_ref, w_ref, o_ref, t_ref):
-    for c in range(2):
-        for z in range(Z):
-            (a, na), (b, nb) = chunk_pieces(z)
-            t_ref[a : a + na, :] = m_ref[2 * z + c, 0:FULL, :]
-            t_ref[b : b + nb, :] = m_ref[2 * z + c, FULL:CHUNK, :]
-        attended = dot(t_ref[...], w_ref[...], 0, 0).astype(bf16)
-        o_ref[:, c * SUB : (c + 1) * SUB, :] = attended.reshape(ROWS, SUB, EMBED)
-
-
-def final(m, w):
+    )(me, own, other, *laid)
+
+
+def final_kernel(me_ref, *refs):
+    pieces, w_ref, o_ref, t_ref = refs[:Z], refs[Z], refs[Z + 1], refs[Z + 2]
+    for s, piece in enumerate(pieces):
+        full, half = chunk_rows(lax.rem(me_ref[2] - s + Z, Z))
+        t_ref[pl.ds(full, FULL), :] = piece[0:FULL, :]
+        t_ref[pl.ds(half, HALF), :] = piece[FULL:CHUNK, :]
+    for h in range(2):
+        attended = dot(t_ref[:, h * TOKENS : (h + 1) * TOKENS], w_ref[...], 0, 0).astype(bf16)
+        o_ref[:, h * SUB : (h + 1) * SUB, :] = attended.reshape(ROWS, SUB, EMBED)
+
+
+def final(me, pieces, w):
     return pl.pallas_call(
         final_kernel,
         out_shape=jax.ShapeDtypeStruct((ROWS, RES, EMBED), bf16),
-        in_specs=[VMEM] * 2,
+        in_specs=[SMEM] + [VMEM] * (Z + 1),
         out_specs=VMEM,
-        scratch_shapes=[pltpu.VMEM((EMBED, ROWS * SUB), bf16)],
-        compiler_params=PARAMS,
-    )(m, w)
+        scratch_shapes=[pltpu.VMEM((EMBED, ROWS * RES), bf16)],
+        compiler_params=PARAMS,
+    )(me, *pieces, w)
 
 
 def flip(x, axes, n, s):
@@ -339,34 +355,37 @@
     return own, far, flip(own, "c", 2, 1), flip(far, "c", 2, 1)
 
 
+def spread(pieces):
+    got = {0: pieces[0]}
+    for s in (1, 7, 2, 6, 3, 5, 4):
+        got[s] = lax.ppermute(pieces[s], "z", [(i, (i + s) % Z) for i in range(Z)])
+    return [got[s] for s in range(Z)]
+
+
 def local(x, wq, wk, wv, wf):
     me = jnp.stack([lax.axis_index(("y", "xh")), lax.axis_index("c"), lax.axis_index("z")])
     me = me.astype(jnp.int32)
-    n, k = key_chunks(x, wk)
+    n, k = key_chunks(me, x, wk)
     q = query_chunks(n, wq)
     v = value_chunks(n, wv)
-    k = lax.all_to_all(k, "z", 0, 0, tiled=True)
-    q, k = lax.optimization_barrier((q, k))
+    k = jnp.stack(spread(k))
+    q, v, k = lax.optimization_barrier((q, v, k))
     q = lax.all_to_all(q, ("z", "c"), 0, 0, tiled=True)
     k00, k01, k10, k11 = gather4(k)
-    parts = score(me, q, keys_laid(k00, k10), k01, k11)
+    parts = score(me, q, keys_laid(me, k00, k10), k01, k11)
     v, kept = lax.optimization_barrier((v, parts[0]))
     parts = [kept] + [flip(parts[s], "y", 4, s) for s in range(1, 4)]
     v = lax.all_to_all(v, "z", 0, 0, tiled=True)
     own, shared, give, give_shared = total(parts)
-    v, own = lax.optimization_barrier((v, own))
-    vs = gather4(v)
-    rows = ROWS * 2 * PEERS
-    probs = softmax(
-        1.0 / math.sqrt(DH * rows),
-        own,
-        flip(give, "xh", 2, 1),
-        flip(shared, "z", Z, 1),
-        flip(give_shared, ("xh", "z"), 2 * Z, Z + 1),
-    )
+    got = flip(give, "xh", 2, 1)
+    near = flip(shared, "z", Z, 1)
+    far = flip(give_shared, ("xh", "z"), 2 * Z, Z + 1)
+    v, got = lax.optimization_barrier((v, got))
+    whole, shared = values_laid(me, v, flip(v, "xl", 2, 1))
+    probs = softmax(1.0 / math.sqrt(DH * ROWS * 2 * PEERS), own, got, near, far)
     probs = lax.all_to_all(probs, ("y", "xh"), 0, 0, tiled=True)
-    mixed = lax.all_to_all(mix(me, values_laid(me, vs), probs), ("z", "c"), 0, 0, tiled=True)
-    return final(mixed, wf)
+    shared, probs = lax.optimization_barrier((shared, probs))
+    return final(me, spread(mix(me, (whole, shared), probs, flip(probs, "c", 2, 1))), wf)
 
 
 def solution(mesh):

time: 188 us -> 183 us (0.973)
  blocking collectives: 29.3 us -> 0 us
  starting transfers between devices: 38.4 us -> 59.9 us
  waiting for transfers between devices: 85 us -> 95.7 us
  local copies, waits for them, and re-layouts: 11.9 us -> 3.25 us
    ppermute x0 -> x14, starting transfers between devices: none -> 31.1 us  [spread(): got[s] = lax.ppermute(pieces[s], 'z', [(i, (i + s) % Z) for i in range(Z)])]
    all_to_all x1 -> x0, blocking collectives: 29.3 us -> none  [local(): lax.all_to_all(mix(me, values_laid(me, vs), probs), ('z', 'c'), 0, 0, til...]
    all_to_all x1 -> x0, waiting for transfers between devices: 20.5 us -> none  [local(): k = lax.all_to_all(k, 'z', 0, 0, tiled=True)]
    ppermute x0 -> x14, waiting for transfers between devices: none -> 20.1 us  [spread(): got[s] = lax.ppermute(pieces[s], 'z', [(i, (i + s) % Z) for i in range(Z)])]
    ppermute x12 -> x11, waiting for transfers between devices: 58 us -> 70.5 us  [flip(): return lax.ppermute(x, axes, [(i, i ^ s) for i in range(n)])]
    all_to_all x1 -> x0, starting transfers between devices: 9.03 us -> none  [local(): k = lax.all_to_all(k, 'z', 0, 0, tiled=True)]
    unnamed x30 -> x29, local copies, waits for them, and re-layouts: 11.9 us -> 3.24 us
    all_to_all x1, waiting for transfers between devices: 4.91 us -> 0.01 us  [local(): probs = lax.all_to_all(probs, ('y', 'xh'), 0, 0, tiled=True)]
  transfers between devices with their start and end apart: 16 -> 28, of which waited for: 13 -> 15; matrix products, arithmetic and copies ran while one was open for 0% -> 0% of each run, Pallas kernels for 5% -> 4%
where the time goes in v6:
time: 183 us; the launch traced here: 180 us
  waiting for transfers between devices  95.7 us (52%)
  starting transfers between devices  59.9 us (33%)
  Pallas kernels  21.2 us (12%)
  local copies, waits for them, and re-layouts  3.25 us (2%)
    ppermute x11, waiting for transfers between devices, flip(): return lax.ppermute(x, axes, [(i, i ^ s) for i in range(n)])  70.5 us
    ppermute x14, starting transfers between devices, spread(): got[s] = lax.ppermute(pieces[s], 'z', [(i, (i + s) % Z) for i in range(Z)])  31.1 us
    ppermute x14, waiting for transfers between devices, spread(): got[s] = lax.ppermute(pieces[s], 'z', [(i, (i + s) % Z) for i in range(Z)])  20.1 us
    ppermute x11, starting transfers between devices, flip(): return lax.ppermute(x, axes, [(i, i ^ s) for i in range(n)])  15.6 us
    all_to_all x1, starting transfers between devices, local(): q = lax.all_to_all(q, ('z', 'c'), 0, 0, tiled=True)  5.97 us
    all_to_all x1, waiting for transfers between devices, local(): q = lax.all_to_all(q, ('z', 'c'), 0, 0, tiled=True)  5.09 us
    pallas_call x1, Pallas kernels, score(): pl.pallas_call(score_kernel, out_shape=(pltpu.HBM((2, SUB, LOGITS), f32),...  5.03 us
    all_to_all x1, starting transfers between devices, local(): v = lax.all_to_all(v, 'z', 0, 0, tiled=True)  3.69 us
  transfers between devices with their start and end apart: 28, of which 15 were waited for; matrix products, arithmetic and copies ran while one was open for 0% of the time, Pallas kernels for 4%

profile of v6, /device:TPU:1, one launch (start us, length us, event | category | flops | bytes accessed | tf_op | source)
XLA Modules:
  0.0 180.4 jit_solution(491047610280008156)
XLA Ops:
  0.1 3.0 %shard_map.55 = (bf16[2,8,32,768]{3,2,1,0:T(8,128)(2,1)S(1)}, bf16[96,512]{1,0:T(8,128)(2,1)S(1)}, bf16[96,512]{1,0:T(8,128)(2,1)S(1)}, bf16[96,512]{1,0:T(8,128...) custom-call(s32[3]{0:T(128)S(1)} %pad_add_fusion.me_ref, ...), custom_call_target="tpu_custom_call" | custom-call | tf_op jit(solution)/shard_map/pallas_call | solution.py:97
  3.1 2.5 %collective-permute-start = (bf16[96,512]{1,0:T(8,128)(2,1)S(1)}, bf16[96,512]{1,0:T(8,128)(2,1)S(1)}, u32[]{:S(2)}, u32[]{:S(2)}) collective-permute-start(bf16[96,512]{1,0:T(8,128)(2,1)S(1)} %get-tuple-element.45), channel_id=1, source_target_pairs={{0,2},{2,4},{4,6},{6,8},{8,10},{10,12},{12,14},{14,0},{1,3},{3,5},... | collective-permute-start | bytes 294920 | tf_op jit(solution)/shard_map/ppermute | solution.py:361
  5.6 3.0 %collective-permute-start.1 = (bf16[96,512]{1,0:T(8,128)(2,1)S(1)}, bf16[96,512]{1,0:T(8,128)(2,1)S(1)}, u32[]{:S(2)}, u32[]{:S(2)}) collective-permute-start(bf16[96,512]{1,0:T(8,128)(2,1)S(1)} %get-tuple-element.46), channel_id=1, source_target_pairs={{0,4},{2,6},{4,8},{6,10},{8,12},{10,14},{12,0},{14,2},{1,5},{3,7},... | collective-permute-start | bytes 294920 | tf_op jit(solution)/shard_map/ppermute | solution.py:361
  8.6 3.8 %collective-permute-start.2 = (bf16[96,512]{1,0:T(8,128)(2,1)S(1)}, bf16[96,512]{1,0:T(8,128)(2,1)S(1)}, u32[]{:S(2)}, u32[]{:S(2)}) collective-permute-start(bf16[96,512]{1,0:T(8,128)(2,1)S(1)} %get-tuple-element.47), channel_id=1, source_target_pairs={{0,6},{2,8},{4,10},{6,12},{8,14},{10,0},{12,2},{14,4},{1,7},{3,9},... | collective-permute-start | bytes 294920 | tf_op jit(solution)/shard_map/ppermute | solution.py:361
  12.8 4.5 %collective-permute-start.4 = (bf16[96,512]{1,0:T(8,128)(2,1)S(1)}, bf16[96,512]{1,0:T(8,128)(2,1)S(1)}, u32[]{:S(2)}, u32[]{:S(2)}) collective-permute-start(bf16[96,512]{1,0:T(8,128)(2,1)S(1)} %get-tuple-element.49), channel_id=1, source_target_pairs={{0,10},{2,12},{4,14},{6,0},{8,2},{10,4},{12,6},{14,8},{1,11},{3,13... | collective-permute-start | bytes 294920 | tf_op jit(solution)/shard_map/ppermute | solution.py:361
  20.8 2.4 %collective-permute-start.5 = (bf16[96,512]{1,0:T(8,128)(2,1)S(1)}, bf16[96,512]{1,0:T(8,128)(2,1)S(1)}, u32[]{:S(2)}, u32[]{:S(2)}) collective-permute-start(bf16[96,512]{1,0:T(8,128)(2,1)S(1)} %get-tuple-element.50), channel_id=1, source_target_pairs={{0,12},{2,14},{4,0},{6,2},{8,4},{10,6},{12,8},{14,10},{1,13},{3,15... | collective-permute-start | bytes 294920 | tf_op jit(solution)/shard_map/ppermute | solution.py:361
  24.7 7.7 %collective-permute-done.5 = bf16[96,512]{1,0:T(8,128)(2,1)S(1)} collective-permute-done((bf16[96,512]{1,0:T(8,128)(2,1)S(1)}, bf16[96,512]{1,0:T(8,128)(2,1)S(1)}, u32[]{:S(2)}, u32[]{:S(2)}) %collective-permute-start.5) | collective-permute-done | bytes 98336 | tf_op jit(solution)/shard_map/ppermute | solution.py:361
  32.4 6.0 %all-to-all-start = ((bf16[16,128,256]{2,1,0:T(8,128)(2,1)}), bf16[16,128,256]{2,1,0:T(8,128)(2,1)S(1)}, u32[]{:S(2)}, u32[]{:S(2)}) async-start(bf16[16,128,256]{2,1,0:T(8,128)(2,1)} %shard_map.56), calls=%async_computation | async-start | bytes 2097152 | tf_op jit(solution)/shard_map/all_to_all | solution.py:373
  40.0 17.3 %collective-permute-done.7.refs_0_ = bf16[8,96,512]{2,1,0:T(8,128)(2,1)S(1)} collective-permute-done((bf16[8,96,512]{2,1,0:T(8,128)(2,1)S(1)}, bf16[8,96,512]{2,1,0:T(8,128)(2,1)S(1)}, u32[]{:S(2)}, u32[]{:S(2)}) %collective-permute-start.7) | collective-permute-done | bytes 786464 | tf_op jit(solution)/shard_map/ppermute | solution.py:350
  61.2 5.1 %all-to-all-done.refs_2_ = bf16[16,128,256]{2,1,0:T(8,128)(2,1)S(1)} async-done(((bf16[16,128,256]{2,1,0:T(8,128)(2,1)}), bf16[16,128,256]{2,1,0:T(8,128)(2,1)S(1)}, u32[]{:S(2)}, u32[]{:S(2)}) %all-to-all-start) | async-done | bytes 1048608 | tf_op jit(solution)/shard_map/all_to_all | solution.py:373
  68.6 5.0 %shard_map.59 = (f32[2,32,1536]{2,1,0:T(8,128)}, f32[2,32,1536]{2,1,0:T(8,128)}, f32[2,32,1536]{2,1,0:T(8,128)}, f32[2,32,1536]{2,1,0:T(8,128)}) custom-call(s32[3]{0:T(128)S(1)} %pad_add_fusion.me_ref, bf16[8,96,512]{2,1,0:T(8,128)(2,1)S(1)} %copy-done.4, bf16[8,96,512]{2,1,0:T(8,128)(2,1)S(1)} %copy-done.6, ...), custom_call_target="tpu_custom_call" | custom-call | tf_op jit(solution)/shard_map/pallas_call | solution.py:215
  73.6 3.7 %all-to-all-start.1 = ((bf16[8,96,512]{2,1,0:T(8,128)(2,1)}), bf16[8,96,512]{2,1,0:T(8,128)(2,1)S(1)}, u32[]{:S(2)}, u32[]{:S(2)}) async-start(bf16[8,96,512]{2,1,0:T(8,128)(2,1)} %shard_map.57), calls=%async_computation.1 | async-start | bytes 1572864 | tf_op jit(solution)/shard_map/all_to_all | solution.py:378
  78.7 2.6 %collective-permute-start.11 = (f32[2,32,1536]{2,1,0:T(8,128)S(1)}, f32[2,32,1536]{2,1,0:T(8,128)S(1)}, u32[]{:S(2)}, u32[]{:S(2)}) collective-permute-start(f32[2,32,1536]{2,1,0:T(8,128)S(1)} %copy-done.9), channel_id=1, source_target_pairs={{0,128},{64,192},{128,0},{192,64},{1,129},{65,193},{129,1},{193,65... | collective-permute-start | bytes 1179656 | tf_op jit(solution)/shard_map/ppermute | solution.py:350
  81.3 6.9 %collective-permute-done.10.p1 = f32[2,32,1536]{2,1,0:T(8,128)S(1)} collective-permute-done((f32[2,32,1536]{2,1,0:T(8,128)S(1)}, f32[2,32,1536]{2,1,0:T(8,128)S(1)}, u32[]{:S(2)}, u32[]{:S(2)}) %collective-permute-start.10) | collective-permute-done | bytes 393248 | tf_op jit(solution)/shard_map/ppermute | solution.py:350
  88.3 10.9 %collective-permute-done.11.p2 = f32[2,32,1536]{2,1,0:T(8,128)S(1)} collective-permute-done((f32[2,32,1536]{2,1,0:T(8,128)S(1)}, f32[2,32,1536]{2,1,0:T(8,128)S(1)}, u32[]{:S(2)}, u32[]{:S(2)}) %collective-permute-start.11) | collective-permute-done | bytes 393248 | tf_op jit(solution)/shard_map/ppermute | solution.py:350
  99.1 2.0 %collective-permute-done.12.p3 = f32[2,32,1536]{2,1,0:T(8,128)S(1)} collective-permute-done((f32[2,32,1536]{2,1,0:T(8,128)S(1)}, f32[2,32,1536]{2,1,0:T(8,128)S(1)}, u32[]{:S(2)}, u32[]{:S(2)}) %collective-permute-start.12) | collective-permute-done | bytes 393248 | tf_op jit(solution)/shard_map/ppermute | solution.py:350
  101.2 2.8 %collective-permute-start.13 = (f32[32,1536]{1,0:T(8,128)S(1)}, f32[32,1536]{1,0:T(8,128)S(1)}, u32[]{:S(2)}, u32[]{:S(2)}) collective-permute-start(f32[32,1536]{1,0:T(8,128)S(1)} %get-tuple-element.63), channel_id=1, source_target_pairs={{0,32},{32,0},{1,33},{33,1},{2,34},{34,2},{3,35},{35,3},{4,36},{36... | collective-permute-start | bytes 589832 | tf_op jit(solution)/shard_map/ppermute | solution.py:350
  105.5 2.4 %collective-permute-done.13.got = f32[32,1536]{1,0:T(8,128)S(1)} collective-permute-done((f32[32,1536]{1,0:T(8,128)S(1)}, f32[32,1536]{1,0:T(8,128)S(1)}, u32[]{:S(2)}, u32[]{:S(2)}) %collective-permute-start.13) | collective-permute-done | bytes 196640 | tf_op jit(solution)/shard_map/ppermute | solution.py:350
  107.8 2.6 %collective-permute-done.16.far = f32[32,512]{1,0:T(8,128)S(1)} collective-permute-done((f32[32,512]{1,0:T(8,128)S(1)}, f32[32,512]{1,0:T(8,128)S(1)}, u32[]{:S(2)}, u32[]{:S(2)}) %collective-permute-start.16) | collective-permute-done | bytes 65568 | tf_op jit(solution)/shard_map/ppermute | solution.py:350
  111.7 3.6 %all-to-all-start.2 = ((bf16[8,2,32,1024]{3,2,1,0:T(8,128)(2,1)}), bf16[8,2,32,1024]{3,2,1,0:T(8,128)(2,1)S(1)}, u32[]{:S(2)}, u32[]{:S(2)}) async-start(bf16[8,2,32,1024]{3,2,1,0:T(8,128)(2,1)} %shard_map.62), calls=%async_computation.2 | async-start | bytes 2097152 | tf_op jit(solution)/shard_map/all_to_all | solution.py:386
  116.2 26.2 %collective-permute-done.14.far_hbm = bf16[8,96,512]{2,1,0:T(8,128)(2,1)S(1)} collective-permute-done((bf16[8,96,512]{2,1,0:T(8,128)(2,1)S(1)}, bf16[8,96,512]{2,1,0:T(8,128)(2,1)S(1)}, u32[]{:S(2)}, u32[]{:S(2)}) %collective-permute-start.14) | collective-permute-done | bytes 786464 | tf_op jit(solution)/shard_map/ppermute | solution.py:350
  142.3 2.0 %shard_map.61 = (bf16[512,1024]{1,0:T(8,128)(2,1)S(1)}, bf16[256,1024]{1,0:T(8,128)(2,1)S(1)}) custom-call(s32[3]{0:T(128)S(1)} %pad_add_fusion.me_ref, bf16[8,96,512]{2,1,0:T(8,128)(2,1)S(1)} %all-to-all-done.1.own_hbm, bf16[8,96,512]{2,1,0:T(8,128)(2,1)S(1)} %collective-permute-done.14.far_hbm), custom_call_target="tpu_custom_call" | custom-call | bytes 6291456 | tf_op jit(solution)/shard_map/pallas_call | solution.py:285
  144.3 3.7 %collective-permute-start.17 = (bf16[8,2,32,1024]{3,2,1,0:T(8,128)(2,1)S(1)}, bf16[8,2,32,1024]{3,2,1,0:T(8,128)(2,1)S(1)}, u32[]{:S(2)}, u32[]{:S(2)}) collective-permute-start(bf16[8,2,32,1024]{3,2,1,0:T(8,128)(2,1)S(1)} %all-to-all-done.2.own_hbm), channel_id=1, source_target_pairs={{0,16},{16,0},{1,17},{17,1},{2,18},{18,2},{3,19},{19,3},{4,20},{20... | collective-permute-start | bytes 3145736 | tf_op jit(solution)/shard_map/ppermute | solution.py:350
  148.0 2.3 %collective-permute-done.17.other_hbm = bf16[8,2,32,1024]{3,2,1,0:T(8,128)(2,1)S(1)} collective-permute-done((bf16[8,2,32,1024]{3,2,1,0:T(8,128)(2,1)S(1)}, bf16[8,2,32,1024]{3,2,1,0:T(8,128)(2,1)S(1)}, u32[]{:S(2)}, u32[]{:S(2)}) %collective-permute-start.17) | collective-permute-done | bytes 1048608 | tf_op jit(solution)/shard_map/ppermute | solution.py:350
  150.3 2.1 %shard_map.63 = (bf16[96,512]{1,0:T(8,128)(2,1)S(1)}, bf16[96,512]{1,0:T(8,128)(2,1)S(1)}, bf16[96,512]{1,0:T(8,128)(2,1)S(1)}, bf16[96,512]{1,0:T(8,128)(2,1)S(...) custom-call(s32[3]{0:T(128)S(1)} %pad_add_fusion.me_ref, ...), custom_call_target="tpu_custom_call" | custom-call | tf_op jit(solution)/shard_map/pallas_call | solution.py:315
  154.9 3.3 %collective-permute-start.20 = (bf16[96,512]{1,0:T(8,128)(2,1)S(1)}, bf16[96,512]{1,0:T(8,128)(2,1)S(1)}, u32[]{:S(2)}, u32[]{:S(2)}) collective-permute-start(bf16[96,512]{1,0:T(8,128)(2,1)S(1)} %get-tuple-element.76), channel_id=1, source_target_pairs={{0,6},{2,8},{4,10},{6,12},{8,14},{10,0},{12,2},{14,4},{1,7},{3,9},... | collective-permute-start | bytes 294920 | tf_op jit(solution)/shard_map/ppermute | solution.py:361
  158.2 2.2 %collective-permute-start.21 = (bf16[96,512]{1,0:T(8,128)(2,1)S(1)}, bf16[96,512]{1,0:T(8,128)(2,1)S(1)}, u32[]{:S(2)}, u32[]{:S(2)}) collective-permute-start(bf16[96,512]{1,0:T(8,128)(2,1)S(1)} %get-tuple-element.77), channel_id=1, source_target_pairs={{0,8},{2,10},{4,12},{6,14},{8,0},{10,2},{12,4},{14,6},{1,9},{3,11}... | collective-permute-start | bytes 294920 | tf_op jit(solution)/shard_map/ppermute | solution.py:361
  160.5 2.4 %collective-permute-start.22 = (bf16[96,512]{1,0:T(8,128)(2,1)S(1)}, bf16[96,512]{1,0:T(8,128)(2,1)S(1)}, u32[]{:S(2)}, u32[]{:S(2)}) collective-permute-start(bf16[96,512]{1,0:T(8,128)(2,1)S(1)} %get-tuple-element.78), channel_id=1, source_target_pairs={{0,10},{2,12},{4,14},{6,0},{8,2},{10,4},{12,6},{14,8},{1,11},{3,13... | collective-permute-start | bytes 294920 | tf_op jit(solution)/shard_map/ppermute | solution.py:361
  162.9 3.3 %collective-permute-start.23 = (bf16[96,512]{1,0:T(8,128)(2,1)S(1)}, bf16[96,512]{1,0:T(8,128)(2,1)S(1)}, u32[]{:S(2)}, u32[]{:S(2)}) collective-permute-start(bf16[96,512]{1,0:T(8,128)(2,1)S(1)} %get-tuple-element.79), channel_id=1, source_target_pairs={{0,12},{2,14},{4,0},{6,2},{8,4},{10,6},{12,8},{14,10},{1,13},{3,15... | collective-permute-start | bytes 294920 | tf_op jit(solution)/shard_map/ppermute | solution.py:361
  167.1 5.3 %collective-permute-done.21.refs_4_ = bf16[96,512]{1,0:T(8,128)(2,1)S(1)} collective-permute-done((bf16[96,512]{1,0:T(8,128)(2,1)S(1)}, bf16[96,512]{1,0:T(8,128)(2,1)S(1)}, u32[]{:S(2)}, u32[]{:S(2)}) %collective-permute-start.21) | collective-permute-done | bytes 98336 | tf_op jit(solution)/shard_map/ppermute | solution.py:361
  172.6 5.5 %collective-permute-done.23.refs_6_ = bf16[96,512]{1,0:T(8,128)(2,1)S(1)} collective-permute-done((bf16[96,512]{1,0:T(8,128)(2,1)S(1)}, bf16[96,512]{1,0:T(8,128)(2,1)S(1)}, u32[]{:S(2)}, u32[]{:S(2)}) %collective-permute-start.23) | collective-permute-done | bytes 98336 | tf_op jit(solution)/shard_map/ppermute | solution.py:361
  178.1 2.3 %shard_map.64 = bf16[8,64,768]{2,1,0:T(8,128)(2,1)} custom-call(s32[3]{0:T(128)S(1)} %pad_add_fusion.me_ref, bf16[96,512]{1,0:T(8,128)(2,1)S(1)} %get-tuple-element.73.refs_0_, bf16[96,512]{1,0:T(8,128)(2,1)S(1)} %collective-permute-done.18.refs_1_, bf16[96,512]{1,0:T(8,128)(2,1)S(1)} %collective-permute-done.19.refs_2_, ...), custom_call_target="tpu_custom_call" | custom-call | tf_op jit(solution)/shard_map/pallas_call | solution.py:339
  (65 shorter events, 22.0 us)
Async XLA Ops:
  0.0 17.3 %copy-start.1 = (bf16[768,768]{1,0:T(8,128)(2,1)S(1)}, bf16[768,768]{1,0:T(8,128)(2,1)}, u32[]{:S(2)}) copy-start(bf16[768,768]{1,0:T(8,128)(2,1)} %w_ref.3) | copy-start | bytes 3538948
  3.1 17.8 %collective-permute-start = (bf16[96,512]{1,0:T(8,128)(2,1)S(1)}, bf16[96,512]{1,0:T(8,128)(2,1)S(1)}, u32[]{:S(2)}, u32[]{:S(2)}) collective-permute-start(bf16[96,512]{1,0:T(8,128)(2,1)S(1)} %get-tuple-element.45), channel_id=1, source_target_pairs={{0,2},{2,4},{4,6},{6,8},{8,10},{10,12},{12,14},{14,0},{1,3},{3,5},... | collective-permute-start | bytes 294920 | tf_op jit(solution)/shard_map/ppermute | solution.py:361
  5.6 17.6 %collective-permute-start.1 = (bf16[96,512]{1,0:T(8,128)(2,1)S(1)}, bf16[96,512]{1,0:T(8,128)(2,1)S(1)}, u32[]{:S(2)}, u32[]{:S(2)}) collective-permute-start(bf16[96,512]{1,0:T(8,128)(2,1)S(1)} %get-tuple-element.46), channel_id=1, source_target_pairs={{0,4},{2,6},{4,8},{6,10},{8,12},{10,14},{12,0},{14,2},{1,5},{3,7},... | collective-permute-start | bytes 294920 | tf_op jit(solution)/shard_map/ppermute | solution.py:361
  8.6 15.5 %collective-permute-start.2 = (bf16[96,512]{1,0:T(8,128)(2,1)S(1)}, bf16[96,512]{1,0:T(8,128)(2,1)S(1)}, u32[]{:S(2)}, u32[]{:S(2)}) collective-permute-start(bf16[96,512]{1,0:T(8,128)(2,1)S(1)} %get-tuple-element.47), channel_id=1, source_target_pairs={{0,6},{2,8},{4,10},{6,12},{8,14},{10,0},{12,2},{14,4},{1,7},{3,9},... | collective-permute-start | bytes 294920 | tf_op jit(solution)/shard_map/ppermute | solution.py:361
  12.4 12.3 %collective-permute-start.3 = (bf16[96,512]{1,0:T(8,128)(2,1)S(1)}, bf16[96,512]{1,0:T(8,128)(2,1)S(1)}, u32[]{:S(2)}, u32[]{:S(2)}) collective-permute-start(bf16[96,512]{1,0:T(8,128)(2,1)S(1)} %get-tuple-element.48), channel_id=1, source_target_pairs={{0,8},{2,10},{4,12},{6,14},{8,0},{10,2},{12,4},{14,6},{1,9},{3,11}... | collective-permute-start | bytes 294920 | tf_op jit(solution)/shard_map/ppermute | solution.py:361
  12.8 11.8 %collective-permute-start.4 = (bf16[96,512]{1,0:T(8,128)(2,1)S(1)}, bf16[96,512]{1,0:T(8,128)(2,1)S(1)}, u32[]{:S(2)}, u32[]{:S(2)}) collective-permute-start(bf16[96,512]{1,0:T(8,128)(2,1)S(1)} %get-tuple-element.49), channel_id=1, source_target_pairs={{0,10},{2,12},{4,14},{6,0},{8,2},{10,4},{12,6},{14,8},{1,11},{3,13... | collective-permute-start | bytes 294920 | tf_op jit(solution)/shard_map/ppermute | solution.py:361
  20.8 11.5 %collective-permute-start.5 = (bf16[96,512]{1,0:T(8,128)(2,1)S(1)}, bf16[96,512]{1,0:T(8,128)(2,1)S(1)}, u32[]{:S(2)}, u32[]{:S(2)}) collective-permute-start(bf16[96,512]{1,0:T(8,128)(2,1)S(1)} %get-tuple-element.50), channel_id=1, source_target_pairs={{0,12},{2,14},{4,0},{6,2},{8,4},{10,6},{12,8},{14,10},{1,13},{3,15... | collective-permute-start | bytes 294920 | tf_op jit(solution)/shard_map/ppermute | solution.py:361
  23.2 9.1 %collective-permute-start.6 = (bf16[96,512]{1,0:T(8,128)(2,1)S(1)}, bf16[96,512]{1,0:T(8,128)(2,1)S(1)}, u32[]{:S(2)}, u32[]{:S(2)}) collective-permute-start(bf16[96,512]{1,0:T(8,128)(2,1)S(1)} %get-tuple-element.51), channel_id=1, source_target_pairs={{0,14},{2,0},{4,2},{6,4},{8,6},{10,8},{12,10},{14,12},{1,15},{3,1}... | collective-permute-start | bytes 294920 | tf_op jit(solution)/shard_map/ppermute | solution.py:361
  32.4 33.9 %all-to-all-start = ((bf16[16,128,256]{2,1,0:T(8,128)(2,1)}), bf16[16,128,256]{2,1,0:T(8,128)(2,1)S(1)}, u32[]{:S(2)}, u32[]{:S(2)}) async-start(bf16[16,128,256]{2,1,0:T(8,128)(2,1)} %shard_map.56), calls=%async_computation | async-start | bytes 2097152 | tf_op jit(solution)/shard_map/all_to_all | solution.py:373
  38.4 19.0 %collective-permute-start.7 = (bf16[8,96,512]{2,1,0:T(8,128)(2,1)S(1)}, bf16[8,96,512]{2,1,0:T(8,128)(2,1)S(1)}, u32[]{:S(2)}, u32[]{:S(2)}) collective-permute-start(bf16[8,96,512]{2,1,0:T(8,128)(2,1)S(1)} %bitcast_dynamic-update-slice_fusion.own), channel_id=1, source_target_pairs={{0,1},{1,0},{2,3},{3,2},{4,5},{5,4},{6,7},{7,6},{8,9},{9,8},{10,11... | collective-permute-start | bytes 2359304 | tf_op jit(solution)/shard_map/ppermute | solution.py:350
  39.6 18.8 %collective-permute-start.9 = (bf16[8,96,512]{2,1,0:T(8,128)(2,1)S(1)}, bf16[8,96,512]{2,1,0:T(8,128)(2,1)S(1)}, u32[]{:S(2)}, u32[]{:S(2)}) collective-permute-start(bf16[8,96,512]{2,1,0:T(8,128)(2,1)S(1)} %bitcast_dynamic-update-slice_fusion.own), channel_id=1, source_target_pairs={{0,16},{16,0},{1,17},{17,1},{2,18},{18,2},{3,19},{19,3},{4,20},{20... | collective-permute-start | bytes 2359304 | tf_op jit(solution)/shard_map/ppermute | solution.py:350
  57.3 3.0 %collective-permute-start.8 = (bf16[8,96,512]{2,1,0:T(8,128)(2,1)S(1)}, bf16[8,96,512]{2,1,0:T(8,128)(2,1)S(1)}, u32[]{:S(2)}, u32[]{:S(2)}) collective-permute-start(bf16[8,96,512]{2,1,0:T(8,128)(2,1)S(1)} %collective-permute-done.7.refs_0_), channel_id=1, source_target_pairs={{0,16},{16,0},{1,17},{17,1},{2,18},{18,2},{3,19},{19,3},{4,20},{20... | collective-permute-start | bytes 2359304 | tf_op jit(solution)/shard_map/ppermute | solution.py:350
  73.6 7.7 %copy-start.8 = (f32[2,32,1536]{2,1,0:T(8,128)S(1)}, f32[2,32,1536]{2,1,0:T(8,128)}, u32[]{:S(2)}) copy-start(f32[2,32,1536]{2,1,0:T(8,128)} %get-tuple-element.62) | copy-start | bytes 1179652
  73.6 27.5 %copy-start.7 = (f32[2,32,1536]{2,1,0:T(8,128)S(1)}, f32[2,32,1536]{2,1,0:T(8,128)}, u32[]{:S(2)}) copy-start(f32[2,32,1536]{2,1,0:T(8,128)} %get-tuple-element.59.p0) | copy-start | bytes 1179652
  73.6 34.2 %all-to-all-start.1 = ((bf16[8,96,512]{2,1,0:T(8,128)(2,1)}), bf16[8,96,512]{2,1,0:T(8,128)(2,1)S(1)}, u32[]{:S(2)}, u32[]{:S(2)}) async-start(bf16[8,96,512]{2,1,0:T(8,128)(2,1)} %shard_map.57), calls=%async_computation.1 | async-start | bytes 1572864 | tf_op jit(solution)/shard_map/all_to_all | solution.py:378
  77.4 10.9 %collective-permute-start.10 = (f32[2,32,1536]{2,1,0:T(8,128)S(1)}, f32[2,32,1536]{2,1,0:T(8,128)S(1)}, u32[]{:S(2)}, u32[]{:S(2)}) collective-permute-start(f32[2,32,1536]{2,1,0:T(8,128)S(1)} %copy-done.10), channel_id=1, source_target_pairs={{0,64},{64,0},{128,192},{192,128},{1,65},{65,1},{129,193},{193,129... | collective-permute-start | bytes 1179656 | tf_op jit(solution)/shard_map/ppermute | solution.py:350
  78.7 20.4 %collective-permute-start.11 = (f32[2,32,1536]{2,1,0:T(8,128)S(1)}, f32[2,32,1536]{2,1,0:T(8,128)S(1)}, u32[]{:S(2)}, u32[]{:S(2)}) collective-permute-start(f32[2,32,1536]{2,1,0:T(8,128)S(1)} %copy-done.9), channel_id=1, source_target_pairs={{0,128},{64,192},{128,0},{192,64},{1,129},{65,193},{129,1},{193,65... | collective-permute-start | bytes 1179656 | tf_op jit(solution)/shard_map/ppermute | solution.py:350
  81.3 19.8 %collective-permute-start.12 = (f32[2,32,1536]{2,1,0:T(8,128)S(1)}, f32[2,32,1536]{2,1,0:T(8,128)S(1)}, u32[]{:S(2)}, u32[]{:S(2)}) collective-permute-start(f32[2,32,1536]{2,1,0:T(8,128)S(1)} %copy-done.8), channel_id=1, source_target_pairs={{0,192},{64,128},{128,64},{192,0},{1,193},{65,129},{129,65},{193,1... | collective-permute-start | bytes 1179656 | tf_op jit(solution)/shard_map/ppermute | solution.py:350
  101.2 6.6 %collective-permute-start.13 = (f32[32,1536]{1,0:T(8,128)S(1)}, f32[32,1536]{1,0:T(8,128)S(1)}, u32[]{:S(2)}, u32[]{:S(2)}) collective-permute-start(f32[32,1536]{1,0:T(8,128)S(1)} %get-tuple-element.63), channel_id=1, source_target_pairs={{0,32},{32,0},{1,33},{33,1},{2,34},{34,2},{3,35},{35,3},{4,36},{36... | collective-permute-start | bytes 589832 | tf_op jit(solution)/shard_map/ppermute | solution.py:350
  104.0 3.8 %collective-permute-start.15 = (f32[32,512]{1,0:T(8,128)S(1)}, f32[32,512]{1,0:T(8,128)S(1)}, u32[]{:S(2)}, u32[]{:S(2)}) collective-permute-start(f32[32,512]{1,0:T(8,128)S(1)} %get-tuple-element.68), channel_id=1, source_target_pairs={{0,2},{2,0},{4,6},{6,4},{8,10},{10,8},{12,14},{14,12},{1,3},{3,1},... | collective-permute-start | bytes 196616 | tf_op jit(solution)/shard_map/ppermute | solution.py:350
  104.9 5.5 %collective-permute-start.16 = (f32[32,512]{1,0:T(8,128)S(1)}, f32[32,512]{1,0:T(8,128)S(1)}, u32[]{:S(2)}, u32[]{:S(2)}) collective-permute-start(f32[32,512]{1,0:T(8,128)S(1)} %get-tuple-element.69), channel_id=1, source_target_pairs={{0,34},{2,32},{4,38},{6,36},{8,42},{10,40},{12,46},{14,44},{32,2},... | collective-permute-start | bytes 196616 | tf_op jit(solution)/shard_map/ppermute | solution.py:350
  111.7 32.6 %all-to-all-start.2 = ((bf16[8,2,32,1024]{3,2,1,0:T(8,128)(2,1)}), bf16[8,2,32,1024]{3,2,1,0:T(8,128)(2,1)S(1)}, u32[]{:S(2)}, u32[]{:S(2)}) async-start(bf16[8,2,32,1024]{3,2,1,0:T(8,128)(2,1)} %shard_map.62), calls=%async_computation.2 | async-start | bytes 2097152 | tf_op jit(solution)/shard_map/all_to_all | solution.py:386
  115.2 27.1 %collective-permute-start.14 = (bf16[8,96,512]{2,1,0:T(8,128)(2,1)S(1)}, bf16[8,96,512]{2,1,0:T(8,128)(2,1)S(1)}, u32[]{:S(2)}, u32[]{:S(2)}) collective-permute-start(bf16[8,96,512]{2,1,0:T(8,128)(2,1)S(1)} %all-to-all-done.1.own_hbm), channel_id=1, source_target_pairs={{0,1},{1,0},{2,3},{3,2},{4,5},{5,4},{6,7},{7,6},{8,9},{9,8},{10,11... | collective-permute-start | bytes 2359304 | tf_op jit(solution)/shard_map/ppermute | solution.py:350
  144.3 6.0 %collective-permute-start.17 = (bf16[8,2,32,1024]{3,2,1,0:T(8,128)(2,1)S(1)}, bf16[8,2,32,1024]{3,2,1,0:T(8,128)(2,1)S(1)}, u32[]{:S(2)}, u32[]{:S(2)}) collective-permute-start(bf16[8,2,32,1024]{3,2,1,0:T(8,128)(2,1)S(1)} %all-to-all-done.2.own_hbm), channel_id=1, source_target_pairs={{0,16},{16,0},{1,17},{17,1},{2,18},{18,2},{3,19},{19,3},{4,20},{20... | collective-permute-start | bytes 3145736 | tf_op jit(solution)/shard_map/ppermute | solution.py:350
  150.3 27.7 %copy-start = (bf16[768,768]{1,0:T(8,128)(2,1)S(1)}, bf16[768,768]{1,0:T(8,128)(2,1)}, u32[]{:S(2)}) copy-start(bf16[768,768]{1,0:T(8,128)(2,1)} %refs_8_.1) | copy-start | bytes 3538948
  152.5 10.5 %collective-permute-start.18 = (bf16[96,512]{1,0:T(8,128)(2,1)S(1)}, bf16[96,512]{1,0:T(8,128)(2,1)S(1)}, u32[]{:S(2)}, u32[]{:S(2)}) collective-permute-start(bf16[96,512]{1,0:T(8,128)(2,1)S(1)} %get-tuple-element.74), channel_id=1, source_target_pairs={{0,2},{2,4},{4,6},{6,8},{8,10},{10,12},{12,14},{14,0},{1,3},{3,5},... | collective-permute-start | bytes 294920 | tf_op jit(solution)/shard_map/ppermute | solution.py:361
  153.3 12.9 %collective-permute-start.19 = (bf16[96,512]{1,0:T(8,128)(2,1)S(1)}, bf16[96,512]{1,0:T(8,128)(2,1)S(1)}, u32[]{:S(2)}, u32[]{:S(2)}) collective-permute-start(bf16[96,512]{1,0:T(8,128)(2,1)S(1)} %get-tuple-element.75), channel_id=1, source_target_pairs={{0,4},{2,6},{4,8},{6,10},{8,12},{10,14},{12,0},{14,2},{1,5},{3,7},... | collective-permute-start | bytes 294920 | tf_op jit(solution)/shard_map/ppermute | solution.py:361
  154.9 12.2 %collective-permute-start.20 = (bf16[96,512]{1,0:T(8,128)(2,1)S(1)}, bf16[96,512]{1,0:T(8,128)(2,1)S(1)}, u32[]{:S(2)}, u32[]{:S(2)}) collective-permute-start(bf16[96,512]{1,0:T(8,128)(2,1)S(1)} %get-tuple-element.76), channel_id=1, source_target_pairs={{0,6},{2,8},{4,10},{6,12},{8,14},{10,0},{12,2},{14,4},{1,7},{3,9},... | collective-permute-start | bytes 294920 | tf_op jit(solution)/shard_map/ppermute | solution.py:361
  158.2 14.2 %collective-permute-start.21 = (bf16[96,512]{1,0:T(8,128)(2,1)S(1)}, bf16[96,512]{1,0:T(8,128)(2,1)S(1)}, u32[]{:S(2)}, u32[]{:S(2)}) collective-permute-start(bf16[96,512]{1,0:T(8,128)(2,1)S(1)} %get-tuple-element.77), channel_id=1, source_target_pairs={{0,8},{2,10},{4,12},{6,14},{8,0},{10,2},{12,4},{14,6},{1,9},{3,11}... | collective-permute-start | bytes 294920 | tf_op jit(solution)/shard_map/ppermute | solution.py:361
  160.5 12.1 %collective-permute-start.22 = (bf16[96,512]{1,0:T(8,128)(2,1)S(1)}, bf16[96,512]{1,0:T(8,128)(2,1)S(1)}, u32[]{:S(2)}, u32[]{:S(2)}) collective-permute-start(bf16[96,512]{1,0:T(8,128)(2,1)S(1)} %get-tuple-element.78), channel_id=1, source_target_pairs={{0,10},{2,12},{4,14},{6,0},{8,2},{10,4},{12,6},{14,8},{1,11},{3,13... | collective-permute-start | bytes 294920 | tf_op jit(solution)/shard_map/ppermute | solution.py:361
  162.9 15.1 %collective-permute-start.23 = (bf16[96,512]{1,0:T(8,128)(2,1)S(1)}, bf16[96,512]{1,0:T(8,128)(2,1)S(1)}, u32[]{:S(2)}, u32[]{:S(2)}) collective-permute-start(bf16[96,512]{1,0:T(8,128)(2,1)S(1)} %get-tuple-element.79), channel_id=1, source_target_pairs={{0,12},{2,14},{4,0},{6,2},{8,4},{10,6},{12,8},{14,10},{1,13},{3,15... | collective-permute-start | bytes 294920 | tf_op jit(solution)/shard_map/ppermute | solution.py:361
  166.2 11.8 %collective-permute-start.24 = (bf16[96,512]{1,0:T(8,128)(2,1)S(1)}, bf16[96,512]{1,0:T(8,128)(2,1)S(1)}, u32[]{:S(2)}, u32[]{:S(2)}) collective-permute-start(bf16[96,512]{1,0:T(8,128)(2,1)S(1)} %get-tuple-element.80), channel_id=1, source_target_pairs={{0,14},{2,0},{4,2},{6,4},{8,6},{10,8},{12,10},{14,12},{1,15},{3,1}... | collective-permute-start | bytes 294920 | tf_op jit(solution)/shard_map/ppermute | solution.py:361
  (7 other events, 16.7 us)

commit v7 on v6

--- a/solution.py
+++ b/solution.py
@@ -36,7 +36,6 @@
 VMEM = pl.BlockSpec(memory_space=pltpu.VMEM)
 SMEM = pl.BlockSpec(memory_space=pltpu.SMEM)
 ANY = pl.BlockSpec(memory_space=pl.ANY)
-HBM = pl.BlockSpec(memory_space=pltpu.HBM)
 
 
 def chunk_pieces(z):
@@ -131,23 +130,25 @@
     )(n, w)
 
 
-def value_kernel(n_ref, w_ref, v_ref):
-    t = dot(w_ref[...], n_ref[...].reshape(ROWS * RES, EMBED), 0, 1).astype(bf16)
-    for z in range(Z):
-        (a, na), (b, nb) = chunk_pieces(z)
-        v_ref[z, 0:FULL, :] = t[a : a + na]
-        v_ref[z, FULL:CHUNK, :] = t[b : b + nb]
-
-
-def value_chunks(n, w):
+def value_kernel(me_ref, n_ref, w_ref, *rest):
+    outs, t_ref = rest[:Z], rest[Z]
+    t_ref[...] = dot(w_ref[...], n_ref[...].reshape(ROWS * RES, EMBED), 0, 1).astype(bf16)
+    for s, out in enumerate(outs):
+        full, half = chunk_rows(lax.rem(me_ref[2] + s, Z))
+        out[0:FULL, :] = t_ref[pl.ds(full, FULL), :]
+        out[FULL:CHUNK, :] = t_ref[pl.ds(half, HALF), :]
+
+
+def value_chunks(me, n, w):
     return pl.pallas_call(
         value_kernel,
-        out_shape=jax.ShapeDtypeStruct((Z, CHUNK, ROWS * RES), bf16),
-        in_specs=[VMEM, VMEM],
-        out_specs=VMEM,
+        out_shape=(jax.ShapeDtypeStruct((CHUNK, ROWS * RES), bf16),) * Z,
+        in_specs=[SMEM, VMEM, VMEM],
+        out_specs=(VMEM,) * Z,
+        scratch_shapes=[pltpu.VMEM((EMBED, ROWS * RES), bf16)],
         compiler_params=PARAMS,
         cost_estimate=PROJECTION,
-    )(n, w)
+    )(me, n, w)
 
 
 def lay_keys(me, own, other, kf, kh):
@@ -182,8 +183,8 @@
 
 
 def score_kernel(me_ref, *refs):
-    sources, results, rest = refs[:5], refs[5:9], refs[9:]
-    outs, (qf, qh, kf1, kh1), sems = rest[5], rest[6:10], rest[10]
+    sources, outs, rest = refs[:5], refs[5:9], refs[9:]
+    (qf, qh, kf1, kh1), sems = rest[5:9], rest[9]
     own, other, q_ref, kf0, kh0 = rest[:5]
     copies = fetches(sources, rest[:5], sems)
     for copy in copies[:2]:
@@ -204,21 +205,18 @@
     for a, b in ((qf, kf0), (qf, kf1), (qh, kh0), (qh, kh1)):
         t = dot(a[...], b[...], 0, 0)
         for p in range(PEERS):
-            outs[p // 2, p % 2, :, first : first + t.shape[1]] = t[p * SUB : (p + 1) * SUB]
+            outs[p // 2][p % 2, :, first : first + t.shape[1]] = t[p * SUB : (p + 1) * SUB]
         first += t.shape[1]
-    for copy in fetches([outs.at[s] for s in range(4)], results, sems):
-        copy.wait()
 
 
 def score(me, q, laid, own, other):
     rows = 2 * ROWS * FULL
     return pl.pallas_call(
         score_kernel,
-        out_shape=(pltpu.HBM((2, SUB, LOGITS), f32),) * 4,
+        out_shape=(jax.ShapeDtypeStruct((2, SUB, LOGITS), f32),) * 4,
         in_specs=[SMEM] + [ANY] * 5,
-        out_specs=(HBM,) * 4,
+        out_specs=(VMEM,) * 4,
         scratch_shapes=[pltpu.VMEM(a.shape, bf16) for a in (own, other, q, *laid)]
-        + [pltpu.VMEM((4, 2, SUB, LOGITS), f32)]
         + [pltpu.VMEM((rows, QUERIES), bf16)] * 2
         + [pltpu.VMEM(s, bf16) for s in KEY_SHAPES]
         + [pltpu.SemaphoreType.DMA((5,))],
@@ -264,47 +262,49 @@
     )(*parts)
 
 
-def values_kernel(me_ref, own_hbm, far_hbm, vf, vh, own, far, sems):
-    for copy in fetches((own_hbm, far_hbm), (own, far), sems):
-        copy.wait()
-    odd = lax.rem(me_ref[2], 2)
+def values_kernel(me_ref, v_hbm, vf, vh, v, sems):
+    fetches((v_hbm,), (v,), sems)[0].wait()
+    z = me_ref[2]
+    odd = lax.rem(z, 2)
+    where = [lax.rem(z - source + Z, Z) for source in range(Z)]
     halves = [
-        ref[z, FULL:CHUNK, pl.ds(pl.multiple_of(h * TOKENS, TOKENS), TOKENS)]
-        for h in (odd, 1 - odd)
-        for ref in (own, far)
-        for z in range(Z)
+        v[i, FULL:CHUNK, pl.ds(pl.multiple_of(h * TOKENS, TOKENS), TOKENS)] for h in (odd, 1 - odd) for i in where
     ]
-    whole = [ref[z, 0:FULL, h * TOKENS : (h + 1) * TOKENS] for ref in (own, far) for z in range(Z) for h in range(2)]
+    whole = [v[i, 0:FULL, h * TOKENS : (h + 1) * TOKENS] for i in where for h in range(2)]
     for r in range(ROWS):
         lanes = slice(r * SUB, (r + 1) * SUB)
         vf[r * FULL : (r + 1) * FULL, :] = jnp.concatenate([b[:, lanes] for b in whole], axis=1)
         vh[r * HALF : (r + 1) * HALF, :] = jnp.concatenate([b[:, lanes] for b in halves], axis=1)
 
 
-def values_laid(me, own, far):
+def values_laid(me, v):
     return pl.pallas_call(
         values_kernel,
-        out_shape=tuple(jax.ShapeDtypeStruct((ROWS * n, KEYS), bf16) for n in (FULL, HALF)),
-        in_specs=[SMEM] + [ANY] * 2,
+        out_shape=tuple(jax.ShapeDtypeStruct((ROWS * n, KEYS // 2), bf16) for n in (FULL, HALF)),
+        in_specs=[SMEM, ANY],
         out_specs=(VMEM,) * 2,
-        scratch_shapes=[pltpu.VMEM(own.shape, bf16)] * 2 + [pltpu.SemaphoreType.DMA((2,))],
-        compiler_params=WIDE,
+        scratch_shapes=[pltpu.VMEM(v.shape, bf16), pltpu.SemaphoreType.DMA((1,))],
+        compiler_params=PARAMS,
         cost_estimate=LAYOUT,
-    )(me, own, far)
-
-
-def mix_kernel(me_ref, own_hbm, other_hbm, vf_hbm, vh_hbm, *rest):
-    outs, (p_ref, vf, vh, sems) = rest[:Z], rest[Z:]
+    )(me, v)
+
+
+def mix_kernel(me_ref, own_hbm, other_hbm, *rest):
+    laid, outs, (p_ref, vf0, vh0, vf1, vh1, sems) = rest[:4], rest[4 : 4 + Z], rest[4 + Z :]
     core, z = me_ref[1], me_ref[2]
     copies = fetches(
-        (own_hbm, other_hbm, vf_hbm, vh_hbm), (p_ref.at[core], p_ref.at[1 - core], vf, vh), sems
+        (own_hbm, other_hbm, *laid), (p_ref.at[core], p_ref.at[1 - core], vf0, vh0, vf1, vh1), sems
     )
     for copy in copies:
         copy.wait()
-    for i, (v, first, n) in enumerate(((vf, 0, FULL), (vh, FULL, HALF))):
+    quarter = KEYS // 4
+    for i, (near, far, first, n) in enumerate(((vf0, vf1, 0, FULL), (vh0, vh1, FULL, HALF))):
         for h in range(2):
             probs = jnp.concatenate([p_ref[h, lax.rem(z + s, Z), i] for s in range(Z)], axis=0)
-            mixed = dot(v[...], probs, 1, 1).astype(bf16)
+            quarters = [probs[:, k * quarter : (k + 1) * quarter] for k in range(4)]
+            a, b = (quarters[:2], quarters[2:]) if i == 0 else (quarters[::2], quarters[1::2])
+            mixed = dot(near[...], jnp.concatenate(a, axis=1), 1, 1) + dot(far[...], jnp.concatenate(b, axis=1), 1, 1)
+            mixed = mixed.astype(bf16)
             for s, out in enumerate(outs):
                 out[first : first + n, h * TOKENS : (h + 1) * TOKENS] = jnp.concatenate(
                     [mixed[r * n : (r + 1) * n, s * SUB : (s + 1) * SUB] for r in range(ROWS)], axis=1
@@ -315,11 +315,11 @@
     return pl.pallas_call(
         mix_kernel,
         out_shape=(jax.ShapeDtypeStruct((CHUNK, ROWS * RES), bf16),) * Z,
-        in_specs=[SMEM] + [ANY] * 4,
+        in_specs=[SMEM] + [ANY] * 6,
         out_specs=(VMEM,) * Z,
         scratch_shapes=[pltpu.VMEM((2, *own.shape), bf16)]
         + [pltpu.VMEM(a.shape, bf16) for a in laid]
-        + [pltpu.SemaphoreType.DMA((4,))],
+        + [pltpu.SemaphoreType.DMA((6,))],
         compiler_params=WIDE,
     )(me, own, other, *laid)
 
@@ -366,26 +366,26 @@
     me = jnp.stack([lax.axis_index(("y", "xh")), lax.axis_index("c"), lax.axis_index("z")])
     me = me.astype(jnp.int32)
     n, k = key_chunks(me, x, wk)
+    k = spread(k)
+    n, k[2] = lax.optimization_barrier((n, k[2]))
     q = query_chunks(n, wq)
-    v = value_chunks(n, wv)
-    k = jnp.stack(spread(k))
-    q, v, k = lax.optimization_barrier((q, v, k))
+    k = jnp.stack(k)
+    q, k = lax.optimization_barrier((q, k))
     q = lax.all_to_all(q, ("z", "c"), 0, 0, tiled=True)
     k00, k01, k10, k11 = gather4(k)
     parts = score(me, q, keys_laid(me, k00, k10), k01, k11)
-    v, kept = lax.optimization_barrier((v, parts[0]))
-    parts = [kept] + [flip(parts[s], "y", 4, s) for s in range(1, 4)]
-    v = lax.all_to_all(v, "z", 0, 0, tiled=True)
+    parts = [parts[0]] + [flip(parts[s], "y", 4, s) for s in range(1, 4)]
+    n, parts[1] = lax.optimization_barrier((n, parts[1]))
+    v = jnp.stack(spread(value_chunks(me, n, wv)))
     own, shared, give, give_shared = total(parts)
     got = flip(give, "xh", 2, 1)
     near = flip(shared, "z", Z, 1)
     far = flip(give_shared, ("xh", "z"), 2 * Z, Z + 1)
-    v, got = lax.optimization_barrier((v, got))
-    whole, shared = values_laid(me, v, flip(v, "xl", 2, 1))
     probs = softmax(1.0 / math.sqrt(DH * ROWS * 2 * PEERS), own, got, near, far)
     probs = lax.all_to_all(probs, ("y", "xh"), 0, 0, tiled=True)
-    shared, probs = lax.optimization_barrier((shared, probs))
-    return final(me, spread(mix(me, (whole, shared), probs, flip(probs, "c", 2, 1))), wf)
+    laid = [*values_laid(me, v), *values_laid(me, flip(v, "xl", 2, 1))]
+    laid[3], probs = lax.optimization_barrier((laid[3], probs))
+    return final(me, spread(mix(me, laid, probs, flip(probs, "c", 2, 1))), wf)
 
 
 def solution(mesh):

time: 183 us -> 190 us (1.038)
  waiting for transfers between devices: 95.7 us -> 107 us
    ppermute x14 -> x21, waiting for transfers between devices: 20.1 us -> 32 us  [spread(): got[s] = lax.ppermute(pieces[s], 'z', [(i, (i + s) % Z) for i in range(Z)])]
    ppermute x14 -> x21, starting transfers between devices: 31.1 us -> 37.3 us  [spread(): got[s] = lax.ppermute(pieces[s], 'z', [(i, (i + s) % Z) for i in range(Z)])]
    all_to_all x1 -> x0, starting transfers between devices: 3.69 us -> none  [local(): v = lax.all_to_all(v, 'z', 0, 0, tiled=True)]
    ppermute x11, starting transfers between devices: 15.6 us -> 12.3 us  [flip(): return lax.ppermute(x, axes, [(i, i ^ s) for i in range(n)])]
  transfers between devices with their start and end apart: 28 -> 34, of which waited for: 15 -> 18; matrix products, arithmetic and copies ran while one was open for 0% -> 0% of each run, Pallas kernels for 4% -> 5%
where the time goes in v7:
time: 190 us; the launch traced here: 189 us
  waiting for transfers between devices  107 us (56%)
  starting transfers between devices  58.1 us (31%)
  Pallas kernels  20.4 us (11%)
  local copies, waits for them, and re-layouts  3.3 us (2%)
    ppermute x11, waiting for transfers between devices, flip(): return lax.ppermute(x, axes, [(i, i ^ s) for i in range(n)])  69.5 us
    ppermute x21, starting transfers between devices, spread(): got[s] = lax.ppermute(pieces[s], 'z', [(i, (i + s) % Z) for i in range(Z)])  37.3 us
    ppermute x21, waiting for transfers between devices, spread(): got[s] = lax.ppermute(pieces[s], 'z', [(i, (i + s) % Z) for i in range(Z)])  32 us
    ppermute x11, starting transfers between devices, flip(): return lax.ppermute(x, axes, [(i, i ^ s) for i in range(n)])  12.3 us
    all_to_all x1, waiting for transfers between devices, local(): q = lax.all_to_all(q, ('z', 'c'), 0, 0, tiled=True)  5.09 us
    all_to_all x1, starting transfers between devices, local(): q = lax.all_to_all(q, ('z', 'c'), 0, 0, tiled=True)  5.06 us
    pallas_call x1, Pallas kernels, score(): pl.pallas_call(score_kernel, out_shape=(jax.ShapeDtypeStruct((2, SUB, LOG...  3.88 us
  transfers between devices with their start and end apart: 34, of which 18 were waited for; matrix products, arithmetic and copies ran while one was open for 0% of the time, Pallas kernels for 5%

profile of v7, /device:TPU:1, one launch (start us, length us, event | category | flops | bytes accessed | tf_op | source)
XLA Modules:
  0.0 188.7 jit_solution(7858369492953057247)
XLA Ops:
  0.1 3.0 %shard_map.55 = (bf16[2,8,32,768]{3,2,1,0:T(8,128)(2,1)S(1)}, bf16[96,512]{1,0:T(8,128)(2,1)S(1)}, bf16[96,512]{1,0:T(8,128)(2,1)S(1)}, bf16[96,512]{1,0:T(8,128...) custom-call(s32[3]{0:T(128)S(1)} %pad_add_fusion.me_ref, ...), custom_call_target="tpu_custom_call" | custom-call | tf_op jit(solution)/shard_map/pallas_call | solution.py:96
  3.1 3.9 %collective-permute-start = (bf16[96,512]{1,0:T(8,128)(2,1)S(1)}, bf16[96,512]{1,0:T(8,128)(2,1)S(1)}, u32[]{:S(2)}, u32[]{:S(2)}) collective-permute-start(bf16[96,512]{1,0:T(8,128)(2,1)S(1)} %get-tuple-element.53), channel_id=1, source_target_pairs={{0,4},{2,6},{4,8},{6,10},{8,12},{10,14},{12,0},{14,2},{1,5},{3,7},... | collective-permute-start | bytes 294920 | tf_op jit(solution)/shard_map/ppermute | solution.py:361
  8.6 3.8 %collective-permute-start.2 = (bf16[96,512]{1,0:T(8,128)(2,1)S(1)}, bf16[96,512]{1,0:T(8,128)(2,1)S(1)}, u32[]{:S(2)}, u32[]{:S(2)}) collective-permute-start(bf16[96,512]{1,0:T(8,128)(2,1)S(1)} %get-tuple-element.58), channel_id=1, source_target_pairs={{0,6},{2,8},{4,10},{6,12},{8,14},{10,0},{12,2},{14,4},{1,7},{3,9},... | collective-permute-start | bytes 294920 | tf_op jit(solution)/shard_map/ppermute | solution.py:361
  12.8 4.5 %collective-permute-start.4 = (bf16[96,512]{1,0:T(8,128)(2,1)S(1)}, bf16[96,512]{1,0:T(8,128)(2,1)S(1)}, u32[]{:S(2)}, u32[]{:S(2)}) collective-permute-start(bf16[96,512]{1,0:T(8,128)(2,1)S(1)} %get-tuple-element.60), channel_id=1, source_target_pairs={{0,10},{2,12},{4,14},{6,0},{8,2},{10,4},{12,6},{14,8},{1,11},{3,13... | collective-permute-start | bytes 294920 | tf_op jit(solution)/shard_map/ppermute | solution.py:361
  17.3 2.5 %collective-permute-start.5 = (bf16[96,512]{1,0:T(8,128)(2,1)S(1)}, bf16[96,512]{1,0:T(8,128)(2,1)S(1)}, u32[]{:S(2)}, u32[]{:S(2)}) collective-permute-start(bf16[96,512]{1,0:T(8,128)(2,1)S(1)} %get-tuple-element.61), channel_id=1, source_target_pairs={{0,12},{2,14},{4,0},{6,2},{8,4},{10,6},{12,8},{14,10},{1,13},{3,15... | collective-permute-start | bytes 294920 | tf_op jit(solution)/shard_map/ppermute | solution.py:361
  20.5 6.5 %collective-permute-done.2 = bf16[96,512]{1,0:T(8,128)(2,1)S(1)} collective-permute-done((bf16[96,512]{1,0:T(8,128)(2,1)S(1)}, bf16[96,512]{1,0:T(8,128)(2,1)S(1)}, u32[]{:S(2)}, u32[]{:S(2)}) %collective-permute-start.2) | collective-permute-done | bytes 98336 | tf_op jit(solution)/shard_map/ppermute | solution.py:361
  27.1 5.1 %collective-permute-done.5 = bf16[96,512]{1,0:T(8,128)(2,1)S(1)} collective-permute-done((bf16[96,512]{1,0:T(8,128)(2,1)S(1)}, bf16[96,512]{1,0:T(8,128)(2,1)S(1)}, u32[]{:S(2)}, u32[]{:S(2)}) %collective-permute-start.5) | collective-permute-done | bytes 98336 | tf_op jit(solution)/shard_map/ppermute | solution.py:361
  32.2 1.8 shard_map.56
  34.1 5.1 %all-to-all-start = ((bf16[16,128,256]{2,1,0:T(8,128)(2,1)}), bf16[16,128,256]{2,1,0:T(8,128)(2,1)S(1)}, u32[]{:S(2)}, u32[]{:S(2)}) async-start(bf16[16,128,256]{2,1,0:T(8,128)(2,1)} %shard_map.56), calls=%async_computation | async-start | bytes 2097152 | tf_op jit(solution)/shard_map/all_to_all | solution.py:374
  40.8 17.3 %collective-permute-done.7.refs_0_ = bf16[8,96,512]{2,1,0:T(8,128)(2,1)S(1)} collective-permute-done((bf16[8,96,512]{2,1,0:T(8,128)(2,1)S(1)}, bf16[8,96,512]{2,1,0:T(8,128)(2,1)S(1)}, u32[]{:S(2)}, u32[]{:S(2)}) %collective-permute-start.7) | collective-permute-done | bytes 786464 | tf_op jit(solution)/shard_map/ppermute | solution.py:350
  59.1 2.0 %shard_map.57 = (bf16[1024,512]{1,0:T(8,128)(2,1)S(1)}, bf16[1024,256]{1,0:T(8,128)(2,1)S(1)}) custom-call(s32[3]{0:T(128)S(1)} %pad_add_fusion.me_ref, bf16[8,96,512]{2,1,0:T(8,128)(2,1)S(1)} %bitcast_dynamic-update-slice_fusion.8.own, bf16[8,96,512]{2,1,0:T(8,128)(2,1)S(1)} %collective-permute-done.9.other), custom_call_target="tpu_custom_call" | custom-call | bytes 6291456 | tf_op jit(solution)/shard_map/pallas_call | solution.py:174
  62.0 5.1 %all-to-all-done.refs_2_ = bf16[16,128,256]{2,1,0:T(8,128)(2,1)S(1)} async-done(((bf16[16,128,256]{2,1,0:T(8,128)(2,1)}), bf16[16,128,256]{2,1,0:T(8,128)(2,1)S(1)}, u32[]{:S(2)}, u32[]{:S(2)}) %all-to-all-start) | async-done | bytes 1048608 | tf_op jit(solution)/shard_map/all_to_all | solution.py:374
  69.3 3.9 %shard_map.58 = (f32[2,32,1536]{2,1,0:T(8,128)S(1)}, f32[2,32,1536]{2,1,0:T(8,128)S(1)}, f32[2,32,1536]{2,1,0:T(8,128)S(1)}, f32[2,32,1536]{2,1,0:T(8,128)S(1)}) custom-call(s32[3]{0:T(128)S(1)} %pad_add_fusion.me_ref, bf16[8,96,512]{2,1,0:T(8,128)(2,1)S(1)} %copy-done.3, bf16[8,96,512]{2,1,0:T(8,128)(2,1)S(1)} %copy-done.5, ...), custom_call_target="tpu_custom_call" | custom-call | tf_op jit(solution)/shard_map/pallas_call | solution.py:214
  74.6 2.6 %collective-permute-start.19 = (f32[2,32,1536]{2,1,0:T(8,128)S(1)}, f32[2,32,1536]{2,1,0:T(8,128)S(1)}, u32[]{:S(2)}, u32[]{:S(2)}) collective-permute-start(f32[2,32,1536]{2,1,0:T(8,128)S(1)} %get-tuple-element.80), channel_id=1, source_target_pairs={{0,128},{64,192},{128,0},{192,64},{1,129},{65,193},{129,1},{193,65... | collective-permute-start | bytes 1179656 | tf_op jit(solution)/shard_map/ppermute | solution.py:350
  77.2 7.2 %collective-permute-done.10.p1 = f32[2,32,1536]{2,1,0:T(8,128)S(1)} collective-permute-done((f32[2,32,1536]{2,1,0:T(8,128)S(1)}, f32[2,32,1536]{2,1,0:T(8,128)S(1)}, u32[]{:S(2)}, u32[]{:S(2)}) %collective-permute-start.10) | collective-permute-done | bytes 393248 | tf_op jit(solution)/shard_map/ppermute | solution.py:350
  87.3 7.3 %collective-permute-done.19.p2 = f32[2,32,1536]{2,1,0:T(8,128)S(1)} collective-permute-done((f32[2,32,1536]{2,1,0:T(8,128)S(1)}, f32[2,32,1536]{2,1,0:T(8,128)S(1)}, u32[]{:S(2)}, u32[]{:S(2)}) %collective-permute-start.19) | collective-permute-done | bytes 393248 | tf_op jit(solution)/shard_map/ppermute | solution.py:350
  96.1 1.8 collective-permute-done.20.p3
  97.9 2.6 %collective-permute-start.16 = (bf16[96,512]{1,0:T(8,128)(2,1)S(1)}, bf16[96,512]{1,0:T(8,128)(2,1)S(1)}, u32[]{:S(2)}, u32[]{:S(2)}) collective-permute-start(bf16[96,512]{1,0:T(8,128)(2,1)S(1)} %get-tuple-element.75), channel_id=1, source_target_pairs={{0,12},{2,14},{4,0},{6,2},{8,4},{10,6},{12,8},{14,10},{1,13},{3,15... | collective-permute-start | bytes 294920 | tf_op jit(solution)/shard_map/ppermute | solution.py:361
  102.2 3.6 %collective-permute-done.14 = bf16[96,512]{1,0:T(8,128)(2,1)S(1)} collective-permute-done((bf16[96,512]{1,0:T(8,128)(2,1)S(1)}, bf16[96,512]{1,0:T(8,128)(2,1)S(1)}, u32[]{:S(2)}, u32[]{:S(2)}) %collective-permute-start.14) | collective-permute-done | bytes 98336 | tf_op jit(solution)/shard_map/ppermute | solution.py:361
  106.9 2.7 %collective-permute-start.21 = (f32[32,1536]{1,0:T(8,128)S(1)}, f32[32,1536]{1,0:T(8,128)S(1)}, u32[]{:S(2)}, u32[]{:S(2)}) collective-permute-start(f32[32,1536]{1,0:T(8,128)S(1)} %get-tuple-element.83), channel_id=1, source_target_pairs={{0,32},{32,0},{1,33},{33,1},{2,34},{34,2},{3,35},{35,3},{4,36},{36... | collective-permute-start | bytes 589832 | tf_op jit(solution)/shard_map/ppermute | solution.py:350
  109.6 2.8 %collective-permute-done.16 = bf16[96,512]{1,0:T(8,128)(2,1)S(1)} collective-permute-done((bf16[96,512]{1,0:T(8,128)(2,1)S(1)}, bf16[96,512]{1,0:T(8,128)(2,1)S(1)}, u32[]{:S(2)}, u32[]{:S(2)}) %collective-permute-start.16) | collective-permute-done | bytes 98336 | tf_op jit(solution)/shard_map/ppermute | solution.py:361
  112.5 2.9 %collective-permute-done.22.near = f32[32,512]{1,0:T(8,128)S(1)} collective-permute-done((f32[32,512]{1,0:T(8,128)S(1)}, f32[32,512]{1,0:T(8,128)S(1)}, u32[]{:S(2)}, u32[]{:S(2)}) %collective-permute-start.22) | collective-permute-done | bytes 65568 | tf_op jit(solution)/shard_map/ppermute | solution.py:350
  115.4 3.9 %collective-permute-done.23.far = f32[32,512]{1,0:T(8,128)S(1)} collective-permute-done((f32[32,512]{1,0:T(8,128)S(1)}, f32[32,512]{1,0:T(8,128)S(1)}, u32[]{:S(2)}, u32[]{:S(2)}) %collective-permute-start.23) | collective-permute-done | bytes 65568 | tf_op jit(solution)/shard_map/ppermute | solution.py:350
  120.5 3.6 %all-to-all-start.1 = ((bf16[8,2,32,1024]{3,2,1,0:T(8,128)(2,1)}), bf16[8,2,32,1024]{3,2,1,0:T(8,128)(2,1)S(1)}, u32[]{:S(2)}, u32[]{:S(2)}) async-start(bf16[8,2,32,1024]{3,2,1,0:T(8,128)(2,1)} %shard_map.62), calls=%async_computation.1 | async-start | bytes 2097152 | tf_op jit(solution)/shard_map/all_to_all | solution.py:385
  124.5 28.2 %collective-permute-done.18.v_hbm = bf16[8,96,512]{2,1,0:T(8,128)(2,1)S(1)} collective-permute-done((bf16[8,96,512]{2,1,0:T(8,128)(2,1)S(1)}, bf16[8,96,512]{2,1,0:T(8,128)(2,1)S(1)}, u32[]{:S(2)}, u32[]{:S(2)}) %collective-permute-start.18) | collective-permute-done | bytes 786464 | tf_op jit(solution)/shard_map/ppermute | solution.py:350
  157.9 2.2 %shard_map.64 = (bf16[96,512]{1,0:T(8,128)(2,1)S(1)}, bf16[96,512]{1,0:T(8,128)(2,1)S(1)}, bf16[96,512]{1,0:T(8,128)(2,1)S(1)}, bf16[96,512]{1,0:T(8,128)(2,1)S(...) custom-call(s32[3]{0:T(128)S(1)} %pad_add_fusion.me_ref, ...), custom_call_target="tpu_custom_call" | custom-call | tf_op jit(solution)/shard_map/pallas_call | solution.py:315
  160.5 3.7 %collective-permute-start.26 = (bf16[96,512]{1,0:T(8,128)(2,1)S(1)}, bf16[96,512]{1,0:T(8,128)(2,1)S(1)}, u32[]{:S(2)}, u32[]{:S(2)}) collective-permute-start(bf16[96,512]{1,0:T(8,128)(2,1)S(1)} %get-tuple-element.93), channel_id=1, source_target_pairs={{0,4},{2,6},{4,8},{6,10},{8,12},{10,14},{12,0},{14,2},{1,5},{3,7},... | collective-permute-start | bytes 294920 | tf_op jit(solution)/shard_map/ppermute | solution.py:361
  165.0 4.6 %collective-permute-start.28 = (bf16[96,512]{1,0:T(8,128)(2,1)S(1)}, bf16[96,512]{1,0:T(8,128)(2,1)S(1)}, u32[]{:S(2)}, u32[]{:S(2)}) collective-permute-start(bf16[96,512]{1,0:T(8,128)(2,1)S(1)} %get-tuple-element.95), channel_id=1, source_target_pairs={{0,8},{2,10},{4,12},{6,14},{8,0},{10,2},{12,4},{14,6},{1,9},{3,11}... | collective-permute-start | bytes 294920 | tf_op jit(solution)/shard_map/ppermute | solution.py:361
  169.5 2.4 %collective-permute-start.30 = (bf16[96,512]{1,0:T(8,128)(2,1)S(1)}, bf16[96,512]{1,0:T(8,128)(2,1)S(1)}, u32[]{:S(2)}, u32[]{:S(2)}) collective-permute-start(bf16[96,512]{1,0:T(8,128)(2,1)S(1)} %get-tuple-element.97), channel_id=1, source_target_pairs={{0,12},{2,14},{4,0},{6,2},{8,4},{10,6},{12,8},{14,10},{1,13},{3,15... | collective-permute-start | bytes 294920 | tf_op jit(solution)/shard_map/ppermute | solution.py:361
  174.9 5.1 %collective-permute-done.28.refs_4_ = bf16[96,512]{1,0:T(8,128)(2,1)S(1)} collective-permute-done((bf16[96,512]{1,0:T(8,128)(2,1)S(1)}, bf16[96,512]{1,0:T(8,128)(2,1)S(1)}, u32[]{:S(2)}, u32[]{:S(2)}) %collective-permute-start.28) | collective-permute-done | bytes 98336 | tf_op jit(solution)/shard_map/ppermute | solution.py:361
  180.0 5.5 %collective-permute-done.30.refs_6_ = bf16[96,512]{1,0:T(8,128)(2,1)S(1)} collective-permute-done((bf16[96,512]{1,0:T(8,128)(2,1)S(1)}, bf16[96,512]{1,0:T(8,128)(2,1)S(1)}, u32[]{:S(2)}, u32[]{:S(2)}) %collective-permute-start.30) | collective-permute-done | bytes 98336 | tf_op jit(solution)/shard_map/ppermute | solution.py:361
  186.4 2.3 %shard_map.65 = bf16[8,64,768]{2,1,0:T(8,128)(2,1)} custom-call(s32[3]{0:T(128)S(1)} %pad_add_fusion.me_ref, bf16[96,512]{1,0:T(8,128)(2,1)S(1)} %get-tuple-element.91.refs_0_, bf16[96,512]{1,0:T(8,128)(2,1)S(1)} %collective-permute-done.25.refs_1_, bf16[96,512]{1,0:T(8,128)(2,1)S(1)} %collective-permute-done.26.refs_2_, ...), custom_call_target="tpu_custom_call" | custom-call | tf_op jit(solution)/shard_map/pallas_call | solution.py:339
  (82 shorter events, 29.4 us)
Async XLA Ops:
  3.1 14.2 %collective-permute-start = (bf16[96,512]{1,0:T(8,128)(2,1)S(1)}, bf16[96,512]{1,0:T(8,128)(2,1)S(1)}, u32[]{:S(2)}, u32[]{:S(2)}) collective-permute-start(bf16[96,512]{1,0:T(8,128)(2,1)S(1)} %get-tuple-element.53), channel_id=1, source_target_pairs={{0,4},{2,6},{4,8},{6,10},{8,12},{10,14},{12,0},{14,2},{1,5},{3,7},... | collective-permute-start | bytes 294920 | tf_op jit(solution)/shard_map/ppermute | solution.py:361
  7.0 12.8 %collective-permute-start.1 = (bf16[96,512]{1,0:T(8,128)(2,1)S(1)}, bf16[96,512]{1,0:T(8,128)(2,1)S(1)}, u32[]{:S(2)}, u32[]{:S(2)}) collective-permute-start(bf16[96,512]{1,0:T(8,128)(2,1)S(1)} %get-tuple-element.56), channel_id=1, source_target_pairs={{0,2},{2,4},{4,6},{6,8},{8,10},{10,12},{12,14},{14,0},{1,3},{3,5},... | collective-permute-start | bytes 294920 | tf_op jit(solution)/shard_map/ppermute | solution.py:361
  8.6 18.5 %collective-permute-start.2 = (bf16[96,512]{1,0:T(8,128)(2,1)S(1)}, bf16[96,512]{1,0:T(8,128)(2,1)S(1)}, u32[]{:S(2)}, u32[]{:S(2)}) collective-permute-start(bf16[96,512]{1,0:T(8,128)(2,1)S(1)} %get-tuple-element.58), channel_id=1, source_target_pairs={{0,6},{2,8},{4,10},{6,12},{8,14},{10,0},{12,2},{14,4},{1,7},{3,9},... | collective-permute-start | bytes 294920 | tf_op jit(solution)/shard_map/ppermute | solution.py:361
  12.4 14.7 %collective-permute-start.3 = (bf16[96,512]{1,0:T(8,128)(2,1)S(1)}, bf16[96,512]{1,0:T(8,128)(2,1)S(1)}, u32[]{:S(2)}, u32[]{:S(2)}) collective-permute-start(bf16[96,512]{1,0:T(8,128)(2,1)S(1)} %get-tuple-element.59), channel_id=1, source_target_pairs={{0,8},{2,10},{4,12},{6,14},{8,0},{10,2},{12,4},{14,6},{1,9},{3,11}... | collective-permute-start | bytes 294920 | tf_op jit(solution)/shard_map/ppermute | solution.py:361
  12.8 14.3 %collective-permute-start.4 = (bf16[96,512]{1,0:T(8,128)(2,1)S(1)}, bf16[96,512]{1,0:T(8,128)(2,1)S(1)}, u32[]{:S(2)}, u32[]{:S(2)}) collective-permute-start(bf16[96,512]{1,0:T(8,128)(2,1)S(1)} %get-tuple-element.60), channel_id=1, source_target_pairs={{0,10},{2,12},{4,14},{6,0},{8,2},{10,4},{12,6},{14,8},{1,11},{3,13... | collective-permute-start | bytes 294920 | tf_op jit(solution)/shard_map/ppermute | solution.py:361
  17.3 14.9 %collective-permute-start.5 = (bf16[96,512]{1,0:T(8,128)(2,1)S(1)}, bf16[96,512]{1,0:T(8,128)(2,1)S(1)}, u32[]{:S(2)}, u32[]{:S(2)}) collective-permute-start(bf16[96,512]{1,0:T(8,128)(2,1)S(1)} %get-tuple-element.61), channel_id=1, source_target_pairs={{0,12},{2,14},{4,0},{6,2},{8,4},{10,6},{12,8},{14,10},{1,13},{3,15... | collective-permute-start | bytes 294920 | tf_op jit(solution)/shard_map/ppermute | solution.py:361
  19.8 14.3 %collective-permute-start.6 = (bf16[96,512]{1,0:T(8,128)(2,1)S(1)}, bf16[96,512]{1,0:T(8,128)(2,1)S(1)}, u32[]{:S(2)}, u32[]{:S(2)}) collective-permute-start(bf16[96,512]{1,0:T(8,128)(2,1)S(1)} %get-tuple-element.62), channel_id=1, source_target_pairs={{0,14},{2,0},{4,2},{6,4},{8,6},{10,8},{12,10},{14,12},{1,15},{3,1}... | collective-permute-start | bytes 294920 | tf_op jit(solution)/shard_map/ppermute | solution.py:361
  34.1 33.0 %all-to-all-start = ((bf16[16,128,256]{2,1,0:T(8,128)(2,1)}), bf16[16,128,256]{2,1,0:T(8,128)(2,1)S(1)}, u32[]{:S(2)}, u32[]{:S(2)}) async-start(bf16[16,128,256]{2,1,0:T(8,128)(2,1)} %shard_map.56), calls=%async_computation | async-start | bytes 2097152 | tf_op jit(solution)/shard_map/all_to_all | solution.py:374
  39.1 19.0 %collective-permute-start.7 = (bf16[8,96,512]{2,1,0:T(8,128)(2,1)S(1)}, bf16[8,96,512]{2,1,0:T(8,128)(2,1)S(1)}, u32[]{:S(2)}, u32[]{:S(2)}) collective-permute-start(bf16[8,96,512]{2,1,0:T(8,128)(2,1)S(1)} %bitcast_dynamic-update-slice_fusion.8.own), channel_id=1, source_target_pairs={{0,1},{1,0},{2,3},{3,2},{4,5},{5,4},{6,7},{7,6},{8,9},{9,8},{10,11... | collective-permute-start | bytes 2359304 | tf_op jit(solution)/shard_map/ppermute | solution.py:350
  40.3 18.8 %collective-permute-start.9 = (bf16[8,96,512]{2,1,0:T(8,128)(2,1)S(1)}, bf16[8,96,512]{2,1,0:T(8,128)(2,1)S(1)}, u32[]{:S(2)}, u32[]{:S(2)}) collective-permute-start(bf16[8,96,512]{2,1,0:T(8,128)(2,1)S(1)} %bitcast_dynamic-update-slice_fusion.8.own), channel_id=1, source_target_pairs={{0,16},{16,0},{1,17},{17,1},{2,18},{18,2},{3,19},{19,3},{4,20},{20... | collective-permute-start | bytes 2359304 | tf_op jit(solution)/shard_map/ppermute | solution.py:350
  73.2 11.2 %collective-permute-start.10 = (f32[2,32,1536]{2,1,0:T(8,128)S(1)}, f32[2,32,1536]{2,1,0:T(8,128)S(1)}, u32[]{:S(2)}, u32[]{:S(2)}) collective-permute-start(f32[2,32,1536]{2,1,0:T(8,128)S(1)} %get-tuple-element.67), channel_id=1, source_target_pairs={{0,64},{64,0},{128,192},{192,128},{1,65},{65,1},{129,193},{193,129... | collective-permute-start | bytes 1179656 | tf_op jit(solution)/shard_map/ppermute | solution.py:350
  74.6 20.1 %collective-permute-start.19 = (f32[2,32,1536]{2,1,0:T(8,128)S(1)}, f32[2,32,1536]{2,1,0:T(8,128)S(1)}, u32[]{:S(2)}, u32[]{:S(2)}) collective-permute-start(f32[2,32,1536]{2,1,0:T(8,128)S(1)} %get-tuple-element.80), channel_id=1, source_target_pairs={{0,128},{64,192},{128,0},{192,64},{1,129},{65,193},{129,1},{193,65... | collective-permute-start | bytes 1179656 | tf_op jit(solution)/shard_map/ppermute | solution.py:350
  77.2 20.6 %collective-permute-start.20 = (f32[2,32,1536]{2,1,0:T(8,128)S(1)}, f32[2,32,1536]{2,1,0:T(8,128)S(1)}, u32[]{:S(2)}, u32[]{:S(2)}) collective-permute-start(f32[2,32,1536]{2,1,0:T(8,128)S(1)} %get-tuple-element.81), channel_id=1, source_target_pairs={{0,192},{64,128},{128,64},{192,0},{1,193},{65,129},{129,65},{193,1... | collective-permute-start | bytes 1179656 | tf_op jit(solution)/shard_map/ppermute | solution.py:350
  85.8 12.1 %collective-permute-start.11 = (bf16[96,512]{1,0:T(8,128)(2,1)S(1)}, bf16[96,512]{1,0:T(8,128)(2,1)S(1)}, u32[]{:S(2)}, u32[]{:S(2)}) collective-permute-start(bf16[96,512]{1,0:T(8,128)(2,1)S(1)} %get-tuple-element.70), channel_id=1, source_target_pairs={{0,2},{2,4},{4,6},{6,8},{8,10},{10,12},{12,14},{14,0},{1,3},{3,5},... | collective-permute-start | bytes 294920 | tf_op jit(solution)/shard_map/ppermute | solution.py:361
  85.9 14.7 %collective-permute-start.12 = (bf16[96,512]{1,0:T(8,128)(2,1)S(1)}, bf16[96,512]{1,0:T(8,128)(2,1)S(1)}, u32[]{:S(2)}, u32[]{:S(2)}) collective-permute-start(bf16[96,512]{1,0:T(8,128)(2,1)S(1)} %get-tuple-element.71), channel_id=1, source_target_pairs={{0,4},{2,6},{4,8},{6,10},{8,12},{10,14},{12,0},{14,2},{1,5},{3,7},... | collective-permute-start | bytes 294920 | tf_op jit(solution)/shard_map/ppermute | solution.py:361
  86.8 14.9 %collective-permute-start.13 = (bf16[96,512]{1,0:T(8,128)(2,1)S(1)}, bf16[96,512]{1,0:T(8,128)(2,1)S(1)}, u32[]{:S(2)}, u32[]{:S(2)}) collective-permute-start(bf16[96,512]{1,0:T(8,128)(2,1)S(1)} %get-tuple-element.72), channel_id=1, source_target_pairs={{0,6},{2,8},{4,10},{6,12},{8,14},{10,0},{12,2},{14,4},{1,7},{3,9},... | collective-permute-start | bytes 294920 | tf_op jit(solution)/shard_map/ppermute | solution.py:361
  94.6 11.1 %collective-permute-start.14 = (bf16[96,512]{1,0:T(8,128)(2,1)S(1)}, bf16[96,512]{1,0:T(8,128)(2,1)S(1)}, u32[]{:S(2)}, u32[]{:S(2)}) collective-permute-start(bf16[96,512]{1,0:T(8,128)(2,1)S(1)} %get-tuple-element.73), channel_id=1, source_target_pairs={{0,8},{2,10},{4,12},{6,14},{8,0},{10,2},{12,4},{14,6},{1,9},{3,11}... | collective-permute-start | bytes 294920 | tf_op jit(solution)/shard_map/ppermute | solution.py:361
  97.8 9.0 %collective-permute-start.15 = (bf16[96,512]{1,0:T(8,128)(2,1)S(1)}, bf16[96,512]{1,0:T(8,128)(2,1)S(1)}, u32[]{:S(2)}, u32[]{:S(2)}) collective-permute-start(bf16[96,512]{1,0:T(8,128)(2,1)S(1)} %get-tuple-element.74), channel_id=1, source_target_pairs={{0,10},{2,12},{4,14},{6,0},{8,2},{10,4},{12,6},{14,8},{1,11},{3,13... | collective-permute-start | bytes 294920 | tf_op jit(solution)/shard_map/ppermute | solution.py:361
  97.9 14.5 %collective-permute-start.16 = (bf16[96,512]{1,0:T(8,128)(2,1)S(1)}, bf16[96,512]{1,0:T(8,128)(2,1)S(1)}, u32[]{:S(2)}, u32[]{:S(2)}) collective-permute-start(bf16[96,512]{1,0:T(8,128)(2,1)S(1)} %get-tuple-element.75), channel_id=1, source_target_pairs={{0,12},{2,14},{4,0},{6,2},{8,4},{10,6},{12,8},{14,10},{1,13},{3,15... | collective-permute-start | bytes 294920 | tf_op jit(solution)/shard_map/ppermute | solution.py:361
  100.6 23.5 %collective-permute-start.17 = (bf16[96,512]{1,0:T(8,128)(2,1)S(1)}, bf16[96,512]{1,0:T(8,128)(2,1)S(1)}, u32[]{:S(2)}, u32[]{:S(2)}) collective-permute-start(bf16[96,512]{1,0:T(8,128)(2,1)S(1)} %get-tuple-element.76), channel_id=1, source_target_pairs={{0,14},{2,0},{4,2},{6,4},{8,6},{10,8},{12,10},{14,12},{1,15},{3,1}... | collective-permute-start | bytes 294920 | tf_op jit(solution)/shard_map/ppermute | solution.py:361
  101.7 13.6 %collective-permute-start.22 = (f32[32,512]{1,0:T(8,128)S(1)}, f32[32,512]{1,0:T(8,128)S(1)}, u32[]{:S(2)}, u32[]{:S(2)}) collective-permute-start(f32[32,512]{1,0:T(8,128)S(1)} %get-tuple-element.84), channel_id=1, source_target_pairs={{0,2},{2,0},{4,6},{6,4},{8,10},{10,8},{12,14},{14,12},{1,3},{3,1},... | collective-permute-start | bytes 196616 | tf_op jit(solution)/shard_map/ppermute | solution.py:350
  105.8 13.5 %collective-permute-start.23 = (f32[32,512]{1,0:T(8,128)S(1)}, f32[32,512]{1,0:T(8,128)S(1)}, u32[]{:S(2)}, u32[]{:S(2)}) collective-permute-start(f32[32,512]{1,0:T(8,128)S(1)} %get-tuple-element.85), channel_id=1, source_target_pairs={{0,34},{2,32},{4,38},{6,36},{8,42},{10,40},{12,46},{14,44},{32,2},... | collective-permute-start | bytes 196616 | tf_op jit(solution)/shard_map/ppermute | solution.py:350
  106.9 12.4 %collective-permute-start.21 = (f32[32,1536]{1,0:T(8,128)S(1)}, f32[32,1536]{1,0:T(8,128)S(1)}, u32[]{:S(2)}, u32[]{:S(2)}) collective-permute-start(f32[32,1536]{1,0:T(8,128)S(1)} %get-tuple-element.83), channel_id=1, source_target_pairs={{0,32},{32,0},{1,33},{33,1},{2,34},{34,2},{3,35},{35,3},{4,36},{36... | collective-permute-start | bytes 589832 | tf_op jit(solution)/shard_map/ppermute | solution.py:350
  120.5 33.5 %all-to-all-start.1 = ((bf16[8,2,32,1024]{3,2,1,0:T(8,128)(2,1)}), bf16[8,2,32,1024]{3,2,1,0:T(8,128)(2,1)S(1)}, u32[]{:S(2)}, u32[]{:S(2)}) async-start(bf16[8,2,32,1024]{3,2,1,0:T(8,128)(2,1)} %shard_map.62), calls=%async_computation.1 | async-start | bytes 2097152 | tf_op jit(solution)/shard_map/all_to_all | solution.py:385
  124.1 28.6 %collective-permute-start.18 = (bf16[8,96,512]{2,1,0:T(8,128)(2,1)S(1)}, bf16[8,96,512]{2,1,0:T(8,128)(2,1)S(1)}, u32[]{:S(2)}, u32[]{:S(2)}) collective-permute-start(bf16[8,96,512]{2,1,0:T(8,128)(2,1)S(1)} %bitcast_dynamic-update-slice_fusion.v_hbm), channel_id=1, source_target_pairs={{0,1},{1,0},{2,3},{3,2},{4,5},{5,4},{6,7},{7,6},{8,9},{9,8},{10,11... | collective-permute-start | bytes 2359304 | tf_op jit(solution)/shard_map/ppermute | solution.py:350
  160.1 9.4 %collective-permute-start.25 = (bf16[96,512]{1,0:T(8,128)(2,1)S(1)}, bf16[96,512]{1,0:T(8,128)(2,1)S(1)}, u32[]{:S(2)}, u32[]{:S(2)}) collective-permute-start(bf16[96,512]{1,0:T(8,128)(2,1)S(1)} %get-tuple-element.92), channel_id=1, source_target_pairs={{0,2},{2,4},{4,6},{6,8},{8,10},{10,12},{12,14},{14,0},{1,3},{3,5},... | collective-permute-start | bytes 294920 | tf_op jit(solution)/shard_map/ppermute | solution.py:361
  160.5 11.5 %collective-permute-start.26 = (bf16[96,512]{1,0:T(8,128)(2,1)S(1)}, bf16[96,512]{1,0:T(8,128)(2,1)S(1)}, u32[]{:S(2)}, u32[]{:S(2)}) collective-permute-start(bf16[96,512]{1,0:T(8,128)(2,1)S(1)} %get-tuple-element.93), channel_id=1, source_target_pairs={{0,4},{2,6},{4,8},{6,10},{8,12},{10,14},{12,0},{14,2},{1,5},{3,7},... | collective-permute-start | bytes 294920 | tf_op jit(solution)/shard_map/ppermute | solution.py:361
  164.2 10.7 %collective-permute-start.27 = (bf16[96,512]{1,0:T(8,128)(2,1)S(1)}, bf16[96,512]{1,0:T(8,128)(2,1)S(1)}, u32[]{:S(2)}, u32[]{:S(2)}) collective-permute-start(bf16[96,512]{1,0:T(8,128)(2,1)S(1)} %get-tuple-element.94), channel_id=1, source_target_pairs={{0,6},{2,8},{4,10},{6,12},{8,14},{10,0},{12,2},{14,4},{1,7},{3,9},... | collective-permute-start | bytes 294920 | tf_op jit(solution)/shard_map/ppermute | solution.py:361
  165.0 15.0 %collective-permute-start.28 = (bf16[96,512]{1,0:T(8,128)(2,1)S(1)}, bf16[96,512]{1,0:T(8,128)(2,1)S(1)}, u32[]{:S(2)}, u32[]{:S(2)}) collective-permute-start(bf16[96,512]{1,0:T(8,128)(2,1)S(1)} %get-tuple-element.95), channel_id=1, source_target_pairs={{0,8},{2,10},{4,12},{6,14},{8,0},{10,2},{12,4},{14,6},{1,9},{3,11}... | collective-permute-start | bytes 294920 | tf_op jit(solution)/shard_map/ppermute | solution.py:361
  169.5 10.4 %collective-permute-start.29 = (bf16[96,512]{1,0:T(8,128)(2,1)S(1)}, bf16[96,512]{1,0:T(8,128)(2,1)S(1)}, u32[]{:S(2)}, u32[]{:S(2)}) collective-permute-start(bf16[96,512]{1,0:T(8,128)(2,1)S(1)} %get-tuple-element.96), channel_id=1, source_target_pairs={{0,10},{2,12},{4,14},{6,0},{8,2},{10,4},{12,6},{14,8},{1,11},{3,13... | collective-permute-start | bytes 294920 | tf_op jit(solution)/shard_map/ppermute | solution.py:361
  169.5 15.9 %collective-permute-start.30 = (bf16[96,512]{1,0:T(8,128)(2,1)S(1)}, bf16[96,512]{1,0:T(8,128)(2,1)S(1)}, u32[]{:S(2)}, u32[]{:S(2)}) collective-permute-start(bf16[96,512]{1,0:T(8,128)(2,1)S(1)} %get-tuple-element.97), channel_id=1, source_target_pairs={{0,12},{2,14},{4,0},{6,2},{8,4},{10,6},{12,8},{14,10},{1,13},{3,15... | collective-permute-start | bytes 294920 | tf_op jit(solution)/shard_map/ppermute | solution.py:361
  172.0 14.4 %collective-permute-start.31 = (bf16[96,512]{1,0:T(8,128)(2,1)S(1)}, bf16[96,512]{1,0:T(8,128)(2,1)S(1)}, u32[]{:S(2)}, u32[]{:S(2)}) collective-permute-start(bf16[96,512]{1,0:T(8,128)(2,1)S(1)} %get-tuple-element.98), channel_id=1, source_target_pairs={{0,14},{2,0},{4,2},{6,4},{8,6},{10,8},{12,10},{14,12},{1,15},{3,1}... | collective-permute-start | bytes 294920 | tf_op jit(solution)/shard_map/ppermute | solution.py:361
  (11 other events, 131.8 us)

commit v8 on v2

--- a/solution.py
+++ b/solution.py
@@ -24,12 +24,14 @@
 
 f32 = jnp.float32
 bf16 = jnp.bfloat16
-PARAMS = pltpu.CompilerParams(vmem_limit_bytes=48 * 1024 * 1024)
+PARAMS = pltpu.CompilerParams(vmem_limit_bytes=16 * 1024 * 1024)
 PROJECTION = pl.CostEstimate(
     flops=2 * ROWS * RES * EMBED * EMBED, bytes_accessed=2 * EMBED * (EMBED + 2 * ROWS * RES), transcendentals=0
 )
 VMEM = pl.BlockSpec(memory_space=pltpu.VMEM)
 SMEM = pl.BlockSpec(memory_space=pltpu.SMEM)
+ANY = pl.BlockSpec(memory_space=pl.ANY)
+LAYOUT = pl.CostEstimate(flops=0, bytes_accessed=16 * ROWS * RES * EMBED, transcendentals=0)
 
 
 def chunk_pieces(z):
@@ -56,12 +58,26 @@
         out[FULL:CHUNK, :] = t_ref[pl.ds(half, HALF), :]
 
 
-def key_kernel(me_ref, x_ref, w_ref, n_ref, *rest):
-    outs, t_ref = rest[:Z], rest[Z]
+def fetches(sources, buffers, sems):
+    copies = [pltpu.make_async_copy(a, b, sems.at[i]) for i, (a, b) in enumerate(zip(sources, buffers))]
+    for copy in copies:
+        copy.start()
+    return copies
+
+
+def in_hbm(*arrays):
+    return [pltpu.with_memory_space_constraint(a, pltpu.HBM) for a in arrays]
+
+
+def key_kernel(me_ref, x_hbm, w_hbm, n_ref, *rest):
+    outs, (x_ref, w_ref, t_ref, sems) = rest[:Z], rest[Z:]
+    copy_x, copy_w = fetches((x_hbm, w_hbm), (x_ref, w_ref), sems)
+    copy_x.wait()
     x = x_ref[...].astype(f32)
     centred = x - jnp.mean(x, axis=-1, keepdims=True)
     var = jnp.mean(centred * centred, axis=-1, keepdims=True)
     n_ref[...] = (centred * lax.rsqrt(var + 1e-05)).astype(bf16)
+    copy_w.wait()
     t_ref[...] = dot(w_ref[...], n_ref[...].reshape(ROWS * RES, EMBED), 0, 1).astype(bf16)
     send_pieces(me_ref[2], t_ref, outs)
 
@@ -71,11 +87,16 @@
         key_kernel,
         out_shape=(jax.ShapeDtypeStruct((ROWS, RES, EMBED), bf16),)
         + (jax.ShapeDtypeStruct((CHUNK, ROWS * RES), bf16),) * Z,
-        in_specs=[SMEM, VMEM, VMEM],
+        in_specs=[SMEM, ANY, ANY],
         out_specs=(VMEM,) * (Z + 1),
-        scratch_shapes=[pltpu.VMEM((EMBED, ROWS * RES), bf16)],
-        compiler_params=PARAMS,
-    )(me, x, w)
+        scratch_shapes=[
+            pltpu.VMEM((ROWS, RES, EMBED), bf16),
+            pltpu.VMEM((EMBED, EMBED), bf16),
+            pltpu.VMEM((EMBED, ROWS * RES), bf16),
+            pltpu.SemaphoreType.DMA((2,)),
+        ],
+        compiler_params=PARAMS,
+    )(me, *in_hbm(x, w))
     return n, k
 
 
@@ -200,36 +221,48 @@
     )(full, half, other)
 
 
-def mix_kernel(me_ref, v00, v01, v10, v11, p_ref, o_ref, vf, vh):
-    core, z = me_ref[1], me_ref[2]
-    pf, ph = (p_ref[:, i].reshape(QUERIES, KEYS) for i in range(2))
-    for cr, vs in ((0, (v00, v01)), (1, (v10, v11))):
-        c = jnp.bitwise_xor(core, cr)
-        values = arrived(z, vs)
+def values_kernel(me_ref, v00, v01, v10, v11, vf, vh):
+    for cr, vs in enumerate(((v00, v01), (v10, v11))):
+        values = arrived(me_ref[2], vs)
         for r in range(ROWS):
+            n = cr * ROWS + r
             t = widen(values, r)
-            vf[r * FULL : (r + 1) * FULL, :] = t[:FULL]
-            vh[r * HALF : (r + 1) * HALF, :] = t[FULL:]
-        for v, p, first, n in ((vf, pf, 0, FULL), (vh, ph, FULL, HALF)):
-            mixed = dot(v[...], p, 1, 1).astype(bf16)
+            vf[n * FULL : (n + 1) * FULL, :] = t[:FULL]
+            vh[n * HALF : (n + 1) * HALF, :] = t[FULL:]
+
+
+def values_laid(me, vs):
+    return pl.pallas_call(
+        values_kernel,
+        out_shape=tuple(jax.ShapeDtypeStruct((2 * ROWS * n, KEYS), bf16) for n in (FULL, HALF)),
+        in_specs=[SMEM] + [VMEM] * 4,
+        out_specs=(VMEM,) * 2,
+        compiler_params=PARAMS,
+        cost_estimate=LAYOUT,
+    )(me, *vs)
+
+
+def mix_kernel(me_ref, vf, vh, p_ref, o_ref):
+    core = me_ref[1]
+    for i, (v, first, n) in enumerate(((vf, 0, FULL), (vh, FULL, HALF))):
+        probs = p_ref[:, i].reshape(QUERIES, KEYS)
+        for cr in range(2):
+            c = jnp.bitwise_xor(core, cr)
+            mixed = dot(v[cr * ROWS * n : (cr + 1) * ROWS * n, :], probs, 1, 1).astype(bf16)
             for s in range(PEERS):
                 o_ref[2 * s + c, first : first + n, :] = jnp.concatenate(
                     [mixed[r * n : (r + 1) * n, s * SUB : (s + 1) * SUB] for r in range(ROWS)], axis=1
                 )
 
 
-def mix(me, vs, probs):
+def mix(me, laid, probs):
     return pl.pallas_call(
         mix_kernel,
         out_shape=jax.ShapeDtypeStruct((2 * Z, CHUNK, ROWS * SUB), bf16),
-        in_specs=[SMEM] + [VMEM] * 5,
-        out_specs=VMEM,
-        scratch_shapes=[
-            pltpu.VMEM((ROWS * FULL, KEYS), bf16),
-            pltpu.VMEM((ROWS * HALF, KEYS), bf16),
-        ],
-        compiler_params=PARAMS,
-    )(me, *vs, probs)
+        in_specs=[SMEM] + [VMEM] * 3,
+        out_specs=VMEM,
+        compiler_params=PARAMS,
+    )(me, *laid, probs)
 
 
 def final_kernel(m_ref, w_ref, o_ref, t_ref):
@@ -262,29 +295,32 @@
     return own, far, flip(own, "c", 2, 1), flip(far, "c", 2, 1)
 
 
-def spread(pieces):
-    got = {0: pieces[0]}
-    for s in (1, 7, 2, 6, 3, 5, 4):
-        got[s] = lax.ppermute(pieces[s], "z", [(i, (i + s) % Z) for i in range(Z)])
-    return jnp.stack([got[s] for s in range(Z)])
+def shift(x, s):
+    return lax.ppermute(x, "z", [(i, (i + s) % Z) for i in range(Z)])
 
 
 def local(x, wq, wk, wv, wf):
     me = jnp.stack([lax.axis_index(("y", "xh")), lax.axis_index("c"), lax.axis_index("z")])
     me = me.astype(jnp.int32)
     n, k = key_chunks(me, x, wk)
-    q = query_chunks(n, wq)
-    v = value_chunks(me, n, wv)
-    ks = gather4(spread(k))
+    for s in (1, 7, 2, 6, 3, 5, 4):
+        k[s] = shift(k[s], s)
+    q, k[2] = lax.optimization_barrier((query_chunks(n, wq), k[2]))
     q = lax.all_to_all(q, ("z", "c"), 0, 0, tiled=True)
-    v, scores = lax.optimization_barrier((v, score(me, q, ks)))
+    v = list(value_chunks(me, n, wv))
+    k = jnp.stack(k)
+    k_far, v[4] = lax.optimization_barrier((flip(k, "xl", 2, 1), v[4]))
+    scores = score(me, q, (k, k_far, flip(k, "c", 2, 1), flip(k_far, "c", 2, 1)))
+    *v, scores = lax.optimization_barrier((*v, scores))
     parts = lax.all_to_all(scores, ("y", "xh"), 0, 0, tiled=True)
-    vs = gather4(spread(v))
+    for s in (3, 5, 4, 2, 6, 1, 7):
+        v[s] = shift(v[s], s)
     full, half = total(parts)
     rows = ROWS * 2 * PEERS
     probs = softmax(1.0 / math.sqrt(DH * rows), full, half, flip(half, "z", Z, 1))
     probs = lax.all_to_all(probs, ("y", "xh"), 0, 0, tiled=True)
-    mixed = lax.all_to_all(mix(me, vs, probs), ("z", "c"), 0, 0, tiled=True)
+    laid = values_laid(me, gather4(jnp.stack(v)))
+    mixed = lax.all_to_all(mix(me, laid, probs), ("z", "c"), 0, 0, tiled=True)
     return final(mixed, wf)
 
 

time: 172 us -> 167 us (0.971)
  waiting for transfers between devices: 61.9 us -> 56.8 us
  local copies, waits for them, and re-layouts: 8.24 us -> 6.07 us
    all_to_all x1, waiting for transfers between devices: 5.56 us -> 10.2 us  [local(): q = lax.all_to_all(q, ('z', 'c'), 0, 0, tiled=True)]
    ppermute x7, waiting for transfers between devices: 20.5 us -> 16.1 us  [flip(): return lax.ppermute(x, axes, [(i, i ^ s) for i in range(n)])]
    all_to_all x1, waiting for transfers between devices: 8.01 us -> 4.75 us  [local(): probs = lax.all_to_all(probs, ('y', 'xh'), 0, 0, tiled=True)]
    unnamed x40 -> x52, local copies, waits for them, and re-layouts: 8.23 us -> 6.05 us
    ppermute x14, waiting for transfers between devices: 25.6 us -> 23.4 us  [shift(): return lax.ppermute(x, 'z', [(i, (i + s) % Z) for i in range(Z)])]
    pallas_call x0 -> x1, Pallas kernels: none -> 2.02 us  [values_laid(): pl.pallas_call(values_kernel, out_shape=tuple((jax.ShapeDtypeStruct((2 *...]
  transfers between devices with their start and end apart: 24 -> 24, of which waited for: 16 -> 14; matrix products, arithmetic and copies ran while one was open for 0% -> 0% of each run, Pallas kernels for 3% -> 4%
where the time goes in v8:
time: 167 us
  waiting for transfers between devices  56.8 us (34%)
  starting transfers between devices  54.9 us (33%)
  blocking collectives  30.3 us (18%)
  Pallas kernels  18.4 us (11%)
  local copies, waits for them, and re-layouts  6.07 us (4%)
    all_to_all x1, blocking collectives, local(): mixed = lax.all_to_all(mix(me, laid, probs), ('z', 'c'), 0, 0, tiled=True)  30.3 us
    ppermute x14, starting transfers between devices, shift(): return lax.ppermute(x, 'z', [(i, (i + s) % Z) for i in range(Z)])  29.1 us
    ppermute x14, waiting for transfers between devices, shift(): return lax.ppermute(x, 'z', [(i, (i + s) % Z) for i in range(Z)])  23.4 us
    ppermute x7, waiting for transfers between devices, flip(): return lax.ppermute(x, axes, [(i, i ^ s) for i in range(n)])  16.1 us
    all_to_all x1, waiting for transfers between devices, local(): q = lax.all_to_all(q, ('z', 'c'), 0, 0, tiled=True)  10.2 us
    ppermute x7, starting transfers between devices, flip(): return lax.ppermute(x, axes, [(i, i ^ s) for i in range(n)])  9.42 us
    all_to_all x1, starting transfers between devices, local(): parts = lax.all_to_all(scores, ('y', 'xh'), 0, 0, tiled=True)  6.51 us
    all_to_all x1, starting transfers between devices, local(): q = lax.all_to_all(q, ('z', 'c'), 0, 0, tiled=True)  6.31 us
  transfers between devices with their start and end apart: 24, of which 14 were waited for; matrix products, arithmetic and copies ran while one was open for 0% of the time, Pallas kernels for 4%

profile of v8, /device:TPU:1, one launch (start us, length us, event | category | flops | bytes accessed | tf_op | source)
XLA Modules:
  0.0 166.8 jit_solution(14900845883996206411)
XLA Ops:
  0.1 3.0 %shard_map.55 = (bf16[8,64,768]{2,1,0:T(8,128)(2,1)S(1)}, bf16[96,512]{1,0:T(8,128)(2,1)S(1)}, bf16[96,512]{1,0:T(8,128)(2,1)S(1)}, bf16[96,512]{1,0:T(8,128)(2,...) custom-call(s32[3]{0:T(128)S(1)} %pad_add_fusion.me_ref, ...), custom_call_target="tpu_custom_call" | custom-call | tf_op jit(solution)/shard_map/pallas_call | solution.py:86
  3.1 2.5 %collective-permute-start = (bf16[96,512]{1,0:T(8,128)(2,1)S(1)}, bf16[96,512]{1,0:T(8,128)(2,1)S(1)}, u32[]{:S(2)}, u32[]{:S(2)}) collective-permute-start(bf16[96,512]{1,0:T(8,128)(2,1)S(1)} %get-tuple-element.45), channel_id=1, source_target_pairs={{0,2},{2,4},{4,6},{6,8},{8,10},{10,12},{12,14},{14,0},{1,3},{3,5},... | collective-permute-start | bytes 294920 | tf_op jit(solution)/shard_map/ppermute | solution.py:299
  5.6 3.0 %collective-permute-start.1 = (bf16[96,512]{1,0:T(8,128)(2,1)S(1)}, bf16[96,512]{1,0:T(8,128)(2,1)S(1)}, u32[]{:S(2)}, u32[]{:S(2)}) collective-permute-start(bf16[96,512]{1,0:T(8,128)(2,1)S(1)} %get-tuple-element.46), channel_id=1, source_target_pairs={{0,4},{2,6},{4,8},{6,10},{8,12},{10,14},{12,0},{14,2},{1,5},{3,7},... | collective-permute-start | bytes 294920 | tf_op jit(solution)/shard_map/ppermute | solution.py:299
  8.6 3.8 %collective-permute-start.2 = (bf16[96,512]{1,0:T(8,128)(2,1)S(1)}, bf16[96,512]{1,0:T(8,128)(2,1)S(1)}, u32[]{:S(2)}, u32[]{:S(2)}) collective-permute-start(bf16[96,512]{1,0:T(8,128)(2,1)S(1)} %get-tuple-element.48), channel_id=1, source_target_pairs={{0,6},{2,8},{4,10},{6,12},{8,14},{10,0},{12,2},{14,4},{1,7},{3,9},... | collective-permute-start | bytes 294920 | tf_op jit(solution)/shard_map/ppermute | solution.py:299
  12.8 4.5 %collective-permute-start.4 = (bf16[96,512]{1,0:T(8,128)(2,1)S(1)}, bf16[96,512]{1,0:T(8,128)(2,1)S(1)}, u32[]{:S(2)}, u32[]{:S(2)}) collective-permute-start(bf16[96,512]{1,0:T(8,128)(2,1)S(1)} %get-tuple-element.50), channel_id=1, source_target_pairs={{0,10},{2,12},{4,14},{6,0},{8,2},{10,4},{12,6},{14,8},{1,11},{3,13... | collective-permute-start | bytes 294920 | tf_op jit(solution)/shard_map/ppermute | solution.py:299
  17.3 1.7 %shard_map.57 = bf16[16,96,256]{2,1,0:T(8,128)(2,1)} custom-call(bf16[8,64,768]{2,1,0:T(8,128)(2,1)S(1)} %get-tuple-element.39.n_ref, bf16[768,768]{1,0:T(8,128)(2,1)S(1)} %copy-done), custom_call_target="tpu_custom_call" | custom-call | flops 603979776 | bytes 2752512 | tf_op jit(solution)/shard_map/pallas_call | solution.py:114
  19.0 2.4 %collective-permute-start.5 = (bf16[96,512]{1,0:T(8,128)(2,1)S(1)}, bf16[96,512]{1,0:T(8,128)(2,1)S(1)}, u32[]{:S(2)}, u32[]{:S(2)}) collective-permute-start(bf16[96,512]{1,0:T(8,128)(2,1)S(1)} %get-tuple-element.51), channel_id=1, source_target_pairs={{0,12},{2,14},{4,0},{6,2},{8,4},{10,6},{12,8},{14,10},{1,13},{3,15... | collective-permute-start | bytes 294920 | tf_op jit(solution)/shard_map/ppermute | solution.py:299
  22.4 2.2 %collective-permute-done.3 = bf16[96,512]{1,0:T(8,128)(2,1)S(1)} collective-permute-done((bf16[96,512]{1,0:T(8,128)(2,1)S(1)}, bf16[96,512]{1,0:T(8,128)(2,1)S(1)}, u32[]{:S(2)}, u32[]{:S(2)}) %collective-permute-start.3) | collective-permute-done | bytes 98336 | tf_op jit(solution)/shard_map/ppermute | solution.py:299
  24.7 7.6 %collective-permute-done.5 = bf16[96,512]{1,0:T(8,128)(2,1)S(1)} collective-permute-done((bf16[96,512]{1,0:T(8,128)(2,1)S(1)}, bf16[96,512]{1,0:T(8,128)(2,1)S(1)}, u32[]{:S(2)}, u32[]{:S(2)}) %collective-permute-start.5) | collective-permute-done | bytes 98336 | tf_op jit(solution)/shard_map/ppermute | solution.py:299
  33.6 6.3 %all-to-all-start = ((bf16[16,96,256]{2,1,0:T(8,128)(2,1)}), bf16[16,96,256]{2,1,0:T(8,128)(2,1)S(1)}, u32[]{:S(2)}, u32[]{:S(2)}) async-start(bf16[16,96,256]{2,1,0:T(8,128)(2,1)} %shard_map.57), calls=%async_computation | async-start | bytes 1572864 | tf_op jit(solution)/shard_map/all_to_all | solution.py:309
  41.2 2.1 %shard_map.56 = (bf16[96,512]{1,0:T(8,128)(2,1)S(1)}, bf16[96,512]{1,0:T(8,128)(2,1)}, bf16[96,512]{1,0:T(8,128)(2,1)}, bf16[96,512]{1,0:T(8,128)(2,1)S(1)}, bf1...) custom-call(s32[3]{0:T(128)S(1)} %pad_add_fusion.me_ref, ...), custom_call_target="tpu_custom_call" | custom-call | flops 603979776 | bytes 2752512 | tf_op jit(solution)/shard_map/pallas_call | solution.py:131
  44.8 5.3 %collective-permute-done.7.k01 = bf16[8,96,512]{2,1,0:T(8,128)(2,1)S(1)} collective-permute-done((bf16[8,96,512]{2,1,0:T(8,128)(2,1)S(1)}, bf16[8,96,512]{2,1,0:T(8,128)(2,1)S(1)}, u32[]{:S(2)}, u32[]{:S(2)}) %collective-permute-start.7) | collective-permute-done | bytes 786464 | tf_op jit(solution)/shard_map/ppermute | solution.py:290
  50.1 2.3 %collective-permute-start.9 = (bf16[8,96,512]{2,1,0:T(8,128)(2,1)S(1)}, bf16[8,96,512]{2,1,0:T(8,128)(2,1)}, u32[]{:S(2)}, u32[]{:S(2)}) collective-permute-start(bf16[8,96,512]{2,1,0:T(8,128)(2,1)S(1)} %collective-permute-done.7.k01), channel_id=1, source_target_pairs={{0,16},{16,0},{1,17},{17,1},{2,18},{18,2},{3,19},{19,3},{4,20},{20... | collective-permute-start | bytes 2359304 | tf_op jit(solution)/shard_map/ppermute | solution.py:290
  52.4 10.2 %all-to-all-done.q_ref = bf16[16,96,256]{2,1,0:T(8,128)(2,1)S(1)} async-done(((bf16[16,96,256]{2,1,0:T(8,128)(2,1)}), bf16[16,96,256]{2,1,0:T(8,128)(2,1)S(1)}, u32[]{:S(2)}, u32[]{:S(2)}) %all-to-all-start) | async-done | bytes 786464 | tf_op jit(solution)/shard_map/all_to_all | solution.py:309
  62.6 4.7 %shard_map.58 = f32[8,2,32,1024]{3,2,1,0:T(8,128)} custom-call(s32[3]{0:T(128)S(1)} %pad_add_fusion.me_ref, bf16[16,96,256]{2,1,0:T(8,128)(2,1)S(1)} %all-to-all-done.q_ref, bf16[8,96,512]{2,1,0:T(8,128)(2,1)S(1)} %bitcast_dynamic-update-slice_fusion.8.k00, bf16[8,96,512]{2,1,0:T(8,128)(2,1)S(1)} %collective-permute-done.7.k01, ...), custom_call_target="tpu_custom_call" | custom-call | tf_op jit(solution)/shard_map/pallas_call | solution.py:172
  67.3 6.5 %all-to-all-start.1 = ((f32[8,2,32,1024]{3,2,1,0:T(8,128)}), f32[8,2,32,1024]{3,2,1,0:T(8,128)S(1)}, u32[]{:S(2)}, u32[]{:S(2)}) async-start(f32[8,2,32,1024]{3,2,1,0:T(8,128)} %shard_map.58), calls=%async_computation.1 | async-start | bytes 4194304 | tf_op jit(solution)/shard_map/all_to_all | solution.py:315
  76.5 3.1 %collective-permute-start.13 = (bf16[96,512]{1,0:T(8,128)(2,1)S(1)}, bf16[96,512]{1,0:T(8,128)(2,1)S(1)}, u32[]{:S(2)}, u32[]{:S(2)}) collective-permute-start(bf16[96,512]{1,0:T(8,128)(2,1)S(1)} %copy-done.16), channel_id=1, source_target_pairs={{0,8},{2,10},{4,12},{6,14},{8,0},{10,2},{12,4},{14,6},{1,9},{3,11}... | collective-permute-start | bytes 294920 | tf_op jit(solution)/shard_map/ppermute | solution.py:299
  84.0 3.3 %collective-permute-start.16 = (bf16[96,512]{1,0:T(8,128)(2,1)S(1)}, bf16[96,512]{1,0:T(8,128)(2,1)S(1)}, u32[]{:S(2)}, u32[]{:S(2)}) collective-permute-start(bf16[96,512]{1,0:T(8,128)(2,1)S(1)} %copy-done.10), channel_id=1, source_target_pairs={{0,14},{2,0},{4,2},{6,4},{8,6},{10,8},{12,10},{14,12},{1,15},{3,1}... | collective-permute-start | bytes 294920 | tf_op jit(solution)/shard_map/ppermute | solution.py:299
  87.3 4.2 %collective-permute-done.12 = bf16[96,512]{1,0:T(8,128)(2,1)S(1)} collective-permute-done((bf16[96,512]{1,0:T(8,128)(2,1)S(1)}, bf16[96,512]{1,0:T(8,128)(2,1)S(1)}, u32[]{:S(2)}, u32[]{:S(2)}) %collective-permute-start.12) | collective-permute-done | bytes 98336 | tf_op jit(solution)/shard_map/ppermute | solution.py:299
  91.6 5.8 %collective-permute-done.15 = bf16[96,512]{1,0:T(8,128)(2,1)S(1)} collective-permute-done((bf16[96,512]{1,0:T(8,128)(2,1)S(1)}, bf16[96,512]{1,0:T(8,128)(2,1)S(1)}, u32[]{:S(2)}, u32[]{:S(2)}) %collective-permute-start.15) | collective-permute-done | bytes 98336 | tf_op jit(solution)/shard_map/ppermute | solution.py:299
  99.2 2.3 %all-to-all-done.1.parts = f32[8,2,32,1024]{3,2,1,0:T(8,128)S(1)} async-done(((f32[8,2,32,1024]{3,2,1,0:T(8,128)}), f32[8,2,32,1024]{3,2,1,0:T(8,128)S(1)}, u32[]{:S(2)}, u32[]{:S(2)}) %all-to-all-start.1) | async-done | bytes 2097184 | tf_op jit(solution)/shard_map/all_to_all | solution.py:315
  101.7 5.6 %collective-permute-done.20.other = f32[32,1024]{1,0:T(8,128)S(1)} collective-permute-done((f32[32,1024]{1,0:T(8,128)S(1)}, f32[32,1024]{1,0:T(8,128)S(1)}, u32[]{:S(2)}, u32[]{:S(2)}) %collective-permute-start.20) | collective-permute-done | bytes 131104 | tf_op jit(solution)/shard_map/ppermute | solution.py:290
  108.5 3.6 %all-to-all-start.2 = ((bf16[8,2,32,1024]{3,2,1,0:T(8,128)(2,1)}), bf16[8,2,32,1024]{3,2,1,0:T(8,128)(2,1)S(1)}, u32[]{:S(2)}, u32[]{:S(2)}) async-start(bf16[8,2,32,1024]{3,2,1,0:T(8,128)(2,1)} %shard_map.61), calls=%async_computation.2 | async-start | bytes 2097152 | tf_op jit(solution)/shard_map/all_to_all | solution.py:321
  112.1 2.2 %collective-permute-start.18 = (bf16[8,96,512]{2,1,0:T(8,128)(2,1)S(1)}, bf16[8,96,512]{2,1,0:T(8,128)(2,1)S(1)}, u32[]{:S(2)}, u32[]{:S(2)}) collective-permute-start(bf16[8,96,512]{2,1,0:T(8,128)(2,1)S(1)} %bitcast_dynamic-update-slice_fusion.v00), channel_id=1, source_target_pairs={{0,16},{16,0},{1,17},{17,1},{2,18},{18,2},{3,19},{19,3},{4,20},{20... | collective-permute-start | bytes 2359304 | tf_op jit(solution)/shard_map/ppermute | solution.py:290
  114.3 3.1 %collective-permute-done.17.v01 = bf16[8,96,512]{2,1,0:T(8,128)(2,1)} collective-permute-done((bf16[8,96,512]{2,1,0:T(8,128)(2,1)S(1)}, bf16[8,96,512]{2,1,0:T(8,128)(2,1)}, u32[]{:S(2)}, u32[]{:S(2)}) %collective-permute-start.17) | collective-permute-done | bytes 786464 | tf_op jit(solution)/shard_map/ppermute | solution.py:290
  117.4 3.2 %collective-permute-start.19 = (bf16[8,96,512]{2,1,0:T(8,128)(2,1)}, bf16[8,96,512]{2,1,0:T(8,128)(2,1)S(1)}, u32[]{:S(2)}, u32[]{:S(2)}) collective-permute-start(bf16[8,96,512]{2,1,0:T(8,128)(2,1)} %collective-permute-done.17.v01), channel_id=1, source_target_pairs={{0,16},{16,0},{1,17},{17,1},{2,18},{18,2},{3,19},{19,3},{4,20},{20... | collective-permute-start | bytes 2359304 | tf_op jit(solution)/shard_map/ppermute | solution.py:290
  120.6 2.1 %collective-permute-done.19.v11 = bf16[8,96,512]{2,1,0:T(8,128)(2,1)S(1)} collective-permute-done((bf16[8,96,512]{2,1,0:T(8,128)(2,1)}, bf16[8,96,512]{2,1,0:T(8,128)(2,1)S(1)}, u32[]{:S(2)}, u32[]{:S(2)}) %collective-permute-start.19) | collective-permute-done | bytes 786464 | tf_op jit(solution)/shard_map/ppermute | solution.py:290
  123.9 2.0 %shard_map.59 = (bf16[1024,1024]{1,0:T(8,128)(2,1)S(1)}, bf16[512,1024]{1,0:T(8,128)(2,1)S(1)}) custom-call(s32[3]{0:T(128)S(1)} %pad_add_fusion.me_ref, bf16[8,96,512]{2,1,0:T(8,128)(2,1)S(1)} %copy-done.5, bf16[8,96,512]{2,1,0:T(8,128)(2,1)} %collective-permute-done.17.v01, bf16[8,96,512]{2,1,0:T(8,128)(2,1)S(1)} %collective-permute-done.18.v10, ...), custom_call_target="tpu_custom_call" | custom-call | bytes 6291456 | tf_op jit(solution)/shard_map/pallas_call | solution.py:235
  126.9 4.7 %all-to-all-done.2.p_ref = bf16[8,2,32,1024]{3,2,1,0:T(8,128)(2,1)S(1)} async-done(((bf16[8,2,32,1024]{3,2,1,0:T(8,128)(2,1)}), bf16[8,2,32,1024]{3,2,1,0:T(8,128)(2,1)S(1)}, u32[]{:S(2)}, u32[]{:S(2)}) %all-to-all-start.2) | async-done | bytes 1048608 | tf_op jit(solution)/shard_map/all_to_all | solution.py:321
  132.9 1.9 %shard_map.62 = bf16[16,96,256]{2,1,0:T(8,128)(2,1)S(1)} custom-call(s32[3]{0:T(128)S(1)} %pad_add_fusion.me_ref, bf16[1024,1024]{1,0:T(8,128)(2,1)S(1)} %get-tuple-element.68.vf, bf16[512,1024]{1,0:T(8,128)(2,1)S(1)} %copy-done.3, bf16[8,2,32,1024]{3,2,1,0:T(8,128)(2,1)S(1)} %all-to-all-done.2.p_ref), custom_call_target="tpu_custom_call" | custom-call | tf_op jit(solution)/shard_map/pallas_call | solution.py:259
  134.8 30.3 %all_to_all.20.m_ref = bf16[16,96,256]{2,1,0:T(8,128)(2,1)S(1)} all-to-all(bf16[16,96,256]{2,1,0:T(8,128)(2,1)S(1)} %shard_map.62), channel_id=1, replica_groups=mesh['y'=4,'xh'=2,'c'=2,'z'=8,'xl'=2] {'z','c'}, dimensions={0} | all-to-all | bytes 1572864 | tf_op jit(solution)/shard_map/all_to_all | solution.py:323
  165.1 1.7 %shard_map.63 = bf16[8,64,768]{2,1,0:T(8,128)(2,1)} custom-call(bf16[16,96,256]{2,1,0:T(8,128)(2,1)S(1)} %all_to_all.20.m_ref, bf16[768,768]{1,0:T(8,128)(2,1)S(1)} %copy-done.1), custom_call_target="tpu_custom_call" | custom-call | tf_op jit(solution)/shard_map/pallas_call | solution.py:279
  (81 shorter events, 19.3 us)
Async XLA Ops:
  0.0 17.3 %copy-start = (bf16[768,768]{1,0:T(8,128)(2,1)S(1)}, bf16[768,768]{1,0:T(8,128)(2,1)}, u32[]{:S(2)}) copy-start(bf16[768,768]{1,0:T(8,128)(2,1)} %w_ref.4) | copy-start | bytes 3538948
  3.1 18.3 %collective-permute-start = (bf16[96,512]{1,0:T(8,128)(2,1)S(1)}, bf16[96,512]{1,0:T(8,128)(2,1)S(1)}, u32[]{:S(2)}, u32[]{:S(2)}) collective-permute-start(bf16[96,512]{1,0:T(8,128)(2,1)S(1)} %get-tuple-element.45), channel_id=1, source_target_pairs={{0,2},{2,4},{4,6},{6,8},{8,10},{10,12},{12,14},{14,0},{1,3},{3,5},... | collective-permute-start | bytes 294920 | tf_op jit(solution)/shard_map/ppermute | solution.py:299
  5.6 13.4 %collective-permute-start.1 = (bf16[96,512]{1,0:T(8,128)(2,1)S(1)}, bf16[96,512]{1,0:T(8,128)(2,1)S(1)}, u32[]{:S(2)}, u32[]{:S(2)}) collective-permute-start(bf16[96,512]{1,0:T(8,128)(2,1)S(1)} %get-tuple-element.46), channel_id=1, source_target_pairs={{0,4},{2,6},{4,8},{6,10},{8,12},{10,14},{12,0},{14,2},{1,5},{3,7},... | collective-permute-start | bytes 294920 | tf_op jit(solution)/shard_map/ppermute | solution.py:299
  8.6 13.8 %collective-permute-start.2 = (bf16[96,512]{1,0:T(8,128)(2,1)S(1)}, bf16[96,512]{1,0:T(8,128)(2,1)S(1)}, u32[]{:S(2)}, u32[]{:S(2)}) collective-permute-start(bf16[96,512]{1,0:T(8,128)(2,1)S(1)} %get-tuple-element.48), channel_id=1, source_target_pairs={{0,6},{2,8},{4,10},{6,12},{8,14},{10,0},{12,2},{14,4},{1,7},{3,9},... | collective-permute-start | bytes 294920 | tf_op jit(solution)/shard_map/ppermute | solution.py:299
  12.4 12.3 %collective-permute-start.3 = (bf16[96,512]{1,0:T(8,128)(2,1)S(1)}, bf16[96,512]{1,0:T(8,128)(2,1)S(1)}, u32[]{:S(2)}, u32[]{:S(2)}) collective-permute-start(bf16[96,512]{1,0:T(8,128)(2,1)S(1)} %get-tuple-element.49), channel_id=1, source_target_pairs={{0,8},{2,10},{4,12},{6,14},{8,0},{10,2},{12,4},{14,6},{1,9},{3,11}... | collective-permute-start | bytes 294920 | tf_op jit(solution)/shard_map/ppermute | solution.py:299
  12.8 11.8 %collective-permute-start.4 = (bf16[96,512]{1,0:T(8,128)(2,1)S(1)}, bf16[96,512]{1,0:T(8,128)(2,1)S(1)}, u32[]{:S(2)}, u32[]{:S(2)}) collective-permute-start(bf16[96,512]{1,0:T(8,128)(2,1)S(1)} %get-tuple-element.50), channel_id=1, source_target_pairs={{0,10},{2,12},{4,14},{6,0},{8,2},{10,4},{12,6},{14,8},{1,11},{3,13... | collective-permute-start | bytes 294920 | tf_op jit(solution)/shard_map/ppermute | solution.py:299
  19.0 13.3 %collective-permute-start.5 = (bf16[96,512]{1,0:T(8,128)(2,1)S(1)}, bf16[96,512]{1,0:T(8,128)(2,1)S(1)}, u32[]{:S(2)}, u32[]{:S(2)}) collective-permute-start(bf16[96,512]{1,0:T(8,128)(2,1)S(1)} %get-tuple-element.51), channel_id=1, source_target_pairs={{0,12},{2,14},{4,0},{6,2},{8,4},{10,6},{12,8},{14,10},{1,13},{3,15... | collective-permute-start | bytes 294920 | tf_op jit(solution)/shard_map/ppermute | solution.py:299
  21.4 10.9 %collective-permute-start.6 = (bf16[96,512]{1,0:T(8,128)(2,1)S(1)}, bf16[96,512]{1,0:T(8,128)(2,1)S(1)}, u32[]{:S(2)}, u32[]{:S(2)}) collective-permute-start(bf16[96,512]{1,0:T(8,128)(2,1)S(1)} %get-tuple-element.52), channel_id=1, source_target_pairs={{0,14},{2,0},{4,2},{6,4},{8,6},{10,8},{12,10},{14,12},{1,15},{3,1}... | collective-permute-start | bytes 294920 | tf_op jit(solution)/shard_map/ppermute | solution.py:299
  32.3 17.8 %collective-permute-start.7 = (bf16[8,96,512]{2,1,0:T(8,128)(2,1)S(1)}, bf16[8,96,512]{2,1,0:T(8,128)(2,1)S(1)}, u32[]{:S(2)}, u32[]{:S(2)}) collective-permute-start(bf16[8,96,512]{2,1,0:T(8,128)(2,1)S(1)} %bitcast_dynamic-update-slice_fusion.8.k00), channel_id=1, source_target_pairs={{0,1},{1,0},{2,3},{3,2},{4,5},{5,4},{6,7},{7,6},{8,9},{9,8},{10,11... | collective-permute-start | bytes 2359304 | tf_op jit(solution)/shard_map/ppermute | solution.py:290
  33.6 29.0 %all-to-all-start = ((bf16[16,96,256]{2,1,0:T(8,128)(2,1)}), bf16[16,96,256]{2,1,0:T(8,128)(2,1)S(1)}, u32[]{:S(2)}, u32[]{:S(2)}) async-start(bf16[16,96,256]{2,1,0:T(8,128)(2,1)} %shard_map.57), calls=%async_computation | async-start | bytes 1572864 | tf_op jit(solution)/shard_map/all_to_all | solution.py:309
  44.6 22.7 %copy-start.9 = (bf16[96,512]{1,0:T(8,128)(2,1)}, bf16[96,512]{1,0:T(8,128)(2,1)S(1)}, u32[]{:S(2)}) copy-start(bf16[96,512]{1,0:T(8,128)(2,1)S(1)} %get-tuple-element.67) | copy-start | bytes 294916
  44.6 22.7 %copy-start.11 = (bf16[96,512]{1,0:T(8,128)(2,1)}, bf16[96,512]{1,0:T(8,128)(2,1)S(1)}, u32[]{:S(2)}) copy-start(bf16[96,512]{1,0:T(8,128)(2,1)S(1)} %get-tuple-element.66) | copy-start | bytes 294916
  44.6 22.7 %copy-start.13 = (bf16[96,512]{1,0:T(8,128)(2,1)}, bf16[96,512]{1,0:T(8,128)(2,1)S(1)}, u32[]{:S(2)}) copy-start(bf16[96,512]{1,0:T(8,128)(2,1)S(1)} %get-tuple-element.65) | copy-start | bytes 294916
  44.6 22.7 %copy-start.15 = (bf16[96,512]{1,0:T(8,128)(2,1)}, bf16[96,512]{1,0:T(8,128)(2,1)S(1)}, u32[]{:S(2)}) copy-start(bf16[96,512]{1,0:T(8,128)(2,1)S(1)} %get-tuple-element.64) | copy-start | bytes 294916
  44.6 7.8 %collective-permute-start.8 = (bf16[8,96,512]{2,1,0:T(8,128)(2,1)S(1)}, bf16[8,96,512]{2,1,0:T(8,128)(2,1)S(1)}, u32[]{:S(2)}, u32[]{:S(2)}) collective-permute-start(bf16[8,96,512]{2,1,0:T(8,128)(2,1)S(1)} %bitcast_dynamic-update-slice_fusion.8.k00), channel_id=1, source_target_pairs={{0,16},{16,0},{1,17},{17,1},{2,18},{18,2},{3,19},{19,3},{4,20},{20... | collective-permute-start | bytes 2359304 | tf_op jit(solution)/shard_map/ppermute | solution.py:290
  50.1 12.5 %collective-permute-start.9 = (bf16[8,96,512]{2,1,0:T(8,128)(2,1)S(1)}, bf16[8,96,512]{2,1,0:T(8,128)(2,1)}, u32[]{:S(2)}, u32[]{:S(2)}) collective-permute-start(bf16[8,96,512]{2,1,0:T(8,128)(2,1)S(1)} %collective-permute-done.7.k01), channel_id=1, source_target_pairs={{0,16},{16,0},{1,17},{17,1},{2,18},{18,2},{3,19},{19,3},{4,20},{20... | collective-permute-start | bytes 2359304 | tf_op jit(solution)/shard_map/ppermute | solution.py:290
  67.3 15.1 %copy-start.12 = (bf16[96,512]{1,0:T(8,128)(2,1)S(1)}, bf16[96,512]{1,0:T(8,128)(2,1)}, u32[]{:S(2)}) copy-start(bf16[96,512]{1,0:T(8,128)(2,1)} %copy-done.11) | copy-start | bytes 294916
  67.3 16.7 %copy-start.10 = (bf16[96,512]{1,0:T(8,128)(2,1)S(1)}, bf16[96,512]{1,0:T(8,128)(2,1)}, u32[]{:S(2)}) copy-start(bf16[96,512]{1,0:T(8,128)(2,1)} %copy-done.9) | copy-start | bytes 294916
  67.3 34.1 %all-to-all-start.1 = ((f32[8,2,32,1024]{3,2,1,0:T(8,128)}), f32[8,2,32,1024]{3,2,1,0:T(8,128)S(1)}, u32[]{:S(2)}, u32[]{:S(2)}) async-start(f32[8,2,32,1024]{3,2,1,0:T(8,128)} %shard_map.58), calls=%async_computation.1 | async-start | bytes 4194304 | tf_op jit(solution)/shard_map/all_to_all | solution.py:315
  73.8 8.6 %collective-permute-start.10 = (bf16[96,512]{1,0:T(8,128)(2,1)}, bf16[96,512]{1,0:T(8,128)(2,1)S(1)}, u32[]{:S(2)}, u32[]{:S(2)}) collective-permute-start(bf16[96,512]{1,0:T(8,128)(2,1)} %get-tuple-element.61), channel_id=1, source_target_pairs={{0,2},{2,4},{4,6},{6,8},{8,10},{10,12},{12,14},{14,0},{1,3},{3,5},... | collective-permute-start | bytes 294920 | tf_op jit(solution)/shard_map/ppermute | solution.py:299
  73.9 10.1 %collective-permute-start.11 = (bf16[96,512]{1,0:T(8,128)(2,1)}, bf16[96,512]{1,0:T(8,128)(2,1)S(1)}, u32[]{:S(2)}, u32[]{:S(2)}) collective-permute-start(bf16[96,512]{1,0:T(8,128)(2,1)} %get-tuple-element.62), channel_id=1, source_target_pairs={{0,4},{2,6},{4,8},{6,10},{8,12},{10,14},{12,0},{14,2},{1,5},{3,7},... | collective-permute-start | bytes 294920 | tf_op jit(solution)/shard_map/ppermute | solution.py:299
  75.2 16.3 %collective-permute-start.12 = (bf16[96,512]{1,0:T(8,128)(2,1)S(1)}, bf16[96,512]{1,0:T(8,128)(2,1)S(1)}, u32[]{:S(2)}, u32[]{:S(2)}) collective-permute-start(bf16[96,512]{1,0:T(8,128)(2,1)S(1)} %copy-done.18), channel_id=1, source_target_pairs={{0,6},{2,8},{4,10},{6,12},{8,14},{10,0},{12,2},{14,4},{1,7},{3,9},... | collective-permute-start | bytes 294920 | tf_op jit(solution)/shard_map/ppermute | solution.py:299
  76.5 15.0 %collective-permute-start.13 = (bf16[96,512]{1,0:T(8,128)(2,1)S(1)}, bf16[96,512]{1,0:T(8,128)(2,1)S(1)}, u32[]{:S(2)}, u32[]{:S(2)}) collective-permute-start(bf16[96,512]{1,0:T(8,128)(2,1)S(1)} %copy-done.16), channel_id=1, source_target_pairs={{0,8},{2,10},{4,12},{6,14},{8,0},{10,2},{12,4},{14,6},{1,9},{3,11}... | collective-permute-start | bytes 294920 | tf_op jit(solution)/shard_map/ppermute | solution.py:299
  79.7 11.9 %collective-permute-start.14 = (bf16[96,512]{1,0:T(8,128)(2,1)S(1)}, bf16[96,512]{1,0:T(8,128)(2,1)S(1)}, u32[]{:S(2)}, u32[]{:S(2)}) collective-permute-start(bf16[96,512]{1,0:T(8,128)(2,1)S(1)} %copy-done.14), channel_id=1, source_target_pairs={{0,10},{2,12},{4,14},{6,0},{8,2},{10,4},{12,6},{14,8},{1,11},{3,13... | collective-permute-start | bytes 294920 | tf_op jit(solution)/shard_map/ppermute | solution.py:299
  82.5 15.0 %collective-permute-start.15 = (bf16[96,512]{1,0:T(8,128)(2,1)S(1)}, bf16[96,512]{1,0:T(8,128)(2,1)S(1)}, u32[]{:S(2)}, u32[]{:S(2)}) collective-permute-start(bf16[96,512]{1,0:T(8,128)(2,1)S(1)} %copy-done.12), channel_id=1, source_target_pairs={{0,12},{2,14},{4,0},{6,2},{8,4},{10,6},{12,8},{14,10},{1,13},{3,15... | collective-permute-start | bytes 294920 | tf_op jit(solution)/shard_map/ppermute | solution.py:299
  84.0 15.0 %collective-permute-start.16 = (bf16[96,512]{1,0:T(8,128)(2,1)S(1)}, bf16[96,512]{1,0:T(8,128)(2,1)S(1)}, u32[]{:S(2)}, u32[]{:S(2)}) collective-permute-start(bf16[96,512]{1,0:T(8,128)(2,1)S(1)} %copy-done.10), channel_id=1, source_target_pairs={{0,14},{2,0},{4,2},{6,4},{8,6},{10,8},{12,10},{14,12},{1,15},{3,1}... | collective-permute-start | bytes 294920 | tf_op jit(solution)/shard_map/ppermute | solution.py:299
  99.1 18.3 %collective-permute-start.17 = (bf16[8,96,512]{2,1,0:T(8,128)(2,1)S(1)}, bf16[8,96,512]{2,1,0:T(8,128)(2,1)}, u32[]{:S(2)}, u32[]{:S(2)}) collective-permute-start(bf16[8,96,512]{2,1,0:T(8,128)(2,1)S(1)} %bitcast_dynamic-update-slice_fusion.v00), channel_id=1, source_target_pairs={{0,1},{1,0},{2,3},{3,2},{4,5},{5,4},{6,7},{7,6},{8,9},{9,8},{10,11... | collective-permute-start | bytes 2359304 | tf_op jit(solution)/shard_map/ppermute | solution.py:290
  101.6 5.7 %collective-permute-start.20 = (f32[32,1024]{1,0:T(8,128)S(1)}, f32[32,1024]{1,0:T(8,128)S(1)}, u32[]{:S(2)}, u32[]{:S(2)}) collective-permute-start(f32[32,1024]{1,0:T(8,128)S(1)} %get-tuple-element.72.half), channel_id=1, source_target_pairs={{0,2},{2,0},{4,6},{6,4},{8,10},{10,8},{12,14},{14,12},{1,3},{3,1},... | collective-permute-start | bytes 393224 | tf_op jit(solution)/shard_map/ppermute | solution.py:290
  108.5 23.2 %all-to-all-start.2 = ((bf16[8,2,32,1024]{3,2,1,0:T(8,128)(2,1)}), bf16[8,2,32,1024]{3,2,1,0:T(8,128)(2,1)S(1)}, u32[]{:S(2)}, u32[]{:S(2)}) async-start(bf16[8,2,32,1024]{3,2,1,0:T(8,128)(2,1)} %shard_map.61), calls=%async_computation.2 | async-start | bytes 2097152 | tf_op jit(solution)/shard_map/all_to_all | solution.py:321
  112.1 8.6 %collective-permute-start.18 = (bf16[8,96,512]{2,1,0:T(8,128)(2,1)S(1)}, bf16[8,96,512]{2,1,0:T(8,128)(2,1)S(1)}, u32[]{:S(2)}, u32[]{:S(2)}) collective-permute-start(bf16[8,96,512]{2,1,0:T(8,128)(2,1)S(1)} %bitcast_dynamic-update-slice_fusion.v00), channel_id=1, source_target_pairs={{0,16},{16,0},{1,17},{17,1},{2,18},{18,2},{3,19},{19,3},{4,20},{20... | collective-permute-start | bytes 2359304 | tf_op jit(solution)/shard_map/ppermute | solution.py:290
  117.4 5.4 %collective-permute-start.19 = (bf16[8,96,512]{2,1,0:T(8,128)(2,1)}, bf16[8,96,512]{2,1,0:T(8,128)(2,1)S(1)}, u32[]{:S(2)}, u32[]{:S(2)}) collective-permute-start(bf16[8,96,512]{2,1,0:T(8,128)(2,1)} %collective-permute-done.17.v01), channel_id=1, source_target_pairs={{0,16},{16,0},{1,17},{17,1},{2,18},{18,2},{3,19},{19,3},{4,20},{20... | collective-permute-start | bytes 2359304 | tf_op jit(solution)/shard_map/ppermute | solution.py:290
  134.8 30.3 %copy-start.1 = (bf16[768,768]{1,0:T(8,128)(2,1)S(1)}, bf16[768,768]{1,0:T(8,128)(2,1)}, u32[]{:S(2)}) copy-start(bf16[768,768]{1,0:T(8,128)(2,1)} %w_ref.5) | copy-start | bytes 3538948
  (11 other events, 61.9 us)

commit v9 on v8

--- a/solution.py
+++ b/solution.py
@@ -310,10 +310,12 @@
     v = list(value_chunks(me, n, wv))
     k = jnp.stack(k)
     k_far, v[4] = lax.optimization_barrier((flip(k, "xl", 2, 1), v[4]))
+    for s in (3, 5):
+        v[s] = shift(v[s], s)
     scores = score(me, q, (k, k_far, flip(k, "c", 2, 1), flip(k_far, "c", 2, 1)))
     *v, scores = lax.optimization_barrier((*v, scores))
     parts = lax.all_to_all(scores, ("y", "xh"), 0, 0, tiled=True)
-    for s in (3, 5, 4, 2, 6, 1, 7):
+    for s in (4, 2, 6, 1, 7):
         v[s] = shift(v[s], s)
     full, half = total(parts)
     rows = ROWS * 2 * PEERS

time: 167 us -> 164 us (0.982)
  waiting for transfers between devices: 56.8 us -> 49.4 us
  local copies, waits for them, and re-layouts: 6.07 us -> 9.09 us
  starting transfers between devices: 54.9 us -> 57.2 us
    all_to_all x1, waiting for transfers between devices: 2.28 us -> 10.2 us  [local(): parts = lax.all_to_all(scores, ('y', 'xh'), 0, 0, tiled=True)]
    ppermute x7, waiting for transfers between devices: 16.1 us -> 10.3 us  [flip(): return lax.ppermute(x, axes, [(i, i ^ s) for i in range(n)])]
    ppermute x14, waiting for transfers between devices: 23.4 us -> 18.4 us  [shift(): return lax.ppermute(x, 'z', [(i, (i + s) % Z) for i in range(Z)])]
    all_to_all x1, waiting for transfers between devices: 10.2 us -> 5.55 us  [local(): q = lax.all_to_all(q, ('z', 'c'), 0, 0, tiled=True)]
    unnamed x52, local copies, waits for them, and re-layouts: 6.05 us -> 9.07 us
  transfers between devices with their start and end apart: 24 -> 24, of which waited for: 14 -> 13; matrix products, arithmetic and copies ran while one was open for 0% -> 1% of each run, Pallas kernels for 4% -> 7%
where the time goes in v9:
time: 164 us
  starting transfers between devices  57.2 us (35%)
  waiting for transfers between devices  49.4 us (30%)
  blocking collectives  29.8 us (18%)
  Pallas kernels  17.7 us (11%)
  local copies, waits for them, and re-layouts  9.09 us (6%)
    all_to_all x1, blocking collectives, local(): mixed = lax.all_to_all(mix(me, laid, probs), ('z', 'c'), 0, 0, tiled=True)  29.8 us
    ppermute x14, starting transfers between devices, shift(): return lax.ppermute(x, 'z', [(i, (i + s) % Z) for i in range(Z)])  28.9 us
    ppermute x14, waiting for transfers between devices, shift(): return lax.ppermute(x, 'z', [(i, (i + s) % Z) for i in range(Z)])  18.4 us
    ppermute x7, starting transfers between devices, flip(): return lax.ppermute(x, axes, [(i, i ^ s) for i in range(n)])  10.9 us
    ppermute x7, waiting for transfers between devices, flip(): return lax.ppermute(x, axes, [(i, i ^ s) for i in range(n)])  10.3 us
    all_to_all x1, waiting for transfers between devices, local(): parts = lax.all_to_all(scores, ('y', 'xh'), 0, 0, tiled=True)  10.2 us
    unnamed x52, local copies, waits for them, and re-layouts  9.07 us
    all_to_all x1, starting transfers between devices, local(): parts = lax.all_to_all(scores, ('y', 'xh'), 0, 0, tiled=True)  6.5 us
  transfers between devices with their start and end apart: 24, of which 13 were waited for; matrix products, arithmetic and copies ran while one was open for 1% of the time, Pallas kernels for 7%

profile of v9, /device:TPU:1, one launch (start us, length us, event | category | flops | bytes accessed | tf_op | source)
XLA Modules:
  0.0 163.5 jit_solution(4048670485833409957)
XLA Ops:
  0.1 3.0 %shard_map.55 = (bf16[8,64,768]{2,1,0:T(8,128)(2,1)S(1)}, bf16[96,512]{1,0:T(8,128)(2,1)S(1)}, bf16[96,512]{1,0:T(8,128)(2,1)S(1)}, bf16[96,512]{1,0:T(8,128)(2,...) custom-call(s32[3]{0:T(128)S(1)} %pad_add_fusion.me_ref, ...), custom_call_target="tpu_custom_call" | custom-call | tf_op jit(solution)/shard_map/pallas_call | solution.py:86
  3.1 2.5 %collective-permute-start.1 = (bf16[96,512]{1,0:T(8,128)(2,1)S(1)}, bf16[96,512]{1,0:T(8,128)(2,1)S(1)}, u32[]{:S(2)}, u32[]{:S(2)}) collective-permute-start(bf16[96,512]{1,0:T(8,128)(2,1)S(1)} %get-tuple-element.45), channel_id=1, source_target_pairs={{0,2},{2,4},{4,6},{6,8},{8,10},{10,12},{12,14},{14,0},{1,3},{3,5},... | collective-permute-start | bytes 294920 | tf_op jit(solution)/shard_map/ppermute | solution.py:299
  5.6 3.0 %collective-permute-start.2 = (bf16[96,512]{1,0:T(8,128)(2,1)S(1)}, bf16[96,512]{1,0:T(8,128)(2,1)S(1)}, u32[]{:S(2)}, u32[]{:S(2)}) collective-permute-start(bf16[96,512]{1,0:T(8,128)(2,1)S(1)} %get-tuple-element.46), channel_id=1, source_target_pairs={{0,4},{2,6},{4,8},{6,10},{8,12},{10,14},{12,0},{14,2},{1,5},{3,7},... | collective-permute-start | bytes 294920 | tf_op jit(solution)/shard_map/ppermute | solution.py:299
  8.6 3.8 %collective-permute-start.3 = (bf16[96,512]{1,0:T(8,128)(2,1)S(1)}, bf16[96,512]{1,0:T(8,128)(2,1)S(1)}, u32[]{:S(2)}, u32[]{:S(2)}) collective-permute-start(bf16[96,512]{1,0:T(8,128)(2,1)S(1)} %get-tuple-element.48), channel_id=1, source_target_pairs={{0,6},{2,8},{4,10},{6,12},{8,14},{10,0},{12,2},{14,4},{1,7},{3,9},... | collective-permute-start | bytes 294920 | tf_op jit(solution)/shard_map/ppermute | solution.py:299
  12.8 4.5 %collective-permute-start.5 = (bf16[96,512]{1,0:T(8,128)(2,1)S(1)}, bf16[96,512]{1,0:T(8,128)(2,1)S(1)}, u32[]{:S(2)}, u32[]{:S(2)}) collective-permute-start(bf16[96,512]{1,0:T(8,128)(2,1)S(1)} %get-tuple-element.50), channel_id=1, source_target_pairs={{0,10},{2,12},{4,14},{6,0},{8,2},{10,4},{12,6},{14,8},{1,11},{3,13... | collective-permute-start | bytes 294920 | tf_op jit(solution)/shard_map/ppermute | solution.py:299
  17.3 1.7 %shard_map.57 = bf16[16,96,256]{2,1,0:T(8,128)(2,1)} custom-call(bf16[8,64,768]{2,1,0:T(8,128)(2,1)S(1)} %get-tuple-element.39.n_ref, bf16[768,768]{1,0:T(8,128)(2,1)S(1)} %copy-done), custom_call_target="tpu_custom_call" | custom-call | flops 603979776 | bytes 2752512 | tf_op jit(solution)/shard_map/pallas_call | solution.py:114
  19.0 2.4 %collective-permute-start.6 = (bf16[96,512]{1,0:T(8,128)(2,1)S(1)}, bf16[96,512]{1,0:T(8,128)(2,1)S(1)}, u32[]{:S(2)}, u32[]{:S(2)}) collective-permute-start(bf16[96,512]{1,0:T(8,128)(2,1)S(1)} %get-tuple-element.51), channel_id=1, source_target_pairs={{0,12},{2,14},{4,0},{6,2},{8,4},{10,6},{12,8},{14,10},{1,13},{3,15... | collective-permute-start | bytes 294920 | tf_op jit(solution)/shard_map/ppermute | solution.py:299
  22.4 2.2 %collective-permute-done.4 = bf16[96,512]{1,0:T(8,128)(2,1)S(1)} collective-permute-done((bf16[96,512]{1,0:T(8,128)(2,1)S(1)}, bf16[96,512]{1,0:T(8,128)(2,1)S(1)}, u32[]{:S(2)}, u32[]{:S(2)}) %collective-permute-start.4) | collective-permute-done | bytes 98336 | tf_op jit(solution)/shard_map/ppermute | solution.py:299
  24.7 7.6 %collective-permute-done.6 = bf16[96,512]{1,0:T(8,128)(2,1)S(1)} collective-permute-done((bf16[96,512]{1,0:T(8,128)(2,1)S(1)}, bf16[96,512]{1,0:T(8,128)(2,1)S(1)}, u32[]{:S(2)}, u32[]{:S(2)}) %collective-permute-start.6) | collective-permute-done | bytes 98336 | tf_op jit(solution)/shard_map/ppermute | solution.py:299
  33.6 6.3 %all-to-all-start = ((bf16[16,96,256]{2,1,0:T(8,128)(2,1)}), bf16[16,96,256]{2,1,0:T(8,128)(2,1)S(1)}, u32[]{:S(2)}, u32[]{:S(2)}) async-start(bf16[16,96,256]{2,1,0:T(8,128)(2,1)} %shard_map.57), calls=%async_computation | async-start | bytes 1572864 | tf_op jit(solution)/shard_map/all_to_all | solution.py:309
  45.2 4.9 %collective-permute-done.8.k01 = bf16[8,96,512]{2,1,0:T(8,128)(2,1)S(1)} collective-permute-done((bf16[8,96,512]{2,1,0:T(8,128)(2,1)S(1)}, bf16[8,96,512]{2,1,0:T(8,128)(2,1)S(1)}, u32[]{:S(2)}, u32[]{:S(2)}) %collective-permute-start.8) | collective-permute-done | bytes 786464 | tf_op jit(solution)/shard_map/ppermute | solution.py:290
  50.1 2.3 %collective-permute-start.11 = (bf16[8,96,512]{2,1,0:T(8,128)(2,1)S(1)}, bf16[8,96,512]{2,1,0:T(8,128)(2,1)}, u32[]{:S(2)}, u32[]{:S(2)}) collective-permute-start(bf16[8,96,512]{2,1,0:T(8,128)(2,1)S(1)} %collective-permute-done.8.k01), channel_id=1, source_target_pairs={{0,16},{16,0},{1,17},{17,1},{2,18},{18,2},{3,19},{19,3},{4,20},{20... | collective-permute-start | bytes 2359304 | tf_op jit(solution)/shard_map/ppermute | solution.py:290
  52.4 3.9 %collective-permute-start = (bf16[96,512]{1,0:T(8,128)(2,1)S(1)}, bf16[96,512]{1,0:T(8,128)(2,1)}, u32[]{:S(2)}, u32[]{:S(2)}) collective-permute-start(bf16[96,512]{1,0:T(8,128)(2,1)S(1)} %get-tuple-element.43), channel_id=1, source_target_pairs={{0,6},{2,8},{4,10},{6,12},{8,14},{10,0},{12,2},{14,4},{1,7},{3,9},... | collective-permute-start | bytes 294920 | tf_op jit(solution)/shard_map/ppermute | solution.py:299
  56.8 5.5 %all-to-all-done.q_ref = bf16[16,96,256]{2,1,0:T(8,128)(2,1)S(1)} async-done(((bf16[16,96,256]{2,1,0:T(8,128)(2,1)}), bf16[16,96,256]{2,1,0:T(8,128)(2,1)S(1)}, u32[]{:S(2)}, u32[]{:S(2)}) %all-to-all-start) | async-done | bytes 786464 | tf_op jit(solution)/shard_map/all_to_all | solution.py:309
  62.4 4.7 %shard_map.58 = f32[8,2,32,1024]{3,2,1,0:T(8,128)} custom-call(s32[3]{0:T(128)S(1)} %pad_add_fusion.me_ref, bf16[16,96,256]{2,1,0:T(8,128)(2,1)S(1)} %all-to-all-done.q_ref, bf16[8,96,512]{2,1,0:T(8,128)(2,1)S(1)} %bitcast_dynamic-update-slice_fusion.8.k00, bf16[8,96,512]{2,1,0:T(8,128)(2,1)S(1)} %collective-permute-done.8.k01, ...), custom_call_target="tpu_custom_call" | custom-call | tf_op jit(solution)/shard_map/pallas_call | solution.py:172
  68.1 6.5 %all-to-all-start.1 = ((f32[8,2,32,1024]{3,2,1,0:T(8,128)}), f32[8,2,32,1024]{3,2,1,0:T(8,128)S(1)}, u32[]{:S(2)}, u32[]{:S(2)}) async-start(f32[8,2,32,1024]{3,2,1,0:T(8,128)} %shard_map.58), calls=%async_computation.1 | async-start | bytes 4194304 | tf_op jit(solution)/shard_map/all_to_all | solution.py:317
  74.7 2.2 %collective-permute-start.13 = (bf16[96,512]{1,0:T(8,128)(2,1)S(1)}, bf16[96,512]{1,0:T(8,128)(2,1)S(1)}, u32[]{:S(2)}, u32[]{:S(2)}) collective-permute-start(bf16[96,512]{1,0:T(8,128)(2,1)S(1)} %copy-done.16), channel_id=1, source_target_pairs={{0,4},{2,6},{4,8},{6,10},{8,12},{10,14},{12,0},{14,2},{1,5},{3,7},... | collective-permute-start | bytes 294920 | tf_op jit(solution)/shard_map/ppermute | solution.py:299
  76.9 2.2 %collective-permute-start.14 = (bf16[96,512]{1,0:T(8,128)(2,1)S(1)}, bf16[96,512]{1,0:T(8,128)(2,1)S(1)}, u32[]{:S(2)}, u32[]{:S(2)}) collective-permute-start(bf16[96,512]{1,0:T(8,128)(2,1)S(1)} %copy-done.14), channel_id=1, source_target_pairs={{0,8},{2,10},{4,12},{6,14},{8,0},{10,2},{12,4},{14,6},{1,9},{3,11}... | collective-permute-start | bytes 294920 | tf_op jit(solution)/shard_map/ppermute | solution.py:299
  79.1 2.1 %collective-permute-start.15 = (bf16[96,512]{1,0:T(8,128)(2,1)S(1)}, bf16[96,512]{1,0:T(8,128)(2,1)S(1)}, u32[]{:S(2)}, u32[]{:S(2)}) collective-permute-start(bf16[96,512]{1,0:T(8,128)(2,1)S(1)} %copy-done.12), channel_id=1, source_target_pairs={{0,12},{2,14},{4,0},{6,2},{8,4},{10,6},{12,8},{14,10},{1,13},{3,15... | collective-permute-start | bytes 294920 | tf_op jit(solution)/shard_map/ppermute | solution.py:299
  82.7 4.8 %collective-permute-done.14 = bf16[96,512]{1,0:T(8,128)(2,1)S(1)} collective-permute-done((bf16[96,512]{1,0:T(8,128)(2,1)S(1)}, bf16[96,512]{1,0:T(8,128)(2,1)S(1)}, u32[]{:S(2)}, u32[]{:S(2)}) %collective-permute-start.14) | collective-permute-done | bytes 98336 | tf_op jit(solution)/shard_map/ppermute | solution.py:299
  88.5 2.5 %collective-permute-done.16 = bf16[96,512]{1,0:T(8,128)(2,1)S(1)} collective-permute-done((bf16[96,512]{1,0:T(8,128)(2,1)S(1)}, bf16[96,512]{1,0:T(8,128)(2,1)S(1)}, u32[]{:S(2)}, u32[]{:S(2)}) %collective-permute-start.16) | collective-permute-done | bytes 98336 | tf_op jit(solution)/shard_map/ppermute | solution.py:299
  91.1 10.2 %all-to-all-done.1.parts = f32[8,2,32,1024]{3,2,1,0:T(8,128)S(1)} async-done(((f32[8,2,32,1024]{3,2,1,0:T(8,128)}), f32[8,2,32,1024]{3,2,1,0:T(8,128)S(1)}, u32[]{:S(2)}, u32[]{:S(2)}) %all-to-all-start.1) | async-done | bytes 2097184 | tf_op jit(solution)/shard_map/all_to_all | solution.py:317
  102.4 3.3 %collective-permute-done.20.other = f32[32,1024]{1,0:T(8,128)S(1)} collective-permute-done((f32[32,1024]{1,0:T(8,128)S(1)}, f32[32,1024]{1,0:T(8,128)S(1)}, u32[]{:S(2)}, u32[]{:S(2)}) %collective-permute-start.20) | collective-permute-done | bytes 131104 | tf_op jit(solution)/shard_map/ppermute | solution.py:290
  107.0 4.6 %all-to-all-start.2 = ((bf16[8,2,32,1024]{3,2,1,0:T(8,128)(2,1)}), bf16[8,2,32,1024]{3,2,1,0:T(8,128)(2,1)S(1)}, u32[]{:S(2)}, u32[]{:S(2)}) async-start(bf16[8,2,32,1024]{3,2,1,0:T(8,128)(2,1)} %shard_map.61), calls=%async_computation.2 | async-start | bytes 2097152 | tf_op jit(solution)/shard_map/all_to_all | solution.py:323
  111.6 4.7 %collective-permute-start.18 = (bf16[8,96,512]{2,1,0:T(8,128)(2,1)S(1)}, bf16[8,96,512]{2,1,0:T(8,128)(2,1)S(1)}, u32[]{:S(2)}, u32[]{:S(2)}) collective-permute-start(bf16[8,96,512]{2,1,0:T(8,128)(2,1)S(1)} %bitcast_dynamic-update-slice_fusion.v00), channel_id=1, source_target_pairs={{0,16},{16,0},{1,17},{17,1},{2,18},{18,2},{3,19},{19,3},{4,20},{20... | collective-permute-start | bytes 2359304 | tf_op jit(solution)/shard_map/ppermute | solution.py:290
  116.2 1.5 collective-permute-start.19
  118.2 1.7 %collective-permute-done.19.v11 = bf16[8,96,512]{2,1,0:T(8,128)(2,1)S(1)} collective-permute-done((bf16[8,96,512]{2,1,0:T(8,128)(2,1)}, bf16[8,96,512]{2,1,0:T(8,128)(2,1)S(1)}, u32[]{:S(2)}, u32[]{:S(2)}) %collective-permute-start.19) | collective-permute-done | bytes 786464 | tf_op jit(solution)/shard_map/ppermute | solution.py:290
  121.0 2.0 %shard_map.59 = (bf16[1024,1024]{1,0:T(8,128)(2,1)S(1)}, bf16[512,1024]{1,0:T(8,128)(2,1)S(1)}) custom-call(s32[3]{0:T(128)S(1)} %pad_add_fusion.me_ref, bf16[8,96,512]{2,1,0:T(8,128)(2,1)S(1)} %copy-done.5, bf16[8,96,512]{2,1,0:T(8,128)(2,1)} %collective-permute-done.17.v01, bf16[8,96,512]{2,1,0:T(8,128)(2,1)S(1)} %collective-permute-done.18.v10, ...), custom_call_target="tpu_custom_call" | custom-call | bytes 6291456 | tf_op jit(solution)/shard_map/pallas_call | solution.py:235
  124.0 4.9 %all-to-all-done.2.p_ref = bf16[8,2,32,1024]{3,2,1,0:T(8,128)(2,1)S(1)} async-done(((bf16[8,2,32,1024]{3,2,1,0:T(8,128)(2,1)}), bf16[8,2,32,1024]{3,2,1,0:T(8,128)(2,1)S(1)}, u32[]{:S(2)}, u32[]{:S(2)}) %all-to-all-start.2) | async-done | bytes 1048608 | tf_op jit(solution)/shard_map/all_to_all | solution.py:323
  130.2 1.9 %shard_map.62 = bf16[16,96,256]{2,1,0:T(8,128)(2,1)S(1)} custom-call(s32[3]{0:T(128)S(1)} %pad_add_fusion.me_ref, bf16[1024,1024]{1,0:T(8,128)(2,1)S(1)} %get-tuple-element.68.vf, bf16[512,1024]{1,0:T(8,128)(2,1)S(1)} %copy-done.3, bf16[8,2,32,1024]{3,2,1,0:T(8,128)(2,1)S(1)} %all-to-all-done.2.p_ref), custom_call_target="tpu_custom_call" | custom-call | tf_op jit(solution)/shard_map/pallas_call | solution.py:259
  132.1 29.8 %all_to_all.20.m_ref = bf16[16,96,256]{2,1,0:T(8,128)(2,1)S(1)} all-to-all(bf16[16,96,256]{2,1,0:T(8,128)(2,1)S(1)} %shard_map.62), channel_id=1, replica_groups=mesh['y'=4,'xh'=2,'c'=2,'z'=8,'xl'=2] {'z','c'}, dimensions={0} | all-to-all | bytes 1572864 | tf_op jit(solution)/shard_map/all_to_all | solution.py:325
  161.8 1.7 %shard_map.63 = bf16[8,64,768]{2,1,0:T(8,128)(2,1)} custom-call(bf16[16,96,256]{2,1,0:T(8,128)(2,1)S(1)} %all_to_all.20.m_ref, bf16[768,768]{1,0:T(8,128)(2,1)S(1)} %copy-done.1), custom_call_target="tpu_custom_call" | custom-call | tf_op jit(solution)/shard_map/pallas_call | solution.py:279
  (81 shorter events, 18.4 us)
Async XLA Ops:
  0.0 17.3 %copy-start = (bf16[768,768]{1,0:T(8,128)(2,1)S(1)}, bf16[768,768]{1,0:T(8,128)(2,1)}, u32[]{:S(2)}) copy-start(bf16[768,768]{1,0:T(8,128)(2,1)} %w_ref.4) | copy-start | bytes 3538948
  3.1 18.3 %collective-permute-start.1 = (bf16[96,512]{1,0:T(8,128)(2,1)S(1)}, bf16[96,512]{1,0:T(8,128)(2,1)S(1)}, u32[]{:S(2)}, u32[]{:S(2)}) collective-permute-start(bf16[96,512]{1,0:T(8,128)(2,1)S(1)} %get-tuple-element.45), channel_id=1, source_target_pairs={{0,2},{2,4},{4,6},{6,8},{8,10},{10,12},{12,14},{14,0},{1,3},{3,5},... | collective-permute-start | bytes 294920 | tf_op jit(solution)/shard_map/ppermute | solution.py:299
  5.6 13.4 %collective-permute-start.2 = (bf16[96,512]{1,0:T(8,128)(2,1)S(1)}, bf16[96,512]{1,0:T(8,128)(2,1)S(1)}, u32[]{:S(2)}, u32[]{:S(2)}) collective-permute-start(bf16[96,512]{1,0:T(8,128)(2,1)S(1)} %get-tuple-element.46), channel_id=1, source_target_pairs={{0,4},{2,6},{4,8},{6,10},{8,12},{10,14},{12,0},{14,2},{1,5},{3,7},... | collective-permute-start | bytes 294920 | tf_op jit(solution)/shard_map/ppermute | solution.py:299
  8.6 13.8 %collective-permute-start.3 = (bf16[96,512]{1,0:T(8,128)(2,1)S(1)}, bf16[96,512]{1,0:T(8,128)(2,1)S(1)}, u32[]{:S(2)}, u32[]{:S(2)}) collective-permute-start(bf16[96,512]{1,0:T(8,128)(2,1)S(1)} %get-tuple-element.48), channel_id=1, source_target_pairs={{0,6},{2,8},{4,10},{6,12},{8,14},{10,0},{12,2},{14,4},{1,7},{3,9},... | collective-permute-start | bytes 294920 | tf_op jit(solution)/shard_map/ppermute | solution.py:299
  12.4 12.3 %collective-permute-start.4 = (bf16[96,512]{1,0:T(8,128)(2,1)S(1)}, bf16[96,512]{1,0:T(8,128)(2,1)S(1)}, u32[]{:S(2)}, u32[]{:S(2)}) collective-permute-start(bf16[96,512]{1,0:T(8,128)(2,1)S(1)} %get-tuple-element.49), channel_id=1, source_target_pairs={{0,8},{2,10},{4,12},{6,14},{8,0},{10,2},{12,4},{14,6},{1,9},{3,11}... | collective-permute-start | bytes 294920 | tf_op jit(solution)/shard_map/ppermute | solution.py:299
  12.8 11.8 %collective-permute-start.5 = (bf16[96,512]{1,0:T(8,128)(2,1)S(1)}, bf16[96,512]{1,0:T(8,128)(2,1)S(1)}, u32[]{:S(2)}, u32[]{:S(2)}) collective-permute-start(bf16[96,512]{1,0:T(8,128)(2,1)S(1)} %get-tuple-element.50), channel_id=1, source_target_pairs={{0,10},{2,12},{4,14},{6,0},{8,2},{10,4},{12,6},{14,8},{1,11},{3,13... | collective-permute-start | bytes 294920 | tf_op jit(solution)/shard_map/ppermute | solution.py:299
  19.0 13.3 %collective-permute-start.6 = (bf16[96,512]{1,0:T(8,128)(2,1)S(1)}, bf16[96,512]{1,0:T(8,128)(2,1)S(1)}, u32[]{:S(2)}, u32[]{:S(2)}) collective-permute-start(bf16[96,512]{1,0:T(8,128)(2,1)S(1)} %get-tuple-element.51), channel_id=1, source_target_pairs={{0,12},{2,14},{4,0},{6,2},{8,4},{10,6},{12,8},{14,10},{1,13},{3,15... | collective-permute-start | bytes 294920 | tf_op jit(solution)/shard_map/ppermute | solution.py:299
  21.4 10.9 %collective-permute-start.7 = (bf16[96,512]{1,0:T(8,128)(2,1)S(1)}, bf16[96,512]{1,0:T(8,128)(2,1)S(1)}, u32[]{:S(2)}, u32[]{:S(2)}) collective-permute-start(bf16[96,512]{1,0:T(8,128)(2,1)S(1)} %get-tuple-element.52), channel_id=1, source_target_pairs={{0,14},{2,0},{4,2},{6,4},{8,6},{10,8},{12,10},{14,12},{1,15},{3,1}... | collective-permute-start | bytes 294920 | tf_op jit(solution)/shard_map/ppermute | solution.py:299
  32.3 17.8 %collective-permute-start.8 = (bf16[8,96,512]{2,1,0:T(8,128)(2,1)S(1)}, bf16[8,96,512]{2,1,0:T(8,128)(2,1)S(1)}, u32[]{:S(2)}, u32[]{:S(2)}) collective-permute-start(bf16[8,96,512]{2,1,0:T(8,128)(2,1)S(1)} %bitcast_dynamic-update-slice_fusion.8.k00), channel_id=1, source_target_pairs={{0,1},{1,0},{2,3},{3,2},{4,5},{5,4},{6,7},{7,6},{8,9},{9,8},{10,11... | collective-permute-start | bytes 2359304 | tf_op jit(solution)/shard_map/ppermute | solution.py:290
  33.6 28.8 %all-to-all-start = ((bf16[16,96,256]{2,1,0:T(8,128)(2,1)}), bf16[16,96,256]{2,1,0:T(8,128)(2,1)S(1)}, u32[]{:S(2)}, u32[]{:S(2)}) async-start(bf16[16,96,256]{2,1,0:T(8,128)(2,1)} %shard_map.57), calls=%async_computation | async-start | bytes 1572864 | tf_op jit(solution)/shard_map/all_to_all | solution.py:309
  45.1 21.9 %copy-start.9 = (bf16[96,512]{1,0:T(8,128)(2,1)}, bf16[96,512]{1,0:T(8,128)(2,1)S(1)}, u32[]{:S(2)}) copy-start(bf16[96,512]{1,0:T(8,128)(2,1)S(1)} %get-tuple-element.67) | copy-start | bytes 294916
  45.1 21.9 %copy-start.11 = (bf16[96,512]{1,0:T(8,128)(2,1)}, bf16[96,512]{1,0:T(8,128)(2,1)S(1)}, u32[]{:S(2)}) copy-start(bf16[96,512]{1,0:T(8,128)(2,1)S(1)} %get-tuple-element.66) | copy-start | bytes 294916
  45.1 11.7 %collective-permute-start.10 = (bf16[8,96,512]{2,1,0:T(8,128)(2,1)S(1)}, bf16[8,96,512]{2,1,0:T(8,128)(2,1)S(1)}, u32[]{:S(2)}, u32[]{:S(2)}) collective-permute-start(bf16[8,96,512]{2,1,0:T(8,128)(2,1)S(1)} %bitcast_dynamic-update-slice_fusion.8.k00), channel_id=1, source_target_pairs={{0,16},{16,0},{1,17},{17,1},{2,18},{18,2},{3,19},{19,3},{4,20},{20... | collective-permute-start | bytes 2359304 | tf_op jit(solution)/shard_map/ppermute | solution.py:290
  50.1 12.3 %collective-permute-start.11 = (bf16[8,96,512]{2,1,0:T(8,128)(2,1)S(1)}, bf16[8,96,512]{2,1,0:T(8,128)(2,1)}, u32[]{:S(2)}, u32[]{:S(2)}) collective-permute-start(bf16[8,96,512]{2,1,0:T(8,128)(2,1)S(1)} %collective-permute-done.8.k01), channel_id=1, source_target_pairs={{0,16},{16,0},{1,17},{17,1},{2,18},{18,2},{3,19},{19,3},{4,20},{20... | collective-permute-start | bytes 2359304 | tf_op jit(solution)/shard_map/ppermute | solution.py:290
  52.4 15.7 %collective-permute-start = (bf16[96,512]{1,0:T(8,128)(2,1)S(1)}, bf16[96,512]{1,0:T(8,128)(2,1)}, u32[]{:S(2)}, u32[]{:S(2)}) collective-permute-start(bf16[96,512]{1,0:T(8,128)(2,1)S(1)} %get-tuple-element.43), channel_id=1, source_target_pairs={{0,6},{2,8},{4,10},{6,12},{8,14},{10,0},{12,2},{14,4},{1,7},{3,9},... | collective-permute-start | bytes 294920 | tf_op jit(solution)/shard_map/ppermute | solution.py:299
  56.2 11.8 %collective-permute-start.9 = (bf16[96,512]{1,0:T(8,128)(2,1)S(1)}, bf16[96,512]{1,0:T(8,128)(2,1)}, u32[]{:S(2)}, u32[]{:S(2)}) collective-permute-start(bf16[96,512]{1,0:T(8,128)(2,1)S(1)} %get-tuple-element.55), channel_id=1, source_target_pairs={{0,10},{2,12},{4,14},{6,0},{8,2},{10,4},{12,6},{14,8},{1,11},{3,13... | collective-permute-start | bytes 294920 | tf_op jit(solution)/shard_map/ppermute | solution.py:299
  68.0 11.0 %copy-start.12 = (bf16[96,512]{1,0:T(8,128)(2,1)S(1)}, bf16[96,512]{1,0:T(8,128)(2,1)}, u32[]{:S(2)}) copy-start(bf16[96,512]{1,0:T(8,128)(2,1)} %copy-done.11) | copy-start | bytes 294916
  68.0 13.2 %copy-start.10 = (bf16[96,512]{1,0:T(8,128)(2,1)S(1)}, bf16[96,512]{1,0:T(8,128)(2,1)}, u32[]{:S(2)}) copy-start(bf16[96,512]{1,0:T(8,128)(2,1)} %copy-done.9) | copy-start | bytes 294916
  68.1 13.7 %copy-start.7 = (bf16[96,512]{1,0:T(8,128)(2,1)S(1)}, bf16[96,512]{1,0:T(8,128)(2,1)}, u32[]{:S(2)}) copy-start(bf16[96,512]{1,0:T(8,128)(2,1)} %copy-done.6) | copy-start | bytes 294916
  68.1 33.3 %all-to-all-start.1 = ((f32[8,2,32,1024]{3,2,1,0:T(8,128)}), f32[8,2,32,1024]{3,2,1,0:T(8,128)S(1)}, u32[]{:S(2)}, u32[]{:S(2)}) async-start(f32[8,2,32,1024]{3,2,1,0:T(8,128)} %shard_map.58), calls=%async_computation.1 | async-start | bytes 4194304 | tf_op jit(solution)/shard_map/all_to_all | solution.py:317
  74.6 7.2 %collective-permute-start.12 = (bf16[96,512]{1,0:T(8,128)(2,1)S(1)}, bf16[96,512]{1,0:T(8,128)(2,1)S(1)}, u32[]{:S(2)}, u32[]{:S(2)}) collective-permute-start(bf16[96,512]{1,0:T(8,128)(2,1)S(1)} %copy-done.18), channel_id=1, source_target_pairs={{0,2},{2,4},{4,6},{6,8},{8,10},{10,12},{12,14},{14,0},{1,3},{3,5},... | collective-permute-start | bytes 294920 | tf_op jit(solution)/shard_map/ppermute | solution.py:299
  74.7 7.1 %collective-permute-start.13 = (bf16[96,512]{1,0:T(8,128)(2,1)S(1)}, bf16[96,512]{1,0:T(8,128)(2,1)S(1)}, u32[]{:S(2)}, u32[]{:S(2)}) collective-permute-start(bf16[96,512]{1,0:T(8,128)(2,1)S(1)} %copy-done.16), channel_id=1, source_target_pairs={{0,4},{2,6},{4,8},{6,10},{8,12},{10,14},{12,0},{14,2},{1,5},{3,7},... | collective-permute-start | bytes 294920 | tf_op jit(solution)/shard_map/ppermute | solution.py:299
  76.9 10.7 %collective-permute-start.14 = (bf16[96,512]{1,0:T(8,128)(2,1)S(1)}, bf16[96,512]{1,0:T(8,128)(2,1)S(1)}, u32[]{:S(2)}, u32[]{:S(2)}) collective-permute-start(bf16[96,512]{1,0:T(8,128)(2,1)S(1)} %copy-done.14), channel_id=1, source_target_pairs={{0,8},{2,10},{4,12},{6,14},{8,0},{10,2},{12,4},{14,6},{1,9},{3,11}... | collective-permute-start | bytes 294920 | tf_op jit(solution)/shard_map/ppermute | solution.py:299
  79.1 9.4 %collective-permute-start.15 = (bf16[96,512]{1,0:T(8,128)(2,1)S(1)}, bf16[96,512]{1,0:T(8,128)(2,1)S(1)}, u32[]{:S(2)}, u32[]{:S(2)}) collective-permute-start(bf16[96,512]{1,0:T(8,128)(2,1)S(1)} %copy-done.12), channel_id=1, source_target_pairs={{0,12},{2,14},{4,0},{6,2},{8,4},{10,6},{12,8},{14,10},{1,13},{3,15... | collective-permute-start | bytes 294920 | tf_op jit(solution)/shard_map/ppermute | solution.py:299
  81.2 9.8 %collective-permute-start.16 = (bf16[96,512]{1,0:T(8,128)(2,1)S(1)}, bf16[96,512]{1,0:T(8,128)(2,1)S(1)}, u32[]{:S(2)}, u32[]{:S(2)}) collective-permute-start(bf16[96,512]{1,0:T(8,128)(2,1)S(1)} %copy-done.10), channel_id=1, source_target_pairs={{0,14},{2,0},{4,2},{6,4},{8,6},{10,8},{12,10},{14,12},{1,15},{3,1}... | collective-permute-start | bytes 294920 | tf_op jit(solution)/shard_map/ppermute | solution.py:299
  91.0 20.6 %copy-start.4 = (bf16[8,96,512]{2,1,0:T(8,128)(2,1)}, bf16[8,96,512]{2,1,0:T(8,128)(2,1)S(1)}, u32[]{:S(2)}) copy-start(bf16[8,96,512]{2,1,0:T(8,128)(2,1)S(1)} %bitcast_dynamic-update-slice_fusion.v00) | copy-start | bytes 2359300
  91.0 25.3 %collective-permute-start.17 = (bf16[8,96,512]{2,1,0:T(8,128)(2,1)S(1)}, bf16[8,96,512]{2,1,0:T(8,128)(2,1)}, u32[]{:S(2)}, u32[]{:S(2)}) collective-permute-start(bf16[8,96,512]{2,1,0:T(8,128)(2,1)S(1)} %bitcast_dynamic-update-slice_fusion.v00), channel_id=1, source_target_pairs={{0,1},{1,0},{2,3},{3,2},{4,5},{5,4},{6,7},{7,6},{8,9},{9,8},{10,11... | collective-permute-start | bytes 2359304 | tf_op jit(solution)/shard_map/ppermute | solution.py:290
  101.4 4.3 %collective-permute-start.20 = (f32[32,1024]{1,0:T(8,128)S(1)}, f32[32,1024]{1,0:T(8,128)S(1)}, u32[]{:S(2)}, u32[]{:S(2)}) collective-permute-start(f32[32,1024]{1,0:T(8,128)S(1)} %get-tuple-element.72.half), channel_id=1, source_target_pairs={{0,2},{2,0},{4,6},{6,4},{8,10},{10,8},{12,14},{14,12},{1,3},{3,1},... | collective-permute-start | bytes 393224 | tf_op jit(solution)/shard_map/ppermute | solution.py:290
  107.0 21.9 %all-to-all-start.2 = ((bf16[8,2,32,1024]{3,2,1,0:T(8,128)(2,1)}), bf16[8,2,32,1024]{3,2,1,0:T(8,128)(2,1)S(1)}, u32[]{:S(2)}, u32[]{:S(2)}) async-start(bf16[8,2,32,1024]{3,2,1,0:T(8,128)(2,1)} %shard_map.61), calls=%async_computation.2 | async-start | bytes 2097152 | tf_op jit(solution)/shard_map/all_to_all | solution.py:323
  111.6 6.6 %collective-permute-start.18 = (bf16[8,96,512]{2,1,0:T(8,128)(2,1)S(1)}, bf16[8,96,512]{2,1,0:T(8,128)(2,1)S(1)}, u32[]{:S(2)}, u32[]{:S(2)}) collective-permute-start(bf16[8,96,512]{2,1,0:T(8,128)(2,1)S(1)} %bitcast_dynamic-update-slice_fusion.v00), channel_id=1, source_target_pairs={{0,16},{16,0},{1,17},{17,1},{2,18},{18,2},{3,19},{19,3},{4,20},{20... | collective-permute-start | bytes 2359304 | tf_op jit(solution)/shard_map/ppermute | solution.py:290
  116.2 3.6 %collective-permute-start.19 = (bf16[8,96,512]{2,1,0:T(8,128)(2,1)}, bf16[8,96,512]{2,1,0:T(8,128)(2,1)S(1)}, u32[]{:S(2)}, u32[]{:S(2)}) collective-permute-start(bf16[8,96,512]{2,1,0:T(8,128)(2,1)} %collective-permute-done.17.v01), channel_id=1, source_target_pairs={{0,16},{16,0},{1,17},{17,1},{2,18},{18,2},{3,19},{19,3},{4,20},{20... | collective-permute-start | bytes 2359304 | tf_op jit(solution)/shard_map/ppermute | solution.py:290
  132.0 29.8 %copy-start.1 = (bf16[768,768]{1,0:T(8,128)(2,1)S(1)}, bf16[768,768]{1,0:T(8,128)(2,1)}, u32[]{:S(2)}) copy-start(bf16[768,768]{1,0:T(8,128)(2,1)} %w_ref.5) | copy-start | bytes 3538948
  (11 other events, 29.2 us)

commit v10 on v3

--- a/solution.py
+++ b/solution.py
@@ -19,20 +19,24 @@
 HALF = CHUNK - DH
 PEERS = 8
 SUB = RES // 2
-KSTEP = 2 * FULL + FULL
+TOKENS = ROWS * SUB
 QUERIES = Z * SUB
 KEYS = 2 * Z * RES
+LOGITS = KEYS + KEYS // 2
 
 f32 = jnp.float32
 bf16 = jnp.bfloat16
-PARAMS = pltpu.CompilerParams(vmem_limit_bytes=8 * 1024 * 1024)
+PARAMS = pltpu.CompilerParams(vmem_limit_bytes=16 * 1024 * 1024)
 PROJECTION = pl.CostEstimate(
     flops=2 * ROWS * RES * EMBED * EMBED, bytes_accessed=2 * EMBED * (EMBED + 2 * ROWS * RES), transcendentals=0
 )
 LAYOUT = pl.CostEstimate(flops=0, bytes_accessed=16 * ROWS * RES * EMBED, transcendentals=0)
 KEY_SHAPES = ((2 * ROWS * FULL, KEYS // 2), (2 * ROWS * FULL, KEYS // 4))
+WIDE = pltpu.CompilerParams(vmem_limit_bytes=16 * 1024 * 1024)
 VMEM = pl.BlockSpec(memory_space=pltpu.VMEM)
 SMEM = pl.BlockSpec(memory_space=pltpu.SMEM)
+ANY = pl.BlockSpec(memory_space=pl.ANY)
+HBM = pl.BlockSpec(memory_space=pltpu.HBM)
 
 
 def chunk_pieces(z):
@@ -46,62 +50,80 @@
     return lax.dot_general(a, b, (((ca,), (cb,)), ((), ())), preferred_element_type=f32)
 
 
+def shared_head(z):
+    return z // 2 * (2 * CHUNK) + FULL
+
+
 def chunk_rows(z):
     odd = lax.rem(z, 2)
     base = z * CHUNK
     return pl.multiple_of(base + odd * HALF, HALF), pl.multiple_of(base + (1 - odd) * FULL, HALF)
 
 
-def send_pieces(z, t_ref, outs):
-    for s, out in enumerate(outs):
-        full, half = chunk_rows(lax.rem(z + s, Z))
-        out[0:FULL, :] = t_ref[pl.ds(full, FULL), :]
-        out[FULL:CHUNK, :] = t_ref[pl.ds(half, HALF), :]
-
-
-def key_kernel(me_ref, x_ref, w_ref, n_ref, *rest):
-    outs, t_ref = rest[:Z], rest[Z]
+def fetches(sources, buffers, sems):
+    copies = [pltpu.make_async_copy(a, b, sems.at[i]) for i, (a, b) in enumerate(zip(sources, buffers))]
+    for copy in copies:
+        copy.start()
+    return copies
+
+
+def in_hbm(*arrays):
+    return [pltpu.with_memory_space_constraint(a, pltpu.HBM) for a in arrays]
+
+
+def key_kernel(me_ref, x_hbm, w_hbm, n_ref, *rest):
+    outs, (x_ref, w_ref, t_ref, sems) = rest[:Z], rest[Z:]
+    copy_x, copy_w = fetches((x_hbm, w_hbm), (x_ref, w_ref), sems)
+    copy_x.wait()
     x = x_ref[...].astype(f32)
     centred = x - jnp.mean(x, axis=-1, keepdims=True)
     var = jnp.mean(centred * centred, axis=-1, keepdims=True)
-    n_ref[...] = (centred * lax.rsqrt(var + 1e-05)).astype(bf16)
+    normed = (centred * lax.rsqrt(var + 1e-05)).astype(bf16)
+    for h in range(2):
+        n_ref[h] = normed[:, h * SUB : (h + 1) * SUB, :]
+    copy_w.wait()
     t_ref[...] = dot(w_ref[...], n_ref[...].reshape(ROWS * RES, EMBED), 0, 1).astype(bf16)
     for s, out in enumerate(outs):
         z = lax.rem(me_ref[2] + s, Z)
+        first, odd = shared_head(z), lax.rem(z, 2)
+        lanes = pl.ds(pl.multiple_of(odd * TOKENS, TOKENS), TOKENS)
         out[0:FULL, :] = t_ref[pl.ds(chunk_rows(z)[0], FULL), :]
-        if s % 2 == 0:
-            shared = pl.multiple_of(lax.div(z, 2) * (2 * CHUNK) + FULL, FULL)
-            out[FULL:, :] = t_ref[pl.ds(shared, FULL), :]
+        for d in range(2):
+            rows = pl.ds(pl.multiple_of(first + d * HALF, HALF), HALF)
+            out[FULL:CHUNK, d * TOKENS : (d + 1) * TOKENS] = t_ref[rows, lanes]
 
 
 def key_chunks(me, x, w):
     n, *k = pl.pallas_call(
         key_kernel,
-        out_shape=(jax.ShapeDtypeStruct((ROWS, RES, EMBED), bf16),)
-        + tuple(jax.ShapeDtypeStruct((FULL * (2 - s % 2), ROWS * RES), bf16) for s in range(Z)),
-        in_specs=[SMEM, VMEM, VMEM],
-        out_specs=(VMEM,) * (Z + 1),
-        scratch_shapes=[pltpu.VMEM((EMBED, ROWS * RES), bf16)],
-        compiler_params=PARAMS,
-    )(me, x, w)
+        out_shape=(jax.ShapeDtypeStruct((2, ROWS, SUB, EMBED), bf16),)
+        + (jax.ShapeDtypeStruct((CHUNK, ROWS * RES), bf16),) * Z,
+        in_specs=[SMEM, ANY, ANY],
+        out_specs=(VMEM,) * (1 + Z),
+        scratch_shapes=[
+            pltpu.VMEM((ROWS, RES, EMBED), bf16),
+            pltpu.VMEM((EMBED, EMBED), bf16),
+            pltpu.VMEM((EMBED, ROWS * RES), bf16),
+            pltpu.SemaphoreType.DMA((2,)),
+        ],
+        compiler_params=PARAMS,
+    )(me, *in_hbm(x, w))
     return n, k
 
 
 def query_kernel(n_ref, w_ref, q_ref):
     for c in range(2):
-        n = n_ref[:, c * SUB : (c + 1) * SUB, :].reshape(ROWS * SUB, EMBED)
-        t = dot(w_ref[...], n, 0, 1).astype(bf16)
+        t = dot(w_ref[...], n_ref[c].reshape(TOKENS, EMBED), 0, 1).astype(bf16)
         for z in range(Z):
-            (a, na), _ = chunk_pieces(z)
-            b = (z // 2) * 2 * CHUNK + FULL
-            q_ref[2 * z + c, 0:FULL, :] = t[a : a + na]
+            a, b = chunk_pieces(z)[0][0], shared_head(z)
+            q_ref[2 * z + c, 0:FULL, :] = t[a : a + FULL]
             q_ref[2 * z + c, FULL:, :] = t[b : b + FULL]
 
 
 def query_chunks(n, w):
     return pl.pallas_call(
         query_kernel,
-        out_shape=jax.ShapeDtypeStruct((2 * Z, 2 * FULL, ROWS * SUB), bf16),
+        out_shape=jax.ShapeDtypeStruct((2 * Z, 2 * FULL, TOKENS), bf16),
         in_specs=[VMEM] * 2,
         out_specs=VMEM,
         compiler_params=PARAMS,
@@ -112,7 +134,10 @@
 def value_kernel(me_ref, n_ref, w_ref, *rest):
     outs, t_ref = rest[:Z], rest[Z]
     t_ref[...] = dot(w_ref[...], n_ref[...].reshape(ROWS * RES, EMBED), 0, 1).astype(bf16)
-    send_pieces(me_ref[2], t_ref, outs)
+    for s, out in enumerate(outs):
+        full, half = chunk_rows(lax.rem(me_ref[2] + s, Z))
+        out[0:FULL, :] = t_ref[pl.ds(full, FULL), :]
+        out[FULL:CHUNK, :] = t_ref[pl.ds(half, HALF), :]
 
 
 def value_chunks(me, n, w):
@@ -127,24 +152,17 @@
     )(me, n, w)
 
 
-def widen(blocks, r):
-    return jnp.concatenate([b[:, r * RES : (r + 1) * RES] for b in blocks], axis=1)
-
-
-def lay_keys(z, own, other, kf, kh):
-    def piece(ref, source, extra):
-        s = lax.rem(z - source + Z, Z)
-        first = lax.div(s, 2) * KSTEP + lax.rem(s, 2) * (2 * FULL) + extra
-        return ref[pl.ds(pl.multiple_of(first, FULL), FULL), :]
-
-    odd = lax.rem(z, 2)
+def lay_keys(me, own, other, kf, kh):
+    where = [lax.rem(me - z + Z, Z) for z in range(Z)]
     for cr, ref in enumerate((own, other)):
-        whole = [piece(ref, source, 0) for source in range(Z)]
-        shared = [piece(ref, 2 * source + odd, FULL) for source in range(Z // 2)]
         for r in range(ROWS):
-            rows = slice((cr * ROWS + r) * FULL, (cr * ROWS + r + 1) * FULL)
-            kf[rows, :] = widen(whole, r)
-            kh[rows, :] = widen(shared, r)
+            n = (cr * ROWS + r) * FULL
+            whole = [ref[z, 0:FULL, h * TOKENS + r * SUB : h * TOKENS + (r + 1) * SUB] for z in where for h in range(2)]
+            kf[n : n + FULL, :] = jnp.concatenate(whole, axis=1)
+            for d in range(2):
+                first = d * TOKENS + r * SUB
+                shared = [ref[z, FULL:CHUNK, first : first + SUB] for z in where]
+                kh[n + d * HALF : n + (d + 1) * HALF, :] = jnp.concatenate(shared, axis=1)
 
 
 def keys_kernel(me_ref, own, other, kf, kh):
@@ -163,29 +181,28 @@
 
 
 def score_kernel(me_ref, q_ref, kf0, kh0, own, other, out, qf, qh, kf1, kh1):
-    core = me_ref[1]
     lay_keys(me_ref[2], own, other, kf1, kh1)
     for cr in range(2):
-        c = jnp.bitwise_xor(core, cr)
+        c = jnp.bitwise_xor(me_ref[1], cr)
         queries = [q_ref[2 * p + c] for p in range(PEERS)]
         for r in range(ROWS):
-            rows = slice((cr * ROWS + r) * FULL, (cr * ROWS + r + 1) * FULL)
+            n = (cr * ROWS + r) * FULL
             t = jnp.concatenate([b[:, r * SUB : (r + 1) * SUB] for b in queries], axis=1)
-            qf[rows, :] = t[:FULL]
-            qh[rows, :] = t[FULL:]
+            qf[n : n + FULL, :] = t[:FULL]
+            qh[n : n + FULL, :] = t[FULL:]
     first = 0
     for a, b in ((qf, kf0), (qf, kf1), (qh, kh0), (qh, kh1)):
-        s = dot(a[...], b[...], 0, 0)
+        t = dot(a[...], b[...], 0, 0)
         for p in range(PEERS):
-            out[p, :, first : first + s.shape[1]] = s[p * SUB : (p + 1) * SUB]
-        first += s.shape[1]
+            out[p, :, first : first + t.shape[1]] = t[p * SUB : (p + 1) * SUB]
+        first += t.shape[1]
 
 
 def score(me, q, laid, own, other):
     rows = 2 * ROWS * FULL
     return pl.pallas_call(
         score_kernel,
-        out_shape=jax.ShapeDtypeStruct((PEERS, SUB, KEYS + KEYS // 2), f32),
+        out_shape=jax.ShapeDtypeStruct((PEERS, SUB, LOGITS), f32),
         in_specs=[SMEM] + [VMEM] * 5,
         out_specs=VMEM,
         scratch_shapes=[pltpu.VMEM((rows, QUERIES), bf16)] * 2 + [pltpu.VMEM(s, bf16) for s in KEY_SHAPES],
@@ -233,19 +250,20 @@
 def values_kernel(me_ref, v00, v01, v10, v11, vf, vh):
     z = me_ref[2]
     odd = lax.rem(z, 2)
+    where = [lax.rem(z - source + Z, Z) for source in range(Z)]
     for cr, refs in enumerate(((v00, v01), (v10, v11))):
-        blocks = [[ref[lax.rem(z - source + Z, Z)] for source in range(Z)] for ref in refs]
-        shared = [
-            ref[lax.rem(z - (2 * source + parity) + Z, Z), FULL:CHUNK, :]
-            for parity in (odd, 1 - odd)
+        halves = [
+            ref[i, FULL:CHUNK, pl.ds(pl.multiple_of(h * TOKENS, TOKENS), TOKENS)]
+            for h in (odd, 1 - odd)
             for ref in refs
-            for source in range(Z // 2)
+            for i in where
         ]
-        whole = [b[:FULL] for ref in blocks for b in ref]
+        whole = [ref[i, 0:FULL, h * TOKENS : (h + 1) * TOKENS] for ref in refs for i in where for h in range(2)]
         for r in range(ROWS):
             n = cr * ROWS + r
-            vf[n * FULL : (n + 1) * FULL, :] = widen(whole, r)
-            vh[n * HALF : (n + 1) * HALF, :] = widen(shared, r)
+            lanes = slice(r * SUB, (r + 1) * SUB)
+            vf[n * FULL : (n + 1) * FULL, :] = jnp.concatenate([b[:, lanes] for b in whole], axis=1)
+            vh[n * HALF : (n + 1) * HALF, :] = jnp.concatenate([b[:, lanes] for b in halves], axis=1)
 
 
 def values_laid(me, vs):
@@ -312,33 +330,33 @@
     return own, far, flip(own, "c", 2, 1), flip(far, "c", 2, 1)
 
 
-ORDER = (1, 7, 2, 6, 3, 5, 4)
-
-
-def spread(pieces):
-    got = {0: pieces[0]}
-    for s in ORDER:
-        got[s] = lax.ppermute(pieces[s], "z", [(i, (i + s) % Z) for i in range(Z)])
-    return [got[s] for s in range(Z)]
+def shift(x, s):
+    return lax.ppermute(x, "z", [(i, (i + s) % Z) for i in range(Z)])
 
 
 def local(x, wq, wk, wv, wf):
     me = jnp.stack([lax.axis_index(("y", "xh")), lax.axis_index("c"), lax.axis_index("z")])
     me = me.astype(jnp.int32)
     n, k = key_chunks(me, x, wk)
-    q = query_chunks(n, wq)
-    v = value_chunks(me, n, wv)
-    k = spread(k)
-    q, k[1] = lax.optimization_barrier((q, k[1]))
+    for s in (1, 7, 2, 6, 3, 5, 4):
+        k[s] = shift(k[s], s)
+    q, k[1], k[7], k[2], k[6] = lax.optimization_barrier((query_chunks(n, wq), k[1], k[7], k[2], k[6]))
     q = lax.all_to_all(q, ("z", "c"), 0, 0, tiled=True)
-    k00, k01, k10, k11 = gather4(jnp.concatenate(k))
-    v, scores = lax.optimization_barrier((v, score(me, q, keys_laid(me, k00, k10), k01, k11)))
+    v = list(value_chunks(me, n, wv))
+    k = jnp.stack(k)
+    k_far, v[4] = lax.optimization_barrier((flip(k, "xl", 2, 1), v[4]))
+    for s in (3, 5):
+        v[s] = shift(v[s], s)
+    scores = score(me, q, keys_laid(me, k, flip(k, "c", 2, 1)), k_far, flip(k_far, "c", 2, 1))
+    *v, scores = lax.optimization_barrier((*v, scores))
     parts = lax.all_to_all(scores, ("y", "xh"), 0, 0, tiled=True)
-    laid = values_laid(me, gather4(jnp.stack(spread(v))))
+    for s in (4, 2, 6, 1, 7):
+        v[s] = shift(v[s], s)
     full, half = total(parts)
     rows = ROWS * 2 * PEERS
     probs = softmax(1.0 / math.sqrt(DH * rows), full, half, flip(half, "z", Z, 1))
     probs = lax.all_to_all(probs, ("y", "xh"), 0, 0, tiled=True)
+    laid = values_laid(me, gather4(jnp.stack(v)))
     mixed = lax.all_to_all(mix(me, laid, probs), ("z", "c"), 0, 0, tiled=True)
     return final(mixed, wf)
 

time: 192 us -> 164 us (0.85)
  waiting for transfers between devices: 60.7 us -> 19.4 us
  starting transfers between devices: 67.9 us -> 74.7 us
  Pallas kernels: 16.5 us -> 21.7 us
    ppermute x14, waiting for transfers between devices: 37.5 us -> 6.14 us  [shift(): return lax.ppermute(x, 'z', [(i, (i + s) % Z) for i in range(Z)])]
    ppermute x7, waiting for transfers between devices: 19.3 us -> 5.35 us  [flip(): return lax.ppermute(x, axes, [(i, i ^ s) for i in range(n)])]
    ppermute x7, starting transfers between devices: 15.5 us -> 24.4 us  [flip(): return lax.ppermute(x, axes, [(i, i ^ s) for i in range(n)])]
    all_to_all x1, starting transfers between devices: 7.17 us -> 3.79 us  [local(): probs = lax.all_to_all(probs, ('y', 'xh'), 0, 0, tiled=True)]
    all_to_all x1, waiting for transfers between devices: 0.01 us -> 3.2 us  [local(): parts = lax.all_to_all(scores, ('y', 'xh'), 0, 0, tiled=True)]
    unnamed x72, local copies, waits for them, and re-layouts: 13.7 us -> 15.8 us
  transfers between devices with their start and end apart: 24 -> 24, of which waited for: 11 -> 7; matrix products, arithmetic and copies ran while one was open for 2% -> 3% of each run, Pallas kernels for 4% -> 9%
where the time goes in v10:
time: 164 us; the launch traced here: 163 us
  starting transfers between devices  74.7 us (46%)
  blocking collectives  30.8 us (19%)
  Pallas kernels  21.7 us (13%)
  waiting for transfers between devices  19.4 us (12%)
  local copies, waits for them, and re-layouts  15.8 us (10%)
    ppermute x14, starting transfers between devices, shift(): return lax.ppermute(x, 'z', [(i, (i + s) % Z) for i in range(Z)])  33.5 us
    all_to_all x1, blocking collectives, local(): mixed = lax.all_to_all(mix(me, laid, probs), ('z', 'c'), 0, 0, tiled=True)  30.8 us
    ppermute x7, starting transfers between devices, flip(): return lax.ppermute(x, axes, [(i, i ^ s) for i in range(n)])  24.4 us
    unnamed x72, local copies, waits for them, and re-layouts  15.8 us
    all_to_all x1, starting transfers between devices, local(): parts = lax.all_to_all(scores, ('y', 'xh'), 0, 0, tiled=True)  6.79 us
    all_to_all x1, starting transfers between devices, local(): q = lax.all_to_all(q, ('z', 'c'), 0, 0, tiled=True)  6.22 us
    ppermute x14, waiting for transfers between devices, shift(): return lax.ppermute(x, 'z', [(i, (i + s) % Z) for i in range(Z)])  6.14 us
    ppermute x7, waiting for transfers between devices, flip(): return lax.ppermute(x, axes, [(i, i ^ s) for i in range(n)])  5.35 us
  transfers between devices with their start and end apart: 24, of which 7 were waited for; matrix products, arithmetic and copies ran while one was open for 3% of the time, Pallas kernels for 9%

profile of v10, /device:TPU:1, one launch (start us, length us, event | category | flops | bytes accessed | tf_op | source)
XLA Modules:
  0.0 162.8 jit_solution(776304079460915164)
XLA Ops:
  0.1 3.0 %shard_map.55 = (bf16[2,8,32,768]{3,2,1,0:T(8,128)(2,1)S(1)}, bf16[96,512]{1,0:T(8,128)(2,1)S(1)}, bf16[96,512]{1,0:T(8,128)(2,1)S(1)}, bf16[96,512]{1,0:T(8,128...) custom-call(s32[3]{0:T(128)S(1)} %pad_add_fusion.me_ref, ...), custom_call_target="tpu_custom_call" | custom-call | tf_op jit(solution)/shard_map/pallas_call | solution.py:97
  3.1 2.5 %collective-permute-start.1 = (bf16[96,512]{1,0:T(8,128)(2,1)S(1)}, bf16[96,512]{1,0:T(8,128)(2,1)S(1)}, u32[]{:S(2)}, u32[]{:S(2)}) collective-permute-start(bf16[96,512]{1,0:T(8,128)(2,1)S(1)} %get-tuple-element.50), channel_id=1, source_target_pairs={{0,2},{2,4},{4,6},{6,8},{8,10},{10,12},{12,14},{14,0},{1,3},{3,5},... | collective-permute-start | bytes 294920 | tf_op jit(solution)/shard_map/ppermute | solution.py:334
  5.6 4.0 %collective-permute-start.2 = (bf16[96,512]{1,0:T(8,128)(2,1)S(1)}, bf16[96,512]{1,0:T(8,128)(2,1)S(1)}, u32[]{:S(2)}, u32[]{:S(2)}) collective-permute-start(bf16[96,512]{1,0:T(8,128)(2,1)S(1)} %get-tuple-element.51), channel_id=1, source_target_pairs={{0,14},{2,0},{4,2},{6,4},{8,6},{10,8},{12,10},{14,12},{1,15},{3,1}... | collective-permute-start | bytes 294920 | tf_op jit(solution)/shard_map/ppermute | solution.py:334
  9.6 3.6 %collective-permute-start.4 = (bf16[96,512]{1,0:T(8,128)(2,1)S(1)}, bf16[96,512]{1,0:T(8,128)(2,1)}, u32[]{:S(2)}, u32[]{:S(2)}) collective-permute-start(bf16[96,512]{1,0:T(8,128)(2,1)S(1)} %get-tuple-element.53), channel_id=1, source_target_pairs={{0,12},{2,14},{4,0},{6,2},{8,4},{10,6},{12,8},{14,10},{1,13},{3,15... | collective-permute-start | bytes 294920 | tf_op jit(solution)/shard_map/ppermute | solution.py:334
  13.5 1.8 %shard_map.57 = bf16[16,128,256]{2,1,0:T(8,128)(2,1)} custom-call(bf16[2,8,32,768]{3,2,1,0:T(8,128)(2,1)S(1)} %get-tuple-element.44.n_ref, bf16[768,768]{1,0:T(8,128)(2,1)S(1)} %copy-done), custom_call_target="tpu_custom_call" | custom-call | flops 603979776 | bytes 2752512 | tf_op jit(solution)/shard_map/pallas_call | solution.py:124
  15.4 3.6 %collective-permute-start.6 = (bf16[96,512]{1,0:T(8,128)(2,1)S(1)}, bf16[96,512]{1,0:T(8,128)(2,1)}, u32[]{:S(2)}, u32[]{:S(2)}) collective-permute-start(bf16[96,512]{1,0:T(8,128)(2,1)S(1)} %get-tuple-element.57), channel_id=1, source_target_pairs={{0,8},{2,10},{4,12},{6,14},{8,0},{10,2},{12,4},{14,6},{1,9},{3,11}... | collective-permute-start | bytes 294920 | tf_op jit(solution)/shard_map/ppermute | solution.py:334
  19.0 4.5 %collective-permute-start.7 = (bf16[96,512]{1,0:T(8,128)(2,1)S(1)}, bf16[96,512]{1,0:T(8,128)(2,1)S(1)}, u32[]{:S(2)}, u32[]{:S(2)}) collective-permute-start(bf16[96,512]{1,0:T(8,128)(2,1)S(1)} %get-tuple-element.58), channel_id=1, source_target_pairs={{0,10},{2,12},{4,14},{6,0},{8,2},{10,4},{12,6},{14,8},{1,11},{3,13... | collective-permute-start | bytes 294920 | tf_op jit(solution)/shard_map/ppermute | solution.py:334
  24.1 6.2 %all-to-all-start = ((bf16[16,128,256]{2,1,0:T(8,128)(2,1)}), bf16[16,128,256]{2,1,0:T(8,128)(2,1)S(1)}, u32[]{:S(2)}, u32[]{:S(2)}) async-start(bf16[16,128,256]{2,1,0:T(8,128)(2,1)} %shard_map.57), calls=%async_computation | async-start | bytes 2097152 | tf_op jit(solution)/shard_map/all_to_all | solution.py:344
  34.6 2.1 %shard_map.56 = (bf16[96,512]{1,0:T(8,128)(2,1)S(1)}, bf16[96,512]{1,0:T(8,128)(2,1)S(1)}, bf16[96,512]{1,0:T(8,128)(2,1)S(1)}, bf16[96,512]{1,0:T(8,128)(2,1)},...) custom-call(s32[3]{0:T(128)S(1)} %pad_add_fusion.me_ref, ...), custom_call_target="tpu_custom_call" | custom-call | flops 603979776 | bytes 2752512 | tf_op jit(solution)/shard_map/pallas_call | solution.py:144
  38.6 7.4 %collective-permute-start.10 = (bf16[8,96,512]{2,1,0:T(8,128)(2,1)S(1)}, bf16[8,96,512]{2,1,0:T(8,128)(2,1)S(1)}, u32[]{:S(2)}, u32[]{:S(2)}) collective-permute-start(bf16[8,96,512]{2,1,0:T(8,128)(2,1)S(1)} %bitcast_dynamic-update-slice_fusion.8.own), channel_id=1, source_target_pairs={{0,16},{16,0},{1,17},{17,1},{2,18},{18,2},{3,19},{19,3},{4,20},{20... | collective-permute-start | bytes 2359304 | tf_op jit(solution)/shard_map/ppermute | solution.py:325
  45.9 7.4 %collective-permute-start.11 = (bf16[8,96,512]{2,1,0:T(8,128)(2,1)S(1)}, bf16[8,96,512]{2,1,0:T(8,128)(2,1)S(1)}, u32[]{:S(2)}, u32[]{:S(2)}) collective-permute-start(bf16[8,96,512]{2,1,0:T(8,128)(2,1)S(1)} %collective-permute-done.8.own), channel_id=1, source_target_pairs={{0,16},{16,0},{1,17},{17,1},{2,18},{18,2},{3,19},{19,3},{4,20},{20... | collective-permute-start | bytes 2359304 | tf_op jit(solution)/shard_map/ppermute | solution.py:325
  53.3 3.2 %collective-permute-start = (bf16[96,512]{1,0:T(8,128)(2,1)}, bf16[96,512]{1,0:T(8,128)(2,1)}, u32[]{:S(2)}, u32[]{:S(2)}) collective-permute-start(bf16[96,512]{1,0:T(8,128)(2,1)} %get-tuple-element.48), channel_id=1, source_target_pairs={{0,6},{2,8},{4,10},{6,12},{8,14},{10,0},{12,2},{14,4},{1,7},{3,9},... | collective-permute-start | bytes 294920 | tf_op jit(solution)/shard_map/ppermute | solution.py:334
  57.8 1.8 %shard_map.58 = (bf16[1024,512]{1,0:T(8,128)(2,1)S(1)}, bf16[1024,256]{1,0:T(8,128)(2,1)S(1)}) custom-call(s32[3]{0:T(128)S(1)} %pad_add_fusion.me_ref, bf16[8,96,512]{2,1,0:T(8,128)(2,1)S(1)} %bitcast_dynamic-update-slice_fusion.8.own, bf16[8,96,512]{2,1,0:T(8,128)(2,1)S(1)} %collective-permute-done.10.other), custom_call_target="tpu_custom_call" | custom-call | bytes 6291456 | tf_op jit(solution)/shard_map/pallas_call | solution.py:173
  62.9 5.0 %shard_map.59 = f32[8,32,1536]{2,1,0:T(8,128)} custom-call(s32[3]{0:T(128)S(1)} %pad_add_fusion.me_ref, bf16[16,128,256]{2,1,0:T(8,128)(2,1)S(1)} %all-to-all-done.q_ref, bf16[1024,512]{1,0:T(8,128)(2,1)S(1)} %get-tuple-element.67.kf0, bf16[1024,256]{1,0:T(8,128)(2,1)S(1)} %get-tuple-element.68.kh0, bf16[8,96,512]{2,1,0:T(8,128)(2,1)S(1)} %copy-done.7, ...), custom_call_target="tpu_custom_call" | custom-call | tf_op jit(solution)/shard_map/pallas_call | solution.py:203
  67.9 6.8 %all-to-all-start.1 = ((f32[8,32,1536]{2,1,0:T(8,128)}), f32[8,32,1536]{2,1,0:T(8,128)S(1)}, u32[]{:S(2)}, u32[]{:S(2)}) async-start(f32[8,32,1536]{2,1,0:T(8,128)} %shard_map.59), calls=%async_computation.1 | async-start | bytes 3145728 | tf_op jit(solution)/shard_map/all_to_all | solution.py:352
  74.7 3.3 %collective-permute-start.12 = (bf16[96,512]{1,0:T(8,128)(2,1)S(1)}, bf16[96,512]{1,0:T(8,128)(2,1)S(1)}, u32[]{:S(2)}, u32[]{:S(2)}) collective-permute-start(bf16[96,512]{1,0:T(8,128)(2,1)S(1)} %copy-done.22), channel_id=1, source_target_pairs={{0,2},{2,4},{4,6},{6,8},{8,10},{10,12},{12,14},{14,0},{1,3},{3,5},... | collective-permute-start | bytes 294920 | tf_op jit(solution)/shard_map/ppermute | solution.py:334
  78.0 2.5 %collective-permute-start.14 = (bf16[96,512]{1,0:T(8,128)(2,1)S(1)}, bf16[96,512]{1,0:T(8,128)(2,1)S(1)}, u32[]{:S(2)}, u32[]{:S(2)}) collective-permute-start(bf16[96,512]{1,0:T(8,128)(2,1)S(1)} %copy-done.18), channel_id=1, source_target_pairs={{0,8},{2,10},{4,12},{6,14},{8,0},{10,2},{12,4},{14,6},{1,9},{3,11}... | collective-permute-start | bytes 294920 | tf_op jit(solution)/shard_map/ppermute | solution.py:334
  80.5 3.5 %collective-permute-start.15 = (bf16[96,512]{1,0:T(8,128)(2,1)S(1)}, bf16[96,512]{1,0:T(8,128)(2,1)S(1)}, u32[]{:S(2)}, u32[]{:S(2)}) collective-permute-start(bf16[96,512]{1,0:T(8,128)(2,1)S(1)} %copy-done.16), channel_id=1, source_target_pairs={{0,12},{2,14},{4,0},{6,2},{8,4},{10,6},{12,8},{14,10},{1,13},{3,15... | collective-permute-start | bytes 294920 | tf_op jit(solution)/shard_map/ppermute | solution.py:334
  86.1 1.9 %collective-permute-done.14 = bf16[96,512]{1,0:T(8,128)(2,1)S(1)} collective-permute-done((bf16[96,512]{1,0:T(8,128)(2,1)S(1)}, bf16[96,512]{1,0:T(8,128)(2,1)S(1)}, u32[]{:S(2)}, u32[]{:S(2)}) %collective-permute-start.14) | collective-permute-done | bytes 98336 | tf_op jit(solution)/shard_map/ppermute | solution.py:334
  88.8 4.2 %collective-permute-done.15 = bf16[96,512]{1,0:T(8,128)(2,1)S(1)} collective-permute-done((bf16[96,512]{1,0:T(8,128)(2,1)S(1)}, bf16[96,512]{1,0:T(8,128)(2,1)S(1)}, u32[]{:S(2)}, u32[]{:S(2)}) %collective-permute-start.15) | collective-permute-done | bytes 98336 | tf_op jit(solution)/shard_map/ppermute | solution.py:334
  93.5 3.2 %all-to-all-done.1.parts = f32[8,32,1536]{2,1,0:T(8,128)S(1)} async-done(((f32[8,32,1536]{2,1,0:T(8,128)}), f32[8,32,1536]{2,1,0:T(8,128)S(1)}, u32[]{:S(2)}, u32[]{:S(2)}) %all-to-all-start.1) | async-done | bytes 1572896 | tf_op jit(solution)/shard_map/all_to_all | solution.py:352
  96.8 3.3 %collective-permute-start.20 = (f32[32,512]{1,0:T(8,128)S(1)}, f32[32,512]{1,0:T(8,128)S(1)}, u32[]{:S(2)}, u32[]{:S(2)}) collective-permute-start(f32[32,512]{1,0:T(8,128)S(1)} %get-tuple-element.82.half), channel_id=1, source_target_pairs={{0,2},{2,0},{4,6},{6,4},{8,10},{10,8},{12,14},{14,12},{1,3},{3,1},... | collective-permute-start | bytes 196616 | tf_op jit(solution)/shard_map/ppermute | solution.py:325
  100.1 2.0 %collective-permute-done.20.other = f32[32,512]{1,0:T(8,128)S(1)} collective-permute-done((f32[32,512]{1,0:T(8,128)S(1)}, f32[32,512]{1,0:T(8,128)S(1)}, u32[]{:S(2)}, u32[]{:S(2)}) %collective-permute-start.20) | collective-permute-done | bytes 65568 | tf_op jit(solution)/shard_map/ppermute | solution.py:325
  103.3 3.8 %all-to-all-start.2 = ((bf16[8,2,32,1024]{3,2,1,0:T(8,128)(2,1)}), bf16[8,2,32,1024]{3,2,1,0:T(8,128)(2,1)S(1)}, u32[]{:S(2)}, u32[]{:S(2)}) async-start(bf16[8,2,32,1024]{3,2,1,0:T(8,128)(2,1)} %shard_map.62), calls=%async_computation.2 | async-start | bytes 2097152 | tf_op jit(solution)/shard_map/all_to_all | solution.py:358
  107.1 2.2 %collective-permute-start.18 = (bf16[8,96,512]{2,1,0:T(8,128)(2,1)S(1)}, bf16[8,96,512]{2,1,0:T(8,128)(2,1)S(1)}, u32[]{:S(2)}, u32[]{:S(2)}) collective-permute-start(bf16[8,96,512]{2,1,0:T(8,128)(2,1)S(1)} %bitcast_dynamic-update-slice_fusion.v00), channel_id=1, source_target_pairs={{0,16},{16,0},{1,17},{17,1},{2,18},{18,2},{3,19},{19,3},{4,20},{20... | collective-permute-start | bytes 2359304 | tf_op jit(solution)/shard_map/ppermute | solution.py:325
  109.3 2.4 %collective-permute-done.17.v01 = bf16[8,96,512]{2,1,0:T(8,128)(2,1)S(1)} collective-permute-done((bf16[8,96,512]{2,1,0:T(8,128)(2,1)S(1)}, bf16[8,96,512]{2,1,0:T(8,128)(2,1)S(1)}, u32[]{:S(2)}, u32[]{:S(2)}) %collective-permute-start.17) | collective-permute-done | bytes 786464 | tf_op jit(solution)/shard_map/ppermute | solution.py:325
  111.7 2.5 %collective-permute-start.19 = (bf16[8,96,512]{2,1,0:T(8,128)(2,1)S(1)}, bf16[8,96,512]{2,1,0:T(8,128)(2,1)S(1)}, u32[]{:S(2)}, u32[]{:S(2)}) collective-permute-start(bf16[8,96,512]{2,1,0:T(8,128)(2,1)S(1)} %collective-permute-done.17.v01), channel_id=1, source_target_pairs={{0,16},{16,0},{1,17},{17,1},{2,18},{18,2},{3,19},{19,3},{4,20},{20... | collective-permute-start | bytes 2359304 | tf_op jit(solution)/shard_map/ppermute | solution.py:325
  118.4 3.1 %shard_map.60 = (bf16[1024,1024]{1,0:T(8,128)(2,1)S(1)}, bf16[512,1024]{1,0:T(8,128)(2,1)S(1)}) custom-call(s32[3]{0:T(128)S(1)} %pad_add_fusion.me_ref, bf16[8,96,512]{2,1,0:T(8,128)(2,1)S(1)} %copy-done.5, bf16[8,96,512]{2,1,0:T(8,128)(2,1)S(1)} %copy-done.9, bf16[8,96,512]{2,1,0:T(8,128)(2,1)S(1)} %collective-permute-done.18.v10, ...), custom_call_target="tpu_custom_call" | custom-call | bytes 6291456 | tf_op jit(solution)/shard_map/pallas_call | solution.py:270
  122.5 4.7 %all-to-all-done.2.p_ref = bf16[8,2,32,1024]{3,2,1,0:T(8,128)(2,1)S(1)} async-done(((bf16[8,2,32,1024]{3,2,1,0:T(8,128)(2,1)}), bf16[8,2,32,1024]{3,2,1,0:T(8,128)(2,1)S(1)}, u32[]{:S(2)}, u32[]{:S(2)}) %all-to-all-start.2) | async-done | bytes 1048608 | tf_op jit(solution)/shard_map/all_to_all | solution.py:358
  128.4 1.9 %shard_map.63 = bf16[16,96,256]{2,1,0:T(8,128)(2,1)S(1)} custom-call(s32[3]{0:T(128)S(1)} %pad_add_fusion.me_ref, bf16[1024,1024]{1,0:T(8,128)(2,1)S(1)} %get-tuple-element.78.vf, bf16[512,1024]{1,0:T(8,128)(2,1)S(1)} %copy-done.3, bf16[8,2,32,1024]{3,2,1,0:T(8,128)(2,1)S(1)} %all-to-all-done.2.p_ref), custom_call_target="tpu_custom_call" | custom-call | tf_op jit(solution)/shard_map/pallas_call | solution.py:294
  130.3 30.8 %all_to_all.20.m_ref = bf16[16,96,256]{2,1,0:T(8,128)(2,1)S(1)} all-to-all(bf16[16,96,256]{2,1,0:T(8,128)(2,1)S(1)} %shard_map.63), channel_id=1, replica_groups=mesh['y'=4,'xh'=2,'c'=2,'z'=8,'xl'=2] {'z','c'}, dimensions={0} | all-to-all | bytes 1572864 | tf_op jit(solution)/shard_map/all_to_all | solution.py:360
  161.1 1.7 %shard_map.64 = bf16[8,64,768]{2,1,0:T(8,128)(2,1)} custom-call(bf16[16,96,256]{2,1,0:T(8,128)(2,1)S(1)} %all_to_all.20.m_ref, bf16[768,768]{1,0:T(8,128)(2,1)S(1)} %copy-done.1), custom_call_target="tpu_custom_call" | custom-call | tf_op jit(solution)/shard_map/pallas_call | solution.py:314
  (102 shorter events, 22.7 us)
Async XLA Ops:
  0.0 13.5 %copy-start = (bf16[768,768]{1,0:T(8,128)(2,1)S(1)}, bf16[768,768]{1,0:T(8,128)(2,1)}, u32[]{:S(2)}) copy-start(bf16[768,768]{1,0:T(8,128)(2,1)} %w_ref.4) | copy-start | bytes 3538948
  3.1 12.3 %collective-permute-start.1 = (bf16[96,512]{1,0:T(8,128)(2,1)S(1)}, bf16[96,512]{1,0:T(8,128)(2,1)S(1)}, u32[]{:S(2)}, u32[]{:S(2)}) collective-permute-start(bf16[96,512]{1,0:T(8,128)(2,1)S(1)} %get-tuple-element.50), channel_id=1, source_target_pairs={{0,2},{2,4},{4,6},{6,8},{8,10},{10,12},{12,14},{14,0},{1,3},{3,5},... | collective-permute-start | bytes 294920 | tf_op jit(solution)/shard_map/ppermute | solution.py:334
  5.6 13.4 %collective-permute-start.2 = (bf16[96,512]{1,0:T(8,128)(2,1)S(1)}, bf16[96,512]{1,0:T(8,128)(2,1)S(1)}, u32[]{:S(2)}, u32[]{:S(2)}) collective-permute-start(bf16[96,512]{1,0:T(8,128)(2,1)S(1)} %get-tuple-element.51), channel_id=1, source_target_pairs={{0,14},{2,0},{4,2},{6,4},{8,6},{10,8},{12,10},{14,12},{1,15},{3,1}... | collective-permute-start | bytes 294920 | tf_op jit(solution)/shard_map/ppermute | solution.py:334
  9.6 13.8 %collective-permute-start.3 = (bf16[96,512]{1,0:T(8,128)(2,1)S(1)}, bf16[96,512]{1,0:T(8,128)(2,1)S(1)}, u32[]{:S(2)}, u32[]{:S(2)}) collective-permute-start(bf16[96,512]{1,0:T(8,128)(2,1)S(1)} %get-tuple-element.52), channel_id=1, source_target_pairs={{0,4},{2,6},{4,8},{6,10},{8,12},{10,14},{12,0},{14,2},{1,5},{3,7},... | collective-permute-start | bytes 294920 | tf_op jit(solution)/shard_map/ppermute | solution.py:334
  9.6 14.5 %collective-permute-start.4 = (bf16[96,512]{1,0:T(8,128)(2,1)S(1)}, bf16[96,512]{1,0:T(8,128)(2,1)}, u32[]{:S(2)}, u32[]{:S(2)}) collective-permute-start(bf16[96,512]{1,0:T(8,128)(2,1)S(1)} %get-tuple-element.53), channel_id=1, source_target_pairs={{0,12},{2,14},{4,0},{6,2},{8,4},{10,6},{12,8},{14,10},{1,13},{3,15... | collective-permute-start | bytes 294920 | tf_op jit(solution)/shard_map/ppermute | solution.py:334
  13.2 17.2 %collective-permute-start.5 = (bf16[96,512]{1,0:T(8,128)(2,1)S(1)}, bf16[96,512]{1,0:T(8,128)(2,1)}, u32[]{:S(2)}, u32[]{:S(2)}) collective-permute-start(bf16[96,512]{1,0:T(8,128)(2,1)S(1)} %get-tuple-element.56), channel_id=1, source_target_pairs={{0,6},{2,8},{4,10},{6,12},{8,14},{10,0},{12,2},{14,4},{1,7},{3,9},... | collective-permute-start | bytes 294920 | tf_op jit(solution)/shard_map/ppermute | solution.py:334
  15.4 16.0 %collective-permute-start.6 = (bf16[96,512]{1,0:T(8,128)(2,1)S(1)}, bf16[96,512]{1,0:T(8,128)(2,1)}, u32[]{:S(2)}, u32[]{:S(2)}) collective-permute-start(bf16[96,512]{1,0:T(8,128)(2,1)S(1)} %get-tuple-element.57), channel_id=1, source_target_pairs={{0,8},{2,10},{4,12},{6,14},{8,0},{10,2},{12,4},{14,6},{1,9},{3,11}... | collective-permute-start | bytes 294920 | tf_op jit(solution)/shard_map/ppermute | solution.py:334
  19.0 13.3 %collective-permute-start.7 = (bf16[96,512]{1,0:T(8,128)(2,1)S(1)}, bf16[96,512]{1,0:T(8,128)(2,1)S(1)}, u32[]{:S(2)}, u32[]{:S(2)}) collective-permute-start(bf16[96,512]{1,0:T(8,128)(2,1)S(1)} %get-tuple-element.58), channel_id=1, source_target_pairs={{0,10},{2,12},{4,14},{6,0},{8,2},{10,4},{12,6},{14,8},{1,11},{3,13... | collective-permute-start | bytes 294920 | tf_op jit(solution)/shard_map/ppermute | solution.py:334
  24.1 36.5 %all-to-all-start = ((bf16[16,128,256]{2,1,0:T(8,128)(2,1)}), bf16[16,128,256]{2,1,0:T(8,128)(2,1)S(1)}, u32[]{:S(2)}, u32[]{:S(2)}) async-start(bf16[16,128,256]{2,1,0:T(8,128)(2,1)} %shard_map.57), calls=%async_computation | async-start | bytes 2097152 | tf_op jit(solution)/shard_map/all_to_all | solution.py:344
  33.3 12.7 %collective-permute-start.8 = (bf16[8,96,512]{2,1,0:T(8,128)(2,1)S(1)}, bf16[8,96,512]{2,1,0:T(8,128)(2,1)S(1)}, u32[]{:S(2)}, u32[]{:S(2)}) collective-permute-start(bf16[8,96,512]{2,1,0:T(8,128)(2,1)S(1)} %bitcast_dynamic-update-slice_fusion.8.own), channel_id=1, source_target_pairs={{0,1},{1,0},{2,3},{3,2},{4,5},{5,4},{6,7},{7,6},{8,9},{9,8},{10,11... | collective-permute-start | bytes 2359304 | tf_op jit(solution)/shard_map/ppermute | solution.py:325
  38.6 21.1 %copy-start.17 = (bf16[96,512]{1,0:T(8,128)(2,1)}, bf16[96,512]{1,0:T(8,128)(2,1)S(1)}, u32[]{:S(2)}) copy-start(bf16[96,512]{1,0:T(8,128)(2,1)S(1)} %get-tuple-element.74) | copy-start | bytes 294916
  38.6 21.1 %copy-start.19 = (bf16[96,512]{1,0:T(8,128)(2,1)}, bf16[96,512]{1,0:T(8,128)(2,1)S(1)}, u32[]{:S(2)}) copy-start(bf16[96,512]{1,0:T(8,128)(2,1)S(1)} %get-tuple-element.72) | copy-start | bytes 294916
  38.6 19.3 %collective-permute-start.10 = (bf16[8,96,512]{2,1,0:T(8,128)(2,1)S(1)}, bf16[8,96,512]{2,1,0:T(8,128)(2,1)S(1)}, u32[]{:S(2)}, u32[]{:S(2)}) collective-permute-start(bf16[8,96,512]{2,1,0:T(8,128)(2,1)S(1)} %bitcast_dynamic-update-slice_fusion.8.own), channel_id=1, source_target_pairs={{0,16},{16,0},{1,17},{17,1},{2,18},{18,2},{3,19},{19,3},{4,20},{20... | collective-permute-start | bytes 2359304 | tf_op jit(solution)/shard_map/ppermute | solution.py:325
  45.9 13.8 %copy-start.6 = (bf16[8,96,512]{2,1,0:T(8,128)(2,1)}, bf16[8,96,512]{2,1,0:T(8,128)(2,1)S(1)}, u32[]{:S(2)}) copy-start(bf16[8,96,512]{2,1,0:T(8,128)(2,1)S(1)} %collective-permute-done.8.own) | copy-start | bytes 2359300
  45.9 13.8 %collective-permute-start.11 = (bf16[8,96,512]{2,1,0:T(8,128)(2,1)S(1)}, bf16[8,96,512]{2,1,0:T(8,128)(2,1)S(1)}, u32[]{:S(2)}, u32[]{:S(2)}) collective-permute-start(bf16[8,96,512]{2,1,0:T(8,128)(2,1)S(1)} %collective-permute-done.8.own), channel_id=1, source_target_pairs={{0,16},{16,0},{1,17},{17,1},{2,18},{18,2},{3,19},{19,3},{4,20},{20... | collective-permute-start | bytes 2359304 | tf_op jit(solution)/shard_map/ppermute | solution.py:325
  53.3 14.5 %collective-permute-start = (bf16[96,512]{1,0:T(8,128)(2,1)}, bf16[96,512]{1,0:T(8,128)(2,1)}, u32[]{:S(2)}, u32[]{:S(2)}) collective-permute-start(bf16[96,512]{1,0:T(8,128)(2,1)} %get-tuple-element.48), channel_id=1, source_target_pairs={{0,6},{2,8},{4,10},{6,12},{8,14},{10,0},{12,2},{14,4},{1,7},{3,9},... | collective-permute-start | bytes 294920 | tf_op jit(solution)/shard_map/ppermute | solution.py:334
  56.5 11.3 %collective-permute-start.9 = (bf16[96,512]{1,0:T(8,128)(2,1)}, bf16[96,512]{1,0:T(8,128)(2,1)}, u32[]{:S(2)}, u32[]{:S(2)}) collective-permute-start(bf16[96,512]{1,0:T(8,128)(2,1)} %get-tuple-element.63), channel_id=1, source_target_pairs={{0,10},{2,12},{4,14},{6,0},{8,2},{10,4},{12,6},{14,8},{1,11},{3,13... | collective-permute-start | bytes 294920 | tf_op jit(solution)/shard_map/ppermute | solution.py:334
  67.9 12.7 %copy-start.16 = (bf16[96,512]{1,0:T(8,128)(2,1)S(1)}, bf16[96,512]{1,0:T(8,128)(2,1)}, u32[]{:S(2)}) copy-start(bf16[96,512]{1,0:T(8,128)(2,1)} %copy-done.15) | copy-start | bytes 294916
  67.9 16.1 %copy-start.14 = (bf16[96,512]{1,0:T(8,128)(2,1)S(1)}, bf16[96,512]{1,0:T(8,128)(2,1)}, u32[]{:S(2)}) copy-start(bf16[96,512]{1,0:T(8,128)(2,1)} %copy-done.13) | copy-start | bytes 294916
  67.9 28.8 %all-to-all-start.1 = ((f32[8,32,1536]{2,1,0:T(8,128)}), f32[8,32,1536]{2,1,0:T(8,128)S(1)}, u32[]{:S(2)}, u32[]{:S(2)}) async-start(f32[8,32,1536]{2,1,0:T(8,128)} %shard_map.59), calls=%async_computation.1 | async-start | bytes 3145728 | tf_op jit(solution)/shard_map/all_to_all | solution.py:352
  74.7 10.4 %collective-permute-start.12 = (bf16[96,512]{1,0:T(8,128)(2,1)S(1)}, bf16[96,512]{1,0:T(8,128)(2,1)S(1)}, u32[]{:S(2)}, u32[]{:S(2)}) collective-permute-start(bf16[96,512]{1,0:T(8,128)(2,1)S(1)} %copy-done.22), channel_id=1, source_target_pairs={{0,2},{2,4},{4,6},{6,8},{8,10},{10,12},{12,14},{14,0},{1,3},{3,5},... | collective-permute-start | bytes 294920 | tf_op jit(solution)/shard_map/ppermute | solution.py:334
  78.0 7.1 %collective-permute-start.13 = (bf16[96,512]{1,0:T(8,128)(2,1)S(1)}, bf16[96,512]{1,0:T(8,128)(2,1)S(1)}, u32[]{:S(2)}, u32[]{:S(2)}) collective-permute-start(bf16[96,512]{1,0:T(8,128)(2,1)S(1)} %copy-done.20), channel_id=1, source_target_pairs={{0,4},{2,6},{4,8},{6,10},{8,12},{10,14},{12,0},{14,2},{1,5},{3,7},... | collective-permute-start | bytes 294920 | tf_op jit(solution)/shard_map/ppermute | solution.py:334
  78.0 9.9 %collective-permute-start.14 = (bf16[96,512]{1,0:T(8,128)(2,1)S(1)}, bf16[96,512]{1,0:T(8,128)(2,1)S(1)}, u32[]{:S(2)}, u32[]{:S(2)}) collective-permute-start(bf16[96,512]{1,0:T(8,128)(2,1)S(1)} %copy-done.18), channel_id=1, source_target_pairs={{0,8},{2,10},{4,12},{6,14},{8,0},{10,2},{12,4},{14,6},{1,9},{3,11}... | collective-permute-start | bytes 294920 | tf_op jit(solution)/shard_map/ppermute | solution.py:334
  80.5 12.6 %collective-permute-start.15 = (bf16[96,512]{1,0:T(8,128)(2,1)S(1)}, bf16[96,512]{1,0:T(8,128)(2,1)S(1)}, u32[]{:S(2)}, u32[]{:S(2)}) collective-permute-start(bf16[96,512]{1,0:T(8,128)(2,1)S(1)} %copy-done.16), channel_id=1, source_target_pairs={{0,12},{2,14},{4,0},{6,2},{8,4},{10,6},{12,8},{14,10},{1,13},{3,15... | collective-permute-start | bytes 294920 | tf_op jit(solution)/shard_map/ppermute | solution.py:334
  84.0 9.1 %collective-permute-start.16 = (bf16[96,512]{1,0:T(8,128)(2,1)S(1)}, bf16[96,512]{1,0:T(8,128)(2,1)S(1)}, u32[]{:S(2)}, u32[]{:S(2)}) collective-permute-start(bf16[96,512]{1,0:T(8,128)(2,1)S(1)} %copy-done.14), channel_id=1, source_target_pairs={{0,14},{2,0},{4,2},{6,4},{8,6},{10,8},{12,10},{14,12},{1,15},{3,1}... | collective-permute-start | bytes 294920 | tf_op jit(solution)/shard_map/ppermute | solution.py:334
  93.1 14.0 %copy-start.4 = (bf16[8,96,512]{2,1,0:T(8,128)(2,1)}, bf16[8,96,512]{2,1,0:T(8,128)(2,1)S(1)}, u32[]{:S(2)}) copy-start(bf16[8,96,512]{2,1,0:T(8,128)(2,1)S(1)} %bitcast_dynamic-update-slice_fusion.v00) | copy-start | bytes 2359300
  93.1 18.6 %collective-permute-start.17 = (bf16[8,96,512]{2,1,0:T(8,128)(2,1)S(1)}, bf16[8,96,512]{2,1,0:T(8,128)(2,1)S(1)}, u32[]{:S(2)}, u32[]{:S(2)}) collective-permute-start(bf16[8,96,512]{2,1,0:T(8,128)(2,1)S(1)} %bitcast_dynamic-update-slice_fusion.v00), channel_id=1, source_target_pairs={{0,1},{1,0},{2,3},{3,2},{4,5},{5,4},{6,7},{7,6},{8,9},{9,8},{10,11... | collective-permute-start | bytes 2359304 | tf_op jit(solution)/shard_map/ppermute | solution.py:325
  96.8 5.2 %collective-permute-start.20 = (f32[32,512]{1,0:T(8,128)S(1)}, f32[32,512]{1,0:T(8,128)S(1)}, u32[]{:S(2)}, u32[]{:S(2)}) collective-permute-start(f32[32,512]{1,0:T(8,128)S(1)} %get-tuple-element.82.half), channel_id=1, source_target_pairs={{0,2},{2,0},{4,6},{6,4},{8,10},{10,8},{12,14},{14,12},{1,3},{3,1},... | collective-permute-start | bytes 196616 | tf_op jit(solution)/shard_map/ppermute | solution.py:325
  103.3 23.8 %all-to-all-start.2 = ((bf16[8,2,32,1024]{3,2,1,0:T(8,128)(2,1)}), bf16[8,2,32,1024]{3,2,1,0:T(8,128)(2,1)S(1)}, u32[]{:S(2)}, u32[]{:S(2)}) async-start(bf16[8,2,32,1024]{3,2,1,0:T(8,128)(2,1)} %shard_map.62), calls=%async_computation.2 | async-start | bytes 2097152 | tf_op jit(solution)/shard_map/all_to_all | solution.py:358
  107.1 8.0 %collective-permute-start.18 = (bf16[8,96,512]{2,1,0:T(8,128)(2,1)S(1)}, bf16[8,96,512]{2,1,0:T(8,128)(2,1)S(1)}, u32[]{:S(2)}, u32[]{:S(2)}) collective-permute-start(bf16[8,96,512]{2,1,0:T(8,128)(2,1)S(1)} %bitcast_dynamic-update-slice_fusion.v00), channel_id=1, source_target_pairs={{0,16},{16,0},{1,17},{17,1},{2,18},{18,2},{3,19},{19,3},{4,20},{20... | collective-permute-start | bytes 2359304 | tf_op jit(solution)/shard_map/ppermute | solution.py:325
  111.7 4.4 %collective-permute-start.19 = (bf16[8,96,512]{2,1,0:T(8,128)(2,1)S(1)}, bf16[8,96,512]{2,1,0:T(8,128)(2,1)S(1)}, u32[]{:S(2)}, u32[]{:S(2)}) collective-permute-start(bf16[8,96,512]{2,1,0:T(8,128)(2,1)S(1)} %collective-permute-done.17.v01), channel_id=1, source_target_pairs={{0,16},{16,0},{1,17},{17,1},{2,18},{18,2},{3,19},{19,3},{4,20},{20... | collective-permute-start | bytes 2359304 | tf_op jit(solution)/shard_map/ppermute | solution.py:325
  130.3 30.8 %copy-start.1 = (bf16[768,768]{1,0:T(8,128)(2,1)S(1)}, bf16[768,768]{1,0:T(8,128)(2,1)}, u32[]{:S(2)}) copy-start(bf16[768,768]{1,0:T(8,128)(2,1)} %w_ref.5) | copy-start | bytes 3538948
  (21 other events, 76.6 us)

commit v11 on v10

--- a/solution.py
+++ b/solution.py
@@ -180,8 +180,14 @@
     )(me, own, other)
 
 
-def score_kernel(me_ref, q_ref, kf0, kh0, own, other, out, qf, qh, kf1, kh1):
+def score_kernel(me_ref, q_hbm, kf_hbm, kh_hbm, own_hbm, other_hbm, out, qf, qh, kf1, kh1, *rest):
+    own, other, q_ref, kf0, kh0, sems = rest
+    copies = fetches((own_hbm, other_hbm, q_hbm, kf_hbm, kh_hbm), rest[:5], sems)
+    for copy in copies[:2]:
+        copy.wait()
     lay_keys(me_ref[2], own, other, kf1, kh1)
+    for copy in copies[2:]:
+        copy.wait()
     for cr in range(2):
         c = jnp.bitwise_xor(me_ref[1], cr)
         queries = [q_ref[2 * p + c] for p in range(PEERS)]
@@ -203,11 +209,14 @@
     return pl.pallas_call(
         score_kernel,
         out_shape=jax.ShapeDtypeStruct((PEERS, SUB, LOGITS), f32),
-        in_specs=[SMEM] + [VMEM] * 5,
-        out_specs=VMEM,
-        scratch_shapes=[pltpu.VMEM((rows, QUERIES), bf16)] * 2 + [pltpu.VMEM(s, bf16) for s in KEY_SHAPES],
-        compiler_params=PARAMS,
-    )(me, q, *laid, own, other)
+        in_specs=[SMEM] + [ANY] * 5,
+        out_specs=VMEM,
+        scratch_shapes=[pltpu.VMEM((rows, QUERIES), bf16)] * 2
+        + [pltpu.VMEM(s, bf16) for s in KEY_SHAPES]
+        + [pltpu.VMEM(a.shape, bf16) for a in (own, other, q, *laid)]
+        + [pltpu.SemaphoreType.DMA((5,))],
+        compiler_params=PARAMS,
+    )(me, *in_hbm(q), *laid, *in_hbm(own), other)
 
 
 def total_kernel(parts, full, half):
@@ -247,7 +256,10 @@
     )(full, half, other)
 
 
-def values_kernel(me_ref, v00, v01, v10, v11, vf, vh):
+def values_kernel(me_ref, *refs):
+    (vf, vh), (v00, v01, v10, v11), sems = refs[4:6], refs[6:10], refs[10]
+    for copy in fetches(refs[:4], refs[6:10], sems):
+        copy.wait()
     z = me_ref[2]
     odd = lax.rem(z, 2)
     where = [lax.rem(z - source + Z, Z) for source in range(Z)]
@@ -270,11 +282,12 @@
     return pl.pallas_call(
         values_kernel,
         out_shape=tuple(jax.ShapeDtypeStruct((2 * ROWS * n, KEYS), bf16) for n in (FULL, HALF)),
-        in_specs=[SMEM] + [VMEM] * 4,
+        in_specs=[SMEM] + [ANY] * 4,
         out_specs=(VMEM,) * 2,
+        scratch_shapes=[pltpu.VMEM(v.shape, bf16) for v in vs] + [pltpu.SemaphoreType.DMA((4,))],
         compiler_params=PARAMS,
         cost_estimate=LAYOUT,
-    )(me, *vs)
+    )(me, *in_hbm(*vs[:2]), *vs[2:])
 
 
 def mix_kernel(me_ref, vf, vh, p_ref, o_ref):
@@ -344,10 +357,11 @@
     q = lax.all_to_all(q, ("z", "c"), 0, 0, tiled=True)
     v = list(value_chunks(me, n, wv))
     k = jnp.stack(k)
-    k_far, v[4] = lax.optimization_barrier((flip(k, "xl", 2, 1), v[4]))
+    near, shared = keys_laid(me, k, flip(k, "c", 2, 1))
+    k_far, v[4], shared = lax.optimization_barrier((flip(k, "xl", 2, 1), v[4], shared))
     for s in (3, 5):
         v[s] = shift(v[s], s)
-    scores = score(me, q, keys_laid(me, k, flip(k, "c", 2, 1)), k_far, flip(k_far, "c", 2, 1))
+    scores = score(me, q, (near, shared), k_far, flip(k_far, "c", 2, 1))
     *v, scores = lax.optimization_barrier((*v, scores))
     parts = lax.all_to_all(scores, ("y", "xh"), 0, 0, tiled=True)
     for s in (4, 2, 6, 1, 7):

time: 164 us -> 165 us (level)
  waiting for transfers between devices: 19.4 us -> 37.4 us
  local copies, waits for them, and re-layouts: 15.8 us -> 3.33 us
  starting transfers between devices: 74.7 us -> 69.1 us
    ppermute x7, waiting for transfers between devices: 5.35 us -> 20.9 us  [flip(): return lax.ppermute(x, axes, [(i, i ^ s) for i in range(n)])]
    unnamed x72 -> x30, local copies, waits for them, and re-layouts: 15.8 us -> 3.32 us
    ppermute x7, starting transfers between devices: 24.4 us -> 18.9 us  [flip(): return lax.ppermute(x, axes, [(i, i ^ s) for i in range(n)])]
  transfers between devices with their start and end apart: 24 -> 24, of which waited for: 7 -> 9; matrix products, arithmetic and copies ran while one was open for 3% -> 1% of each run, Pallas kernels for 9% -> 10%
where the time goes in v11:
time: 165 us; the launch traced here: 164 us
  starting transfers between devices  69.1 us (42%)
  waiting for transfers between devices  37.4 us (23%)
  blocking collectives  31 us (19%)
  Pallas kernels  23.3 us (14%)
  local copies, waits for them, and re-layouts  3.33 us (2%)
    ppermute x14, starting transfers between devices, shift(): return lax.ppermute(x, 'z', [(i, (i + s) % Z) for i in range(Z)])  33.2 us
    all_to_all x1, blocking collectives, local(): mixed = lax.all_to_all(mix(me, laid, probs), ('z', 'c'), 0, 0, tiled=True)  31 us
    ppermute x7, waiting for transfers between devices, flip(): return lax.ppermute(x, axes, [(i, i ^ s) for i in range(n)])  20.9 us
    ppermute x7, starting transfers between devices, flip(): return lax.ppermute(x, axes, [(i, i ^ s) for i in range(n)])  18.9 us
    ppermute x14, waiting for transfers between devices, shift(): return lax.ppermute(x, 'z', [(i, (i + s) % Z) for i in range(Z)])  7.69 us
    all_to_all x1, starting transfers between devices, local(): q = lax.all_to_all(q, ('z', 'c'), 0, 0, tiled=True)  6.69 us
    all_to_all x1, starting transfers between devices, local(): parts = lax.all_to_all(scores, ('y', 'xh'), 0, 0, tiled=True)  6.66 us
    pallas_call x1, Pallas kernels, score(): pl.pallas_call(score_kernel, out_shape=jax.ShapeDtypeStruct((PEERS, SUB,...  5.93 us
  transfers between devices with their start and end apart: 24, of which 9 were waited for; matrix products, arithmetic and copies ran while one was open for 1% of the time, Pallas kernels for 10%

profile of v11, /device:TPU:1, one launch (start us, length us, event | category | flops | bytes accessed | tf_op | source)
XLA Modules:
  0.0 164.5 jit_solution(2355142182263036198)
XLA Ops:
  0.1 3.0 %shard_map.55 = (bf16[2,8,32,768]{3,2,1,0:T(8,128)(2,1)S(1)}, bf16[96,512]{1,0:T(8,128)(2,1)S(1)}, bf16[96,512]{1,0:T(8,128)(2,1)S(1)}, bf16[96,512]{1,0:T(8,128...) custom-call(s32[3]{0:T(128)S(1)} %pad_add_fusion.me_ref, ...), custom_call_target="tpu_custom_call" | custom-call | tf_op jit(solution)/shard_map/pallas_call | solution.py:97
  3.1 2.5 %collective-permute-start.1 = (bf16[96,512]{1,0:T(8,128)(2,1)S(1)}, bf16[96,512]{1,0:T(8,128)(2,1)S(1)}, u32[]{:S(2)}, u32[]{:S(2)}) collective-permute-start(bf16[96,512]{1,0:T(8,128)(2,1)S(1)} %get-tuple-element.51), channel_id=1, source_target_pairs={{0,2},{2,4},{4,6},{6,8},{8,10},{10,12},{12,14},{14,0},{1,3},{3,5},... | collective-permute-start | bytes 294920 | tf_op jit(solution)/shard_map/ppermute | solution.py:347
  5.6 4.0 %collective-permute-start.2 = (bf16[96,512]{1,0:T(8,128)(2,1)S(1)}, bf16[96,512]{1,0:T(8,128)(2,1)S(1)}, u32[]{:S(2)}, u32[]{:S(2)}) collective-permute-start(bf16[96,512]{1,0:T(8,128)(2,1)S(1)} %get-tuple-element.52), channel_id=1, source_target_pairs={{0,14},{2,0},{4,2},{6,4},{8,6},{10,8},{12,10},{14,12},{1,15},{3,1}... | collective-permute-start | bytes 294920 | tf_op jit(solution)/shard_map/ppermute | solution.py:347
  9.6 3.6 %collective-permute-start.4 = (bf16[96,512]{1,0:T(8,128)(2,1)S(1)}, bf16[96,512]{1,0:T(8,128)(2,1)S(1)}, u32[]{:S(2)}, u32[]{:S(2)}) collective-permute-start(bf16[96,512]{1,0:T(8,128)(2,1)S(1)} %get-tuple-element.54), channel_id=1, source_target_pairs={{0,12},{2,14},{4,0},{6,2},{8,4},{10,6},{12,8},{14,10},{1,13},{3,15... | collective-permute-start | bytes 294920 | tf_op jit(solution)/shard_map/ppermute | solution.py:347
  13.5 1.8 %shard_map.57 = bf16[16,128,256]{2,1,0:T(8,128)(2,1)} custom-call(bf16[2,8,32,768]{3,2,1,0:T(8,128)(2,1)S(1)} %get-tuple-element.45.n_ref, bf16[768,768]{1,0:T(8,128)(2,1)S(1)} %copy-done), custom_call_target="tpu_custom_call" | custom-call | flops 603979776 | bytes 2752512 | tf_op jit(solution)/shard_map/pallas_call | solution.py:124
  15.4 3.6 %collective-permute-start.6 = (bf16[96,512]{1,0:T(8,128)(2,1)S(1)}, bf16[96,512]{1,0:T(8,128)(2,1)S(1)}, u32[]{:S(2)}, u32[]{:S(2)}) collective-permute-start(bf16[96,512]{1,0:T(8,128)(2,1)S(1)} %get-tuple-element.58), channel_id=1, source_target_pairs={{0,8},{2,10},{4,12},{6,14},{8,0},{10,2},{12,4},{14,6},{1,9},{3,11}... | collective-permute-start | bytes 294920 | tf_op jit(solution)/shard_map/ppermute | solution.py:347
  19.0 4.5 %collective-permute-start.7 = (bf16[96,512]{1,0:T(8,128)(2,1)S(1)}, bf16[96,512]{1,0:T(8,128)(2,1)S(1)}, u32[]{:S(2)}, u32[]{:S(2)}) collective-permute-start(bf16[96,512]{1,0:T(8,128)(2,1)S(1)} %get-tuple-element.59), channel_id=1, source_target_pairs={{0,10},{2,12},{4,14},{6,0},{8,2},{10,4},{12,6},{14,8},{1,11},{3,13... | collective-permute-start | bytes 294920 | tf_op jit(solution)/shard_map/ppermute | solution.py:347
  23.4 6.7 %all-to-all-start = ((bf16[16,128,256]{2,1,0:T(8,128)(2,1)}), bf16[16,128,256]{2,1,0:T(8,128)(2,1)}, u32[]{:S(2)}, u32[]{:S(2)}) async-start(bf16[16,128,256]{2,1,0:T(8,128)(2,1)} %shard_map.57), calls=%async_computation | async-start | bytes 2097152 | tf_op jit(solution)/shard_map/all_to_all | solution.py:357
  31.3 8.3 %collective-permute-start.9 = (bf16[8,96,512]{2,1,0:T(8,128)(2,1)S(1)}, bf16[8,96,512]{2,1,0:T(8,128)(2,1)S(1)}, u32[]{:S(2)}, u32[]{:S(2)}) collective-permute-start(bf16[8,96,512]{2,1,0:T(8,128)(2,1)S(1)} %bitcast_dynamic-update-slice_fusion.8.own), channel_id=1, source_target_pairs={{0,16},{16,0},{1,17},{17,1},{2,18},{18,2},{3,19},{19,3},{4,20},{20... | collective-permute-start | bytes 2359304 | tf_op jit(solution)/shard_map/ppermute | solution.py:338
  39.6 1.2 collective-permute-start.8
  40.8 1.4 shard_map.56
  42.2 1.8 %shard_map.58 = (bf16[1024,512]{1,0:T(8,128)(2,1)S(1)}, bf16[1024,256]{1,0:T(8,128)(2,1)S(1)}) custom-call(s32[3]{0:T(128)S(1)} %pad_add_fusion.me_ref, bf16[8,96,512]{2,1,0:T(8,128)(2,1)S(1)} %bitcast_dynamic-update-slice_fusion.8.own, bf16[8,96,512]{2,1,0:T(8,128)(2,1)S(1)} %collective-permute-done.9.other), custom_call_target="tpu_custom_call" | custom-call | bytes 6291456 | tf_op jit(solution)/shard_map/pallas_call | solution.py:173
  44.0 14.6 %collective-permute-done.8.own_hbm = bf16[8,96,512]{2,1,0:T(8,128)(2,1)S(1)} collective-permute-done((bf16[8,96,512]{2,1,0:T(8,128)(2,1)S(1)}, bf16[8,96,512]{2,1,0:T(8,128)(2,1)S(1)}, u32[]{:S(2)}, u32[]{:S(2)}) %collective-permute-start.8) | collective-permute-done | bytes 786464 | tf_op jit(solution)/shard_map/ppermute | solution.py:338
  59.5 5.4 %collective-permute-start.10 = (bf16[96,512]{1,0:T(8,128)(2,1)S(1)}, bf16[96,512]{1,0:T(8,128)(2,1)S(1)}, u32[]{:S(2)}, u32[]{:S(2)}) collective-permute-start(bf16[96,512]{1,0:T(8,128)(2,1)S(1)} %get-tuple-element.65), channel_id=1, source_target_pairs={{0,10},{2,12},{4,14},{6,0},{8,2},{10,4},{12,6},{14,8},{1,11},{3,13... | collective-permute-start | bytes 294920 | tf_op jit(solution)/shard_map/ppermute | solution.py:347
  65.0 5.9 %shard_map.59 = f32[8,32,1536]{2,1,0:T(8,128)} custom-call(s32[3]{0:T(128)S(1)} %pad_add_fusion.me_ref, bf16[16,128,256]{2,1,0:T(8,128)(2,1)} %all-to-all-done.q_hbm, bf16[1024,512]{1,0:T(8,128)(2,1)S(1)} %get-tuple-element.69.kf_hbm, bf16[1024,256]{1,0:T(8,128)(2,1)S(1)} %get-tuple-element.70.kh_hbm, bf16[8,96,512]{2,1,0:T(8,128)(2,1)} %copy-done.7, ...), custom_call_target="tpu_custom_call" | custom-call | tf_op jit(solution)/shard_map/pallas_call | solution.py:209
  70.9 6.7 %all-to-all-start.1 = ((f32[8,32,1536]{2,1,0:T(8,128)}), f32[8,32,1536]{2,1,0:T(8,128)S(1)}, u32[]{:S(2)}, u32[]{:S(2)}) async-start(f32[8,32,1536]{2,1,0:T(8,128)} %shard_map.59), calls=%async_computation.1 | async-start | bytes 3145728 | tf_op jit(solution)/shard_map/all_to_all | solution.py:366
  77.6 2.4 %collective-permute-start.13 = (bf16[96,512]{1,0:T(8,128)(2,1)S(1)}, bf16[96,512]{1,0:T(8,128)(2,1)S(1)}, u32[]{:S(2)}, u32[]{:S(2)}) collective-permute-start(bf16[96,512]{1,0:T(8,128)(2,1)S(1)} %get-tuple-element.74), channel_id=1, source_target_pairs={{0,4},{2,6},{4,8},{6,10},{8,12},{10,14},{12,0},{14,2},{1,5},{3,7},... | collective-permute-start | bytes 294920 | tf_op jit(solution)/shard_map/ppermute | solution.py:347
  80.0 3.3 %collective-permute-start.14 = (bf16[96,512]{1,0:T(8,128)(2,1)S(1)}, bf16[96,512]{1,0:T(8,128)(2,1)S(1)}, u32[]{:S(2)}, u32[]{:S(2)}) collective-permute-start(bf16[96,512]{1,0:T(8,128)(2,1)S(1)} %get-tuple-element.76), channel_id=1, source_target_pairs={{0,8},{2,10},{4,12},{6,14},{8,0},{10,2},{12,4},{14,6},{1,9},{3,11}... | collective-permute-start | bytes 294920 | tf_op jit(solution)/shard_map/ppermute | solution.py:347
  83.2 3.6 %collective-permute-start.15 = (bf16[96,512]{1,0:T(8,128)(2,1)S(1)}, bf16[96,512]{1,0:T(8,128)(2,1)S(1)}, u32[]{:S(2)}, u32[]{:S(2)}) collective-permute-start(bf16[96,512]{1,0:T(8,128)(2,1)S(1)} %get-tuple-element.78), channel_id=1, source_target_pairs={{0,12},{2,14},{4,0},{6,2},{8,4},{10,6},{12,8},{14,10},{1,13},{3,15... | collective-permute-start | bytes 294920 | tf_op jit(solution)/shard_map/ppermute | solution.py:347
  86.9 5.3 %collective-permute-done.14 = bf16[96,512]{1,0:T(8,128)(2,1)S(1)} collective-permute-done((bf16[96,512]{1,0:T(8,128)(2,1)S(1)}, bf16[96,512]{1,0:T(8,128)(2,1)S(1)}, u32[]{:S(2)}, u32[]{:S(2)}) %collective-permute-start.14) | collective-permute-done | bytes 98336 | tf_op jit(solution)/shard_map/ppermute | solution.py:347
  95.1 4.6 %all-to-all-done.1.parts = f32[8,32,1536]{2,1,0:T(8,128)S(1)} async-done(((f32[8,32,1536]{2,1,0:T(8,128)}), f32[8,32,1536]{2,1,0:T(8,128)S(1)}, u32[]{:S(2)}, u32[]{:S(2)}) %all-to-all-start.1) | async-done | bytes 1572896 | tf_op jit(solution)/shard_map/all_to_all | solution.py:366
  99.8 3.4 %collective-permute-done.20.other = f32[32,512]{1,0:T(8,128)S(1)} collective-permute-done((f32[32,512]{1,0:T(8,128)S(1)}, f32[32,512]{1,0:T(8,128)S(1)}, u32[]{:S(2)}, u32[]{:S(2)}) %collective-permute-start.20) | collective-permute-done | bytes 65568 | tf_op jit(solution)/shard_map/ppermute | solution.py:338
  103.2 1.2 shard_map.62
  104.4 3.7 %all-to-all-start.2 = ((bf16[8,2,32,1024]{3,2,1,0:T(8,128)(2,1)}), bf16[8,2,32,1024]{3,2,1,0:T(8,128)(2,1)S(1)}, u32[]{:S(2)}, u32[]{:S(2)}) async-start(bf16[8,2,32,1024]{3,2,1,0:T(8,128)(2,1)} %shard_map.62), calls=%async_computation.2 | async-start | bytes 2097152 | tf_op jit(solution)/shard_map/all_to_all | solution.py:372
  108.1 2.7 %collective-permute-start.18 = (bf16[8,96,512]{2,1,0:T(8,128)(2,1)S(1)}, bf16[8,96,512]{2,1,0:T(8,128)(2,1)S(1)}, u32[]{:S(2)}, u32[]{:S(2)}) collective-permute-start(bf16[8,96,512]{2,1,0:T(8,128)(2,1)S(1)} %bitcast_dynamic-update-slice_fusion.refs_0_), channel_id=1, source_target_pairs={{0,16},{16,0},{1,17},{17,1},{2,18},{18,2},{3,19},{19,3},{4,20},{20... | collective-permute-start | bytes 2359304 | tf_op jit(solution)/shard_map/ppermute | solution.py:338
  111.8 5.3 %collective-permute-start.19 = (bf16[8,96,512]{2,1,0:T(8,128)(2,1)S(1)}, bf16[8,96,512]{2,1,0:T(8,128)(2,1)S(1)}, u32[]{:S(2)}, u32[]{:S(2)}) collective-permute-start(bf16[8,96,512]{2,1,0:T(8,128)(2,1)S(1)} %collective-permute-done.17.refs_1_), channel_id=1, source_target_pairs={{0,16},{16,0},{1,17},{17,1},{2,18},{18,2},{3,19},{19,3},{4,20},{20... | collective-permute-start | bytes 2359304 | tf_op jit(solution)/shard_map/ppermute | solution.py:338
  117.1 1.9 %collective-permute-done.19.refs_3_ = bf16[8,96,512]{2,1,0:T(8,128)(2,1)S(1)} collective-permute-done((bf16[8,96,512]{2,1,0:T(8,128)(2,1)S(1)}, bf16[8,96,512]{2,1,0:T(8,128)(2,1)S(1)}, u32[]{:S(2)}, u32[]{:S(2)}) %collective-permute-start.19) | collective-permute-done | bytes 786464 | tf_op jit(solution)/shard_map/ppermute | solution.py:338
  119.0 4.5 %shard_map.60 = (bf16[1024,1024]{1,0:T(8,128)(2,1)S(1)}, bf16[512,1024]{1,0:T(8,128)(2,1)S(1)}) custom-call(s32[3]{0:T(128)S(1)} %pad_add_fusion.me_ref, bf16[8,96,512]{2,1,0:T(8,128)(2,1)} %copy-done.5, bf16[8,96,512]{2,1,0:T(8,128)(2,1)} %copy-done.6, bf16[8,96,512]{2,1,0:T(8,128)(2,1)S(1)} %collective-permute-done.18.refs_2_, ...), custom_call_target="tpu_custom_call" | custom-call | bytes 6291456 | tf_op jit(solution)/shard_map/pallas_call | solution.py:282
  124.5 4.2 %all-to-all-done.2.p_ref = bf16[8,2,32,1024]{3,2,1,0:T(8,128)(2,1)S(1)} async-done(((bf16[8,2,32,1024]{3,2,1,0:T(8,128)(2,1)}), bf16[8,2,32,1024]{3,2,1,0:T(8,128)(2,1)S(1)}, u32[]{:S(2)}, u32[]{:S(2)}) %all-to-all-start.2) | async-done | bytes 1048608 | tf_op jit(solution)/shard_map/all_to_all | solution.py:372
  129.9 1.9 %shard_map.63 = bf16[16,96,256]{2,1,0:T(8,128)(2,1)S(1)} custom-call(s32[3]{0:T(128)S(1)} %pad_add_fusion.me_ref, bf16[1024,1024]{1,0:T(8,128)(2,1)S(1)} %get-tuple-element.80.vf, bf16[512,1024]{1,0:T(8,128)(2,1)S(1)} %copy-done.3, bf16[8,2,32,1024]{3,2,1,0:T(8,128)(2,1)S(1)} %all-to-all-done.2.p_ref), custom_call_target="tpu_custom_call" | custom-call | tf_op jit(solution)/shard_map/pallas_call | solution.py:307
  131.8 31.0 %all_to_all.20.m_ref = bf16[16,96,256]{2,1,0:T(8,128)(2,1)S(1)} all-to-all(bf16[16,96,256]{2,1,0:T(8,128)(2,1)S(1)} %shard_map.63), channel_id=1, replica_groups=mesh['y'=4,'xh'=2,'c'=2,'z'=8,'xl'=2] {'z','c'}, dimensions={0} | all-to-all | bytes 1572864 | tf_op jit(solution)/shard_map/all_to_all | solution.py:374
  162.8 1.7 %shard_map.64 = bf16[8,64,768]{2,1,0:T(8,128)(2,1)} custom-call(bf16[16,96,256]{2,1,0:T(8,128)(2,1)S(1)} %all_to_all.20.m_ref, bf16[768,768]{1,0:T(8,128)(2,1)S(1)} %copy-done.1), custom_call_target="tpu_custom_call" | custom-call | tf_op jit(solution)/shard_map/pallas_call | solution.py:327
  (60 shorter events, 8.6 us)
Async XLA Ops:
  0.0 13.5 %copy-start = (bf16[768,768]{1,0:T(8,128)(2,1)S(1)}, bf16[768,768]{1,0:T(8,128)(2,1)}, u32[]{:S(2)}) copy-start(bf16[768,768]{1,0:T(8,128)(2,1)} %w_ref.4) | copy-start | bytes 3538948
  3.1 12.3 %collective-permute-start.1 = (bf16[96,512]{1,0:T(8,128)(2,1)S(1)}, bf16[96,512]{1,0:T(8,128)(2,1)S(1)}, u32[]{:S(2)}, u32[]{:S(2)}) collective-permute-start(bf16[96,512]{1,0:T(8,128)(2,1)S(1)} %get-tuple-element.51), channel_id=1, source_target_pairs={{0,2},{2,4},{4,6},{6,8},{8,10},{10,12},{12,14},{14,0},{1,3},{3,5},... | collective-permute-start | bytes 294920 | tf_op jit(solution)/shard_map/ppermute | solution.py:347
  5.6 13.4 %collective-permute-start.2 = (bf16[96,512]{1,0:T(8,128)(2,1)S(1)}, bf16[96,512]{1,0:T(8,128)(2,1)S(1)}, u32[]{:S(2)}, u32[]{:S(2)}) collective-permute-start(bf16[96,512]{1,0:T(8,128)(2,1)S(1)} %get-tuple-element.52), channel_id=1, source_target_pairs={{0,14},{2,0},{4,2},{6,4},{8,6},{10,8},{12,10},{14,12},{1,15},{3,1}... | collective-permute-start | bytes 294920 | tf_op jit(solution)/shard_map/ppermute | solution.py:347
  9.6 13.8 %collective-permute-start.3 = (bf16[96,512]{1,0:T(8,128)(2,1)S(1)}, bf16[96,512]{1,0:T(8,128)(2,1)S(1)}, u32[]{:S(2)}, u32[]{:S(2)}) collective-permute-start(bf16[96,512]{1,0:T(8,128)(2,1)S(1)} %get-tuple-element.53), channel_id=1, source_target_pairs={{0,4},{2,6},{4,8},{6,10},{8,12},{10,14},{12,0},{14,2},{1,5},{3,7},... | collective-permute-start | bytes 294920 | tf_op jit(solution)/shard_map/ppermute | solution.py:347
  9.6 13.8 %collective-permute-start.4 = (bf16[96,512]{1,0:T(8,128)(2,1)S(1)}, bf16[96,512]{1,0:T(8,128)(2,1)S(1)}, u32[]{:S(2)}, u32[]{:S(2)}) collective-permute-start(bf16[96,512]{1,0:T(8,128)(2,1)S(1)} %get-tuple-element.54), channel_id=1, source_target_pairs={{0,12},{2,14},{4,0},{6,2},{8,4},{10,6},{12,8},{14,10},{1,13},{3,15... | collective-permute-start | bytes 294920 | tf_op jit(solution)/shard_map/ppermute | solution.py:347
  13.2 17.0 %collective-permute-start.5 = (bf16[96,512]{1,0:T(8,128)(2,1)S(1)}, bf16[96,512]{1,0:T(8,128)(2,1)}, u32[]{:S(2)}, u32[]{:S(2)}) collective-permute-start(bf16[96,512]{1,0:T(8,128)(2,1)S(1)} %get-tuple-element.57), channel_id=1, source_target_pairs={{0,6},{2,8},{4,10},{6,12},{8,14},{10,0},{12,2},{14,4},{1,7},{3,9},... | collective-permute-start | bytes 294920 | tf_op jit(solution)/shard_map/ppermute | solution.py:347
  15.4 15.8 %collective-permute-start.6 = (bf16[96,512]{1,0:T(8,128)(2,1)S(1)}, bf16[96,512]{1,0:T(8,128)(2,1)S(1)}, u32[]{:S(2)}, u32[]{:S(2)}) collective-permute-start(bf16[96,512]{1,0:T(8,128)(2,1)S(1)} %get-tuple-element.58), channel_id=1, source_target_pairs={{0,8},{2,10},{4,12},{6,14},{8,0},{10,2},{12,4},{14,6},{1,9},{3,11}... | collective-permute-start | bytes 294920 | tf_op jit(solution)/shard_map/ppermute | solution.py:347
  19.0 12.2 %collective-permute-start.7 = (bf16[96,512]{1,0:T(8,128)(2,1)S(1)}, bf16[96,512]{1,0:T(8,128)(2,1)S(1)}, u32[]{:S(2)}, u32[]{:S(2)}) collective-permute-start(bf16[96,512]{1,0:T(8,128)(2,1)S(1)} %get-tuple-element.59), channel_id=1, source_target_pairs={{0,10},{2,12},{4,14},{6,0},{8,2},{10,4},{12,6},{14,8},{1,11},{3,13... | collective-permute-start | bytes 294920 | tf_op jit(solution)/shard_map/ppermute | solution.py:347
  23.4 41.5 %all-to-all-start = ((bf16[16,128,256]{2,1,0:T(8,128)(2,1)}), bf16[16,128,256]{2,1,0:T(8,128)(2,1)}, u32[]{:S(2)}, u32[]{:S(2)}) async-start(bf16[16,128,256]{2,1,0:T(8,128)(2,1)} %shard_map.57), calls=%async_computation | async-start | bytes 2097152 | tf_op jit(solution)/shard_map/all_to_all | solution.py:357
  30.1 10.7 %copy-start.4 = (bf16[768,768]{1,0:T(8,128)(2,1)S(1)}, bf16[768,768]{1,0:T(8,128)(2,1)}, u32[]{:S(2)}) copy-start(bf16[768,768]{1,0:T(8,128)(2,1)} %w_ref.3) | copy-start | bytes 3538948
  31.3 10.9 %collective-permute-start.9 = (bf16[8,96,512]{2,1,0:T(8,128)(2,1)S(1)}, bf16[8,96,512]{2,1,0:T(8,128)(2,1)S(1)}, u32[]{:S(2)}, u32[]{:S(2)}) collective-permute-start(bf16[8,96,512]{2,1,0:T(8,128)(2,1)S(1)} %bitcast_dynamic-update-slice_fusion.8.own), channel_id=1, source_target_pairs={{0,16},{16,0},{1,17},{17,1},{2,18},{18,2},{3,19},{19,3},{4,20},{20... | collective-permute-start | bytes 2359304 | tf_op jit(solution)/shard_map/ppermute | solution.py:338
  39.6 19.1 %collective-permute-start.8 = (bf16[8,96,512]{2,1,0:T(8,128)(2,1)S(1)}, bf16[8,96,512]{2,1,0:T(8,128)(2,1)S(1)}, u32[]{:S(2)}, u32[]{:S(2)}) collective-permute-start(bf16[8,96,512]{2,1,0:T(8,128)(2,1)S(1)} %bitcast_dynamic-update-slice_fusion.8.own), channel_id=1, source_target_pairs={{0,1},{1,0},{2,3},{3,2},{4,5},{5,4},{6,7},{7,6},{8,9},{9,8},{10,11... | collective-permute-start | bytes 2359304 | tf_op jit(solution)/shard_map/ppermute | solution.py:338
  58.7 6.3 %copy-start.7 = (bf16[8,96,512]{2,1,0:T(8,128)(2,1)}, bf16[8,96,512]{2,1,0:T(8,128)(2,1)S(1)}, u32[]{:S(2)}) copy-start(bf16[8,96,512]{2,1,0:T(8,128)(2,1)S(1)} %collective-permute-done.8.own_hbm) | copy-start | bytes 2359300
  58.7 6.3 %collective-permute-start.11 = (bf16[8,96,512]{2,1,0:T(8,128)(2,1)S(1)}, bf16[8,96,512]{2,1,0:T(8,128)(2,1)S(1)}, u32[]{:S(2)}, u32[]{:S(2)}) collective-permute-start(bf16[8,96,512]{2,1,0:T(8,128)(2,1)S(1)} %collective-permute-done.8.own_hbm), channel_id=1, source_target_pairs={{0,16},{16,0},{1,17},{17,1},{2,18},{18,2},{3,19},{19,3},{4,20},{20... | collective-permute-start | bytes 2359304 | tf_op jit(solution)/shard_map/ppermute | solution.py:338
  59.5 11.4 %collective-permute-start = (bf16[96,512]{1,0:T(8,128)(2,1)S(1)}, bf16[96,512]{1,0:T(8,128)(2,1)S(1)}, u32[]{:S(2)}, u32[]{:S(2)}) collective-permute-start(bf16[96,512]{1,0:T(8,128)(2,1)S(1)} %get-tuple-element.49), channel_id=1, source_target_pairs={{0,6},{2,8},{4,10},{6,12},{8,14},{10,0},{12,2},{14,4},{1,7},{3,9},... | collective-permute-start | bytes 294920 | tf_op jit(solution)/shard_map/ppermute | solution.py:347
  59.5 11.4 %collective-permute-start.10 = (bf16[96,512]{1,0:T(8,128)(2,1)S(1)}, bf16[96,512]{1,0:T(8,128)(2,1)S(1)}, u32[]{:S(2)}, u32[]{:S(2)}) collective-permute-start(bf16[96,512]{1,0:T(8,128)(2,1)S(1)} %get-tuple-element.65), channel_id=1, source_target_pairs={{0,10},{2,12},{4,14},{6,0},{8,2},{10,4},{12,6},{14,8},{1,11},{3,13... | collective-permute-start | bytes 294920 | tf_op jit(solution)/shard_map/ppermute | solution.py:347
  70.9 28.7 %all-to-all-start.1 = ((f32[8,32,1536]{2,1,0:T(8,128)}), f32[8,32,1536]{2,1,0:T(8,128)S(1)}, u32[]{:S(2)}, u32[]{:S(2)}) async-start(f32[8,32,1536]{2,1,0:T(8,128)} %shard_map.59), calls=%async_computation.1 | async-start | bytes 3145728 | tf_op jit(solution)/shard_map/all_to_all | solution.py:366
  77.6 9.2 %collective-permute-start.12 = (bf16[96,512]{1,0:T(8,128)(2,1)S(1)}, bf16[96,512]{1,0:T(8,128)(2,1)S(1)}, u32[]{:S(2)}, u32[]{:S(2)}) collective-permute-start(bf16[96,512]{1,0:T(8,128)(2,1)S(1)} %get-tuple-element.73), channel_id=1, source_target_pairs={{0,2},{2,4},{4,6},{6,8},{8,10},{10,12},{12,14},{14,0},{1,3},{3,5},... | collective-permute-start | bytes 294920 | tf_op jit(solution)/shard_map/ppermute | solution.py:347
  77.6 9.3 %collective-permute-start.13 = (bf16[96,512]{1,0:T(8,128)(2,1)S(1)}, bf16[96,512]{1,0:T(8,128)(2,1)S(1)}, u32[]{:S(2)}, u32[]{:S(2)}) collective-permute-start(bf16[96,512]{1,0:T(8,128)(2,1)S(1)} %get-tuple-element.74), channel_id=1, source_target_pairs={{0,4},{2,6},{4,8},{6,10},{8,12},{10,14},{12,0},{14,2},{1,5},{3,7},... | collective-permute-start | bytes 294920 | tf_op jit(solution)/shard_map/ppermute | solution.py:347
  80.0 12.2 %collective-permute-start.14 = (bf16[96,512]{1,0:T(8,128)(2,1)S(1)}, bf16[96,512]{1,0:T(8,128)(2,1)S(1)}, u32[]{:S(2)}, u32[]{:S(2)}) collective-permute-start(bf16[96,512]{1,0:T(8,128)(2,1)S(1)} %get-tuple-element.76), channel_id=1, source_target_pairs={{0,8},{2,10},{4,12},{6,14},{8,0},{10,2},{12,4},{14,6},{1,9},{3,11}... | collective-permute-start | bytes 294920 | tf_op jit(solution)/shard_map/ppermute | solution.py:347
  83.2 10.2 %collective-permute-start.15 = (bf16[96,512]{1,0:T(8,128)(2,1)S(1)}, bf16[96,512]{1,0:T(8,128)(2,1)S(1)}, u32[]{:S(2)}, u32[]{:S(2)}) collective-permute-start(bf16[96,512]{1,0:T(8,128)(2,1)S(1)} %get-tuple-element.78), channel_id=1, source_target_pairs={{0,12},{2,14},{4,0},{6,2},{8,4},{10,6},{12,8},{14,10},{1,13},{3,15... | collective-permute-start | bytes 294920 | tf_op jit(solution)/shard_map/ppermute | solution.py:347
  86.8 7.8 %collective-permute-start.16 = (bf16[96,512]{1,0:T(8,128)(2,1)S(1)}, bf16[96,512]{1,0:T(8,128)(2,1)S(1)}, u32[]{:S(2)}, u32[]{:S(2)}) collective-permute-start(bf16[96,512]{1,0:T(8,128)(2,1)S(1)} %get-tuple-element.79), channel_id=1, source_target_pairs={{0,14},{2,0},{4,2},{6,4},{8,6},{10,8},{12,10},{14,12},{1,15},{3,1}... | collective-permute-start | bytes 294920 | tf_op jit(solution)/shard_map/ppermute | solution.py:347
  94.6 13.5 %copy-start.5 = (bf16[8,96,512]{2,1,0:T(8,128)(2,1)}, bf16[8,96,512]{2,1,0:T(8,128)(2,1)S(1)}, u32[]{:S(2)}) copy-start(bf16[8,96,512]{2,1,0:T(8,128)(2,1)S(1)} %bitcast_dynamic-update-slice_fusion.refs_0_) | copy-start | bytes 2359300
  94.6 17.2 %collective-permute-start.17 = (bf16[8,96,512]{2,1,0:T(8,128)(2,1)S(1)}, bf16[8,96,512]{2,1,0:T(8,128)(2,1)S(1)}, u32[]{:S(2)}, u32[]{:S(2)}) collective-permute-start(bf16[8,96,512]{2,1,0:T(8,128)(2,1)S(1)} %bitcast_dynamic-update-slice_fusion.refs_0_), channel_id=1, source_target_pairs={{0,1},{1,0},{2,3},{3,2},{4,5},{5,4},{6,7},{7,6},{8,9},{9,8},{10,11... | collective-permute-start | bytes 2359304 | tf_op jit(solution)/shard_map/ppermute | solution.py:338
  99.7 3.5 %collective-permute-start.20 = (f32[32,512]{1,0:T(8,128)S(1)}, f32[32,512]{1,0:T(8,128)S(1)}, u32[]{:S(2)}, u32[]{:S(2)}) collective-permute-start(f32[32,512]{1,0:T(8,128)S(1)} %get-tuple-element.84.half), channel_id=1, source_target_pairs={{0,2},{2,0},{4,6},{6,4},{8,10},{10,8},{12,14},{14,12},{1,3},{3,1},... | collective-permute-start | bytes 196616 | tf_op jit(solution)/shard_map/ppermute | solution.py:338
  104.4 24.2 %all-to-all-start.2 = ((bf16[8,2,32,1024]{3,2,1,0:T(8,128)(2,1)}), bf16[8,2,32,1024]{3,2,1,0:T(8,128)(2,1)S(1)}, u32[]{:S(2)}, u32[]{:S(2)}) async-start(bf16[8,2,32,1024]{3,2,1,0:T(8,128)(2,1)} %shard_map.62), calls=%async_computation.2 | async-start | bytes 2097152 | tf_op jit(solution)/shard_map/all_to_all | solution.py:372
  108.1 9.0 %collective-permute-start.18 = (bf16[8,96,512]{2,1,0:T(8,128)(2,1)S(1)}, bf16[8,96,512]{2,1,0:T(8,128)(2,1)S(1)}, u32[]{:S(2)}, u32[]{:S(2)}) collective-permute-start(bf16[8,96,512]{2,1,0:T(8,128)(2,1)S(1)} %bitcast_dynamic-update-slice_fusion.refs_0_), channel_id=1, source_target_pairs={{0,16},{16,0},{1,17},{17,1},{2,18},{18,2},{3,19},{19,3},{4,20},{20... | collective-permute-start | bytes 2359304 | tf_op jit(solution)/shard_map/ppermute | solution.py:338
  111.8 5.3 %copy-start.6 = (bf16[8,96,512]{2,1,0:T(8,128)(2,1)}, bf16[8,96,512]{2,1,0:T(8,128)(2,1)S(1)}, u32[]{:S(2)}) copy-start(bf16[8,96,512]{2,1,0:T(8,128)(2,1)S(1)} %collective-permute-done.17.refs_1_) | copy-start | bytes 2359300
  111.8 7.2 %collective-permute-start.19 = (bf16[8,96,512]{2,1,0:T(8,128)(2,1)S(1)}, bf16[8,96,512]{2,1,0:T(8,128)(2,1)S(1)}, u32[]{:S(2)}, u32[]{:S(2)}) collective-permute-start(bf16[8,96,512]{2,1,0:T(8,128)(2,1)S(1)} %collective-permute-done.17.refs_1_), channel_id=1, source_target_pairs={{0,16},{16,0},{1,17},{17,1},{2,18},{18,2},{3,19},{19,3},{4,20},{20... | collective-permute-start | bytes 2359304 | tf_op jit(solution)/shard_map/ppermute | solution.py:338
  123.5 1.0 copy-start.2
  128.6 1.2 copy-start.3
  131.8 31.1 %copy-start.1 = (bf16[768,768]{1,0:T(8,128)(2,1)S(1)}, bf16[768,768]{1,0:T(8,128)(2,1)}, u32[]{:S(2)}) copy-start(bf16[768,768]{1,0:T(8,128)(2,1)} %w_ref.5) | copy-start | bytes 3538948

commit v12 on v11

--- a/solution.py
+++ b/solution.py
@@ -353,18 +353,21 @@
     n, k = key_chunks(me, x, wk)
     for s in (1, 7, 2, 6, 3, 5, 4):
         k[s] = shift(k[s], s)
-    q, k[1], k[7], k[2], k[6] = lax.optimization_barrier((query_chunks(n, wq), k[1], k[7], k[2], k[6]))
+    early = (1, 7, 2, 6, 3, 5)
+    q, *got = lax.optimization_barrier((query_chunks(n, wq), *(k[s] for s in early)))
+    for s, a in zip(early, got):
+        k[s] = a
     q = lax.all_to_all(q, ("z", "c"), 0, 0, tiled=True)
     v = list(value_chunks(me, n, wv))
     k = jnp.stack(k)
     near, shared = keys_laid(me, k, flip(k, "c", 2, 1))
-    k_far, v[4], shared = lax.optimization_barrier((flip(k, "xl", 2, 1), v[4], shared))
-    for s in (3, 5):
+    for s in (1, 7):
         v[s] = shift(v[s], s)
+    k_far, v[1], v[7], shared = lax.optimization_barrier((flip(k, "xl", 2, 1), v[1], v[7], shared))
     scores = score(me, q, (near, shared), k_far, flip(k_far, "c", 2, 1))
     *v, scores = lax.optimization_barrier((*v, scores))
     parts = lax.all_to_all(scores, ("y", "xh"), 0, 0, tiled=True)
-    for s in (4, 2, 6, 1, 7):
+    for s in (4, 3, 5, 2, 6):
         v[s] = shift(v[s], s)
     full, half = total(parts)
     rows = ROWS * 2 * PEERS

time: 165 us -> 173 us (1.048)
  waiting for transfers between devices: 37.4 us -> 52.7 us
  starting transfers between devices: 69.1 us -> 65.3 us
  blocking collectives: 31 us -> 28 us
    ppermute x14, waiting for transfers between devices: 7.69 us -> 35.1 us  [shift(): return lax.ppermute(x, 'z', [(i, (i + s) % Z) for i in range(Z)])]
    ppermute x7, starting transfers between devices: 18.9 us -> 7.11 us  [flip(): return lax.ppermute(x, axes, [(i, i ^ s) for i in range(n)])]
    ppermute x7, waiting for transfers between devices: 20.9 us -> 11.5 us  [flip(): return lax.ppermute(x, axes, [(i, i ^ s) for i in range(n)])]
    all_to_all x1, starting transfers between devices: 6.69 us -> 11.7 us  [local(): q = lax.all_to_all(q, ('z', 'c'), 0, 0, tiled=True)]
    all_to_all x1, waiting for transfers between devices: 4.59 us -> 0.01 us  [local(): parts = lax.all_to_all(scores, ('y', 'xh'), 0, 0, tiled=True)]
    all_to_all x1, starting transfers between devices: 3.68 us -> 7.25 us  [local(): probs = lax.all_to_all(probs, ('y', 'xh'), 0, 0, tiled=True)]
    all_to_all x1, blocking collectives: 31 us -> 28 us  [local(): mixed = lax.all_to_all(mix(me, laid, probs), ('z', 'c'), 0, 0, tiled=True)]
    all_to_all x1, waiting for transfers between devices: 4.15 us -> 6.12 us  [local(): probs = lax.all_to_all(probs, ('y', 'xh'), 0, 0, tiled=True)]
  transfers between devices with their start and end apart: 24 -> 24, of which waited for: 9 -> 11; matrix products, arithmetic and copies ran while one was open for 1% -> 0% of each run, Pallas kernels for 10% -> 6%
where the time goes in v12:
time: 173 us
  starting transfers between devices  65.3 us (38%)
  waiting for transfers between devices  52.7 us (30%)
  blocking collectives  28 us (16%)
  Pallas kernels  23.3 us (13%)
  local copies, waits for them, and re-layouts  3.23 us (2%)
    ppermute x14, waiting for transfers between devices, shift(): return lax.ppermute(x, 'z', [(i, (i + s) % Z) for i in range(Z)])  35.1 us
    ppermute x14, starting transfers between devices, shift(): return lax.ppermute(x, 'z', [(i, (i + s) % Z) for i in range(Z)])  32.6 us
    all_to_all x1, blocking collectives, local(): mixed = lax.all_to_all(mix(me, laid, probs), ('z', 'c'), 0, 0, tiled=True)  28 us
    all_to_all x1, starting transfers between devices, local(): q = lax.all_to_all(q, ('z', 'c'), 0, 0, tiled=True)  11.7 us
    ppermute x7, waiting for transfers between devices, flip(): return lax.ppermute(x, axes, [(i, i ^ s) for i in range(n)])  11.5 us
    all_to_all x1, starting transfers between devices, local(): probs = lax.all_to_all(probs, ('y', 'xh'), 0, 0, tiled=True)  7.25 us
    ppermute x7, starting transfers between devices, flip(): return lax.ppermute(x, axes, [(i, i ^ s) for i in range(n)])  7.11 us
    all_to_all x1, starting transfers between devices, local(): parts = lax.all_to_all(scores, ('y', 'xh'), 0, 0, tiled=True)  6.66 us
  transfers between devices with their start and end apart: 24, of which 11 were waited for; matrix products, arithmetic and copies ran while one was open for 0% of the time, Pallas kernels for 6%

profile of v12, /device:TPU:1, one launch (start us, length us, event | category | flops | bytes accessed | tf_op | source)
XLA Modules:
  0.0 172.8 jit_solution(15351931807497800808)
XLA Ops:
  0.1 3.0 %shard_map.55 = (bf16[2,8,32,768]{3,2,1,0:T(8,128)(2,1)S(1)}, bf16[96,512]{1,0:T(8,128)(2,1)S(1)}, bf16[96,512]{1,0:T(8,128)(2,1)S(1)}, bf16[96,512]{1,0:T(8,128...) custom-call(s32[3]{0:T(128)S(1)} %pad_add_fusion.me_ref, ...), custom_call_target="tpu_custom_call" | custom-call | tf_op jit(solution)/shard_map/pallas_call | solution.py:97
  3.1 2.5 %collective-permute-start = (bf16[96,512]{1,0:T(8,128)(2,1)S(1)}, bf16[96,512]{1,0:T(8,128)(2,1)S(1)}, u32[]{:S(2)}, u32[]{:S(2)}) collective-permute-start(bf16[96,512]{1,0:T(8,128)(2,1)S(1)} %get-tuple-element.51), channel_id=1, source_target_pairs={{0,2},{2,4},{4,6},{6,8},{8,10},{10,12},{12,14},{14,0},{1,3},{3,5},... | collective-permute-start | bytes 294920 | tf_op jit(solution)/shard_map/ppermute | solution.py:347
  5.6 4.0 %collective-permute-start.1 = (bf16[96,512]{1,0:T(8,128)(2,1)S(1)}, bf16[96,512]{1,0:T(8,128)(2,1)S(1)}, u32[]{:S(2)}, u32[]{:S(2)}) collective-permute-start(bf16[96,512]{1,0:T(8,128)(2,1)S(1)} %get-tuple-element.52), channel_id=1, source_target_pairs={{0,14},{2,0},{4,2},{6,4},{8,6},{10,8},{12,10},{14,12},{1,15},{3,1}... | collective-permute-start | bytes 294920 | tf_op jit(solution)/shard_map/ppermute | solution.py:347
  9.6 3.6 %collective-permute-start.3 = (bf16[96,512]{1,0:T(8,128)(2,1)S(1)}, bf16[96,512]{1,0:T(8,128)(2,1)S(1)}, u32[]{:S(2)}, u32[]{:S(2)}) collective-permute-start(bf16[96,512]{1,0:T(8,128)(2,1)S(1)} %get-tuple-element.54), channel_id=1, source_target_pairs={{0,12},{2,14},{4,0},{6,2},{8,4},{10,6},{12,8},{14,10},{1,13},{3,15... | collective-permute-start | bytes 294920 | tf_op jit(solution)/shard_map/ppermute | solution.py:347
  13.5 4.2 %collective-permute-start.5 = (bf16[96,512]{1,0:T(8,128)(2,1)S(1)}, bf16[96,512]{1,0:T(8,128)(2,1)S(1)}, u32[]{:S(2)}, u32[]{:S(2)}) collective-permute-start(bf16[96,512]{1,0:T(8,128)(2,1)S(1)} %get-tuple-element.56), channel_id=1, source_target_pairs={{0,10},{2,12},{4,14},{6,0},{8,2},{10,4},{12,6},{14,8},{1,11},{3,13... | collective-permute-start | bytes 294920 | tf_op jit(solution)/shard_map/ppermute | solution.py:347
  17.7 1.8 %shard_map.57 = bf16[16,128,256]{2,1,0:T(8,128)(2,1)} custom-call(bf16[2,8,32,768]{3,2,1,0:T(8,128)(2,1)S(1)} %get-tuple-element.48.n_ref, bf16[768,768]{1,0:T(8,128)(2,1)S(1)} %copy-done), custom_call_target="tpu_custom_call" | custom-call | flops 603979776 | bytes 2752512 | tf_op jit(solution)/shard_map/pallas_call | solution.py:124
  19.5 3.9 %collective-permute-start.6 = (bf16[96,512]{1,0:T(8,128)(2,1)S(1)}, bf16[96,512]{1,0:T(8,128)(2,1)S(1)}, u32[]{:S(2)}, u32[]{:S(2)}) collective-permute-start(bf16[96,512]{1,0:T(8,128)(2,1)S(1)} %get-tuple-element.60), channel_id=1, source_target_pairs={{0,8},{2,10},{4,12},{6,14},{8,0},{10,2},{12,4},{14,6},{1,9},{3,11}... | collective-permute-start | bytes 294920 | tf_op jit(solution)/shard_map/ppermute | solution.py:347
  23.4 1.4 collective-permute-done.4
  24.8 11.7 %all-to-all-start = ((bf16[16,128,256]{2,1,0:T(8,128)(2,1)}), bf16[16,128,256]{2,1,0:T(8,128)(2,1)}, u32[]{:S(2)}, u32[]{:S(2)}) async-start(bf16[16,128,256]{2,1,0:T(8,128)(2,1)} %shard_map.57), calls=%async_computation | async-start | bytes 2097152 | tf_op jit(solution)/shard_map/all_to_all | solution.py:360
  38.1 1.4 shard_map.56
  39.5 1.7 collective-permute-start.8
  42.5 1.8 %shard_map.58 = (bf16[1024,512]{1,0:T(8,128)(2,1)S(1)}, bf16[1024,256]{1,0:T(8,128)(2,1)S(1)}) custom-call(s32[3]{0:T(128)S(1)} %pad_add_fusion.me_ref, bf16[8,96,512]{2,1,0:T(8,128)(2,1)S(1)} %bitcast_dynamic-update-slice_fusion.8.own, bf16[8,96,512]{2,1,0:T(8,128)(2,1)S(1)} %collective-permute-done.10.other), custom_call_target="tpu_custom_call" | custom-call | bytes 6291456 | tf_op jit(solution)/shard_map/pallas_call | solution.py:173
  44.3 20.3 %collective-permute-done.8 = bf16[96,512]{1,0:T(8,128)(2,1)S(1)} collective-permute-done((bf16[96,512]{1,0:T(8,128)(2,1)S(1)}, bf16[96,512]{1,0:T(8,128)(2,1)S(1)}, u32[]{:S(2)}, u32[]{:S(2)}) %collective-permute-start.8) | collective-permute-done | bytes 98336 | tf_op jit(solution)/shard_map/ppermute | solution.py:347
  66.4 1.9 %collective-permute-done.11.other_hbm = bf16[8,96,512]{2,1,0:T(8,128)(2,1)S(1)} collective-permute-done((bf16[8,96,512]{2,1,0:T(8,128)(2,1)S(1)}, bf16[8,96,512]{2,1,0:T(8,128)(2,1)S(1)}, u32[]{:S(2)}, u32[]{:S(2)}) %collective-permute-start.11) | collective-permute-done | bytes 786464 | tf_op jit(solution)/shard_map/ppermute | solution.py:338
  68.3 5.9 %shard_map.59 = f32[8,32,1536]{2,1,0:T(8,128)} custom-call(s32[3]{0:T(128)S(1)} %pad_add_fusion.me_ref, bf16[16,128,256]{2,1,0:T(8,128)(2,1)} %all-to-all-done.q_hbm, bf16[1024,512]{1,0:T(8,128)(2,1)S(1)} %get-tuple-element.75.kf_hbm, bf16[1024,256]{1,0:T(8,128)(2,1)S(1)} %get-tuple-element.76.kh_hbm, bf16[8,96,512]{2,1,0:T(8,128)(2,1)} %copy-done.6, ...), custom_call_target="tpu_custom_call" | custom-call | tf_op jit(solution)/shard_map/pallas_call | solution.py:209
  74.2 6.7 %all-to-all-start.1 = ((f32[8,32,1536]{2,1,0:T(8,128)}), f32[8,32,1536]{2,1,0:T(8,128)S(1)}, u32[]{:S(2)}, u32[]{:S(2)}) async-start(f32[8,32,1536]{2,1,0:T(8,128)} %shard_map.59), calls=%async_computation.1 | async-start | bytes 3145728 | tf_op jit(solution)/shard_map/all_to_all | solution.py:369
  81.9 3.1 %collective-permute-start.13 = (bf16[96,512]{1,0:T(8,128)(2,1)S(1)}, bf16[96,512]{1,0:T(8,128)(2,1)S(1)}, u32[]{:S(2)}, u32[]{:S(2)}) collective-permute-start(bf16[96,512]{1,0:T(8,128)(2,1)S(1)} %get-tuple-element.81), channel_id=1, source_target_pairs={{0,6},{2,8},{4,10},{6,12},{8,14},{10,0},{12,2},{14,4},{1,7},{3,9},... | collective-permute-start | bytes 294920 | tf_op jit(solution)/shard_map/ppermute | solution.py:347
  86.3 3.2 %collective-permute-start.15 = (bf16[96,512]{1,0:T(8,128)(2,1)S(1)}, bf16[96,512]{1,0:T(8,128)(2,1)S(1)}, u32[]{:S(2)}, u32[]{:S(2)}) collective-permute-start(bf16[96,512]{1,0:T(8,128)(2,1)S(1)} %get-tuple-element.83), channel_id=1, source_target_pairs={{0,10},{2,12},{4,14},{6,0},{8,2},{10,4},{12,6},{14,8},{1,11},{3,13... | collective-permute-start | bytes 294920 | tf_op jit(solution)/shard_map/ppermute | solution.py:347
  89.5 2.4 %collective-permute-start.16 = (bf16[96,512]{1,0:T(8,128)(2,1)S(1)}, bf16[96,512]{1,0:T(8,128)(2,1)S(1)}, u32[]{:S(2)}, u32[]{:S(2)}) collective-permute-start(bf16[96,512]{1,0:T(8,128)(2,1)S(1)} %get-tuple-element.84), channel_id=1, source_target_pairs={{0,12},{2,14},{4,0},{6,2},{8,4},{10,6},{12,8},{14,10},{1,13},{3,15... | collective-permute-start | bytes 294920 | tf_op jit(solution)/shard_map/ppermute | solution.py:347
  92.4 5.5 %collective-permute-done.14 = bf16[96,512]{1,0:T(8,128)(2,1)S(1)} collective-permute-done((bf16[96,512]{1,0:T(8,128)(2,1)S(1)}, bf16[96,512]{1,0:T(8,128)(2,1)S(1)}, u32[]{:S(2)}, u32[]{:S(2)}) %collective-permute-start.14) | collective-permute-done | bytes 98336 | tf_op jit(solution)/shard_map/ppermute | solution.py:347
  98.8 6.7 %collective-permute-done.16 = bf16[96,512]{1,0:T(8,128)(2,1)S(1)} collective-permute-done((bf16[96,512]{1,0:T(8,128)(2,1)S(1)}, bf16[96,512]{1,0:T(8,128)(2,1)S(1)}, u32[]{:S(2)}, u32[]{:S(2)}) %collective-permute-start.16) | collective-permute-done | bytes 98336 | tf_op jit(solution)/shard_map/ppermute | solution.py:347
  106.1 3.4 %collective-permute-done.20.other = f32[32,512]{1,0:T(8,128)S(1)} collective-permute-done((f32[32,512]{1,0:T(8,128)S(1)}, f32[32,512]{1,0:T(8,128)S(1)}, u32[]{:S(2)}, u32[]{:S(2)}) %collective-permute-start.20) | collective-permute-done | bytes 65568 | tf_op jit(solution)/shard_map/ppermute | solution.py:338
  110.7 7.3 %all-to-all-start.2 = ((bf16[8,2,32,1024]{3,2,1,0:T(8,128)(2,1)}), bf16[8,2,32,1024]{3,2,1,0:T(8,128)(2,1)S(1)}, u32[]{:S(2)}, u32[]{:S(2)}) async-start(bf16[8,2,32,1024]{3,2,1,0:T(8,128)(2,1)} %shard_map.62), calls=%async_computation.2 | async-start | bytes 2097152 | tf_op jit(solution)/shard_map/all_to_all | solution.py:375
  118.0 2.0 %collective-permute-start.18 = (bf16[8,96,512]{2,1,0:T(8,128)(2,1)S(1)}, bf16[8,96,512]{2,1,0:T(8,128)(2,1)S(1)}, u32[]{:S(2)}, u32[]{:S(2)}) collective-permute-start(bf16[8,96,512]{2,1,0:T(8,128)(2,1)S(1)} %bitcast_dynamic-update-slice_fusion.refs_0_), channel_id=1, source_target_pairs={{0,16},{16,0},{1,17},{17,1},{2,18},{18,2},{3,19},{19,3},{4,20},{20... | collective-permute-start | bytes 2359304 | tf_op jit(solution)/shard_map/ppermute | solution.py:338
  120.0 4.3 %collective-permute-done.17.refs_1_ = bf16[8,96,512]{2,1,0:T(8,128)(2,1)S(1)} collective-permute-done((bf16[8,96,512]{2,1,0:T(8,128)(2,1)S(1)}, bf16[8,96,512]{2,1,0:T(8,128)(2,1)S(1)}, u32[]{:S(2)}, u32[]{:S(2)}) %collective-permute-start.17) | collective-permute-done | bytes 786464 | tf_op jit(solution)/shard_map/ppermute | solution.py:338
  124.2 2.3 %collective-permute-start.19 = (bf16[8,96,512]{2,1,0:T(8,128)(2,1)S(1)}, bf16[8,96,512]{2,1,0:T(8,128)(2,1)S(1)}, u32[]{:S(2)}, u32[]{:S(2)}) collective-permute-start(bf16[8,96,512]{2,1,0:T(8,128)(2,1)S(1)} %collective-permute-done.17.refs_1_), channel_id=1, source_target_pairs={{0,16},{16,0},{1,17},{17,1},{2,18},{18,2},{3,19},{19,3},{4,20},{20... | collective-permute-start | bytes 2359304 | tf_op jit(solution)/shard_map/ppermute | solution.py:338
  126.5 1.9 %collective-permute-done.19.refs_3_ = bf16[8,96,512]{2,1,0:T(8,128)(2,1)S(1)} collective-permute-done((bf16[8,96,512]{2,1,0:T(8,128)(2,1)S(1)}, bf16[8,96,512]{2,1,0:T(8,128)(2,1)S(1)}, u32[]{:S(2)}, u32[]{:S(2)}) %collective-permute-start.19) | collective-permute-done | bytes 786464 | tf_op jit(solution)/shard_map/ppermute | solution.py:338
  128.4 4.5 %shard_map.60 = (bf16[1024,1024]{1,0:T(8,128)(2,1)S(1)}, bf16[512,1024]{1,0:T(8,128)(2,1)S(1)}) custom-call(s32[3]{0:T(128)S(1)} %pad_add_fusion.me_ref, bf16[8,96,512]{2,1,0:T(8,128)(2,1)} %copy-done.5, bf16[8,96,512]{2,1,0:T(8,128)(2,1)} %copy-done.7, bf16[8,96,512]{2,1,0:T(8,128)(2,1)S(1)} %collective-permute-done.18.refs_2_, ...), custom_call_target="tpu_custom_call" | custom-call | bytes 6291456 | tf_op jit(solution)/shard_map/pallas_call | solution.py:282
  133.9 6.1 %all-to-all-done.2.p_ref = bf16[8,2,32,1024]{3,2,1,0:T(8,128)(2,1)S(1)} async-done(((bf16[8,2,32,1024]{3,2,1,0:T(8,128)(2,1)}), bf16[8,2,32,1024]{3,2,1,0:T(8,128)(2,1)S(1)}, u32[]{:S(2)}, u32[]{:S(2)}) %all-to-all-start.2) | async-done | bytes 1048608 | tf_op jit(solution)/shard_map/all_to_all | solution.py:375
  141.2 1.9 %shard_map.63 = bf16[16,96,256]{2,1,0:T(8,128)(2,1)S(1)} custom-call(s32[3]{0:T(128)S(1)} %pad_add_fusion.me_ref, bf16[1024,1024]{1,0:T(8,128)(2,1)S(1)} %get-tuple-element.86.vf, bf16[512,1024]{1,0:T(8,128)(2,1)S(1)} %copy-done.3, bf16[8,2,32,1024]{3,2,1,0:T(8,128)(2,1)S(1)} %all-to-all-done.2.p_ref), custom_call_target="tpu_custom_call" | custom-call | tf_op jit(solution)/shard_map/pallas_call | solution.py:307
  143.1 28.0 %all_to_all.20.m_ref = bf16[16,96,256]{2,1,0:T(8,128)(2,1)S(1)} all-to-all(bf16[16,96,256]{2,1,0:T(8,128)(2,1)S(1)} %shard_map.63), channel_id=1, replica_groups=mesh['y'=4,'xh'=2,'c'=2,'z'=8,'xl'=2] {'z','c'}, dimensions={0} | all-to-all | bytes 1572864 | tf_op jit(solution)/shard_map/all_to_all | solution.py:377
  171.1 1.7 shard_map.64
  (60 shorter events, 12.6 us)
Async XLA Ops:
  0.0 17.7 %copy-start = (bf16[768,768]{1,0:T(8,128)(2,1)S(1)}, bf16[768,768]{1,0:T(8,128)(2,1)}, u32[]{:S(2)}) copy-start(bf16[768,768]{1,0:T(8,128)(2,1)} %w_ref.4) | copy-start | bytes 3538948
  3.1 10.5 %collective-permute-start = (bf16[96,512]{1,0:T(8,128)(2,1)S(1)}, bf16[96,512]{1,0:T(8,128)(2,1)S(1)}, u32[]{:S(2)}, u32[]{:S(2)}) collective-permute-start(bf16[96,512]{1,0:T(8,128)(2,1)S(1)} %get-tuple-element.51), channel_id=1, source_target_pairs={{0,2},{2,4},{4,6},{6,8},{8,10},{10,12},{12,14},{14,0},{1,3},{3,5},... | collective-permute-start | bytes 294920 | tf_op jit(solution)/shard_map/ppermute | solution.py:347
  5.6 13.9 %collective-permute-start.1 = (bf16[96,512]{1,0:T(8,128)(2,1)S(1)}, bf16[96,512]{1,0:T(8,128)(2,1)S(1)}, u32[]{:S(2)}, u32[]{:S(2)}) collective-permute-start(bf16[96,512]{1,0:T(8,128)(2,1)S(1)} %get-tuple-element.52), channel_id=1, source_target_pairs={{0,14},{2,0},{4,2},{6,4},{8,6},{10,8},{12,10},{14,12},{1,15},{3,1}... | collective-permute-start | bytes 294920 | tf_op jit(solution)/shard_map/ppermute | solution.py:347
  9.6 13.8 %collective-permute-start.2 = (bf16[96,512]{1,0:T(8,128)(2,1)S(1)}, bf16[96,512]{1,0:T(8,128)(2,1)S(1)}, u32[]{:S(2)}, u32[]{:S(2)}) collective-permute-start(bf16[96,512]{1,0:T(8,128)(2,1)S(1)} %get-tuple-element.53), channel_id=1, source_target_pairs={{0,4},{2,6},{4,8},{6,10},{8,12},{10,14},{12,0},{14,2},{1,5},{3,7},... | collective-permute-start | bytes 294920 | tf_op jit(solution)/shard_map/ppermute | solution.py:347
  9.6 13.8 %collective-permute-start.3 = (bf16[96,512]{1,0:T(8,128)(2,1)S(1)}, bf16[96,512]{1,0:T(8,128)(2,1)S(1)}, u32[]{:S(2)}, u32[]{:S(2)}) collective-permute-start(bf16[96,512]{1,0:T(8,128)(2,1)S(1)} %get-tuple-element.54), channel_id=1, source_target_pairs={{0,12},{2,14},{4,0},{6,2},{8,4},{10,6},{12,8},{14,10},{1,13},{3,15... | collective-permute-start | bytes 294920 | tf_op jit(solution)/shard_map/ppermute | solution.py:347
  13.2 11.6 %collective-permute-start.4 = (bf16[96,512]{1,0:T(8,128)(2,1)S(1)}, bf16[96,512]{1,0:T(8,128)(2,1)S(1)}, u32[]{:S(2)}, u32[]{:S(2)}) collective-permute-start(bf16[96,512]{1,0:T(8,128)(2,1)S(1)} %get-tuple-element.55), channel_id=1, source_target_pairs={{0,6},{2,8},{4,10},{6,12},{8,14},{10,0},{12,2},{14,4},{1,7},{3,9},... | collective-permute-start | bytes 294920 | tf_op jit(solution)/shard_map/ppermute | solution.py:347
  13.5 11.3 %collective-permute-start.5 = (bf16[96,512]{1,0:T(8,128)(2,1)S(1)}, bf16[96,512]{1,0:T(8,128)(2,1)S(1)}, u32[]{:S(2)}, u32[]{:S(2)}) collective-permute-start(bf16[96,512]{1,0:T(8,128)(2,1)S(1)} %get-tuple-element.56), channel_id=1, source_target_pairs={{0,10},{2,12},{4,14},{6,0},{8,2},{10,4},{12,6},{14,8},{1,11},{3,13... | collective-permute-start | bytes 294920 | tf_op jit(solution)/shard_map/ppermute | solution.py:347
  19.5 17.0 %collective-permute-start.6 = (bf16[96,512]{1,0:T(8,128)(2,1)S(1)}, bf16[96,512]{1,0:T(8,128)(2,1)S(1)}, u32[]{:S(2)}, u32[]{:S(2)}) collective-permute-start(bf16[96,512]{1,0:T(8,128)(2,1)S(1)} %get-tuple-element.60), channel_id=1, source_target_pairs={{0,8},{2,10},{4,12},{6,14},{8,0},{10,2},{12,4},{14,6},{1,9},{3,11}... | collective-permute-start | bytes 294920 | tf_op jit(solution)/shard_map/ppermute | solution.py:347
  24.8 43.5 %all-to-all-start = ((bf16[16,128,256]{2,1,0:T(8,128)(2,1)}), bf16[16,128,256]{2,1,0:T(8,128)(2,1)}, u32[]{:S(2)}, u32[]{:S(2)}) async-start(bf16[16,128,256]{2,1,0:T(8,128)(2,1)} %shard_map.57), calls=%async_computation | async-start | bytes 2097152 | tf_op jit(solution)/shard_map/all_to_all | solution.py:360
  36.5 1.6 copy-start.4
  36.6 5.8 %collective-permute-start.10 = (bf16[8,96,512]{2,1,0:T(8,128)(2,1)S(1)}, bf16[8,96,512]{2,1,0:T(8,128)(2,1)S(1)}, u32[]{:S(2)}, u32[]{:S(2)}) collective-permute-start(bf16[8,96,512]{2,1,0:T(8,128)(2,1)S(1)} %bitcast_dynamic-update-slice_fusion.8.own), channel_id=1, source_target_pairs={{0,16},{16,0},{1,17},{17,1},{2,18},{18,2},{3,19},{19,3},{4,20},{20... | collective-permute-start | bytes 2359304 | tf_op jit(solution)/shard_map/ppermute | solution.py:338
  36.9 27.7 %collective-permute-start.7 = (bf16[8,96,512]{2,1,0:T(8,128)(2,1)S(1)}, bf16[8,96,512]{2,1,0:T(8,128)(2,1)S(1)}, u32[]{:S(2)}, u32[]{:S(2)}) collective-permute-start(bf16[8,96,512]{2,1,0:T(8,128)(2,1)S(1)} %bitcast_dynamic-update-slice_fusion.8.own), channel_id=1, source_target_pairs={{0,1},{1,0},{2,3},{3,2},{4,5},{5,4},{6,7},{7,6},{8,9},{9,8},{10,11... | collective-permute-start | bytes 2359304 | tf_op jit(solution)/shard_map/ppermute | solution.py:338
  39.5 25.1 %collective-permute-start.8 = (bf16[96,512]{1,0:T(8,128)(2,1)S(1)}, bf16[96,512]{1,0:T(8,128)(2,1)S(1)}, u32[]{:S(2)}, u32[]{:S(2)}) collective-permute-start(bf16[96,512]{1,0:T(8,128)(2,1)S(1)} %get-tuple-element.64), channel_id=1, source_target_pairs={{0,2},{2,4},{4,6},{6,8},{8,10},{10,12},{12,14},{14,0},{1,3},{3,5},... | collective-permute-start | bytes 294920 | tf_op jit(solution)/shard_map/ppermute | solution.py:347
  41.1 23.4 %collective-permute-start.9 = (bf16[96,512]{1,0:T(8,128)(2,1)S(1)}, bf16[96,512]{1,0:T(8,128)(2,1)S(1)}, u32[]{:S(2)}, u32[]{:S(2)}) collective-permute-start(bf16[96,512]{1,0:T(8,128)(2,1)S(1)} %get-tuple-element.65), channel_id=1, source_target_pairs={{0,14},{2,0},{4,2},{6,4},{8,6},{10,8},{12,10},{14,12},{1,15},{3,1}... | collective-permute-start | bytes 294920 | tf_op jit(solution)/shard_map/ppermute | solution.py:347
  64.6 0.9 copy-start.6
  65.5 2.8 %collective-permute-start.11 = (bf16[8,96,512]{2,1,0:T(8,128)(2,1)S(1)}, bf16[8,96,512]{2,1,0:T(8,128)(2,1)S(1)}, u32[]{:S(2)}, u32[]{:S(2)}) collective-permute-start(bf16[8,96,512]{2,1,0:T(8,128)(2,1)S(1)} %collective-permute-done.7.own_hbm), channel_id=1, source_target_pairs={{0,16},{16,0},{1,17},{17,1},{2,18},{18,2},{3,19},{19,3},{4,20},{20... | collective-permute-start | bytes 2359304 | tf_op jit(solution)/shard_map/ppermute | solution.py:338
  74.2 31.7 %all-to-all-start.1 = ((f32[8,32,1536]{2,1,0:T(8,128)}), f32[8,32,1536]{2,1,0:T(8,128)S(1)}, u32[]{:S(2)}, u32[]{:S(2)}) async-start(f32[8,32,1536]{2,1,0:T(8,128)} %shard_map.59), calls=%async_computation.1 | async-start | bytes 3145728 | tf_op jit(solution)/shard_map/all_to_all | solution.py:369
  80.9 11.1 %collective-permute-start.12 = (bf16[96,512]{1,0:T(8,128)(2,1)S(1)}, bf16[96,512]{1,0:T(8,128)(2,1)S(1)}, u32[]{:S(2)}, u32[]{:S(2)}) collective-permute-start(bf16[96,512]{1,0:T(8,128)(2,1)S(1)} %get-tuple-element.80), channel_id=1, source_target_pairs={{0,4},{2,6},{4,8},{6,10},{8,12},{10,14},{12,0},{14,2},{1,5},{3,7},... | collective-permute-start | bytes 294920 | tf_op jit(solution)/shard_map/ppermute | solution.py:347
  81.9 10.5 %collective-permute-start.13 = (bf16[96,512]{1,0:T(8,128)(2,1)S(1)}, bf16[96,512]{1,0:T(8,128)(2,1)S(1)}, u32[]{:S(2)}, u32[]{:S(2)}) collective-permute-start(bf16[96,512]{1,0:T(8,128)(2,1)S(1)} %get-tuple-element.81), channel_id=1, source_target_pairs={{0,6},{2,8},{4,10},{6,12},{8,14},{10,0},{12,2},{14,4},{1,7},{3,9},... | collective-permute-start | bytes 294920 | tf_op jit(solution)/shard_map/ppermute | solution.py:347
  85.1 12.9 %collective-permute-start.14 = (bf16[96,512]{1,0:T(8,128)(2,1)S(1)}, bf16[96,512]{1,0:T(8,128)(2,1)S(1)}, u32[]{:S(2)}, u32[]{:S(2)}) collective-permute-start(bf16[96,512]{1,0:T(8,128)(2,1)S(1)} %get-tuple-element.82), channel_id=1, source_target_pairs={{0,8},{2,10},{4,12},{6,14},{8,0},{10,2},{12,4},{14,6},{1,9},{3,11}... | collective-permute-start | bytes 294920 | tf_op jit(solution)/shard_map/ppermute | solution.py:347
  86.3 12.4 %collective-permute-start.15 = (bf16[96,512]{1,0:T(8,128)(2,1)S(1)}, bf16[96,512]{1,0:T(8,128)(2,1)S(1)}, u32[]{:S(2)}, u32[]{:S(2)}) collective-permute-start(bf16[96,512]{1,0:T(8,128)(2,1)S(1)} %get-tuple-element.83), channel_id=1, source_target_pairs={{0,10},{2,12},{4,14},{6,0},{8,2},{10,4},{12,6},{14,8},{1,11},{3,13... | collective-permute-start | bytes 294920 | tf_op jit(solution)/shard_map/ppermute | solution.py:347
  89.5 15.9 %collective-permute-start.16 = (bf16[96,512]{1,0:T(8,128)(2,1)S(1)}, bf16[96,512]{1,0:T(8,128)(2,1)S(1)}, u32[]{:S(2)}, u32[]{:S(2)}) collective-permute-start(bf16[96,512]{1,0:T(8,128)(2,1)S(1)} %get-tuple-element.84), channel_id=1, source_target_pairs={{0,12},{2,14},{4,0},{6,2},{8,4},{10,6},{12,8},{14,10},{1,13},{3,15... | collective-permute-start | bytes 294920 | tf_op jit(solution)/shard_map/ppermute | solution.py:347
  105.5 12.5 %copy-start.5 = (bf16[8,96,512]{2,1,0:T(8,128)(2,1)}, bf16[8,96,512]{2,1,0:T(8,128)(2,1)S(1)}, u32[]{:S(2)}) copy-start(bf16[8,96,512]{2,1,0:T(8,128)(2,1)S(1)} %bitcast_dynamic-update-slice_fusion.refs_0_) | copy-start | bytes 2359300
  105.5 18.7 %collective-permute-start.17 = (bf16[8,96,512]{2,1,0:T(8,128)(2,1)S(1)}, bf16[8,96,512]{2,1,0:T(8,128)(2,1)S(1)}, u32[]{:S(2)}, u32[]{:S(2)}) collective-permute-start(bf16[8,96,512]{2,1,0:T(8,128)(2,1)S(1)} %bitcast_dynamic-update-slice_fusion.refs_0_), channel_id=1, source_target_pairs={{0,1},{1,0},{2,3},{3,2},{4,5},{5,4},{6,7},{7,6},{8,9},{9,8},{10,11... | collective-permute-start | bytes 2359304 | tf_op jit(solution)/shard_map/ppermute | solution.py:338
  106.0 3.5 %collective-permute-start.20 = (f32[32,512]{1,0:T(8,128)S(1)}, f32[32,512]{1,0:T(8,128)S(1)}, u32[]{:S(2)}, u32[]{:S(2)}) collective-permute-start(f32[32,512]{1,0:T(8,128)S(1)} %get-tuple-element.90.half), channel_id=1, source_target_pairs={{0,2},{2,0},{4,6},{6,4},{8,10},{10,8},{12,14},{14,12},{1,3},{3,1},... | collective-permute-start | bytes 196616 | tf_op jit(solution)/shard_map/ppermute | solution.py:338
  110.7 29.3 %all-to-all-start.2 = ((bf16[8,2,32,1024]{3,2,1,0:T(8,128)(2,1)}), bf16[8,2,32,1024]{3,2,1,0:T(8,128)(2,1)S(1)}, u32[]{:S(2)}, u32[]{:S(2)}) async-start(bf16[8,2,32,1024]{3,2,1,0:T(8,128)(2,1)} %shard_map.62), calls=%async_computation.2 | async-start | bytes 2097152 | tf_op jit(solution)/shard_map/all_to_all | solution.py:375
  118.0 8.5 %collective-permute-start.18 = (bf16[8,96,512]{2,1,0:T(8,128)(2,1)S(1)}, bf16[8,96,512]{2,1,0:T(8,128)(2,1)S(1)}, u32[]{:S(2)}, u32[]{:S(2)}) collective-permute-start(bf16[8,96,512]{2,1,0:T(8,128)(2,1)S(1)} %bitcast_dynamic-update-slice_fusion.refs_0_), channel_id=1, source_target_pairs={{0,16},{16,0},{1,17},{17,1},{2,18},{18,2},{3,19},{19,3},{4,20},{20... | collective-permute-start | bytes 2359304 | tf_op jit(solution)/shard_map/ppermute | solution.py:338
  124.2 2.3 %copy-start.7 = (bf16[8,96,512]{2,1,0:T(8,128)(2,1)}, bf16[8,96,512]{2,1,0:T(8,128)(2,1)S(1)}, u32[]{:S(2)}) copy-start(bf16[8,96,512]{2,1,0:T(8,128)(2,1)S(1)} %collective-permute-done.17.refs_1_) | copy-start | bytes 2359300
  124.2 4.2 %collective-permute-start.19 = (bf16[8,96,512]{2,1,0:T(8,128)(2,1)S(1)}, bf16[8,96,512]{2,1,0:T(8,128)(2,1)S(1)}, u32[]{:S(2)}, u32[]{:S(2)}) collective-permute-start(bf16[8,96,512]{2,1,0:T(8,128)(2,1)S(1)} %collective-permute-done.17.refs_1_), channel_id=1, source_target_pairs={{0,16},{16,0},{1,17},{17,1},{2,18},{18,2},{3,19},{19,3},{4,20},{20... | collective-permute-start | bytes 2359304 | tf_op jit(solution)/shard_map/ppermute | solution.py:338
  132.9 1.0 copy-start.2
  140.0 1.2 copy-start.3
  143.1 28.0 %copy-start.1 = (bf16[768,768]{1,0:T(8,128)(2,1)S(1)}, bf16[768,768]{1,0:T(8,128)(2,1)}, u32[]{:S(2)}) copy-start(bf16[768,768]{1,0:T(8,128)(2,1)} %w_ref.5) | copy-start | bytes 3538948

commit v13 on v11

--- a/solution.py
+++ b/solution.py
@@ -353,7 +353,10 @@
     n, k = key_chunks(me, x, wk)
     for s in (1, 7, 2, 6, 3, 5, 4):
         k[s] = shift(k[s], s)
-    q, k[1], k[7], k[2], k[6] = lax.optimization_barrier((query_chunks(n, wq), k[1], k[7], k[2], k[6]))
+    early = (1, 7, 2, 6, 3)
+    q, *got = lax.optimization_barrier((query_chunks(n, wq), *(k[s] for s in early)))
+    for s, a in zip(early, got):
+        k[s] = a
     q = lax.all_to_all(q, ("z", "c"), 0, 0, tiled=True)
     v = list(value_chunks(me, n, wv))
     k = jnp.stack(k)

time: 165 us -> 162 us (0.982)
  starting transfers between devices: 69.1 us -> 60.9 us
  waiting for transfers between devices: 37.4 us -> 44.4 us
  blocking collectives: 31 us -> 29.2 us
    ppermute x7, starting transfers between devices: 18.9 us -> 12.3 us  [flip(): return lax.ppermute(x, axes, [(i, i ^ s) for i in range(n)])]
    ppermute x14, waiting for transfers between devices: 7.69 us -> 14.2 us  [shift(): return lax.ppermute(x, 'z', [(i, (i + s) % Z) for i in range(Z)])]
    all_to_all x1, waiting for transfers between devices: 4.59 us -> 2.3 us  [local(): parts = lax.all_to_all(scores, ('y', 'xh'), 0, 0, tiled=True)]
    all_to_all x1, waiting for transfers between devices: 0.01 us -> 2.21 us  [local(): q = lax.all_to_all(q, ('z', 'c'), 0, 0, tiled=True)]
    all_to_all x1, blocking collectives: 31 us -> 29.2 us  [local(): mixed = lax.all_to_all(mix(me, laid, probs), ('z', 'c'), 0, 0, tiled=True)]
  transfers between devices with their start and end apart: 24 -> 24, of which waited for: 9 -> 12; matrix products, arithmetic and copies ran while one was open for 1% -> 1% of each run, Pallas kernels for 10% -> 10%
where the time goes in v13:
time: 162 us; the launch traced here: 161 us
  starting transfers between devices  60.9 us (38%)
  waiting for transfers between devices  44.4 us (27%)
  blocking collectives  29.2 us (18%)
  Pallas kernels  23.3 us (14%)
  local copies, waits for them, and re-layouts  3.34 us (2%)
    ppermute x14, starting transfers between devices, shift(): return lax.ppermute(x, 'z', [(i, (i + s) % Z) for i in range(Z)])  32.3 us
    all_to_all x1, blocking collectives, local(): mixed = lax.all_to_all(mix(me, laid, probs), ('z', 'c'), 0, 0, tiled=True)  29.2 us
    ppermute x7, waiting for transfers between devices, flip(): return lax.ppermute(x, axes, [(i, i ^ s) for i in range(n)])  20.4 us
    ppermute x14, waiting for transfers between devices, shift(): return lax.ppermute(x, 'z', [(i, (i + s) % Z) for i in range(Z)])  14.2 us
    ppermute x7, starting transfers between devices, flip(): return lax.ppermute(x, axes, [(i, i ^ s) for i in range(n)])  12.3 us
    all_to_all x1, starting transfers between devices, local(): parts = lax.all_to_all(scores, ('y', 'xh'), 0, 0, tiled=True)  6.65 us
    all_to_all x1, starting transfers between devices, local(): q = lax.all_to_all(q, ('z', 'c'), 0, 0, tiled=True)  5.95 us
    pallas_call x1, Pallas kernels, score(): pl.pallas_call(score_kernel, out_shape=jax.ShapeDtypeStruct((PEERS, SUB,...  5.93 us
  transfers between devices with their start and end apart: 24, of which 12 were waited for; matrix products, arithmetic and copies ran while one was open for 1% of the time, Pallas kernels for 10%

profile of v13, /device:TPU:1, one launch (start us, length us, event | category | flops | bytes accessed | tf_op | source)
XLA Modules:
  0.0 161.4 jit_solution(13507145333013896009)
XLA Ops:
  0.1 3.0 %shard_map.55 = (bf16[2,8,32,768]{3,2,1,0:T(8,128)(2,1)S(1)}, bf16[96,512]{1,0:T(8,128)(2,1)S(1)}, bf16[96,512]{1,0:T(8,128)(2,1)S(1)}, bf16[96,512]{1,0:T(8,128...) custom-call(s32[3]{0:T(128)S(1)} %pad_add_fusion.me_ref, ...), custom_call_target="tpu_custom_call" | custom-call | tf_op jit(solution)/shard_map/pallas_call | solution.py:97
  3.1 2.5 %collective-permute-start.1 = (bf16[96,512]{1,0:T(8,128)(2,1)S(1)}, bf16[96,512]{1,0:T(8,128)(2,1)S(1)}, u32[]{:S(2)}, u32[]{:S(2)}) collective-permute-start(bf16[96,512]{1,0:T(8,128)(2,1)S(1)} %get-tuple-element.52), channel_id=1, source_target_pairs={{0,2},{2,4},{4,6},{6,8},{8,10},{10,12},{12,14},{14,0},{1,3},{3,5},... | collective-permute-start | bytes 294920 | tf_op jit(solution)/shard_map/ppermute | solution.py:347
  5.6 4.0 %collective-permute-start.2 = (bf16[96,512]{1,0:T(8,128)(2,1)S(1)}, bf16[96,512]{1,0:T(8,128)(2,1)S(1)}, u32[]{:S(2)}, u32[]{:S(2)}) collective-permute-start(bf16[96,512]{1,0:T(8,128)(2,1)S(1)} %get-tuple-element.53), channel_id=1, source_target_pairs={{0,14},{2,0},{4,2},{6,4},{8,6},{10,8},{12,10},{14,12},{1,15},{3,1}... | collective-permute-start | bytes 294920 | tf_op jit(solution)/shard_map/ppermute | solution.py:347
  9.6 3.6 %collective-permute-start.4 = (bf16[96,512]{1,0:T(8,128)(2,1)S(1)}, bf16[96,512]{1,0:T(8,128)(2,1)S(1)}, u32[]{:S(2)}, u32[]{:S(2)}) collective-permute-start(bf16[96,512]{1,0:T(8,128)(2,1)S(1)} %get-tuple-element.55), channel_id=1, source_target_pairs={{0,12},{2,14},{4,0},{6,2},{8,4},{10,6},{12,8},{14,10},{1,13},{3,15... | collective-permute-start | bytes 294920 | tf_op jit(solution)/shard_map/ppermute | solution.py:347
  13.5 1.8 %shard_map.57 = bf16[16,128,256]{2,1,0:T(8,128)(2,1)} custom-call(bf16[2,8,32,768]{3,2,1,0:T(8,128)(2,1)S(1)} %get-tuple-element.46.n_ref, bf16[768,768]{1,0:T(8,128)(2,1)S(1)} %copy-done), custom_call_target="tpu_custom_call" | custom-call | flops 603979776 | bytes 2752512 | tf_op jit(solution)/shard_map/pallas_call | solution.py:124
  15.4 3.6 %collective-permute-start.6 = (bf16[96,512]{1,0:T(8,128)(2,1)S(1)}, bf16[96,512]{1,0:T(8,128)(2,1)S(1)}, u32[]{:S(2)}, u32[]{:S(2)}) collective-permute-start(bf16[96,512]{1,0:T(8,128)(2,1)S(1)} %get-tuple-element.60), channel_id=1, source_target_pairs={{0,8},{2,10},{4,12},{6,14},{8,0},{10,2},{12,4},{14,6},{1,9},{3,11}... | collective-permute-start | bytes 294920 | tf_op jit(solution)/shard_map/ppermute | solution.py:347
  19.0 4.5 %collective-permute-start.7 = (bf16[96,512]{1,0:T(8,128)(2,1)S(1)}, bf16[96,512]{1,0:T(8,128)(2,1)S(1)}, u32[]{:S(2)}, u32[]{:S(2)}) collective-permute-start(bf16[96,512]{1,0:T(8,128)(2,1)S(1)} %get-tuple-element.61), channel_id=1, source_target_pairs={{0,10},{2,12},{4,14},{6,0},{8,2},{10,4},{12,6},{14,8},{1,11},{3,13... | collective-permute-start | bytes 294920 | tf_op jit(solution)/shard_map/ppermute | solution.py:347
  23.4 3.6 %collective-permute-done.5 = bf16[96,512]{1,0:T(8,128)(2,1)} collective-permute-done((bf16[96,512]{1,0:T(8,128)(2,1)S(1)}, bf16[96,512]{1,0:T(8,128)(2,1)}, u32[]{:S(2)}, u32[]{:S(2)}) %collective-permute-start.5) | collective-permute-done | bytes 98336 | tf_op jit(solution)/shard_map/ppermute | solution.py:347
  27.0 5.9 %all-to-all-start = ((bf16[16,128,256]{2,1,0:T(8,128)(2,1)}), bf16[16,128,256]{2,1,0:T(8,128)(2,1)}, u32[]{:S(2)}, u32[]{:S(2)}) async-start(bf16[16,128,256]{2,1,0:T(8,128)(2,1)} %shard_map.57), calls=%async_computation | async-start | bytes 2097152 | tf_op jit(solution)/shard_map/all_to_all | solution.py:360
  36.9 1.8 %shard_map.58 = (bf16[1024,512]{1,0:T(8,128)(2,1)S(1)}, bf16[1024,256]{1,0:T(8,128)(2,1)S(1)}) custom-call(s32[3]{0:T(128)S(1)} %pad_add_fusion.me_ref, bf16[8,96,512]{2,1,0:T(8,128)(2,1)S(1)} %bitcast_dynamic-update-slice_fusion.8.own, bf16[8,96,512]{2,1,0:T(8,128)(2,1)S(1)} %collective-permute-done.9.other), custom_call_target="tpu_custom_call" | custom-call | bytes 6291456 | tf_op jit(solution)/shard_map/pallas_call | solution.py:173
  38.8 14.4 %collective-permute-done.8.own_hbm = bf16[8,96,512]{2,1,0:T(8,128)(2,1)S(1)} collective-permute-done((bf16[8,96,512]{2,1,0:T(8,128)(2,1)S(1)}, bf16[8,96,512]{2,1,0:T(8,128)(2,1)S(1)}, u32[]{:S(2)}, u32[]{:S(2)}) %collective-permute-start.8) | collective-permute-done | bytes 786464 | tf_op jit(solution)/shard_map/ppermute | solution.py:338
  54.3 3.4 %collective-permute-start = (bf16[96,512]{1,0:T(8,128)(2,1)S(1)}, bf16[96,512]{1,0:T(8,128)(2,1)S(1)}, u32[]{:S(2)}, u32[]{:S(2)}) collective-permute-start(bf16[96,512]{1,0:T(8,128)(2,1)S(1)} %get-tuple-element.50), channel_id=1, source_target_pairs={{0,6},{2,8},{4,10},{6,12},{8,14},{10,0},{12,2},{14,4},{1,7},{3,9},... | collective-permute-start | bytes 294920 | tf_op jit(solution)/shard_map/ppermute | solution.py:347
  58.9 2.2 %all-to-all-done.q_hbm = bf16[16,128,256]{2,1,0:T(8,128)(2,1)} async-done(((bf16[16,128,256]{2,1,0:T(8,128)(2,1)}), bf16[16,128,256]{2,1,0:T(8,128)(2,1)}, u32[]{:S(2)}, u32[]{:S(2)}) %all-to-all-start) | async-done | bytes 1048608 | tf_op jit(solution)/shard_map/all_to_all | solution.py:360
  61.1 5.9 %shard_map.59 = f32[8,32,1536]{2,1,0:T(8,128)} custom-call(s32[3]{0:T(128)S(1)} %pad_add_fusion.me_ref, bf16[16,128,256]{2,1,0:T(8,128)(2,1)} %all-to-all-done.q_hbm, bf16[1024,512]{1,0:T(8,128)(2,1)S(1)} %get-tuple-element.71.kf_hbm, bf16[1024,256]{1,0:T(8,128)(2,1)S(1)} %get-tuple-element.72.kh_hbm, bf16[8,96,512]{2,1,0:T(8,128)(2,1)} %copy-done.7, ...), custom_call_target="tpu_custom_call" | custom-call | tf_op jit(solution)/shard_map/pallas_call | solution.py:209
  67.5 6.6 %all-to-all-start.1 = ((f32[8,32,1536]{2,1,0:T(8,128)}), f32[8,32,1536]{2,1,0:T(8,128)S(1)}, u32[]{:S(2)}, u32[]{:S(2)}) async-start(f32[8,32,1536]{2,1,0:T(8,128)} %shard_map.59), calls=%async_computation.1 | async-start | bytes 3145728 | tf_op jit(solution)/shard_map/all_to_all | solution.py:369
  74.2 4.5 %collective-permute-start.12 = (bf16[96,512]{1,0:T(8,128)(2,1)S(1)}, bf16[96,512]{1,0:T(8,128)(2,1)S(1)}, u32[]{:S(2)}, u32[]{:S(2)}) collective-permute-start(bf16[96,512]{1,0:T(8,128)(2,1)S(1)} %get-tuple-element.75), channel_id=1, source_target_pairs={{0,2},{2,4},{4,6},{6,8},{8,10},{10,12},{12,14},{14,0},{1,3},{3,5},... | collective-permute-start | bytes 294920 | tf_op jit(solution)/shard_map/ppermute | solution.py:347
  80.3 1.9 %collective-permute-start.15 = (bf16[96,512]{1,0:T(8,128)(2,1)S(1)}, bf16[96,512]{1,0:T(8,128)(2,1)S(1)}, u32[]{:S(2)}, u32[]{:S(2)}) collective-permute-start(bf16[96,512]{1,0:T(8,128)(2,1)S(1)} %get-tuple-element.80), channel_id=1, source_target_pairs={{0,12},{2,14},{4,0},{6,2},{8,4},{10,6},{12,8},{14,10},{1,13},{3,15... | collective-permute-start | bytes 294920 | tf_op jit(solution)/shard_map/ppermute | solution.py:347
  85.0 2.8 %collective-permute-done.14 = bf16[96,512]{1,0:T(8,128)(2,1)S(1)} collective-permute-done((bf16[96,512]{1,0:T(8,128)(2,1)S(1)}, bf16[96,512]{1,0:T(8,128)(2,1)S(1)}, u32[]{:S(2)}, u32[]{:S(2)}) %collective-permute-start.14) | collective-permute-done | bytes 98336 | tf_op jit(solution)/shard_map/ppermute | solution.py:347
  87.9 5.6 %collective-permute-done.15 = bf16[96,512]{1,0:T(8,128)(2,1)S(1)} collective-permute-done((bf16[96,512]{1,0:T(8,128)(2,1)S(1)}, bf16[96,512]{1,0:T(8,128)(2,1)S(1)}, u32[]{:S(2)}, u32[]{:S(2)}) %collective-permute-start.15) | collective-permute-done | bytes 98336 | tf_op jit(solution)/shard_map/ppermute | solution.py:347
  93.9 2.3 %all-to-all-done.1.parts = f32[8,32,1536]{2,1,0:T(8,128)S(1)} async-done(((f32[8,32,1536]{2,1,0:T(8,128)}), f32[8,32,1536]{2,1,0:T(8,128)S(1)}, u32[]{:S(2)}, u32[]{:S(2)}) %all-to-all-start.1) | async-done | bytes 1572896 | tf_op jit(solution)/shard_map/all_to_all | solution.py:369
  96.3 4.6 %collective-permute-start.20 = (f32[32,512]{1,0:T(8,128)S(1)}, f32[32,512]{1,0:T(8,128)S(1)}, u32[]{:S(2)}, u32[]{:S(2)}) collective-permute-start(f32[32,512]{1,0:T(8,128)S(1)} %get-tuple-element.86.half), channel_id=1, source_target_pairs={{0,2},{2,0},{4,6},{6,4},{8,10},{10,8},{12,14},{14,12},{1,3},{3,1},... | collective-permute-start | bytes 196616 | tf_op jit(solution)/shard_map/ppermute | solution.py:338
  100.9 2.0 %collective-permute-done.20.other = f32[32,512]{1,0:T(8,128)S(1)} collective-permute-done((f32[32,512]{1,0:T(8,128)S(1)}, f32[32,512]{1,0:T(8,128)S(1)}, u32[]{:S(2)}, u32[]{:S(2)}) %collective-permute-start.20) | collective-permute-done | bytes 65568 | tf_op jit(solution)/shard_map/ppermute | solution.py:338
  104.1 3.7 %all-to-all-start.2 = ((bf16[8,2,32,1024]{3,2,1,0:T(8,128)(2,1)}), bf16[8,2,32,1024]{3,2,1,0:T(8,128)(2,1)S(1)}, u32[]{:S(2)}, u32[]{:S(2)}) async-start(bf16[8,2,32,1024]{3,2,1,0:T(8,128)(2,1)} %shard_map.62), calls=%async_computation.2 | async-start | bytes 2097152 | tf_op jit(solution)/shard_map/all_to_all | solution.py:375
  107.8 2.2 %collective-permute-start.18 = (bf16[8,96,512]{2,1,0:T(8,128)(2,1)S(1)}, bf16[8,96,512]{2,1,0:T(8,128)(2,1)S(1)}, u32[]{:S(2)}, u32[]{:S(2)}) collective-permute-start(bf16[8,96,512]{2,1,0:T(8,128)(2,1)S(1)} %bitcast_dynamic-update-slice_fusion.refs_0_), channel_id=1, source_target_pairs={{0,16},{16,0},{1,17},{17,1},{2,18},{18,2},{3,19},{19,3},{4,20},{20... | collective-permute-start | bytes 2359304 | tf_op jit(solution)/shard_map/ppermute | solution.py:338
  110.0 2.1 %collective-permute-done.17.refs_1_ = bf16[8,96,512]{2,1,0:T(8,128)(2,1)S(1)} collective-permute-done((bf16[8,96,512]{2,1,0:T(8,128)(2,1)S(1)}, bf16[8,96,512]{2,1,0:T(8,128)(2,1)S(1)}, u32[]{:S(2)}, u32[]{:S(2)}) %collective-permute-start.17) | collective-permute-done | bytes 786464 | tf_op jit(solution)/shard_map/ppermute | solution.py:338
  112.1 2.5 %collective-permute-start.19 = (bf16[8,96,512]{2,1,0:T(8,128)(2,1)S(1)}, bf16[8,96,512]{2,1,0:T(8,128)(2,1)S(1)}, u32[]{:S(2)}, u32[]{:S(2)}) collective-permute-start(bf16[8,96,512]{2,1,0:T(8,128)(2,1)S(1)} %collective-permute-done.17.refs_1_), channel_id=1, source_target_pairs={{0,16},{16,0},{1,17},{17,1},{2,18},{18,2},{3,19},{19,3},{4,20},{20... | collective-permute-start | bytes 2359304 | tf_op jit(solution)/shard_map/ppermute | solution.py:338
  114.7 1.9 %collective-permute-done.19.refs_3_ = bf16[8,96,512]{2,1,0:T(8,128)(2,1)S(1)} collective-permute-done((bf16[8,96,512]{2,1,0:T(8,128)(2,1)S(1)}, bf16[8,96,512]{2,1,0:T(8,128)(2,1)S(1)}, u32[]{:S(2)}, u32[]{:S(2)}) %collective-permute-start.19) | collective-permute-done | bytes 786464 | tf_op jit(solution)/shard_map/ppermute | solution.py:338
  116.6 4.5 %shard_map.60 = (bf16[1024,1024]{1,0:T(8,128)(2,1)S(1)}, bf16[512,1024]{1,0:T(8,128)(2,1)S(1)}) custom-call(s32[3]{0:T(128)S(1)} %pad_add_fusion.me_ref, bf16[8,96,512]{2,1,0:T(8,128)(2,1)} %copy-done.5, bf16[8,96,512]{2,1,0:T(8,128)(2,1)} %copy-done.6, bf16[8,96,512]{2,1,0:T(8,128)(2,1)S(1)} %collective-permute-done.18.refs_2_, ...), custom_call_target="tpu_custom_call" | custom-call | bytes 6291456 | tf_op jit(solution)/shard_map/pallas_call | solution.py:282
  122.0 5.4 %all-to-all-done.2.p_ref = bf16[8,2,32,1024]{3,2,1,0:T(8,128)(2,1)S(1)} async-done(((bf16[8,2,32,1024]{3,2,1,0:T(8,128)(2,1)}), bf16[8,2,32,1024]{3,2,1,0:T(8,128)(2,1)S(1)}, u32[]{:S(2)}, u32[]{:S(2)}) %all-to-all-start.2) | async-done | bytes 1048608 | tf_op jit(solution)/shard_map/all_to_all | solution.py:375
  128.6 1.9 %shard_map.63 = bf16[16,96,256]{2,1,0:T(8,128)(2,1)S(1)} custom-call(s32[3]{0:T(128)S(1)} %pad_add_fusion.me_ref, bf16[1024,1024]{1,0:T(8,128)(2,1)S(1)} %get-tuple-element.82.vf, bf16[512,1024]{1,0:T(8,128)(2,1)S(1)} %copy-done.3, bf16[8,2,32,1024]{3,2,1,0:T(8,128)(2,1)S(1)} %all-to-all-done.2.p_ref), custom_call_target="tpu_custom_call" | custom-call | tf_op jit(solution)/shard_map/pallas_call | solution.py:307
  130.5 29.2 %all_to_all.20.m_ref = bf16[16,96,256]{2,1,0:T(8,128)(2,1)S(1)} all-to-all(bf16[16,96,256]{2,1,0:T(8,128)(2,1)S(1)} %shard_map.63), channel_id=1, replica_groups=mesh['y'=4,'xh'=2,'c'=2,'z'=8,'xl'=2] {'z','c'}, dimensions={0} | all-to-all | bytes 1572864 | tf_op jit(solution)/shard_map/all_to_all | solution.py:377
  159.7 1.7 %shard_map.64 = bf16[8,64,768]{2,1,0:T(8,128)(2,1)} custom-call(bf16[16,96,256]{2,1,0:T(8,128)(2,1)S(1)} %all_to_all.20.m_ref, bf16[768,768]{1,0:T(8,128)(2,1)S(1)} %copy-done.1), custom_call_target="tpu_custom_call" | custom-call | tf_op jit(solution)/shard_map/pallas_call | solution.py:327
  (60 shorter events, 15.5 us)
Async XLA Ops:
  0.0 13.5 %copy-start = (bf16[768,768]{1,0:T(8,128)(2,1)S(1)}, bf16[768,768]{1,0:T(8,128)(2,1)}, u32[]{:S(2)}) copy-start(bf16[768,768]{1,0:T(8,128)(2,1)} %w_ref.4) | copy-start | bytes 3538948
  3.1 12.3 %collective-permute-start.1 = (bf16[96,512]{1,0:T(8,128)(2,1)S(1)}, bf16[96,512]{1,0:T(8,128)(2,1)S(1)}, u32[]{:S(2)}, u32[]{:S(2)}) collective-permute-start(bf16[96,512]{1,0:T(8,128)(2,1)S(1)} %get-tuple-element.52), channel_id=1, source_target_pairs={{0,2},{2,4},{4,6},{6,8},{8,10},{10,12},{12,14},{14,0},{1,3},{3,5},... | collective-permute-start | bytes 294920 | tf_op jit(solution)/shard_map/ppermute | solution.py:347
  5.6 13.4 %collective-permute-start.2 = (bf16[96,512]{1,0:T(8,128)(2,1)S(1)}, bf16[96,512]{1,0:T(8,128)(2,1)S(1)}, u32[]{:S(2)}, u32[]{:S(2)}) collective-permute-start(bf16[96,512]{1,0:T(8,128)(2,1)S(1)} %get-tuple-element.53), channel_id=1, source_target_pairs={{0,14},{2,0},{4,2},{6,4},{8,6},{10,8},{12,10},{14,12},{1,15},{3,1}... | collective-permute-start | bytes 294920 | tf_op jit(solution)/shard_map/ppermute | solution.py:347
  9.6 13.8 %collective-permute-start.3 = (bf16[96,512]{1,0:T(8,128)(2,1)S(1)}, bf16[96,512]{1,0:T(8,128)(2,1)S(1)}, u32[]{:S(2)}, u32[]{:S(2)}) collective-permute-start(bf16[96,512]{1,0:T(8,128)(2,1)S(1)} %get-tuple-element.54), channel_id=1, source_target_pairs={{0,4},{2,6},{4,8},{6,10},{8,12},{10,14},{12,0},{14,2},{1,5},{3,7},... | collective-permute-start | bytes 294920 | tf_op jit(solution)/shard_map/ppermute | solution.py:347
  9.6 13.8 %collective-permute-start.4 = (bf16[96,512]{1,0:T(8,128)(2,1)S(1)}, bf16[96,512]{1,0:T(8,128)(2,1)S(1)}, u32[]{:S(2)}, u32[]{:S(2)}) collective-permute-start(bf16[96,512]{1,0:T(8,128)(2,1)S(1)} %get-tuple-element.55), channel_id=1, source_target_pairs={{0,12},{2,14},{4,0},{6,2},{8,4},{10,6},{12,8},{14,10},{1,13},{3,15... | collective-permute-start | bytes 294920 | tf_op jit(solution)/shard_map/ppermute | solution.py:347
  13.2 13.8 %collective-permute-start.5 = (bf16[96,512]{1,0:T(8,128)(2,1)S(1)}, bf16[96,512]{1,0:T(8,128)(2,1)}, u32[]{:S(2)}, u32[]{:S(2)}) collective-permute-start(bf16[96,512]{1,0:T(8,128)(2,1)S(1)} %get-tuple-element.56), channel_id=1, source_target_pairs={{0,6},{2,8},{4,10},{6,12},{8,14},{10,0},{12,2},{14,4},{1,7},{3,9},... | collective-permute-start | bytes 294920 | tf_op jit(solution)/shard_map/ppermute | solution.py:347
  15.4 18.6 %collective-permute-start.6 = (bf16[96,512]{1,0:T(8,128)(2,1)S(1)}, bf16[96,512]{1,0:T(8,128)(2,1)S(1)}, u32[]{:S(2)}, u32[]{:S(2)}) collective-permute-start(bf16[96,512]{1,0:T(8,128)(2,1)S(1)} %get-tuple-element.60), channel_id=1, source_target_pairs={{0,8},{2,10},{4,12},{6,14},{8,0},{10,2},{12,4},{14,6},{1,9},{3,11}... | collective-permute-start | bytes 294920 | tf_op jit(solution)/shard_map/ppermute | solution.py:347
  19.0 15.0 %collective-permute-start.7 = (bf16[96,512]{1,0:T(8,128)(2,1)S(1)}, bf16[96,512]{1,0:T(8,128)(2,1)S(1)}, u32[]{:S(2)}, u32[]{:S(2)}) collective-permute-start(bf16[96,512]{1,0:T(8,128)(2,1)S(1)} %get-tuple-element.61), channel_id=1, source_target_pairs={{0,10},{2,12},{4,14},{6,0},{8,2},{10,4},{12,6},{14,8},{1,11},{3,13... | collective-permute-start | bytes 294920 | tf_op jit(solution)/shard_map/ppermute | solution.py:347
  27.0 34.1 %all-to-all-start = ((bf16[16,128,256]{2,1,0:T(8,128)(2,1)}), bf16[16,128,256]{2,1,0:T(8,128)(2,1)}, u32[]{:S(2)}, u32[]{:S(2)}) async-start(bf16[16,128,256]{2,1,0:T(8,128)(2,1)} %shard_map.57), calls=%async_computation | async-start | bytes 2097152 | tf_op jit(solution)/shard_map/all_to_all | solution.py:360
  33.0 2.6 %copy-start.4 = (bf16[768,768]{1,0:T(8,128)(2,1)S(1)}, bf16[768,768]{1,0:T(8,128)(2,1)}, u32[]{:S(2)}) copy-start(bf16[768,768]{1,0:T(8,128)(2,1)} %w_ref.3) | copy-start | bytes 3538948
  34.1 2.9 %collective-permute-start.9 = (bf16[8,96,512]{2,1,0:T(8,128)(2,1)S(1)}, bf16[8,96,512]{2,1,0:T(8,128)(2,1)S(1)}, u32[]{:S(2)}, u32[]{:S(2)}) collective-permute-start(bf16[8,96,512]{2,1,0:T(8,128)(2,1)S(1)} %bitcast_dynamic-update-slice_fusion.8.own), channel_id=1, source_target_pairs={{0,16},{16,0},{1,17},{17,1},{2,18},{18,2},{3,19},{19,3},{4,20},{20... | collective-permute-start | bytes 2359304 | tf_op jit(solution)/shard_map/ppermute | solution.py:338
  34.3 18.9 %collective-permute-start.8 = (bf16[8,96,512]{2,1,0:T(8,128)(2,1)S(1)}, bf16[8,96,512]{2,1,0:T(8,128)(2,1)S(1)}, u32[]{:S(2)}, u32[]{:S(2)}) collective-permute-start(bf16[8,96,512]{2,1,0:T(8,128)(2,1)S(1)} %bitcast_dynamic-update-slice_fusion.8.own), channel_id=1, source_target_pairs={{0,1},{1,0},{2,3},{3,2},{4,5},{5,4},{6,7},{7,6},{8,9},{9,8},{10,11... | collective-permute-start | bytes 2359304 | tf_op jit(solution)/shard_map/ppermute | solution.py:338
  53.2 5.7 %copy-start.7 = (bf16[8,96,512]{2,1,0:T(8,128)(2,1)}, bf16[8,96,512]{2,1,0:T(8,128)(2,1)S(1)}, u32[]{:S(2)}) copy-start(bf16[8,96,512]{2,1,0:T(8,128)(2,1)S(1)} %collective-permute-done.8.own_hbm) | copy-start | bytes 2359300
  53.2 5.7 %collective-permute-start.11 = (bf16[8,96,512]{2,1,0:T(8,128)(2,1)S(1)}, bf16[8,96,512]{2,1,0:T(8,128)(2,1)S(1)}, u32[]{:S(2)}, u32[]{:S(2)}) collective-permute-start(bf16[8,96,512]{2,1,0:T(8,128)(2,1)S(1)} %collective-permute-done.8.own_hbm), channel_id=1, source_target_pairs={{0,16},{16,0},{1,17},{17,1},{2,18},{18,2},{3,19},{19,3},{4,20},{20... | collective-permute-start | bytes 2359304 | tf_op jit(solution)/shard_map/ppermute | solution.py:338
  54.3 13.3 %collective-permute-start = (bf16[96,512]{1,0:T(8,128)(2,1)S(1)}, bf16[96,512]{1,0:T(8,128)(2,1)S(1)}, u32[]{:S(2)}, u32[]{:S(2)}) collective-permute-start(bf16[96,512]{1,0:T(8,128)(2,1)S(1)} %get-tuple-element.50), channel_id=1, source_target_pairs={{0,6},{2,8},{4,10},{6,12},{8,14},{10,0},{12,2},{14,4},{1,7},{3,9},... | collective-permute-start | bytes 294920 | tf_op jit(solution)/shard_map/ppermute | solution.py:347
  57.7 9.9 %collective-permute-start.10 = (bf16[96,512]{1,0:T(8,128)(2,1)S(1)}, bf16[96,512]{1,0:T(8,128)(2,1)S(1)}, u32[]{:S(2)}, u32[]{:S(2)}) collective-permute-start(bf16[96,512]{1,0:T(8,128)(2,1)S(1)} %get-tuple-element.67), channel_id=1, source_target_pairs={{0,10},{2,12},{4,14},{6,0},{8,2},{10,4},{12,6},{14,8},{1,11},{3,13... | collective-permute-start | bytes 294920 | tf_op jit(solution)/shard_map/ppermute | solution.py:347
  67.5 28.7 %all-to-all-start.1 = ((f32[8,32,1536]{2,1,0:T(8,128)}), f32[8,32,1536]{2,1,0:T(8,128)S(1)}, u32[]{:S(2)}, u32[]{:S(2)}) async-start(f32[8,32,1536]{2,1,0:T(8,128)} %shard_map.59), calls=%async_computation.1 | async-start | bytes 3145728 | tf_op jit(solution)/shard_map/all_to_all | solution.py:369
  74.2 9.1 %collective-permute-start.12 = (bf16[96,512]{1,0:T(8,128)(2,1)S(1)}, bf16[96,512]{1,0:T(8,128)(2,1)S(1)}, u32[]{:S(2)}, u32[]{:S(2)}) collective-permute-start(bf16[96,512]{1,0:T(8,128)(2,1)S(1)} %get-tuple-element.75), channel_id=1, source_target_pairs={{0,2},{2,4},{4,6},{6,8},{8,10},{10,12},{12,14},{14,0},{1,3},{3,5},... | collective-permute-start | bytes 294920 | tf_op jit(solution)/shard_map/ppermute | solution.py:347
  78.6 6.4 %collective-permute-start.13 = (bf16[96,512]{1,0:T(8,128)(2,1)S(1)}, bf16[96,512]{1,0:T(8,128)(2,1)S(1)}, u32[]{:S(2)}, u32[]{:S(2)}) collective-permute-start(bf16[96,512]{1,0:T(8,128)(2,1)S(1)} %get-tuple-element.76), channel_id=1, source_target_pairs={{0,4},{2,6},{4,8},{6,10},{8,12},{10,14},{12,0},{14,2},{1,5},{3,7},... | collective-permute-start | bytes 294920 | tf_op jit(solution)/shard_map/ppermute | solution.py:347
  78.6 9.2 %collective-permute-start.14 = (bf16[96,512]{1,0:T(8,128)(2,1)S(1)}, bf16[96,512]{1,0:T(8,128)(2,1)S(1)}, u32[]{:S(2)}, u32[]{:S(2)}) collective-permute-start(bf16[96,512]{1,0:T(8,128)(2,1)S(1)} %get-tuple-element.78), channel_id=1, source_target_pairs={{0,8},{2,10},{4,12},{6,14},{8,0},{10,2},{12,4},{14,6},{1,9},{3,11}... | collective-permute-start | bytes 294920 | tf_op jit(solution)/shard_map/ppermute | solution.py:347
  80.3 13.2 %collective-permute-start.15 = (bf16[96,512]{1,0:T(8,128)(2,1)S(1)}, bf16[96,512]{1,0:T(8,128)(2,1)S(1)}, u32[]{:S(2)}, u32[]{:S(2)}) collective-permute-start(bf16[96,512]{1,0:T(8,128)(2,1)S(1)} %get-tuple-element.80), channel_id=1, source_target_pairs={{0,12},{2,14},{4,0},{6,2},{8,4},{10,6},{12,8},{14,10},{1,13},{3,15... | collective-permute-start | bytes 294920 | tf_op jit(solution)/shard_map/ppermute | solution.py:347
  82.2 11.3 %collective-permute-start.16 = (bf16[96,512]{1,0:T(8,128)(2,1)S(1)}, bf16[96,512]{1,0:T(8,128)(2,1)S(1)}, u32[]{:S(2)}, u32[]{:S(2)}) collective-permute-start(bf16[96,512]{1,0:T(8,128)(2,1)S(1)} %get-tuple-element.81), channel_id=1, source_target_pairs={{0,14},{2,0},{4,2},{6,4},{8,6},{10,8},{12,10},{14,12},{1,15},{3,1}... | collective-permute-start | bytes 294920 | tf_op jit(solution)/shard_map/ppermute | solution.py:347
  93.5 14.3 %copy-start.5 = (bf16[8,96,512]{2,1,0:T(8,128)(2,1)}, bf16[8,96,512]{2,1,0:T(8,128)(2,1)S(1)}, u32[]{:S(2)}) copy-start(bf16[8,96,512]{2,1,0:T(8,128)(2,1)S(1)} %bitcast_dynamic-update-slice_fusion.refs_0_) | copy-start | bytes 2359300
  93.5 18.6 %collective-permute-start.17 = (bf16[8,96,512]{2,1,0:T(8,128)(2,1)S(1)}, bf16[8,96,512]{2,1,0:T(8,128)(2,1)S(1)}, u32[]{:S(2)}, u32[]{:S(2)}) collective-permute-start(bf16[8,96,512]{2,1,0:T(8,128)(2,1)S(1)} %bitcast_dynamic-update-slice_fusion.refs_0_), channel_id=1, source_target_pairs={{0,1},{1,0},{2,3},{3,2},{4,5},{5,4},{6,7},{7,6},{8,9},{9,8},{10,11... | collective-permute-start | bytes 2359304 | tf_op jit(solution)/shard_map/ppermute | solution.py:338
  96.3 6.5 %collective-permute-start.20 = (f32[32,512]{1,0:T(8,128)S(1)}, f32[32,512]{1,0:T(8,128)S(1)}, u32[]{:S(2)}, u32[]{:S(2)}) collective-permute-start(f32[32,512]{1,0:T(8,128)S(1)} %get-tuple-element.86.half), channel_id=1, source_target_pairs={{0,2},{2,0},{4,6},{6,4},{8,10},{10,8},{12,14},{14,12},{1,3},{3,1},... | collective-permute-start | bytes 196616 | tf_op jit(solution)/shard_map/ppermute | solution.py:338
  104.1 23.3 %all-to-all-start.2 = ((bf16[8,2,32,1024]{3,2,1,0:T(8,128)(2,1)}), bf16[8,2,32,1024]{3,2,1,0:T(8,128)(2,1)S(1)}, u32[]{:S(2)}, u32[]{:S(2)}) async-start(bf16[8,2,32,1024]{3,2,1,0:T(8,128)(2,1)} %shard_map.62), calls=%async_computation.2 | async-start | bytes 2097152 | tf_op jit(solution)/shard_map/all_to_all | solution.py:375
  107.8 6.9 %collective-permute-start.18 = (bf16[8,96,512]{2,1,0:T(8,128)(2,1)S(1)}, bf16[8,96,512]{2,1,0:T(8,128)(2,1)S(1)}, u32[]{:S(2)}, u32[]{:S(2)}) collective-permute-start(bf16[8,96,512]{2,1,0:T(8,128)(2,1)S(1)} %bitcast_dynamic-update-slice_fusion.refs_0_), channel_id=1, source_target_pairs={{0,16},{16,0},{1,17},{17,1},{2,18},{18,2},{3,19},{19,3},{4,20},{20... | collective-permute-start | bytes 2359304 | tf_op jit(solution)/shard_map/ppermute | solution.py:338
  112.1 2.5 %copy-start.6 = (bf16[8,96,512]{2,1,0:T(8,128)(2,1)}, bf16[8,96,512]{2,1,0:T(8,128)(2,1)S(1)}, u32[]{:S(2)}) copy-start(bf16[8,96,512]{2,1,0:T(8,128)(2,1)S(1)} %collective-permute-done.17.refs_1_) | copy-start | bytes 2359300
  112.1 4.5 %collective-permute-start.19 = (bf16[8,96,512]{2,1,0:T(8,128)(2,1)S(1)}, bf16[8,96,512]{2,1,0:T(8,128)(2,1)S(1)}, u32[]{:S(2)}, u32[]{:S(2)}) collective-permute-start(bf16[8,96,512]{2,1,0:T(8,128)(2,1)S(1)} %collective-permute-done.17.refs_1_), channel_id=1, source_target_pairs={{0,16},{16,0},{1,17},{17,1},{2,18},{18,2},{3,19},{19,3},{4,20},{20... | collective-permute-start | bytes 2359304 | tf_op jit(solution)/shard_map/ppermute | solution.py:338
  121.0 1.0 copy-start.2
  127.4 1.2 copy-start.3
  130.5 29.2 %copy-start.1 = (bf16[768,768]{1,0:T(8,128)(2,1)S(1)}, bf16[768,768]{1,0:T(8,128)(2,1)}, u32[]{:S(2)}) copy-start(bf16[768,768]{1,0:T(8,128)(2,1)} %w_ref.5) | copy-start | bytes 3538948

commit v14 on v13

--- a/solution.py
+++ b/solution.py
@@ -281,7 +281,10 @@
 def values_laid(me, vs):
     return pl.pallas_call(
         values_kernel,
-        out_shape=tuple(jax.ShapeDtypeStruct((2 * ROWS * n, KEYS), bf16) for n in (FULL, HALF)),
+        out_shape=(
+            jax.ShapeDtypeStruct((2 * ROWS * FULL, KEYS), bf16),
+            pltpu.HBM((2 * ROWS * HALF, KEYS), bf16),
+        ),
         in_specs=[SMEM] + [ANY] * 4,
         out_specs=(VMEM,) * 2,
         scratch_shapes=[pltpu.VMEM(v.shape, bf16) for v in vs] + [pltpu.SemaphoreType.DMA((4,))],
@@ -290,9 +293,12 @@
     )(me, *in_hbm(*vs[:2]), *vs[2:])
 
 
-def mix_kernel(me_ref, vf, vh, p_ref, o_ref):
+def mix_kernel(me_ref, vf, vh_hbm, p_ref, o_ref, vh, sems):
     core = me_ref[1]
+    copy = fetches((vh_hbm,), (vh,), sems)[0]
     for i, (v, first, n) in enumerate(((vf, 0, FULL), (vh, FULL, HALF))):
+        if i == 1:
+            copy.wait()
         probs = p_ref[:, i].reshape(QUERIES, KEYS)
         for cr in range(2):
             c = jnp.bitwise_xor(core, cr)
@@ -304,13 +310,15 @@
 
 
 def mix(me, laid, probs):
+    whole, shared = laid
     return pl.pallas_call(
         mix_kernel,
         out_shape=jax.ShapeDtypeStruct((2 * Z, CHUNK, ROWS * SUB), bf16),
-        in_specs=[SMEM] + [VMEM] * 3,
-        out_specs=VMEM,
-        compiler_params=PARAMS,
-    )(me, *laid, probs)
+        in_specs=[SMEM, VMEM, ANY, VMEM],
+        out_specs=VMEM,
+        scratch_shapes=[pltpu.VMEM(shared.shape, bf16), pltpu.SemaphoreType.DMA((1,))],
+        compiler_params=PARAMS,
+    )(me, whole, *in_hbm(shared), probs)
 
 
 def final_kernel(m_ref, w_ref, o_ref, t_ref):
@@ -362,12 +370,12 @@
     k = jnp.stack(k)
     near, shared = keys_laid(me, k, flip(k, "c", 2, 1))
     k_far, v[4], shared = lax.optimization_barrier((flip(k, "xl", 2, 1), v[4], shared))
-    for s in (3, 5):
+    for s in (2, 6):
         v[s] = shift(v[s], s)
     scores = score(me, q, (near, shared), k_far, flip(k_far, "c", 2, 1))
     *v, scores = lax.optimization_barrier((*v, scores))
     parts = lax.all_to_all(scores, ("y", "xh"), 0, 0, tiled=True)
-    for s in (4, 2, 6, 1, 7):
+    for s in (4, 3, 5, 1, 7):
         v[s] = shift(v[s], s)
     full, half = total(parts)
     rows = ROWS * 2 * PEERS

time: 162 us -> 161 us (level)
  blocking collectives: 29.2 us -> 32.3 us
  local copies, waits for them, and re-layouts: 3.34 us -> 1.14 us
  waiting for transfers between devices: 44.4 us -> 42.2 us
    all_to_all x1, waiting for transfers between devices: 5.39 us -> 1.78 us  [local(): probs = lax.all_to_all(probs, ('y', 'xh'), 0, 0, tiled=True)]
    all_to_all x1, blocking collectives: 29.2 us -> 32.3 us  [local(): mixed = lax.all_to_all(mix(me, laid, probs), ('z', 'c'), 0, 0, tiled=True)]
    unnamed x30 -> x26, local copies, waits for them, and re-layouts: 3.32 us -> 1.12 us
    all_to_all x1, waiting for transfers between devices: 2.3 us -> 4.08 us  [local(): parts = lax.all_to_all(scores, ('y', 'xh'), 0, 0, tiled=True)]
    ppermute x14, starting transfers between devices: 32.3 us -> 30.6 us  [shift(): return lax.ppermute(x, 'z', [(i, (i + s) % Z) for i in range(Z)])]
  transfers between devices with their start and end apart: 24 -> 24, of which waited for: 12 -> 13; matrix products, arithmetic and copies ran while one was open for 1% -> 1% of each run, Pallas kernels for 10% -> 11%
where the time goes in v14:
time: 161 us; the launch traced here: 160 us
  starting transfers between devices  59.8 us (37%)
  waiting for transfers between devices  42.2 us (26%)
  blocking collectives  32.3 us (20%)
  Pallas kernels  24.8 us (15%)
    all_to_all x1, blocking collectives, local(): mixed = lax.all_to_all(mix(me, laid, probs), ('z', 'c'), 0, 0, tiled=True)  32.3 us
    ppermute x14, starting transfers between devices, shift(): return lax.ppermute(x, 'z', [(i, (i + s) % Z) for i in range(Z)])  30.6 us
    ppermute x7, waiting for transfers between devices, flip(): return lax.ppermute(x, axes, [(i, i ^ s) for i in range(n)])  19.8 us
    ppermute x14, waiting for transfers between devices, shift(): return lax.ppermute(x, 'z', [(i, (i + s) % Z) for i in range(Z)])  13.5 us
    ppermute x7, starting transfers between devices, flip(): return lax.ppermute(x, axes, [(i, i ^ s) for i in range(n)])  12.9 us
    all_to_all x1, starting transfers between devices, local(): parts = lax.all_to_all(scores, ('y', 'xh'), 0, 0, tiled=True)  6.65 us
    all_to_all x1, starting transfers between devices, local(): q = lax.all_to_all(q, ('z', 'c'), 0, 0, tiled=True)  5.95 us
    pallas_call x1, Pallas kernels, score(): pl.pallas_call(score_kernel, out_shape=jax.ShapeDtypeStruct((PEERS, SUB,...  5.92 us
  transfers between devices with their start and end apart: 24, of which 13 were waited for; matrix products, arithmetic and copies ran while one was open for 1% of the time, Pallas kernels for 11%

profile of v14, /device:TPU:1, one launch (start us, length us, event | category | flops | bytes accessed | tf_op | source)
XLA Modules:
  0.0 160.5 jit_solution(3004849937082541698)
XLA Ops:
  0.1 3.0 %shard_map.55 = (bf16[2,8,32,768]{3,2,1,0:T(8,128)(2,1)S(1)}, bf16[96,512]{1,0:T(8,128)(2,1)S(1)}, bf16[96,512]{1,0:T(8,128)(2,1)S(1)}, bf16[96,512]{1,0:T(8,128...) custom-call(s32[3]{0:T(128)S(1)} %pad_add_fusion.me_ref, ...), custom_call_target="tpu_custom_call" | custom-call | tf_op jit(solution)/shard_map/pallas_call | solution.py:97
  3.1 2.5 %collective-permute-start.1 = (bf16[96,512]{1,0:T(8,128)(2,1)S(1)}, bf16[96,512]{1,0:T(8,128)(2,1)S(1)}, u32[]{:S(2)}, u32[]{:S(2)}) collective-permute-start(bf16[96,512]{1,0:T(8,128)(2,1)S(1)} %get-tuple-element.52), channel_id=1, source_target_pairs={{0,2},{2,4},{4,6},{6,8},{8,10},{10,12},{12,14},{14,0},{1,3},{3,5},... | collective-permute-start | bytes 294920 | tf_op jit(solution)/shard_map/ppermute | solution.py:355
  5.6 4.0 %collective-permute-start.2 = (bf16[96,512]{1,0:T(8,128)(2,1)S(1)}, bf16[96,512]{1,0:T(8,128)(2,1)S(1)}, u32[]{:S(2)}, u32[]{:S(2)}) collective-permute-start(bf16[96,512]{1,0:T(8,128)(2,1)S(1)} %get-tuple-element.53), channel_id=1, source_target_pairs={{0,14},{2,0},{4,2},{6,4},{8,6},{10,8},{12,10},{14,12},{1,15},{3,1}... | collective-permute-start | bytes 294920 | tf_op jit(solution)/shard_map/ppermute | solution.py:355
  9.6 3.6 %collective-permute-start.4 = (bf16[96,512]{1,0:T(8,128)(2,1)S(1)}, bf16[96,512]{1,0:T(8,128)(2,1)S(1)}, u32[]{:S(2)}, u32[]{:S(2)}) collective-permute-start(bf16[96,512]{1,0:T(8,128)(2,1)S(1)} %get-tuple-element.55), channel_id=1, source_target_pairs={{0,12},{2,14},{4,0},{6,2},{8,4},{10,6},{12,8},{14,10},{1,13},{3,15... | collective-permute-start | bytes 294920 | tf_op jit(solution)/shard_map/ppermute | solution.py:355
  13.5 1.8 %shard_map.57 = bf16[16,128,256]{2,1,0:T(8,128)(2,1)} custom-call(bf16[2,8,32,768]{3,2,1,0:T(8,128)(2,1)S(1)} %get-tuple-element.46.n_ref, bf16[768,768]{1,0:T(8,128)(2,1)S(1)} %copy-done), custom_call_target="tpu_custom_call" | custom-call | flops 603979776 | bytes 2752512 | tf_op jit(solution)/shard_map/pallas_call | solution.py:124
  15.3 3.6 %collective-permute-start.6 = (bf16[96,512]{1,0:T(8,128)(2,1)S(1)}, bf16[96,512]{1,0:T(8,128)(2,1)S(1)}, u32[]{:S(2)}, u32[]{:S(2)}) collective-permute-start(bf16[96,512]{1,0:T(8,128)(2,1)S(1)} %get-tuple-element.60), channel_id=1, source_target_pairs={{0,8},{2,10},{4,12},{6,14},{8,0},{10,2},{12,4},{14,6},{1,9},{3,11}... | collective-permute-start | bytes 294920 | tf_op jit(solution)/shard_map/ppermute | solution.py:355
  19.0 4.5 %collective-permute-start.7 = (bf16[96,512]{1,0:T(8,128)(2,1)S(1)}, bf16[96,512]{1,0:T(8,128)(2,1)S(1)}, u32[]{:S(2)}, u32[]{:S(2)}) collective-permute-start(bf16[96,512]{1,0:T(8,128)(2,1)S(1)} %get-tuple-element.61), channel_id=1, source_target_pairs={{0,10},{2,12},{4,14},{6,0},{8,2},{10,4},{12,6},{14,8},{1,11},{3,13... | collective-permute-start | bytes 294920 | tf_op jit(solution)/shard_map/ppermute | solution.py:355
  23.4 3.6 %collective-permute-done.5 = bf16[96,512]{1,0:T(8,128)(2,1)} collective-permute-done((bf16[96,512]{1,0:T(8,128)(2,1)S(1)}, bf16[96,512]{1,0:T(8,128)(2,1)}, u32[]{:S(2)}, u32[]{:S(2)}) %collective-permute-start.5) | collective-permute-done | bytes 98336 | tf_op jit(solution)/shard_map/ppermute | solution.py:355
  27.0 5.9 %all-to-all-start = ((bf16[16,128,256]{2,1,0:T(8,128)(2,1)}), bf16[16,128,256]{2,1,0:T(8,128)(2,1)}, u32[]{:S(2)}, u32[]{:S(2)}) async-start(bf16[16,128,256]{2,1,0:T(8,128)(2,1)} %shard_map.57), calls=%async_computation | async-start | bytes 2097152 | tf_op jit(solution)/shard_map/all_to_all | solution.py:368
  36.9 1.8 %shard_map.58 = (bf16[1024,512]{1,0:T(8,128)(2,1)S(1)}, bf16[1024,256]{1,0:T(8,128)(2,1)S(1)}) custom-call(s32[3]{0:T(128)S(1)} %pad_add_fusion.me_ref, bf16[8,96,512]{2,1,0:T(8,128)(2,1)S(1)} %bitcast_dynamic-update-slice_fusion.8.own, bf16[8,96,512]{2,1,0:T(8,128)(2,1)S(1)} %collective-permute-done.9.other), custom_call_target="tpu_custom_call" | custom-call | bytes 6291456 | tf_op jit(solution)/shard_map/pallas_call | solution.py:173
  38.8 14.4 %collective-permute-done.8.own_hbm = bf16[8,96,512]{2,1,0:T(8,128)(2,1)S(1)} collective-permute-done((bf16[8,96,512]{2,1,0:T(8,128)(2,1)S(1)}, bf16[8,96,512]{2,1,0:T(8,128)(2,1)S(1)}, u32[]{:S(2)}, u32[]{:S(2)}) %collective-permute-start.8) | collective-permute-done | bytes 786464 | tf_op jit(solution)/shard_map/ppermute | solution.py:346
  54.3 2.5 %collective-permute-start = (bf16[96,512]{1,0:T(8,128)(2,1)S(1)}, bf16[96,512]{1,0:T(8,128)(2,1)S(1)}, u32[]{:S(2)}, u32[]{:S(2)}) collective-permute-start(bf16[96,512]{1,0:T(8,128)(2,1)S(1)} %get-tuple-element.49), channel_id=1, source_target_pairs={{0,4},{2,6},{4,8},{6,10},{8,12},{10,14},{12,0},{14,2},{1,5},{3,7},... | collective-permute-start | bytes 294920 | tf_op jit(solution)/shard_map/ppermute | solution.py:355
  58.0 3.0 %all-to-all-done.q_hbm = bf16[16,128,256]{2,1,0:T(8,128)(2,1)} async-done(((bf16[16,128,256]{2,1,0:T(8,128)(2,1)}), bf16[16,128,256]{2,1,0:T(8,128)(2,1)}, u32[]{:S(2)}, u32[]{:S(2)}) %all-to-all-start) | async-done | bytes 1048608 | tf_op jit(solution)/shard_map/all_to_all | solution.py:368
  61.0 5.9 %shard_map.59 = f32[8,32,1536]{2,1,0:T(8,128)} custom-call(s32[3]{0:T(128)S(1)} %pad_add_fusion.me_ref, bf16[16,128,256]{2,1,0:T(8,128)(2,1)} %all-to-all-done.q_hbm, bf16[1024,512]{1,0:T(8,128)(2,1)S(1)} %get-tuple-element.71.kf_hbm, bf16[1024,256]{1,0:T(8,128)(2,1)S(1)} %get-tuple-element.72.kh_hbm, bf16[8,96,512]{2,1,0:T(8,128)(2,1)} %copy-done.5, ...), custom_call_target="tpu_custom_call" | custom-call | tf_op jit(solution)/shard_map/pallas_call | solution.py:209
  67.0 6.7 %all-to-all-start.1 = ((f32[8,32,1536]{2,1,0:T(8,128)}), f32[8,32,1536]{2,1,0:T(8,128)S(1)}, u32[]{:S(2)}, u32[]{:S(2)}) async-start(f32[8,32,1536]{2,1,0:T(8,128)} %shard_map.59), calls=%async_computation.1 | async-start | bytes 3145728 | tf_op jit(solution)/shard_map/all_to_all | solution.py:377
  73.6 2.6 %collective-permute-start.13 = (bf16[96,512]{1,0:T(8,128)(2,1)S(1)}, bf16[96,512]{1,0:T(8,128)(2,1)S(1)}, u32[]{:S(2)}, u32[]{:S(2)}) collective-permute-start(bf16[96,512]{1,0:T(8,128)(2,1)S(1)} %get-tuple-element.77), channel_id=1, source_target_pairs={{0,6},{2,8},{4,10},{6,12},{8,14},{10,0},{12,2},{14,4},{1,7},{3,9},... | collective-permute-start | bytes 294920 | tf_op jit(solution)/shard_map/ppermute | solution.py:355
  76.3 3.0 %collective-permute-start.14 = (bf16[96,512]{1,0:T(8,128)(2,1)S(1)}, bf16[96,512]{1,0:T(8,128)(2,1)S(1)}, u32[]{:S(2)}, u32[]{:S(2)}) collective-permute-start(bf16[96,512]{1,0:T(8,128)(2,1)S(1)} %get-tuple-element.78), channel_id=1, source_target_pairs={{0,8},{2,10},{4,12},{6,14},{8,0},{10,2},{12,4},{14,6},{1,9},{3,11}... | collective-permute-start | bytes 294920 | tf_op jit(solution)/shard_map/ppermute | solution.py:355
  79.3 1.5 collective-permute-start.15
  82.3 2.2 %collective-permute-done.13 = bf16[96,512]{1,0:T(8,128)(2,1)S(1)} collective-permute-done((bf16[96,512]{1,0:T(8,128)(2,1)S(1)}, bf16[96,512]{1,0:T(8,128)(2,1)S(1)}, u32[]{:S(2)}, u32[]{:S(2)}) %collective-permute-start.13) | collective-permute-done | bytes 98336 | tf_op jit(solution)/shard_map/ppermute | solution.py:355
  84.6 4.6 %collective-permute-done.14 = bf16[96,512]{1,0:T(8,128)(2,1)S(1)} collective-permute-done((bf16[96,512]{1,0:T(8,128)(2,1)S(1)}, bf16[96,512]{1,0:T(8,128)(2,1)S(1)}, u32[]{:S(2)}, u32[]{:S(2)}) %collective-permute-start.14) | collective-permute-done | bytes 98336 | tf_op jit(solution)/shard_map/ppermute | solution.py:355
  89.2 1.7 %collective-permute-done.15 = bf16[96,512]{1,0:T(8,128)(2,1)S(1)} collective-permute-done((bf16[96,512]{1,0:T(8,128)(2,1)S(1)}, bf16[96,512]{1,0:T(8,128)(2,1)S(1)}, u32[]{:S(2)}, u32[]{:S(2)}) %collective-permute-start.15) | collective-permute-done | bytes 98336 | tf_op jit(solution)/shard_map/ppermute | solution.py:355
  92.3 4.1 %all-to-all-done.1.parts = f32[8,32,1536]{2,1,0:T(8,128)S(1)} async-done(((f32[8,32,1536]{2,1,0:T(8,128)}), f32[8,32,1536]{2,1,0:T(8,128)S(1)}, u32[]{:S(2)}, u32[]{:S(2)}) %all-to-all-start.1) | async-done | bytes 1572896 | tf_op jit(solution)/shard_map/all_to_all | solution.py:377
  96.6 3.4 %collective-permute-done.20.other = f32[32,512]{1,0:T(8,128)S(1)} collective-permute-done((f32[32,512]{1,0:T(8,128)S(1)}, f32[32,512]{1,0:T(8,128)S(1)}, u32[]{:S(2)}, u32[]{:S(2)}) %collective-permute-start.20) | collective-permute-done | bytes 65568 | tf_op jit(solution)/shard_map/ppermute | solution.py:346
  101.2 3.7 %all-to-all-start.2 = ((bf16[8,2,32,1024]{3,2,1,0:T(8,128)(2,1)}), bf16[8,2,32,1024]{3,2,1,0:T(8,128)(2,1)S(1)}, u32[]{:S(2)}, u32[]{:S(2)}) async-start(bf16[8,2,32,1024]{3,2,1,0:T(8,128)(2,1)} %shard_map.62), calls=%async_computation.2 | async-start | bytes 2097152 | tf_op jit(solution)/shard_map/all_to_all | solution.py:383
  105.0 3.7 %collective-permute-start.18 = (bf16[8,96,512]{2,1,0:T(8,128)(2,1)S(1)}, bf16[8,96,512]{2,1,0:T(8,128)(2,1)S(1)}, u32[]{:S(2)}, u32[]{:S(2)}) collective-permute-start(bf16[8,96,512]{2,1,0:T(8,128)(2,1)S(1)} %bitcast_dynamic-update-slice_fusion.refs_0_), channel_id=1, source_target_pairs={{0,16},{16,0},{1,17},{17,1},{2,18},{18,2},{3,19},{19,3},{4,20},{20... | collective-permute-start | bytes 2359304 | tf_op jit(solution)/shard_map/ppermute | solution.py:346
  108.7 6.2 %collective-permute-start.19 = (bf16[8,96,512]{2,1,0:T(8,128)(2,1)S(1)}, bf16[8,96,512]{2,1,0:T(8,128)(2,1)S(1)}, u32[]{:S(2)}, u32[]{:S(2)}) collective-permute-start(bf16[8,96,512]{2,1,0:T(8,128)(2,1)S(1)} %collective-permute-done.17.refs_1_), channel_id=1, source_target_pairs={{0,16},{16,0},{1,17},{17,1},{2,18},{18,2},{3,19},{19,3},{4,20},{20... | collective-permute-start | bytes 2359304 | tf_op jit(solution)/shard_map/ppermute | solution.py:346
  114.9 1.9 %collective-permute-done.19.refs_3_ = bf16[8,96,512]{2,1,0:T(8,128)(2,1)S(1)} collective-permute-done((bf16[8,96,512]{2,1,0:T(8,128)(2,1)S(1)}, bf16[8,96,512]{2,1,0:T(8,128)(2,1)S(1)}, u32[]{:S(2)}, u32[]{:S(2)}) %collective-permute-start.19) | collective-permute-done | bytes 786464 | tf_op jit(solution)/shard_map/ppermute | solution.py:346
  116.8 5.4 %shard_map.60 = (bf16[1024,1024]{1,0:T(8,128)(2,1)S(1)}, bf16[512,1024]{1,0:T(8,128)(2,1)}) custom-call(s32[3]{0:T(128)S(1)} %pad_add_fusion.me_ref, bf16[8,96,512]{2,1,0:T(8,128)(2,1)} %copy-done.3, bf16[8,96,512]{2,1,0:T(8,128)(2,1)} %copy-done.4, bf16[8,96,512]{2,1,0:T(8,128)(2,1)S(1)} %collective-permute-done.18.refs_2_, ...), custom_call_target="tpu_custom_call" | custom-call | bytes 6291456 | tf_op jit(solution)/shard_map/pallas_call | solution.py:282
  122.2 1.8 %all-to-all-done.2.p_ref = bf16[8,2,32,1024]{3,2,1,0:T(8,128)(2,1)S(1)} async-done(((bf16[8,2,32,1024]{3,2,1,0:T(8,128)(2,1)}), bf16[8,2,32,1024]{3,2,1,0:T(8,128)(2,1)S(1)}, u32[]{:S(2)}, u32[]{:S(2)}) %all-to-all-start.2) | async-done | bytes 1048608 | tf_op jit(solution)/shard_map/all_to_all | solution.py:383
  124.0 2.5 %shard_map.63 = bf16[16,96,256]{2,1,0:T(8,128)(2,1)S(1)} custom-call(s32[3]{0:T(128)S(1)} %pad_add_fusion.me_ref, bf16[1024,1024]{1,0:T(8,128)(2,1)S(1)} %get-tuple-element.82.vf, bf16[512,1024]{1,0:T(8,128)(2,1)} %get-tuple-element.83.vh_hbm, bf16[8,2,32,1024]{3,2,1,0:T(8,128)(2,1)S(1)} %all-to-all-done.2.p_ref), custom_call_target="tpu_custom_call" | custom-call | tf_op jit(solution)/shard_map/pallas_call | solution.py:314
  126.5 32.3 %all_to_all.20.m_ref = bf16[16,96,256]{2,1,0:T(8,128)(2,1)S(1)} all-to-all(bf16[16,96,256]{2,1,0:T(8,128)(2,1)S(1)} %shard_map.63), channel_id=1, replica_groups=mesh['y'=4,'xh'=2,'c'=2,'z'=8,'xl'=2] {'z','c'}, dimensions={0} | all-to-all | bytes 1572864 | tf_op jit(solution)/shard_map/all_to_all | solution.py:385
  158.8 1.7 %shard_map.64 = bf16[8,64,768]{2,1,0:T(8,128)(2,1)} custom-call(bf16[16,96,256]{2,1,0:T(8,128)(2,1)S(1)} %all_to_all.20.m_ref, bf16[768,768]{1,0:T(8,128)(2,1)S(1)} %copy-done.1), custom_call_target="tpu_custom_call" | custom-call | tf_op jit(solution)/shard_map/pallas_call | solution.py:335
  (56 shorter events, 11.2 us)
Async XLA Ops:
  0.0 13.5 %copy-start = (bf16[768,768]{1,0:T(8,128)(2,1)S(1)}, bf16[768,768]{1,0:T(8,128)(2,1)}, u32[]{:S(2)}) copy-start(bf16[768,768]{1,0:T(8,128)(2,1)} %w_ref.4) | copy-start | bytes 3538948
  3.1 12.3 %collective-permute-start.1 = (bf16[96,512]{1,0:T(8,128)(2,1)S(1)}, bf16[96,512]{1,0:T(8,128)(2,1)S(1)}, u32[]{:S(2)}, u32[]{:S(2)}) collective-permute-start(bf16[96,512]{1,0:T(8,128)(2,1)S(1)} %get-tuple-element.52), channel_id=1, source_target_pairs={{0,2},{2,4},{4,6},{6,8},{8,10},{10,12},{12,14},{14,0},{1,3},{3,5},... | collective-permute-start | bytes 294920 | tf_op jit(solution)/shard_map/ppermute | solution.py:355
  5.6 13.4 %collective-permute-start.2 = (bf16[96,512]{1,0:T(8,128)(2,1)S(1)}, bf16[96,512]{1,0:T(8,128)(2,1)S(1)}, u32[]{:S(2)}, u32[]{:S(2)}) collective-permute-start(bf16[96,512]{1,0:T(8,128)(2,1)S(1)} %get-tuple-element.53), channel_id=1, source_target_pairs={{0,14},{2,0},{4,2},{6,4},{8,6},{10,8},{12,10},{14,12},{1,15},{3,1}... | collective-permute-start | bytes 294920 | tf_op jit(solution)/shard_map/ppermute | solution.py:355
  9.6 13.8 %collective-permute-start.3 = (bf16[96,512]{1,0:T(8,128)(2,1)S(1)}, bf16[96,512]{1,0:T(8,128)(2,1)S(1)}, u32[]{:S(2)}, u32[]{:S(2)}) collective-permute-start(bf16[96,512]{1,0:T(8,128)(2,1)S(1)} %get-tuple-element.54), channel_id=1, source_target_pairs={{0,4},{2,6},{4,8},{6,10},{8,12},{10,14},{12,0},{14,2},{1,5},{3,7},... | collective-permute-start | bytes 294920 | tf_op jit(solution)/shard_map/ppermute | solution.py:355
  9.6 13.8 %collective-permute-start.4 = (bf16[96,512]{1,0:T(8,128)(2,1)S(1)}, bf16[96,512]{1,0:T(8,128)(2,1)S(1)}, u32[]{:S(2)}, u32[]{:S(2)}) collective-permute-start(bf16[96,512]{1,0:T(8,128)(2,1)S(1)} %get-tuple-element.55), channel_id=1, source_target_pairs={{0,12},{2,14},{4,0},{6,2},{8,4},{10,6},{12,8},{14,10},{1,13},{3,15... | collective-permute-start | bytes 294920 | tf_op jit(solution)/shard_map/ppermute | solution.py:355
  13.2 13.8 %collective-permute-start.5 = (bf16[96,512]{1,0:T(8,128)(2,1)S(1)}, bf16[96,512]{1,0:T(8,128)(2,1)}, u32[]{:S(2)}, u32[]{:S(2)}) collective-permute-start(bf16[96,512]{1,0:T(8,128)(2,1)S(1)} %get-tuple-element.56), channel_id=1, source_target_pairs={{0,6},{2,8},{4,10},{6,12},{8,14},{10,0},{12,2},{14,4},{1,7},{3,9},... | collective-permute-start | bytes 294920 | tf_op jit(solution)/shard_map/ppermute | solution.py:355
  15.3 18.6 %collective-permute-start.6 = (bf16[96,512]{1,0:T(8,128)(2,1)S(1)}, bf16[96,512]{1,0:T(8,128)(2,1)S(1)}, u32[]{:S(2)}, u32[]{:S(2)}) collective-permute-start(bf16[96,512]{1,0:T(8,128)(2,1)S(1)} %get-tuple-element.60), channel_id=1, source_target_pairs={{0,8},{2,10},{4,12},{6,14},{8,0},{10,2},{12,4},{14,6},{1,9},{3,11}... | collective-permute-start | bytes 294920 | tf_op jit(solution)/shard_map/ppermute | solution.py:355
  19.0 15.1 %collective-permute-start.7 = (bf16[96,512]{1,0:T(8,128)(2,1)S(1)}, bf16[96,512]{1,0:T(8,128)(2,1)S(1)}, u32[]{:S(2)}, u32[]{:S(2)}) collective-permute-start(bf16[96,512]{1,0:T(8,128)(2,1)S(1)} %get-tuple-element.61), channel_id=1, source_target_pairs={{0,10},{2,12},{4,14},{6,0},{8,2},{10,4},{12,6},{14,8},{1,11},{3,13... | collective-permute-start | bytes 294920 | tf_op jit(solution)/shard_map/ppermute | solution.py:355
  27.0 34.0 %all-to-all-start = ((bf16[16,128,256]{2,1,0:T(8,128)(2,1)}), bf16[16,128,256]{2,1,0:T(8,128)(2,1)}, u32[]{:S(2)}, u32[]{:S(2)}) async-start(bf16[16,128,256]{2,1,0:T(8,128)(2,1)} %shard_map.57), calls=%async_computation | async-start | bytes 2097152 | tf_op jit(solution)/shard_map/all_to_all | solution.py:368
  33.0 2.6 %copy-start.2 = (bf16[768,768]{1,0:T(8,128)(2,1)S(1)}, bf16[768,768]{1,0:T(8,128)(2,1)}, u32[]{:S(2)}) copy-start(bf16[768,768]{1,0:T(8,128)(2,1)} %w_ref.3) | copy-start | bytes 3538948
  34.1 2.9 %collective-permute-start.9 = (bf16[8,96,512]{2,1,0:T(8,128)(2,1)S(1)}, bf16[8,96,512]{2,1,0:T(8,128)(2,1)S(1)}, u32[]{:S(2)}, u32[]{:S(2)}) collective-permute-start(bf16[8,96,512]{2,1,0:T(8,128)(2,1)S(1)} %bitcast_dynamic-update-slice_fusion.8.own), channel_id=1, source_target_pairs={{0,16},{16,0},{1,17},{17,1},{2,18},{18,2},{3,19},{19,3},{4,20},{20... | collective-permute-start | bytes 2359304 | tf_op jit(solution)/shard_map/ppermute | solution.py:346
  34.3 18.9 %collective-permute-start.8 = (bf16[8,96,512]{2,1,0:T(8,128)(2,1)S(1)}, bf16[8,96,512]{2,1,0:T(8,128)(2,1)S(1)}, u32[]{:S(2)}, u32[]{:S(2)}) collective-permute-start(bf16[8,96,512]{2,1,0:T(8,128)(2,1)S(1)} %bitcast_dynamic-update-slice_fusion.8.own), channel_id=1, source_target_pairs={{0,1},{1,0},{2,3},{3,2},{4,5},{5,4},{6,7},{7,6},{8,9},{9,8},{10,11... | collective-permute-start | bytes 2359304 | tf_op jit(solution)/shard_map/ppermute | solution.py:346
  53.2 4.8 %copy-start.5 = (bf16[8,96,512]{2,1,0:T(8,128)(2,1)}, bf16[8,96,512]{2,1,0:T(8,128)(2,1)S(1)}, u32[]{:S(2)}) copy-start(bf16[8,96,512]{2,1,0:T(8,128)(2,1)S(1)} %collective-permute-done.8.own_hbm) | copy-start | bytes 2359300
  53.2 4.8 %collective-permute-start.11 = (bf16[8,96,512]{2,1,0:T(8,128)(2,1)S(1)}, bf16[8,96,512]{2,1,0:T(8,128)(2,1)S(1)}, u32[]{:S(2)}, u32[]{:S(2)}) collective-permute-start(bf16[8,96,512]{2,1,0:T(8,128)(2,1)S(1)} %collective-permute-done.8.own_hbm), channel_id=1, source_target_pairs={{0,16},{16,0},{1,17},{17,1},{2,18},{18,2},{3,19},{19,3},{4,20},{20... | collective-permute-start | bytes 2359304 | tf_op jit(solution)/shard_map/ppermute | solution.py:346
  54.3 12.7 %collective-permute-start = (bf16[96,512]{1,0:T(8,128)(2,1)S(1)}, bf16[96,512]{1,0:T(8,128)(2,1)S(1)}, u32[]{:S(2)}, u32[]{:S(2)}) collective-permute-start(bf16[96,512]{1,0:T(8,128)(2,1)S(1)} %get-tuple-element.49), channel_id=1, source_target_pairs={{0,4},{2,6},{4,8},{6,10},{8,12},{10,14},{12,0},{14,2},{1,5},{3,7},... | collective-permute-start | bytes 294920 | tf_op jit(solution)/shard_map/ppermute | solution.py:355
  56.8 10.2 %collective-permute-start.10 = (bf16[96,512]{1,0:T(8,128)(2,1)S(1)}, bf16[96,512]{1,0:T(8,128)(2,1)S(1)}, u32[]{:S(2)}, u32[]{:S(2)}) collective-permute-start(bf16[96,512]{1,0:T(8,128)(2,1)S(1)} %get-tuple-element.68), channel_id=1, source_target_pairs={{0,12},{2,14},{4,0},{6,2},{8,4},{10,6},{12,8},{14,10},{1,13},{3,15... | collective-permute-start | bytes 294920 | tf_op jit(solution)/shard_map/ppermute | solution.py:355
  67.0 29.5 %all-to-all-start.1 = ((f32[8,32,1536]{2,1,0:T(8,128)}), f32[8,32,1536]{2,1,0:T(8,128)S(1)}, u32[]{:S(2)}, u32[]{:S(2)}) async-start(f32[8,32,1536]{2,1,0:T(8,128)} %shard_map.59), calls=%async_computation.1 | async-start | bytes 3145728 | tf_op jit(solution)/shard_map/all_to_all | solution.py:377
  73.6 8.7 %collective-permute-start.12 = (bf16[96,512]{1,0:T(8,128)(2,1)S(1)}, bf16[96,512]{1,0:T(8,128)(2,1)S(1)}, u32[]{:S(2)}, u32[]{:S(2)}) collective-permute-start(bf16[96,512]{1,0:T(8,128)(2,1)S(1)} %get-tuple-element.75), channel_id=1, source_target_pairs={{0,2},{2,4},{4,6},{6,8},{8,10},{10,12},{12,14},{14,0},{1,3},{3,5},... | collective-permute-start | bytes 294920 | tf_op jit(solution)/shard_map/ppermute | solution.py:355
  73.6 11.0 %collective-permute-start.13 = (bf16[96,512]{1,0:T(8,128)(2,1)S(1)}, bf16[96,512]{1,0:T(8,128)(2,1)S(1)}, u32[]{:S(2)}, u32[]{:S(2)}) collective-permute-start(bf16[96,512]{1,0:T(8,128)(2,1)S(1)} %get-tuple-element.77), channel_id=1, source_target_pairs={{0,6},{2,8},{4,10},{6,12},{8,14},{10,0},{12,2},{14,4},{1,7},{3,9},... | collective-permute-start | bytes 294920 | tf_op jit(solution)/shard_map/ppermute | solution.py:355
  76.3 12.9 %collective-permute-start.14 = (bf16[96,512]{1,0:T(8,128)(2,1)S(1)}, bf16[96,512]{1,0:T(8,128)(2,1)S(1)}, u32[]{:S(2)}, u32[]{:S(2)}) collective-permute-start(bf16[96,512]{1,0:T(8,128)(2,1)S(1)} %get-tuple-element.78), channel_id=1, source_target_pairs={{0,8},{2,10},{4,12},{6,14},{8,0},{10,2},{12,4},{14,6},{1,9},{3,11}... | collective-permute-start | bytes 294920 | tf_op jit(solution)/shard_map/ppermute | solution.py:355
  79.3 11.6 %collective-permute-start.15 = (bf16[96,512]{1,0:T(8,128)(2,1)S(1)}, bf16[96,512]{1,0:T(8,128)(2,1)S(1)}, u32[]{:S(2)}, u32[]{:S(2)}) collective-permute-start(bf16[96,512]{1,0:T(8,128)(2,1)S(1)} %get-tuple-element.79), channel_id=1, source_target_pairs={{0,10},{2,12},{4,14},{6,0},{8,2},{10,4},{12,6},{14,8},{1,11},{3,13... | collective-permute-start | bytes 294920 | tf_op jit(solution)/shard_map/ppermute | solution.py:355
  80.7 11.2 %collective-permute-start.16 = (bf16[96,512]{1,0:T(8,128)(2,1)S(1)}, bf16[96,512]{1,0:T(8,128)(2,1)S(1)}, u32[]{:S(2)}, u32[]{:S(2)}) collective-permute-start(bf16[96,512]{1,0:T(8,128)(2,1)S(1)} %get-tuple-element.81), channel_id=1, source_target_pairs={{0,14},{2,0},{4,2},{6,4},{8,6},{10,8},{12,10},{14,12},{1,15},{3,1}... | collective-permute-start | bytes 294920 | tf_op jit(solution)/shard_map/ppermute | solution.py:355
  91.9 13.0 %copy-start.3 = (bf16[8,96,512]{2,1,0:T(8,128)(2,1)}, bf16[8,96,512]{2,1,0:T(8,128)(2,1)S(1)}, u32[]{:S(2)}) copy-start(bf16[8,96,512]{2,1,0:T(8,128)(2,1)S(1)} %bitcast_dynamic-update-slice_fusion.refs_0_) | copy-start | bytes 2359300
  91.9 16.7 %collective-permute-start.17 = (bf16[8,96,512]{2,1,0:T(8,128)(2,1)S(1)}, bf16[8,96,512]{2,1,0:T(8,128)(2,1)S(1)}, u32[]{:S(2)}, u32[]{:S(2)}) collective-permute-start(bf16[8,96,512]{2,1,0:T(8,128)(2,1)S(1)} %bitcast_dynamic-update-slice_fusion.refs_0_), channel_id=1, source_target_pairs={{0,1},{1,0},{2,3},{3,2},{4,5},{5,4},{6,7},{7,6},{8,9},{9,8},{10,11... | collective-permute-start | bytes 2359304 | tf_op jit(solution)/shard_map/ppermute | solution.py:346
  96.5 3.5 %collective-permute-start.20 = (f32[32,512]{1,0:T(8,128)S(1)}, f32[32,512]{1,0:T(8,128)S(1)}, u32[]{:S(2)}, u32[]{:S(2)}) collective-permute-start(f32[32,512]{1,0:T(8,128)S(1)} %get-tuple-element.86.half), channel_id=1, source_target_pairs={{0,2},{2,0},{4,6},{6,4},{8,10},{10,8},{12,14},{14,12},{1,3},{3,1},... | collective-permute-start | bytes 196616 | tf_op jit(solution)/shard_map/ppermute | solution.py:346
  101.2 22.8 %all-to-all-start.2 = ((bf16[8,2,32,1024]{3,2,1,0:T(8,128)(2,1)}), bf16[8,2,32,1024]{3,2,1,0:T(8,128)(2,1)S(1)}, u32[]{:S(2)}, u32[]{:S(2)}) async-start(bf16[8,2,32,1024]{3,2,1,0:T(8,128)(2,1)} %shard_map.62), calls=%async_computation.2 | async-start | bytes 2097152 | tf_op jit(solution)/shard_map/all_to_all | solution.py:383
  105.0 9.9 %collective-permute-start.18 = (bf16[8,96,512]{2,1,0:T(8,128)(2,1)S(1)}, bf16[8,96,512]{2,1,0:T(8,128)(2,1)S(1)}, u32[]{:S(2)}, u32[]{:S(2)}) collective-permute-start(bf16[8,96,512]{2,1,0:T(8,128)(2,1)S(1)} %bitcast_dynamic-update-slice_fusion.refs_0_), channel_id=1, source_target_pairs={{0,16},{16,0},{1,17},{17,1},{2,18},{18,2},{3,19},{19,3},{4,20},{20... | collective-permute-start | bytes 2359304 | tf_op jit(solution)/shard_map/ppermute | solution.py:346
  108.7 6.2 %copy-start.4 = (bf16[8,96,512]{2,1,0:T(8,128)(2,1)}, bf16[8,96,512]{2,1,0:T(8,128)(2,1)S(1)}, u32[]{:S(2)}) copy-start(bf16[8,96,512]{2,1,0:T(8,128)(2,1)S(1)} %collective-permute-done.17.refs_1_) | copy-start | bytes 2359300
  108.7 8.1 %collective-permute-start.19 = (bf16[8,96,512]{2,1,0:T(8,128)(2,1)S(1)}, bf16[8,96,512]{2,1,0:T(8,128)(2,1)S(1)}, u32[]{:S(2)}, u32[]{:S(2)}) collective-permute-start(bf16[8,96,512]{2,1,0:T(8,128)(2,1)S(1)} %collective-permute-done.17.refs_1_), channel_id=1, source_target_pairs={{0,16},{16,0},{1,17},{17,1},{2,18},{18,2},{3,19},{19,3},{4,20},{20... | collective-permute-start | bytes 2359304 | tf_op jit(solution)/shard_map/ppermute | solution.py:346
  126.5 32.3 %copy-start.1 = (bf16[768,768]{1,0:T(8,128)(2,1)S(1)}, bf16[768,768]{1,0:T(8,128)(2,1)}, u32[]{:S(2)}) copy-start(bf16[768,768]{1,0:T(8,128)(2,1)} %w_ref.5) | copy-start | bytes 3538948

commit v15 on v14

--- a/solution.py
+++ b/solution.py
@@ -359,9 +359,9 @@
     me = jnp.stack([lax.axis_index(("y", "xh")), lax.axis_index("c"), lax.axis_index("z")])
     me = me.astype(jnp.int32)
     n, k = key_chunks(me, x, wk)
-    for s in (1, 7, 2, 6, 3, 5, 4):
+    for s in (4, 3, 5, 2, 6, 1, 7):
         k[s] = shift(k[s], s)
-    early = (1, 7, 2, 6, 3)
+    early = (4, 3, 5, 2)
     q, *got = lax.optimization_barrier((query_chunks(n, wq), *(k[s] for s in early)))
     for s, a in zip(early, got):
         k[s] = a

time: 161 us -> 162 us (level)
    all_to_all x1, starting transfers between devices: 5.95 us -> 8.29 us  [local(): q = lax.all_to_all(q, ('z', 'c'), 0, 0, tiled=True)]
  transfers between devices with their start and end apart: 24 -> 24, of which waited for: 13 -> 12; matrix products, arithmetic and copies ran while one was open for 1% -> 1% of each run, Pallas kernels for 11% -> 11%
where the time goes in v15:
time: 162 us
  starting transfers between devices  60 us (37%)
  waiting for transfers between devices  43.4 us (27%)
  blocking collectives  32.1 us (20%)
  Pallas kernels  24.8 us (15%)
    all_to_all x1, blocking collectives, local(): mixed = lax.all_to_all(mix(me, laid, probs), ('z', 'c'), 0, 0, tiled=True)  32.1 us
    ppermute x14, starting transfers between devices, shift(): return lax.ppermute(x, 'z', [(i, (i + s) % Z) for i in range(Z)])  29.3 us
    ppermute x7, waiting for transfers between devices, flip(): return lax.ppermute(x, axes, [(i, i ^ s) for i in range(n)])  20.9 us
    ppermute x14, waiting for transfers between devices, shift(): return lax.ppermute(x, 'z', [(i, (i + s) % Z) for i in range(Z)])  14.1 us
    ppermute x7, starting transfers between devices, flip(): return lax.ppermute(x, axes, [(i, i ^ s) for i in range(n)])  11.9 us
    all_to_all x1, starting transfers between devices, local(): q = lax.all_to_all(q, ('z', 'c'), 0, 0, tiled=True)  8.29 us
    all_to_all x1, starting transfers between devices, local(): parts = lax.all_to_all(scores, ('y', 'xh'), 0, 0, tiled=True)  6.66 us
    pallas_call x1, Pallas kernels, score(): pl.pallas_call(score_kernel, out_shape=jax.ShapeDtypeStruct((PEERS, SUB,...  5.92 us
  transfers between devices with their start and end apart: 24, of which 12 were waited for; matrix products, arithmetic and copies ran while one was open for 1% of the time, Pallas kernels for 11%

profile of v15, /device:TPU:1, one launch (start us, length us, event | category | flops | bytes accessed | tf_op | source)
XLA Modules:
  0.0 161.7 jit_solution(2053002277828502302)
XLA Ops:
  0.1 3.0 %shard_map.55 = (bf16[2,8,32,768]{3,2,1,0:T(8,128)(2,1)S(1)}, bf16[96,512]{1,0:T(8,128)(2,1)S(1)}, bf16[96,512]{1,0:T(8,128)(2,1)S(1)}, bf16[96,512]{1,0:T(8,128...) custom-call(s32[3]{0:T(128)S(1)} %pad_add_fusion.me_ref, ...), custom_call_target="tpu_custom_call" | custom-call | tf_op jit(solution)/shard_map/pallas_call | solution.py:97
  3.1 2.5 %collective-permute-start.1 = (bf16[96,512]{1,0:T(8,128)(2,1)S(1)}, bf16[96,512]{1,0:T(8,128)(2,1)S(1)}, u32[]{:S(2)}, u32[]{:S(2)}) collective-permute-start(bf16[96,512]{1,0:T(8,128)(2,1)S(1)} %get-tuple-element.51), channel_id=1, source_target_pairs={{0,2},{2,4},{4,6},{6,8},{8,10},{10,12},{12,14},{14,0},{1,3},{3,5},... | collective-permute-start | bytes 294920 | tf_op jit(solution)/shard_map/ppermute | solution.py:355
  5.6 6.0 %collective-permute-start.2 = (bf16[96,512]{1,0:T(8,128)(2,1)S(1)}, bf16[96,512]{1,0:T(8,128)(2,1)S(1)}, u32[]{:S(2)}, u32[]{:S(2)}) collective-permute-start(bf16[96,512]{1,0:T(8,128)(2,1)S(1)} %get-tuple-element.52), channel_id=1, source_target_pairs={{0,8},{2,10},{4,12},{6,14},{8,0},{10,2},{12,4},{14,6},{1,9},{3,11}... | collective-permute-start | bytes 294920 | tf_op jit(solution)/shard_map/ppermute | solution.py:355
  12.6 3.5 %collective-permute-start.4 = (bf16[96,512]{1,0:T(8,128)(2,1)S(1)}, bf16[96,512]{1,0:T(8,128)(2,1)S(1)}, u32[]{:S(2)}, u32[]{:S(2)}) collective-permute-start(bf16[96,512]{1,0:T(8,128)(2,1)S(1)} %get-tuple-element.54), channel_id=1, source_target_pairs={{0,10},{2,12},{4,14},{6,0},{8,2},{10,4},{12,6},{14,8},{1,11},{3,13... | collective-permute-start | bytes 294920 | tf_op jit(solution)/shard_map/ppermute | solution.py:355
  17.3 1.8 %shard_map.57 = bf16[16,128,256]{2,1,0:T(8,128)(2,1)} custom-call(bf16[2,8,32,768]{3,2,1,0:T(8,128)(2,1)S(1)} %get-tuple-element.45.n_ref, bf16[768,768]{1,0:T(8,128)(2,1)S(1)} %copy-done), custom_call_target="tpu_custom_call" | custom-call | flops 603979776 | bytes 2752512 | tf_op jit(solution)/shard_map/pallas_call | solution.py:124
  19.1 3.1 %collective-permute-start.6 = (bf16[96,512]{1,0:T(8,128)(2,1)S(1)}, bf16[96,512]{1,0:T(8,128)(2,1)S(1)}, u32[]{:S(2)}, u32[]{:S(2)}) collective-permute-start(bf16[96,512]{1,0:T(8,128)(2,1)S(1)} %get-tuple-element.60), channel_id=1, source_target_pairs={{0,12},{2,14},{4,0},{6,2},{8,4},{10,6},{12,8},{14,10},{1,13},{3,15... | collective-permute-start | bytes 294920 | tf_op jit(solution)/shard_map/ppermute | solution.py:355
  22.2 3.6 %collective-permute-done.3 = bf16[96,512]{1,0:T(8,128)(2,1)S(1)} collective-permute-done((bf16[96,512]{1,0:T(8,128)(2,1)S(1)}, bf16[96,512]{1,0:T(8,128)(2,1)S(1)}, u32[]{:S(2)}, u32[]{:S(2)}) %collective-permute-start.3) | collective-permute-done | bytes 98336 | tf_op jit(solution)/shard_map/ppermute | solution.py:355
  25.9 8.3 %all-to-all-start = ((bf16[16,128,256]{2,1,0:T(8,128)(2,1)}), bf16[16,128,256]{2,1,0:T(8,128)(2,1)}, u32[]{:S(2)}, u32[]{:S(2)}) async-start(bf16[16,128,256]{2,1,0:T(8,128)(2,1)} %shard_map.57), calls=%async_computation | async-start | bytes 2097152 | tf_op jit(solution)/shard_map/all_to_all | solution.py:368
  38.2 1.8 %shard_map.58 = (bf16[1024,512]{1,0:T(8,128)(2,1)S(1)}, bf16[1024,256]{1,0:T(8,128)(2,1)S(1)}) custom-call(s32[3]{0:T(128)S(1)} %pad_add_fusion.me_ref, bf16[8,96,512]{2,1,0:T(8,128)(2,1)S(1)} %bitcast_dynamic-update-slice_fusion.8.own, bf16[8,96,512]{2,1,0:T(8,128)(2,1)S(1)} %collective-permute-done.9.other), custom_call_target="tpu_custom_call" | custom-call | bytes 6291456 | tf_op jit(solution)/shard_map/pallas_call | solution.py:173
  40.0 14.4 %collective-permute-done.8.own_hbm = bf16[8,96,512]{2,1,0:T(8,128)(2,1)S(1)} collective-permute-done((bf16[8,96,512]{2,1,0:T(8,128)(2,1)S(1)}, bf16[8,96,512]{2,1,0:T(8,128)(2,1)S(1)}, u32[]{:S(2)}, u32[]{:S(2)}) %collective-permute-start.8) | collective-permute-done | bytes 786464 | tf_op jit(solution)/shard_map/ppermute | solution.py:346
  55.5 2.5 %collective-permute-start = (bf16[96,512]{1,0:T(8,128)(2,1)S(1)}, bf16[96,512]{1,0:T(8,128)(2,1)S(1)}, u32[]{:S(2)}, u32[]{:S(2)}) collective-permute-start(bf16[96,512]{1,0:T(8,128)(2,1)S(1)} %get-tuple-element.48), channel_id=1, source_target_pairs={{0,4},{2,6},{4,8},{6,10},{8,12},{10,14},{12,0},{14,2},{1,5},{3,7},... | collective-permute-start | bytes 294920 | tf_op jit(solution)/shard_map/ppermute | solution.py:355
  59.2 3.0 %all-to-all-done.q_hbm = bf16[16,128,256]{2,1,0:T(8,128)(2,1)} async-done(((bf16[16,128,256]{2,1,0:T(8,128)(2,1)}), bf16[16,128,256]{2,1,0:T(8,128)(2,1)}, u32[]{:S(2)}, u32[]{:S(2)}) %all-to-all-start) | async-done | bytes 1048608 | tf_op jit(solution)/shard_map/all_to_all | solution.py:368
  62.2 5.9 %shard_map.59 = f32[8,32,1536]{2,1,0:T(8,128)} custom-call(s32[3]{0:T(128)S(1)} %pad_add_fusion.me_ref, bf16[16,128,256]{2,1,0:T(8,128)(2,1)} %all-to-all-done.q_hbm, bf16[1024,512]{1,0:T(8,128)(2,1)S(1)} %get-tuple-element.69.kf_hbm, bf16[1024,256]{1,0:T(8,128)(2,1)S(1)} %get-tuple-element.70.kh_hbm, bf16[8,96,512]{2,1,0:T(8,128)(2,1)} %copy-done.5, ...), custom_call_target="tpu_custom_call" | custom-call | tf_op jit(solution)/shard_map/pallas_call | solution.py:209
  68.2 6.7 %all-to-all-start.1 = ((f32[8,32,1536]{2,1,0:T(8,128)}), f32[8,32,1536]{2,1,0:T(8,128)S(1)}, u32[]{:S(2)}, u32[]{:S(2)}) async-start(f32[8,32,1536]{2,1,0:T(8,128)} %shard_map.59), calls=%async_computation.1 | async-start | bytes 3145728 | tf_op jit(solution)/shard_map/all_to_all | solution.py:377
  74.8 2.6 %collective-permute-start.13 = (bf16[96,512]{1,0:T(8,128)(2,1)S(1)}, bf16[96,512]{1,0:T(8,128)(2,1)S(1)}, u32[]{:S(2)}, u32[]{:S(2)}) collective-permute-start(bf16[96,512]{1,0:T(8,128)(2,1)S(1)} %get-tuple-element.75), channel_id=1, source_target_pairs={{0,6},{2,8},{4,10},{6,12},{8,14},{10,0},{12,2},{14,4},{1,7},{3,9},... | collective-permute-start | bytes 294920 | tf_op jit(solution)/shard_map/ppermute | solution.py:355
  77.5 3.0 %collective-permute-start.14 = (bf16[96,512]{1,0:T(8,128)(2,1)S(1)}, bf16[96,512]{1,0:T(8,128)(2,1)S(1)}, u32[]{:S(2)}, u32[]{:S(2)}) collective-permute-start(bf16[96,512]{1,0:T(8,128)(2,1)S(1)} %get-tuple-element.76), channel_id=1, source_target_pairs={{0,8},{2,10},{4,12},{6,14},{8,0},{10,2},{12,4},{14,6},{1,9},{3,11}... | collective-permute-start | bytes 294920 | tf_op jit(solution)/shard_map/ppermute | solution.py:355
  80.5 1.5 collective-permute-start.15
  83.2 4.8 %collective-permute-done.13 = bf16[96,512]{1,0:T(8,128)(2,1)S(1)} collective-permute-done((bf16[96,512]{1,0:T(8,128)(2,1)S(1)}, bf16[96,512]{1,0:T(8,128)(2,1)S(1)}, u32[]{:S(2)}, u32[]{:S(2)}) %collective-permute-start.13) | collective-permute-done | bytes 98336 | tf_op jit(solution)/shard_map/ppermute | solution.py:355
  88.0 2.3 %collective-permute-done.14 = bf16[96,512]{1,0:T(8,128)(2,1)S(1)} collective-permute-done((bf16[96,512]{1,0:T(8,128)(2,1)S(1)}, bf16[96,512]{1,0:T(8,128)(2,1)S(1)}, u32[]{:S(2)}, u32[]{:S(2)}) %collective-permute-start.14) | collective-permute-done | bytes 98336 | tf_op jit(solution)/shard_map/ppermute | solution.py:355
  90.3 1.7 %collective-permute-done.15 = bf16[96,512]{1,0:T(8,128)(2,1)S(1)} collective-permute-done((bf16[96,512]{1,0:T(8,128)(2,1)S(1)}, bf16[96,512]{1,0:T(8,128)(2,1)S(1)}, u32[]{:S(2)}, u32[]{:S(2)}) %collective-permute-start.15) | collective-permute-done | bytes 98336 | tf_op jit(solution)/shard_map/ppermute | solution.py:355
  92.0 1.6 collective-permute-done.16
  94.1 3.6 %all-to-all-done.1.parts = f32[8,32,1536]{2,1,0:T(8,128)S(1)} async-done(((f32[8,32,1536]{2,1,0:T(8,128)}), f32[8,32,1536]{2,1,0:T(8,128)S(1)}, u32[]{:S(2)}, u32[]{:S(2)}) %all-to-all-start.1) | async-done | bytes 1572896 | tf_op jit(solution)/shard_map/all_to_all | solution.py:377
  97.8 3.4 %collective-permute-done.20.other = f32[32,512]{1,0:T(8,128)S(1)} collective-permute-done((f32[32,512]{1,0:T(8,128)S(1)}, f32[32,512]{1,0:T(8,128)S(1)}, u32[]{:S(2)}, u32[]{:S(2)}) %collective-permute-start.20) | collective-permute-done | bytes 65568 | tf_op jit(solution)/shard_map/ppermute | solution.py:346
  102.4 3.8 %all-to-all-start.2 = ((bf16[8,2,32,1024]{3,2,1,0:T(8,128)(2,1)}), bf16[8,2,32,1024]{3,2,1,0:T(8,128)(2,1)S(1)}, u32[]{:S(2)}, u32[]{:S(2)}) async-start(bf16[8,2,32,1024]{3,2,1,0:T(8,128)(2,1)} %shard_map.62), calls=%async_computation.2 | async-start | bytes 2097152 | tf_op jit(solution)/shard_map/all_to_all | solution.py:383
  106.2 3.4 %collective-permute-start.18 = (bf16[8,96,512]{2,1,0:T(8,128)(2,1)S(1)}, bf16[8,96,512]{2,1,0:T(8,128)(2,1)S(1)}, u32[]{:S(2)}, u32[]{:S(2)}) collective-permute-start(bf16[8,96,512]{2,1,0:T(8,128)(2,1)S(1)} %bitcast_dynamic-update-slice_fusion.refs_0_), channel_id=1, source_target_pairs={{0,16},{16,0},{1,17},{17,1},{2,18},{18,2},{3,19},{19,3},{4,20},{20... | collective-permute-start | bytes 2359304 | tf_op jit(solution)/shard_map/ppermute | solution.py:346
  110.8 5.4 %collective-permute-start.19 = (bf16[8,96,512]{2,1,0:T(8,128)(2,1)S(1)}, bf16[8,96,512]{2,1,0:T(8,128)(2,1)S(1)}, u32[]{:S(2)}, u32[]{:S(2)}) collective-permute-start(bf16[8,96,512]{2,1,0:T(8,128)(2,1)S(1)} %collective-permute-done.17.refs_1_), channel_id=1, source_target_pairs={{0,16},{16,0},{1,17},{17,1},{2,18},{18,2},{3,19},{19,3},{4,20},{20... | collective-permute-start | bytes 2359304 | tf_op jit(solution)/shard_map/ppermute | solution.py:346
  116.2 1.9 %collective-permute-done.19.refs_3_ = bf16[8,96,512]{2,1,0:T(8,128)(2,1)S(1)} collective-permute-done((bf16[8,96,512]{2,1,0:T(8,128)(2,1)S(1)}, bf16[8,96,512]{2,1,0:T(8,128)(2,1)S(1)}, u32[]{:S(2)}, u32[]{:S(2)}) %collective-permute-start.19) | collective-permute-done | bytes 786464 | tf_op jit(solution)/shard_map/ppermute | solution.py:346
  118.1 5.4 %shard_map.60 = (bf16[1024,1024]{1,0:T(8,128)(2,1)S(1)}, bf16[512,1024]{1,0:T(8,128)(2,1)}) custom-call(s32[3]{0:T(128)S(1)} %pad_add_fusion.me_ref, bf16[8,96,512]{2,1,0:T(8,128)(2,1)} %copy-done.3, bf16[8,96,512]{2,1,0:T(8,128)(2,1)} %copy-done.4, bf16[8,96,512]{2,1,0:T(8,128)(2,1)S(1)} %collective-permute-done.18.refs_2_, ...), custom_call_target="tpu_custom_call" | custom-call | bytes 6291456 | tf_op jit(solution)/shard_map/pallas_call | solution.py:282
  123.6 1.9 %all-to-all-done.2.p_ref = bf16[8,2,32,1024]{3,2,1,0:T(8,128)(2,1)S(1)} async-done(((bf16[8,2,32,1024]{3,2,1,0:T(8,128)(2,1)}), bf16[8,2,32,1024]{3,2,1,0:T(8,128)(2,1)S(1)}, u32[]{:S(2)}, u32[]{:S(2)}) %all-to-all-start.2) | async-done | bytes 1048608 | tf_op jit(solution)/shard_map/all_to_all | solution.py:383
  125.5 2.5 %shard_map.63 = bf16[16,96,256]{2,1,0:T(8,128)(2,1)S(1)} custom-call(s32[3]{0:T(128)S(1)} %pad_add_fusion.me_ref, bf16[1024,1024]{1,0:T(8,128)(2,1)S(1)} %get-tuple-element.80.vf, bf16[512,1024]{1,0:T(8,128)(2,1)} %get-tuple-element.81.vh_hbm, bf16[8,2,32,1024]{3,2,1,0:T(8,128)(2,1)S(1)} %all-to-all-done.2.p_ref), custom_call_target="tpu_custom_call" | custom-call | tf_op jit(solution)/shard_map/pallas_call | solution.py:314
  127.9 32.1 %all_to_all.20.m_ref = bf16[16,96,256]{2,1,0:T(8,128)(2,1)S(1)} all-to-all(bf16[16,96,256]{2,1,0:T(8,128)(2,1)S(1)} %shard_map.63), channel_id=1, replica_groups=mesh['y'=4,'xh'=2,'c'=2,'z'=8,'xl'=2] {'z','c'}, dimensions={0} | all-to-all | bytes 1572864 | tf_op jit(solution)/shard_map/all_to_all | solution.py:385
  160.1 1.7 %shard_map.64 = bf16[8,64,768]{2,1,0:T(8,128)(2,1)} custom-call(bf16[16,96,256]{2,1,0:T(8,128)(2,1)S(1)} %all_to_all.20.m_ref, bf16[768,768]{1,0:T(8,128)(2,1)S(1)} %copy-done.1), custom_call_target="tpu_custom_call" | custom-call | tf_op jit(solution)/shard_map/pallas_call | solution.py:335
  (56 shorter events, 12.8 us)
Async XLA Ops:
  0.0 17.3 %copy-start = (bf16[768,768]{1,0:T(8,128)(2,1)S(1)}, bf16[768,768]{1,0:T(8,128)(2,1)}, u32[]{:S(2)}) copy-start(bf16[768,768]{1,0:T(8,128)(2,1)} %w_ref.4) | copy-start | bytes 3538948
  3.1 31.1 %collective-permute-start.1 = (bf16[96,512]{1,0:T(8,128)(2,1)S(1)}, bf16[96,512]{1,0:T(8,128)(2,1)S(1)}, u32[]{:S(2)}, u32[]{:S(2)}) collective-permute-start(bf16[96,512]{1,0:T(8,128)(2,1)S(1)} %get-tuple-element.51), channel_id=1, source_target_pairs={{0,2},{2,4},{4,6},{6,8},{8,10},{10,12},{12,14},{14,0},{1,3},{3,5},... | collective-permute-start | bytes 294920 | tf_op jit(solution)/shard_map/ppermute | solution.py:355
  5.6 13.5 %collective-permute-start.2 = (bf16[96,512]{1,0:T(8,128)(2,1)S(1)}, bf16[96,512]{1,0:T(8,128)(2,1)S(1)}, u32[]{:S(2)}, u32[]{:S(2)}) collective-permute-start(bf16[96,512]{1,0:T(8,128)(2,1)S(1)} %get-tuple-element.52), channel_id=1, source_target_pairs={{0,8},{2,10},{4,12},{6,14},{8,0},{10,2},{12,4},{14,6},{1,9},{3,11}... | collective-permute-start | bytes 294920 | tf_op jit(solution)/shard_map/ppermute | solution.py:355
  11.6 14.2 %collective-permute-start.3 = (bf16[96,512]{1,0:T(8,128)(2,1)S(1)}, bf16[96,512]{1,0:T(8,128)(2,1)S(1)}, u32[]{:S(2)}, u32[]{:S(2)}) collective-permute-start(bf16[96,512]{1,0:T(8,128)(2,1)S(1)} %get-tuple-element.53), channel_id=1, source_target_pairs={{0,6},{2,8},{4,10},{6,12},{8,14},{10,0},{12,2},{14,4},{1,7},{3,9},... | collective-permute-start | bytes 294920 | tf_op jit(solution)/shard_map/ppermute | solution.py:355
  12.6 13.2 %collective-permute-start.4 = (bf16[96,512]{1,0:T(8,128)(2,1)S(1)}, bf16[96,512]{1,0:T(8,128)(2,1)S(1)}, u32[]{:S(2)}, u32[]{:S(2)}) collective-permute-start(bf16[96,512]{1,0:T(8,128)(2,1)S(1)} %get-tuple-element.54), channel_id=1, source_target_pairs={{0,10},{2,12},{4,14},{6,0},{8,2},{10,4},{12,6},{14,8},{1,11},{3,13... | collective-permute-start | bytes 294920 | tf_op jit(solution)/shard_map/ppermute | solution.py:355
  16.1 9.8 %collective-permute-start.5 = (bf16[96,512]{1,0:T(8,128)(2,1)S(1)}, bf16[96,512]{1,0:T(8,128)(2,1)}, u32[]{:S(2)}, u32[]{:S(2)}) collective-permute-start(bf16[96,512]{1,0:T(8,128)(2,1)S(1)} %get-tuple-element.55), channel_id=1, source_target_pairs={{0,4},{2,6},{4,8},{6,10},{8,12},{10,14},{12,0},{14,2},{1,5},{3,7},... | collective-permute-start | bytes 294920 | tf_op jit(solution)/shard_map/ppermute | solution.py:355
  19.1 16.1 %collective-permute-start.6 = (bf16[96,512]{1,0:T(8,128)(2,1)S(1)}, bf16[96,512]{1,0:T(8,128)(2,1)S(1)}, u32[]{:S(2)}, u32[]{:S(2)}) collective-permute-start(bf16[96,512]{1,0:T(8,128)(2,1)S(1)} %get-tuple-element.60), channel_id=1, source_target_pairs={{0,12},{2,14},{4,0},{6,2},{8,4},{10,6},{12,8},{14,10},{1,13},{3,15... | collective-permute-start | bytes 294920 | tf_op jit(solution)/shard_map/ppermute | solution.py:355
  25.9 9.4 %collective-permute-start.7 = (bf16[96,512]{1,0:T(8,128)(2,1)S(1)}, bf16[96,512]{1,0:T(8,128)(2,1)S(1)}, u32[]{:S(2)}, u32[]{:S(2)}) collective-permute-start(bf16[96,512]{1,0:T(8,128)(2,1)S(1)} %get-tuple-element.61), channel_id=1, source_target_pairs={{0,14},{2,0},{4,2},{6,4},{8,6},{10,8},{12,10},{14,12},{1,15},{3,1}... | collective-permute-start | bytes 294920 | tf_op jit(solution)/shard_map/ppermute | solution.py:355
  25.9 36.3 %all-to-all-start = ((bf16[16,128,256]{2,1,0:T(8,128)(2,1)}), bf16[16,128,256]{2,1,0:T(8,128)(2,1)}, u32[]{:S(2)}, u32[]{:S(2)}) async-start(bf16[16,128,256]{2,1,0:T(8,128)(2,1)} %shard_map.57), calls=%async_computation | async-start | bytes 2097152 | tf_op jit(solution)/shard_map/all_to_all | solution.py:368
  34.2 2.6 %copy-start.2 = (bf16[768,768]{1,0:T(8,128)(2,1)S(1)}, bf16[768,768]{1,0:T(8,128)(2,1)}, u32[]{:S(2)}) copy-start(bf16[768,768]{1,0:T(8,128)(2,1)} %w_ref.3) | copy-start | bytes 3538948
  35.3 2.9 %collective-permute-start.9 = (bf16[8,96,512]{2,1,0:T(8,128)(2,1)S(1)}, bf16[8,96,512]{2,1,0:T(8,128)(2,1)S(1)}, u32[]{:S(2)}, u32[]{:S(2)}) collective-permute-start(bf16[8,96,512]{2,1,0:T(8,128)(2,1)S(1)} %bitcast_dynamic-update-slice_fusion.8.own), channel_id=1, source_target_pairs={{0,16},{16,0},{1,17},{17,1},{2,18},{18,2},{3,19},{19,3},{4,20},{20... | collective-permute-start | bytes 2359304 | tf_op jit(solution)/shard_map/ppermute | solution.py:346
  35.5 18.9 %collective-permute-start.8 = (bf16[8,96,512]{2,1,0:T(8,128)(2,1)S(1)}, bf16[8,96,512]{2,1,0:T(8,128)(2,1)S(1)}, u32[]{:S(2)}, u32[]{:S(2)}) collective-permute-start(bf16[8,96,512]{2,1,0:T(8,128)(2,1)S(1)} %bitcast_dynamic-update-slice_fusion.8.own), channel_id=1, source_target_pairs={{0,1},{1,0},{2,3},{3,2},{4,5},{5,4},{6,7},{7,6},{8,9},{9,8},{10,11... | collective-permute-start | bytes 2359304 | tf_op jit(solution)/shard_map/ppermute | solution.py:346
  54.4 4.8 %copy-start.5 = (bf16[8,96,512]{2,1,0:T(8,128)(2,1)}, bf16[8,96,512]{2,1,0:T(8,128)(2,1)S(1)}, u32[]{:S(2)}) copy-start(bf16[8,96,512]{2,1,0:T(8,128)(2,1)S(1)} %collective-permute-done.8.own_hbm) | copy-start | bytes 2359300
  54.4 4.8 %collective-permute-start.11 = (bf16[8,96,512]{2,1,0:T(8,128)(2,1)S(1)}, bf16[8,96,512]{2,1,0:T(8,128)(2,1)S(1)}, u32[]{:S(2)}, u32[]{:S(2)}) collective-permute-start(bf16[8,96,512]{2,1,0:T(8,128)(2,1)S(1)} %collective-permute-done.8.own_hbm), channel_id=1, source_target_pairs={{0,16},{16,0},{1,17},{17,1},{2,18},{18,2},{3,19},{19,3},{4,20},{20... | collective-permute-start | bytes 2359304 | tf_op jit(solution)/shard_map/ppermute | solution.py:346
  55.5 12.7 %collective-permute-start = (bf16[96,512]{1,0:T(8,128)(2,1)S(1)}, bf16[96,512]{1,0:T(8,128)(2,1)S(1)}, u32[]{:S(2)}, u32[]{:S(2)}) collective-permute-start(bf16[96,512]{1,0:T(8,128)(2,1)S(1)} %get-tuple-element.48), channel_id=1, source_target_pairs={{0,4},{2,6},{4,8},{6,10},{8,12},{10,14},{12,0},{14,2},{1,5},{3,7},... | collective-permute-start | bytes 294920 | tf_op jit(solution)/shard_map/ppermute | solution.py:355
  58.0 10.2 %collective-permute-start.10 = (bf16[96,512]{1,0:T(8,128)(2,1)S(1)}, bf16[96,512]{1,0:T(8,128)(2,1)S(1)}, u32[]{:S(2)}, u32[]{:S(2)}) collective-permute-start(bf16[96,512]{1,0:T(8,128)(2,1)S(1)} %get-tuple-element.66), channel_id=1, source_target_pairs={{0,12},{2,14},{4,0},{6,2},{8,4},{10,6},{12,8},{14,10},{1,13},{3,15... | collective-permute-start | bytes 294920 | tf_op jit(solution)/shard_map/ppermute | solution.py:355
  68.2 29.5 %all-to-all-start.1 = ((f32[8,32,1536]{2,1,0:T(8,128)}), f32[8,32,1536]{2,1,0:T(8,128)S(1)}, u32[]{:S(2)}, u32[]{:S(2)}) async-start(f32[8,32,1536]{2,1,0:T(8,128)} %shard_map.59), calls=%async_computation.1 | async-start | bytes 3145728 | tf_op jit(solution)/shard_map/all_to_all | solution.py:377
  74.8 8.3 %collective-permute-start.12 = (bf16[96,512]{1,0:T(8,128)(2,1)S(1)}, bf16[96,512]{1,0:T(8,128)(2,1)S(1)}, u32[]{:S(2)}, u32[]{:S(2)}) collective-permute-start(bf16[96,512]{1,0:T(8,128)(2,1)S(1)} %get-tuple-element.73), channel_id=1, source_target_pairs={{0,2},{2,4},{4,6},{6,8},{8,10},{10,12},{12,14},{14,0},{1,3},{3,5},... | collective-permute-start | bytes 294920 | tf_op jit(solution)/shard_map/ppermute | solution.py:355
  74.8 13.2 %collective-permute-start.13 = (bf16[96,512]{1,0:T(8,128)(2,1)S(1)}, bf16[96,512]{1,0:T(8,128)(2,1)S(1)}, u32[]{:S(2)}, u32[]{:S(2)}) collective-permute-start(bf16[96,512]{1,0:T(8,128)(2,1)S(1)} %get-tuple-element.75), channel_id=1, source_target_pairs={{0,6},{2,8},{4,10},{6,12},{8,14},{10,0},{12,2},{14,4},{1,7},{3,9},... | collective-permute-start | bytes 294920 | tf_op jit(solution)/shard_map/ppermute | solution.py:355
  77.5 12.8 %collective-permute-start.14 = (bf16[96,512]{1,0:T(8,128)(2,1)S(1)}, bf16[96,512]{1,0:T(8,128)(2,1)S(1)}, u32[]{:S(2)}, u32[]{:S(2)}) collective-permute-start(bf16[96,512]{1,0:T(8,128)(2,1)S(1)} %get-tuple-element.76), channel_id=1, source_target_pairs={{0,8},{2,10},{4,12},{6,14},{8,0},{10,2},{12,4},{14,6},{1,9},{3,11}... | collective-permute-start | bytes 294920 | tf_op jit(solution)/shard_map/ppermute | solution.py:355
  80.5 11.5 %collective-permute-start.15 = (bf16[96,512]{1,0:T(8,128)(2,1)S(1)}, bf16[96,512]{1,0:T(8,128)(2,1)S(1)}, u32[]{:S(2)}, u32[]{:S(2)}) collective-permute-start(bf16[96,512]{1,0:T(8,128)(2,1)S(1)} %get-tuple-element.77), channel_id=1, source_target_pairs={{0,10},{2,12},{4,14},{6,0},{8,2},{10,4},{12,6},{14,8},{1,11},{3,13... | collective-permute-start | bytes 294920 | tf_op jit(solution)/shard_map/ppermute | solution.py:355
  82.0 11.7 %collective-permute-start.16 = (bf16[96,512]{1,0:T(8,128)(2,1)S(1)}, bf16[96,512]{1,0:T(8,128)(2,1)S(1)}, u32[]{:S(2)}, u32[]{:S(2)}) collective-permute-start(bf16[96,512]{1,0:T(8,128)(2,1)S(1)} %get-tuple-element.79), channel_id=1, source_target_pairs={{0,14},{2,0},{4,2},{6,4},{8,6},{10,8},{12,10},{14,12},{1,15},{3,1}... | collective-permute-start | bytes 294920 | tf_op jit(solution)/shard_map/ppermute | solution.py:355
  93.6 12.6 %copy-start.3 = (bf16[8,96,512]{2,1,0:T(8,128)(2,1)}, bf16[8,96,512]{2,1,0:T(8,128)(2,1)S(1)}, u32[]{:S(2)}) copy-start(bf16[8,96,512]{2,1,0:T(8,128)(2,1)S(1)} %bitcast_dynamic-update-slice_fusion.refs_0_) | copy-start | bytes 2359300
  93.6 17.1 %collective-permute-start.17 = (bf16[8,96,512]{2,1,0:T(8,128)(2,1)S(1)}, bf16[8,96,512]{2,1,0:T(8,128)(2,1)S(1)}, u32[]{:S(2)}, u32[]{:S(2)}) collective-permute-start(bf16[8,96,512]{2,1,0:T(8,128)(2,1)S(1)} %bitcast_dynamic-update-slice_fusion.refs_0_), channel_id=1, source_target_pairs={{0,1},{1,0},{2,3},{3,2},{4,5},{5,4},{6,7},{7,6},{8,9},{9,8},{10,11... | collective-permute-start | bytes 2359304 | tf_op jit(solution)/shard_map/ppermute | solution.py:346
  97.7 3.5 %collective-permute-start.20 = (f32[32,512]{1,0:T(8,128)S(1)}, f32[32,512]{1,0:T(8,128)S(1)}, u32[]{:S(2)}, u32[]{:S(2)}) collective-permute-start(f32[32,512]{1,0:T(8,128)S(1)} %get-tuple-element.84.half), channel_id=1, source_target_pairs={{0,2},{2,0},{4,6},{6,4},{8,10},{10,8},{12,14},{14,12},{1,3},{3,1},... | collective-permute-start | bytes 196616 | tf_op jit(solution)/shard_map/ppermute | solution.py:346
  102.4 23.0 %all-to-all-start.2 = ((bf16[8,2,32,1024]{3,2,1,0:T(8,128)(2,1)}), bf16[8,2,32,1024]{3,2,1,0:T(8,128)(2,1)S(1)}, u32[]{:S(2)}, u32[]{:S(2)}) async-start(bf16[8,2,32,1024]{3,2,1,0:T(8,128)(2,1)} %shard_map.62), calls=%async_computation.2 | async-start | bytes 2097152 | tf_op jit(solution)/shard_map/all_to_all | solution.py:383
  106.2 10.0 %collective-permute-start.18 = (bf16[8,96,512]{2,1,0:T(8,128)(2,1)S(1)}, bf16[8,96,512]{2,1,0:T(8,128)(2,1)S(1)}, u32[]{:S(2)}, u32[]{:S(2)}) collective-permute-start(bf16[8,96,512]{2,1,0:T(8,128)(2,1)S(1)} %bitcast_dynamic-update-slice_fusion.refs_0_), channel_id=1, source_target_pairs={{0,16},{16,0},{1,17},{17,1},{2,18},{18,2},{3,19},{19,3},{4,20},{20... | collective-permute-start | bytes 2359304 | tf_op jit(solution)/shard_map/ppermute | solution.py:346
  110.8 5.5 %copy-start.4 = (bf16[8,96,512]{2,1,0:T(8,128)(2,1)}, bf16[8,96,512]{2,1,0:T(8,128)(2,1)S(1)}, u32[]{:S(2)}) copy-start(bf16[8,96,512]{2,1,0:T(8,128)(2,1)S(1)} %collective-permute-done.17.refs_1_) | copy-start | bytes 2359300
  110.8 7.4 %collective-permute-start.19 = (bf16[8,96,512]{2,1,0:T(8,128)(2,1)S(1)}, bf16[8,96,512]{2,1,0:T(8,128)(2,1)S(1)}, u32[]{:S(2)}, u32[]{:S(2)}) collective-permute-start(bf16[8,96,512]{2,1,0:T(8,128)(2,1)S(1)} %collective-permute-done.17.refs_1_), channel_id=1, source_target_pairs={{0,16},{16,0},{1,17},{17,1},{2,18},{18,2},{3,19},{19,3},{4,20},{20... | collective-permute-start | bytes 2359304 | tf_op jit(solution)/shard_map/ppermute | solution.py:346
  127.9 32.1 %copy-start.1 = (bf16[768,768]{1,0:T(8,128)(2,1)S(1)}, bf16[768,768]{1,0:T(8,128)(2,1)}, u32[]{:S(2)}) copy-start(bf16[768,768]{1,0:T(8,128)(2,1)} %w_ref.5) | copy-start | bytes 3538948

commit v16 on v14

--- a/solution.py
+++ b/solution.py
@@ -73,15 +73,23 @@
 
 def key_kernel(me_ref, x_hbm, w_hbm, n_ref, *rest):
     outs, (x_ref, w_ref, t_ref, sems) = rest[:Z], rest[Z:]
-    copy_x, copy_w = fetches((x_hbm, w_hbm), (x_ref, w_ref), sems)
-    copy_x.wait()
-    x = x_ref[...].astype(f32)
-    centred = x - jnp.mean(x, axis=-1, keepdims=True)
-    var = jnp.mean(centred * centred, axis=-1, keepdims=True)
-    normed = (centred * lax.rsqrt(var + 1e-05)).astype(bf16)
-    for h in range(2):
-        n_ref[h] = normed[:, h * SUB : (h + 1) * SUB, :]
-    copy_w.wait()
+    rows = [slice(r, r + 2) for r in range(0, ROWS, 2)]
+    columns = [slice(c, c + EMBED // 4) for c in range(0, EMBED, EMBED // 4)]
+    copies = fetches(
+        [x_hbm.at[r] for r in rows] + [w_hbm.at[c] for c in columns],
+        [x_ref.at[r] for r in rows] + [w_ref.at[c] for c in columns],
+        sems,
+    )
+    for r, copy in zip(rows, copies):
+        copy.wait()
+        x = x_ref[r].astype(f32)
+        centred = x - jnp.mean(x, axis=-1, keepdims=True)
+        var = jnp.mean(centred * centred, axis=-1, keepdims=True)
+        normed = (centred * lax.rsqrt(var + 1e-05)).astype(bf16)
+        for h in range(2):
+            n_ref[h, r] = normed[:, h * SUB : (h + 1) * SUB, :]
+    for copy in copies[len(rows) :]:
+        copy.wait()
     t_ref[...] = dot(w_ref[...], n_ref[...].reshape(ROWS * RES, EMBED), 0, 1).astype(bf16)
     for s, out in enumerate(outs):
         z = lax.rem(me_ref[2] + s, Z)
@@ -104,7 +112,7 @@
             pltpu.VMEM((ROWS, RES, EMBED), bf16),
             pltpu.VMEM((EMBED, EMBED), bf16),
             pltpu.VMEM((EMBED, ROWS * RES), bf16),
-            pltpu.SemaphoreType.DMA((2,)),
+            pltpu.SemaphoreType.DMA((8,)),
         ],
         compiler_params=PARAMS,
     )(me, *in_hbm(x, w))

time: 161 us -> 161 us (level)
  no operation moved by 1% of the time
where the time goes in v16:
time: 161 us
  starting transfers between devices  59.8 us (37%)
  waiting for transfers between devices  42.2 us (26%)
  blocking collectives  32.3 us (20%)
  Pallas kernels  25.1 us (16%)
    all_to_all x1, blocking collectives, local(): mixed = lax.all_to_all(mix(me, laid, probs), ('z', 'c'), 0, 0, tiled=True)  32.3 us
    ppermute x14, starting transfers between devices, shift(): return lax.ppermute(x, 'z', [(i, (i + s) % Z) for i in range(Z)])  30.6 us
    ppermute x7, waiting for transfers between devices, flip(): return lax.ppermute(x, axes, [(i, i ^ s) for i in range(n)])  19.8 us
    ppermute x14, waiting for transfers between devices, shift(): return lax.ppermute(x, 'z', [(i, (i + s) % Z) for i in range(Z)])  13.5 us
    ppermute x7, starting transfers between devices, flip(): return lax.ppermute(x, axes, [(i, i ^ s) for i in range(n)])  12.9 us
    all_to_all x1, starting transfers between devices, local(): parts = lax.all_to_all(scores, ('y', 'xh'), 0, 0, tiled=True)  6.68 us
    all_to_all x1, starting transfers between devices, local(): q = lax.all_to_all(q, ('z', 'c'), 0, 0, tiled=True)  5.95 us
    pallas_call x1, Pallas kernels, score(): pl.pallas_call(score_kernel, out_shape=jax.ShapeDtypeStruct((PEERS, SUB,...  5.92 us
  transfers between devices with their start and end apart: 24, of which 13 were waited for; matrix products, arithmetic and copies ran while one was open for 1% of the time, Pallas kernels for 11%

profile of v16, /device:TPU:1, one launch (start us, length us, event | category | flops | bytes accessed | tf_op | source)
XLA Modules:
  0.0 160.8 jit_solution(2551743864160880411)
XLA Ops:
  0.1 3.3 %shard_map.55 = (bf16[2,8,32,768]{3,2,1,0:T(8,128)(2,1)S(1)}, bf16[96,512]{1,0:T(8,128)(2,1)S(1)}, bf16[96,512]{1,0:T(8,128)(2,1)S(1)}, bf16[96,512]{1,0:T(8,128...) custom-call(s32[3]{0:T(128)S(1)} %pad_add_fusion.me_ref, ...), custom_call_target="tpu_custom_call" | custom-call | tf_op jit(solution)/shard_map/pallas_call | solution.py:105
  3.4 2.5 %collective-permute-start.1 = (bf16[96,512]{1,0:T(8,128)(2,1)S(1)}, bf16[96,512]{1,0:T(8,128)(2,1)S(1)}, u32[]{:S(2)}, u32[]{:S(2)}) collective-permute-start(bf16[96,512]{1,0:T(8,128)(2,1)S(1)} %get-tuple-element.52), channel_id=1, source_target_pairs={{0,2},{2,4},{4,6},{6,8},{8,10},{10,12},{12,14},{14,0},{1,3},{3,5},... | collective-permute-start | bytes 294920 | tf_op jit(solution)/shard_map/ppermute | solution.py:363
  5.9 4.0 %collective-permute-start.2 = (bf16[96,512]{1,0:T(8,128)(2,1)S(1)}, bf16[96,512]{1,0:T(8,128)(2,1)S(1)}, u32[]{:S(2)}, u32[]{:S(2)}) collective-permute-start(bf16[96,512]{1,0:T(8,128)(2,1)S(1)} %get-tuple-element.53), channel_id=1, source_target_pairs={{0,14},{2,0},{4,2},{6,4},{8,6},{10,8},{12,10},{14,12},{1,15},{3,1}... | collective-permute-start | bytes 294920 | tf_op jit(solution)/shard_map/ppermute | solution.py:363
  10.0 3.6 %collective-permute-start.4 = (bf16[96,512]{1,0:T(8,128)(2,1)S(1)}, bf16[96,512]{1,0:T(8,128)(2,1)S(1)}, u32[]{:S(2)}, u32[]{:S(2)}) collective-permute-start(bf16[96,512]{1,0:T(8,128)(2,1)S(1)} %get-tuple-element.55), channel_id=1, source_target_pairs={{0,12},{2,14},{4,0},{6,2},{8,4},{10,6},{12,8},{14,10},{1,13},{3,15... | collective-permute-start | bytes 294920 | tf_op jit(solution)/shard_map/ppermute | solution.py:363
  13.9 1.8 %shard_map.57 = bf16[16,128,256]{2,1,0:T(8,128)(2,1)} custom-call(bf16[2,8,32,768]{3,2,1,0:T(8,128)(2,1)S(1)} %get-tuple-element.46.n_ref, bf16[768,768]{1,0:T(8,128)(2,1)S(1)} %copy-done), custom_call_target="tpu_custom_call" | custom-call | flops 603979776 | bytes 2752512 | tf_op jit(solution)/shard_map/pallas_call | solution.py:132
  15.7 3.6 %collective-permute-start.6 = (bf16[96,512]{1,0:T(8,128)(2,1)S(1)}, bf16[96,512]{1,0:T(8,128)(2,1)S(1)}, u32[]{:S(2)}, u32[]{:S(2)}) collective-permute-start(bf16[96,512]{1,0:T(8,128)(2,1)S(1)} %get-tuple-element.60), channel_id=1, source_target_pairs={{0,8},{2,10},{4,12},{6,14},{8,0},{10,2},{12,4},{14,6},{1,9},{3,11}... | collective-permute-start | bytes 294920 | tf_op jit(solution)/shard_map/ppermute | solution.py:363
  19.3 4.5 %collective-permute-start.7 = (bf16[96,512]{1,0:T(8,128)(2,1)S(1)}, bf16[96,512]{1,0:T(8,128)(2,1)S(1)}, u32[]{:S(2)}, u32[]{:S(2)}) collective-permute-start(bf16[96,512]{1,0:T(8,128)(2,1)S(1)} %get-tuple-element.61), channel_id=1, source_target_pairs={{0,10},{2,12},{4,14},{6,0},{8,2},{10,4},{12,6},{14,8},{1,11},{3,13... | collective-permute-start | bytes 294920 | tf_op jit(solution)/shard_map/ppermute | solution.py:363
  23.7 3.6 %collective-permute-done.5 = bf16[96,512]{1,0:T(8,128)(2,1)} collective-permute-done((bf16[96,512]{1,0:T(8,128)(2,1)S(1)}, bf16[96,512]{1,0:T(8,128)(2,1)}, u32[]{:S(2)}, u32[]{:S(2)}) %collective-permute-start.5) | collective-permute-done | bytes 98336 | tf_op jit(solution)/shard_map/ppermute | solution.py:363
  27.3 5.9 %all-to-all-start = ((bf16[16,128,256]{2,1,0:T(8,128)(2,1)}), bf16[16,128,256]{2,1,0:T(8,128)(2,1)}, u32[]{:S(2)}, u32[]{:S(2)}) async-start(bf16[16,128,256]{2,1,0:T(8,128)(2,1)} %shard_map.57), calls=%async_computation | async-start | bytes 2097152 | tf_op jit(solution)/shard_map/all_to_all | solution.py:376
  37.3 1.8 %shard_map.58 = (bf16[1024,512]{1,0:T(8,128)(2,1)S(1)}, bf16[1024,256]{1,0:T(8,128)(2,1)S(1)}) custom-call(s32[3]{0:T(128)S(1)} %pad_add_fusion.me_ref, bf16[8,96,512]{2,1,0:T(8,128)(2,1)S(1)} %bitcast_dynamic-update-slice_fusion.8.own, bf16[8,96,512]{2,1,0:T(8,128)(2,1)S(1)} %collective-permute-done.9.other), custom_call_target="tpu_custom_call" | custom-call | bytes 6291456 | tf_op jit(solution)/shard_map/pallas_call | solution.py:181
  39.1 14.4 %collective-permute-done.8.own_hbm = bf16[8,96,512]{2,1,0:T(8,128)(2,1)S(1)} collective-permute-done((bf16[8,96,512]{2,1,0:T(8,128)(2,1)S(1)}, bf16[8,96,512]{2,1,0:T(8,128)(2,1)S(1)}, u32[]{:S(2)}, u32[]{:S(2)}) %collective-permute-start.8) | collective-permute-done | bytes 786464 | tf_op jit(solution)/shard_map/ppermute | solution.py:354
  54.6 2.5 %collective-permute-start = (bf16[96,512]{1,0:T(8,128)(2,1)S(1)}, bf16[96,512]{1,0:T(8,128)(2,1)S(1)}, u32[]{:S(2)}, u32[]{:S(2)}) collective-permute-start(bf16[96,512]{1,0:T(8,128)(2,1)S(1)} %get-tuple-element.49), channel_id=1, source_target_pairs={{0,4},{2,6},{4,8},{6,10},{8,12},{10,14},{12,0},{14,2},{1,5},{3,7},... | collective-permute-start | bytes 294920 | tf_op jit(solution)/shard_map/ppermute | solution.py:363
  58.3 3.0 %all-to-all-done.q_hbm = bf16[16,128,256]{2,1,0:T(8,128)(2,1)} async-done(((bf16[16,128,256]{2,1,0:T(8,128)(2,1)}), bf16[16,128,256]{2,1,0:T(8,128)(2,1)}, u32[]{:S(2)}, u32[]{:S(2)}) %all-to-all-start) | async-done | bytes 1048608 | tf_op jit(solution)/shard_map/all_to_all | solution.py:376
  61.3 5.9 %shard_map.59 = f32[8,32,1536]{2,1,0:T(8,128)} custom-call(s32[3]{0:T(128)S(1)} %pad_add_fusion.me_ref, bf16[16,128,256]{2,1,0:T(8,128)(2,1)} %all-to-all-done.q_hbm, bf16[1024,512]{1,0:T(8,128)(2,1)S(1)} %get-tuple-element.71.kf_hbm, bf16[1024,256]{1,0:T(8,128)(2,1)S(1)} %get-tuple-element.72.kh_hbm, bf16[8,96,512]{2,1,0:T(8,128)(2,1)} %copy-done.5, ...), custom_call_target="tpu_custom_call" | custom-call | tf_op jit(solution)/shard_map/pallas_call | solution.py:217
  67.3 6.7 %all-to-all-start.1 = ((f32[8,32,1536]{2,1,0:T(8,128)}), f32[8,32,1536]{2,1,0:T(8,128)S(1)}, u32[]{:S(2)}, u32[]{:S(2)}) async-start(f32[8,32,1536]{2,1,0:T(8,128)} %shard_map.59), calls=%async_computation.1 | async-start | bytes 3145728 | tf_op jit(solution)/shard_map/all_to_all | solution.py:385
  73.9 2.6 %collective-permute-start.13 = (bf16[96,512]{1,0:T(8,128)(2,1)S(1)}, bf16[96,512]{1,0:T(8,128)(2,1)S(1)}, u32[]{:S(2)}, u32[]{:S(2)}) collective-permute-start(bf16[96,512]{1,0:T(8,128)(2,1)S(1)} %get-tuple-element.77), channel_id=1, source_target_pairs={{0,6},{2,8},{4,10},{6,12},{8,14},{10,0},{12,2},{14,4},{1,7},{3,9},... | collective-permute-start | bytes 294920 | tf_op jit(solution)/shard_map/ppermute | solution.py:363
  76.6 3.0 %collective-permute-start.14 = (bf16[96,512]{1,0:T(8,128)(2,1)S(1)}, bf16[96,512]{1,0:T(8,128)(2,1)S(1)}, u32[]{:S(2)}, u32[]{:S(2)}) collective-permute-start(bf16[96,512]{1,0:T(8,128)(2,1)S(1)} %get-tuple-element.78), channel_id=1, source_target_pairs={{0,8},{2,10},{4,12},{6,14},{8,0},{10,2},{12,4},{14,6},{1,9},{3,11}... | collective-permute-start | bytes 294920 | tf_op jit(solution)/shard_map/ppermute | solution.py:363
  79.6 1.5 collective-permute-start.15
  82.6 3.5 %collective-permute-done.13 = bf16[96,512]{1,0:T(8,128)(2,1)S(1)} collective-permute-done((bf16[96,512]{1,0:T(8,128)(2,1)S(1)}, bf16[96,512]{1,0:T(8,128)(2,1)S(1)}, u32[]{:S(2)}, u32[]{:S(2)}) %collective-permute-start.13) | collective-permute-done | bytes 98336 | tf_op jit(solution)/shard_map/ppermute | solution.py:363
  86.1 3.2 %collective-permute-done.14 = bf16[96,512]{1,0:T(8,128)(2,1)S(1)} collective-permute-done((bf16[96,512]{1,0:T(8,128)(2,1)S(1)}, bf16[96,512]{1,0:T(8,128)(2,1)S(1)}, u32[]{:S(2)}, u32[]{:S(2)}) %collective-permute-start.14) | collective-permute-done | bytes 98336 | tf_op jit(solution)/shard_map/ppermute | solution.py:363
  89.4 1.8 %collective-permute-done.15 = bf16[96,512]{1,0:T(8,128)(2,1)S(1)} collective-permute-done((bf16[96,512]{1,0:T(8,128)(2,1)S(1)}, bf16[96,512]{1,0:T(8,128)(2,1)S(1)}, u32[]{:S(2)}, u32[]{:S(2)}) %collective-permute-start.15) | collective-permute-done | bytes 98336 | tf_op jit(solution)/shard_map/ppermute | solution.py:363
  92.7 4.1 %all-to-all-done.1.parts = f32[8,32,1536]{2,1,0:T(8,128)S(1)} async-done(((f32[8,32,1536]{2,1,0:T(8,128)}), f32[8,32,1536]{2,1,0:T(8,128)S(1)}, u32[]{:S(2)}, u32[]{:S(2)}) %all-to-all-start.1) | async-done | bytes 1572896 | tf_op jit(solution)/shard_map/all_to_all | solution.py:385
  96.9 3.4 %collective-permute-done.20.other = f32[32,512]{1,0:T(8,128)S(1)} collective-permute-done((f32[32,512]{1,0:T(8,128)S(1)}, f32[32,512]{1,0:T(8,128)S(1)}, u32[]{:S(2)}, u32[]{:S(2)}) %collective-permute-start.20) | collective-permute-done | bytes 65568 | tf_op jit(solution)/shard_map/ppermute | solution.py:354
  101.6 3.7 %all-to-all-start.2 = ((bf16[8,2,32,1024]{3,2,1,0:T(8,128)(2,1)}), bf16[8,2,32,1024]{3,2,1,0:T(8,128)(2,1)S(1)}, u32[]{:S(2)}, u32[]{:S(2)}) async-start(bf16[8,2,32,1024]{3,2,1,0:T(8,128)(2,1)} %shard_map.62), calls=%async_computation.2 | async-start | bytes 2097152 | tf_op jit(solution)/shard_map/all_to_all | solution.py:391
  105.3 3.7 %collective-permute-start.18 = (bf16[8,96,512]{2,1,0:T(8,128)(2,1)S(1)}, bf16[8,96,512]{2,1,0:T(8,128)(2,1)S(1)}, u32[]{:S(2)}, u32[]{:S(2)}) collective-permute-start(bf16[8,96,512]{2,1,0:T(8,128)(2,1)S(1)} %bitcast_dynamic-update-slice_fusion.refs_0_), channel_id=1, source_target_pairs={{0,16},{16,0},{1,17},{17,1},{2,18},{18,2},{3,19},{19,3},{4,20},{20... | collective-permute-start | bytes 2359304 | tf_op jit(solution)/shard_map/ppermute | solution.py:354
  109.0 6.2 %collective-permute-start.19 = (bf16[8,96,512]{2,1,0:T(8,128)(2,1)S(1)}, bf16[8,96,512]{2,1,0:T(8,128)(2,1)S(1)}, u32[]{:S(2)}, u32[]{:S(2)}) collective-permute-start(bf16[8,96,512]{2,1,0:T(8,128)(2,1)S(1)} %collective-permute-done.17.refs_1_), channel_id=1, source_target_pairs={{0,16},{16,0},{1,17},{17,1},{2,18},{18,2},{3,19},{19,3},{4,20},{20... | collective-permute-start | bytes 2359304 | tf_op jit(solution)/shard_map/ppermute | solution.py:354
  115.2 1.9 %collective-permute-done.19.refs_3_ = bf16[8,96,512]{2,1,0:T(8,128)(2,1)S(1)} collective-permute-done((bf16[8,96,512]{2,1,0:T(8,128)(2,1)S(1)}, bf16[8,96,512]{2,1,0:T(8,128)(2,1)S(1)}, u32[]{:S(2)}, u32[]{:S(2)}) %collective-permute-start.19) | collective-permute-done | bytes 786464 | tf_op jit(solution)/shard_map/ppermute | solution.py:354
  117.1 5.4 %shard_map.60 = (bf16[1024,1024]{1,0:T(8,128)(2,1)S(1)}, bf16[512,1024]{1,0:T(8,128)(2,1)}) custom-call(s32[3]{0:T(128)S(1)} %pad_add_fusion.me_ref, bf16[8,96,512]{2,1,0:T(8,128)(2,1)} %copy-done.3, bf16[8,96,512]{2,1,0:T(8,128)(2,1)} %copy-done.4, bf16[8,96,512]{2,1,0:T(8,128)(2,1)S(1)} %collective-permute-done.18.refs_2_, ...), custom_call_target="tpu_custom_call" | custom-call | bytes 6291456 | tf_op jit(solution)/shard_map/pallas_call | solution.py:290
  122.6 1.7 %all-to-all-done.2.p_ref = bf16[8,2,32,1024]{3,2,1,0:T(8,128)(2,1)S(1)} async-done(((bf16[8,2,32,1024]{3,2,1,0:T(8,128)(2,1)}), bf16[8,2,32,1024]{3,2,1,0:T(8,128)(2,1)S(1)}, u32[]{:S(2)}, u32[]{:S(2)}) %all-to-all-start.2) | async-done | bytes 1048608 | tf_op jit(solution)/shard_map/all_to_all | solution.py:391
  124.3 2.5 %shard_map.63 = bf16[16,96,256]{2,1,0:T(8,128)(2,1)S(1)} custom-call(s32[3]{0:T(128)S(1)} %pad_add_fusion.me_ref, bf16[1024,1024]{1,0:T(8,128)(2,1)S(1)} %get-tuple-element.82.vf, bf16[512,1024]{1,0:T(8,128)(2,1)} %get-tuple-element.83.vh_hbm, bf16[8,2,32,1024]{3,2,1,0:T(8,128)(2,1)S(1)} %all-to-all-done.2.p_ref), custom_call_target="tpu_custom_call" | custom-call | tf_op jit(solution)/shard_map/pallas_call | solution.py:322
  126.8 32.3 %all_to_all.20.m_ref = bf16[16,96,256]{2,1,0:T(8,128)(2,1)S(1)} all-to-all(bf16[16,96,256]{2,1,0:T(8,128)(2,1)S(1)} %shard_map.63), channel_id=1, replica_groups=mesh['y'=4,'xh'=2,'c'=2,'z'=8,'xl'=2] {'z','c'}, dimensions={0} | all-to-all | bytes 1572864 | tf_op jit(solution)/shard_map/all_to_all | solution.py:393
  159.1 1.7 %shard_map.64 = bf16[8,64,768]{2,1,0:T(8,128)(2,1)} custom-call(bf16[16,96,256]{2,1,0:T(8,128)(2,1)S(1)} %all_to_all.20.m_ref, bf16[768,768]{1,0:T(8,128)(2,1)S(1)} %copy-done.1), custom_call_target="tpu_custom_call" | custom-call | tf_op jit(solution)/shard_map/pallas_call | solution.py:343
  (56 shorter events, 11.2 us)
Async XLA Ops:
  0.0 13.9 %copy-start = (bf16[768,768]{1,0:T(8,128)(2,1)S(1)}, bf16[768,768]{1,0:T(8,128)(2,1)}, u32[]{:S(2)}) copy-start(bf16[768,768]{1,0:T(8,128)(2,1)} %w_ref.4) | copy-start | bytes 3538948
  3.4 12.3 %collective-permute-start.1 = (bf16[96,512]{1,0:T(8,128)(2,1)S(1)}, bf16[96,512]{1,0:T(8,128)(2,1)S(1)}, u32[]{:S(2)}, u32[]{:S(2)}) collective-permute-start(bf16[96,512]{1,0:T(8,128)(2,1)S(1)} %get-tuple-element.52), channel_id=1, source_target_pairs={{0,2},{2,4},{4,6},{6,8},{8,10},{10,12},{12,14},{14,0},{1,3},{3,5},... | collective-permute-start | bytes 294920 | tf_op jit(solution)/shard_map/ppermute | solution.py:363
  5.9 13.4 %collective-permute-start.2 = (bf16[96,512]{1,0:T(8,128)(2,1)S(1)}, bf16[96,512]{1,0:T(8,128)(2,1)S(1)}, u32[]{:S(2)}, u32[]{:S(2)}) collective-permute-start(bf16[96,512]{1,0:T(8,128)(2,1)S(1)} %get-tuple-element.53), channel_id=1, source_target_pairs={{0,14},{2,0},{4,2},{6,4},{8,6},{10,8},{12,10},{14,12},{1,15},{3,1}... | collective-permute-start | bytes 294920 | tf_op jit(solution)/shard_map/ppermute | solution.py:363
  9.9 13.8 %collective-permute-start.3 = (bf16[96,512]{1,0:T(8,128)(2,1)S(1)}, bf16[96,512]{1,0:T(8,128)(2,1)S(1)}, u32[]{:S(2)}, u32[]{:S(2)}) collective-permute-start(bf16[96,512]{1,0:T(8,128)(2,1)S(1)} %get-tuple-element.54), channel_id=1, source_target_pairs={{0,4},{2,6},{4,8},{6,10},{8,12},{10,14},{12,0},{14,2},{1,5},{3,7},... | collective-permute-start | bytes 294920 | tf_op jit(solution)/shard_map/ppermute | solution.py:363
  10.0 13.8 %collective-permute-start.4 = (bf16[96,512]{1,0:T(8,128)(2,1)S(1)}, bf16[96,512]{1,0:T(8,128)(2,1)S(1)}, u32[]{:S(2)}, u32[]{:S(2)}) collective-permute-start(bf16[96,512]{1,0:T(8,128)(2,1)S(1)} %get-tuple-element.55), channel_id=1, source_target_pairs={{0,12},{2,14},{4,0},{6,2},{8,4},{10,6},{12,8},{14,10},{1,13},{3,15... | collective-permute-start | bytes 294920 | tf_op jit(solution)/shard_map/ppermute | solution.py:363
  13.5 13.8 %collective-permute-start.5 = (bf16[96,512]{1,0:T(8,128)(2,1)S(1)}, bf16[96,512]{1,0:T(8,128)(2,1)}, u32[]{:S(2)}, u32[]{:S(2)}) collective-permute-start(bf16[96,512]{1,0:T(8,128)(2,1)S(1)} %get-tuple-element.56), channel_id=1, source_target_pairs={{0,6},{2,8},{4,10},{6,12},{8,14},{10,0},{12,2},{14,4},{1,7},{3,9},... | collective-permute-start | bytes 294920 | tf_op jit(solution)/shard_map/ppermute | solution.py:363
  15.7 18.6 %collective-permute-start.6 = (bf16[96,512]{1,0:T(8,128)(2,1)S(1)}, bf16[96,512]{1,0:T(8,128)(2,1)S(1)}, u32[]{:S(2)}, u32[]{:S(2)}) collective-permute-start(bf16[96,512]{1,0:T(8,128)(2,1)S(1)} %get-tuple-element.60), channel_id=1, source_target_pairs={{0,8},{2,10},{4,12},{6,14},{8,0},{10,2},{12,4},{14,6},{1,9},{3,11}... | collective-permute-start | bytes 294920 | tf_op jit(solution)/shard_map/ppermute | solution.py:363
  19.3 15.1 %collective-permute-start.7 = (bf16[96,512]{1,0:T(8,128)(2,1)S(1)}, bf16[96,512]{1,0:T(8,128)(2,1)S(1)}, u32[]{:S(2)}, u32[]{:S(2)}) collective-permute-start(bf16[96,512]{1,0:T(8,128)(2,1)S(1)} %get-tuple-element.61), channel_id=1, source_target_pairs={{0,10},{2,12},{4,14},{6,0},{8,2},{10,4},{12,6},{14,8},{1,11},{3,13... | collective-permute-start | bytes 294920 | tf_op jit(solution)/shard_map/ppermute | solution.py:363
  27.3 34.0 %all-to-all-start = ((bf16[16,128,256]{2,1,0:T(8,128)(2,1)}), bf16[16,128,256]{2,1,0:T(8,128)(2,1)}, u32[]{:S(2)}, u32[]{:S(2)}) async-start(bf16[16,128,256]{2,1,0:T(8,128)(2,1)} %shard_map.57), calls=%async_computation | async-start | bytes 2097152 | tf_op jit(solution)/shard_map/all_to_all | solution.py:376
  33.3 2.6 %copy-start.2 = (bf16[768,768]{1,0:T(8,128)(2,1)S(1)}, bf16[768,768]{1,0:T(8,128)(2,1)}, u32[]{:S(2)}) copy-start(bf16[768,768]{1,0:T(8,128)(2,1)} %w_ref.3) | copy-start | bytes 3538948
  34.4 2.9 %collective-permute-start.9 = (bf16[8,96,512]{2,1,0:T(8,128)(2,1)S(1)}, bf16[8,96,512]{2,1,0:T(8,128)(2,1)S(1)}, u32[]{:S(2)}, u32[]{:S(2)}) collective-permute-start(bf16[8,96,512]{2,1,0:T(8,128)(2,1)S(1)} %bitcast_dynamic-update-slice_fusion.8.own), channel_id=1, source_target_pairs={{0,16},{16,0},{1,17},{17,1},{2,18},{18,2},{3,19},{19,3},{4,20},{20... | collective-permute-start | bytes 2359304 | tf_op jit(solution)/shard_map/ppermute | solution.py:354
  34.6 18.9 %collective-permute-start.8 = (bf16[8,96,512]{2,1,0:T(8,128)(2,1)S(1)}, bf16[8,96,512]{2,1,0:T(8,128)(2,1)S(1)}, u32[]{:S(2)}, u32[]{:S(2)}) collective-permute-start(bf16[8,96,512]{2,1,0:T(8,128)(2,1)S(1)} %bitcast_dynamic-update-slice_fusion.8.own), channel_id=1, source_target_pairs={{0,1},{1,0},{2,3},{3,2},{4,5},{5,4},{6,7},{7,6},{8,9},{9,8},{10,11... | collective-permute-start | bytes 2359304 | tf_op jit(solution)/shard_map/ppermute | solution.py:354
  53.5 4.8 %copy-start.5 = (bf16[8,96,512]{2,1,0:T(8,128)(2,1)}, bf16[8,96,512]{2,1,0:T(8,128)(2,1)S(1)}, u32[]{:S(2)}) copy-start(bf16[8,96,512]{2,1,0:T(8,128)(2,1)S(1)} %collective-permute-done.8.own_hbm) | copy-start | bytes 2359300
  53.5 4.8 %collective-permute-start.11 = (bf16[8,96,512]{2,1,0:T(8,128)(2,1)S(1)}, bf16[8,96,512]{2,1,0:T(8,128)(2,1)S(1)}, u32[]{:S(2)}, u32[]{:S(2)}) collective-permute-start(bf16[8,96,512]{2,1,0:T(8,128)(2,1)S(1)} %collective-permute-done.8.own_hbm), channel_id=1, source_target_pairs={{0,16},{16,0},{1,17},{17,1},{2,18},{18,2},{3,19},{19,3},{4,20},{20... | collective-permute-start | bytes 2359304 | tf_op jit(solution)/shard_map/ppermute | solution.py:354
  54.6 12.7 %collective-permute-start = (bf16[96,512]{1,0:T(8,128)(2,1)S(1)}, bf16[96,512]{1,0:T(8,128)(2,1)S(1)}, u32[]{:S(2)}, u32[]{:S(2)}) collective-permute-start(bf16[96,512]{1,0:T(8,128)(2,1)S(1)} %get-tuple-element.49), channel_id=1, source_target_pairs={{0,4},{2,6},{4,8},{6,10},{8,12},{10,14},{12,0},{14,2},{1,5},{3,7},... | collective-permute-start | bytes 294920 | tf_op jit(solution)/shard_map/ppermute | solution.py:363
  57.1 10.2 %collective-permute-start.10 = (bf16[96,512]{1,0:T(8,128)(2,1)S(1)}, bf16[96,512]{1,0:T(8,128)(2,1)S(1)}, u32[]{:S(2)}, u32[]{:S(2)}) collective-permute-start(bf16[96,512]{1,0:T(8,128)(2,1)S(1)} %get-tuple-element.68), channel_id=1, source_target_pairs={{0,12},{2,14},{4,0},{6,2},{8,4},{10,6},{12,8},{14,10},{1,13},{3,15... | collective-permute-start | bytes 294920 | tf_op jit(solution)/shard_map/ppermute | solution.py:363
  67.3 29.5 %all-to-all-start.1 = ((f32[8,32,1536]{2,1,0:T(8,128)}), f32[8,32,1536]{2,1,0:T(8,128)S(1)}, u32[]{:S(2)}, u32[]{:S(2)}) async-start(f32[8,32,1536]{2,1,0:T(8,128)} %shard_map.59), calls=%async_computation.1 | async-start | bytes 3145728 | tf_op jit(solution)/shard_map/all_to_all | solution.py:385
  73.9 8.7 %collective-permute-start.12 = (bf16[96,512]{1,0:T(8,128)(2,1)S(1)}, bf16[96,512]{1,0:T(8,128)(2,1)S(1)}, u32[]{:S(2)}, u32[]{:S(2)}) collective-permute-start(bf16[96,512]{1,0:T(8,128)(2,1)S(1)} %get-tuple-element.75), channel_id=1, source_target_pairs={{0,2},{2,4},{4,6},{6,8},{8,10},{10,12},{12,14},{14,0},{1,3},{3,5},... | collective-permute-start | bytes 294920 | tf_op jit(solution)/shard_map/ppermute | solution.py:363
  73.9 12.2 %collective-permute-start.13 = (bf16[96,512]{1,0:T(8,128)(2,1)S(1)}, bf16[96,512]{1,0:T(8,128)(2,1)S(1)}, u32[]{:S(2)}, u32[]{:S(2)}) collective-permute-start(bf16[96,512]{1,0:T(8,128)(2,1)S(1)} %get-tuple-element.77), channel_id=1, source_target_pairs={{0,6},{2,8},{4,10},{6,12},{8,14},{10,0},{12,2},{14,4},{1,7},{3,9},... | collective-permute-start | bytes 294920 | tf_op jit(solution)/shard_map/ppermute | solution.py:363
  76.6 12.8 %collective-permute-start.14 = (bf16[96,512]{1,0:T(8,128)(2,1)S(1)}, bf16[96,512]{1,0:T(8,128)(2,1)S(1)}, u32[]{:S(2)}, u32[]{:S(2)}) collective-permute-start(bf16[96,512]{1,0:T(8,128)(2,1)S(1)} %get-tuple-element.78), channel_id=1, source_target_pairs={{0,8},{2,10},{4,12},{6,14},{8,0},{10,2},{12,4},{14,6},{1,9},{3,11}... | collective-permute-start | bytes 294920 | tf_op jit(solution)/shard_map/ppermute | solution.py:363
  79.6 11.6 %collective-permute-start.15 = (bf16[96,512]{1,0:T(8,128)(2,1)S(1)}, bf16[96,512]{1,0:T(8,128)(2,1)S(1)}, u32[]{:S(2)}, u32[]{:S(2)}) collective-permute-start(bf16[96,512]{1,0:T(8,128)(2,1)S(1)} %get-tuple-element.79), channel_id=1, source_target_pairs={{0,10},{2,12},{4,14},{6,0},{8,2},{10,4},{12,6},{14,8},{1,11},{3,13... | collective-permute-start | bytes 294920 | tf_op jit(solution)/shard_map/ppermute | solution.py:363
  81.1 11.2 %collective-permute-start.16 = (bf16[96,512]{1,0:T(8,128)(2,1)S(1)}, bf16[96,512]{1,0:T(8,128)(2,1)S(1)}, u32[]{:S(2)}, u32[]{:S(2)}) collective-permute-start(bf16[96,512]{1,0:T(8,128)(2,1)S(1)} %get-tuple-element.81), channel_id=1, source_target_pairs={{0,14},{2,0},{4,2},{6,4},{8,6},{10,8},{12,10},{14,12},{1,15},{3,1}... | collective-permute-start | bytes 294920 | tf_op jit(solution)/shard_map/ppermute | solution.py:363
  92.3 13.0 %copy-start.3 = (bf16[8,96,512]{2,1,0:T(8,128)(2,1)}, bf16[8,96,512]{2,1,0:T(8,128)(2,1)S(1)}, u32[]{:S(2)}) copy-start(bf16[8,96,512]{2,1,0:T(8,128)(2,1)S(1)} %bitcast_dynamic-update-slice_fusion.refs_0_) | copy-start | bytes 2359300
  92.3 16.8 %collective-permute-start.17 = (bf16[8,96,512]{2,1,0:T(8,128)(2,1)S(1)}, bf16[8,96,512]{2,1,0:T(8,128)(2,1)S(1)}, u32[]{:S(2)}, u32[]{:S(2)}) collective-permute-start(bf16[8,96,512]{2,1,0:T(8,128)(2,1)S(1)} %bitcast_dynamic-update-slice_fusion.refs_0_), channel_id=1, source_target_pairs={{0,1},{1,0},{2,3},{3,2},{4,5},{5,4},{6,7},{7,6},{8,9},{9,8},{10,11... | collective-permute-start | bytes 2359304 | tf_op jit(solution)/shard_map/ppermute | solution.py:354
  96.8 3.5 %collective-permute-start.20 = (f32[32,512]{1,0:T(8,128)S(1)}, f32[32,512]{1,0:T(8,128)S(1)}, u32[]{:S(2)}, u32[]{:S(2)}) collective-permute-start(f32[32,512]{1,0:T(8,128)S(1)} %get-tuple-element.86.half), channel_id=1, source_target_pairs={{0,2},{2,0},{4,6},{6,4},{8,10},{10,8},{12,14},{14,12},{1,3},{3,1},... | collective-permute-start | bytes 196616 | tf_op jit(solution)/shard_map/ppermute | solution.py:354
  101.6 22.8 %all-to-all-start.2 = ((bf16[8,2,32,1024]{3,2,1,0:T(8,128)(2,1)}), bf16[8,2,32,1024]{3,2,1,0:T(8,128)(2,1)S(1)}, u32[]{:S(2)}, u32[]{:S(2)}) async-start(bf16[8,2,32,1024]{3,2,1,0:T(8,128)(2,1)} %shard_map.62), calls=%async_computation.2 | async-start | bytes 2097152 | tf_op jit(solution)/shard_map/all_to_all | solution.py:391
  105.3 9.9 %collective-permute-start.18 = (bf16[8,96,512]{2,1,0:T(8,128)(2,1)S(1)}, bf16[8,96,512]{2,1,0:T(8,128)(2,1)S(1)}, u32[]{:S(2)}, u32[]{:S(2)}) collective-permute-start(bf16[8,96,512]{2,1,0:T(8,128)(2,1)S(1)} %bitcast_dynamic-update-slice_fusion.refs_0_), channel_id=1, source_target_pairs={{0,16},{16,0},{1,17},{17,1},{2,18},{18,2},{3,19},{19,3},{4,20},{20... | collective-permute-start | bytes 2359304 | tf_op jit(solution)/shard_map/ppermute | solution.py:354
  109.0 6.2 %copy-start.4 = (bf16[8,96,512]{2,1,0:T(8,128)(2,1)}, bf16[8,96,512]{2,1,0:T(8,128)(2,1)S(1)}, u32[]{:S(2)}) copy-start(bf16[8,96,512]{2,1,0:T(8,128)(2,1)S(1)} %collective-permute-done.17.refs_1_) | copy-start | bytes 2359300
  109.0 8.1 %collective-permute-start.19 = (bf16[8,96,512]{2,1,0:T(8,128)(2,1)S(1)}, bf16[8,96,512]{2,1,0:T(8,128)(2,1)S(1)}, u32[]{:S(2)}, u32[]{:S(2)}) collective-permute-start(bf16[8,96,512]{2,1,0:T(8,128)(2,1)S(1)} %collective-permute-done.17.refs_1_), channel_id=1, source_target_pairs={{0,16},{16,0},{1,17},{17,1},{2,18},{18,2},{3,19},{19,3},{4,20},{20... | collective-permute-start | bytes 2359304 | tf_op jit(solution)/shard_map/ppermute | solution.py:354
  126.8 32.3 %copy-start.1 = (bf16[768,768]{1,0:T(8,128)(2,1)S(1)}, bf16[768,768]{1,0:T(8,128)(2,1)}, u32[]{:S(2)}) copy-start(bf16[768,768]{1,0:T(8,128)(2,1)} %w_ref.5) | copy-start | bytes 3538948

commit v17 on v14

--- a/solution.py
+++ b/solution.py
@@ -369,13 +369,13 @@
     v = list(value_chunks(me, n, wv))
     k = jnp.stack(k)
     near, shared = keys_laid(me, k, flip(k, "c", 2, 1))
-    k_far, v[4], shared = lax.optimization_barrier((flip(k, "xl", 2, 1), v[4], shared))
-    for s in (2, 6):
+    k_far, v[7], shared = lax.optimization_barrier((flip(k, "xl", 2, 1), v[7], shared))
+    for s in (4,):
         v[s] = shift(v[s], s)
     scores = score(me, q, (near, shared), k_far, flip(k_far, "c", 2, 1))
     *v, scores = lax.optimization_barrier((*v, scores))
     parts = lax.all_to_all(scores, ("y", "xh"), 0, 0, tiled=True)
-    for s in (4, 3, 5, 1, 7):
+    for s in (3, 5, 2, 6, 1, 7):
         v[s] = shift(v[s], s)
     full, half = total(parts)
     rows = ROWS * 2 * PEERS

time: 161 us -> 162 us (level)
  starting transfers between devices: 59.8 us -> 61.5 us
    ppermute x14, starting transfers between devices: 30.6 us -> 33.6 us  [shift(): return lax.ppermute(x, 'z', [(i, (i + s) % Z) for i in range(Z)])]
    ppermute x7, waiting for transfers between devices: 19.8 us -> 21.8 us  [flip(): return lax.ppermute(x, axes, [(i, i ^ s) for i in range(n)])]
    ppermute x7, starting transfers between devices: 12.9 us -> 11 us  [flip(): return lax.ppermute(x, axes, [(i, i ^ s) for i in range(n)])]
    all_to_all x1, waiting for transfers between devices: 3.01 us -> 1.21 us  [local(): q = lax.all_to_all(q, ('z', 'c'), 0, 0, tiled=True)]
  transfers between devices with their start and end apart: 24 -> 24, of which waited for: 13 -> 11; matrix products, arithmetic and copies ran while one was open for 1% -> 1% of each run, Pallas kernels for 11% -> 11%
where the time goes in v17:
time: 162 us; the launch traced here: 161 us
  starting transfers between devices  61.5 us (38%)
  waiting for transfers between devices  42.1 us (26%)
  blocking collectives  31.5 us (19%)
  Pallas kernels  24.8 us (15%)
    ppermute x14, starting transfers between devices, shift(): return lax.ppermute(x, 'z', [(i, (i + s) % Z) for i in range(Z)])  33.6 us
    all_to_all x1, blocking collectives, local(): mixed = lax.all_to_all(mix(me, laid, probs), ('z', 'c'), 0, 0, tiled=True)  31.5 us
    ppermute x7, waiting for transfers between devices, flip(): return lax.ppermute(x, axes, [(i, i ^ s) for i in range(n)])  21.8 us
    ppermute x14, waiting for transfers between devices, shift(): return lax.ppermute(x, 'z', [(i, (i + s) % Z) for i in range(Z)])  13.8 us
    ppermute x7, starting transfers between devices, flip(): return lax.ppermute(x, axes, [(i, i ^ s) for i in range(n)])  11 us
    all_to_all x1, starting transfers between devices, local(): parts = lax.all_to_all(scores, ('y', 'xh'), 0, 0, tiled=True)  6.66 us
    all_to_all x1, starting transfers between devices, local(): q = lax.all_to_all(q, ('z', 'c'), 0, 0, tiled=True)  5.95 us
    pallas_call x1, Pallas kernels, score(): pl.pallas_call(score_kernel, out_shape=jax.ShapeDtypeStruct((PEERS, SUB,...  5.92 us
  transfers between devices with their start and end apart: 24, of which 11 were waited for; matrix products, arithmetic and copies ran while one was open for 1% of the time, Pallas kernels for 11%

profile of v17, /device:TPU:1, one launch (start us, length us, event | category | flops | bytes accessed | tf_op | source)
XLA Modules:
  0.0 161.3 jit_solution(12295740439861921989)
XLA Ops:
  0.1 3.0 %shard_map.55 = (bf16[2,8,32,768]{3,2,1,0:T(8,128)(2,1)S(1)}, bf16[96,512]{1,0:T(8,128)(2,1)S(1)}, bf16[96,512]{1,0:T(8,128)(2,1)S(1)}, bf16[96,512]{1,0:T(8,128...) custom-call(s32[3]{0:T(128)S(1)} %pad_add_fusion.me_ref, ...), custom_call_target="tpu_custom_call" | custom-call | tf_op jit(solution)/shard_map/pallas_call | solution.py:97
  3.1 2.5 %collective-permute-start.1 = (bf16[96,512]{1,0:T(8,128)(2,1)S(1)}, bf16[96,512]{1,0:T(8,128)(2,1)S(1)}, u32[]{:S(2)}, u32[]{:S(2)}) collective-permute-start(bf16[96,512]{1,0:T(8,128)(2,1)S(1)} %get-tuple-element.55), channel_id=1, source_target_pairs={{0,2},{2,4},{4,6},{6,8},{8,10},{10,12},{12,14},{14,0},{1,3},{3,5},... | collective-permute-start | bytes 294920 | tf_op jit(solution)/shard_map/ppermute | solution.py:355
  5.6 4.0 %collective-permute-start.2 = (bf16[96,512]{1,0:T(8,128)(2,1)S(1)}, bf16[96,512]{1,0:T(8,128)(2,1)S(1)}, u32[]{:S(2)}, u32[]{:S(2)}) collective-permute-start(bf16[96,512]{1,0:T(8,128)(2,1)S(1)} %get-tuple-element.56), channel_id=1, source_target_pairs={{0,14},{2,0},{4,2},{6,4},{8,6},{10,8},{12,10},{14,12},{1,15},{3,1}... | collective-permute-start | bytes 294920 | tf_op jit(solution)/shard_map/ppermute | solution.py:355
  9.6 3.6 %collective-permute-start.4 = (bf16[96,512]{1,0:T(8,128)(2,1)S(1)}, bf16[96,512]{1,0:T(8,128)(2,1)S(1)}, u32[]{:S(2)}, u32[]{:S(2)}) collective-permute-start(bf16[96,512]{1,0:T(8,128)(2,1)S(1)} %get-tuple-element.58), channel_id=1, source_target_pairs={{0,12},{2,14},{4,0},{6,2},{8,4},{10,6},{12,8},{14,10},{1,13},{3,15... | collective-permute-start | bytes 294920 | tf_op jit(solution)/shard_map/ppermute | solution.py:355
  13.5 1.8 %shard_map.57 = bf16[16,128,256]{2,1,0:T(8,128)(2,1)} custom-call(bf16[2,8,32,768]{3,2,1,0:T(8,128)(2,1)S(1)} %get-tuple-element.46.n_ref, bf16[768,768]{1,0:T(8,128)(2,1)S(1)} %copy-done), custom_call_target="tpu_custom_call" | custom-call | flops 603979776 | bytes 2752512 | tf_op jit(solution)/shard_map/pallas_call | solution.py:124
  15.3 3.6 %collective-permute-start.6 = (bf16[96,512]{1,0:T(8,128)(2,1)S(1)}, bf16[96,512]{1,0:T(8,128)(2,1)S(1)}, u32[]{:S(2)}, u32[]{:S(2)}) collective-permute-start(bf16[96,512]{1,0:T(8,128)(2,1)S(1)} %get-tuple-element.63), channel_id=1, source_target_pairs={{0,8},{2,10},{4,12},{6,14},{8,0},{10,2},{12,4},{14,6},{1,9},{3,11}... | collective-permute-start | bytes 294920 | tf_op jit(solution)/shard_map/ppermute | solution.py:355
  19.0 4.5 %collective-permute-start.7 = (bf16[96,512]{1,0:T(8,128)(2,1)S(1)}, bf16[96,512]{1,0:T(8,128)(2,1)S(1)}, u32[]{:S(2)}, u32[]{:S(2)}) collective-permute-start(bf16[96,512]{1,0:T(8,128)(2,1)S(1)} %get-tuple-element.64), channel_id=1, source_target_pairs={{0,10},{2,12},{4,14},{6,0},{8,2},{10,4},{12,6},{14,8},{1,11},{3,13... | collective-permute-start | bytes 294920 | tf_op jit(solution)/shard_map/ppermute | solution.py:355
  23.4 3.6 %collective-permute-done.5 = bf16[96,512]{1,0:T(8,128)(2,1)} collective-permute-done((bf16[96,512]{1,0:T(8,128)(2,1)S(1)}, bf16[96,512]{1,0:T(8,128)(2,1)}, u32[]{:S(2)}, u32[]{:S(2)}) %collective-permute-start.5) | collective-permute-done | bytes 98336 | tf_op jit(solution)/shard_map/ppermute | solution.py:355
  27.0 5.9 %all-to-all-start = ((bf16[16,128,256]{2,1,0:T(8,128)(2,1)}), bf16[16,128,256]{2,1,0:T(8,128)(2,1)}, u32[]{:S(2)}, u32[]{:S(2)}) async-start(bf16[16,128,256]{2,1,0:T(8,128)(2,1)} %shard_map.57), calls=%async_computation | async-start | bytes 2097152 | tf_op jit(solution)/shard_map/all_to_all | solution.py:368
  36.9 1.8 %shard_map.58 = (bf16[1024,512]{1,0:T(8,128)(2,1)S(1)}, bf16[1024,256]{1,0:T(8,128)(2,1)S(1)}) custom-call(s32[3]{0:T(128)S(1)} %pad_add_fusion.me_ref, bf16[8,96,512]{2,1,0:T(8,128)(2,1)S(1)} %bitcast_dynamic-update-slice_fusion.8.own, bf16[8,96,512]{2,1,0:T(8,128)(2,1)S(1)} %collective-permute-done.9.other), custom_call_target="tpu_custom_call" | custom-call | bytes 6291456 | tf_op jit(solution)/shard_map/pallas_call | solution.py:173
  38.8 14.4 %collective-permute-done.8.own_hbm = bf16[8,96,512]{2,1,0:T(8,128)(2,1)S(1)} collective-permute-done((bf16[8,96,512]{2,1,0:T(8,128)(2,1)S(1)}, bf16[8,96,512]{2,1,0:T(8,128)(2,1)S(1)}, u32[]{:S(2)}, u32[]{:S(2)}) %collective-permute-start.8) | collective-permute-done | bytes 786464 | tf_op jit(solution)/shard_map/ppermute | solution.py:346
  54.3 5.5 %collective-permute-start = (bf16[96,512]{1,0:T(8,128)(2,1)S(1)}, bf16[96,512]{1,0:T(8,128)(2,1)S(1)}, u32[]{:S(2)}, u32[]{:S(2)}) collective-permute-start(bf16[96,512]{1,0:T(8,128)(2,1)S(1)} %get-tuple-element.51), channel_id=1, source_target_pairs={{0,8},{2,10},{4,12},{6,14},{8,0},{10,2},{12,4},{14,6},{1,9},{3,11}... | collective-permute-start | bytes 294920 | tf_op jit(solution)/shard_map/ppermute | solution.py:355
  61.0 5.9 %shard_map.59 = f32[8,32,1536]{2,1,0:T(8,128)} custom-call(s32[3]{0:T(128)S(1)} %pad_add_fusion.me_ref, bf16[16,128,256]{2,1,0:T(8,128)(2,1)} %all-to-all-done.q_hbm, bf16[1024,512]{1,0:T(8,128)(2,1)S(1)} %get-tuple-element.71.kf_hbm, bf16[1024,256]{1,0:T(8,128)(2,1)S(1)} %get-tuple-element.72.kh_hbm, bf16[8,96,512]{2,1,0:T(8,128)(2,1)} %copy-done.5, ...), custom_call_target="tpu_custom_call" | custom-call | tf_op jit(solution)/shard_map/pallas_call | solution.py:209
  66.9 6.7 %all-to-all-start.1 = ((f32[8,32,1536]{2,1,0:T(8,128)}), f32[8,32,1536]{2,1,0:T(8,128)S(1)}, u32[]{:S(2)}, u32[]{:S(2)}) async-start(f32[8,32,1536]{2,1,0:T(8,128)} %shard_map.59), calls=%async_computation.1 | async-start | bytes 3145728 | tf_op jit(solution)/shard_map/all_to_all | solution.py:377
  73.6 1.7 %collective-permute-start.12 = (bf16[96,512]{1,0:T(8,128)(2,1)S(1)}, bf16[96,512]{1,0:T(8,128)(2,1)S(1)}, u32[]{:S(2)}, u32[]{:S(2)}) collective-permute-start(bf16[96,512]{1,0:T(8,128)(2,1)S(1)} %get-tuple-element.76), channel_id=1, source_target_pairs={{0,4},{2,6},{4,8},{6,10},{8,12},{10,14},{12,0},{14,2},{1,5},{3,7},... | collective-permute-start | bytes 294920 | tf_op jit(solution)/shard_map/ppermute | solution.py:355
  75.3 2.2 %collective-permute-start.13 = (bf16[96,512]{1,0:T(8,128)(2,1)S(1)}, bf16[96,512]{1,0:T(8,128)(2,1)S(1)}, u32[]{:S(2)}, u32[]{:S(2)}) collective-permute-start(bf16[96,512]{1,0:T(8,128)(2,1)S(1)} %get-tuple-element.77), channel_id=1, source_target_pairs={{0,6},{2,8},{4,10},{6,12},{8,14},{10,0},{12,2},{14,4},{1,7},{3,9},... | collective-permute-start | bytes 294920 | tf_op jit(solution)/shard_map/ppermute | solution.py:355
  77.5 2.3 %collective-permute-start.14 = (bf16[96,512]{1,0:T(8,128)(2,1)S(1)}, bf16[96,512]{1,0:T(8,128)(2,1)S(1)}, u32[]{:S(2)}, u32[]{:S(2)}) collective-permute-start(bf16[96,512]{1,0:T(8,128)(2,1)S(1)} %get-tuple-element.79), channel_id=1, source_target_pairs={{0,10},{2,12},{4,14},{6,0},{8,2},{10,4},{12,6},{14,8},{1,11},{3,13... | collective-permute-start | bytes 294920 | tf_op jit(solution)/shard_map/ppermute | solution.py:355
  79.8 1.9 %collective-permute-start.15 = (bf16[96,512]{1,0:T(8,128)(2,1)S(1)}, bf16[96,512]{1,0:T(8,128)(2,1)S(1)}, u32[]{:S(2)}, u32[]{:S(2)}) collective-permute-start(bf16[96,512]{1,0:T(8,128)(2,1)S(1)} %get-tuple-element.80), channel_id=1, source_target_pairs={{0,12},{2,14},{4,0},{6,2},{8,4},{10,6},{12,8},{14,10},{1,13},{3,15... | collective-permute-start | bytes 294920 | tf_op jit(solution)/shard_map/ppermute | solution.py:355
  83.2 6.8 %collective-permute-done.13 = bf16[96,512]{1,0:T(8,128)(2,1)S(1)} collective-permute-done((bf16[96,512]{1,0:T(8,128)(2,1)S(1)}, bf16[96,512]{1,0:T(8,128)(2,1)S(1)}, u32[]{:S(2)}, u32[]{:S(2)}) %collective-permute-start.13) | collective-permute-done | bytes 98336 | tf_op jit(solution)/shard_map/ppermute | solution.py:355
  90.1 2.4 %collective-permute-done.15 = bf16[96,512]{1,0:T(8,128)(2,1)S(1)} collective-permute-done((bf16[96,512]{1,0:T(8,128)(2,1)S(1)}, bf16[96,512]{1,0:T(8,128)(2,1)S(1)}, u32[]{:S(2)}, u32[]{:S(2)}) %collective-permute-start.15) | collective-permute-done | bytes 98336 | tf_op jit(solution)/shard_map/ppermute | solution.py:355
  93.9 2.7 %all-to-all-done.1.parts = f32[8,32,1536]{2,1,0:T(8,128)S(1)} async-done(((f32[8,32,1536]{2,1,0:T(8,128)}), f32[8,32,1536]{2,1,0:T(8,128)S(1)}, u32[]{:S(2)}, u32[]{:S(2)}) %all-to-all-start.1) | async-done | bytes 1572896 | tf_op jit(solution)/shard_map/all_to_all | solution.py:377
  96.8 3.4 %collective-permute-done.20.other = f32[32,512]{1,0:T(8,128)S(1)} collective-permute-done((f32[32,512]{1,0:T(8,128)S(1)}, f32[32,512]{1,0:T(8,128)S(1)}, u32[]{:S(2)}, u32[]{:S(2)}) %collective-permute-start.20) | collective-permute-done | bytes 65568 | tf_op jit(solution)/shard_map/ppermute | solution.py:346
  101.4 4.3 %all-to-all-start.2 = ((bf16[8,2,32,1024]{3,2,1,0:T(8,128)(2,1)}), bf16[8,2,32,1024]{3,2,1,0:T(8,128)(2,1)S(1)}, u32[]{:S(2)}, u32[]{:S(2)}) async-start(bf16[8,2,32,1024]{3,2,1,0:T(8,128)(2,1)} %shard_map.62), calls=%async_computation.2 | async-start | bytes 2097152 | tf_op jit(solution)/shard_map/all_to_all | solution.py:383
  105.7 3.3 %collective-permute-start.18 = (bf16[8,96,512]{2,1,0:T(8,128)(2,1)S(1)}, bf16[8,96,512]{2,1,0:T(8,128)(2,1)S(1)}, u32[]{:S(2)}, u32[]{:S(2)}) collective-permute-start(bf16[8,96,512]{2,1,0:T(8,128)(2,1)S(1)} %bitcast_dynamic-update-slice_fusion.refs_0_), channel_id=1, source_target_pairs={{0,16},{16,0},{1,17},{17,1},{2,18},{18,2},{3,19},{19,3},{4,20},{20... | collective-permute-start | bytes 2359304 | tf_op jit(solution)/shard_map/ppermute | solution.py:346
  109.0 2.1 %collective-permute-done.17.refs_1_ = bf16[8,96,512]{2,1,0:T(8,128)(2,1)S(1)} collective-permute-done((bf16[8,96,512]{2,1,0:T(8,128)(2,1)S(1)}, bf16[8,96,512]{2,1,0:T(8,128)(2,1)S(1)}, u32[]{:S(2)}, u32[]{:S(2)}) %collective-permute-start.17) | collective-permute-done | bytes 786464 | tf_op jit(solution)/shard_map/ppermute | solution.py:346
  111.0 4.6 %collective-permute-start.19 = (bf16[8,96,512]{2,1,0:T(8,128)(2,1)S(1)}, bf16[8,96,512]{2,1,0:T(8,128)(2,1)S(1)}, u32[]{:S(2)}, u32[]{:S(2)}) collective-permute-start(bf16[8,96,512]{2,1,0:T(8,128)(2,1)S(1)} %collective-permute-done.17.refs_1_), channel_id=1, source_target_pairs={{0,16},{16,0},{1,17},{17,1},{2,18},{18,2},{3,19},{19,3},{4,20},{20... | collective-permute-start | bytes 2359304 | tf_op jit(solution)/shard_map/ppermute | solution.py:346
  115.7 1.9 %collective-permute-done.19.refs_3_ = bf16[8,96,512]{2,1,0:T(8,128)(2,1)S(1)} collective-permute-done((bf16[8,96,512]{2,1,0:T(8,128)(2,1)S(1)}, bf16[8,96,512]{2,1,0:T(8,128)(2,1)S(1)}, u32[]{:S(2)}, u32[]{:S(2)}) %collective-permute-start.19) | collective-permute-done | bytes 786464 | tf_op jit(solution)/shard_map/ppermute | solution.py:346
  117.6 5.4 %shard_map.60 = (bf16[1024,1024]{1,0:T(8,128)(2,1)S(1)}, bf16[512,1024]{1,0:T(8,128)(2,1)}) custom-call(s32[3]{0:T(128)S(1)} %pad_add_fusion.me_ref, bf16[8,96,512]{2,1,0:T(8,128)(2,1)} %copy-done.3, bf16[8,96,512]{2,1,0:T(8,128)(2,1)} %copy-done.4, bf16[8,96,512]{2,1,0:T(8,128)(2,1)S(1)} %collective-permute-done.18.refs_2_, ...), custom_call_target="tpu_custom_call" | custom-call | bytes 6291456 | tf_op jit(solution)/shard_map/pallas_call | solution.py:282
  123.0 2.6 %all-to-all-done.2.p_ref = bf16[8,2,32,1024]{3,2,1,0:T(8,128)(2,1)S(1)} async-done(((bf16[8,2,32,1024]{3,2,1,0:T(8,128)(2,1)}), bf16[8,2,32,1024]{3,2,1,0:T(8,128)(2,1)S(1)}, u32[]{:S(2)}, u32[]{:S(2)}) %all-to-all-start.2) | async-done | bytes 1048608 | tf_op jit(solution)/shard_map/all_to_all | solution.py:383
  125.6 2.5 %shard_map.63 = bf16[16,96,256]{2,1,0:T(8,128)(2,1)S(1)} custom-call(s32[3]{0:T(128)S(1)} %pad_add_fusion.me_ref, bf16[1024,1024]{1,0:T(8,128)(2,1)S(1)} %get-tuple-element.82.vf, bf16[512,1024]{1,0:T(8,128)(2,1)} %get-tuple-element.83.vh_hbm, bf16[8,2,32,1024]{3,2,1,0:T(8,128)(2,1)S(1)} %all-to-all-done.2.p_ref), custom_call_target="tpu_custom_call" | custom-call | tf_op jit(solution)/shard_map/pallas_call | solution.py:314
  128.1 31.5 %all_to_all.20.m_ref = bf16[16,96,256]{2,1,0:T(8,128)(2,1)S(1)} all-to-all(bf16[16,96,256]{2,1,0:T(8,128)(2,1)S(1)} %shard_map.63), channel_id=1, replica_groups=mesh['y'=4,'xh'=2,'c'=2,'z'=8,'xl'=2] {'z','c'}, dimensions={0} | all-to-all | bytes 1572864 | tf_op jit(solution)/shard_map/all_to_all | solution.py:385
  159.7 1.7 %shard_map.64 = bf16[8,64,768]{2,1,0:T(8,128)(2,1)} custom-call(bf16[16,96,256]{2,1,0:T(8,128)(2,1)S(1)} %all_to_all.20.m_ref, bf16[768,768]{1,0:T(8,128)(2,1)S(1)} %copy-done.1), custom_call_target="tpu_custom_call" | custom-call | tf_op jit(solution)/shard_map/pallas_call | solution.py:335
  (56 shorter events, 11.0 us)
Async XLA Ops:
  0.0 13.5 %copy-start = (bf16[768,768]{1,0:T(8,128)(2,1)S(1)}, bf16[768,768]{1,0:T(8,128)(2,1)}, u32[]{:S(2)}) copy-start(bf16[768,768]{1,0:T(8,128)(2,1)} %w_ref.4) | copy-start | bytes 3538948
  3.1 12.3 %collective-permute-start.1 = (bf16[96,512]{1,0:T(8,128)(2,1)S(1)}, bf16[96,512]{1,0:T(8,128)(2,1)S(1)}, u32[]{:S(2)}, u32[]{:S(2)}) collective-permute-start(bf16[96,512]{1,0:T(8,128)(2,1)S(1)} %get-tuple-element.55), channel_id=1, source_target_pairs={{0,2},{2,4},{4,6},{6,8},{8,10},{10,12},{12,14},{14,0},{1,3},{3,5},... | collective-permute-start | bytes 294920 | tf_op jit(solution)/shard_map/ppermute | solution.py:355
  5.6 13.4 %collective-permute-start.2 = (bf16[96,512]{1,0:T(8,128)(2,1)S(1)}, bf16[96,512]{1,0:T(8,128)(2,1)S(1)}, u32[]{:S(2)}, u32[]{:S(2)}) collective-permute-start(bf16[96,512]{1,0:T(8,128)(2,1)S(1)} %get-tuple-element.56), channel_id=1, source_target_pairs={{0,14},{2,0},{4,2},{6,4},{8,6},{10,8},{12,10},{14,12},{1,15},{3,1}... | collective-permute-start | bytes 294920 | tf_op jit(solution)/shard_map/ppermute | solution.py:355
  9.6 13.8 %collective-permute-start.3 = (bf16[96,512]{1,0:T(8,128)(2,1)S(1)}, bf16[96,512]{1,0:T(8,128)(2,1)S(1)}, u32[]{:S(2)}, u32[]{:S(2)}) collective-permute-start(bf16[96,512]{1,0:T(8,128)(2,1)S(1)} %get-tuple-element.57), channel_id=1, source_target_pairs={{0,4},{2,6},{4,8},{6,10},{8,12},{10,14},{12,0},{14,2},{1,5},{3,7},... | collective-permute-start | bytes 294920 | tf_op jit(solution)/shard_map/ppermute | solution.py:355
  9.6 13.8 %collective-permute-start.4 = (bf16[96,512]{1,0:T(8,128)(2,1)S(1)}, bf16[96,512]{1,0:T(8,128)(2,1)S(1)}, u32[]{:S(2)}, u32[]{:S(2)}) collective-permute-start(bf16[96,512]{1,0:T(8,128)(2,1)S(1)} %get-tuple-element.58), channel_id=1, source_target_pairs={{0,12},{2,14},{4,0},{6,2},{8,4},{10,6},{12,8},{14,10},{1,13},{3,15... | collective-permute-start | bytes 294920 | tf_op jit(solution)/shard_map/ppermute | solution.py:355
  13.2 13.8 %collective-permute-start.5 = (bf16[96,512]{1,0:T(8,128)(2,1)S(1)}, bf16[96,512]{1,0:T(8,128)(2,1)}, u32[]{:S(2)}, u32[]{:S(2)}) collective-permute-start(bf16[96,512]{1,0:T(8,128)(2,1)S(1)} %get-tuple-element.59), channel_id=1, source_target_pairs={{0,6},{2,8},{4,10},{6,12},{8,14},{10,0},{12,2},{14,4},{1,7},{3,9},... | collective-permute-start | bytes 294920 | tf_op jit(solution)/shard_map/ppermute | solution.py:355
  15.3 18.6 %collective-permute-start.6 = (bf16[96,512]{1,0:T(8,128)(2,1)S(1)}, bf16[96,512]{1,0:T(8,128)(2,1)S(1)}, u32[]{:S(2)}, u32[]{:S(2)}) collective-permute-start(bf16[96,512]{1,0:T(8,128)(2,1)S(1)} %get-tuple-element.63), channel_id=1, source_target_pairs={{0,8},{2,10},{4,12},{6,14},{8,0},{10,2},{12,4},{14,6},{1,9},{3,11}... | collective-permute-start | bytes 294920 | tf_op jit(solution)/shard_map/ppermute | solution.py:355
  19.0 15.1 %collective-permute-start.7 = (bf16[96,512]{1,0:T(8,128)(2,1)S(1)}, bf16[96,512]{1,0:T(8,128)(2,1)S(1)}, u32[]{:S(2)}, u32[]{:S(2)}) collective-permute-start(bf16[96,512]{1,0:T(8,128)(2,1)S(1)} %get-tuple-element.64), channel_id=1, source_target_pairs={{0,10},{2,12},{4,14},{6,0},{8,2},{10,4},{12,6},{14,8},{1,11},{3,13... | collective-permute-start | bytes 294920 | tf_op jit(solution)/shard_map/ppermute | solution.py:355
  27.0 34.0 %all-to-all-start = ((bf16[16,128,256]{2,1,0:T(8,128)(2,1)}), bf16[16,128,256]{2,1,0:T(8,128)(2,1)}, u32[]{:S(2)}, u32[]{:S(2)}) async-start(bf16[16,128,256]{2,1,0:T(8,128)(2,1)} %shard_map.57), calls=%async_computation | async-start | bytes 2097152 | tf_op jit(solution)/shard_map/all_to_all | solution.py:368
  33.0 2.6 %copy-start.2 = (bf16[768,768]{1,0:T(8,128)(2,1)S(1)}, bf16[768,768]{1,0:T(8,128)(2,1)}, u32[]{:S(2)}) copy-start(bf16[768,768]{1,0:T(8,128)(2,1)} %w_ref.3) | copy-start | bytes 3538948
  34.1 2.9 %collective-permute-start.9 = (bf16[8,96,512]{2,1,0:T(8,128)(2,1)S(1)}, bf16[8,96,512]{2,1,0:T(8,128)(2,1)S(1)}, u32[]{:S(2)}, u32[]{:S(2)}) collective-permute-start(bf16[8,96,512]{2,1,0:T(8,128)(2,1)S(1)} %bitcast_dynamic-update-slice_fusion.8.own), channel_id=1, source_target_pairs={{0,16},{16,0},{1,17},{17,1},{2,18},{18,2},{3,19},{19,3},{4,20},{20... | collective-permute-start | bytes 2359304 | tf_op jit(solution)/shard_map/ppermute | solution.py:346
  34.3 18.9 %collective-permute-start.8 = (bf16[8,96,512]{2,1,0:T(8,128)(2,1)S(1)}, bf16[8,96,512]{2,1,0:T(8,128)(2,1)S(1)}, u32[]{:S(2)}, u32[]{:S(2)}) collective-permute-start(bf16[8,96,512]{2,1,0:T(8,128)(2,1)S(1)} %bitcast_dynamic-update-slice_fusion.8.own), channel_id=1, source_target_pairs={{0,1},{1,0},{2,3},{3,2},{4,5},{5,4},{6,7},{7,6},{8,9},{9,8},{10,11... | collective-permute-start | bytes 2359304 | tf_op jit(solution)/shard_map/ppermute | solution.py:346
  53.2 6.6 %copy-start.5 = (bf16[8,96,512]{2,1,0:T(8,128)(2,1)}, bf16[8,96,512]{2,1,0:T(8,128)(2,1)S(1)}, u32[]{:S(2)}) copy-start(bf16[8,96,512]{2,1,0:T(8,128)(2,1)S(1)} %collective-permute-done.8.own_hbm) | copy-start | bytes 2359300
  53.2 6.6 %collective-permute-start.10 = (bf16[8,96,512]{2,1,0:T(8,128)(2,1)S(1)}, bf16[8,96,512]{2,1,0:T(8,128)(2,1)S(1)}, u32[]{:S(2)}, u32[]{:S(2)}) collective-permute-start(bf16[8,96,512]{2,1,0:T(8,128)(2,1)S(1)} %collective-permute-done.8.own_hbm), channel_id=1, source_target_pairs={{0,16},{16,0},{1,17},{17,1},{2,18},{18,2},{3,19},{19,3},{4,20},{20... | collective-permute-start | bytes 2359304 | tf_op jit(solution)/shard_map/ppermute | solution.py:346
  54.3 12.7 %collective-permute-start = (bf16[96,512]{1,0:T(8,128)(2,1)S(1)}, bf16[96,512]{1,0:T(8,128)(2,1)S(1)}, u32[]{:S(2)}, u32[]{:S(2)}) collective-permute-start(bf16[96,512]{1,0:T(8,128)(2,1)S(1)} %get-tuple-element.51), channel_id=1, source_target_pairs={{0,8},{2,10},{4,12},{6,14},{8,0},{10,2},{12,4},{14,6},{1,9},{3,11}... | collective-permute-start | bytes 294920 | tf_op jit(solution)/shard_map/ppermute | solution.py:355
  66.9 29.7 %all-to-all-start.1 = ((f32[8,32,1536]{2,1,0:T(8,128)}), f32[8,32,1536]{2,1,0:T(8,128)S(1)}, u32[]{:S(2)}, u32[]{:S(2)}) async-start(f32[8,32,1536]{2,1,0:T(8,128)} %shard_map.59), calls=%async_computation.1 | async-start | bytes 3145728 | tf_op jit(solution)/shard_map/all_to_all | solution.py:377
  73.6 8.1 %collective-permute-start.11 = (bf16[96,512]{1,0:T(8,128)(2,1)S(1)}, bf16[96,512]{1,0:T(8,128)(2,1)S(1)}, u32[]{:S(2)}, u32[]{:S(2)}) collective-permute-start(bf16[96,512]{1,0:T(8,128)(2,1)S(1)} %get-tuple-element.75), channel_id=1, source_target_pairs={{0,2},{2,4},{4,6},{6,8},{8,10},{10,12},{12,14},{14,0},{1,3},{3,5},... | collective-permute-start | bytes 294920 | tf_op jit(solution)/shard_map/ppermute | solution.py:355
  73.6 9.6 %collective-permute-start.12 = (bf16[96,512]{1,0:T(8,128)(2,1)S(1)}, bf16[96,512]{1,0:T(8,128)(2,1)S(1)}, u32[]{:S(2)}, u32[]{:S(2)}) collective-permute-start(bf16[96,512]{1,0:T(8,128)(2,1)S(1)} %get-tuple-element.76), channel_id=1, source_target_pairs={{0,4},{2,6},{4,8},{6,10},{8,12},{10,14},{12,0},{14,2},{1,5},{3,7},... | collective-permute-start | bytes 294920 | tf_op jit(solution)/shard_map/ppermute | solution.py:355
  75.3 14.7 %collective-permute-start.13 = (bf16[96,512]{1,0:T(8,128)(2,1)S(1)}, bf16[96,512]{1,0:T(8,128)(2,1)S(1)}, u32[]{:S(2)}, u32[]{:S(2)}) collective-permute-start(bf16[96,512]{1,0:T(8,128)(2,1)S(1)} %get-tuple-element.77), channel_id=1, source_target_pairs={{0,6},{2,8},{4,10},{6,12},{8,14},{10,0},{12,2},{14,4},{1,7},{3,9},... | collective-permute-start | bytes 294920 | tf_op jit(solution)/shard_map/ppermute | solution.py:355
  77.5 12.6 %collective-permute-start.14 = (bf16[96,512]{1,0:T(8,128)(2,1)S(1)}, bf16[96,512]{1,0:T(8,128)(2,1)S(1)}, u32[]{:S(2)}, u32[]{:S(2)}) collective-permute-start(bf16[96,512]{1,0:T(8,128)(2,1)S(1)} %get-tuple-element.79), channel_id=1, source_target_pairs={{0,10},{2,12},{4,14},{6,0},{8,2},{10,4},{12,6},{14,8},{1,11},{3,13... | collective-permute-start | bytes 294920 | tf_op jit(solution)/shard_map/ppermute | solution.py:355
  79.8 12.6 %collective-permute-start.15 = (bf16[96,512]{1,0:T(8,128)(2,1)S(1)}, bf16[96,512]{1,0:T(8,128)(2,1)S(1)}, u32[]{:S(2)}, u32[]{:S(2)}) collective-permute-start(bf16[96,512]{1,0:T(8,128)(2,1)S(1)} %get-tuple-element.80), channel_id=1, source_target_pairs={{0,12},{2,14},{4,0},{6,2},{8,4},{10,6},{12,8},{14,10},{1,13},{3,15... | collective-permute-start | bytes 294920 | tf_op jit(solution)/shard_map/ppermute | solution.py:355
  81.8 11.7 %collective-permute-start.16 = (bf16[96,512]{1,0:T(8,128)(2,1)S(1)}, bf16[96,512]{1,0:T(8,128)(2,1)S(1)}, u32[]{:S(2)}, u32[]{:S(2)}) collective-permute-start(bf16[96,512]{1,0:T(8,128)(2,1)S(1)} %get-tuple-element.81), channel_id=1, source_target_pairs={{0,14},{2,0},{4,2},{6,4},{8,6},{10,8},{12,10},{14,12},{1,15},{3,1}... | collective-permute-start | bytes 294920 | tf_op jit(solution)/shard_map/ppermute | solution.py:355
  93.5 12.2 %copy-start.3 = (bf16[8,96,512]{2,1,0:T(8,128)(2,1)}, bf16[8,96,512]{2,1,0:T(8,128)(2,1)S(1)}, u32[]{:S(2)}) copy-start(bf16[8,96,512]{2,1,0:T(8,128)(2,1)S(1)} %bitcast_dynamic-update-slice_fusion.refs_0_) | copy-start | bytes 2359300
  93.5 17.5 %collective-permute-start.17 = (bf16[8,96,512]{2,1,0:T(8,128)(2,1)S(1)}, bf16[8,96,512]{2,1,0:T(8,128)(2,1)S(1)}, u32[]{:S(2)}, u32[]{:S(2)}) collective-permute-start(bf16[8,96,512]{2,1,0:T(8,128)(2,1)S(1)} %bitcast_dynamic-update-slice_fusion.refs_0_), channel_id=1, source_target_pairs={{0,1},{1,0},{2,3},{3,2},{4,5},{5,4},{6,7},{7,6},{8,9},{9,8},{10,11... | collective-permute-start | bytes 2359304 | tf_op jit(solution)/shard_map/ppermute | solution.py:346
  96.7 3.5 %collective-permute-start.20 = (f32[32,512]{1,0:T(8,128)S(1)}, f32[32,512]{1,0:T(8,128)S(1)}, u32[]{:S(2)}, u32[]{:S(2)}) collective-permute-start(f32[32,512]{1,0:T(8,128)S(1)} %get-tuple-element.86.half), channel_id=1, source_target_pairs={{0,2},{2,0},{4,6},{6,4},{8,10},{10,8},{12,14},{14,12},{1,3},{3,1},... | collective-permute-start | bytes 196616 | tf_op jit(solution)/shard_map/ppermute | solution.py:346
  101.4 24.2 %all-to-all-start.2 = ((bf16[8,2,32,1024]{3,2,1,0:T(8,128)(2,1)}), bf16[8,2,32,1024]{3,2,1,0:T(8,128)(2,1)S(1)}, u32[]{:S(2)}, u32[]{:S(2)}) async-start(bf16[8,2,32,1024]{3,2,1,0:T(8,128)(2,1)} %shard_map.62), calls=%async_computation.2 | async-start | bytes 2097152 | tf_op jit(solution)/shard_map/all_to_all | solution.py:383
  105.7 10.0 %collective-permute-start.18 = (bf16[8,96,512]{2,1,0:T(8,128)(2,1)S(1)}, bf16[8,96,512]{2,1,0:T(8,128)(2,1)S(1)}, u32[]{:S(2)}, u32[]{:S(2)}) collective-permute-start(bf16[8,96,512]{2,1,0:T(8,128)(2,1)S(1)} %bitcast_dynamic-update-slice_fusion.refs_0_), channel_id=1, source_target_pairs={{0,16},{16,0},{1,17},{17,1},{2,18},{18,2},{3,19},{19,3},{4,20},{20... | collective-permute-start | bytes 2359304 | tf_op jit(solution)/shard_map/ppermute | solution.py:346
  111.0 4.6 %copy-start.4 = (bf16[8,96,512]{2,1,0:T(8,128)(2,1)}, bf16[8,96,512]{2,1,0:T(8,128)(2,1)S(1)}, u32[]{:S(2)}) copy-start(bf16[8,96,512]{2,1,0:T(8,128)(2,1)S(1)} %collective-permute-done.17.refs_1_) | copy-start | bytes 2359300
  111.0 6.5 %collective-permute-start.19 = (bf16[8,96,512]{2,1,0:T(8,128)(2,1)S(1)}, bf16[8,96,512]{2,1,0:T(8,128)(2,1)S(1)}, u32[]{:S(2)}, u32[]{:S(2)}) collective-permute-start(bf16[8,96,512]{2,1,0:T(8,128)(2,1)S(1)} %collective-permute-done.17.refs_1_), channel_id=1, source_target_pairs={{0,16},{16,0},{1,17},{17,1},{2,18},{18,2},{3,19},{19,3},{4,20},{20... | collective-permute-start | bytes 2359304 | tf_op jit(solution)/shard_map/ppermute | solution.py:346
  128.1 31.6 %copy-start.1 = (bf16[768,768]{1,0:T(8,128)(2,1)S(1)}, bf16[768,768]{1,0:T(8,128)(2,1)}, u32[]{:S(2)}) copy-start(bf16[768,768]{1,0:T(8,128)(2,1)} %w_ref.5) | copy-start | bytes 3538948

commit v18 on v14

--- a/solution.py
+++ b/solution.py
@@ -370,12 +370,12 @@
     k = jnp.stack(k)
     near, shared = keys_laid(me, k, flip(k, "c", 2, 1))
     k_far, v[4], shared = lax.optimization_barrier((flip(k, "xl", 2, 1), v[4], shared))
-    for s in (2, 6):
+    for s in (2, 6, 1):
         v[s] = shift(v[s], s)
     scores = score(me, q, (near, shared), k_far, flip(k_far, "c", 2, 1))
     *v, scores = lax.optimization_barrier((*v, scores))
     parts = lax.all_to_all(scores, ("y", "xh"), 0, 0, tiled=True)
-    for s in (4, 3, 5, 1, 7):
+    for s in (4, 3, 5, 7):
         v[s] = shift(v[s], s)
     full, half = total(parts)
     rows = ROWS * 2 * PEERS

time: 161 us -> 160 us (level)
  waiting for transfers between devices: 42.2 us -> 46.3 us
  blocking collectives: 32.3 us -> 29.1 us
  starting transfers between devices: 59.8 us -> 56.7 us
    ppermute x7, starting transfers between devices: 12.9 us -> 9.1 us  [flip(): return lax.ppermute(x, axes, [(i, i ^ s) for i in range(n)])]
    all_to_all x1, blocking collectives: 32.3 us -> 29.1 us  [local(): mixed = lax.all_to_all(mix(me, laid, probs), ('z', 'c'), 0, 0, tiled=True)]
    ppermute x7, waiting for transfers between devices: 19.8 us -> 22.8 us  [flip(): return lax.ppermute(x, axes, [(i, i ^ s) for i in range(n)])]
    all_to_all x1, waiting for transfers between devices: 1.78 us -> 4.46 us  [local(): probs = lax.all_to_all(probs, ('y', 'xh'), 0, 0, tiled=True)]
    all_to_all x1, waiting for transfers between devices: 3.01 us -> 1.09 us  [local(): q = lax.all_to_all(q, ('z', 'c'), 0, 0, tiled=True)]
  transfers between devices with their start and end apart: 24 -> 24, of which waited for: 13 -> 10; matrix products, arithmetic and copies ran while one was open for 1% -> 1% of each run, Pallas kernels for 11% -> 11%
where the time goes in v18:
time: 160 us; the launch traced here: 159 us
  starting transfers between devices  56.7 us (35%)
  waiting for transfers between devices  46.3 us (29%)
  blocking collectives  29.1 us (18%)
  Pallas kernels  24.8 us (16%)
  local copies, waits for them, and re-layouts  2.04 us (1%)
    ppermute x14, starting transfers between devices, shift(): return lax.ppermute(x, 'z', [(i, (i + s) % Z) for i in range(Z)])  31.3 us
    all_to_all x1, blocking collectives, local(): mixed = lax.all_to_all(mix(me, laid, probs), ('z', 'c'), 0, 0, tiled=True)  29.1 us
    ppermute x7, waiting for transfers between devices, flip(): return lax.ppermute(x, axes, [(i, i ^ s) for i in range(n)])  22.8 us
    ppermute x14, waiting for transfers between devices, shift(): return lax.ppermute(x, 'z', [(i, (i + s) % Z) for i in range(Z)])  14.3 us
    ppermute x7, starting transfers between devices, flip(): return lax.ppermute(x, axes, [(i, i ^ s) for i in range(n)])  9.1 us
    all_to_all x1, starting transfers between devices, local(): parts = lax.all_to_all(scores, ('y', 'xh'), 0, 0, tiled=True)  6.65 us
    all_to_all x1, starting transfers between devices, local(): q = lax.all_to_all(q, ('z', 'c'), 0, 0, tiled=True)  5.95 us
    pallas_call x1, Pallas kernels, score(): pl.pallas_call(score_kernel, out_shape=jax.ShapeDtypeStruct((PEERS, SUB,...  5.94 us
  transfers between devices with their start and end apart: 24, of which 10 were waited for; matrix products, arithmetic and copies ran while one was open for 1% of the time, Pallas kernels for 11%

profile of v18, /device:TPU:1, one launch (start us, length us, event | category | flops | bytes accessed | tf_op | source)
XLA Modules:
  0.0 159.3 jit_solution(12071427883807790523)
XLA Ops:
  0.1 3.0 %shard_map.55 = (bf16[2,8,32,768]{3,2,1,0:T(8,128)(2,1)S(1)}, bf16[96,512]{1,0:T(8,128)(2,1)S(1)}, bf16[96,512]{1,0:T(8,128)(2,1)S(1)}, bf16[96,512]{1,0:T(8,128...) custom-call(s32[3]{0:T(128)S(1)} %pad_add_fusion.me_ref, ...), custom_call_target="tpu_custom_call" | custom-call | tf_op jit(solution)/shard_map/pallas_call | solution.py:97
  3.1 2.5 %collective-permute-start.2 = (bf16[96,512]{1,0:T(8,128)(2,1)S(1)}, bf16[96,512]{1,0:T(8,128)(2,1)S(1)}, u32[]{:S(2)}, u32[]{:S(2)}) collective-permute-start(bf16[96,512]{1,0:T(8,128)(2,1)S(1)} %get-tuple-element.52), channel_id=1, source_target_pairs={{0,2},{2,4},{4,6},{6,8},{8,10},{10,12},{12,14},{14,0},{1,3},{3,5},... | collective-permute-start | bytes 294920 | tf_op jit(solution)/shard_map/ppermute | solution.py:355
  5.6 4.0 %collective-permute-start.3 = (bf16[96,512]{1,0:T(8,128)(2,1)S(1)}, bf16[96,512]{1,0:T(8,128)(2,1)S(1)}, u32[]{:S(2)}, u32[]{:S(2)}) collective-permute-start(bf16[96,512]{1,0:T(8,128)(2,1)S(1)} %get-tuple-element.53), channel_id=1, source_target_pairs={{0,14},{2,0},{4,2},{6,4},{8,6},{10,8},{12,10},{14,12},{1,15},{3,1}... | collective-permute-start | bytes 294920 | tf_op jit(solution)/shard_map/ppermute | solution.py:355
  9.6 3.6 %collective-permute-start.5 = (bf16[96,512]{1,0:T(8,128)(2,1)S(1)}, bf16[96,512]{1,0:T(8,128)(2,1)S(1)}, u32[]{:S(2)}, u32[]{:S(2)}) collective-permute-start(bf16[96,512]{1,0:T(8,128)(2,1)S(1)} %get-tuple-element.55), channel_id=1, source_target_pairs={{0,12},{2,14},{4,0},{6,2},{8,4},{10,6},{12,8},{14,10},{1,13},{3,15... | collective-permute-start | bytes 294920 | tf_op jit(solution)/shard_map/ppermute | solution.py:355
  13.5 1.8 %shard_map.57 = bf16[16,128,256]{2,1,0:T(8,128)(2,1)} custom-call(bf16[2,8,32,768]{3,2,1,0:T(8,128)(2,1)S(1)} %get-tuple-element.46.n_ref, bf16[768,768]{1,0:T(8,128)(2,1)S(1)} %copy-done), custom_call_target="tpu_custom_call" | custom-call | flops 603979776 | bytes 2752512 | tf_op jit(solution)/shard_map/pallas_call | solution.py:124
  15.3 3.6 %collective-permute-start.7 = (bf16[96,512]{1,0:T(8,128)(2,1)S(1)}, bf16[96,512]{1,0:T(8,128)(2,1)S(1)}, u32[]{:S(2)}, u32[]{:S(2)}) collective-permute-start(bf16[96,512]{1,0:T(8,128)(2,1)S(1)} %get-tuple-element.60), channel_id=1, source_target_pairs={{0,8},{2,10},{4,12},{6,14},{8,0},{10,2},{12,4},{14,6},{1,9},{3,11}... | collective-permute-start | bytes 294920 | tf_op jit(solution)/shard_map/ppermute | solution.py:355
  19.0 4.5 %collective-permute-start.8 = (bf16[96,512]{1,0:T(8,128)(2,1)S(1)}, bf16[96,512]{1,0:T(8,128)(2,1)S(1)}, u32[]{:S(2)}, u32[]{:S(2)}) collective-permute-start(bf16[96,512]{1,0:T(8,128)(2,1)S(1)} %get-tuple-element.61), channel_id=1, source_target_pairs={{0,10},{2,12},{4,14},{6,0},{8,2},{10,4},{12,6},{14,8},{1,11},{3,13... | collective-permute-start | bytes 294920 | tf_op jit(solution)/shard_map/ppermute | solution.py:355
  23.4 3.6 %collective-permute-done.6 = bf16[96,512]{1,0:T(8,128)(2,1)} collective-permute-done((bf16[96,512]{1,0:T(8,128)(2,1)S(1)}, bf16[96,512]{1,0:T(8,128)(2,1)}, u32[]{:S(2)}, u32[]{:S(2)}) %collective-permute-start.6) | collective-permute-done | bytes 98336 | tf_op jit(solution)/shard_map/ppermute | solution.py:355
  27.0 5.9 %all-to-all-start = ((bf16[16,128,256]{2,1,0:T(8,128)(2,1)}), bf16[16,128,256]{2,1,0:T(8,128)(2,1)}, u32[]{:S(2)}, u32[]{:S(2)}) async-start(bf16[16,128,256]{2,1,0:T(8,128)(2,1)} %shard_map.57), calls=%async_computation | async-start | bytes 2097152 | tf_op jit(solution)/shard_map/all_to_all | solution.py:368
  36.9 1.8 %shard_map.58 = (bf16[1024,512]{1,0:T(8,128)(2,1)S(1)}, bf16[1024,256]{1,0:T(8,128)(2,1)S(1)}) custom-call(s32[3]{0:T(128)S(1)} %pad_add_fusion.me_ref, bf16[8,96,512]{2,1,0:T(8,128)(2,1)S(1)} %bitcast_dynamic-update-slice_fusion.8.own, bf16[8,96,512]{2,1,0:T(8,128)(2,1)S(1)} %collective-permute-done.10.other), custom_call_target="tpu_custom_call" | custom-call | bytes 6291456 | tf_op jit(solution)/shard_map/pallas_call | solution.py:173
  38.8 14.4 %collective-permute-done.9.own_hbm = bf16[8,96,512]{2,1,0:T(8,128)(2,1)S(1)} collective-permute-done((bf16[8,96,512]{2,1,0:T(8,128)(2,1)S(1)}, bf16[8,96,512]{2,1,0:T(8,128)(2,1)S(1)}, u32[]{:S(2)}, u32[]{:S(2)}) %collective-permute-start.9) | collective-permute-done | bytes 786464 | tf_op jit(solution)/shard_map/ppermute | solution.py:346
  54.3 2.0 %collective-permute-start = (bf16[96,512]{1,0:T(8,128)(2,1)S(1)}, bf16[96,512]{1,0:T(8,128)(2,1)S(1)}, u32[]{:S(2)}, u32[]{:S(2)}) collective-permute-start(bf16[96,512]{1,0:T(8,128)(2,1)S(1)} %get-tuple-element.48), channel_id=1, source_target_pairs={{0,2},{2,4},{4,6},{6,8},{8,10},{10,12},{12,14},{14,0},{1,3},{3,5},... | collective-permute-start | bytes 294920 | tf_op jit(solution)/shard_map/ppermute | solution.py:355
  56.3 1.6 %collective-permute-start.1 = (bf16[96,512]{1,0:T(8,128)(2,1)S(1)}, bf16[96,512]{1,0:T(8,128)(2,1)S(1)}, u32[]{:S(2)}, u32[]{:S(2)}) collective-permute-start(bf16[96,512]{1,0:T(8,128)(2,1)S(1)} %get-tuple-element.49), channel_id=1, source_target_pairs={{0,4},{2,6},{4,8},{6,10},{8,12},{10,14},{12,0},{14,2},{1,5},{3,7},... | collective-permute-start | bytes 294920 | tf_op jit(solution)/shard_map/ppermute | solution.py:355
  58.0 2.0 %collective-permute-start.11 = (bf16[96,512]{1,0:T(8,128)(2,1)S(1)}, bf16[96,512]{1,0:T(8,128)(2,1)S(1)}, u32[]{:S(2)}, u32[]{:S(2)}) collective-permute-start(bf16[96,512]{1,0:T(8,128)(2,1)S(1)} %get-tuple-element.68), channel_id=1, source_target_pairs={{0,12},{2,14},{4,0},{6,2},{8,4},{10,6},{12,8},{14,10},{1,13},{3,15... | collective-permute-start | bytes 294920 | tf_op jit(solution)/shard_map/ppermute | solution.py:355
  61.0 5.9 %shard_map.59 = f32[8,32,1536]{2,1,0:T(8,128)} custom-call(s32[3]{0:T(128)S(1)} %pad_add_fusion.me_ref, bf16[16,128,256]{2,1,0:T(8,128)(2,1)} %all-to-all-done.q_hbm, bf16[1024,512]{1,0:T(8,128)(2,1)S(1)} %get-tuple-element.71.kf_hbm, bf16[1024,256]{1,0:T(8,128)(2,1)S(1)} %get-tuple-element.72.kh_hbm, bf16[8,96,512]{2,1,0:T(8,128)(2,1)} %copy-done.4, ...), custom_call_target="tpu_custom_call" | custom-call | tf_op jit(solution)/shard_map/pallas_call | solution.py:209
  67.0 6.7 %all-to-all-start.1 = ((f32[8,32,1536]{2,1,0:T(8,128)}), f32[8,32,1536]{2,1,0:T(8,128)S(1)}, u32[]{:S(2)}, u32[]{:S(2)}) async-start(f32[8,32,1536]{2,1,0:T(8,128)} %shard_map.59), calls=%async_computation.1 | async-start | bytes 3145728 | tf_op jit(solution)/shard_map/all_to_all | solution.py:377
  75.1 2.6 %collective-permute-start.14 = (bf16[96,512]{1,0:T(8,128)(2,1)S(1)}, bf16[96,512]{1,0:T(8,128)(2,1)S(1)}, u32[]{:S(2)}, u32[]{:S(2)}) collective-permute-start(bf16[96,512]{1,0:T(8,128)(2,1)S(1)} %get-tuple-element.78), channel_id=1, source_target_pairs={{0,8},{2,10},{4,12},{6,14},{8,0},{10,2},{12,4},{14,6},{1,9},{3,11}... | collective-permute-start | bytes 294920 | tf_op jit(solution)/shard_map/ppermute | solution.py:355
  77.7 3.0 %collective-permute-start.15 = (bf16[96,512]{1,0:T(8,128)(2,1)S(1)}, bf16[96,512]{1,0:T(8,128)(2,1)S(1)}, u32[]{:S(2)}, u32[]{:S(2)}) collective-permute-start(bf16[96,512]{1,0:T(8,128)(2,1)S(1)} %get-tuple-element.79), channel_id=1, source_target_pairs={{0,10},{2,12},{4,14},{6,0},{8,2},{10,4},{12,6},{14,8},{1,11},{3,13... | collective-permute-start | bytes 294920 | tf_op jit(solution)/shard_map/ppermute | solution.py:355
  81.7 5.3 %collective-permute-done.13 = bf16[96,512]{1,0:T(8,128)(2,1)S(1)} collective-permute-done((bf16[96,512]{1,0:T(8,128)(2,1)S(1)}, bf16[96,512]{1,0:T(8,128)(2,1)S(1)}, u32[]{:S(2)}, u32[]{:S(2)}) %collective-permute-start.13) | collective-permute-done | bytes 98336 | tf_op jit(solution)/shard_map/ppermute | solution.py:355
  87.1 5.4 %collective-permute-done.16 = bf16[96,512]{1,0:T(8,128)(2,1)S(1)} collective-permute-done((bf16[96,512]{1,0:T(8,128)(2,1)S(1)}, bf16[96,512]{1,0:T(8,128)(2,1)S(1)}, u32[]{:S(2)}, u32[]{:S(2)}) %collective-permute-start.16) | collective-permute-done | bytes 98336 | tf_op jit(solution)/shard_map/ppermute | solution.py:355
  92.9 3.6 %all-to-all-done.1.parts = f32[8,32,1536]{2,1,0:T(8,128)S(1)} async-done(((f32[8,32,1536]{2,1,0:T(8,128)}), f32[8,32,1536]{2,1,0:T(8,128)S(1)}, u32[]{:S(2)}, u32[]{:S(2)}) %all-to-all-start.1) | async-done | bytes 1572896 | tf_op jit(solution)/shard_map/all_to_all | solution.py:377
  96.8 3.4 %collective-permute-done.20.other = f32[32,512]{1,0:T(8,128)S(1)} collective-permute-done((f32[32,512]{1,0:T(8,128)S(1)}, f32[32,512]{1,0:T(8,128)S(1)}, u32[]{:S(2)}, u32[]{:S(2)}) %collective-permute-start.20) | collective-permute-done | bytes 65568 | tf_op jit(solution)/shard_map/ppermute | solution.py:346
  101.4 3.7 %all-to-all-start.2 = ((bf16[8,2,32,1024]{3,2,1,0:T(8,128)(2,1)}), bf16[8,2,32,1024]{3,2,1,0:T(8,128)(2,1)S(1)}, u32[]{:S(2)}, u32[]{:S(2)}) async-start(bf16[8,2,32,1024]{3,2,1,0:T(8,128)(2,1)} %shard_map.62), calls=%async_computation.2 | async-start | bytes 2097152 | tf_op jit(solution)/shard_map/all_to_all | solution.py:383
  105.0 2.5 %collective-permute-start.18 = (bf16[8,96,512]{2,1,0:T(8,128)(2,1)S(1)}, bf16[8,96,512]{2,1,0:T(8,128)(2,1)S(1)}, u32[]{:S(2)}, u32[]{:S(2)}) collective-permute-start(bf16[8,96,512]{2,1,0:T(8,128)(2,1)S(1)} %bitcast_dynamic-update-slice_fusion.refs_0_), channel_id=1, source_target_pairs={{0,16},{16,0},{1,17},{17,1},{2,18},{18,2},{3,19},{19,3},{4,20},{20... | collective-permute-start | bytes 2359304 | tf_op jit(solution)/shard_map/ppermute | solution.py:346
  107.6 3.0 %collective-permute-done.17.refs_1_ = bf16[8,96,512]{2,1,0:T(8,128)(2,1)S(1)} collective-permute-done((bf16[8,96,512]{2,1,0:T(8,128)(2,1)S(1)}, bf16[8,96,512]{2,1,0:T(8,128)(2,1)S(1)}, u32[]{:S(2)}, u32[]{:S(2)}) %collective-permute-start.17) | collective-permute-done | bytes 786464 | tf_op jit(solution)/shard_map/ppermute | solution.py:346
  110.6 3.6 %collective-permute-start.19 = (bf16[8,96,512]{2,1,0:T(8,128)(2,1)S(1)}, bf16[8,96,512]{2,1,0:T(8,128)(2,1)S(1)}, u32[]{:S(2)}, u32[]{:S(2)}) collective-permute-start(bf16[8,96,512]{2,1,0:T(8,128)(2,1)S(1)} %collective-permute-done.17.refs_1_), channel_id=1, source_target_pairs={{0,16},{16,0},{1,17},{17,1},{2,18},{18,2},{3,19},{19,3},{4,20},{20... | collective-permute-start | bytes 2359304 | tf_op jit(solution)/shard_map/ppermute | solution.py:346
  114.2 1.9 %collective-permute-done.19.refs_3_ = bf16[8,96,512]{2,1,0:T(8,128)(2,1)S(1)} collective-permute-done((bf16[8,96,512]{2,1,0:T(8,128)(2,1)S(1)}, bf16[8,96,512]{2,1,0:T(8,128)(2,1)S(1)}, u32[]{:S(2)}, u32[]{:S(2)}) %collective-permute-start.19) | collective-permute-done | bytes 786464 | tf_op jit(solution)/shard_map/ppermute | solution.py:346
  116.1 5.4 %shard_map.60 = (bf16[1024,1024]{1,0:T(8,128)(2,1)S(1)}, bf16[512,1024]{1,0:T(8,128)(2,1)}) custom-call(s32[3]{0:T(128)S(1)} %pad_add_fusion.me_ref, bf16[8,96,512]{2,1,0:T(8,128)(2,1)} %copy-done.3, bf16[8,96,512]{2,1,0:T(8,128)(2,1)} %copy-done.5, bf16[8,96,512]{2,1,0:T(8,128)(2,1)S(1)} %collective-permute-done.18.refs_2_, ...), custom_call_target="tpu_custom_call" | custom-call | bytes 6291456 | tf_op jit(solution)/shard_map/pallas_call | solution.py:282
  121.5 4.5 %all-to-all-done.2.p_ref = bf16[8,2,32,1024]{3,2,1,0:T(8,128)(2,1)S(1)} async-done(((bf16[8,2,32,1024]{3,2,1,0:T(8,128)(2,1)}), bf16[8,2,32,1024]{3,2,1,0:T(8,128)(2,1)S(1)}, u32[]{:S(2)}, u32[]{:S(2)}) %all-to-all-start.2) | async-done | bytes 1048608 | tf_op jit(solution)/shard_map/all_to_all | solution.py:383
  126.0 2.5 %shard_map.63 = bf16[16,96,256]{2,1,0:T(8,128)(2,1)S(1)} custom-call(s32[3]{0:T(128)S(1)} %pad_add_fusion.me_ref, bf16[1024,1024]{1,0:T(8,128)(2,1)S(1)} %get-tuple-element.82.vf, bf16[512,1024]{1,0:T(8,128)(2,1)} %get-tuple-element.83.vh_hbm, bf16[8,2,32,1024]{3,2,1,0:T(8,128)(2,1)S(1)} %all-to-all-done.2.p_ref), custom_call_target="tpu_custom_call" | custom-call | tf_op jit(solution)/shard_map/pallas_call | solution.py:314
  128.5 29.1 %all_to_all.20.m_ref = bf16[16,96,256]{2,1,0:T(8,128)(2,1)S(1)} all-to-all(bf16[16,96,256]{2,1,0:T(8,128)(2,1)S(1)} %shard_map.63), channel_id=1, replica_groups=mesh['y'=4,'xh'=2,'c'=2,'z'=8,'xl'=2] {'z','c'}, dimensions={0} | all-to-all | bytes 1572864 | tf_op jit(solution)/shard_map/all_to_all | solution.py:385
  157.6 1.7 %shard_map.64 = bf16[8,64,768]{2,1,0:T(8,128)(2,1)} custom-call(bf16[16,96,256]{2,1,0:T(8,128)(2,1)S(1)} %all_to_all.20.m_ref, bf16[768,768]{1,0:T(8,128)(2,1)S(1)} %copy-done.1), custom_call_target="tpu_custom_call" | custom-call | tf_op jit(solution)/shard_map/pallas_call | solution.py:335
  (58 shorter events, 10.7 us)
Async XLA Ops:
  0.0 13.5 %copy-start = (bf16[768,768]{1,0:T(8,128)(2,1)S(1)}, bf16[768,768]{1,0:T(8,128)(2,1)}, u32[]{:S(2)}) copy-start(bf16[768,768]{1,0:T(8,128)(2,1)} %w_ref.4) | copy-start | bytes 3538948
  3.1 12.3 %collective-permute-start.2 = (bf16[96,512]{1,0:T(8,128)(2,1)S(1)}, bf16[96,512]{1,0:T(8,128)(2,1)S(1)}, u32[]{:S(2)}, u32[]{:S(2)}) collective-permute-start(bf16[96,512]{1,0:T(8,128)(2,1)S(1)} %get-tuple-element.52), channel_id=1, source_target_pairs={{0,2},{2,4},{4,6},{6,8},{8,10},{10,12},{12,14},{14,0},{1,3},{3,5},... | collective-permute-start | bytes 294920 | tf_op jit(solution)/shard_map/ppermute | solution.py:355
  5.6 13.4 %collective-permute-start.3 = (bf16[96,512]{1,0:T(8,128)(2,1)S(1)}, bf16[96,512]{1,0:T(8,128)(2,1)S(1)}, u32[]{:S(2)}, u32[]{:S(2)}) collective-permute-start(bf16[96,512]{1,0:T(8,128)(2,1)S(1)} %get-tuple-element.53), channel_id=1, source_target_pairs={{0,14},{2,0},{4,2},{6,4},{8,6},{10,8},{12,10},{14,12},{1,15},{3,1}... | collective-permute-start | bytes 294920 | tf_op jit(solution)/shard_map/ppermute | solution.py:355
  9.6 13.8 %collective-permute-start.4 = (bf16[96,512]{1,0:T(8,128)(2,1)S(1)}, bf16[96,512]{1,0:T(8,128)(2,1)S(1)}, u32[]{:S(2)}, u32[]{:S(2)}) collective-permute-start(bf16[96,512]{1,0:T(8,128)(2,1)S(1)} %get-tuple-element.54), channel_id=1, source_target_pairs={{0,4},{2,6},{4,8},{6,10},{8,12},{10,14},{12,0},{14,2},{1,5},{3,7},... | collective-permute-start | bytes 294920 | tf_op jit(solution)/shard_map/ppermute | solution.py:355
  9.6 13.8 %collective-permute-start.5 = (bf16[96,512]{1,0:T(8,128)(2,1)S(1)}, bf16[96,512]{1,0:T(8,128)(2,1)S(1)}, u32[]{:S(2)}, u32[]{:S(2)}) collective-permute-start(bf16[96,512]{1,0:T(8,128)(2,1)S(1)} %get-tuple-element.55), channel_id=1, source_target_pairs={{0,12},{2,14},{4,0},{6,2},{8,4},{10,6},{12,8},{14,10},{1,13},{3,15... | collective-permute-start | bytes 294920 | tf_op jit(solution)/shard_map/ppermute | solution.py:355
  13.2 13.8 %collective-permute-start.6 = (bf16[96,512]{1,0:T(8,128)(2,1)S(1)}, bf16[96,512]{1,0:T(8,128)(2,1)}, u32[]{:S(2)}, u32[]{:S(2)}) collective-permute-start(bf16[96,512]{1,0:T(8,128)(2,1)S(1)} %get-tuple-element.56), channel_id=1, source_target_pairs={{0,6},{2,8},{4,10},{6,12},{8,14},{10,0},{12,2},{14,4},{1,7},{3,9},... | collective-permute-start | bytes 294920 | tf_op jit(solution)/shard_map/ppermute | solution.py:355
  15.3 18.7 %collective-permute-start.7 = (bf16[96,512]{1,0:T(8,128)(2,1)S(1)}, bf16[96,512]{1,0:T(8,128)(2,1)S(1)}, u32[]{:S(2)}, u32[]{:S(2)}) collective-permute-start(bf16[96,512]{1,0:T(8,128)(2,1)S(1)} %get-tuple-element.60), channel_id=1, source_target_pairs={{0,8},{2,10},{4,12},{6,14},{8,0},{10,2},{12,4},{14,6},{1,9},{3,11}... | collective-permute-start | bytes 294920 | tf_op jit(solution)/shard_map/ppermute | solution.py:355
  19.0 15.1 %collective-permute-start.8 = (bf16[96,512]{1,0:T(8,128)(2,1)S(1)}, bf16[96,512]{1,0:T(8,128)(2,1)S(1)}, u32[]{:S(2)}, u32[]{:S(2)}) collective-permute-start(bf16[96,512]{1,0:T(8,128)(2,1)S(1)} %get-tuple-element.61), channel_id=1, source_target_pairs={{0,10},{2,12},{4,14},{6,0},{8,2},{10,4},{12,6},{14,8},{1,11},{3,13... | collective-permute-start | bytes 294920 | tf_op jit(solution)/shard_map/ppermute | solution.py:355
  27.0 34.0 %all-to-all-start = ((bf16[16,128,256]{2,1,0:T(8,128)(2,1)}), bf16[16,128,256]{2,1,0:T(8,128)(2,1)}, u32[]{:S(2)}, u32[]{:S(2)}) async-start(bf16[16,128,256]{2,1,0:T(8,128)(2,1)} %shard_map.57), calls=%async_computation | async-start | bytes 2097152 | tf_op jit(solution)/shard_map/all_to_all | solution.py:368
  33.0 2.6 %copy-start.2 = (bf16[768,768]{1,0:T(8,128)(2,1)S(1)}, bf16[768,768]{1,0:T(8,128)(2,1)}, u32[]{:S(2)}) copy-start(bf16[768,768]{1,0:T(8,128)(2,1)} %w_ref.3) | copy-start | bytes 3538948
  34.1 2.9 %collective-permute-start.10 = (bf16[8,96,512]{2,1,0:T(8,128)(2,1)S(1)}, bf16[8,96,512]{2,1,0:T(8,128)(2,1)S(1)}, u32[]{:S(2)}, u32[]{:S(2)}) collective-permute-start(bf16[8,96,512]{2,1,0:T(8,128)(2,1)S(1)} %bitcast_dynamic-update-slice_fusion.8.own), channel_id=1, source_target_pairs={{0,16},{16,0},{1,17},{17,1},{2,18},{18,2},{3,19},{19,3},{4,20},{20... | collective-permute-start | bytes 2359304 | tf_op jit(solution)/shard_map/ppermute | solution.py:346
  34.3 18.9 %collective-permute-start.9 = (bf16[8,96,512]{2,1,0:T(8,128)(2,1)S(1)}, bf16[8,96,512]{2,1,0:T(8,128)(2,1)S(1)}, u32[]{:S(2)}, u32[]{:S(2)}) collective-permute-start(bf16[8,96,512]{2,1,0:T(8,128)(2,1)S(1)} %bitcast_dynamic-update-slice_fusion.8.own), channel_id=1, source_target_pairs={{0,1},{1,0},{2,3},{3,2},{4,5},{5,4},{6,7},{7,6},{8,9},{9,8},{10,11... | collective-permute-start | bytes 2359304 | tf_op jit(solution)/shard_map/ppermute | solution.py:346
  53.2 6.7 %copy-start.4 = (bf16[8,96,512]{2,1,0:T(8,128)(2,1)}, bf16[8,96,512]{2,1,0:T(8,128)(2,1)S(1)}, u32[]{:S(2)}) copy-start(bf16[8,96,512]{2,1,0:T(8,128)(2,1)S(1)} %collective-permute-done.9.own_hbm) | copy-start | bytes 2359300
  53.2 6.7 %collective-permute-start.12 = (bf16[8,96,512]{2,1,0:T(8,128)(2,1)S(1)}, bf16[8,96,512]{2,1,0:T(8,128)(2,1)S(1)}, u32[]{:S(2)}, u32[]{:S(2)}) collective-permute-start(bf16[8,96,512]{2,1,0:T(8,128)(2,1)S(1)} %collective-permute-done.9.own_hbm), channel_id=1, source_target_pairs={{0,16},{16,0},{1,17},{17,1},{2,18},{18,2},{3,19},{19,3},{4,20},{20... | collective-permute-start | bytes 2359304 | tf_op jit(solution)/shard_map/ppermute | solution.py:346
  54.3 12.7 %collective-permute-start = (bf16[96,512]{1,0:T(8,128)(2,1)S(1)}, bf16[96,512]{1,0:T(8,128)(2,1)S(1)}, u32[]{:S(2)}, u32[]{:S(2)}) collective-permute-start(bf16[96,512]{1,0:T(8,128)(2,1)S(1)} %get-tuple-element.48), channel_id=1, source_target_pairs={{0,2},{2,4},{4,6},{6,8},{8,10},{10,12},{12,14},{14,0},{1,3},{3,5},... | collective-permute-start | bytes 294920 | tf_op jit(solution)/shard_map/ppermute | solution.py:355
  56.3 10.6 %collective-permute-start.1 = (bf16[96,512]{1,0:T(8,128)(2,1)S(1)}, bf16[96,512]{1,0:T(8,128)(2,1)S(1)}, u32[]{:S(2)}, u32[]{:S(2)}) collective-permute-start(bf16[96,512]{1,0:T(8,128)(2,1)S(1)} %get-tuple-element.49), channel_id=1, source_target_pairs={{0,4},{2,6},{4,8},{6,10},{8,12},{10,14},{12,0},{14,2},{1,5},{3,7},... | collective-permute-start | bytes 294920 | tf_op jit(solution)/shard_map/ppermute | solution.py:355
  58.0 9.0 %collective-permute-start.11 = (bf16[96,512]{1,0:T(8,128)(2,1)S(1)}, bf16[96,512]{1,0:T(8,128)(2,1)S(1)}, u32[]{:S(2)}, u32[]{:S(2)}) collective-permute-start(bf16[96,512]{1,0:T(8,128)(2,1)S(1)} %get-tuple-element.68), channel_id=1, source_target_pairs={{0,12},{2,14},{4,0},{6,2},{8,4},{10,6},{12,8},{14,10},{1,13},{3,15... | collective-permute-start | bytes 294920 | tf_op jit(solution)/shard_map/ppermute | solution.py:355
  67.0 13.8 %copy-start.6 = (bf16[96,512]{1,0:T(8,128)(2,1)}, bf16[96,512]{1,0:T(8,128)(2,1)S(1)}, u32[]{:S(2)}) copy-start(bf16[96,512]{1,0:T(8,128)(2,1)S(1)} %collective-permute-done.1) | copy-start | bytes 294916
  67.0 29.6 %all-to-all-start.1 = ((f32[8,32,1536]{2,1,0:T(8,128)}), f32[8,32,1536]{2,1,0:T(8,128)S(1)}, u32[]{:S(2)}, u32[]{:S(2)}) async-start(f32[8,32,1536]{2,1,0:T(8,128)} %shard_map.59), calls=%async_computation.1 | async-start | bytes 3145728 | tf_op jit(solution)/shard_map/all_to_all | solution.py:377
  73.6 13.3 %collective-permute-start.13 = (bf16[96,512]{1,0:T(8,128)(2,1)S(1)}, bf16[96,512]{1,0:T(8,128)(2,1)S(1)}, u32[]{:S(2)}, u32[]{:S(2)}) collective-permute-start(bf16[96,512]{1,0:T(8,128)(2,1)S(1)} %get-tuple-element.77), channel_id=1, source_target_pairs={{0,6},{2,8},{4,10},{6,12},{8,14},{10,0},{12,2},{14,4},{1,7},{3,9},... | collective-permute-start | bytes 294920 | tf_op jit(solution)/shard_map/ppermute | solution.py:355
  75.1 11.9 %collective-permute-start.14 = (bf16[96,512]{1,0:T(8,128)(2,1)S(1)}, bf16[96,512]{1,0:T(8,128)(2,1)S(1)}, u32[]{:S(2)}, u32[]{:S(2)}) collective-permute-start(bf16[96,512]{1,0:T(8,128)(2,1)S(1)} %get-tuple-element.78), channel_id=1, source_target_pairs={{0,8},{2,10},{4,12},{6,14},{8,0},{10,2},{12,4},{14,6},{1,9},{3,11}... | collective-permute-start | bytes 294920 | tf_op jit(solution)/shard_map/ppermute | solution.py:355
  77.7 9.3 %collective-permute-start.15 = (bf16[96,512]{1,0:T(8,128)(2,1)S(1)}, bf16[96,512]{1,0:T(8,128)(2,1)S(1)}, u32[]{:S(2)}, u32[]{:S(2)}) collective-permute-start(bf16[96,512]{1,0:T(8,128)(2,1)S(1)} %get-tuple-element.79), channel_id=1, source_target_pairs={{0,10},{2,12},{4,14},{6,0},{8,2},{10,4},{12,6},{14,8},{1,11},{3,13... | collective-permute-start | bytes 294920 | tf_op jit(solution)/shard_map/ppermute | solution.py:355
  80.8 11.7 %collective-permute-start.16 = (bf16[96,512]{1,0:T(8,128)(2,1)S(1)}, bf16[96,512]{1,0:T(8,128)(2,1)S(1)}, u32[]{:S(2)}, u32[]{:S(2)}) collective-permute-start(bf16[96,512]{1,0:T(8,128)(2,1)S(1)} %get-tuple-element.81), channel_id=1, source_target_pairs={{0,14},{2,0},{4,2},{6,4},{8,6},{10,8},{12,10},{14,12},{1,15},{3,1}... | collective-permute-start | bytes 294920 | tf_op jit(solution)/shard_map/ppermute | solution.py:355
  92.5 12.5 %copy-start.3 = (bf16[8,96,512]{2,1,0:T(8,128)(2,1)}, bf16[8,96,512]{2,1,0:T(8,128)(2,1)S(1)}, u32[]{:S(2)}) copy-start(bf16[8,96,512]{2,1,0:T(8,128)(2,1)S(1)} %bitcast_dynamic-update-slice_fusion.refs_0_) | copy-start | bytes 2359300
  92.5 18.1 %collective-permute-start.17 = (bf16[8,96,512]{2,1,0:T(8,128)(2,1)S(1)}, bf16[8,96,512]{2,1,0:T(8,128)(2,1)S(1)}, u32[]{:S(2)}, u32[]{:S(2)}) collective-permute-start(bf16[8,96,512]{2,1,0:T(8,128)(2,1)S(1)} %bitcast_dynamic-update-slice_fusion.refs_0_), channel_id=1, source_target_pairs={{0,1},{1,0},{2,3},{3,2},{4,5},{5,4},{6,7},{7,6},{8,9},{9,8},{10,11... | collective-permute-start | bytes 2359304 | tf_op jit(solution)/shard_map/ppermute | solution.py:346
  96.7 3.5 %collective-permute-start.20 = (f32[32,512]{1,0:T(8,128)S(1)}, f32[32,512]{1,0:T(8,128)S(1)}, u32[]{:S(2)}, u32[]{:S(2)}) collective-permute-start(f32[32,512]{1,0:T(8,128)S(1)} %get-tuple-element.86.half), channel_id=1, source_target_pairs={{0,2},{2,0},{4,6},{6,4},{8,10},{10,8},{12,14},{14,12},{1,3},{3,1},... | collective-permute-start | bytes 196616 | tf_op jit(solution)/shard_map/ppermute | solution.py:346
  101.4 24.6 %all-to-all-start.2 = ((bf16[8,2,32,1024]{3,2,1,0:T(8,128)(2,1)}), bf16[8,2,32,1024]{3,2,1,0:T(8,128)(2,1)S(1)}, u32[]{:S(2)}, u32[]{:S(2)}) async-start(bf16[8,2,32,1024]{3,2,1,0:T(8,128)(2,1)} %shard_map.62), calls=%async_computation.2 | async-start | bytes 2097152 | tf_op jit(solution)/shard_map/all_to_all | solution.py:383
  105.0 9.1 %collective-permute-start.18 = (bf16[8,96,512]{2,1,0:T(8,128)(2,1)S(1)}, bf16[8,96,512]{2,1,0:T(8,128)(2,1)S(1)}, u32[]{:S(2)}, u32[]{:S(2)}) collective-permute-start(bf16[8,96,512]{2,1,0:T(8,128)(2,1)S(1)} %bitcast_dynamic-update-slice_fusion.refs_0_), channel_id=1, source_target_pairs={{0,16},{16,0},{1,17},{17,1},{2,18},{18,2},{3,19},{19,3},{4,20},{20... | collective-permute-start | bytes 2359304 | tf_op jit(solution)/shard_map/ppermute | solution.py:346
  110.6 3.6 %copy-start.5 = (bf16[8,96,512]{2,1,0:T(8,128)(2,1)}, bf16[8,96,512]{2,1,0:T(8,128)(2,1)S(1)}, u32[]{:S(2)}) copy-start(bf16[8,96,512]{2,1,0:T(8,128)(2,1)S(1)} %collective-permute-done.17.refs_1_) | copy-start | bytes 2359300
  110.6 5.5 %collective-permute-start.19 = (bf16[8,96,512]{2,1,0:T(8,128)(2,1)S(1)}, bf16[8,96,512]{2,1,0:T(8,128)(2,1)S(1)}, u32[]{:S(2)}, u32[]{:S(2)}) collective-permute-start(bf16[8,96,512]{2,1,0:T(8,128)(2,1)S(1)} %collective-permute-done.17.refs_1_), channel_id=1, source_target_pairs={{0,16},{16,0},{1,17},{17,1},{2,18},{18,2},{3,19},{19,3},{4,20},{20... | collective-permute-start | bytes 2359304 | tf_op jit(solution)/shard_map/ppermute | solution.py:346
  128.5 29.1 %copy-start.1 = (bf16[768,768]{1,0:T(8,128)(2,1)S(1)}, bf16[768,768]{1,0:T(8,128)(2,1)}, u32[]{:S(2)}) copy-start(bf16[768,768]{1,0:T(8,128)(2,1)} %w_ref.5) | copy-start | bytes 3538948
